TPU v7x, 32 devices: a whole 2x2x4 slice. The times are simulated.
32 devices in a mesh: groups: 2 (over x), pos: 8 (over z, y), head: 2 (over core).
Axes of the slice: x: 2, y: 2, z: 4, core: 2. Of those that a mesh axis runs over, the one named last changes fastest.
Arguments:
- enc_keys: bfloat16 [8192, 2048], P(('groups', 'pos'), 'head'), parts along dimension 0, may hold values from -64 to 64
- enc_values: bfloat16 [8192, 2048], P(('groups', 'pos'), 'head'), parts along dimension 0, may hold values from -6 to 6
- input_ids: int32 [8192], P(('groups', 'pos')), parts along dimension 0, may hold values from 0 to 2
- latent_queries: bfloat16 [4096, 2048], P('groups', 'head'), parts along dimension 0, may hold values from -40 to 40
- latent_array: bfloat16 [4096, 2048], P(('groups', 'pos')), parts along dimension 0, may hold values from -0.29882812 to 0.29882812
- w_out: bfloat16 [2048, 2048], P('head', 'pos'), may hold values from -0.125 to 0.125
- norm_gain: float32 [2048], replicated, may hold values from 0.1 to 1.9
- w_key: bfloat16 [2048, 2048], P('pos', 'head'), may hold values from -0.125 to 0.125
- w_value: bfloat16 [2048, 2048], P('pos', 'head'), may hold values from -0.125 to 0.125
- query_features: bfloat16 [8192, 2048], P(('groups', 'pos'), 'head'), parts along dimension 0, may hold values from -120 to 120
- query_ids: int32 [8192], P(('groups', 'pos')), parts along dimension 0, may hold values from 0 to 2
- query_table: bfloat16 [3, 2048], P(None, 'head'), may hold values from -6 to 6
- enc_bias: float32 [3, 16], P(None, 'head'), may hold values from -2 to 2
- query_counts: int32 [6], P('groups'), parts along dimension 0, may hold values from 512 to 1364
Outputs:
- latents_out: float32 [4096, 2048], P(('groups', 'pos'), 'head'), parts along dimension 0
- decoded: float32 [8192, 2048], P(('groups', 'pos'), 'head'), parts along dimension 0
There are 2 independent parts, one for each index of `groups`. A program takes and returns all parts, laid end to end along the dimension named above; an argument that names none is the same for every part. Nothing has to cross between parts.
All inputs are finite; a program needn't handle non-finite values.
Results may differ from a plain program's by a relative error of at most 0.03.
Values may be sent and summed in bfloat16 or wider, within the bound.
No kernel may reach another device: no remote copies, remote signals or barrier semaphores. Data moves between devices by JAX's collectives and lax.ppermute only.
A program may use at most 128 MiB of HBM per device.

v0:
```python
import jax
import jax.numpy as jnp
from jax import lax
from jax.sharding import PartitionSpec as P

HEAD_DIM = 128


norm_eps = 1e-06


def prefix(shard, axis, combine, identity):
    peers, place = (lax.axis_size(axis), lax.axis_index(axis))
    everything = lax.all_gather(shard, axis)
    start = jnp.broadcast_to(jnp.asarray(identity, shard.dtype), shard.shape)

    def step(k, before):
        reached = k < place
        new = combine(before, everything[k])
        return jnp.where(reached, new, before)

    return lax.fori_loop(0, peers, step, start)


def on_device(
    enc_keys,
    enc_values,
    input_ids,
    latent_queries,
    latent_array,
    w_out,
    norm_gain,
    w_key,
    w_value,
    query_features,
    query_ids,
    query_table,
    enc_bias,
    query_counts,
):
    tok_rows = enc_keys.shape[0]
    half_width = enc_keys.shape[1]
    local_heads = half_width // HEAD_DIM
    score_scale = HEAD_DIM ** (-0.5)
    modality = jnp.arange(enc_bias.shape[0], dtype=jnp.int32)
    in_onehot = (input_ids[:, None] == modality[None, :]).astype(jnp.float32)
    bias_rows = jnp.dot(in_onehot, enc_bias, precision=lax.Precision.HIGHEST)
    bias_heads = bias_rows.T[:, None, :]
    keys_split = enc_keys.reshape(tok_rows, local_heads, HEAD_DIM)
    values_split = enc_values.reshape(tok_rows, local_heads, HEAD_DIM)
    lat_total = latent_queries.shape[0]
    block_rows = min(512, lat_total)
    query_blocks = latent_queries.reshape(
        lat_total // block_rows, block_rows, local_heads, HEAD_DIM
    )

    def encode_block(block_queries):
        scores = (
            jnp.einsum(
                "nha,tha->hnt", block_queries, keys_split, preferred_element_type=jnp.float32
            )
            * score_scale
            + bias_heads
        )
        highest = jnp.max(scores, axis=2)
        weights = jnp.exp(scores - highest[:, :, None])
        totals = jnp.sum(weights, axis=2)
        summed = jnp.einsum(
            "hnt,tha->nha",
            weights.astype(jnp.bfloat16),
            values_split,
            preferred_element_type=jnp.float32,
        )
        return (highest.T, totals.T, summed.reshape(block_rows, half_width))

    block_max, block_tot, block_acc = lax.map(encode_block, query_blocks)
    row_highest = block_max.reshape(lat_total, local_heads)
    row_totals = block_tot.reshape(lat_total, local_heads)
    row_sums = block_acc.reshape(lat_total, half_width)
    own_rows = latent_array.shape[0]
    global_max = lax.pmax(row_highest, "pos")
    factor = jnp.exp(row_highest - global_max)
    scaled_sums = (row_sums.reshape(lat_total, local_heads, HEAD_DIM) * factor[:, :, None]).reshape(
        lat_total, half_width
    )
    totals, summed = (
        lax.psum_scatter(row_totals * factor, "pos", scatter_dimension=0, tiled=True),
        lax.psum_scatter(scaled_sums, "pos", scatter_dimension=0, tiled=True),
    )
    summed = summed.reshape(own_rows, local_heads, HEAD_DIM)
    attended = (summed / totals[:, :, None]).reshape(own_rows, half_width).astype(jnp.bfloat16)
    partial_value = jnp.dot(
        attended,
        lax.all_gather(w_out, "pos", axis=1, tiled=True),
        preferred_element_type=jnp.float32,
    )
    offset = lax.axis_index("head") * half_width
    projected = lax.psum(partial_value, "head")
    updated = latent_array.astype(jnp.float32) + projected
    mean_square = jnp.mean(updated * updated, axis=1, keepdims=True)
    normed_full = updated * lax.rsqrt(mean_square + norm_eps) * norm_gain
    normed = normed_full.astype(jnp.bfloat16)
    own_cols = lax.dynamic_slice_in_dim(normed_full, offset, half_width, 1)
    pieces = (
        lax.all_gather(w_key, "pos", axis=0, tiled=True),
        lax.all_gather(w_value, "pos", axis=0, tiled=True),
    )
    key_sum = jnp.dot(normed, pieces[0], preferred_element_type=jnp.float32)
    value_sum = jnp.dot(normed, pieces[1], preferred_element_type=jnp.float32)
    latent_keys = key_sum.astype(jnp.bfloat16)
    latent_values = value_sum.astype(jnp.bfloat16)
    q_onehot = (query_ids[:, None] == modality[None, :]).astype(jnp.int32)
    local_counts = jnp.sum(q_onehot, axis=0)
    before = prefix(
        local_counts, "pos", lambda earlier, later: earlier + later, jnp.zeros_like(local_counts)
    )
    within = jnp.cumsum(q_onehot, axis=0) - q_onehot
    ranked = jnp.sum((within + before[None, :]) * q_onehot, axis=1)
    limits = jnp.sum(q_onehot * query_counts[None, :], axis=1)
    kept_rows = ranked < limits
    lookup = jnp.dot(q_onehot.astype(jnp.bfloat16), query_table, preferred_element_type=jnp.float32)
    queries = (
        (query_features.astype(jnp.float32) + lookup)
        .astype(jnp.bfloat16)
        .reshape(tok_rows, local_heads, HEAD_DIM)
    )

    def fold_rows(running, key_rows, value_rows):
        running_max, running_tot, running_acc = running
        key_heads = key_rows.reshape(key_rows.shape[0], local_heads, HEAD_DIM)
        value_heads = value_rows.reshape(value_rows.shape[0], local_heads, HEAD_DIM)
        scores = (
            jnp.einsum("tha,rha->htr", queries, key_heads, preferred_element_type=jnp.float32)
            * score_scale
        )
        new_max = jnp.maximum(running_max, jnp.max(scores, axis=2))
        fade = jnp.exp(running_max - new_max)
        weights = jnp.exp(scores - new_max[:, :, None])
        new_tot = running_tot * fade + jnp.sum(weights, axis=2)
        new_acc = running_acc * fade[:, :, None] + jnp.einsum(
            "htr,rha->hta",
            weights.astype(jnp.bfloat16),
            value_heads,
            preferred_element_type=jnp.float32,
        )
        return (new_max, new_tot, new_acc)

    start_state = (
        jnp.full((local_heads, tok_rows), -jnp.inf, jnp.float32),
        jnp.zeros((local_heads, tok_rows), jnp.float32),
        jnp.zeros((local_heads, tok_rows, HEAD_DIM), jnp.float32),
    )
    running = start_state
    pieces = (
        lax.all_gather(latent_keys, "pos", axis=0, tiled=True),
        lax.all_gather(latent_values, "pos", axis=0, tiled=True),
    )
    row_count = pieces[0].shape[0]
    key_blocks = pieces[0].reshape(row_count // 512, 512, half_width)
    value_blocks = pieces[1].reshape(row_count // 512, 512, half_width)

    def scan_step(state, pair):
        return (fold_rows(state, pair[0], pair[1]), None)

    running, ignored = lax.scan(scan_step, running, (key_blocks, value_blocks))
    final_max, final_tot, final_acc = running
    dec_heads = final_acc / final_tot[:, :, None]
    dec_rows = jnp.transpose(dec_heads, (1, 0, 2)).reshape(tok_rows, half_width)
    decoded = jnp.where(kept_rows[:, None], dec_rows, 0.0)
    return (own_cols, decoded)


def solution(mesh):
    return jax.shard_map(
        on_device,
        mesh=mesh,
        in_specs=(
            P(("groups", "pos"), "head"),
            P(("groups", "pos"), "head"),
            P(("groups", "pos")),
            P("groups", "head"),
            P(("groups", "pos"), None),
            P("head", "pos"),
            P(),
            P("pos", "head"),
            P("pos", "head"),
            P(("groups", "pos"), "head"),
            P(("groups", "pos")),
            P(None, "head"),
            P(None, "head"),
            P("groups"),
        ),
        out_specs=(P(("groups", "pos"), "head"), P(("groups", "pos"), "head")),
        check_vma=False,
    )
```

profile of v0, /device:TPU:0, one launch (start us, length us, event | category | flops | bytes accessed | tf_op | source)
XLA Modules:
  0.0 852.0 jit_solution(433945212445187131)
XLA Ops:
  7.3 5.3 copy.48
  13.8 2.3 copy.26
  16.4 52.4 %while.43 = (s32[]{:T(128)}, f32[4,512,8]{1,2,0:T(8,128)S(1)}, f32[4,512,8]{1,2,0:T(8,128)S(1)}, f32[4,512,1024]{2,1,0:T(8,128)}, bf16[4,512,8,128]{3,2,1,0:T(8,...) while((s32[]{:T(128)}, f32[4,512,8]{1,2,0:T(8,128)S(1)}, ...), condition=%wide.region_3.4_spmd, body=%wide.region_0.3_spmd.sunk | while | flops 1096802304 | bytes 41074800 | solution.py:76
  17.7 1.9 fusion.61
  19.7 1.9 fusion.62
  21.5 4.6 fusion.63
  26.1 1.9 copy.68
  30.8 1.9 fusion.61
  32.7 1.9 fusion.62
  34.6 4.6 fusion.63
  39.2 1.9 copy.68
  43.9 1.9 fusion.61
  45.8 1.9 fusion.62
  47.7 4.6 fusion.63
  52.3 1.9 copy.68
  57.0 1.9 fusion.61
  60.8 4.6 fusion.63
  65.4 1.9 copy.68
  69.5 71.4 %all-reduce.4.cloned.1.call-done = f32[2048,8]{0,1:T(8,128)} async-done(((f32[2048,8]{0,1:T(8,128)}), f32[2048,8]{0,1:T(8,128)}) %all-reduce.4.cloned.1.call-update) | async-done | bytes 65552 | tf_op jit(solution)/shard_map/pmax | solution.py:81
  143.5 6.4 mul.67
  149.9 12.2 %bitcast_multiply_fusion = f32[2048,1024]{1,0:T(8,128)} fusion(f32[256,8,8,128]{3,2,1,0:T(8,128)} %bitcast.125, f32[4,512,1024]{2,1,0:T(8,128)} %get-tuple-element.163), kind=kLoop, calls=%fused_computation.35 | loop fusion | flops 2097152 | bytes 25165824 | tf_op jit(solution)/shard_map/mul | solution.py:83
  162.3 44.1 %reduce-scatter.5.cloned.1.call-done = f32[256,8]{0,1:T(8,128)} async-done(((f32[2048,8]{0,1:T(8,128)}), f32[256,8]{0,1:T(8,128)}) %reduce-scatter.5.cloned.1.call-update) | async-done | bytes 8208 | tf_op jit(solution)/shard_map/reduce_scatter | solution.py:87
  207.3 75.5 %all-gather.7.cloned.1.call-done = bf16[1024,2048]{1,0:T(8,128)(2,1)} async-done(((bf16[1024,256]{1,0:T(8,128)(2,1)}), bf16[1024,2048]{1,0:T(8,128)(2,1)}) %all-gather.7.cloned.1.call-update) | async-done | bytes 4194320 | tf_op jit(solution)/shard_map/all_gather | solution.py:94
  282.8 151.2 %reduce-scatter.3.cloned.1.call-done = f32[256,1024]{1,0:T(8,128)} async-done(((f32[2048,1024]{1,0:T(8,128)}), f32[256,1024]{1,0:T(8,128)}) %reduce-scatter.3.cloned.1.call-update) | async-done | bytes 1048592 | tf_op jit(solution)/shard_map/reduce_scatter | solution.py:88
  434.3 5.2 fusion.24
  440.9 19.0 %all-reduce.6.cloned.1.call-done = f32[256,2048]{1,0:T(8,128)} async-done(((f32[256,2048]{1,0:T(8,128)}), f32[256,2048]{1,0:T(8,128)}) %all-reduce.6.cloned.1.call-update) | async-done | bytes 2097168 | tf_op jit(solution)/shard_map/psum | solution.py:98
  459.9 2.1 multiply_reduce_fusion
  462.5 74.2 %all-gather.9.cloned.1.call-done = bf16[2048,1024]{1,0:T(8,128)(2,1)} async-done(((bf16[256,1024]{1,0:T(8,128)(2,1)}), bf16[2048,1024]{1,0:T(8,128)(2,1)}) %all-gather.9.cloned.1.call-update) | async-done | bytes 4194320 | tf_op jit(solution)/shard_map/all_gather | solution.py:105
  536.7 4.3 convolution_convert_fusion.1
  541.1 69.7 %all-gather.13.cloned.1.call-done = bf16[2048,1024]{1,0:T(8,128)(2,1)} async-done(((bf16[256,1024]{1,0:T(8,128)(2,1)}), bf16[2048,1024]{1,0:T(8,128)(2,1)}) %all-gather.13.cloned.1.call-update) | async-done | bytes 4194320 | tf_op jit(solution)/shard_map/all_gather | solution.py:106
  610.7 4.3 convolution_convert_fusion
  616.7 9.7 %all-reduce = s32[24]{0:T(128)S(1)} all-reduce(s32[24]{0:T(128)S(1)} %dynamic-update-slice), channel_id=2, replica_groups=mesh['groups'=2,'pos'=8,'head'=2] {'pos'}, use_global_device_ids=true, to_apply=%add | all-reduce | flops 24 | bytes 192
  631.0 53.8 %all-gather.11.cloned.1.call-done = bf16[2048,1024]{1,0:T(8,128)(2,1)} async-done(((bf16[256,1024]{1,0:T(8,128)(2,1)}), bf16[2048,1024]{1,0:T(8,128)(2,1)}) %all-gather.11.cloned.1.call-update) | async-done | bytes 4194320 | tf_op jit(solution)/shard_map/all_gather | solution.py:155
  684.8 74.1 %all-gather.15.cloned.1.call-done = bf16[2048,1024]{1,0:T(8,128)(2,1)} async-done(((bf16[256,1024]{1,0:T(8,128)(2,1)}), bf16[2048,1024]{1,0:T(8,128)(2,1)}) %all-gather.15.cloned.1.call-update) | async-done | bytes 4194320 | tf_op jit(solution)/shard_map/all_gather | solution.py:156
  758.9 83.5 %while.45 = (s32[]{:T(128)}, f32[8,512]{1,0:T(8,128)S(1)}, f32[8,512]{1,0:T(8,128)S(1)}, f32[8,512,128]{2,1,0:T(8,128)}, bf16[4,512,1024]{2,1,0:T(8,128)(2,1)}, ...) while((s32[]{:T(128)}, f32[8,512]{1,0:T(8,128)S(1)}, ...), condition=%wide.region_19.20_spmd.clone, body=%wide.region_16.19_spmd.clone.sunk | while | flops 1092112384 | bytes 41156720 | solution.py:165
  761.1 5.8 bitcast_reduce_fusion.2
  766.9 4.8 fusion.68
  772.3 7.0 fusion.70
  781.6 5.8 bitcast_reduce_fusion.2
  787.3 4.8 fusion.68
  792.8 7.6 fusion.70
  802.6 5.8 bitcast_reduce_fusion.2
  808.4 4.8 fusion.68
  813.8 7.6 fusion.70
  823.6 5.8 bitcast_reduce_fusion.2
  829.4 4.8 fusion.68
  834.8 7.6 fusion.70
  842.4 3.1 bitcast_select_fusion
  (121 shorter events, 38.1 us)
Async XLA Ops:
  7.2 620.7 %copy-start = (bf16[3,1024]{1,0:T(4,128)(2,1)S(1)}, bf16[3,1024]{1,0:T(4,128)(2,1)}, u32[]{:S(2)}) copy-start(bf16[3,1024]{1,0:T(4,128)(2,1)} %param.31) | copy-start | bytes 18436
  7.2 133.7 %all-reduce.4.cloned.1.call-start = ((), (), s32[]{:S(2)}) async-start(), calls=%async_computation.2 | async-start | bytes 131072 | tf_op jit(solution)/shard_map/pmax | solution.py:81
  7.3 5.3 copy-start.5
  12.6 3.5 copy-start.10
  12.6 3.5 copy-start.11
  68.8 0.6 copy-start.6
  69.4 137.0 %reduce-scatter.5.cloned.1.call-start = ((), (), s32[]{:S(2)}) async-start(), calls=%async_computation.4 | async-start | bytes 73728 | tf_op jit(solution)/shard_map/reduce_scatter | solution.py:87
  142.4 140.4 %all-gather.7.cloned.1.call-start = ((), (), s32[]{:S(2)}) async-start(), calls=%async_computation.5 | async-start | bytes 4718592 | tf_op jit(solution)/shard_map/all_gather | solution.py:94
  143.1 290.8 %reduce-scatter.3.cloned.1.call-start = ((), (), s32[]{:S(2)}) async-start(), calls=%async_computation.3 | async-start | bytes 9437184 | tf_op jit(solution)/shard_map/reduce_scatter | solution.py:88
  162.1 297.8 %all-reduce.6.cloned.1.call-start = ((), (), s32[]{:S(2)}) async-start(), calls=%async_computation.6 | async-start | bytes 4194304 | tf_op jit(solution)/shard_map/psum | solution.py:98
  434.3 25.6 %copy-start.3 = (bf16[256,2048]{1,0:T(8,128)(2,1)S(1)}, bf16[256,2048]{1,0:T(8,128)(2,1)}, u32[]{:S(2)}) copy-start(bf16[256,2048]{1,0:T(8,128)(2,1)} %param.24) | copy-start | bytes 3145732
  439.5 22.6 %copy-start.8 = (f32[2048]{0:T(1024)S(1)}, f32[2048]{0:T(1024)}, u32[]{:S(2)}) copy-start(f32[2048]{0:T(1024)} %param.26) | copy-start | bytes 24580
  439.5 97.2 %all-gather.9.cloned.1.call-start = ((), (), s32[]{:S(2)}) async-start(), calls=%async_computation.7 | async-start | bytes 4718592 | tf_op jit(solution)/shard_map/all_gather | solution.py:105
  440.1 170.7 %all-gather.13.cloned.1.call-start = ((), (), s32[]{:S(2)}) async-start(), calls=%async_computation.9 | async-start | bytes 4718592 | tf_op jit(solution)/shard_map/all_gather | solution.py:106
  440.8 244.0 %all-gather.11.cloned.1.call-start = ((), (), s32[]{:S(2)}) async-start(), calls=%async_computation.8 | async-start | bytes 4718592 | tf_op jit(solution)/shard_map/all_gather | solution.py:155
  459.9 2.2 copy-start.2
  541.0 74.1 %copy-start.12 = (u32[32]{0:T(128)S(1)}, u32[32]{0:T(128)}, u32[]{:S(2)}) copy-start(u32[32]{0:T(128)} %constant.90) | copy-start | bytes 388
  541.0 75.3 %copy-start.7 = (s32[512]{0:T(512)S(1)}, s32[512]{0:T(512)}, u32[]{:S(2)}) copy-start(s32[512]{0:T(512)} %param.30) | copy-start | bytes 6148
  541.0 86.8 %copy-start.4 = (bf16[512,1024]{1,0:T(8,128)(2,1)S(1)}, bf16[512,1024]{1,0:T(8,128)(2,1)}, u32[]{:S(2)}) copy-start(bf16[512,1024]{1,0:T(8,128)(2,1)} %param.29) | copy-start | bytes 3145732
  541.0 217.8 %all-gather.15.cloned.1.call-start = ((), (), s32[]{:S(2)}) async-start(), calls=%async_computation.10 | async-start | bytes 4718592 | tf_op jit(solution)/shard_map/all_gather | solution.py:156
  615.0 14.8 %copy-start.9 = (s32[3]{0:T(128)S(1)}, s32[3]{0:T(128)}, u32[]{:S(2)}) copy-start(s32[3]{0:T(128)} %param.33) | copy-start | bytes 40
  842.4 3.1 copy-start.1
Sparse Core Ops, SparseCore 0:
  69.6 71.2 all-reduce.3
  145.2 61.1 reduce-scatter.4
  208.7 74.0 all-gather.6
  286.7 147.2 reduce-scatter.2
  439.6 20.2 all-reduce.5
  462.1 74.5 all-gather.8
  539.0 71.6 all-gather.12
  613.1 71.6 all-gather.10
  687.2 71.6 all-gather.14
where the time goes:
time: 853 us; the launch traced here: 852 us
  waiting for transfers between devices  635 us (74%)
  matrix products  93.3 us (11%)
  local copies, waits for them, and re-layouts  50.7 us (6%)
  other arithmetic  47.6 us (6%)
  between operations  14.7 us (2%)
  blocking collectives  9.74 us (1%)
    reduce_scatter x1, waiting for transfers between devices, on_device(): lax.psum_scatter(scaled_sums, 'pos', scatter_dimension=0, tiled=True)  151 us
    all_gather x1, waiting for transfers between devices, on_device(): lax.all_gather(w_out, 'pos', axis=1, tiled=True)  75.5 us
    all_gather x1, waiting for transfers between devices, on_device(): lax.all_gather(w_key, 'pos', axis=0, tiled=True)  74.2 us
    all_gather x1, waiting for transfers between devices, on_device(): lax.all_gather(latent_values, 'pos', axis=0, tiled=True)  74.1 us
    pmax x1, waiting for transfers between devices, on_device(): global_max = lax.pmax(row_highest, 'pos')  71.4 us
    all_gather x1, waiting for transfers between devices, on_device(): lax.all_gather(w_value, 'pos', axis=0, tiled=True)  69.7 us
    all_gather x1, waiting for transfers between devices, on_device(): lax.all_gather(latent_keys, 'pos', axis=0, tiled=True)  53.8 us
    reduce_scatter x1, waiting for transfers between devices, on_device(): lax.psum_scatter(row_totals * factor, 'pos', scatter_dimension=0, tiled=T...  44.1 us
  transfers between devices with their start and end apart: 9, of which 9 were waited for; matrix products, arithmetic and copies ran while one was open for 4% of the time, Pallas kernels for 0%

commit v1 on v0

--- a/solution.py
+++ b/solution.py
@@ -1,6 +1,10 @@
+import functools
+
 import jax
 import jax.numpy as jnp
 from jax import lax
+from jax.experimental import pallas as pl
+from jax.experimental.pallas import tpu as pltpu
 from jax.sharding import PartitionSpec as P
 
 HEAD_DIM = 128
@@ -22,7 +26,7 @@
     return lax.fori_loop(0, peers, step, start)
 
 
-def on_device(
+def plain_on_device(
     enc_keys,
     enc_values,
     input_ids,
@@ -170,9 +174,419 @@
     return (own_cols, decoded)
 
 
+LANES = 128
+EXTRA = 16
+LOG2E = 1.4426950408889634
+EXP2_SCALE = LOG2E * HEAD_DIM**-0.5
+NT = (((1,), (1,)), ((), ()))
+
+
+def params(mib):
+    return pltpu.CompilerParams(vmem_limit_bytes=mib << 20)
+
+
+def cost(flops, nbytes, exps=0):
+    return pl.CostEstimate(flops=int(flops), bytes_accessed=int(nbytes), transcendentals=int(exps))
+
+
+def whole(shape):
+    return pl.BlockSpec(shape, lambda *args: (0,) * len(shape))
+
+
+def pack_kernel(k_ref, v_ref, extra_ref, out_ref):
+    tokens = k_ref.shape[0]
+    out_ref[:tokens, :HEAD_DIM] = k_ref[...]
+    out_ref[:tokens, HEAD_DIM:] = v_ref[...]
+    out_ref[tokens:, :] = extra_ref[...]
+
+
+def pack(keys, values, extra):
+    tokens, width = keys.shape
+    heads = width // HEAD_DIM
+    column = pl.BlockSpec((tokens, HEAD_DIM), lambda h: (0, h))
+    block = (tokens + EXTRA, 2 * HEAD_DIM)
+    return pl.pallas_call(
+        pack_kernel,
+        grid=(heads,),
+        in_specs=[column, column, whole(extra.shape)],
+        out_specs=pl.BlockSpec(block, lambda h: (h, 0)),
+        out_shape=jax.ShapeDtypeStruct((heads * block[0], block[1]), keys.dtype),
+        compiler_params=params(16),
+        cost_estimate=cost(0, 8 * tokens * width),
+        name="pack_heads",
+    )(keys, values, extra)
+
+
+def encode_kernel(pos, tokens, ids_ref, q_ref, kv_ref, bias_ref, out_ref):
+    rows = q_ref.shape[0]
+    head = ids_ref[0]
+    queries = q_ref[...]
+    ones = jnp.ones((tokens, LANES), jnp.bfloat16)
+    row_bits = kv_ref.shape[1]
+    top = jnp.full((rows, 1), -jnp.inf, jnp.float32)
+    acc = jnp.zeros((rows, 2 * HEAD_DIM), jnp.float32)
+    for j in range(pos):
+        base = j * (tokens + EXTRA)
+        band = slice(base, base + tokens)
+        scores = lax.dot_general(
+            queries, kv_ref[band, :HEAD_DIM], NT, preferred_element_type=jnp.float32
+        )
+        tail = kv_ref[base + tokens : base + tokens + EXTRA, :].astype(jnp.float32)
+        kind = jnp.concatenate([tail[r : r + 1] for r in range(tokens // row_bits)], axis=1)
+        bias = jnp.zeros_like(kind)
+        for m in range(bias_ref.shape[0]):
+            bias = jnp.where(kind == m, bias_ref[m, head] * LOG2E, bias)
+        scores = scores * EXP2_SCALE + bias
+        new_top = jnp.maximum(top, jnp.max(scores, axis=1, keepdims=True))
+        weights = jnp.exp2(scores - new_top).astype(jnp.bfloat16)
+        acc = acc * jnp.exp2(top - new_top) + jnp.dot(
+            weights,
+            jnp.concatenate([kv_ref[band, HEAD_DIM:], ones], axis=1),
+            preferred_element_type=jnp.float32,
+        )
+        top = new_top
+    out_ref[...] = (acc[:, :HEAD_DIM] / acc[:, HEAD_DIM:]).astype(jnp.bfloat16)
+
+
+def encode(head, latent_queries, kv, enc_bias, pos):
+    latents = latent_queries.shape[0]
+    tokens = kv.shape[0] // pos - EXTRA
+    rows = min(512, latents)
+    grid_spec = pltpu.PrefetchScalarGridSpec(
+        num_scalar_prefetch=1,
+        grid=(latents // rows,),
+        in_specs=[
+            pl.BlockSpec((rows, HEAD_DIM), lambda i, ids: (i, ids[0])),
+            whole(kv.shape),
+            pl.BlockSpec(memory_space=pltpu.SMEM),
+        ],
+        out_specs=pl.BlockSpec((rows, HEAD_DIM), lambda i, ids: (i, 0)),
+    )
+    return pl.pallas_call(
+        functools.partial(encode_kernel, pos, tokens),
+        grid_spec=grid_spec,
+        out_shape=jax.ShapeDtypeStruct((latents, HEAD_DIM), jnp.bfloat16),
+        compiler_params=params(32),
+        cost_estimate=cost(
+            16 * latents * tokens * pos * HEAD_DIM, 2 * kv.size, latents * tokens * pos
+        ),
+        name="encode_head",
+    )(head.reshape(1), latent_queries, kv, enc_bias)
+
+
+def project_kernel(heads, att_in_ref, w_ref, out_ref, att_ref):
+    rows = att_ref.shape[0]
+    shares, depth, _ = w_ref.shape
+
+    @pl.when(pl.program_id(0) == 0)
+    def arrange():
+        for h in range(heads):
+            att_ref[:, h * HEAD_DIM : (h + 1) * HEAD_DIM] = att_in_ref[h * rows : (h + 1) * rows, :]
+
+    total = None
+    for k in range(shares):
+        term = jnp.dot(
+            att_ref[:, k * depth : (k + 1) * depth], w_ref[k], preferred_element_type=jnp.float32
+        )
+        total = term if total is None else total + term
+    out_ref[...] = total
+
+
+def project(attended, w_all, rows, depth):
+    heads = attended.shape[0] // rows
+    shares, long, cols = w_all.shape
+    steps = long // depth
+    return pl.pallas_call(
+        functools.partial(project_kernel, heads),
+        grid=(steps,),
+        in_specs=[
+            whole(attended.shape),
+            pl.BlockSpec((shares, depth, cols), lambda i: (0, i, 0)),
+        ],
+        out_specs=pl.BlockSpec((rows, cols), lambda i: (0, i)),
+        out_shape=jax.ShapeDtypeStruct((rows, steps * cols), jnp.float32),
+        scratch_shapes=[pltpu.VMEM((rows, heads * HEAD_DIM), jnp.bfloat16)],
+        compiler_params=params(32),
+        cost_estimate=cost(2 * rows * w_all.size, 2 * w_all.size + 4 * rows * steps * cols),
+        name="project_rows",
+    )(attended, w_all)
+
+
+def norm_kernel(
+    shares, band, ids_ref, mine_ref, theirs_ref, latent_ref, gain_ref, out_ref, normed_ref, full_ref
+):
+    updated = latent_ref[...].astype(jnp.float32) + (mine_ref[...] + theirs_ref[...])
+    mean_square = jnp.mean(updated * updated, axis=1, keepdims=True)
+    full_ref[...] = updated * lax.rsqrt(mean_square + norm_eps) * gain_ref[...]
+    half = out_ref.shape[1]
+    own = full_ref[:, pl.ds(pl.multiple_of(ids_ref[0] * half, half), half)]
+    out_ref[...] = own
+    normed = own.astype(jnp.bfloat16)
+    count = half // (shares * band)
+    for i in range(count):
+        for k in range(shares):
+            source = (i * shares + k) * band
+            target = (k * count + i) * band
+            normed_ref[:, target : target + band] = normed[:, source : source + band]
+
+
+def normalise(place, mine, theirs, latent_array, gain, shares, band):
+    rows, width = mine.shape
+    half = width // 2
+    grid_spec = pltpu.PrefetchScalarGridSpec(
+        num_scalar_prefetch=1,
+        grid=(1,),
+        in_specs=[whole((rows, width))] * 3 + [whole((1, width))],
+        out_specs=[whole((rows, half))] * 2,
+        scratch_shapes=[pltpu.VMEM((rows, width), jnp.float32)],
+    )
+    return pl.pallas_call(
+        functools.partial(norm_kernel, shares, band),
+        grid_spec=grid_spec,
+        out_shape=[
+            jax.ShapeDtypeStruct((rows, half), jnp.float32),
+            jax.ShapeDtypeStruct((rows, half), jnp.bfloat16),
+        ],
+        compiler_params=params(32),
+        cost_estimate=cost(6 * rows * width, 13 * rows * width),
+        name="norm_rows",
+    )(place.reshape(1), mine, theirs, latent_array, gain)
+
+
+def decode_kernel(shares, pieces, first, last, ids_ref, *refs):
+    mine = refs[:pieces]
+    theirs = refs[pieces : 2 * pieces]
+    wk_ref, wv_ref, q_ref = refs[2 * pieces : 2 * pieces + 3]
+    rest = list(refs[2 * pieces + 3 :])
+    if not first:
+        old_max_ref, old_acc_ref = rest[:2]
+        rest = rest[2:]
+    if last:
+        kept_ref, out_ref = rest[:2]
+        rest = rest[2:]
+    else:
+        max_ref, acc_ref = rest[:2]
+        rest = rest[2:]
+    (normed_ref,) = rest
+    rows, half = mine[0].shape
+    part = half // shares
+
+    @pl.when(pl.program_id(0) == 0)
+    def arrange():
+        for r in range(pieces):
+            band = slice(r * rows, (r + 1) * rows)
+            for k in range(shares):
+                cols = slice(k * part, (k + 1) * part)
+                for source, which in ((mine[r], ids_ref[0]), (theirs[r], 1 - ids_ref[0])):
+                    start = pl.multiple_of(k * 2 * part + which * part, part)
+                    normed_ref[band, pl.ds(start, part)] = source[:, cols]
+
+    normed = normed_ref[...]
+    keys = jnp.dot(normed, wk_ref[...], preferred_element_type=jnp.float32).astype(jnp.bfloat16)
+    values = jnp.dot(normed, wv_ref[...], preferred_element_type=jnp.float32).astype(jnp.bfloat16)
+    ones = jnp.ones((keys.shape[0], LANES), jnp.bfloat16)
+    for h in range(keys.shape[1] // HEAD_DIM):
+        cols = slice(h * HEAD_DIM, (h + 1) * HEAD_DIM)
+        wide = slice(2 * h * HEAD_DIM, 2 * (h + 1) * HEAD_DIM)
+        scores = lax.dot_general(
+            q_ref[:, cols], keys[:, cols], NT, preferred_element_type=jnp.float32
+        )
+        scores = scores * EXP2_SCALE
+        highest = jnp.max(scores, axis=1, keepdims=True)
+        if not first:
+            old_max = old_max_ref[:, cols]
+            new_max = jnp.maximum(old_max, highest)
+            highest = new_max[:, :1]
+            fade = jnp.exp2(old_max - new_max)
+        weights = jnp.exp2(scores - highest).astype(jnp.bfloat16)
+        summed = jnp.dot(
+            weights,
+            jnp.concatenate([values[:, cols], ones], axis=1),
+            preferred_element_type=jnp.float32,
+        )
+        acc, tot = summed[:, :HEAD_DIM], summed[:, HEAD_DIM:]
+        if not first:
+            old = old_acc_ref[:, wide]
+            acc = acc + old[:, :HEAD_DIM] * fade
+            tot = tot + old[:, HEAD_DIM:] * fade
+        if last:
+            out_ref[:, cols] = jnp.where(kept_ref[...] > 0.0, acc / tot, 0.0)
+        else:
+            if first:
+                new_max = jnp.broadcast_to(highest, acc.shape)
+            max_ref[:, cols] = new_max
+            acc_ref[:, wide] = jnp.concatenate([acc, tot], axis=1)
+
+
+def decode(place, mine, theirs, weights, queries, state, kept, shares):
+    first, last = state is None, kept is not None
+    tokens, width = queries.shape
+    rows, half = mine[0].shape
+    depth = weights.shape[0]
+    pair = 2 * HEAD_DIM
+    steps = width // pair
+    pieces = len(mine)
+    pair_block = pl.BlockSpec((tokens, pair), lambda i, ids: (0, i))
+    wide_block = pl.BlockSpec((tokens, 2 * pair), lambda i, ids: (0, i))
+    in_specs = [whole((rows, half))] * (2 * pieces) + [
+        pl.BlockSpec((depth, pair), lambda i, ids: (0, i)),
+        pl.BlockSpec((depth, pair), lambda i, ids: (0, steps + i)),
+        pair_block,
+    ]
+    args = [*mine, *theirs, weights, weights, queries]
+    if not first:
+        in_specs += [pair_block, wide_block]
+        args += list(state)
+    if last:
+        in_specs += [whole(kept.shape)]
+        args += [kept]
+        out_specs = pair_block
+        out_shape = jax.ShapeDtypeStruct((tokens, width), jnp.float32)
+    else:
+        out_specs = [pair_block, wide_block]
+        out_shape = [
+            jax.ShapeDtypeStruct((tokens, width), jnp.float32),
+            jax.ShapeDtypeStruct((tokens, 2 * width), jnp.float32),
+        ]
+    latents = rows * pieces
+    grid_spec = pltpu.PrefetchScalarGridSpec(
+        num_scalar_prefetch=1,
+        grid=(steps,),
+        in_specs=in_specs,
+        out_specs=out_specs,
+        scratch_shapes=[pltpu.VMEM((latents, 2 * half), jnp.bfloat16)],
+    )
+    return pl.pallas_call(
+        functools.partial(decode_kernel, shares, pieces, first, last),
+        grid_spec=grid_spec,
+        out_shape=out_shape,
+        compiler_params=params(48),
+        cost_estimate=cost(
+            4 * latents * depth * width + 16 * tokens * latents * width,
+            4 * depth * width + 24 * tokens * width,
+            tokens * latents * (width // HEAD_DIM),
+        ),
+        name="decode_rows",
+    )(place.reshape(1), *args)
+
+
+def swap_perm(size):
+    return [(i, i ^ 1) for i in range(size)]
+
+
+def shift_perm(size, k):
+    far = size // 2
+    return [(((z + k) % far) * 2 + y, z * 2 + y) for z in range(far) for y in range(2)]
+
+
+def fast_on_device(
+    sizes,
+    enc_keys,
+    enc_values,
+    input_ids,
+    latent_queries,
+    latent_array,
+    w_out,
+    norm_gain,
+    w_key,
+    w_value,
+    query_features,
+    query_ids,
+    query_table,
+    enc_bias,
+    query_counts,
+):
+    groups, pos = sizes
+    far = pos // 2
+    g = lax.axis_index("groups")
+    p = lax.axis_index("pos")
+    place = lax.axis_index("head")
+    rows = latent_array.shape[0]
+    tokens, half_width = enc_keys.shape
+    heads = half_width // HEAD_DIM
+    mods = enc_bias.shape[0]
+    modality = jnp.arange(mods, dtype=jnp.int32)
+    pair = 2 * HEAD_DIM
+
+    def share(weight):
+        depth = weight.shape[0] // groups
+        own = lax.dynamic_slice_in_dim(weight, g * depth, depth, 0)
+        return lax.all_gather(own, ("groups", "pos"), tiled=True), depth
+
+    out_all, out_depth = share(w_out)
+    out_all = out_all.reshape(groups, pos * out_depth, w_out.shape[1])
+    kv_all, kv_depth = share(jnp.concatenate([w_key, w_value], axis=1))
+
+    q_onehot = (query_ids[:, None] == modality[None, :]).astype(jnp.int32)
+    local_counts = jnp.sum(q_onehot, axis=0)
+    id_rows = tokens // pair
+    counted = jnp.concatenate([local_counts // 16, local_counts % 16])
+    extra = jnp.concatenate(
+        [
+            input_ids.reshape(id_rows, pair),
+            jnp.pad(counted[None, :], ((0, EXTRA - id_rows - 1), (0, pair - 2 * mods))),
+        ]
+    ).astype(jnp.bfloat16)
+    payload = pack(enc_keys, enc_values, extra)
+    kv = lax.all_to_all(payload, "pos", 0, 0, tiled=True)
+    attended = encode(p, latent_queries, kv, enc_bias, pos)
+    attended = lax.all_to_all(attended, "pos", 0, 0, tiled=True)
+
+    partial_value = project(attended, out_all, rows, out_depth)
+    theirs = lax.ppermute(partial_value, "head", swap_perm(2))
+    own_cols, normed = normalise(
+        place, partial_value, theirs, latent_array, norm_gain[None, :], groups, kv_depth
+    )
+
+    counts = kv.reshape(pos, tokens + EXTRA, pair)[:, tokens + id_rows, : 2 * mods]
+    counts = counts.astype(jnp.int32)
+    counts = counts[:, :mods] * 16 + counts[:, mods:]
+    earlier = jnp.arange(pos, dtype=jnp.int32)[:, None] < p
+    before = jnp.sum(jnp.where(earlier, counts, 0), axis=0)
+    within = jnp.cumsum(q_onehot, axis=0) - q_onehot
+    ranked = jnp.sum((within + before[None, :]) * q_onehot, axis=1)
+    limits = jnp.sum(q_onehot * query_counts[None, :], axis=1)
+    kept = (ranked < limits).astype(jnp.float32)[:, None]
+    lookup = jnp.dot(q_onehot.astype(jnp.bfloat16), query_table, preferred_element_type=jnp.float32)
+    queries = (query_features.astype(jnp.float32) + lookup).astype(jnp.bfloat16)
+
+    state = None
+    shifts = sorted(range(far), key=lambda k: min(k, far - k))
+    arrived = {0: normed}
+    for k in shifts[1:]:
+        arrived[k] = lax.ppermute(normed, "pos", shift_perm(pos, k))
+    for k in shifts:
+        mine = [arrived[k], lax.ppermute(arrived[k], "pos", swap_perm(pos))]
+        others = [lax.ppermute(v, "head", swap_perm(2)) for v in mine]
+        state = decode(
+            place, mine, others, kv_all, queries, state, kept if k == shifts[-1] else None, groups
+        )
+    return (own_cols, state)
+
+
+def on_device(sizes, *args):
+    groups, pos, head = sizes
+    enc_keys, latent_array, w_out, w_key = args[0], args[4], args[5], args[7]
+    fits = (
+        head == 2
+        and pos % 2 == 0
+        and pos > 2
+        and enc_keys.shape[1] == pos * HEAD_DIM
+        and enc_keys.shape[0] % (2 * HEAD_DIM) == 0
+        and enc_keys.shape[0] < 2048
+        and w_key.shape[0] % (LANES * groups) == 0
+        and w_out.shape[0] % (LANES * groups) == 0
+        and w_out.shape[1] % LANES == 0
+        and latent_array.shape[0] % LANES == 0
+    )
+    if fits:
+        return fast_on_device((groups, pos), *args)
+    return plain_on_device(*args)
+
+
 def solution(mesh):
     return jax.shard_map(
-        on_device,
+        functools.partial(on_device, tuple(mesh.shape[a] for a in ("groups", "pos", "head"))),
         mesh=mesh,
         in_specs=(
             P(("groups", "pos"), "head"),

time: 853 us -> 347 us (0.41)
  waiting for transfers between devices: 635 us -> 193 us
  matrix products: 93.3 us -> 1.72 us
  Pallas kernels: 0 us -> 81 us
  other arithmetic: 47.6 us -> 3.49 us
  local copies, waits for them, and re-layouts: 50.7 us -> 11.8 us
  starting transfers between devices: 0.54 us -> 16.8 us
  blocking collectives: 9.74 us -> 23.2 us
    all_gather x5 -> x2, waiting for transfers between devices: 347 us -> 58.7 us  [share(): return (lax.all_gather(own, ('groups', 'pos'), tiled=True), depth)]
    reduce_scatter x2 -> x0, waiting for transfers between devices: 195 us -> none  [the longest x1 151 us: on_device(): lax.psum_scatter(scaled_sums, 'pos', scatter_dimension=0, tiled=True)]
    dot_general x21 -> x1, matrix products: 93.3 us -> 1.72 us  [fast_on_device(): jnp.dot(q_onehot.astype(jnp.bfloat16), query_table, preferred_element_typ...]
    pallas_call x0 -> x8, Pallas kernels: none -> 81 us  [the longest x4 58.2 us: decode(): pl.pallas_call(functools.partial(decode_kernel, shares, pieces, first, la...]
    pmax x1 -> x0, waiting for transfers between devices: 71.4 us -> none  [on_device(): global_max = lax.pmax(row_highest, 'pos')]
    ppermute x0 -> x16, waiting for transfers between devices: none -> 68.1 us  [the longest x3 57.1 us: fast_on_device(): arrived[k] = lax.ppermute(normed, 'pos', shift_perm(pos, k))]
    all_to_all x0 -> x1, waiting for transfers between devices: none -> 66.4 us  [fast_on_device(): kv = lax.all_to_all(payload, 'pos', 0, 0, tiled=True)]
    reduce_sum x11 -> x3, other arithmetic: 29.1 us -> 0.3 us  [the longest x1 0.12 us: fast_on_device(): local_counts = jnp.sum(q_onehot, axis=0)]
  transfers between devices with their start and end apart: 9 -> 19, of which waited for: 9 -> 7; matrix products, arithmetic and copies ran while one was open for 4% -> 2% of each run, Pallas kernels for 0% -> 19%
where the time goes in v1:
time: 347 us; the launch traced here: 346 us
  waiting for transfers between devices  193 us (56%)
  Pallas kernels  81 us (23%)
  blocking collectives  23.2 us (7%)
  starting transfers between devices  16.8 us (5%)
  between operations  14.3 us (4%)
  local copies, waits for them, and re-layouts  11.8 us (3%)
  other arithmetic  3.49 us (1%)
    all_to_all x1, waiting for transfers between devices, fast_on_device(): kv = lax.all_to_all(payload, 'pos', 0, 0, tiled=True)  66.4 us
    all_gather x2, waiting for transfers between devices, share(): return (lax.all_gather(own, ('groups', 'pos'), tiled=True), depth)  58.7 us
    pallas_call x4, Pallas kernels, decode(): pl.pallas_call(functools.partial(decode_kernel, shares, pieces, first, la...  58.2 us
    ppermute x3, waiting for transfers between devices, fast_on_device(): arrived[k] = lax.ppermute(normed, 'pos', shift_perm(pos, k))  57.1 us
    all_to_all x1, blocking collectives, fast_on_device(): attended = lax.all_to_all(attended, 'pos', 0, 0, tiled=True)  23.2 us
    pallas_call x1, Pallas kernels, encode(): pl.pallas_call(functools.partial(encode_kernel, pos, tokens), grid_spec=g...  12.7 us
    unnamed x30, local copies, waits for them, and re-layouts  10 us
    ppermute x4, waiting for transfers between devices, fast_on_device(): mine = [arrived[k], lax.ppermute(arrived[k], 'pos', swap_perm(pos))]  7.81 us
  transfers between devices with their start and end apart: 19, of which 7 were waited for; matrix products, arithmetic and copies ran while one was open for 2% of the time, Pallas kernels for 19%

profile of v1, /device:TPU:0, one launch (start us, length us, event | category | flops | bytes accessed | tf_op | source)
XLA Modules:
  0.0 345.6 jit_solution(4248023984700656462)
XLA Ops:
  7.3 0.9 copy-done
  8.2 0.7 constant_dynamic-slice_fusion
  9.0 1.9 fusion
  11.0 0.1 convert_reduce_fusion
  11.1 0.1 maximum_bitcast_fusion
  11.2 3.5 %pack_heads.1 = bf16[4224,256]{1,0:T(8,128)(2,1)} custom-call(bf16[512,1024]{1,0:T(8,128)(2,1)S(1)} %copy-done.3, bf16[512,1024]{1,0:T(8,128)(2,1)S(1)} %copy-done.4, bf16[16,256]{1,0:T(8,128)(2,1)S(1)} %fusion.5.extra_ref), custom_call_target="tpu_custom_call" | custom-call | bytes 4194304 | tf_op jit(solution)/shard_map/pack_heads/pallas_call | solution.py:208
  14.7 7.4 %all-to-all-start = ((bf16[8,528,256]{2,1,0:T(8,128)(2,1)}), bf16[8,528,256]{2,1,0:T(8,128)(2,1)S(1)}, u32[]{:S(2)}, u32[]{:S(2)}) async-start(bf16[8,528,256]{2,1,0:T(8,128)(2,1)} %bitcast.3), calls=%async_computation | async-start | bytes 4325376 | tf_op jit(solution)/shard_map/all_to_all | solution.py:531
  22.2 66.4 %all-to-all-done = bf16[8,528,256]{2,1,0:T(8,128)(2,1)S(1)} async-done(((bf16[8,528,256]{2,1,0:T(8,128)(2,1)}), bf16[8,528,256]{2,1,0:T(8,128)(2,1)S(1)}, u32[]{:S(2)}, u32[]{:S(2)}) %all-to-all-start) | async-done | bytes 2162720 | tf_op jit(solution)/shard_map/all_to_all | solution.py:531
  88.6 3.0 copy-done.7
  91.6 12.7 %encode_head.1 = bf16[2048,128]{1,0:T(8,128)(2,1)S(1)} custom-call(s32[1]{0:T(128)} %bitcast.1.ids_ref, bf16[2048,1024]{1,0:T(8,128)(2,1)S(1)} %copy-done.7, bf16[4224,256]{1,0:T(8,128)(2,1)S(1)} %bitcast.30, f32[3,8]{1,0:T(4,128)S(1)} %copy-done.8), custom_call_target="tpu_custom_call" | custom-call | flops 17179869184 | bytes 2162688 | tf_op jit(solution)/shard_map/encode_head/pallas_call | solution.py:265
  104.3 23.2 %all_to_all.22 = bf16[8,256,128]{2,1,0:T(8,128)(2,1)S(1)} all-to-all(bf16[8,256,128]{2,1,0:T(8,128)(2,1)S(1)} %bitcast.32), channel_id=1, replica_groups=mesh['groups'=2,'pos'=8,'head'=2] {'pos'}, dimensions={0} | all-to-all | bytes 1048576 | tf_op jit(solution)/shard_map/all_to_all | solution.py:533
  127.5 2.2 copy-done.1
  129.7 3.0 project_rows.1.mine_ref
  132.7 0.1 collective-permute-start
  132.8 0.9 reduce-window.6
  133.8 0.2 slice_reduce_fusion
  134.0 3.1 collective-permute-done.theirs_ref
  137.1 1.2 copy-done.5
  138.3 3.5 %norm_rows.1 = (f32[256,1024]{1,0:T(8,128)}, bf16[256,1024]{1,0:T(8,128)(2,1)}) custom-call(s32[1]{0:T(128)} %bitcast.ids_ref, f32[256,2048]{1,0:T(8,128)S(1)} %project_rows.1.mine_ref, f32[256,2048]{1,0:T(8,128)} %collective-permute-done.theirs_ref, bf16[256,2048]{1,0:T(8,128)(2,1)S(1)} %copy-done.5, f32[1,2048]{1,0:T(1,128)S(1)} %bitcast.33), custom_call_target="tpu_custom_call" | custom-call | flops 3145728 | bytes 6815744 | tf_op jit(solution)/shard_map/norm_rows/pallas_call | solution.py:343
  141.8 1.5 collective-permute-start.13
  143.3 1.4 collective-permute-start.9
  144.8 0.2 reduce-window.9
  144.9 0.1 add_bitcast_fusion
  145.0 1.7 add_convert_fusion.refs_6_
  146.7 0.7 slice.21
  147.5 0.8 collective-permute-start.5
  148.3 7.8 %collective-permute-done.13.refs_1_ = bf16[256,1024]{1,0:T(8,128)(2,1)} collective-permute-done((bf16[256,1024]{1,0:T(8,128)(2,1)}, bf16[256,1024]{1,0:T(8,128)(2,1)}, u32[]{:S(2)}, u32[]{:S(2)}) %collective-permute-start.13) | collective-permute-done | bytes 524320 | tf_op jit(solution)/shard_map/ppermute | solution.py:559
  156.1 4.4 %collective-permute-done.9.refs_0_ = bf16[256,1024]{1,0:T(8,128)(2,1)S(1)} collective-permute-done((bf16[256,1024]{1,0:T(8,128)(2,1)}, bf16[256,1024]{1,0:T(8,128)(2,1)S(1)}, u32[]{:S(2)}, u32[]{:S(2)}) %collective-permute-start.9) | collective-permute-done | bytes 524320 | tf_op jit(solution)/shard_map/ppermute | solution.py:557
  160.5 1.4 collective-permute-start.10
  161.9 0.1 select_reduce_fusion.1
  162.0 0.1 select_reduce_fusion
  162.1 0.1 copy.22.refs_9_
  162.3 0.1 collective-permute-start.11
  162.4 13.4 %collective-permute-done.5.refs_0_ = bf16[256,1024]{1,0:T(8,128)(2,1)S(1)} collective-permute-done((bf16[256,1024]{1,0:T(8,128)(2,1)}, bf16[256,1024]{1,0:T(8,128)(2,1)S(1)}, u32[]{:S(2)}, u32[]{:S(2)}) %collective-permute-start.5) | collective-permute-done | bytes 524320 | tf_op jit(solution)/shard_map/ppermute | solution.py:557
  175.8 1.4 collective-permute-start.6
  177.2 39.3 %collective-permute-done.1.refs_0_ = bf16[256,1024]{1,0:T(8,128)(2,1)S(1)} collective-permute-done((bf16[256,1024]{1,0:T(8,128)(2,1)}, bf16[256,1024]{1,0:T(8,128)(2,1)S(1)}, u32[]{:S(2)}, u32[]{:S(2)}) %collective-permute-start.1) | collective-permute-done | bytes 524320 | tf_op jit(solution)/shard_map/ppermute | solution.py:557
  216.6 0.1 collective-permute-start.7
  216.7 1.6 collective-permute-start.2
  218.3 0.2 collective-permute-start.12
  218.5 58.7 %all-gather.5.cloned.1.call-done.refs_4_.refs_5_ = bf16[2048,2048]{1,0:T(8,128)(2,1)} async-done(((bf16[128,2048]{1,0:T(8,128)(2,1)}), bf16[2048,2048]{1,0:T(8,128)(2,1)}) %all-gather.5.cloned.1.call-update) | async-done | bytes 8388624 | tf_op jit(solution)/shard_map/all_gather | solution.py:514
  277.2 12.3 %decode_rows.4 = (f32[512,1024]{1,0:T(8,128)S(1)}, f32[512,2048]{1,0:T(8,128)}) custom-call(s32[1]{0:T(128)} %bitcast.ids_ref, bf16[256,1024]{1,0:T(8,128)(2,1)} %get-tuple-element.11.refs_0_, bf16[256,1024]{1,0:T(8,128)(2,1)} %collective-permute-done.13.refs_1_, bf16[256,1024]{1,0:T(8,128)(2,1)} %collective-permute-done.14.refs_2_, ...), custom_call_target="tpu_custom_call" | custom-call | flops 8589934592 | bytes 20971520 | tf_op jit(solution)/shard_map/decode_rows/pallas_call | solution.py:459
  289.6 1.3 copy-done.9
  290.9 0.5 collective-permute-start.8
  291.4 0.1 collective-permute-start.4
  291.5 15.6 %decode_rows.5 = (f32[512,1024]{1,0:T(8,128)S(1)}, f32[512,2048]{1,0:T(8,128)}) custom-call(s32[1]{0:T(128)} %bitcast.ids_ref, bf16[256,1024]{1,0:T(8,128)(2,1)S(1)} %collective-permute-done.9.refs_0_, bf16[256,1024]{1,0:T(8,128)(2,1)} %collective-permute-done.10.refs_1_, bf16[256,1024]{1,0:T(8,128)(2,1)} %collective-permute-done.11.refs_2_, ...), custom_call_target="tpu_custom_call" | custom-call | flops 8589934592 | bytes 20971520 | tf_op jit(solution)/shard_map/decode_rows/pallas_call | solution.py:459
  307.1 1.3 copy-done.10
  308.4 15.4 %decode_rows.6 = (f32[512,1024]{1,0:T(8,128)S(1)}, f32[512,2048]{1,0:T(8,128)}) custom-call(s32[1]{0:T(128)} %bitcast.ids_ref, bf16[256,1024]{1,0:T(8,128)(2,1)S(1)} %collective-permute-done.5.refs_0_, bf16[256,1024]{1,0:T(8,128)(2,1)} %collective-permute-done.6.refs_1_, bf16[256,1024]{1,0:T(8,128)(2,1)} %collective-permute-done.7.refs_2_, ...), custom_call_target="tpu_custom_call" | custom-call | flops 8589934592 | bytes 20971520 | tf_op jit(solution)/shard_map/decode_rows/pallas_call | solution.py:459
  323.9 14.9 %decode_rows.7 = f32[512,1024]{1,0:T(8,128)} custom-call(s32[1]{0:T(128)} %bitcast.ids_ref, bf16[256,1024]{1,0:T(8,128)(2,1)S(1)} %collective-permute-done.1.refs_0_, bf16[256,1024]{1,0:T(8,128)(2,1)} %collective-permute-done.2.refs_1_, bf16[256,1024]{1,0:T(8,128)(2,1)S(1)} %collective-permute-done.3.refs_2_, ...), custom_call_target="tpu_custom_call" | custom-call | flops 8589934592 | bytes 20971520 | tf_op jit(solution)/shard_map/decode_rows/pallas_call | solution.py:459
  (52 shorter events, 0.3 us)
Async XLA Ops:
  7.2 1.0 copy-start
  7.2 3.7 %copy-start.13 = (s32[512]{0:T(512)S(1)}, s32[512]{0:T(512)}, u32[]{:S(2)}) copy-start(s32[512]{0:T(512)} %param.16) | copy-start | bytes 6148
  7.2 3.8 %copy-start.11 = (s32[512]{0:T(512)S(1)}, s32[512]{0:T(512)}, u32[]{:S(2)}) copy-start(s32[512]{0:T(512)} %param.24) | copy-start | bytes 6148
  7.2 4.0 %copy-start.3 = (bf16[512,1024]{1,0:T(8,128)(2,1)S(1)}, bf16[512,1024]{1,0:T(8,128)(2,1)}, u32[]{:S(2)}) copy-start(bf16[512,1024]{1,0:T(8,128)(2,1)} %k_ref.1) | copy-start | bytes 3145732
  7.2 4.0 %copy-start.4 = (bf16[512,1024]{1,0:T(8,128)(2,1)S(1)}, bf16[512,1024]{1,0:T(8,128)(2,1)}, u32[]{:S(2)}) copy-start(bf16[512,1024]{1,0:T(8,128)(2,1)} %v_ref.1) | copy-start | bytes 3145732
  7.2 120.3 %all-gather.3.cloned.1.call-start = ((), (), s32[]{:S(2)}) async-start(), calls=%async_computation.2 | async-start | bytes 4456448 | tf_op jit(solution)/shard_map/all_gather | solution.py:514
  9.0 268.3 %all-gather.5.cloned.1.call-start = ((), (), s32[]{:S(2)}) async-start(), calls=%async_computation.3 | async-start | bytes 8912896 | tf_op jit(solution)/shard_map/all_gather | solution.py:514
  14.7 73.8 %copy-start.8 = (f32[3,8]{1,0:T(4,128)S(1)}, f32[3,8]{1,0:T(4,128)}, u32[]{:S(2)}) copy-start(f32[3,8]{1,0:T(4,128)} %bias_ref.1) | copy-start | bytes 292
  14.7 73.8 %all-to-all-start = ((bf16[8,528,256]{2,1,0:T(8,128)(2,1)}), bf16[8,528,256]{2,1,0:T(8,128)(2,1)S(1)}, u32[]{:S(2)}, u32[]{:S(2)}) async-start(bf16[8,528,256]{2,1,0:T(8,128)(2,1)} %bitcast.3), calls=%async_computation | async-start | bytes 4325376 | tf_op jit(solution)/shard_map/all_to_all | solution.py:531
  88.6 15.7 %copy-start.2 = (bf16[8,528,256]{2,1,0:T(8,128)(2,1)}, bf16[8,528,256]{2,1,0:T(8,128)(2,1)S(1)}, u32[]{:S(2)}) copy-start(bf16[8,528,256]{2,1,0:T(8,128)(2,1)S(1)} %all-to-all-done) | copy-start | bytes 6488068
  88.6 3.0 copy-start.7
  127.5 2.2 copy-start.1
  129.7 7.4 %copy-start.6 = (f32[2048]{0:T(1024)S(1)}, f32[2048]{0:T(1024)}, u32[]{:S(2)}) copy-start(f32[2048]{0:T(1024)} %param.20) | copy-start | bytes 24580
  132.7 4.4 %collective-permute-start = (f32[256,2048]{1,0:T(8,128)S(1)}, f32[256,2048]{1,0:T(8,128)}, u32[]{:S(2)}, u32[]{:S(2)}) collective-permute-start(f32[256,2048]{1,0:T(8,128)S(1)} %project_rows.1.mine_ref), channel_id=1, source_target_pairs={{0,1},{1,0},{2,3},{3,2},{4,5},{5,4},{6,7},{7,6},{8,9},{9,8},{10,11... | collective-permute-start | bytes 6291464 | tf_op jit(solution)/shard_map/ppermute | solution.py:536
  137.1 1.2 copy-start.5
  138.3 6.7 %copy-start.12 = (bf16[3,1024]{1,0:T(4,128)(2,1)S(1)}, bf16[3,1024]{1,0:T(4,128)(2,1)}, u32[]{:S(2)}) copy-start(bf16[3,1024]{1,0:T(4,128)(2,1)} %param.25) | copy-start | bytes 18436
  141.8 20.2 %copy-start.14 = (s32[3]{0:T(128)S(1)}, s32[3]{0:T(128)}, u32[]{:S(2)}) copy-start(s32[3]{0:T(128)} %param.27) | copy-start | bytes 40
  141.8 14.3 %collective-permute-start.13 = (bf16[256,1024]{1,0:T(8,128)(2,1)}, bf16[256,1024]{1,0:T(8,128)(2,1)}, u32[]{:S(2)}, u32[]{:S(2)}) collective-permute-start(bf16[256,1024]{1,0:T(8,128)(2,1)} %get-tuple-element.11.refs_0_), channel_id=1, source_target_pairs={{0,2},{2,0},{4,6},{6,4},{8,10},{10,8},{12,14},{14,12},{1,3},{3,1},... | collective-permute-start | bytes 1572872 | tf_op jit(solution)/shard_map/ppermute | solution.py:559
  143.3 17.2 %collective-permute-start.9 = (bf16[256,1024]{1,0:T(8,128)(2,1)}, bf16[256,1024]{1,0:T(8,128)(2,1)S(1)}, u32[]{:S(2)}, u32[]{:S(2)}) collective-permute-start(bf16[256,1024]{1,0:T(8,128)(2,1)} %get-tuple-element.11.refs_0_), channel_id=1, source_target_pairs={{4,0},{6,2},{8,4},{10,6},{12,8},{14,10},{0,12},{2,14},{5,1},{7,3},... | collective-permute-start | bytes 1572872 | tf_op jit(solution)/shard_map/ppermute | solution.py:557
  147.5 14.8 %collective-permute-start.14 = (bf16[256,1024]{1,0:T(8,128)(2,1)}, bf16[256,1024]{1,0:T(8,128)(2,1)}, u32[]{:S(2)}, u32[]{:S(2)}) collective-permute-start(bf16[256,1024]{1,0:T(8,128)(2,1)} %get-tuple-element.11.refs_0_), channel_id=1, source_target_pairs={{0,1},{1,0},{2,3},{3,2},{4,5},{5,4},{6,7},{7,6},{8,9},{9,8},{10,11... | collective-permute-start | bytes 1572872 | tf_op jit(solution)/shard_map/ppermute | solution.py:560
  147.5 28.3 %collective-permute-start.5 = (bf16[256,1024]{1,0:T(8,128)(2,1)}, bf16[256,1024]{1,0:T(8,128)(2,1)S(1)}, u32[]{:S(2)}, u32[]{:S(2)}) collective-permute-start(bf16[256,1024]{1,0:T(8,128)(2,1)} %get-tuple-element.11.refs_0_), channel_id=1, source_target_pairs={{12,0},{14,2},{0,4},{2,6},{4,8},{6,10},{8,12},{10,14},{13,1},{15,3... | collective-permute-start | bytes 1572872 | tf_op jit(solution)/shard_map/ppermute | solution.py:557
  148.3 68.2 %collective-permute-start.1 = (bf16[256,1024]{1,0:T(8,128)(2,1)}, bf16[256,1024]{1,0:T(8,128)(2,1)S(1)}, u32[]{:S(2)}, u32[]{:S(2)}) collective-permute-start(bf16[256,1024]{1,0:T(8,128)(2,1)} %get-tuple-element.11.refs_0_), channel_id=1, source_target_pairs={{8,0},{10,2},{12,4},{14,6},{0,8},{2,10},{4,12},{6,14},{9,1},{11,3}... | collective-permute-start | bytes 1572872 | tf_op jit(solution)/shard_map/ppermute | solution.py:557
  156.1 60.5 %collective-permute-start.15 = (bf16[256,1024]{1,0:T(8,128)(2,1)}, bf16[256,1024]{1,0:T(8,128)(2,1)}, u32[]{:S(2)}, u32[]{:S(2)}) collective-permute-start(bf16[256,1024]{1,0:T(8,128)(2,1)} %collective-permute-done.13.refs_1_), channel_id=1, source_target_pairs={{0,1},{1,0},{2,3},{3,2},{4,5},{5,4},{6,7},{7,6},{8,9},{9,8},{10,11... | collective-permute-start | bytes 1572872 | tf_op jit(solution)/shard_map/ppermute | solution.py:560
  160.5 57.8 %collective-permute-start.10 = (bf16[256,1024]{1,0:T(8,128)(2,1)S(1)}, bf16[256,1024]{1,0:T(8,128)(2,1)}, u32[]{:S(2)}, u32[]{:S(2)}) collective-permute-start(bf16[256,1024]{1,0:T(8,128)(2,1)S(1)} %collective-permute-done.9.refs_0_), channel_id=1, source_target_pairs={{0,2},{2,0},{4,6},{6,4},{8,10},{10,8},{12,14},{14,12},{1,3},{3,1},... | collective-permute-start | bytes 1572872 | tf_op jit(solution)/shard_map/ppermute | solution.py:559
  162.3 128.6 %collective-permute-start.11 = (bf16[256,1024]{1,0:T(8,128)(2,1)S(1)}, bf16[256,1024]{1,0:T(8,128)(2,1)}, u32[]{:S(2)}, u32[]{:S(2)}) collective-permute-start(bf16[256,1024]{1,0:T(8,128)(2,1)S(1)} %collective-permute-done.9.refs_0_), channel_id=1, source_target_pairs={{0,1},{1,0},{2,3},{3,2},{4,5},{5,4},{6,7},{7,6},{8,9},{9,8},{10,11... | collective-permute-start | bytes 1572872 | tf_op jit(solution)/shard_map/ppermute | solution.py:560
  175.8 115.1 %collective-permute-start.6 = (bf16[256,1024]{1,0:T(8,128)(2,1)S(1)}, bf16[256,1024]{1,0:T(8,128)(2,1)}, u32[]{:S(2)}, u32[]{:S(2)}) collective-permute-start(bf16[256,1024]{1,0:T(8,128)(2,1)S(1)} %collective-permute-done.5.refs_0_), channel_id=1, source_target_pairs={{0,2},{2,0},{4,6},{6,4},{8,10},{10,8},{12,14},{14,12},{1,3},{3,1},... | collective-permute-start | bytes 1572872 | tf_op jit(solution)/shard_map/ppermute | solution.py:559
  216.6 91.9 %collective-permute-start.7 = (bf16[256,1024]{1,0:T(8,128)(2,1)S(1)}, bf16[256,1024]{1,0:T(8,128)(2,1)}, u32[]{:S(2)}, u32[]{:S(2)}) collective-permute-start(bf16[256,1024]{1,0:T(8,128)(2,1)S(1)} %collective-permute-done.5.refs_0_), channel_id=1, source_target_pairs={{0,1},{1,0},{2,3},{3,2},{4,5},{5,4},{6,7},{7,6},{8,9},{9,8},{10,11... | collective-permute-start | bytes 1572872 | tf_op jit(solution)/shard_map/ppermute | solution.py:560
  216.7 74.8 %collective-permute-start.2 = (bf16[256,1024]{1,0:T(8,128)(2,1)S(1)}, bf16[256,1024]{1,0:T(8,128)(2,1)}, u32[]{:S(2)}, u32[]{:S(2)}) collective-permute-start(bf16[256,1024]{1,0:T(8,128)(2,1)S(1)} %collective-permute-done.1.refs_0_), channel_id=1, source_target_pairs={{0,2},{2,0},{4,6},{6,4},{8,10},{10,8},{12,14},{14,12},{1,3},{3,1},... | collective-permute-start | bytes 1572872 | tf_op jit(solution)/shard_map/ppermute | solution.py:559
  218.3 73.2 %collective-permute-start.12 = (bf16[256,1024]{1,0:T(8,128)(2,1)}, bf16[256,1024]{1,0:T(8,128)(2,1)}, u32[]{:S(2)}, u32[]{:S(2)}) collective-permute-start(bf16[256,1024]{1,0:T(8,128)(2,1)} %collective-permute-done.10.refs_1_), channel_id=1, source_target_pairs={{0,1},{1,0},{2,3},{3,2},{4,5},{5,4},{6,7},{7,6},{8,9},{9,8},{10,11... | collective-permute-start | bytes 1572872 | tf_op jit(solution)/shard_map/ppermute | solution.py:560
  289.6 1.3 copy-start.9
  290.9 33.0 %collective-permute-start.3 = (bf16[256,1024]{1,0:T(8,128)(2,1)S(1)}, bf16[256,1024]{1,0:T(8,128)(2,1)S(1)}, u32[]{:S(2)}, u32[]{:S(2)}) collective-permute-start(bf16[256,1024]{1,0:T(8,128)(2,1)S(1)} %collective-permute-done.1.refs_0_), channel_id=1, source_target_pairs={{0,1},{1,0},{2,3},{3,2},{4,5},{5,4},{6,7},{7,6},{8,9},{9,8},{10,11... | collective-permute-start | bytes 1572872 | tf_op jit(solution)/shard_map/ppermute | solution.py:560
  290.9 17.5 %collective-permute-start.8 = (bf16[256,1024]{1,0:T(8,128)(2,1)}, bf16[256,1024]{1,0:T(8,128)(2,1)S(1)}, u32[]{:S(2)}, u32[]{:S(2)}) collective-permute-start(bf16[256,1024]{1,0:T(8,128)(2,1)} %collective-permute-done.6.refs_1_), channel_id=1, source_target_pairs={{0,1},{1,0},{2,3},{3,2},{4,5},{5,4},{6,7},{7,6},{8,9},{9,8},{10,11... | collective-permute-start | bytes 1572872 | tf_op jit(solution)/shard_map/ppermute | solution.py:560
  291.4 32.4 %collective-permute-start.4 = (bf16[256,1024]{1,0:T(8,128)(2,1)}, bf16[256,1024]{1,0:T(8,128)(2,1)S(1)}, u32[]{:S(2)}, u32[]{:S(2)}) collective-permute-start(bf16[256,1024]{1,0:T(8,128)(2,1)} %collective-permute-done.2.refs_1_), channel_id=1, source_target_pairs={{0,1},{1,0},{2,3},{3,2},{4,5},{5,4},{6,7},{7,6},{8,9},{9,8},{10,11... | collective-permute-start | bytes 1572872 | tf_op jit(solution)/shard_map/ppermute | solution.py:560
  307.1 1.3 copy-start.10
Sparse Core Ops, SparseCore 0:
  11.4 110.8 all-gather.2
  125.0 152.1 all-gather.4

commit v2 on v1

--- a/solution.py
+++ b/solution.py
@@ -217,9 +217,8 @@
     )(keys, values, extra)
 
 
-def encode_kernel(pos, tokens, ids_ref, q_ref, kv_ref, bias_ref, out_ref):
+def encode_kernel(pos, tokens, q_ref, kv_ref, bias_ref, out_ref):
     rows = q_ref.shape[0]
-    head = ids_ref[0]
     queries = q_ref[...]
     ones = jnp.ones((tokens, LANES), jnp.bfloat16)
     row_bits = kv_ref.shape[1]
@@ -235,7 +234,7 @@
         kind = jnp.concatenate([tail[r : r + 1] for r in range(tokens // row_bits)], axis=1)
         bias = jnp.zeros_like(kind)
         for m in range(bias_ref.shape[0]):
-            bias = jnp.where(kind == m, bias_ref[m, head] * LOG2E, bias)
+            bias = jnp.where(kind == m, bias_ref[m] * LOG2E, bias)
         scores = scores * EXP2_SCALE + bias
         new_top = jnp.maximum(top, jnp.max(scores, axis=1, keepdims=True))
         weights = jnp.exp2(scores - new_top).astype(jnp.bfloat16)
@@ -248,68 +247,66 @@
     out_ref[...] = (acc[:, :HEAD_DIM] / acc[:, HEAD_DIM:]).astype(jnp.bfloat16)
 
 
-def encode(head, latent_queries, kv, enc_bias, pos):
-    latents = latent_queries.shape[0]
+def encode(queries, kv, bias, pos):
+    latents = queries.shape[0]
     tokens = kv.shape[0] // pos - EXTRA
     rows = min(512, latents)
-    grid_spec = pltpu.PrefetchScalarGridSpec(
-        num_scalar_prefetch=1,
-        grid=(latents // rows,),
-        in_specs=[
-            pl.BlockSpec((rows, HEAD_DIM), lambda i, ids: (i, ids[0])),
-            whole(kv.shape),
-            pl.BlockSpec(memory_space=pltpu.SMEM),
-        ],
-        out_specs=pl.BlockSpec((rows, HEAD_DIM), lambda i, ids: (i, 0)),
-    )
+    block = pl.BlockSpec((rows, HEAD_DIM), lambda i: (i, 0))
     return pl.pallas_call(
         functools.partial(encode_kernel, pos, tokens),
-        grid_spec=grid_spec,
+        grid=(latents // rows,),
+        in_specs=[block, whole(kv.shape), pl.BlockSpec(memory_space=pltpu.SMEM)],
+        out_specs=block,
         out_shape=jax.ShapeDtypeStruct((latents, HEAD_DIM), jnp.bfloat16),
         compiler_params=params(32),
         cost_estimate=cost(
             16 * latents * tokens * pos * HEAD_DIM, 2 * kv.size, latents * tokens * pos
         ),
         name="encode_head",
-    )(head.reshape(1), latent_queries, kv, enc_bias)
-
-
-def project_kernel(heads, att_in_ref, w_ref, out_ref, att_ref):
+    )(queries, kv, bias)
+
+
+def project_kernel(heads, slots, ids_ref, att_in_ref, *refs):
+    w_refs, out_ref, att_ref = refs[:-2], refs[-2], refs[-1]
     rows = att_ref.shape[0]
-    shares, depth, _ = w_ref.shape
-
-    @pl.when(pl.program_id(0) == 0)
-    def arrange():
-        for h in range(heads):
-            att_ref[:, h * HEAD_DIM : (h + 1) * HEAD_DIM] = att_in_ref[h * rows : (h + 1) * rows, :]
-
-    total = None
-    for k in range(shares):
-        term = jnp.dot(
-            att_ref[:, k * depth : (k + 1) * depth], w_ref[k], preferred_element_type=jnp.float32
-        )
-        total = term if total is None else total + term
-    out_ref[...] = total
-
-
-def project(attended, w_all, rows, depth):
+    for h in range(heads):
+        att_ref[:, h * HEAD_DIM : (h + 1) * HEAD_DIM] = att_in_ref[h * rows : (h + 1) * rows, :]
+    depth = att_ref.shape[1] // 2
+    cols = w_refs[0].shape[1]
+    bands = [
+        w.at[r * depth : (r + 1) * depth, :] for w in w_refs for r in range(w.shape[0] // depth)
+    ]
+    halves = []
+    for k in range(2):
+        start = pl.multiple_of(ids_ref[slots + k] * depth, depth)
+        halves.append(att_ref[:, pl.ds(start, depth)])
+    for j in range(slots):
+        total = jnp.dot(halves[0], bands[j][...], preferred_element_type=jnp.float32) + jnp.dot(
+            halves[1], bands[slots + j][...], preferred_element_type=jnp.float32
+        )
+        out_ref[:, pl.ds(pl.multiple_of(ids_ref[j] * cols, cols), cols)] = total
+
+
+def project(ids, attended, weights, rows):
+    slots = ids.shape[0] - 2
     heads = attended.shape[0] // rows
-    shares, long, cols = w_all.shape
-    steps = long // depth
+    out_cols = slots * weights[0].shape[1]
+    width = heads * HEAD_DIM
+    grid_spec = pltpu.PrefetchScalarGridSpec(
+        num_scalar_prefetch=1,
+        grid=(1,),
+        in_specs=[whole(v.shape) for v in (attended, *weights)],
+        out_specs=whole((rows, out_cols)),
+        scratch_shapes=[pltpu.VMEM((rows, width), jnp.bfloat16)],
+    )
     return pl.pallas_call(
-        functools.partial(project_kernel, heads),
-        grid=(steps,),
-        in_specs=[
-            whole(attended.shape),
-            pl.BlockSpec((shares, depth, cols), lambda i: (0, i, 0)),
-        ],
-        out_specs=pl.BlockSpec((rows, cols), lambda i: (0, i)),
-        out_shape=jax.ShapeDtypeStruct((rows, steps * cols), jnp.float32),
-        scratch_shapes=[pltpu.VMEM((rows, heads * HEAD_DIM), jnp.bfloat16)],
+        functools.partial(project_kernel, heads, slots),
+        grid_spec=grid_spec,
+        out_shape=jax.ShapeDtypeStruct((rows, out_cols), jnp.float32),
         compiler_params=params(32),
-        cost_estimate=cost(2 * rows * w_all.size, 2 * w_all.size + 4 * rows * steps * cols),
+        cost_estimate=cost(2 * rows * width * out_cols, 2 * width * out_cols + 4 * rows * out_cols),
         name="project_rows",
-    )(attended, w_all)
+    )(ids, attended, *weights)
 
 
 def norm_kernel(
@@ -381,41 +378,47 @@
                     start = pl.multiple_of(k * 2 * part + which * part, part)
                     normed_ref[band, pl.ds(start, part)] = source[:, cols]
 
-    normed = normed_ref[...]
-    keys = jnp.dot(normed, wk_ref[...], preferred_element_type=jnp.float32).astype(jnp.bfloat16)
-    values = jnp.dot(normed, wv_ref[...], preferred_element_type=jnp.float32).astype(jnp.bfloat16)
-    ones = jnp.ones((keys.shape[0], LANES), jnp.bfloat16)
-    for h in range(keys.shape[1] // HEAD_DIM):
+    latents = normed_ref.shape[0]
+    chunk = min(512, latents)
+    ones = jnp.ones((chunk, LANES), jnp.bfloat16)
+    heads = q_ref.shape[1] // HEAD_DIM
+    tops = [None] * heads
+    accs = [None] * heads
+    for h in range(0 if first else heads):
+        tops[h] = old_max_ref[:, h * HEAD_DIM : h * HEAD_DIM + 1]
+        accs[h] = old_acc_ref[:, 2 * h * HEAD_DIM : 2 * (h + 1) * HEAD_DIM]
+    for start in range(0, latents, chunk):
+        normed = normed_ref[start : start + chunk, :]
+        keys = jnp.dot(normed, wk_ref[...], preferred_element_type=jnp.float32)
+        keys = keys.astype(jnp.bfloat16)
+        values = jnp.dot(normed, wv_ref[...], preferred_element_type=jnp.float32)
+        values = values.astype(jnp.bfloat16)
+        for h in range(heads):
+            cols = slice(h * HEAD_DIM, (h + 1) * HEAD_DIM)
+            scores = lax.dot_general(
+                q_ref[:, cols], keys[:, cols], NT, preferred_element_type=jnp.float32
+            )
+            scores = scores * EXP2_SCALE
+            top = jnp.max(scores, axis=1, keepdims=True)
+            if tops[h] is not None:
+                top = jnp.maximum(top, tops[h])
+            weights = jnp.exp2(scores - top).astype(jnp.bfloat16)
+            summed = jnp.dot(
+                weights,
+                jnp.concatenate([values[:, cols], ones], axis=1),
+                preferred_element_type=jnp.float32,
+            )
+            if tops[h] is not None:
+                summed = summed + accs[h] * jnp.exp2(tops[h] - top)
+            tops[h], accs[h] = top, summed
+    for h in range(heads):
         cols = slice(h * HEAD_DIM, (h + 1) * HEAD_DIM)
-        wide = slice(2 * h * HEAD_DIM, 2 * (h + 1) * HEAD_DIM)
-        scores = lax.dot_general(
-            q_ref[:, cols], keys[:, cols], NT, preferred_element_type=jnp.float32
-        )
-        scores = scores * EXP2_SCALE
-        highest = jnp.max(scores, axis=1, keepdims=True)
-        if not first:
-            old_max = old_max_ref[:, cols]
-            new_max = jnp.maximum(old_max, highest)
-            highest = new_max[:, :1]
-            fade = jnp.exp2(old_max - new_max)
-        weights = jnp.exp2(scores - highest).astype(jnp.bfloat16)
-        summed = jnp.dot(
-            weights,
-            jnp.concatenate([values[:, cols], ones], axis=1),
-            preferred_element_type=jnp.float32,
-        )
-        acc, tot = summed[:, :HEAD_DIM], summed[:, HEAD_DIM:]
-        if not first:
-            old = old_acc_ref[:, wide]
-            acc = acc + old[:, :HEAD_DIM] * fade
-            tot = tot + old[:, HEAD_DIM:] * fade
         if last:
-            out_ref[:, cols] = jnp.where(kept_ref[...] > 0.0, acc / tot, 0.0)
+            result = accs[h][:, :HEAD_DIM] / accs[h][:, HEAD_DIM:]
+            out_ref[:, cols] = jnp.where(kept_ref[...] > 0.0, result, 0.0)
         else:
-            if first:
-                new_max = jnp.broadcast_to(highest, acc.shape)
-            max_ref[:, cols] = new_max
-            acc_ref[:, wide] = jnp.concatenate([acc, tot], axis=1)
+            max_ref[:, cols] = jnp.broadcast_to(tops[h], (tops[h].shape[0], HEAD_DIM))
+            acc_ref[:, 2 * h * HEAD_DIM : 2 * (h + 1) * HEAD_DIM] = accs[h]
 
 
 def decode(place, mine, theirs, weights, queries, state, kept, shares):
@@ -508,14 +511,26 @@
     modality = jnp.arange(mods, dtype=jnp.int32)
     pair = 2 * HEAD_DIM
 
-    def share(weight):
-        depth = weight.shape[0] // groups
-        own = lax.dynamic_slice_in_dim(weight, g * depth, depth, 0)
-        return lax.all_gather(own, ("groups", "pos"), tiled=True), depth
-
-    out_all, out_depth = share(w_out)
-    out_all = out_all.reshape(groups, pos * out_depth, w_out.shape[1])
-    kv_all, kv_depth = share(jnp.concatenate([w_key, w_value], axis=1))
+    out_depth = w_out.shape[0] // 2
+    z, y, x = p // 2, p % 2, g % 2
+    own = lax.dynamic_slice_in_dim(w_out, x * out_depth, out_depth, 0)
+    column = [own] + [lax.ppermute(own, "pos", shift_perm(pos, k)) for k in range(1, far)]
+    column = jnp.concatenate(column)
+    across = lax.ppermute(column, "pos", swap_perm(pos))
+    half = jnp.concatenate([column, across])
+    out_bands = [half, lax.ppermute(half, "groups", swap_perm(groups))]
+    slot_pos = [((z + k) % far) * 2 + (y ^ j) for j in range(2) for k in range(far)]
+    out_ids = jnp.stack([*slot_pos, x, 1 - x]).astype(jnp.int32)
+
+    kv_depth = w_key.shape[0] // groups
+    kv_all = lax.all_gather(
+        jnp.concatenate(
+            [lax.dynamic_slice_in_dim(w, g * kv_depth, kv_depth, 0) for w in (w_key, w_value)],
+            axis=1,
+        ),
+        ("groups", "pos"),
+        tiled=True,
+    )
 
     q_onehot = (query_ids[:, None] == modality[None, :]).astype(jnp.int32)
     local_counts = jnp.sum(q_onehot, axis=0)
@@ -529,10 +544,12 @@
     ).astype(jnp.bfloat16)
     payload = pack(enc_keys, enc_values, extra)
     kv = lax.all_to_all(payload, "pos", 0, 0, tiled=True)
-    attended = encode(p, latent_queries, kv, enc_bias, pos)
+    head_queries = lax.dynamic_slice_in_dim(latent_queries, p * HEAD_DIM, HEAD_DIM, 1)
+    head_bias = lax.dynamic_slice_in_dim(enc_bias, p, 1, 1)[:, 0]
+    attended = encode(head_queries, kv, head_bias, pos)
     attended = lax.all_to_all(attended, "pos", 0, 0, tiled=True)
 
-    partial_value = project(attended, out_all, rows, out_depth)
+    partial_value = project(out_ids, attended, out_bands, rows)
     theirs = lax.ppermute(partial_value, "head", swap_perm(2))
     own_cols, normed = normalise(
         place, partial_value, theirs, latent_array, norm_gain[None, :], groups, kv_depth
@@ -555,11 +572,15 @@
     arrived = {0: normed}
     for k in shifts[1:]:
         arrived[k] = lax.ppermute(normed, "pos", shift_perm(pos, k))
-    for k in shifts:
-        mine = [arrived[k], lax.ppermute(arrived[k], "pos", swap_perm(pos))]
-        others = [lax.ppermute(v, "head", swap_perm(2)) for v in mine]
+    for turn in (shifts[:-1], shifts[-1:]):
+        mine, others = [], []
+        for k in turn:
+            both = [arrived[k], lax.ppermute(arrived[k], "pos", swap_perm(pos))]
+            mine += both
+            others += [lax.ppermute(v, "head", swap_perm(2)) for v in both]
+        last = turn[-1] == shifts[-1]
         state = decode(
-            place, mine, others, kv_all, queries, state, kept if k == shifts[-1] else None, groups
+            place, mine, others, kv_all, queries, state, kept if last else None, groups
         )
     return (own_cols, state)
 
@@ -571,11 +592,12 @@
         head == 2
         and pos % 2 == 0
         and pos > 2
+        and groups % 2 == 0
         and enc_keys.shape[1] == pos * HEAD_DIM
         and enc_keys.shape[0] % (2 * HEAD_DIM) == 0
         and enc_keys.shape[0] < 2048
         and w_key.shape[0] % (LANES * groups) == 0
-        and w_out.shape[0] % (LANES * groups) == 0
+        and w_out.shape[0] % (2 * LANES) == 0
         and w_out.shape[1] % LANES == 0
         and latent_array.shape[0] % LANES == 0
     )

time: 347 us -> 357 us (1.029)
  starting transfers between devices: 16.8 us -> 40.7 us
  blocking collectives: 23.2 us -> 0 us
  waiting for transfers between devices: 193 us -> 215 us
  Pallas kernels: 81 us -> 67.2 us
    ppermute x12 -> x17, waiting for transfers between devices: 7.83 us -> 172 us  [the longest x3 95.7 us: fast_on_device(): lax.ppermute(own, 'pos', shift_perm(pos, k))]
    all_to_all x1, waiting for transfers between devices: 66.4 us -> 0.01 us  [fast_on_device(): kv = lax.all_to_all(payload, 'pos', 0, 0, tiled=True)]
    all_gather x2 -> x1, waiting for transfers between devices: 58.7 us -> 0.02 us  [fast_on_device(): lax.all_gather(jnp.concatenate([lax.dynamic_slice_in_dim(w, g * kv_depth,...]
    all_to_all x1 -> x0, blocking collectives: 23.2 us -> none  [fast_on_device(): attended = lax.all_to_all(attended, 'pos', 0, 0, tiled=True)]
    ppermute x3, waiting for transfers between devices: 57.1 us -> 38.4 us  [fast_on_device(): arrived[k] = lax.ppermute(normed, 'pos', shift_perm(pos, k))]
    pallas_call x4 -> x2, Pallas kernels: 58.2 us -> 42.4 us  [decode(): pl.pallas_call(functools.partial(decode_kernel, shares, pieces, first, la...]
    ppermute x3, starting transfers between devices: 2.27 us -> 12 us  [fast_on_device(): arrived[k] = lax.ppermute(normed, 'pos', shift_perm(pos, k))]
    all_to_all x0 -> x1, starting transfers between devices: none -> 9.23 us  [fast_on_device(): attended = lax.all_to_all(attended, 'pos', 0, 0, tiled=True)]
  transfers between devices with their start and end apart: 19 -> 24, of which waited for: 7 -> 9; matrix products, arithmetic and copies ran while one was open for 2% -> 3% of each run, Pallas kernels for 19% -> 15%
where the time goes in v2:
time: 357 us; the launch traced here: 356 us
  waiting for transfers between devices  215 us (60%)
  Pallas kernels  67.2 us (19%)
  starting transfers between devices  40.7 us (11%)
  between operations  14.4 us (4%)
  local copies, waits for them, and re-layouts  12.4 us (3%)
    ppermute x3, waiting for transfers between devices, fast_on_device(): lax.ppermute(own, 'pos', shift_perm(pos, k))  95.7 us
    ppermute x1, waiting for transfers between devices, fast_on_device(): across = lax.ppermute(column, 'pos', swap_perm(pos))  45.1 us
    pallas_call x2, Pallas kernels, decode(): pl.pallas_call(functools.partial(decode_kernel, shares, pieces, first, la...  42.4 us
    ppermute x3, waiting for transfers between devices, fast_on_device(): arrived[k] = lax.ppermute(normed, 'pos', shift_perm(pos, k))  38.4 us
    ppermute x1, waiting for transfers between devices, fast_on_device(): out_bands = [half, lax.ppermute(half, 'groups', swap_perm(groups))]  18.9 us
    pallas_call x1, Pallas kernels, encode(): pl.pallas_call(functools.partial(encode_kernel, pos, tokens), grid=(laten...  14.3 us
    ppermute x4, waiting for transfers between devices, fast_on_device(): both = [arrived[k], lax.ppermute(arrived[k], 'pos', swap_perm(pos))]  12.7 us
    ppermute x3, starting transfers between devices, fast_on_device(): arrived[k] = lax.ppermute(normed, 'pos', shift_perm(pos, k))  12 us
  transfers between devices with their start and end apart: 24, of which 9 were waited for; matrix products, arithmetic and copies ran while one was open for 3% of the time, Pallas kernels for 15%

profile of v2, /device:TPU:0, one launch (start us, length us, event | category | flops | bytes accessed | tf_op | source)
XLA Modules:
  0.0 356.0 jit_solution(5241014854363258638)
XLA Ops:
  7.3 1.2 constant_dynamic-slice_fusion
  8.5 0.9 pad_maximum_fusion.1
  9.7 3.5 pack_heads.1
  13.2 7.4 %all-to-all-start = ((bf16[8,528,256]{2,1,0:T(8,128)(2,1)}), bf16[8,528,256]{2,1,0:T(8,128)(2,1)}, u32[]{:S(2)}, u32[]{:S(2)}) async-start(bf16[8,528,256]{2,1,0:T(8,128)(2,1)} %bitcast.12), calls=%async_computation | async-start | bytes 4325376 | tf_op jit(solution)/shard_map/all_to_all | solution.py:546
  20.7 2.0 collective-permute-start.2
  22.8 2.4 collective-permute-start.1
  25.1 1.5 collective-permute-start
  26.6 58.0 %collective-permute-done.2 = bf16[512,256]{1,0:T(8,128)(2,1)S(1)} collective-permute-done((bf16[512,256]{1,0:T(8,128)(2,1)S(1)}, bf16[512,256]{1,0:T(8,128)(2,1)S(1)}, u32[]{:S(2)}, u32[]{:S(2)}) %collective-permute-start.2) | collective-permute-done | bytes 262176 | tf_op jit(solution)/shard_map/ppermute | solution.py:517
  84.6 37.6 %collective-permute-done.1 = bf16[512,256]{1,0:T(8,128)(2,1)S(1)} collective-permute-done((bf16[512,256]{1,0:T(8,128)(2,1)S(1)}, bf16[512,256]{1,0:T(8,128)(2,1)S(1)}, u32[]{:S(2)}, u32[]{:S(2)}) %collective-permute-start.1) | collective-permute-done | bytes 262176 | tf_op jit(solution)/shard_map/ppermute | solution.py:517
  122.3 1.0 pad_maximum_fusion
  123.3 1.1 collective-permute-start.3
  124.4 0.2 dynamic-slice_reduce_fusion.bias_ref
  124.5 1.1 constant_dynamic-slice_fusion.3.q_ref
  125.7 45.1 %collective-permute-done.3 = bf16[2048,256]{1,0:T(8,128)(2,1)} collective-permute-done((bf16[2048,256]{1,0:T(8,128)(2,1)}, bf16[2048,256]{1,0:T(8,128)(2,1)}, u32[]{:S(2)}, u32[]{:S(2)}) %collective-permute-start.3) | collective-permute-done | bytes 1048608 | tf_op jit(solution)/shard_map/ppermute | solution.py:519
  170.8 1.3 constant_dynamic-update-slice_fusion.refs_0_
  172.1 1.6 collective-permute-start.4
  173.7 14.3 %encode_head.1 = bf16[2048,128]{1,0:T(8,128)(2,1)} custom-call(bf16[2048,128]{1,0:T(8,128)(2,1)S(1)} %constant_dynamic-slice_fusion.3.q_ref, bf16[4224,256]{1,0:T(8,128)(2,1)} %bitcast.13.kv_ref, f32[3]{0:T(128)S(1)} %dynamic-slice_reduce_fusion.bias_ref), custom_call_target="tpu_custom_call" | custom-call | flops 17179869184 | bytes 2162688 | tf_op jit(solution)/shard_map/encode_head/pallas_call | solution.py:255
  188.0 9.2 %all-to-all-start.1 = ((bf16[8,256,128]{2,1,0:T(8,128)(2,1)}), bf16[8,256,128]{2,1,0:T(8,128)(2,1)S(1)}, u32[]{:S(2)}, u32[]{:S(2)}) async-start(bf16[8,256,128]{2,1,0:T(8,128)(2,1)} %bitcast.14), calls=%async_computation.1 | async-start | bytes 1048576 | tf_op jit(solution)/shard_map/all_to_all | solution.py:550
  197.3 18.9 %collective-permute-done.4.refs_1_ = bf16[4096,256]{1,0:T(8,128)(2,1)} collective-permute-done((bf16[4096,256]{1,0:T(8,128)(2,1)S(1)}, bf16[4096,256]{1,0:T(8,128)(2,1)}, u32[]{:S(2)}, u32[]{:S(2)}) %collective-permute-start.4) | collective-permute-done | bytes 2097184 | tf_op jit(solution)/shard_map/ppermute | solution.py:521
  216.2 1.6 copy-done.2
  217.8 3.6 %project_rows.1.mine_ref = f32[256,2048]{1,0:T(8,128)S(1)} custom-call(s32[10]{0:T(128)S(1)} %stack.43.ids_ref, bf16[2048,128]{1,0:T(8,128)(2,1)S(1)} %bitcast.37, bf16[4096,256]{1,0:T(8,128)(2,1)S(1)} %copy-done.2, bf16[4096,256]{1,0:T(8,128)(2,1)} %collective-permute-done.4.refs_1_), custom_call_target="tpu_custom_call" | custom-call | flops 1073741824 | bytes 6291456 | tf_op jit(solution)/shard_map/project_rows/pallas_call | solution.py:302
  221.4 4.3 %collective-permute-done.5.theirs_ref = f32[256,2048]{1,0:T(8,128)} collective-permute-done((f32[256,2048]{1,0:T(8,128)S(1)}, f32[256,2048]{1,0:T(8,128)}, u32[]{:S(2)}, u32[]{:S(2)}) %collective-permute-start.5) | collective-permute-done | bytes 2097184 | tf_op jit(solution)/shard_map/ppermute | solution.py:553
  225.7 1.2 copy-done.6
  226.9 3.4 norm_rows.1
  230.4 8.2 %collective-permute-start.13 = (bf16[256,1024]{1,0:T(8,128)(2,1)S(1)}, bf16[256,1024]{1,0:T(8,128)(2,1)S(1)}, u32[]{:S(2)}, u32[]{:S(2)}) collective-permute-start(bf16[256,1024]{1,0:T(8,128)(2,1)S(1)} %get-tuple-element.7.refs_0_), channel_id=1, source_target_pairs={{12,0},{14,2},{0,4},{2,6},{4,8},{6,10},{8,12},{10,14},{13,1},{15,3... | collective-permute-start | bytes 1572872 | tf_op jit(solution)/shard_map/ppermute | solution.py:574
  238.6 3.5 collective-permute-start.11
  242.0 0.9 reduce-window.6
  242.9 0.2 slice_reduce_fusion
  243.1 0.6 collective-permute-start.10
  243.7 0.3 collective-permute-start.6
  244.1 10.4 %collective-permute-done.13.refs_4_ = bf16[256,1024]{1,0:T(8,128)(2,1)S(1)} collective-permute-done((bf16[256,1024]{1,0:T(8,128)(2,1)S(1)}, bf16[256,1024]{1,0:T(8,128)(2,1)S(1)}, u32[]{:S(2)}, u32[]{:S(2)}) %collective-permute-start.13) | collective-permute-done | bytes 524320 | tf_op jit(solution)/shard_map/ppermute | solution.py:574
  254.5 0.6 collective-permute-start.14
  255.1 9.1 %collective-permute-done.11.refs_2_ = bf16[256,1024]{1,0:T(8,128)(2,1)} collective-permute-done((bf16[256,1024]{1,0:T(8,128)(2,1)S(1)}, bf16[256,1024]{1,0:T(8,128)(2,1)}, u32[]{:S(2)}, u32[]{:S(2)}) %collective-permute-start.11) | collective-permute-done | bytes 524320 | tf_op jit(solution)/shard_map/ppermute | solution.py:574
  264.2 0.8 collective-permute-start.12
  265.0 0.2 reduce-window.9
  265.3 2.7 add_convert_fusion.refs_14_.refs_6_
  268.0 0.7 slice.21
  268.8 18.9 %collective-permute-done.6.refs_0_ = bf16[256,1024]{1,0:T(8,128)(2,1)S(1)} collective-permute-done((bf16[256,1024]{1,0:T(8,128)(2,1)S(1)}, bf16[256,1024]{1,0:T(8,128)(2,1)S(1)}, u32[]{:S(2)}, u32[]{:S(2)}) %collective-permute-start.6) | collective-permute-done | bytes 524320 | tf_op jit(solution)/shard_map/ppermute | solution.py:574
  287.8 0.8 copy-done.10
  288.6 0.5 collective-permute-start.7
  289.3 0.3 collective-permute-start.18
  290.0 0.2 collective-permute-start.8
  290.3 12.7 %collective-permute-done.7.refs_1_ = bf16[256,1024]{1,0:T(8,128)(2,1)} collective-permute-done((bf16[256,1024]{1,0:T(8,128)(2,1)S(1)}, bf16[256,1024]{1,0:T(8,128)(2,1)}, u32[]{:S(2)}, u32[]{:S(2)}) %collective-permute-start.7) | collective-permute-done | bytes 524320 | tf_op jit(solution)/shard_map/ppermute | solution.py:578
  303.0 1.0 copy-done.9
  304.1 1.0 copy-done.11
  305.1 27.3 %decode_rows.2 = (f32[512,1024]{1,0:T(8,128)}, f32[512,2048]{1,0:T(8,128)}) custom-call(s32[1]{0:T(128)} %bitcast.ids_ref, bf16[256,1024]{1,0:T(8,128)(2,1)S(1)} %get-tuple-element.7.refs_0_, bf16[256,1024]{1,0:T(8,128)(2,1)} %collective-permute-done.10.refs_1_, bf16[256,1024]{1,0:T(8,128)(2,1)} %collective-permute-done.11.refs_2_, ...), custom_call_target="tpu_custom_call" | custom-call | flops 25769803776 | bytes 20971520 | tf_op jit(solution)/shard_map/decode_rows/pallas_call | solution.py:462
  332.4 1.6 copy-done.12
  334.0 15.1 %decode_rows.3 = f32[512,1024]{1,0:T(8,128)} custom-call(s32[1]{0:T(128)} %bitcast.ids_ref, bf16[256,1024]{1,0:T(8,128)(2,1)S(1)} %collective-permute-done.6.refs_0_, bf16[256,1024]{1,0:T(8,128)(2,1)} %collective-permute-done.7.refs_1_, bf16[256,1024]{1,0:T(8,128)(2,1)} %collective-permute-done.8.refs_2_, bf16[256,1024]{1,0:T(8,128)(2,1)} %collective-permute-done.9.refs_3_, ...), custom_call_target="tpu_custom_call" | custom-call | flops 8589934592 | bytes 20971520 | tf_op jit(solution)/shard_map/decode_rows/pallas_call | solution.py:462
  (73 shorter events, 1.4 us)
Async XLA Ops:
  7.2 258.1 %copy-start = (bf16[3,1024]{1,0:T(4,128)(2,1)S(1)}, bf16[3,1024]{1,0:T(4,128)(2,1)}, u32[]{:S(2)}) copy-start(bf16[3,1024]{1,0:T(4,128)(2,1)} %param.25) | copy-start | bytes 18436
  7.2 2.2 copy-start.15
  7.2 2.3 copy-start.14
  7.2 2.5 copy-start.5
  7.2 2.5 copy-start.4
  7.2 295.8 %all-gather.2.cloned.1.call-start = ((), (), s32[]{:S(2)}) async-start(), calls=%async_computation.2 | async-start | bytes 8912896 | tf_op jit(solution)/shard_map/all_gather | solution.py:526
  13.2 7.4 %copy-start.13 = (bf16[1024,256]{1,0:T(8,128)(2,1)S(1)}, bf16[1024,256]{1,0:T(8,128)(2,1)}, u32[]{:S(2)}) copy-start(bf16[1024,256]{1,0:T(8,128)(2,1)} %param.19) | copy-start | bytes 1572868
  13.2 160.5 %all-to-all-start = ((bf16[8,528,256]{2,1,0:T(8,128)(2,1)}), bf16[8,528,256]{2,1,0:T(8,128)(2,1)}, u32[]{:S(2)}, u32[]{:S(2)}) async-start(bf16[8,528,256]{2,1,0:T(8,128)(2,1)} %bitcast.12), calls=%async_computation | async-start | bytes 4325376 | tf_op jit(solution)/shard_map/all_to_all | solution.py:546
  20.6 103.7 %copy-start.16 = (f32[3,8]{1,0:T(4,128)S(1)}, f32[3,8]{1,0:T(4,128)}, u32[]{:S(2)}) copy-start(f32[3,8]{1,0:T(4,128)} %param.26) | copy-start | bytes 292
  20.7 63.9 %collective-permute-start.2 = (bf16[512,256]{1,0:T(8,128)(2,1)S(1)}, bf16[512,256]{1,0:T(8,128)(2,1)S(1)}, u32[]{:S(2)}, u32[]{:S(2)}) collective-permute-start(bf16[512,256]{1,0:T(8,128)(2,1)S(1)} %get-tuple-element.13), channel_id=1, source_target_pairs={{12,0},{14,2},{0,4},{2,6},{4,8},{6,10},{8,12},{10,14},{13,1},{15,3... | collective-permute-start | bytes 786440 | tf_op jit(solution)/shard_map/ppermute | solution.py:517
  22.8 99.5 %collective-permute-start.1 = (bf16[512,256]{1,0:T(8,128)(2,1)S(1)}, bf16[512,256]{1,0:T(8,128)(2,1)S(1)}, u32[]{:S(2)}, u32[]{:S(2)}) collective-permute-start(bf16[512,256]{1,0:T(8,128)(2,1)S(1)} %get-tuple-element.13), channel_id=1, source_target_pairs={{8,0},{10,2},{12,4},{14,6},{0,8},{2,10},{4,12},{6,14},{9,1},{11,3}... | collective-permute-start | bytes 786440 | tf_op jit(solution)/shard_map/ppermute | solution.py:517
  25.1 97.1 %collective-permute-start = (bf16[512,256]{1,0:T(8,128)(2,1)S(1)}, bf16[512,256]{1,0:T(8,128)(2,1)S(1)}, u32[]{:S(2)}, u32[]{:S(2)}) collective-permute-start(bf16[512,256]{1,0:T(8,128)(2,1)S(1)} %get-tuple-element.13), channel_id=1, source_target_pairs={{4,0},{6,2},{8,4},{10,6},{12,8},{14,10},{0,12},{2,14},{5,1},{7,3},... | collective-permute-start | bytes 786440 | tf_op jit(solution)/shard_map/ppermute | solution.py:517
  123.3 47.5 %collective-permute-start.3 = (bf16[2048,256]{1,0:T(8,128)(2,1)}, bf16[2048,256]{1,0:T(8,128)(2,1)}, u32[]{:S(2)}, u32[]{:S(2)}) collective-permute-start(bf16[2048,256]{1,0:T(8,128)(2,1)} %pad_maximum_fusion), channel_id=1, source_target_pairs={{0,2},{2,0},{4,6},{6,4},{8,10},{10,8},{12,14},{14,12},{1,3},{3,1},... | collective-permute-start | bytes 3145736 | tf_op jit(solution)/shard_map/ppermute | solution.py:519
  172.1 15.9 %copy-start.1 = (bf16[4096,256]{1,0:T(8,128)(2,1)}, bf16[4096,256]{1,0:T(8,128)(2,1)S(1)}, u32[]{:S(2)}) copy-start(bf16[4096,256]{1,0:T(8,128)(2,1)S(1)} %constant_dynamic-update-slice_fusion.refs_0_) | copy-start | bytes 6291460
  172.1 44.0 %collective-permute-start.4 = (bf16[4096,256]{1,0:T(8,128)(2,1)S(1)}, bf16[4096,256]{1,0:T(8,128)(2,1)}, u32[]{:S(2)}, u32[]{:S(2)}) collective-permute-start(bf16[4096,256]{1,0:T(8,128)(2,1)S(1)} %constant_dynamic-update-slice_fusion.refs_0_), channel_id=1, source_target_pairs={{0,16},{16,0},{1,17},{17,1},{2,18},{18,2},{3,19},{19,3},{4,20},{20... | collective-permute-start | bytes 6291464 | tf_op jit(solution)/shard_map/ppermute | solution.py:521
  188.0 28.2 %all-to-all-start.1 = ((bf16[8,256,128]{2,1,0:T(8,128)(2,1)}), bf16[8,256,128]{2,1,0:T(8,128)(2,1)S(1)}, u32[]{:S(2)}, u32[]{:S(2)}) async-start(bf16[8,256,128]{2,1,0:T(8,128)(2,1)} %bitcast.14), calls=%async_computation.1 | async-start | bytes 1048576 | tf_op jit(solution)/shard_map/all_to_all | solution.py:550
  216.2 1.6 copy-start.2
  217.7 8.0 %copy-start.7 = (f32[2048]{0:T(1024)S(1)}, f32[2048]{0:T(1024)}, u32[]{:S(2)}) copy-start(f32[2048]{0:T(1024)} %param.20) | copy-start | bytes 24580
  221.4 4.4 %collective-permute-start.5 = (f32[256,2048]{1,0:T(8,128)S(1)}, f32[256,2048]{1,0:T(8,128)}, u32[]{:S(2)}, u32[]{:S(2)}) collective-permute-start(f32[256,2048]{1,0:T(8,128)S(1)} %project_rows.1.mine_ref), channel_id=1, source_target_pairs={{0,1},{1,0},{2,3},{3,2},{4,5},{5,4},{6,7},{7,6},{8,9},{9,8},{10,11... | collective-permute-start | bytes 6291464 | tf_op jit(solution)/shard_map/ppermute | solution.py:553
  225.7 1.2 copy-start.6
  230.4 59.4 %copy-start.17 = (s32[3]{0:T(128)S(1)}, s32[3]{0:T(128)}, u32[]{:S(2)}) copy-start(s32[3]{0:T(128)} %param.27) | copy-start | bytes 40
  230.4 24.2 %collective-permute-start.13 = (bf16[256,1024]{1,0:T(8,128)(2,1)S(1)}, bf16[256,1024]{1,0:T(8,128)(2,1)S(1)}, u32[]{:S(2)}, u32[]{:S(2)}) collective-permute-start(bf16[256,1024]{1,0:T(8,128)(2,1)S(1)} %get-tuple-element.7.refs_0_), channel_id=1, source_target_pairs={{12,0},{14,2},{0,4},{2,6},{4,8},{6,10},{8,12},{10,14},{13,1},{15,3... | collective-permute-start | bytes 1572872 | tf_op jit(solution)/shard_map/ppermute | solution.py:574
  238.6 16.0 %collective-permute-start.15 = (bf16[256,1024]{1,0:T(8,128)(2,1)S(1)}, bf16[256,1024]{1,0:T(8,128)(2,1)S(1)}, u32[]{:S(2)}, u32[]{:S(2)}) collective-permute-start(bf16[256,1024]{1,0:T(8,128)(2,1)S(1)} %get-tuple-element.7.refs_0_), channel_id=1, source_target_pairs={{0,1},{1,0},{2,3},{3,2},{4,5},{5,4},{6,7},{7,6},{8,9},{9,8},{10,11... | collective-permute-start | bytes 1572872 | tf_op jit(solution)/shard_map/ppermute | solution.py:580
  238.6 25.7 %collective-permute-start.11 = (bf16[256,1024]{1,0:T(8,128)(2,1)S(1)}, bf16[256,1024]{1,0:T(8,128)(2,1)}, u32[]{:S(2)}, u32[]{:S(2)}) collective-permute-start(bf16[256,1024]{1,0:T(8,128)(2,1)S(1)} %get-tuple-element.7.refs_0_), channel_id=1, source_target_pairs={{4,0},{6,2},{8,4},{10,6},{12,8},{14,10},{0,12},{2,14},{5,1},{7,3},... | collective-permute-start | bytes 1572872 | tf_op jit(solution)/shard_map/ppermute | solution.py:574
  243.1 25.6 %collective-permute-start.10 = (bf16[256,1024]{1,0:T(8,128)(2,1)S(1)}, bf16[256,1024]{1,0:T(8,128)(2,1)}, u32[]{:S(2)}, u32[]{:S(2)}) collective-permute-start(bf16[256,1024]{1,0:T(8,128)(2,1)S(1)} %get-tuple-element.7.refs_0_), channel_id=1, source_target_pairs={{0,2},{2,0},{4,6},{6,4},{8,10},{10,8},{12,14},{14,12},{1,3},{3,1},... | collective-permute-start | bytes 1572872 | tf_op jit(solution)/shard_map/ppermute | solution.py:578
  243.7 44.0 %collective-permute-start.6 = (bf16[256,1024]{1,0:T(8,128)(2,1)S(1)}, bf16[256,1024]{1,0:T(8,128)(2,1)S(1)}, u32[]{:S(2)}, u32[]{:S(2)}) collective-permute-start(bf16[256,1024]{1,0:T(8,128)(2,1)S(1)} %get-tuple-element.7.refs_0_), channel_id=1, source_target_pairs={{8,0},{10,2},{12,4},{14,6},{0,8},{2,10},{4,12},{6,14},{9,1},{11,3}... | collective-permute-start | bytes 1572872 | tf_op jit(solution)/shard_map/ppermute | solution.py:574
  254.5 33.2 %collective-permute-start.19 = (bf16[256,1024]{1,0:T(8,128)(2,1)S(1)}, bf16[256,1024]{1,0:T(8,128)(2,1)S(1)}, u32[]{:S(2)}, u32[]{:S(2)}) collective-permute-start(bf16[256,1024]{1,0:T(8,128)(2,1)S(1)} %collective-permute-done.13.refs_4_), channel_id=1, source_target_pairs={{0,1},{1,0},{2,3},{3,2},{4,5},{5,4},{6,7},{7,6},{8,9},{9,8},{10,11... | collective-permute-start | bytes 1572872 | tf_op jit(solution)/shard_map/ppermute | solution.py:580
  254.5 35.3 %copy-start.8 = (bf16[256,1024]{1,0:T(8,128)(2,1)}, bf16[256,1024]{1,0:T(8,128)(2,1)S(1)}, u32[]{:S(2)}) copy-start(bf16[256,1024]{1,0:T(8,128)(2,1)S(1)} %collective-permute-done.15.refs_6_) | copy-start | bytes 1572868
  254.5 34.6 %collective-permute-start.14 = (bf16[256,1024]{1,0:T(8,128)(2,1)S(1)}, bf16[256,1024]{1,0:T(8,128)(2,1)}, u32[]{:S(2)}, u32[]{:S(2)}) collective-permute-start(bf16[256,1024]{1,0:T(8,128)(2,1)S(1)} %collective-permute-done.13.refs_4_), channel_id=1, source_target_pairs={{0,2},{2,0},{4,6},{6,4},{8,10},{10,8},{12,14},{14,12},{1,3},{3,1},... | collective-permute-start | bytes 1572872 | tf_op jit(solution)/shard_map/ppermute | solution.py:578
  264.2 25.1 %collective-permute-start.12 = (bf16[256,1024]{1,0:T(8,128)(2,1)}, bf16[256,1024]{1,0:T(8,128)(2,1)}, u32[]{:S(2)}, u32[]{:S(2)}) collective-permute-start(bf16[256,1024]{1,0:T(8,128)(2,1)} %collective-permute-done.11.refs_2_), channel_id=1, source_target_pairs={{0,2},{2,0},{4,6},{6,4},{8,10},{10,8},{12,14},{14,12},{1,3},{3,1},... | collective-permute-start | bytes 1572872 | tf_op jit(solution)/shard_map/ppermute | solution.py:578
  268.7 21.3 %collective-permute-start.17 = (bf16[256,1024]{1,0:T(8,128)(2,1)}, bf16[256,1024]{1,0:T(8,128)(2,1)}, u32[]{:S(2)}, u32[]{:S(2)}) collective-permute-start(bf16[256,1024]{1,0:T(8,128)(2,1)} %collective-permute-done.11.refs_2_), channel_id=1, source_target_pairs={{0,1},{1,0},{2,3},{3,2},{4,5},{5,4},{6,7},{7,6},{8,9},{9,8},{10,11... | collective-permute-start | bytes 1572872 | tf_op jit(solution)/shard_map/ppermute | solution.py:580
  287.7 15.3 %collective-permute-start.16 = (bf16[256,1024]{1,0:T(8,128)(2,1)}, bf16[256,1024]{1,0:T(8,128)(2,1)}, u32[]{:S(2)}, u32[]{:S(2)}) collective-permute-start(bf16[256,1024]{1,0:T(8,128)(2,1)} %collective-permute-done.10.refs_1_), channel_id=1, source_target_pairs={{0,1},{1,0},{2,3},{3,2},{4,5},{5,4},{6,7},{7,6},{8,9},{9,8},{10,11... | collective-permute-start | bytes 1572872 | tf_op jit(solution)/shard_map/ppermute | solution.py:580
  287.8 0.8 copy-start.10
  288.6 14.4 %collective-permute-start.7 = (bf16[256,1024]{1,0:T(8,128)(2,1)S(1)}, bf16[256,1024]{1,0:T(8,128)(2,1)}, u32[]{:S(2)}, u32[]{:S(2)}) collective-permute-start(bf16[256,1024]{1,0:T(8,128)(2,1)S(1)} %collective-permute-done.6.refs_0_), channel_id=1, source_target_pairs={{0,2},{2,0},{4,6},{6,4},{8,10},{10,8},{12,14},{14,12},{1,3},{3,1},... | collective-permute-start | bytes 1572872 | tf_op jit(solution)/shard_map/ppermute | solution.py:578
  289.1 13.9 %collective-permute-start.20 = (bf16[256,1024]{1,0:T(8,128)(2,1)}, bf16[256,1024]{1,0:T(8,128)(2,1)}, u32[]{:S(2)}, u32[]{:S(2)}) collective-permute-start(bf16[256,1024]{1,0:T(8,128)(2,1)} %collective-permute-done.14.refs_5_), channel_id=1, source_target_pairs={{0,1},{1,0},{2,3},{3,2},{4,5},{5,4},{6,7},{7,6},{8,9},{9,8},{10,11... | collective-permute-start | bytes 1572872 | tf_op jit(solution)/shard_map/ppermute | solution.py:580
  289.3 13.7 %collective-permute-start.18 = (bf16[256,1024]{1,0:T(8,128)(2,1)}, bf16[256,1024]{1,0:T(8,128)(2,1)}, u32[]{:S(2)}, u32[]{:S(2)}) collective-permute-start(bf16[256,1024]{1,0:T(8,128)(2,1)} %collective-permute-done.12.refs_3_), channel_id=1, source_target_pairs={{0,1},{1,0},{2,3},{3,2},{4,5},{5,4},{6,7},{7,6},{8,9},{9,8},{10,11... | collective-permute-start | bytes 1572872 | tf_op jit(solution)/shard_map/ppermute | solution.py:580
  290.0 42.4 %copy-start.3 = (bf16[512,1024]{1,0:T(8,128)(2,1)S(1)}, bf16[512,1024]{1,0:T(8,128)(2,1)}, u32[]{:S(2)}) copy-start(bf16[512,1024]{1,0:T(8,128)(2,1)} %add_convert_fusion.refs_14_.refs_6_) | copy-start | bytes 3145732
  290.0 42.4 %collective-permute-start.8 = (bf16[256,1024]{1,0:T(8,128)(2,1)S(1)}, bf16[256,1024]{1,0:T(8,128)(2,1)}, u32[]{:S(2)}, u32[]{:S(2)}) collective-permute-start(bf16[256,1024]{1,0:T(8,128)(2,1)S(1)} %collective-permute-done.6.refs_0_), channel_id=1, source_target_pairs={{0,1},{1,0},{2,3},{3,2},{4,5},{5,4},{6,7},{7,6},{8,9},{9,8},{10,11... | collective-permute-start | bytes 1572872 | tf_op jit(solution)/shard_map/ppermute | solution.py:580
  303.0 29.4 %collective-permute-start.9 = (bf16[256,1024]{1,0:T(8,128)(2,1)}, bf16[256,1024]{1,0:T(8,128)(2,1)}, u32[]{:S(2)}, u32[]{:S(2)}) collective-permute-start(bf16[256,1024]{1,0:T(8,128)(2,1)} %collective-permute-done.7.refs_1_), channel_id=1, source_target_pairs={{0,1},{1,0},{2,3},{3,2},{4,5},{5,4},{6,7},{7,6},{8,9},{9,8},{10,11... | collective-permute-start | bytes 1572872 | tf_op jit(solution)/shard_map/ppermute | solution.py:580
  303.0 1.0 copy-start.9
  304.1 1.0 copy-start.11
  332.4 1.6 copy-start.12
Sparse Core Ops, SparseCore 0:
  10.8 180.4 all-gather.1

commit v3 on v1

--- a/solution.py
+++ b/solution.py
@@ -217,9 +217,8 @@
     )(keys, values, extra)
 
 
-def encode_kernel(pos, tokens, ids_ref, q_ref, kv_ref, bias_ref, out_ref):
+def encode_kernel(pos, tokens, q_ref, kv_ref, bias_ref, out_ref):
     rows = q_ref.shape[0]
-    head = ids_ref[0]
     queries = q_ref[...]
     ones = jnp.ones((tokens, LANES), jnp.bfloat16)
     row_bits = kv_ref.shape[1]
@@ -235,7 +234,7 @@
         kind = jnp.concatenate([tail[r : r + 1] for r in range(tokens // row_bits)], axis=1)
         bias = jnp.zeros_like(kind)
         for m in range(bias_ref.shape[0]):
-            bias = jnp.where(kind == m, bias_ref[m, head] * LOG2E, bias)
+            bias = jnp.where(kind == m, bias_ref[m] * LOG2E, bias)
         scores = scores * EXP2_SCALE + bias
         new_top = jnp.maximum(top, jnp.max(scores, axis=1, keepdims=True))
         weights = jnp.exp2(scores - new_top).astype(jnp.bfloat16)
@@ -248,30 +247,23 @@
     out_ref[...] = (acc[:, :HEAD_DIM] / acc[:, HEAD_DIM:]).astype(jnp.bfloat16)
 
 
-def encode(head, latent_queries, kv, enc_bias, pos):
-    latents = latent_queries.shape[0]
+def encode(queries, kv, bias, pos):
+    latents = queries.shape[0]
     tokens = kv.shape[0] // pos - EXTRA
     rows = min(512, latents)
-    grid_spec = pltpu.PrefetchScalarGridSpec(
-        num_scalar_prefetch=1,
-        grid=(latents // rows,),
-        in_specs=[
-            pl.BlockSpec((rows, HEAD_DIM), lambda i, ids: (i, ids[0])),
-            whole(kv.shape),
-            pl.BlockSpec(memory_space=pltpu.SMEM),
-        ],
-        out_specs=pl.BlockSpec((rows, HEAD_DIM), lambda i, ids: (i, 0)),
-    )
+    block = pl.BlockSpec((rows, HEAD_DIM), lambda i: (i, 0))
     return pl.pallas_call(
         functools.partial(encode_kernel, pos, tokens),
-        grid_spec=grid_spec,
+        grid=(latents // rows,),
+        in_specs=[block, whole(kv.shape), pl.BlockSpec(memory_space=pltpu.SMEM)],
+        out_specs=block,
         out_shape=jax.ShapeDtypeStruct((latents, HEAD_DIM), jnp.bfloat16),
         compiler_params=params(32),
         cost_estimate=cost(
             16 * latents * tokens * pos * HEAD_DIM, 2 * kv.size, latents * tokens * pos
         ),
         name="encode_head",
-    )(head.reshape(1), latent_queries, kv, enc_bias)
+    )(queries, kv, bias)
 
 
 def project_kernel(heads, att_in_ref, w_ref, out_ref, att_ref):
@@ -313,7 +305,7 @@
 
 
 def norm_kernel(
-    shares, band, ids_ref, mine_ref, theirs_ref, latent_ref, gain_ref, out_ref, normed_ref, full_ref
+    ids_ref, mine_ref, theirs_ref, latent_ref, gain_ref, out_ref, normed_ref, other_ref, full_ref
 ):
     updated = latent_ref[...].astype(jnp.float32) + (mine_ref[...] + theirs_ref[...])
     mean_square = jnp.mean(updated * updated, axis=1, keepdims=True)
@@ -321,30 +313,27 @@
     half = out_ref.shape[1]
     own = full_ref[:, pl.ds(pl.multiple_of(ids_ref[0] * half, half), half)]
     out_ref[...] = own
-    normed = own.astype(jnp.bfloat16)
-    count = half // (shares * band)
-    for i in range(count):
-        for k in range(shares):
-            source = (i * shares + k) * band
-            target = (k * count + i) * band
-            normed_ref[:, target : target + band] = normed[:, source : source + band]
-
-
-def normalise(place, mine, theirs, latent_array, gain, shares, band):
+    normed_ref[...] = own.astype(jnp.bfloat16)
+    other = full_ref[:, pl.ds(pl.multiple_of((1 - ids_ref[0]) * half, half), half)]
+    other_ref[...] = other.astype(jnp.bfloat16)
+
+
+def normalise(place, mine, theirs, latent_array, gain):
     rows, width = mine.shape
     half = width // 2
     grid_spec = pltpu.PrefetchScalarGridSpec(
         num_scalar_prefetch=1,
         grid=(1,),
         in_specs=[whole((rows, width))] * 3 + [whole((1, width))],
-        out_specs=[whole((rows, half))] * 2,
+        out_specs=[whole((rows, half))] * 3,
         scratch_shapes=[pltpu.VMEM((rows, width), jnp.float32)],
     )
     return pl.pallas_call(
-        functools.partial(norm_kernel, shares, band),
+        norm_kernel,
         grid_spec=grid_spec,
         out_shape=[
             jax.ShapeDtypeStruct((rows, half), jnp.float32),
+            jax.ShapeDtypeStruct((rows, half), jnp.bfloat16),
             jax.ShapeDtypeStruct((rows, half), jnp.bfloat16),
         ],
         compiler_params=params(32),
@@ -353,121 +342,136 @@
     )(place.reshape(1), mine, theirs, latent_array, gain)
 
 
-def decode_kernel(shares, pieces, first, last, ids_ref, *refs):
-    mine = refs[:pieces]
-    theirs = refs[pieces : 2 * pieces]
-    wk_ref, wv_ref, q_ref = refs[2 * pieces : 2 * pieces + 3]
-    rest = list(refs[2 * pieces + 3 :])
+def latents_kernel(pieces, ids_ref, *refs):
+    mine, theirs = refs[:pieces], refs[pieces : 2 * pieces]
+    w_ref, out_ref, normed_ref = refs[2 * pieces :]
+    rows, half = mine[0].shape
+    slots = ids_ref.shape[0] - 1
+    depth = 2 * half // slots
+
+    @pl.when(pl.program_id(0) == 0)
+    def arrange():
+        for j in range(slots):
+            at = ids_ref[1 + j]
+            is_mine = at // (slots // 2) == ids_ref[0]
+            start = pl.multiple_of((at % (slots // 2)) * depth, depth)
+            for r in range(pieces):
+                both = [v[r][:, pl.ds(start, depth)] for v in (mine, theirs)]
+                normed_ref[r * rows : (r + 1) * rows, j * depth : (j + 1) * depth] = jnp.where(
+                    is_mine, both[0], both[1]
+                )
+
+    out_ref[...] = jnp.dot(
+        normed_ref[...], w_ref[...], preferred_element_type=jnp.float32
+    ).astype(jnp.bfloat16)
+
+
+def latent_keys_values(ids, mine, theirs, weights):
+    pieces = len(mine)
+    rows, half = mine[0].shape
+    depth, width = weights.shape
+    block = min(512, width)
+    grid_spec = pltpu.PrefetchScalarGridSpec(
+        num_scalar_prefetch=1,
+        grid=(width // block,),
+        in_specs=[whole((rows, half))] * (2 * pieces)
+        + [pl.BlockSpec((depth, block), lambda i, ids: (0, i))],
+        out_specs=pl.BlockSpec((rows * pieces, block), lambda i, ids: (0, i)),
+        scratch_shapes=[pltpu.VMEM((rows * pieces, depth), jnp.bfloat16)],
+    )
+    return pl.pallas_call(
+        functools.partial(latents_kernel, pieces),
+        grid_spec=grid_spec,
+        out_shape=jax.ShapeDtypeStruct((rows * pieces, width), jnp.bfloat16),
+        compiler_params=params(40),
+        cost_estimate=cost(2 * rows * pieces * depth * width, 2 * depth * width),
+        name="latent_keys_values",
+    )(ids, *mine, *theirs, weights)
+
+
+def decode_kernel(first, last, *refs):
+    q_ref, k_ref, v_ref = refs[:3]
+    rest = refs[3:]
     if not first:
         old_max_ref, old_acc_ref = rest[:2]
         rest = rest[2:]
-    if last:
-        kept_ref, out_ref = rest[:2]
-        rest = rest[2:]
-    else:
-        max_ref, acc_ref = rest[:2]
-        rest = rest[2:]
-    (normed_ref,) = rest
-    rows, half = mine[0].shape
-    part = half // shares
-
-    @pl.when(pl.program_id(0) == 0)
-    def arrange():
-        for r in range(pieces):
-            band = slice(r * rows, (r + 1) * rows)
-            for k in range(shares):
-                cols = slice(k * part, (k + 1) * part)
-                for source, which in ((mine[r], ids_ref[0]), (theirs[r], 1 - ids_ref[0])):
-                    start = pl.multiple_of(k * 2 * part + which * part, part)
-                    normed_ref[band, pl.ds(start, part)] = source[:, cols]
-
-    normed = normed_ref[...]
-    keys = jnp.dot(normed, wk_ref[...], preferred_element_type=jnp.float32).astype(jnp.bfloat16)
-    values = jnp.dot(normed, wv_ref[...], preferred_element_type=jnp.float32).astype(jnp.bfloat16)
-    ones = jnp.ones((keys.shape[0], LANES), jnp.bfloat16)
-    for h in range(keys.shape[1] // HEAD_DIM):
+    latents = k_ref.shape[0]
+    chunk = min(512, latents)
+    ones = jnp.ones((chunk, LANES), jnp.bfloat16)
+    for h in range(q_ref.shape[1] // HEAD_DIM):
         cols = slice(h * HEAD_DIM, (h + 1) * HEAD_DIM)
         wide = slice(2 * h * HEAD_DIM, 2 * (h + 1) * HEAD_DIM)
-        scores = lax.dot_general(
-            q_ref[:, cols], keys[:, cols], NT, preferred_element_type=jnp.float32
-        )
-        scores = scores * EXP2_SCALE
-        highest = jnp.max(scores, axis=1, keepdims=True)
-        if not first:
-            old_max = old_max_ref[:, cols]
-            new_max = jnp.maximum(old_max, highest)
-            highest = new_max[:, :1]
-            fade = jnp.exp2(old_max - new_max)
-        weights = jnp.exp2(scores - highest).astype(jnp.bfloat16)
-        summed = jnp.dot(
-            weights,
-            jnp.concatenate([values[:, cols], ones], axis=1),
-            preferred_element_type=jnp.float32,
-        )
-        acc, tot = summed[:, :HEAD_DIM], summed[:, HEAD_DIM:]
-        if not first:
-            old = old_acc_ref[:, wide]
-            acc = acc + old[:, :HEAD_DIM] * fade
-            tot = tot + old[:, HEAD_DIM:] * fade
+        if first:
+            top, acc = None, None
+        else:
+            top, acc = old_max_ref[:, cols][:, :1], old_acc_ref[:, wide]
+        for start in range(0, latents, chunk):
+            band = slice(start, start + chunk)
+            scores = lax.dot_general(
+                q_ref[:, cols], k_ref[band, cols], NT, preferred_element_type=jnp.float32
+            )
+            scores = scores * EXP2_SCALE
+            new_top = jnp.max(scores, axis=1, keepdims=True)
+            if top is not None:
+                new_top = jnp.maximum(top, new_top)
+            weights = jnp.exp2(scores - new_top).astype(jnp.bfloat16)
+            summed = jnp.dot(
+                weights,
+                jnp.concatenate([v_ref[band, cols], ones], axis=1),
+                preferred_element_type=jnp.float32,
+            )
+            if top is not None:
+                summed = summed + acc * jnp.exp2(top - new_top)
+            top, acc = new_top, summed
         if last:
-            out_ref[:, cols] = jnp.where(kept_ref[...] > 0.0, acc / tot, 0.0)
+            (out_ref,) = rest
+            out_ref[:, cols] = (acc[:, :HEAD_DIM] / acc[:, HEAD_DIM:]).astype(out_ref.dtype)
         else:
-            if first:
-                new_max = jnp.broadcast_to(highest, acc.shape)
-            max_ref[:, cols] = new_max
-            acc_ref[:, wide] = jnp.concatenate([acc, tot], axis=1)
-
-
-def decode(place, mine, theirs, weights, queries, state, kept, shares):
-    first, last = state is None, kept is not None
+            max_ref, acc_ref = rest
+            max_ref[:, cols] = jnp.broadcast_to(top, (top.shape[0], HEAD_DIM))
+            acc_ref[:, wide] = acc
+
+
+def decode(queries, keys_values, state, out_type):
+    first, last = state is None, out_type is not None
     tokens, width = queries.shape
-    rows, half = mine[0].shape
-    depth = weights.shape[0]
-    pair = 2 * HEAD_DIM
+    latents = keys_values.shape[0]
+    pair = min(2 * HEAD_DIM, width)
     steps = width // pair
-    pieces = len(mine)
-    pair_block = pl.BlockSpec((tokens, pair), lambda i, ids: (0, i))
-    wide_block = pl.BlockSpec((tokens, 2 * pair), lambda i, ids: (0, i))
-    in_specs = [whole((rows, half))] * (2 * pieces) + [
-        pl.BlockSpec((depth, pair), lambda i, ids: (0, i)),
-        pl.BlockSpec((depth, pair), lambda i, ids: (0, steps + i)),
-        pair_block,
+    narrow = pl.BlockSpec((tokens, pair), lambda i: (0, i))
+    wide = pl.BlockSpec((tokens, 2 * pair), lambda i: (0, i))
+    in_specs = [
+        narrow,
+        pl.BlockSpec((latents, pair), lambda i: (0, i)),
+        pl.BlockSpec((latents, pair), lambda i: (0, steps + i)),
     ]
-    args = [*mine, *theirs, weights, weights, queries]
+    args = [queries, keys_values, keys_values]
     if not first:
-        in_specs += [pair_block, wide_block]
+        in_specs += [narrow, wide]
         args += list(state)
     if last:
-        in_specs += [whole(kept.shape)]
-        args += [kept]
-        out_specs = pair_block
-        out_shape = jax.ShapeDtypeStruct((tokens, width), jnp.float32)
+        out_specs = narrow
+        out_shape = jax.ShapeDtypeStruct((tokens, width), out_type)
     else:
-        out_specs = [pair_block, wide_block]
+        out_specs = [narrow, wide]
         out_shape = [
             jax.ShapeDtypeStruct((tokens, width), jnp.float32),
             jax.ShapeDtypeStruct((tokens, 2 * width), jnp.float32),
         ]
-    latents = rows * pieces
-    grid_spec = pltpu.PrefetchScalarGridSpec(
-        num_scalar_prefetch=1,
+    return pl.pallas_call(
+        functools.partial(decode_kernel, first, last),
         grid=(steps,),
         in_specs=in_specs,
         out_specs=out_specs,
-        scratch_shapes=[pltpu.VMEM((latents, 2 * half), jnp.bfloat16)],
-    )
-    return pl.pallas_call(
-        functools.partial(decode_kernel, shares, pieces, first, last),
-        grid_spec=grid_spec,
         out_shape=out_shape,
-        compiler_params=params(48),
+        compiler_params=params(40),
         cost_estimate=cost(
-            4 * latents * depth * width + 16 * tokens * latents * width,
-            4 * depth * width + 24 * tokens * width,
+            16 * tokens * latents * width,
+            4 * latents * width + 16 * tokens * width,
             tokens * latents * (width // HEAD_DIM),
         ),
         name="decode_rows",
-    )(place.reshape(1), *args)
+    )(*args)
 
 
 def swap_perm(size):
@@ -508,14 +512,25 @@
     modality = jnp.arange(mods, dtype=jnp.int32)
     pair = 2 * HEAD_DIM
 
-    def share(weight):
-        depth = weight.shape[0] // groups
-        own = lax.dynamic_slice_in_dim(weight, g * depth, depth, 0)
-        return lax.all_gather(own, ("groups", "pos"), tiled=True), depth
-
-    out_all, out_depth = share(w_out)
-    out_all = out_all.reshape(groups, pos * out_depth, w_out.shape[1])
-    kv_all, kv_depth = share(jnp.concatenate([w_key, w_value], axis=1))
+    far, z, y, x = pos // 2, p // 2, p % 2, g % 2
+    near = swap_perm(pos)
+
+    out_depth = w_out.shape[0] // groups
+    out_all = lax.all_gather(
+        lax.dynamic_slice_in_dim(w_out, g * out_depth, out_depth, 0),
+        ("groups", "pos"),
+        tiled=True,
+    ).reshape(groups, pos * out_depth, w_out.shape[1])
+
+    part = half_width // 2
+
+    def columns(arrays, which):
+        return jnp.concatenate(
+            [lax.dynamic_slice_in_dim(v, which * part, part, 1) for v in arrays], axis=1
+        )
+
+    kv_own = columns((w_key, w_value), y)
+    kv_near = lax.ppermute(columns((w_key, w_value), 1 - y), "pos", near)
 
     q_onehot = (query_ids[:, None] == modality[None, :]).astype(jnp.int32)
     local_counts = jnp.sum(q_onehot, axis=0)
@@ -529,14 +544,32 @@
     ).astype(jnp.bfloat16)
     payload = pack(enc_keys, enc_values, extra)
     kv = lax.all_to_all(payload, "pos", 0, 0, tiled=True)
-    attended = encode(p, latent_queries, kv, enc_bias, pos)
+    head_queries = lax.dynamic_slice_in_dim(latent_queries, p * HEAD_DIM, HEAD_DIM, 1)
+    head_bias = lax.dynamic_slice_in_dim(enc_bias, p, 1, 1)[:, 0]
+    kv_sent, kv = lax.optimization_barrier((jnp.where(x == 0, kv_own, kv_near), kv))
+    kv_bands = [kv_own, kv_near]
+    kv_at = [p, p ^ 1]
+    shifts = sorted(range(far), key=lambda k: min(k, far - k))
+    moved = {}
+    for k in shifts[1:-1]:
+        moved[k] = lax.ppermute(kv_sent, "pos", shift_perm(pos, k))
+    attended = encode(head_queries, kv, head_bias, pos)
+    attended, kv_sent, moved = lax.optimization_barrier((attended, kv_sent, moved))
+    moved[shifts[-1]] = lax.ppermute(kv_sent, "pos", shift_perm(pos, shifts[-1]))
     attended = lax.all_to_all(attended, "pos", 0, 0, tiled=True)
+    attended, moved = lax.optimization_barrier((attended, moved))
 
     partial_value = project(attended, out_all, rows, out_depth)
     theirs = lax.ppermute(partial_value, "head", swap_perm(2))
-    own_cols, normed = normalise(
-        place, partial_value, theirs, latent_array, norm_gain[None, :], groups, kv_depth
-    )
+    own_cols, normed, normed_other = normalise(
+        place, partial_value, theirs, latent_array, norm_gain[None, :]
+    )
+    for k in shifts[1:]:
+        kv_bands += [moved[k], lax.ppermute(moved[k], "groups", swap_perm(groups))]
+        there = ((z + k) % far) * 2
+        kv_at += [there + (y ^ x), there + (1 - (y ^ x))]
+    kv_weights = jnp.concatenate(kv_bands)
+    kv_ids = jnp.stack([place, *kv_at]).astype(jnp.int32)
 
     counts = kv.reshape(pos, tokens + EXTRA, pair)[:, tokens + id_rows, : 2 * mods]
     counts = counts.astype(jnp.int32)
@@ -546,22 +579,46 @@
     within = jnp.cumsum(q_onehot, axis=0) - q_onehot
     ranked = jnp.sum((within + before[None, :]) * q_onehot, axis=1)
     limits = jnp.sum(q_onehot * query_counts[None, :], axis=1)
-    kept = (ranked < limits).astype(jnp.float32)[:, None]
+    kept = ranked < limits
     lookup = jnp.dot(q_onehot.astype(jnp.bfloat16), query_table, preferred_element_type=jnp.float32)
     queries = (query_features.astype(jnp.float32) + lookup).astype(jnp.bfloat16)
 
-    state = None
-    shifts = sorted(range(far), key=lambda k: min(k, far - k))
-    arrived = {0: normed}
-    for k in shifts[1:]:
-        arrived[k] = lax.ppermute(normed, "pos", shift_perm(pos, k))
-    for k in shifts:
-        mine = [arrived[k], lax.ppermute(arrived[k], "pos", swap_perm(pos))]
-        others = [lax.ppermute(v, "head", swap_perm(2)) for v in mine]
-        state = decode(
-            place, mine, others, kv_all, queries, state, kept if k == shifts[-1] else None, groups
-        )
-    return (own_cols, state)
+    own_queries = columns((queries,), y)
+    near_queries = lax.ppermute(columns((queries,), 1 - y), "pos", near)
+
+    def across(value):
+        return lax.ppermute(value, "pos", near)
+
+    def cores(values):
+        return [lax.ppermute(v, "head", swap_perm(2)) for v in values]
+
+    early = [lax.ppermute(normed, "pos", shift_perm(pos, k)) for k in shifts[1:-1]]
+    first = [normed, across(normed), *early]
+    first = lax.optimization_barrier(first)
+    late = lax.ppermute(first[0], "pos", shift_perm(pos, shifts[-1]))
+    first_other = [normed_other, *cores(first[1:])]
+    second = [across(v) for v in first[2:]]
+    keys_values = latent_keys_values(
+        kv_ids, first + second, first_other + cores(second), kv_weights
+    )
+    near_state = decode(near_queries, keys_values, None, None)
+    own_state = decode(own_queries, keys_values, None, None)
+    late_near, near_state, own_state = lax.optimization_barrier(
+        (across(late), near_state, own_state)
+    )
+    last = [late, late_near]
+    last_other = cores(last)
+    keys_values = latent_keys_values(kv_ids, last, last_other, kv_weights)
+    near_state = decode(near_queries, keys_values, near_state, jnp.bfloat16)
+    own_state = decode(own_queries, keys_values, own_state, jnp.float32)
+    from_near = lax.ppermute(near_state, "pos", near).astype(jnp.float32)
+    decoded = jnp.where(
+        y == 0,
+        jnp.concatenate([own_state, from_near], axis=1),
+        jnp.concatenate([from_near, own_state], axis=1),
+    )
+    decoded = jnp.where(kept[:, None], decoded, 0.0)
+    return (own_cols, decoded)
 
 
 def on_device(sizes, *args):
@@ -571,10 +628,11 @@
         head == 2
         and pos % 2 == 0
         and pos > 2
+        and groups % 2 == 0
         and enc_keys.shape[1] == pos * HEAD_DIM
         and enc_keys.shape[0] % (2 * HEAD_DIM) == 0
         and enc_keys.shape[0] < 2048
-        and w_key.shape[0] % (LANES * groups) == 0
+        and w_key.shape[0] % LANES == 0
         and w_out.shape[0] % (LANES * groups) == 0
         and w_out.shape[1] % LANES == 0
         and latent_array.shape[0] % LANES == 0

time: 347 us -> 317 us (0.914)
  waiting for transfers between devices: 193 us -> 166 us
  Pallas kernels: 81 us -> 57.3 us
  blocking collectives: 23.2 us -> 0 us
  starting transfers between devices: 16.8 us -> 39.9 us
  local copies, waits for them, and re-layouts: 11.8 us -> 27.8 us
  other arithmetic: 3.49 us -> 8.67 us
    ppermute x15 -> x23, waiting for transfers between devices: 64.9 us -> 131 us  [the longest x1 34.2 us: fast_on_device(): lax.ppermute(kv_sent, 'pos', shift_perm(pos, shifts[-1]))]
    all_gather x2 -> x1, waiting for transfers between devices: 58.7 us -> 0.01 us  [fast_on_device(): lax.all_gather(lax.dynamic_slice_in_dim(w_out, g * out_depth, out_depth,...]
    all_to_all x1, waiting for transfers between devices: 66.4 us -> 31.5 us  [fast_on_device(): kv = lax.all_to_all(payload, 'pos', 0, 0, tiled=True)]
    pallas_call x6 -> x8, Pallas kernels: 74.4 us -> 50.8 us  [the longest x4 17.8 us: decode(): pl.pallas_call(functools.partial(decode_kernel, first, last), grid=(steps...]
    all_to_all x1 -> x0, blocking collectives: 23.2 us -> none  [fast_on_device(): attended = lax.all_to_all(attended, 'pos', 0, 0, tiled=True)]
    ppermute x15 -> x23, starting transfers between devices: 9.25 us -> 26.3 us  [the longest x4 4.05 us: across(): return lax.ppermute(value, 'pos', near)]
    unnamed x30 -> x57, local copies, waits for them, and re-layouts: 10 us -> 22.4 us
    all_to_all x0 -> x1, starting transfers between devices: none -> 6.1 us  [fast_on_device(): attended = lax.all_to_all(attended, 'pos', 0, 0, tiled=True)]
  transfers between devices with their start and end apart: 19 -> 27, of which waited for: 7 -> 12; matrix products, arithmetic and copies ran while one was open for 2% -> 7% of each run, Pallas kernels for 19% -> 13%
where the time goes in v3:
time: 317 us; the launch traced here: 316 us
  waiting for transfers between devices  166 us (52%)
  Pallas kernels  57.3 us (18%)
  starting transfers between devices  39.9 us (13%)
  local copies, waits for them, and re-layouts  27.8 us (9%)
  between operations  14.4 us (5%)
  other arithmetic  8.67 us (3%)
    ppermute x1, waiting for transfers between devices, fast_on_device(): lax.ppermute(kv_sent, 'pos', shift_perm(pos, shifts[-1]))  34.2 us
    all_to_all x1, waiting for transfers between devices, fast_on_device(): kv = lax.all_to_all(payload, 'pos', 0, 0, tiled=True)  31.5 us
    ppermute x2, waiting for transfers between devices, fast_on_device(): moved[k] = lax.ppermute(kv_sent, 'pos', shift_perm(pos, k))  28.1 us
    ppermute x1, waiting for transfers between devices, fast_on_device(): kv_near = lax.ppermute(columns((w_key, w_value), 1 - y), 'pos', near)  25.3 us
    unnamed x57, local copies, waits for them, and re-layouts  22.4 us
    pallas_call x4, Pallas kernels, decode(): pl.pallas_call(functools.partial(decode_kernel, first, last), grid=(steps...  17.8 us
    pallas_call x2, Pallas kernels, latent_keys_values(): pl.pallas_call(functools.partial(latents_kernel, pieces), grid_spec=grid_...  17.5 us
    ppermute x2, waiting for transfers between devices, fast_on_device(): lax.ppermute(normed, 'pos', shift_perm(pos, k))  16.3 us
  transfers between devices with their start and end apart: 27, of which 12 were waited for; matrix products, arithmetic and copies ran while one was open for 7% of the time, Pallas kernels for 13%

profile of v3, /device:TPU:0, one launch (start us, length us, event | category | flops | bytes accessed | tf_op | source)
XLA Modules:
  0.0 316.1 jit_solution(13711315997146719805)
XLA Ops:
  10.6 1.2 copy-done.3
  11.8 1.2 copy-done.4
  13.0 3.5 %pack_heads.1 = bf16[4224,256]{1,0:T(8,128)(2,1)} custom-call(bf16[512,1024]{1,0:T(8,128)(2,1)S(1)} %copy-done.3, bf16[512,1024]{1,0:T(8,128)(2,1)S(1)} %copy-done.4, bf16[16,256]{1,0:T(8,128)(2,1)S(1)} %fusion.6.extra_ref), custom_call_target="tpu_custom_call" | custom-call | bytes 4194304 | tf_op jit(solution)/shard_map/pack_heads/pallas_call | solution.py:208
  16.5 7.4 %all-to-all-start = ((bf16[8,528,256]{2,1,0:T(8,128)(2,1)}), bf16[8,528,256]{2,1,0:T(8,128)(2,1)S(1)}, u32[]{:S(2)}, u32[]{:S(2)}) async-start(bf16[8,528,256]{2,1,0:T(8,128)(2,1)} %bitcast.2), calls=%async_computation | async-start | bytes 4325376 | tf_op jit(solution)/shard_map/all_to_all | solution.py:546
  23.9 1.3 constant_dynamic-slice_fusion.6
  26.1 2.0 collective-permute-start
  30.2 25.3 %collective-permute-done = bf16[256,1024]{1,0:T(8,128)(2,1)} collective-permute-done((bf16[256,1024]{1,0:T(8,128)(2,1)}, bf16[256,1024]{1,0:T(8,128)(2,1)}, u32[]{:S(2)}, u32[]{:S(2)}) %collective-permute-start) | collective-permute-done | bytes 524320 | tf_op jit(solution)/shard_map/ppermute | solution.py:533
  55.5 2.3 constant_dynamic-update-slice_fusion.6
  57.8 31.5 %all-to-all-done = bf16[8,528,256]{2,1,0:T(8,128)(2,1)S(1)} async-done(((bf16[8,528,256]{2,1,0:T(8,128)(2,1)}), bf16[8,528,256]{2,1,0:T(8,128)(2,1)S(1)}, u32[]{:S(2)}, u32[]{:S(2)}) %all-to-all-start) | async-done | bytes 2162720 | tf_op jit(solution)/shard_map/all_to_all | solution.py:546
  89.3 3.8 %collective-permute-start.1 = (bf16[256,1024]{1,0:T(8,128)(2,1)}, bf16[256,1024]{1,0:T(8,128)(2,1)S(1)}, u32[]{:S(2)}, u32[]{:S(2)}) collective-permute-start(bf16[256,1024]{1,0:T(8,128)(2,1)} %get-tuple-element.32), channel_id=1, source_target_pairs={{4,0},{6,2},{8,4},{10,6},{12,8},{14,10},{0,12},{2,14},{5,1},{7,3},... | collective-permute-start | bytes 1572872 | tf_op jit(solution)/shard_map/ppermute | solution.py:555
  93.1 12.2 %encode_head.1 = bf16[2048,128]{1,0:T(8,128)(2,1)S(1)} custom-call(bf16[2048,128]{1,0:T(8,128)(2,1)S(1)} %constant_dynamic-slice_fusion.8.q_ref, bf16[4224,256]{1,0:T(8,128)(2,1)S(1)} %bitcast.37, f32[3]{0:T(128)S(1)} %fusion.9.bias_ref), custom_call_target="tpu_custom_call" | custom-call | flops 17179869184 | bytes 2162688 | tf_op jit(solution)/shard_map/encode_head/pallas_call | solution.py:255
  106.1 11.2 %collective-permute-done.2 = bf16[256,1024]{1,0:T(8,128)(2,1)S(1)} collective-permute-done((bf16[256,1024]{1,0:T(8,128)(2,1)}, bf16[256,1024]{1,0:T(8,128)(2,1)S(1)}, u32[]{:S(2)}, u32[]{:S(2)}) %collective-permute-start.2) | collective-permute-done | bytes 524320 | tf_op jit(solution)/shard_map/ppermute | solution.py:555
  118.1 17.0 %collective-permute-done.1 = bf16[256,1024]{1,0:T(8,128)(2,1)S(1)} collective-permute-done((bf16[256,1024]{1,0:T(8,128)(2,1)}, bf16[256,1024]{1,0:T(8,128)(2,1)S(1)}, u32[]{:S(2)}, u32[]{:S(2)}) %collective-permute-start.1) | collective-permute-done | bytes 524320 | tf_op jit(solution)/shard_map/ppermute | solution.py:555
  135.8 6.1 %all-to-all-start.1 = ((bf16[8,256,128]{2,1,0:T(8,128)(2,1)}), bf16[8,256,128]{2,1,0:T(8,128)(2,1)S(1)}, u32[]{:S(2)}, u32[]{:S(2)}) async-start(bf16[8,256,128]{2,1,0:T(8,128)(2,1)} %bitcast.39), calls=%async_computation.1 | async-start | bytes 1048576 | tf_op jit(solution)/shard_map/all_to_all | solution.py:559
  141.9 2.9 collective-permute-start.3
  144.8 34.2 %collective-permute-done.3 = bf16[256,1024]{1,0:T(8,128)(2,1)} collective-permute-done((bf16[256,1024]{1,0:T(8,128)(2,1)}, bf16[256,1024]{1,0:T(8,128)(2,1)}, u32[]{:S(2)}, u32[]{:S(2)}) %collective-permute-start.3) | collective-permute-done | bytes 524320 | tf_op jit(solution)/shard_map/ppermute | solution.py:558
  179.1 2.2 copy-done.1
  181.3 3.0 project_rows.1.mine_ref
  184.4 4.3 %collective-permute-done.4.theirs_ref = f32[256,2048]{1,0:T(8,128)} collective-permute-done((f32[256,2048]{1,0:T(8,128)S(1)}, f32[256,2048]{1,0:T(8,128)}, u32[]{:S(2)}, u32[]{:S(2)}) %collective-permute-start.4) | collective-permute-done | bytes 2097184 | tf_op jit(solution)/shard_map/ppermute | solution.py:563
  188.7 1.2 copy-done.5
  189.9 3.3 %norm_rows.1 = (f32[256,1024]{1,0:T(8,128)}, bf16[256,1024]{1,0:T(8,128)(2,1)S(1)}, bf16[256,1024]{1,0:T(8,128)(2,1)S(1)}) custom-call(s32[1]{0:T(128)} %bitcast.ids_ref, f32[256,2048]{1,0:T(8,128)S(1)} %project_rows.1.mine_ref, f32[256,2048]{1,0:T(8,128)} %collective-permute-done.4.theirs_ref, bf16[256,2048]{1,0:T(8,128)(2,1)S(1)} %copy-done.5, ...), custom_call_target="tpu_custom_call" | custom-call | flops 3145728 | bytes 6815744 | tf_op jit(solution)/shard_map/norm_rows/pallas_call | solution.py:331
  194.0 3.8 %collective-permute-start.6 = (bf16[256,1024]{1,0:T(8,128)(2,1)S(1)}, bf16[256,1024]{1,0:T(8,128)(2,1)S(1)}, u32[]{:S(2)}, u32[]{:S(2)}) collective-permute-start(bf16[256,1024]{1,0:T(8,128)(2,1)S(1)} %get-tuple-element.37.refs_0_), channel_id=1, source_target_pairs={{4,0},{6,2},{8,4},{10,6},{12,8},{14,10},{0,12},{2,14},{5,1},{7,3},... | collective-permute-start | bytes 1572872 | tf_op jit(solution)/shard_map/ppermute | solution.py:595
  197.9 1.5 collective-permute-start.5
  199.3 1.5 collective-permute-start.18
  201.4 9.2 %collective-permute-done.7.refs_3_ = bf16[256,1024]{1,0:T(8,128)(2,1)S(1)} collective-permute-done((bf16[256,1024]{1,0:T(8,128)(2,1)S(1)}, bf16[256,1024]{1,0:T(8,128)(2,1)S(1)}, u32[]{:S(2)}, u32[]{:S(2)}) %collective-permute-start.7) | collective-permute-done | bytes 524320 | tf_op jit(solution)/shard_map/ppermute | solution.py:595
  210.6 1.5 collective-permute-start.20
  212.1 7.1 %collective-permute-done.6.refs_2_ = bf16[256,1024]{1,0:T(8,128)(2,1)S(1)} collective-permute-done((bf16[256,1024]{1,0:T(8,128)(2,1)S(1)}, bf16[256,1024]{1,0:T(8,128)(2,1)S(1)}, u32[]{:S(2)}, u32[]{:S(2)}) %collective-permute-start.6) | collective-permute-done | bytes 524320 | tf_op jit(solution)/shard_map/ppermute | solution.py:595
  219.2 2.4 collective-permute-start.8
  221.6 1.5 collective-permute-start.11
  223.9 1.7 add_convert_fusion
  225.8 1.9 constant_dynamic-update-slice_fusion.5
  227.7 7.5 %collective-permute-done.20 = bf16[256,1024]{1,0:T(8,128)(2,1)S(1)} collective-permute-done((bf16[256,1024]{1,0:T(8,128)(2,1)}, bf16[256,1024]{1,0:T(8,128)(2,1)S(1)}, u32[]{:S(2)}, u32[]{:S(2)}) %collective-permute-start.20) | collective-permute-done | bytes 524320 | tf_op jit(solution)/shard_map/ppermute | solution.py:568
  235.1 9.2 %collective-permute-done.8.refs_0_ = bf16[256,1024]{1,0:T(8,128)(2,1)} collective-permute-done((bf16[256,1024]{1,0:T(8,128)(2,1)S(1)}, bf16[256,1024]{1,0:T(8,128)(2,1)}, u32[]{:S(2)}, u32[]{:S(2)}) %collective-permute-start.8) | collective-permute-done | bytes 524320 | tf_op jit(solution)/shard_map/ppermute | solution.py:598
  245.7 1.9 constant_dynamic-update-slice_fusion.4
  247.6 1.9 constant_dynamic-update-slice_fusion.3
  250.3 1.9 constant_dynamic-update-slice_fusion.1
  253.1 1.5 collective-permute-start.10
  255.4 11.8 %latent_keys_values.2.refs_1_.refs_2_ = bf16[1536,1024]{1,0:T(8,128)(2,1)S(1)} custom-call(s32[9]{0:T(128)S(1)} %stack.36.ids_ref, bf16[256,1024]{1,0:T(8,128)(2,1)S(1)} %get-tuple-element.37.refs_0_, bf16[256,1024]{1,0:T(8,128)(2,1)} %collective-permute-done.5.refs_1_, bf16[256,1024]{1,0:T(8,128)(2,1)S(1)} %collective-permute-done.6.refs_2_, ...), custom_call_target="tpu_custom_call" | custom-call | flops 6442450944 | bytes 4194304 | tf_op jit(solution)/shard_map/latent_keys_values/pallas_call | solution.py:382
  267.2 5.2 %decode_rows.5 = (f32[512,512]{1,0:T(8,128)S(1)}, f32[512,1024]{1,0:T(8,128)S(1)}) custom-call(bf16[512,512]{1,0:T(8,128)(2,1)S(1)} %get-tuple-element.56.refs_0_, bf16[1536,1024]{1,0:T(8,128)(2,1)S(1)} %latent_keys_values.2.refs_1_.refs_2_, bf16[1536,1024]{1,0:T(8,128)(2,1)S(1)} %latent_keys_values.2.refs_1_.refs_2_), custom_call_target="tpu_custom_call" | custom-call | flops 6442450944 | bytes 7340032 | tf_op jit(solution)/shard_map/decode_rows/pallas_call | solution.py:461
  272.5 1.3 copy-done.12
  273.8 5.2 %decode_rows.4 = (f32[512,512]{1,0:T(8,128)S(1)}, f32[512,1024]{1,0:T(8,128)S(1)}) custom-call(bf16[512,512]{1,0:T(8,128)(2,1)S(1)} %collective-permute-done.10.refs_0_, bf16[1536,1024]{1,0:T(8,128)(2,1)S(1)} %latent_keys_values.2.refs_1_.refs_2_, bf16[1536,1024]{1,0:T(8,128)(2,1)S(1)} %latent_keys_values.2.refs_1_.refs_2_), custom_call_target="tpu_custom_call" | custom-call | flops 6442450944 | bytes 7340032 | tf_op jit(solution)/shard_map/decode_rows/pallas_call | solution.py:461
  279.1 1.3 copy-done.14
  283.7 5.7 %latent_keys_values.3.refs_1_.refs_2_ = bf16[512,1024]{1,0:T(8,128)(2,1)S(1)} custom-call(s32[9]{0:T(128)S(1)} %stack.36.ids_ref, bf16[256,1024]{1,0:T(8,128)(2,1)} %collective-permute-done.8.refs_0_, bf16[256,1024]{1,0:T(8,128)(2,1)} %collective-permute-done.9.refs_1_, bf16[256,1024]{1,0:T(8,128)(2,1)} %collective-permute-done.21.refs_2_, ...), custom_call_target="tpu_custom_call" | custom-call | flops 2147483648 | bytes 4194304 | tf_op jit(solution)/shard_map/latent_keys_values/pallas_call | solution.py:382
  289.4 3.8 %decode_rows.7 = bf16[512,512]{1,0:T(8,128)(2,1)S(1)} custom-call(bf16[512,512]{1,0:T(8,128)(2,1)S(1)} %copy-done.11, bf16[512,1024]{1,0:T(8,128)(2,1)S(1)} %latent_keys_values.3.refs_1_.refs_2_, bf16[512,1024]{1,0:T(8,128)(2,1)S(1)} %latent_keys_values.3.refs_1_.refs_2_, f32[512,512]{1,0:T(8,128)S(1)} %copy-done.17, f32[512,1024]{1,0:T(8,128)S(1)} %copy-done.15), custom_call_target="tpu_custom_call" | custom-call | flops 2147483648 | bytes 5242880 | tf_op jit(solution)/shard_map/decode_rows/pallas_call | solution.py:461
  293.2 1.5 collective-permute-start.23
  295.0 3.6 %decode_rows.6 = f32[512,512]{1,0:T(8,128)S(1)} custom-call(bf16[512,512]{1,0:T(8,128)(2,1)S(1)} %get-tuple-element.56.refs_0_, bf16[512,1024]{1,0:T(8,128)(2,1)S(1)} %latent_keys_values.3.refs_1_.refs_2_, bf16[512,1024]{1,0:T(8,128)(2,1)S(1)} %latent_keys_values.3.refs_1_.refs_2_, f32[512,512]{1,0:T(8,128)S(1)} %get-tuple-element.50.refs_3_, ...), custom_call_target="tpu_custom_call" | custom-call | flops 2147483648 | bytes 5242880 | tf_op jit(solution)/shard_map/decode_rows/pallas_call | solution.py:461
  298.6 9.0 %collective-permute-done.23 = bf16[512,512]{1,0:T(8,128)(2,1)S(1)} collective-permute-done((bf16[512,512]{1,0:T(8,128)(2,1)S(1)}, bf16[512,512]{1,0:T(8,128)(2,1)S(1)}, u32[]{:S(2)}, u32[]{:S(2)}) %collective-permute-start.23) | collective-permute-done | bytes 524320 | tf_op jit(solution)/shard_map/ppermute | solution.py:614
  307.7 1.6 fusion
  (104 shorter events, 18.8 us)
Async XLA Ops:
  7.2 1.0 copy-start
  7.2 171.9 %all-gather.2.cloned.1.call-start = ((), (), s32[]{:S(2)}) async-start(), calls=%async_computation.2 | async-start | bytes 4456448 | tf_op jit(solution)/shard_map/all_gather | solution.py:519
  10.6 1.2 copy-start.3
  11.8 1.2 copy-start.4
  16.5 11.6 %copy-start.24 = (f32[3,8]{1,0:T(4,128)S(1)}, f32[3,8]{1,0:T(4,128)}, u32[]{:S(2)}) copy-start(f32[3,8]{1,0:T(4,128)} %param.26) | copy-start | bytes 292
  16.5 72.7 %all-to-all-start = ((bf16[8,528,256]{2,1,0:T(8,128)(2,1)}), bf16[8,528,256]{2,1,0:T(8,128)(2,1)S(1)}, u32[]{:S(2)}, u32[]{:S(2)}) async-start(bf16[8,528,256]{2,1,0:T(8,128)(2,1)} %bitcast.2), calls=%async_computation | async-start | bytes 4325376 | tf_op jit(solution)/shard_map/all_to_all | solution.py:546
  25.2 3.1 copy-start.18
  26.1 29.4 %collective-permute-start = (bf16[256,1024]{1,0:T(8,128)(2,1)}, bf16[256,1024]{1,0:T(8,128)(2,1)}, u32[]{:S(2)}, u32[]{:S(2)}) collective-permute-start(bf16[256,1024]{1,0:T(8,128)(2,1)} %pad_maximum_fusion.1), channel_id=1, source_target_pairs={{0,2},{2,0},{4,6},{6,4},{8,10},{10,8},{12,14},{14,12},{1,3},{3,1},... | collective-permute-start | bytes 1572872 | tf_op jit(solution)/shard_map/ppermute | solution.py:533
  89.2 16.0 %copy-start.2 = (bf16[8,528,256]{2,1,0:T(8,128)(2,1)}, bf16[8,528,256]{2,1,0:T(8,128)(2,1)S(1)}, u32[]{:S(2)}) copy-start(bf16[8,528,256]{2,1,0:T(8,128)(2,1)S(1)} %all-to-all-done) | copy-start | bytes 6488068
  89.2 28.0 %collective-permute-start.2 = (bf16[256,1024]{1,0:T(8,128)(2,1)}, bf16[256,1024]{1,0:T(8,128)(2,1)S(1)}, u32[]{:S(2)}, u32[]{:S(2)}) collective-permute-start(bf16[256,1024]{1,0:T(8,128)(2,1)} %get-tuple-element.32), channel_id=1, source_target_pairs={{12,0},{14,2},{0,4},{2,6},{4,8},{6,10},{8,12},{10,14},{13,1},{15,3... | collective-permute-start | bytes 1572872 | tf_op jit(solution)/shard_map/ppermute | solution.py:555
  89.3 45.8 %collective-permute-start.1 = (bf16[256,1024]{1,0:T(8,128)(2,1)}, bf16[256,1024]{1,0:T(8,128)(2,1)S(1)}, u32[]{:S(2)}, u32[]{:S(2)}) collective-permute-start(bf16[256,1024]{1,0:T(8,128)(2,1)} %get-tuple-element.32), channel_id=1, source_target_pairs={{4,0},{6,2},{8,4},{10,6},{12,8},{14,10},{0,12},{2,14},{5,1},{7,3},... | collective-permute-start | bytes 1572872 | tf_op jit(solution)/shard_map/ppermute | solution.py:555
  106.1 82.6 %copy-start.7 = (f32[2048]{0:T(1024)S(1)}, f32[2048]{0:T(1024)}, u32[]{:S(2)}) copy-start(f32[2048]{0:T(1024)} %param.20) | copy-start | bytes 24580
  135.8 43.2 %all-to-all-start.1 = ((bf16[8,256,128]{2,1,0:T(8,128)(2,1)}), bf16[8,256,128]{2,1,0:T(8,128)(2,1)S(1)}, u32[]{:S(2)}, u32[]{:S(2)}) async-start(bf16[8,256,128]{2,1,0:T(8,128)(2,1)} %bitcast.39), calls=%async_computation.1 | async-start | bytes 1048576 | tf_op jit(solution)/shard_map/all_to_all | solution.py:559
  141.9 37.1 %collective-permute-start.3 = (bf16[256,1024]{1,0:T(8,128)(2,1)}, bf16[256,1024]{1,0:T(8,128)(2,1)}, u32[]{:S(2)}, u32[]{:S(2)}) collective-permute-start(bf16[256,1024]{1,0:T(8,128)(2,1)} %get-tuple-element.32), channel_id=1, source_target_pairs={{8,0},{10,2},{12,4},{14,6},{0,8},{2,10},{4,12},{6,14},{9,1},{11,3}... | collective-permute-start | bytes 1572872 | tf_op jit(solution)/shard_map/ppermute | solution.py:558
  179.1 2.2 copy-start.1
  181.3 42.7 %copy-start.23 = (bf16[3,1024]{1,0:T(4,128)(2,1)S(1)}, bf16[3,1024]{1,0:T(4,128)(2,1)}, u32[]{:S(2)}) copy-start(bf16[3,1024]{1,0:T(4,128)(2,1)} %param.25) | copy-start | bytes 18436
  184.3 39.6 %copy-start.22 = (s32[512]{0:T(512)S(1)}, s32[512]{0:T(512)}, u32[]{:S(2)}) copy-start(s32[512]{0:T(512)} %param.24) | copy-start | bytes 6148
  184.3 4.4 %collective-permute-start.4 = (f32[256,2048]{1,0:T(8,128)S(1)}, f32[256,2048]{1,0:T(8,128)}, u32[]{:S(2)}, u32[]{:S(2)}) collective-permute-start(f32[256,2048]{1,0:T(8,128)S(1)} %project_rows.1.mine_ref), channel_id=1, source_target_pairs={{0,1},{1,0},{2,3},{3,2},{4,5},{5,4},{6,7},{7,6},{8,9},{9,8},{10,11... | collective-permute-start | bytes 6291464 | tf_op jit(solution)/shard_map/ppermute | solution.py:563
  188.7 1.2 copy-start.5
  194.0 16.6 %collective-permute-start.7 = (bf16[256,1024]{1,0:T(8,128)(2,1)S(1)}, bf16[256,1024]{1,0:T(8,128)(2,1)S(1)}, u32[]{:S(2)}, u32[]{:S(2)}) collective-permute-start(bf16[256,1024]{1,0:T(8,128)(2,1)S(1)} %get-tuple-element.37.refs_0_), channel_id=1, source_target_pairs={{12,0},{14,2},{0,4},{2,6},{4,8},{6,10},{8,12},{10,14},{13,1},{15,3... | collective-permute-start | bytes 1572872 | tf_op jit(solution)/shard_map/ppermute | solution.py:595
  194.0 25.2 %collective-permute-start.6 = (bf16[256,1024]{1,0:T(8,128)(2,1)S(1)}, bf16[256,1024]{1,0:T(8,128)(2,1)S(1)}, u32[]{:S(2)}, u32[]{:S(2)}) collective-permute-start(bf16[256,1024]{1,0:T(8,128)(2,1)S(1)} %get-tuple-element.37.refs_0_), channel_id=1, source_target_pairs={{4,0},{6,2},{8,4},{10,6},{12,8},{14,10},{0,12},{2,14},{5,1},{7,3},... | collective-permute-start | bytes 1572872 | tf_op jit(solution)/shard_map/ppermute | solution.py:595
  197.9 21.4 %collective-permute-start.5 = (bf16[256,1024]{1,0:T(8,128)(2,1)S(1)}, bf16[256,1024]{1,0:T(8,128)(2,1)}, u32[]{:S(2)}, u32[]{:S(2)}) collective-permute-start(bf16[256,1024]{1,0:T(8,128)(2,1)S(1)} %get-tuple-element.37.refs_0_), channel_id=1, source_target_pairs={{0,2},{2,0},{4,6},{6,4},{8,10},{10,8},{12,14},{14,12},{1,3},{3,1},... | collective-permute-start | bytes 1572872 | tf_op jit(solution)/shard_map/ppermute | solution.py:590
  199.3 23.8 %collective-permute-start.18 = (bf16[256,1024]{1,0:T(8,128)(2,1)}, bf16[256,1024]{1,0:T(8,128)(2,1)S(1)}, u32[]{:S(2)}, u32[]{:S(2)}) collective-permute-start(bf16[256,1024]{1,0:T(8,128)(2,1)} %copy-done.20), channel_id=1, source_target_pairs={{0,16},{16,0},{1,17},{17,1},{2,18},{18,2},{3,19},{19,3},{4,20},{20... | collective-permute-start | bytes 1572872 | tf_op jit(solution)/shard_map/ppermute | solution.py:568
  200.9 26.8 %collective-permute-start.19 = (bf16[256,1024]{1,0:T(8,128)(2,1)}, bf16[256,1024]{1,0:T(8,128)(2,1)S(1)}, u32[]{:S(2)}, u32[]{:S(2)}) collective-permute-start(bf16[256,1024]{1,0:T(8,128)(2,1)} %copy-done.19), channel_id=1, source_target_pairs={{0,16},{16,0},{1,17},{17,1},{2,18},{18,2},{3,19},{19,3},{4,20},{20... | collective-permute-start | bytes 1572872 | tf_op jit(solution)/shard_map/ppermute | solution.py:568
  210.6 24.5 %collective-permute-start.20 = (bf16[256,1024]{1,0:T(8,128)(2,1)}, bf16[256,1024]{1,0:T(8,128)(2,1)S(1)}, u32[]{:S(2)}, u32[]{:S(2)}) collective-permute-start(bf16[256,1024]{1,0:T(8,128)(2,1)} %collective-permute-done.3), channel_id=1, source_target_pairs={{0,16},{16,0},{1,17},{17,1},{2,18},{18,2},{3,19},{19,3},{4,20},{20... | collective-permute-start | bytes 1572872 | tf_op jit(solution)/shard_map/ppermute | solution.py:568
  219.2 25.1 %collective-permute-start.8 = (bf16[256,1024]{1,0:T(8,128)(2,1)S(1)}, bf16[256,1024]{1,0:T(8,128)(2,1)}, u32[]{:S(2)}, u32[]{:S(2)}) collective-permute-start(bf16[256,1024]{1,0:T(8,128)(2,1)S(1)} %get-tuple-element.37.refs_0_), channel_id=1, source_target_pairs={{8,0},{10,2},{12,4},{14,6},{0,8},{2,10},{4,12},{6,14},{9,1},{11,3}... | collective-permute-start | bytes 1572872 | tf_op jit(solution)/shard_map/ppermute | solution.py:598
  221.6 22.7 %collective-permute-start.11 = (bf16[256,1024]{1,0:T(8,128)(2,1)S(1)}, bf16[256,1024]{1,0:T(8,128)(2,1)S(1)}, u32[]{:S(2)}, u32[]{:S(2)}) collective-permute-start(bf16[256,1024]{1,0:T(8,128)(2,1)S(1)} %collective-permute-done.6.refs_2_), channel_id=1, source_target_pairs={{0,2},{2,0},{4,6},{6,4},{8,10},{10,8},{12,14},{14,12},{1,3},{3,1},... | collective-permute-start | bytes 1572872 | tf_op jit(solution)/shard_map/ppermute | solution.py:590
  223.1 22.6 %collective-permute-start.12 = (bf16[256,1024]{1,0:T(8,128)(2,1)S(1)}, bf16[256,1024]{1,0:T(8,128)(2,1)S(1)}, u32[]{:S(2)}, u32[]{:S(2)}) collective-permute-start(bf16[256,1024]{1,0:T(8,128)(2,1)S(1)} %collective-permute-done.7.refs_3_), channel_id=1, source_target_pairs={{0,2},{2,0},{4,6},{6,4},{8,10},{10,8},{12,14},{14,12},{1,3},{3,1},... | collective-permute-start | bytes 1572872 | tf_op jit(solution)/shard_map/ppermute | solution.py:590
  225.6 29.8 %copy-start.9 = (bf16[256,1024]{1,0:T(8,128)(2,1)S(1)}, bf16[256,1024]{1,0:T(8,128)(2,1)}, u32[]{:S(2)}) copy-start(bf16[256,1024]{1,0:T(8,128)(2,1)} %copy-done.8) | copy-start | bytes 1572868
  227.7 27.0 %collective-permute-start.14 = (bf16[256,1024]{1,0:T(8,128)(2,1)S(1)}, bf16[256,1024]{1,0:T(8,128)(2,1)S(1)}, u32[]{:S(2)}, u32[]{:S(2)}) collective-permute-start(bf16[256,1024]{1,0:T(8,128)(2,1)S(1)} %collective-permute-done.6.refs_2_), channel_id=1, source_target_pairs={{0,1},{1,0},{2,3},{3,2},{4,5},{5,4},{6,7},{7,6},{8,9},{9,8},{10,11... | collective-permute-start | bytes 1572872 | tf_op jit(solution)/shard_map/ppermute | solution.py:593
  235.1 19.7 %collective-permute-start.15 = (bf16[256,1024]{1,0:T(8,128)(2,1)S(1)}, bf16[256,1024]{1,0:T(8,128)(2,1)S(1)}, u32[]{:S(2)}, u32[]{:S(2)}) collective-permute-start(bf16[256,1024]{1,0:T(8,128)(2,1)S(1)} %collective-permute-done.7.refs_3_), channel_id=1, source_target_pairs={{0,1},{1,0},{2,3},{3,2},{4,5},{5,4},{6,7},{7,6},{8,9},{9,8},{10,11... | collective-permute-start | bytes 1572872 | tf_op jit(solution)/shard_map/ppermute | solution.py:593
  244.4 8.8 %collective-permute-start.13 = (bf16[256,1024]{1,0:T(8,128)(2,1)}, bf16[256,1024]{1,0:T(8,128)(2,1)S(1)}, u32[]{:S(2)}, u32[]{:S(2)}) collective-permute-start(bf16[256,1024]{1,0:T(8,128)(2,1)} %collective-permute-done.5.refs_1_), channel_id=1, source_target_pairs={{0,1},{1,0},{2,3},{3,2},{4,5},{5,4},{6,7},{7,6},{8,9},{9,8},{10,11... | collective-permute-start | bytes 1572872 | tf_op jit(solution)/shard_map/ppermute | solution.py:593
  244.4 11.0 %collective-permute-start.16 = (bf16[256,1024]{1,0:T(8,128)(2,1)S(1)}, bf16[256,1024]{1,0:T(8,128)(2,1)S(1)}, u32[]{:S(2)}, u32[]{:S(2)}) collective-permute-start(bf16[256,1024]{1,0:T(8,128)(2,1)S(1)} %collective-permute-done.11.refs_4_), channel_id=1, source_target_pairs={{0,1},{1,0},{2,3},{3,2},{4,5},{5,4},{6,7},{7,6},{8,9},{9,8},{10,11... | collective-permute-start | bytes 1572872 | tf_op jit(solution)/shard_map/ppermute | solution.py:593
  245.7 9.7 %collective-permute-start.17 = (bf16[256,1024]{1,0:T(8,128)(2,1)S(1)}, bf16[256,1024]{1,0:T(8,128)(2,1)S(1)}, u32[]{:S(2)}, u32[]{:S(2)}) collective-permute-start(bf16[256,1024]{1,0:T(8,128)(2,1)S(1)} %collective-permute-done.12.refs_5_), channel_id=1, source_target_pairs={{0,1},{1,0},{2,3},{3,2},{4,5},{5,4},{6,7},{7,6},{8,9},{9,8},{10,11... | collective-permute-start | bytes 1572872 | tf_op jit(solution)/shard_map/ppermute | solution.py:593
  253.1 20.7 %collective-permute-start.10 = (bf16[512,512]{1,0:T(8,128)(2,1)S(1)}, bf16[512,512]{1,0:T(8,128)(2,1)S(1)}, u32[]{:S(2)}, u32[]{:S(2)}) collective-permute-start(bf16[512,512]{1,0:T(8,128)(2,1)S(1)} %get-tuple-element.57), channel_id=1, source_target_pairs={{0,2},{2,0},{4,6},{6,4},{8,10},{10,8},{12,14},{14,12},{1,3},{3,1},... | collective-permute-start | bytes 1572872 | tf_op jit(solution)/shard_map/ppermute | solution.py:587
  254.6 29.1 %collective-permute-start.21 = (bf16[256,1024]{1,0:T(8,128)(2,1)}, bf16[256,1024]{1,0:T(8,128)(2,1)}, u32[]{:S(2)}, u32[]{:S(2)}) collective-permute-start(bf16[256,1024]{1,0:T(8,128)(2,1)} %collective-permute-done.8.refs_0_), channel_id=1, source_target_pairs={{0,1},{1,0},{2,3},{3,2},{4,5},{5,4},{6,7},{7,6},{8,9},{9,8},{10,11... | collective-permute-start | bytes 1572872 | tf_op jit(solution)/shard_map/ppermute | solution.py:593
  254.8 26.5 %collective-permute-start.9 = (bf16[256,1024]{1,0:T(8,128)(2,1)}, bf16[256,1024]{1,0:T(8,128)(2,1)}, u32[]{:S(2)}, u32[]{:S(2)}) collective-permute-start(bf16[256,1024]{1,0:T(8,128)(2,1)} %collective-permute-done.8.refs_0_), channel_id=1, source_target_pairs={{0,2},{2,0},{4,6},{6,4},{8,10},{10,8},{12,14},{14,12},{1,3},{3,1},... | collective-permute-start | bytes 1572872 | tf_op jit(solution)/shard_map/ppermute | solution.py:590
  272.5 1.4 copy-start.12
  273.8 5.2 %copy-start.10 = (bf16[512,512]{1,0:T(8,128)(2,1)}, bf16[512,512]{1,0:T(8,128)(2,1)S(1)}, u32[]{:S(2)}) copy-start(bf16[512,512]{1,0:T(8,128)(2,1)S(1)} %collective-permute-done.10.refs_0_) | copy-start | bytes 1572868
  279.0 1.3 copy-start.14
  280.4 1.0 copy-start.16
  281.4 8.0 %copy-start.11 = (bf16[512,512]{1,0:T(8,128)(2,1)S(1)}, bf16[512,512]{1,0:T(8,128)(2,1)}, u32[]{:S(2)}) copy-start(bf16[512,512]{1,0:T(8,128)(2,1)} %copy-done.10) | copy-start | bytes 1572868
  281.4 2.3 collective-permute-start.22
  282.7 6.7 %copy-start.15 = (f32[512,1024]{1,0:T(8,128)S(1)}, f32[512,1024]{1,0:T(8,128)}, u32[]{:S(2)}) copy-start(f32[512,1024]{1,0:T(8,128)} %copy-done.14) | copy-start | bytes 6291460
  282.7 6.7 %copy-start.17 = (f32[512,512]{1,0:T(8,128)S(1)}, f32[512,512]{1,0:T(8,128)}, u32[]{:S(2)}) copy-start(f32[512,512]{1,0:T(8,128)} %copy-done.16) | copy-start | bytes 3145732
  289.4 5.5 %copy-start.25 = (s32[3]{0:T(128)S(1)}, s32[3]{0:T(128)}, u32[]{:S(2)}) copy-start(s32[3]{0:T(128)} %param.27) | copy-start | bytes 40
  289.4 5.5 %copy-start.13 = (f32[512,1024]{1,0:T(8,128)S(1)}, f32[512,1024]{1,0:T(8,128)}, u32[]{:S(2)}) copy-start(f32[512,1024]{1,0:T(8,128)} %copy-done.12) | copy-start | bytes 6291460
  293.2 14.4 %collective-permute-start.23 = (bf16[512,512]{1,0:T(8,128)(2,1)S(1)}, bf16[512,512]{1,0:T(8,128)(2,1)S(1)}, u32[]{:S(2)}, u32[]{:S(2)}) collective-permute-start(bf16[512,512]{1,0:T(8,128)(2,1)S(1)} %decode_rows.7), channel_id=1, source_target_pairs={{0,2},{2,0},{4,6},{6,4},{8,10},{10,8},{12,14},{14,12},{1,3},{3,1},... | collective-permute-start | bytes 1572872 | tf_op jit(solution)/shard_map/ppermute | solution.py:614
  (5 other events, 4.0 us)
Sparse Core Ops, SparseCore 0:
  10.8 126.3 all-gather.1

commit v4 on v3

--- a/solution.py
+++ b/solution.py
@@ -266,42 +266,52 @@
     )(queries, kv, bias)
 
 
-def project_kernel(heads, att_in_ref, w_ref, out_ref, att_ref):
+def project_kernel(heads, far, ids_ref, att_in_ref, *refs):
+    w_refs, out_ref, att_ref = refs[:-2], refs[-2], refs[-1]
     rows = att_ref.shape[0]
-    shares, depth, _ = w_ref.shape
-
-    @pl.when(pl.program_id(0) == 0)
-    def arrange():
-        for h in range(heads):
-            att_ref[:, h * HEAD_DIM : (h + 1) * HEAD_DIM] = att_in_ref[h * rows : (h + 1) * rows, :]
-
-    total = None
-    for k in range(shares):
-        term = jnp.dot(
-            att_ref[:, k * depth : (k + 1) * depth], w_ref[k], preferred_element_type=jnp.float32
-        )
-        total = term if total is None else total + term
-    out_ref[...] = total
-
-
-def project(attended, w_all, rows, depth):
+    for h in range(heads):
+        att_ref[:, h * HEAD_DIM : (h + 1) * HEAD_DIM] = att_in_ref[h * rows : (h + 1) * rows, :]
+    cols = w_refs[0].shape[1]
+    depth = att_ref.shape[1] // 2
+
+    def place(slot, value):
+        out_ref[:, pl.ds(pl.multiple_of(ids_ref[slot] * cols, cols), cols)] = value
+
+    for slot in range(2):
+        place(slot, jnp.dot(att_ref[...], w_refs[slot][...], preferred_element_type=jnp.float32))
+    mine, theirs = [
+        att_ref[:, pl.ds(pl.multiple_of(ids_ref[2 * far + k] * depth, depth), depth)]
+        for k in range(2)
+    ]
+    for j in range(2):
+        for k in range(far - 1):
+            band = slice(k * depth, (k + 1) * depth)
+            total = jnp.dot(
+                mine, w_refs[2 + 2 * j][band, :], preferred_element_type=jnp.float32
+            ) + jnp.dot(theirs, w_refs[3 + 2 * j][band, :], preferred_element_type=jnp.float32)
+            place(2 + j * (far - 1) + k, total)
+
+
+def project(ids, attended, weights, rows):
     heads = attended.shape[0] // rows
-    shares, long, cols = w_all.shape
-    steps = long // depth
+    far = (ids.shape[0] - 2) // 2
+    width = heads * HEAD_DIM
+    out_cols = 2 * far * weights[0].shape[1]
+    grid_spec = pltpu.PrefetchScalarGridSpec(
+        num_scalar_prefetch=1,
+        grid=(1,),
+        in_specs=[whole(v.shape) for v in (attended, *weights)],
+        out_specs=whole((rows, out_cols)),
+        scratch_shapes=[pltpu.VMEM((rows, width), jnp.bfloat16)],
+    )
     return pl.pallas_call(
-        functools.partial(project_kernel, heads),
-        grid=(steps,),
-        in_specs=[
-            whole(attended.shape),
-            pl.BlockSpec((shares, depth, cols), lambda i: (0, i, 0)),
-        ],
-        out_specs=pl.BlockSpec((rows, cols), lambda i: (0, i)),
-        out_shape=jax.ShapeDtypeStruct((rows, steps * cols), jnp.float32),
-        scratch_shapes=[pltpu.VMEM((rows, heads * HEAD_DIM), jnp.bfloat16)],
+        functools.partial(project_kernel, heads, far),
+        grid_spec=grid_spec,
+        out_shape=jax.ShapeDtypeStruct((rows, out_cols), jnp.float32),
         compiler_params=params(32),
-        cost_estimate=cost(2 * rows * w_all.size, 2 * w_all.size + 4 * rows * steps * cols),
+        cost_estimate=cost(2 * rows * width * out_cols, 2 * width * out_cols + 4 * rows * out_cols),
         name="project_rows",
-    )(attended, w_all)
+    )(ids, attended, *weights)
 
 
 def norm_kernel(
@@ -344,7 +354,7 @@
 
 def latents_kernel(pieces, ids_ref, *refs):
     mine, theirs = refs[:pieces], refs[pieces : 2 * pieces]
-    w_ref, out_ref, normed_ref = refs[2 * pieces :]
+    w_refs, (out_ref, normed_ref, w_ref) = refs[2 * pieces : -3], refs[-3:]
     rows, half = mine[0].shape
     slots = ids_ref.shape[0] - 1
     depth = 2 * half // slots
@@ -361,32 +371,38 @@
                     is_mine, both[0], both[1]
                 )
 
+    for j, band in enumerate(w_refs):
+        w_ref[j * depth : (j + 1) * depth, :] = band[...]
     out_ref[...] = jnp.dot(
         normed_ref[...], w_ref[...], preferred_element_type=jnp.float32
     ).astype(jnp.bfloat16)
 
 
-def latent_keys_values(ids, mine, theirs, weights):
+def latent_keys_values(ids, mine, theirs, bands):
     pieces = len(mine)
     rows, half = mine[0].shape
-    depth, width = weights.shape
+    depth, width = bands[0].shape
     block = min(512, width)
+    total = depth * len(bands)
     grid_spec = pltpu.PrefetchScalarGridSpec(
         num_scalar_prefetch=1,
         grid=(width // block,),
         in_specs=[whole((rows, half))] * (2 * pieces)
-        + [pl.BlockSpec((depth, block), lambda i, ids: (0, i))],
+        + [pl.BlockSpec((depth, block), lambda i, ids: (0, i))] * len(bands),
         out_specs=pl.BlockSpec((rows * pieces, block), lambda i, ids: (0, i)),
-        scratch_shapes=[pltpu.VMEM((rows * pieces, depth), jnp.bfloat16)],
+        scratch_shapes=[
+            pltpu.VMEM((rows * pieces, total), jnp.bfloat16),
+            pltpu.VMEM((total, block), jnp.bfloat16),
+        ],
     )
     return pl.pallas_call(
         functools.partial(latents_kernel, pieces),
         grid_spec=grid_spec,
         out_shape=jax.ShapeDtypeStruct((rows * pieces, width), jnp.bfloat16),
         compiler_params=params(40),
-        cost_estimate=cost(2 * rows * pieces * depth * width, 2 * depth * width),
+        cost_estimate=cost(2 * rows * pieces * total * width, 2 * total * width),
         name="latent_keys_values",
-    )(ids, *mine, *theirs, weights)
+    )(ids, *mine, *theirs, *bands)
 
 
 def decode_kernel(first, last, *refs):
@@ -396,7 +412,7 @@
         old_max_ref, old_acc_ref = rest[:2]
         rest = rest[2:]
     latents = k_ref.shape[0]
-    chunk = min(512, latents)
+    chunk = 512 if latents % 512 == 0 else 256 if latents % 256 == 0 else latents
     ones = jnp.ones((chunk, LANES), jnp.bfloat16)
     for h in range(q_ref.shape[1] // HEAD_DIM):
         cols = slice(h * HEAD_DIM, (h + 1) * HEAD_DIM)
@@ -483,6 +499,14 @@
     return [(((z + k) % far) * 2 + y, z * 2 + y) for z in range(far) for y in range(2)]
 
 
+def hop_perm(size, step, way):
+    far = size // 2
+    moves = [(z, z + 1) for z in range(step - 1, far - 1)]
+    if way < 0:
+        moves = [(far - 1 - a, far - 1 - b) for a, b in moves]
+    return [(a * 2 + y, b * 2 + y) for a, b in moves for y in range(2)]
+
+
 def fast_on_device(
     sizes,
     enc_keys,
@@ -502,7 +526,6 @@
 ):
     groups, pos = sizes
     far = pos // 2
-    g = lax.axis_index("groups")
     p = lax.axis_index("pos")
     place = lax.axis_index("head")
     rows = latent_array.shape[0]
@@ -512,15 +535,27 @@
     modality = jnp.arange(mods, dtype=jnp.int32)
     pair = 2 * HEAD_DIM
 
-    far, z, y, x = pos // 2, p // 2, p % 2, g % 2
+    far, z, y, x = pos // 2, p // 2, p % 2, lax.axis_index("groups") % 2
     near = swap_perm(pos)
 
-    out_depth = w_out.shape[0] // groups
-    out_all = lax.all_gather(
-        lax.dynamic_slice_in_dim(w_out, g * out_depth, out_depth, 0),
-        ("groups", "pos"),
-        tiled=True,
-    ).reshape(groups, pos * out_depth, w_out.shape[1])
+    def over_groups(value):
+        return lax.ppermute(value, "groups", swap_perm(groups))
+
+    def over_near(value):
+        return lax.ppermute(value, "pos", near)
+
+    def over_far(value, k):
+        return lax.ppermute(value, "pos", shift_perm(pos, k))
+
+    shifts = sorted(range(far), key=lambda k: min(k, far - k))
+    out_half = w_out.shape[0] // 2
+    out_sent = lax.dynamic_slice_in_dim(w_out, x * out_half, out_half, 0)
+    out_far = [over_far(out_sent, k) for k in shifts[1:]]
+    out_near = over_near(w_out)
+    out_ids = [p, p ^ 1]
+    for j in range(2):
+        out_ids += [((z + k) % far) * 2 + (y ^ j) for k in shifts[1:]]
+    out_ids = jnp.stack([*out_ids, x, 1 - x]).astype(jnp.int32)
 
     part = half_width // 2
 
@@ -530,7 +565,16 @@
         )
 
     kv_own = columns((w_key, w_value), y)
-    kv_near = lax.ppermute(columns((w_key, w_value), 1 - y), "pos", near)
+    kv_near = over_near(columns((w_key, w_value), 1 - y))
+    lookup = jnp.dot(
+        (query_ids[:, None] == modality[None, :]).astype(jnp.bfloat16),
+        query_table,
+        preferred_element_type=jnp.float32,
+    )
+    queries = (query_features.astype(jnp.float32) + lookup).astype(jnp.bfloat16)
+    own_queries = columns((queries,), y)
+    near_queries = over_near(columns((queries,), 1 - y))
+
 
     q_onehot = (query_ids[:, None] == modality[None, :]).astype(jnp.int32)
     local_counts = jnp.sum(q_onehot, axis=0)
@@ -546,29 +590,41 @@
     kv = lax.all_to_all(payload, "pos", 0, 0, tiled=True)
     head_queries = lax.dynamic_slice_in_dim(latent_queries, p * HEAD_DIM, HEAD_DIM, 1)
     head_bias = lax.dynamic_slice_in_dim(enc_bias, p, 1, 1)[:, 0]
-    kv_sent, kv = lax.optimization_barrier((jnp.where(x == 0, kv_own, kv_near), kv))
+    kv_sent = jnp.where(x == 0, kv_own, kv_near)
+    kv, kv_sent, near_queries, out_far, out_near = lax.optimization_barrier(
+        (kv, kv_sent, near_queries, out_far, out_near)
+    )
+    out_far = jnp.concatenate(out_far)
+    out_bands = [out_far, over_near(out_far), over_groups(out_far)]
+
+    def hop(step, pair):
+        return [
+            lax.ppermute(v, "pos", hop_perm(pos, step, way)) for v, way in zip(pair, (1, -1))
+        ]
+
+    hops = {1: hop(1, [kv_sent, kv_sent])}
+    attended = encode(head_queries, kv, head_bias, pos)
+    attended, hops[1], out_bands = lax.optimization_barrier((attended, hops[1], out_bands))
+    out_far, out_across, out_other = out_bands
+    out_bands = [w_out, out_near, out_far, out_other, out_across, over_near(out_other)]
+    hops[2] = hop(2, hops[1])
+    attended = lax.all_to_all(attended, "pos", 0, 0, tiled=True)
+    attended, hops[2], out_bands = lax.optimization_barrier((attended, hops[2], out_bands))
+    for step in range(3, far):
+        hops[step] = hop(step, hops[step - 1])
+    partial_value = project(out_ids, attended, out_bands, rows)
+    theirs = lax.ppermute(partial_value, "head", swap_perm(2))
+    theirs, hops = lax.optimization_barrier((theirs, hops))
+    own_cols, normed, normed_other = normalise(
+        place, partial_value, theirs, latent_array, norm_gain[None, :]
+    )
     kv_bands = [kv_own, kv_near]
     kv_at = [p, p ^ 1]
-    shifts = sorted(range(far), key=lambda k: min(k, far - k))
-    moved = {}
-    for k in shifts[1:-1]:
-        moved[k] = lax.ppermute(kv_sent, "pos", shift_perm(pos, k))
-    attended = encode(head_queries, kv, head_bias, pos)
-    attended, kv_sent, moved = lax.optimization_barrier((attended, kv_sent, moved))
-    moved[shifts[-1]] = lax.ppermute(kv_sent, "pos", shift_perm(pos, shifts[-1]))
-    attended = lax.all_to_all(attended, "pos", 0, 0, tiled=True)
-    attended, moved = lax.optimization_barrier((attended, moved))
-
-    partial_value = project(attended, out_all, rows, out_depth)
-    theirs = lax.ppermute(partial_value, "head", swap_perm(2))
-    own_cols, normed, normed_other = normalise(
-        place, partial_value, theirs, latent_array, norm_gain[None, :]
-    )
-    for k in shifts[1:]:
-        kv_bands += [moved[k], lax.ppermute(moved[k], "groups", swap_perm(groups))]
+    for k in range(1, far):
+        moved = jnp.where(z + k < far, hops[k][1], hops[far - k][0])
+        kv_bands += [moved, over_groups(moved)]
         there = ((z + k) % far) * 2
         kv_at += [there + (y ^ x), there + (1 - (y ^ x))]
-    kv_weights = jnp.concatenate(kv_bands)
     kv_ids = jnp.stack([place, *kv_at]).astype(jnp.int32)
 
     counts = kv.reshape(pos, tokens + EXTRA, pair)[:, tokens + id_rows, : 2 * mods]
@@ -580,37 +636,25 @@
     ranked = jnp.sum((within + before[None, :]) * q_onehot, axis=1)
     limits = jnp.sum(q_onehot * query_counts[None, :], axis=1)
     kept = ranked < limits
-    lookup = jnp.dot(q_onehot.astype(jnp.bfloat16), query_table, preferred_element_type=jnp.float32)
-    queries = (query_features.astype(jnp.float32) + lookup).astype(jnp.bfloat16)
-
-    own_queries = columns((queries,), y)
-    near_queries = lax.ppermute(columns((queries,), 1 - y), "pos", near)
-
-    def across(value):
-        return lax.ppermute(value, "pos", near)
-
     def cores(values):
         return [lax.ppermute(v, "head", swap_perm(2)) for v in values]
 
-    early = [lax.ppermute(normed, "pos", shift_perm(pos, k)) for k in shifts[1:-1]]
-    first = [normed, across(normed), *early]
-    first = lax.optimization_barrier(first)
-    late = lax.ppermute(first[0], "pos", shift_perm(pos, shifts[-1]))
-    first_other = [normed_other, *cores(first[1:])]
-    second = [across(v) for v in first[2:]]
-    keys_values = latent_keys_values(
-        kv_ids, first + second, first_other + cores(second), kv_weights
-    )
-    near_state = decode(near_queries, keys_values, None, None)
-    own_state = decode(own_queries, keys_values, None, None)
-    late_near, near_state, own_state = lax.optimization_barrier(
-        (across(late), near_state, own_state)
-    )
-    last = [late, late_near]
-    last_other = cores(last)
-    keys_values = latent_keys_values(kv_ids, last, last_other, kv_weights)
-    near_state = decode(near_queries, keys_values, near_state, jnp.bfloat16)
-    own_state = decode(own_queries, keys_values, own_state, jnp.float32)
+    def fold(mine, other, states, types):
+        keys_values = latent_keys_values(kv_ids, mine, other, kv_bands)
+        return [
+            decode(q, keys_values, state, kind)
+            for q, state, kind in zip((near_queries, own_queries), states, types)
+        ]
+
+    first = [normed, over_near(normed), *[over_far(normed, k) for k in shifts[1:-1]]]
+    first, kept = lax.optimization_barrier((first, kept))
+    second = [over_far(first[0], shifts[-1]), *[over_near(v) for v in first[2:]]]
+    states = fold(first, [normed_other, *cores(first[1:])], [None, None], [None, None])
+    second, states = lax.optimization_barrier((second, states))
+    last = over_near(second[0])
+    states = fold(second, cores(second), states, [None, None])
+    last, states = lax.optimization_barrier((last, states))
+    near_state, own_state = fold([last], cores([last]), states, [jnp.bfloat16, jnp.float32])
     from_near = lax.ppermute(near_state, "pos", near).astype(jnp.float32)
     decoded = jnp.where(
         y == 0,
@@ -633,7 +677,7 @@
         and enc_keys.shape[0] % (2 * HEAD_DIM) == 0
         and enc_keys.shape[0] < 2048
         and w_key.shape[0] % LANES == 0
-        and w_out.shape[0] % (LANES * groups) == 0
+        and w_out.shape[0] % (2 * LANES) == 0
         and w_out.shape[1] % LANES == 0
         and latent_array.shape[0] % LANES == 0
     )

time: 317 us -> 297 us (0.937)
  waiting for transfers between devices: 166 us -> 132 us
  Pallas kernels: 57.3 us -> 75.5 us
  between operations: 14.4 us -> 1.22 us
  starting transfers between devices: 39.9 us -> 48.4 us
    all_to_all x1, waiting for transfers between devices: 31.5 us -> 0.01 us  [fast_on_device(): kv = lax.all_to_all(payload, 'pos', 0, 0, tiled=True)]
    pallas_call x4 -> x6, Pallas kernels: 17.8 us -> 33.8 us  [decode(): pl.pallas_call(functools.partial(decode_kernel, first, last), grid=(steps...]
    ppermute x15 -> x25, starting transfers between devices: 24 us -> 35.2 us  [the longest x6 10.8 us: over_far(): return lax.ppermute(value, 'pos', shift_perm(pos, k))]
    ppermute x1, waiting for transfers between devices: 4.28 us -> 0.01 us  [fast_on_device(): theirs = lax.ppermute(partial_value, 'head', swap_perm(2))]
    ppermute x7, waiting for transfers between devices: 0.02 us -> 3.85 us  [cores(): return [lax.ppermute(v, 'head', swap_perm(2)) for v in values]]
    unnamed x57 -> x82, local copies, waits for them, and re-layouts: 22.4 us -> 18.8 us
    ppermute x15 -> x25, waiting for transfers between devices: 122 us -> 120 us  [the longest x6 36.5 us: over_far(): return lax.ppermute(value, 'pos', shift_perm(pos, k))]
    pallas_call x2 -> x3, Pallas kernels: 17.5 us -> 18.3 us  [latent_keys_values(): pl.pallas_call(functools.partial(latents_kernel, pieces), grid_spec=grid_...]
  transfers between devices with their start and end apart: 27 -> 36, of which waited for: 12 -> 18; matrix products, arithmetic and copies ran while one was open for 7% -> 6% of each run, Pallas kernels for 13% -> 19%
where the time goes in v4:
time: 297 us; the launch traced here: 296 us
  waiting for transfers between devices  132 us (44%)
  Pallas kernels  75.5 us (25%)
  starting transfers between devices  48.4 us (16%)
  local copies, waits for them, and re-layouts  27.6 us (9%)
  other arithmetic  9 us (3%)
    ppermute x6, waiting for transfers between devices, over_far(): return lax.ppermute(value, 'pos', shift_perm(pos, k))  36.5 us
    ppermute x9, waiting for transfers between devices, over_near(): return lax.ppermute(value, 'pos', near)  35.9 us
    pallas_call x6, Pallas kernels, decode(): pl.pallas_call(functools.partial(decode_kernel, first, last), grid=(steps...  33.8 us
    ppermute x6, waiting for transfers between devices, hop(): lax.ppermute(v, 'pos', hop_perm(pos, step, way))  31.7 us
    unnamed x82, local copies, waits for them, and re-layouts  18.8 us
    pallas_call x3, Pallas kernels, latent_keys_values(): pl.pallas_call(functools.partial(latents_kernel, pieces), grid_spec=grid_...  18.3 us
    ppermute x4, waiting for transfers between devices, over_groups(): return lax.ppermute(value, 'groups', swap_perm(groups))  16.1 us
    pallas_call x1, Pallas kernels, encode(): pl.pallas_call(functools.partial(encode_kernel, pos, tokens), grid=(laten...  13 us
  transfers between devices with their start and end apart: 36, of which 18 were waited for; matrix products, arithmetic and copies ran while one was open for 6% of the time, Pallas kernels for 19%

profile of v4, /device:TPU:0, one launch (start us, length us, event | category | flops | bytes accessed | tf_op | source)
XLA Modules:
  0.0 295.8 jit_solution(1869796482791937165)
XLA Ops:
  4.7 3.5 %pack_heads.1 = bf16[4224,256]{1,0:T(8,128)(2,1)} custom-call(bf16[512,1024]{1,0:T(8,128)(2,1)S(1)} %copy-done.11, bf16[512,1024]{1,0:T(8,128)(2,1)S(1)} %copy-done.12, bf16[16,256]{1,0:T(8,128)(2,1)S(1)} %fusion.5.extra_ref), custom_call_target="tpu_custom_call" | custom-call | bytes 4194304 | tf_op jit(solution)/shard_map/pack_heads/pallas_call | solution.py:208
  8.2 7.4 %all-to-all-start = ((bf16[8,528,256]{2,1,0:T(8,128)(2,1)}), bf16[8,528,256]{2,1,0:T(8,128)(2,1)S(1)}, u32[]{:S(2)}, u32[]{:S(2)}) async-start(bf16[8,528,256]{2,1,0:T(8,128)(2,1)} %bitcast.12), calls=%async_computation | async-start | bytes 4325376 | tf_op jit(solution)/shard_map/all_to_all | solution.py:590
  15.6 2.0 collective-permute-start.5
  17.7 1.8 constant_dynamic-slice_fusion.6
  19.7 1.7 add_convert_fusion
  22.5 1.9 collective-permute-start.1
  24.5 1.7 constant_dynamic-slice_fusion.2
  26.1 2.4 collective-permute-start.4
  28.5 1.5 collective-permute-start.3
  30.1 1.9 constant_dynamic-slice_fusion.8.q_ref
  32.0 33.1 %collective-permute-done.refs_9_.refs_7_.refs_3_ = bf16[256,1024]{1,0:T(8,128)(2,1)S(1)} collective-permute-done((bf16[256,1024]{1,0:T(8,128)(2,1)S(1)}, bf16[256,1024]{1,0:T(8,128)(2,1)S(1)}, u32[]{:S(2)}, u32[]{:S(2)}) %collective-permute-start) | collective-permute-done | bytes 524320 | tf_op jit(solution)/shard_map/ppermute | solution.py:545
  65.1 3.2 %collective-permute-start.2 = (bf16[512,256]{1,0:T(8,128)(2,1)}, bf16[512,256]{1,0:T(8,128)(2,1)S(1)}, u32[]{:S(2)}, u32[]{:S(2)}) collective-permute-start(bf16[512,256]{1,0:T(8,128)(2,1)} %constant_dynamic-slice_fusion.2), channel_id=1, source_target_pairs={{4,0},{6,2},{8,4},{10,6},{12,8},{14,10},{0,12},{2,14},{5,1},{7,3},... | collective-permute-start | bytes 786440 | tf_op jit(solution)/shard_map/ppermute | solution.py:548
  68.3 2.0 pad_maximum_fusion
  70.2 13.4 %collective-permute-done.4 = bf16[512,256]{1,0:T(8,128)(2,1)} collective-permute-done((bf16[512,256]{1,0:T(8,128)(2,1)}, bf16[512,256]{1,0:T(8,128)(2,1)}, u32[]{:S(2)}, u32[]{:S(2)}) %collective-permute-start.4) | collective-permute-done | bytes 262176 | tf_op jit(solution)/shard_map/ppermute | solution.py:548
  83.7 3.9 %collective-permute-done.2 = bf16[512,256]{1,0:T(8,128)(2,1)S(1)} collective-permute-done((bf16[512,256]{1,0:T(8,128)(2,1)}, bf16[512,256]{1,0:T(8,128)(2,1)S(1)}, u32[]{:S(2)}, u32[]{:S(2)}) %collective-permute-start.2) | collective-permute-done | bytes 262176 | tf_op jit(solution)/shard_map/ppermute | solution.py:548
  88.3 1.3 collective-permute-start.7
  89.6 4.6 %collective-permute-start.6 = (bf16[256,1024]{1,0:T(8,128)(2,1)}, bf16[256,1024]{1,0:T(8,128)(2,1)S(1)}, u32[]{:S(2)}, u32[]{:S(2)}) collective-permute-start(bf16[256,1024]{1,0:T(8,128)(2,1)} %get-tuple-element.60), channel_id=1, source_target_pairs={{0,4},{2,6},{4,8},{6,10},{8,12},{10,14},{1,5},{3,7},{5,9},{7,11},{... | collective-permute-start | bytes 1572872 | tf_op jit(solution)/shard_map/ppermute | solution.py:602
  97.1 1.6 collective-permute-start.9
  100.0 13.0 %encode_head.1 = bf16[2048,128]{1,0:T(8,128)(2,1)S(1)} custom-call(bf16[2048,128]{1,0:T(8,128)(2,1)S(1)} %copy-done.23, bf16[4224,256]{1,0:T(8,128)(2,1)S(1)} %bitcast.43, f32[3]{0:T(128)S(1)} %fusion.8.bias_ref), custom_call_target="tpu_custom_call" | custom-call | flops 17179869184 | bytes 2162688 | tf_op jit(solution)/shard_map/encode_head/pallas_call | solution.py:255
  113.0 3.0 %collective-permute-done.9.refs_3_ = bf16[1536,256]{1,0:T(8,128)(2,1)} collective-permute-done((bf16[1536,256]{1,0:T(8,128)(2,1)S(1)}, bf16[1536,256]{1,0:T(8,128)(2,1)}, u32[]{:S(2)}, u32[]{:S(2)}) %collective-permute-start.9) | collective-permute-done | bytes 786464 | tf_op jit(solution)/shard_map/ppermute | solution.py:542
  118.1 3.5 %all-to-all-start.1 = ((bf16[8,256,128]{2,1,0:T(8,128)(2,1)}), bf16[8,256,128]{2,1,0:T(8,128)(2,1)S(1)}, u32[]{:S(2)}, u32[]{:S(2)}) async-start(bf16[8,256,128]{2,1,0:T(8,128)(2,1)} %bitcast.45), calls=%async_computation.1 | async-start | bytes 1048576 | tf_op jit(solution)/shard_map/all_to_all | solution.py:611
  121.6 1.9 collective-permute-start.12
  124.2 1.3 collective-permute-start.11
  125.7 17.6 %collective-permute-done.11 = bf16[256,1024]{1,0:T(8,128)(2,1)} collective-permute-done((bf16[256,1024]{1,0:T(8,128)(2,1)}, bf16[256,1024]{1,0:T(8,128)(2,1)}, u32[]{:S(2)}, u32[]{:S(2)}) %collective-permute-start.11) | collective-permute-done | bytes 524320 | tf_op jit(solution)/shard_map/ppermute | solution.py:602
  143.2 1.7 collective-permute-done.12.refs_5_
  151.2 3.4 %project_rows.1.mine_ref = f32[256,2048]{1,0:T(8,128)S(1)} custom-call(s32[10]{0:T(128)S(1)} %stack.67.ids_ref, bf16[2048,128]{1,0:T(8,128)(2,1)S(1)} %bitcast.44, bf16[1024,256]{1,0:T(8,128)(2,1)} %refs_0_, bf16[1024,256]{1,0:T(8,128)(2,1)} %collective-permute-done.5.refs_1_, bf16[1536,256]{1,0:T(8,128)(2,1)S(1)} %copy-done.10, ...), custom_call_target="tpu_custom_call" | custom-call | flops 1073741824 | bytes 6291456 | tf_op jit(solution)/shard_map/project_rows/pallas_call | solution.py:307
  156.8 1.3 collective-permute-start.15
  159.0 14.1 %collective-permute-done.15 = bf16[256,1024]{1,0:T(8,128)(2,1)S(1)} collective-permute-done((bf16[256,1024]{1,0:T(8,128)(2,1)}, bf16[256,1024]{1,0:T(8,128)(2,1)S(1)}, u32[]{:S(2)}, u32[]{:S(2)}) %collective-permute-start.15) | collective-permute-done | bytes 524320 | tf_op jit(solution)/shard_map/ppermute | solution.py:602
  174.4 3.5 %norm_rows.1 = (f32[256,1024]{1,0:T(8,128)}, bf16[256,1024]{1,0:T(8,128)(2,1)S(1)}, bf16[256,1024]{1,0:T(8,128)(2,1)S(1)}) custom-call(s32[1]{0:T(128)} %bitcast.ids_ref, f32[256,2048]{1,0:T(8,128)S(1)} %project_rows.1.mine_ref, f32[256,2048]{1,0:T(8,128)} %collective-permute-done.13.theirs_ref, bf16[256,2048]{1,0:T(8,128)(2,1)S(1)} %copy-done.13, ...), custom_call_target="tpu_custom_call" | custom-call | flops 3145728 | bytes 6815744 | tf_op jit(solution)/shard_map/norm_rows/pallas_call | solution.py:341
  177.9 3.8 %collective-permute-start.17 = (bf16[256,1024]{1,0:T(8,128)(2,1)S(1)}, bf16[256,1024]{1,0:T(8,128)(2,1)}, u32[]{:S(2)}, u32[]{:S(2)}) collective-permute-start(bf16[256,1024]{1,0:T(8,128)(2,1)S(1)} %get-tuple-element.84.refs_0_), channel_id=1, source_target_pairs={{4,0},{6,2},{8,4},{10,6},{12,8},{14,10},{0,12},{2,14},{5,1},{7,3},... | collective-permute-start | bytes 1572872 | tf_op jit(solution)/shard_map/ppermute | solution.py:548
  184.3 1.5 collective-permute-start.26
  185.9 8.7 %collective-permute-done.18.refs_3_ = bf16[256,1024]{1,0:T(8,128)(2,1)} collective-permute-done((bf16[256,1024]{1,0:T(8,128)(2,1)S(1)}, bf16[256,1024]{1,0:T(8,128)(2,1)}, u32[]{:S(2)}, u32[]{:S(2)}) %collective-permute-start.18) | collective-permute-done | bytes 524320 | tf_op jit(solution)/shard_map/ppermute | solution.py:548
  195.2 7.6 %collective-permute-done.17.refs_2_ = bf16[256,1024]{1,0:T(8,128)(2,1)} collective-permute-done((bf16[256,1024]{1,0:T(8,128)(2,1)S(1)}, bf16[256,1024]{1,0:T(8,128)(2,1)}, u32[]{:S(2)}, u32[]{:S(2)}) %collective-permute-start.17) | collective-permute-done | bytes 524320 | tf_op jit(solution)/shard_map/ppermute | solution.py:548
  203.5 5.3 %collective-permute-done.26.refs_13_.refs_11_.refs_7_ = bf16[256,1024]{1,0:T(8,128)(2,1)} collective-permute-done((bf16[256,1024]{1,0:T(8,128)(2,1)S(1)}, bf16[256,1024]{1,0:T(8,128)(2,1)}, u32[]{:S(2)}, u32[]{:S(2)}) %collective-permute-start.26) | collective-permute-done | bytes 524320 | tf_op jit(solution)/shard_map/ppermute | solution.py:542
  210.1 7.8 %collective-permute-done.25.refs_11_.refs_9_.refs_5_ = bf16[256,1024]{1,0:T(8,128)(2,1)} collective-permute-done((bf16[256,1024]{1,0:T(8,128)(2,1)S(1)}, bf16[256,1024]{1,0:T(8,128)(2,1)}, u32[]{:S(2)}, u32[]{:S(2)}) %collective-permute-start.25) | collective-permute-done | bytes 524320 | tf_op jit(solution)/shard_map/ppermute | solution.py:542
  221.2 8.7 %latent_keys_values.3.refs_1_.refs_2_ = bf16[1024,1024]{1,0:T(8,128)(2,1)S(1)} custom-call(s32[9]{0:T(128)S(1)} %stack.74.ids_ref, bf16[256,1024]{1,0:T(8,128)(2,1)S(1)} %copy-done.26, bf16[256,1024]{1,0:T(8,128)(2,1)} %collective-permute-done.16.refs_1_, bf16[256,1024]{1,0:T(8,128)(2,1)} %collective-permute-done.17.refs_2_, ...), custom_call_target="tpu_custom_call" | custom-call | flops 4294967296 | bytes 4194304 | tf_op jit(solution)/shard_map/latent_keys_values/pallas_call | solution.py:398
  230.0 3.8 %decode_rows.7 = (f32[512,512]{1,0:T(8,128)S(1)}, f32[512,1024]{1,0:T(8,128)S(1)}) custom-call(bf16[512,512]{1,0:T(8,128)(2,1)S(1)} %copy-done.7, bf16[1024,1024]{1,0:T(8,128)(2,1)S(1)} %latent_keys_values.3.refs_1_.refs_2_, bf16[1024,1024]{1,0:T(8,128)(2,1)S(1)} %latent_keys_values.3.refs_1_.refs_2_), custom_call_target="tpu_custom_call" | custom-call | flops 4294967296 | bytes 6291456 | tf_op jit(solution)/shard_map/decode_rows/pallas_call | solution.py:477
  233.8 4.5 %decode_rows.6 = (f32[512,512]{1,0:T(8,128)S(1)}, f32[512,1024]{1,0:T(8,128)S(1)}) custom-call(bf16[512,512]{1,0:T(8,128)(2,1)} %collective-permute-done.1.refs_0_, bf16[1024,1024]{1,0:T(8,128)(2,1)S(1)} %latent_keys_values.3.refs_1_.refs_2_, bf16[1024,1024]{1,0:T(8,128)(2,1)S(1)} %latent_keys_values.3.refs_1_.refs_2_), custom_call_target="tpu_custom_call" | custom-call | flops 4294967296 | bytes 6291456 | tf_op jit(solution)/shard_map/decode_rows/pallas_call | solution.py:477
  238.3 2.8 collective-permute-done.19.refs_0_
  244.6 6.2 %latent_keys_values.4.refs_1_.refs_2_ = bf16[768,1024]{1,0:T(8,128)(2,1)S(1)} custom-call(s32[9]{0:T(128)S(1)} %stack.74.ids_ref, bf16[256,1024]{1,0:T(8,128)(2,1)S(1)} %collective-permute-done.19.refs_0_, bf16[256,1024]{1,0:T(8,128)(2,1)S(1)} %collective-permute-done.20.refs_1_, bf16[256,1024]{1,0:T(8,128)(2,1)S(1)} %collective-permute-done.21.refs_2_, ...), custom_call_target="tpu_custom_call" | custom-call | flops 3221225472 | bytes 4194304 | tf_op jit(solution)/shard_map/latent_keys_values/pallas_call | solution.py:398
  250.8 7.6 %decode_rows.9 = (f32[512,512]{1,0:T(8,128)S(1)}, f32[512,1024]{1,0:T(8,128)S(1)}) custom-call(bf16[512,512]{1,0:T(8,128)(2,1)S(1)} %copy-done.7, bf16[768,1024]{1,0:T(8,128)(2,1)S(1)} %latent_keys_values.4.refs_1_.refs_2_, bf16[768,1024]{1,0:T(8,128)(2,1)S(1)} %latent_keys_values.4.refs_1_.refs_2_, f32[512,512]{1,0:T(8,128)S(1)} %get-tuple-element.107.refs_3_, ...), custom_call_target="tpu_custom_call" | custom-call | flops 3221225472 | bytes 5767168 | tf_op jit(solution)/shard_map/decode_rows/pallas_call | solution.py:477
  259.4 8.4 %decode_rows.8 = (f32[512,512]{1,0:T(8,128)S(1)}, f32[512,1024]{1,0:T(8,128)S(1)}) custom-call(bf16[512,512]{1,0:T(8,128)(2,1)} %collective-permute-done.1.refs_0_, bf16[768,1024]{1,0:T(8,128)(2,1)S(1)} %latent_keys_values.4.refs_1_.refs_2_, bf16[768,1024]{1,0:T(8,128)(2,1)S(1)} %latent_keys_values.4.refs_1_.refs_2_, ...), custom_call_target="tpu_custom_call" | custom-call | flops 3221225472 | bytes 5767168 | tf_op jit(solution)/shard_map/decode_rows/pallas_call | solution.py:477
  268.1 1.8 collective-permute-done.32.refs_1_
  269.8 3.4 %latent_keys_values.5.refs_1_.refs_2_ = bf16[256,1024]{1,0:T(8,128)(2,1)S(1)} custom-call(s32[9]{0:T(128)S(1)} %stack.74.ids_ref, bf16[256,1024]{1,0:T(8,128)(2,1)S(1)} %collective-permute-done.28.refs_0_, bf16[256,1024]{1,0:T(8,128)(2,1)S(1)} %collective-permute-done.32.refs_1_, bf16[256,1024]{1,0:T(8,128)(2,1)S(1)} %get-tuple-element.120.refs_8_.refs_6_.refs_2_, ...), custom_call_target="tpu_custom_call" | custom-call | flops 1073741824 | bytes 4194304 | tf_op jit(solution)/shard_map/latent_keys_values/pallas_call | solution.py:398
  273.3 5.5 %decode_rows.11 = bf16[512,512]{1,0:T(8,128)(2,1)} custom-call(bf16[512,512]{1,0:T(8,128)(2,1)} %collective-permute-done.1.refs_0_, bf16[256,1024]{1,0:T(8,128)(2,1)S(1)} %latent_keys_values.5.refs_1_.refs_2_, bf16[256,1024]{1,0:T(8,128)(2,1)S(1)} %latent_keys_values.5.refs_1_.refs_2_, f32[512,512]{1,0:T(8,128)S(1)} %get-tuple-element.114.refs_3_, ...), custom_call_target="tpu_custom_call" | custom-call | flops 1073741824 | bytes 4718592 | tf_op jit(solution)/shard_map/decode_rows/pallas_call | solution.py:477
  280.8 4.0 %decode_rows.10 = f32[512,512]{1,0:T(8,128)S(1)} custom-call(bf16[512,512]{1,0:T(8,128)(2,1)S(1)} %copy-done.8, bf16[256,1024]{1,0:T(8,128)(2,1)S(1)} %latent_keys_values.5.refs_1_.refs_2_, bf16[256,1024]{1,0:T(8,128)(2,1)S(1)} %latent_keys_values.5.refs_1_.refs_2_, f32[512,512]{1,0:T(8,128)S(1)} %copy-done.15, f32[512,1024]{1,0:T(8,128)S(1)} %copy-done.4), custom_call_target="tpu_custom_call" | custom-call | flops 1073741824 | bytes 4718592 | tf_op jit(solution)/shard_map/decode_rows/pallas_call | solution.py:477
  284.8 8.3 %collective-permute-done.33 = bf16[512,512]{1,0:T(8,128)(2,1)} collective-permute-done((bf16[512,512]{1,0:T(8,128)(2,1)}, bf16[512,512]{1,0:T(8,128)(2,1)}, u32[]{:S(2)}, u32[]{:S(2)}) %collective-permute-start.33) | collective-permute-done | bytes 524320 | tf_op jit(solution)/shard_map/ppermute | solution.py:658
  294.2 1.6 fusion
  (152 shorter events, 40.1 us)
Async XLA Ops:
  0.6 19.1 %copy-start = (bf16[3,1024]{1,0:T(4,128)(2,1)S(1)}, bf16[3,1024]{1,0:T(4,128)(2,1)}, u32[]{:S(2)}) copy-start(bf16[3,1024]{1,0:T(4,128)(2,1)} %param.25) | copy-start | bytes 18436
  8.2 9.4 %copy-start.35 = (bf16[256,1024]{1,0:T(8,128)(2,1)S(1)}, bf16[256,1024]{1,0:T(8,128)(2,1)}, u32[]{:S(2)}) copy-start(bf16[256,1024]{1,0:T(8,128)(2,1)} %param.22) | copy-start | bytes 1572868
  8.2 80.1 %all-to-all-start = ((bf16[8,528,256]{2,1,0:T(8,128)(2,1)}), bf16[8,528,256]{2,1,0:T(8,128)(2,1)S(1)}, u32[]{:S(2)}, u32[]{:S(2)}) async-start(bf16[8,528,256]{2,1,0:T(8,128)(2,1)} %bitcast.12), calls=%async_computation | async-start | bytes 4325376 | tf_op jit(solution)/shard_map/all_to_all | solution.py:590
  15.6 72.0 %collective-permute-start.5 = (bf16[1024,256]{1,0:T(8,128)(2,1)}, bf16[1024,256]{1,0:T(8,128)(2,1)}, u32[]{:S(2)}, u32[]{:S(2)}) collective-permute-start(bf16[1024,256]{1,0:T(8,128)(2,1)} %refs_0_), channel_id=1, source_target_pairs={{0,2},{2,0},{4,6},{6,4},{8,10},{10,8},{12,14},{14,12},{1,3},{3,1},... | collective-permute-start | bytes 1572872 | tf_op jit(solution)/shard_map/ppermute | solution.py:545
  19.5 10.4 %copy-start.38 = (f32[3,8]{1,0:T(4,128)S(1)}, f32[3,8]{1,0:T(4,128)}, u32[]{:S(2)}) copy-start(f32[3,8]{1,0:T(4,128)} %param.26) | copy-start | bytes 292
  19.6 45.5 %collective-permute-start = (bf16[256,1024]{1,0:T(8,128)(2,1)S(1)}, bf16[256,1024]{1,0:T(8,128)(2,1)S(1)}, u32[]{:S(2)}, u32[]{:S(2)}) collective-permute-start(bf16[256,1024]{1,0:T(8,128)(2,1)S(1)} %pad_maximum_fusion.1), channel_id=1, source_target_pairs={{0,2},{2,0},{4,6},{6,4},{8,10},{10,8},{12,14},{14,12},{1,3},{3,1},... | collective-permute-start | bytes 1572872 | tf_op jit(solution)/shard_map/ppermute | solution.py:545
  22.5 65.8 %collective-permute-start.1 = (bf16[512,512]{1,0:T(8,128)(2,1)}, bf16[512,512]{1,0:T(8,128)(2,1)}, u32[]{:S(2)}, u32[]{:S(2)}) collective-permute-start(bf16[512,512]{1,0:T(8,128)(2,1)} %get-tuple-element.119), channel_id=1, source_target_pairs={{0,2},{2,0},{4,6},{6,4},{8,10},{10,8},{12,14},{14,12},{1,3},{3,1},... | collective-permute-start | bytes 1572872 | tf_op jit(solution)/shard_map/ppermute | solution.py:545
  26.1 57.5 %collective-permute-start.4 = (bf16[512,256]{1,0:T(8,128)(2,1)}, bf16[512,256]{1,0:T(8,128)(2,1)}, u32[]{:S(2)}, u32[]{:S(2)}) collective-permute-start(bf16[512,256]{1,0:T(8,128)(2,1)} %constant_dynamic-slice_fusion.2), channel_id=1, source_target_pairs={{8,0},{10,2},{12,4},{14,6},{0,8},{2,10},{4,12},{6,14},{9,1},{11,3}... | collective-permute-start | bytes 786440 | tf_op jit(solution)/shard_map/ppermute | solution.py:548
  28.5 55.2 %collective-permute-start.3 = (bf16[512,256]{1,0:T(8,128)(2,1)}, bf16[512,256]{1,0:T(8,128)(2,1)}, u32[]{:S(2)}, u32[]{:S(2)}) collective-permute-start(bf16[512,256]{1,0:T(8,128)(2,1)} %constant_dynamic-slice_fusion.2), channel_id=1, source_target_pairs={{12,0},{14,2},{0,4},{2,6},{4,8},{6,10},{8,12},{10,14},{13,1},{15,3... | collective-permute-start | bytes 786440 | tf_op jit(solution)/shard_map/ppermute | solution.py:548
  65.1 22.5 %collective-permute-start.2 = (bf16[512,256]{1,0:T(8,128)(2,1)}, bf16[512,256]{1,0:T(8,128)(2,1)S(1)}, u32[]{:S(2)}, u32[]{:S(2)}) collective-permute-start(bf16[512,256]{1,0:T(8,128)(2,1)} %constant_dynamic-slice_fusion.2), channel_id=1, source_target_pairs={{4,0},{6,2},{8,4},{10,6},{12,8},{14,10},{0,12},{2,14},{5,1},{7,3},... | collective-permute-start | bytes 786440 | tf_op jit(solution)/shard_map/ppermute | solution.py:548
  88.3 24.7 %copy-start.2 = (bf16[8,528,256]{2,1,0:T(8,128)(2,1)}, bf16[8,528,256]{2,1,0:T(8,128)(2,1)S(1)}, u32[]{:S(2)}) copy-start(bf16[8,528,256]{2,1,0:T(8,128)(2,1)S(1)} %all-to-all-done) | copy-start | bytes 6488068
  88.3 24.7 %collective-permute-start.7 = (bf16[256,1024]{1,0:T(8,128)(2,1)}, bf16[256,1024]{1,0:T(8,128)(2,1)S(1)}, u32[]{:S(2)}, u32[]{:S(2)}) collective-permute-start(bf16[256,1024]{1,0:T(8,128)(2,1)} %get-tuple-element.60), channel_id=1, source_target_pairs={{12,8},{14,10},{8,4},{10,6},{4,0},{6,2},{13,9},{15,11},{9,5},{11,7... | collective-permute-start | bytes 1572872 | tf_op jit(solution)/shard_map/ppermute | solution.py:602
  89.6 23.4 %collective-permute-start.6 = (bf16[256,1024]{1,0:T(8,128)(2,1)}, bf16[256,1024]{1,0:T(8,128)(2,1)S(1)}, u32[]{:S(2)}, u32[]{:S(2)}) collective-permute-start(bf16[256,1024]{1,0:T(8,128)(2,1)} %get-tuple-element.60), channel_id=1, source_target_pairs={{0,4},{2,6},{4,8},{6,10},{8,12},{10,14},{1,5},{3,7},{5,9},{7,11},{... | collective-permute-start | bytes 1572872 | tf_op jit(solution)/shard_map/ppermute | solution.py:602
  97.1 15.9 %copy-start.9 = (bf16[1536,256]{1,0:T(8,128)(2,1)}, bf16[1536,256]{1,0:T(8,128)(2,1)S(1)}, u32[]{:S(2)}) copy-start(bf16[1536,256]{1,0:T(8,128)(2,1)S(1)} %constant_dynamic-update-slice_fusion.refs_2_) | copy-start | bytes 2359300
  97.1 19.0 %collective-permute-start.9 = (bf16[1536,256]{1,0:T(8,128)(2,1)S(1)}, bf16[1536,256]{1,0:T(8,128)(2,1)}, u32[]{:S(2)}, u32[]{:S(2)}) collective-permute-start(bf16[1536,256]{1,0:T(8,128)(2,1)S(1)} %constant_dynamic-update-slice_fusion.refs_2_), channel_id=1, source_target_pairs={{0,16},{16,0},{1,17},{17,1},{2,18},{18,2},{3,19},{19,3},{4,20},{20... | collective-permute-start | bytes 2359304 | tf_op jit(solution)/shard_map/ppermute | solution.py:542
  98.7 18.5 %collective-permute-start.8 = (bf16[1536,256]{1,0:T(8,128)(2,1)S(1)}, bf16[1536,256]{1,0:T(8,128)(2,1)S(1)}, u32[]{:S(2)}, u32[]{:S(2)}) collective-permute-start(bf16[1536,256]{1,0:T(8,128)(2,1)S(1)} %constant_dynamic-update-slice_fusion.refs_2_), channel_id=1, source_target_pairs={{0,2},{2,0},{4,6},{6,4},{8,10},{10,8},{12,14},{14,12},{1,3},{3,1},... | collective-permute-start | bytes 2359304 | tf_op jit(solution)/shard_map/ppermute | solution.py:545
  118.1 27.8 %all-to-all-start.1 = ((bf16[8,256,128]{2,1,0:T(8,128)(2,1)}), bf16[8,256,128]{2,1,0:T(8,128)(2,1)S(1)}, u32[]{:S(2)}, u32[]{:S(2)}) async-start(bf16[8,256,128]{2,1,0:T(8,128)(2,1)} %bitcast.45), calls=%async_computation.1 | async-start | bytes 1048576 | tf_op jit(solution)/shard_map/all_to_all | solution.py:611
  121.6 23.4 %collective-permute-start.12 = (bf16[1536,256]{1,0:T(8,128)(2,1)}, bf16[1536,256]{1,0:T(8,128)(2,1)S(1)}, u32[]{:S(2)}, u32[]{:S(2)}) collective-permute-start(bf16[1536,256]{1,0:T(8,128)(2,1)} %collective-permute-done.9.refs_3_), channel_id=1, source_target_pairs={{0,2},{2,0},{4,6},{6,4},{8,10},{10,8},{12,14},{14,12},{1,3},{3,1},... | collective-permute-start | bytes 2359304 | tf_op jit(solution)/shard_map/ppermute | solution.py:545
  123.5 2.2 collective-permute-start.10
  124.2 19.1 %collective-permute-start.11 = (bf16[256,1024]{1,0:T(8,128)(2,1)}, bf16[256,1024]{1,0:T(8,128)(2,1)}, u32[]{:S(2)}, u32[]{:S(2)}) collective-permute-start(bf16[256,1024]{1,0:T(8,128)(2,1)} %copy-done.29), channel_id=1, source_target_pairs={{8,4},{10,6},{4,0},{6,2},{9,5},{11,7},{5,1},{7,3},{24,20},{26,22},... | collective-permute-start | bytes 1572872 | tf_op jit(solution)/shard_map/ppermute | solution.py:602
  125.7 20.2 %copy-start.33 = (bf16[256,1024]{1,0:T(8,128)(2,1)}, bf16[256,1024]{1,0:T(8,128)(2,1)S(1)}, u32[]{:S(2)}) copy-start(bf16[256,1024]{1,0:T(8,128)(2,1)S(1)} %collective-permute-done.10) | copy-start | bytes 1572868
  151.2 22.0 %copy-start.24 = (f32[2048]{0:T(1024)S(1)}, f32[2048]{0:T(1024)}, u32[]{:S(2)}) copy-start(f32[2048]{0:T(1024)} %param.20) | copy-start | bytes 24580
  154.6 18.6 %collective-permute-start.13 = (f32[256,2048]{1,0:T(8,128)S(1)}, f32[256,2048]{1,0:T(8,128)}, u32[]{:S(2)}, u32[]{:S(2)}) collective-permute-start(f32[256,2048]{1,0:T(8,128)S(1)} %project_rows.1.mine_ref), channel_id=1, source_target_pairs={{0,1},{1,0},{2,3},{3,2},{4,5},{5,4},{6,7},{7,6},{8,9},{9,8},{10,11... | collective-permute-start | bytes 6291464 | tf_op jit(solution)/shard_map/ppermute | solution.py:616
  156.1 2.9 collective-permute-start.14
  156.8 16.4 %collective-permute-start.15 = (bf16[256,1024]{1,0:T(8,128)(2,1)}, bf16[256,1024]{1,0:T(8,128)(2,1)S(1)}, u32[]{:S(2)}, u32[]{:S(2)}) collective-permute-start(bf16[256,1024]{1,0:T(8,128)(2,1)} %collective-permute-done.11), channel_id=1, source_target_pairs={{4,0},{6,2},{5,1},{7,3},{20,16},{22,18},{21,17},{23,19}} | collective-permute-start | bytes 1572872 | tf_op jit(solution)/shard_map/ppermute | solution.py:602
  174.4 8.8 %copy-start.34 = (bf16[256,1024]{1,0:T(8,128)(2,1)S(1)}, bf16[256,1024]{1,0:T(8,128)(2,1)}, u32[]{:S(2)}) copy-start(bf16[256,1024]{1,0:T(8,128)(2,1)} %copy-done.33) | copy-start | bytes 1572868
  177.9 25.4 %copy-start.25 = (bf16[256,1024]{1,0:T(8,128)(2,1)}, bf16[256,1024]{1,0:T(8,128)(2,1)S(1)}, u32[]{:S(2)}) copy-start(bf16[256,1024]{1,0:T(8,128)(2,1)S(1)} %get-tuple-element.84.refs_0_) | copy-start | bytes 1572868
  177.9 16.7 %collective-permute-start.18 = (bf16[256,1024]{1,0:T(8,128)(2,1)S(1)}, bf16[256,1024]{1,0:T(8,128)(2,1)}, u32[]{:S(2)}, u32[]{:S(2)}) collective-permute-start(bf16[256,1024]{1,0:T(8,128)(2,1)S(1)} %get-tuple-element.84.refs_0_), channel_id=1, source_target_pairs={{12,0},{14,2},{0,4},{2,6},{4,8},{6,10},{8,12},{10,14},{13,1},{15,3... | collective-permute-start | bytes 1572872 | tf_op jit(solution)/shard_map/ppermute | solution.py:548
  177.9 24.9 %collective-permute-start.17 = (bf16[256,1024]{1,0:T(8,128)(2,1)S(1)}, bf16[256,1024]{1,0:T(8,128)(2,1)}, u32[]{:S(2)}, u32[]{:S(2)}) collective-permute-start(bf16[256,1024]{1,0:T(8,128)(2,1)S(1)} %get-tuple-element.84.refs_0_), channel_id=1, source_target_pairs={{4,0},{6,2},{8,4},{10,6},{12,8},{14,10},{0,12},{2,14},{5,1},{7,3},... | collective-permute-start | bytes 1572872 | tf_op jit(solution)/shard_map/ppermute | solution.py:548
  181.7 21.1 %collective-permute-start.16 = (bf16[256,1024]{1,0:T(8,128)(2,1)S(1)}, bf16[256,1024]{1,0:T(8,128)(2,1)}, u32[]{:S(2)}, u32[]{:S(2)}) collective-permute-start(bf16[256,1024]{1,0:T(8,128)(2,1)S(1)} %get-tuple-element.84.refs_0_), channel_id=1, source_target_pairs={{0,2},{2,0},{4,6},{6,4},{8,10},{10,8},{12,14},{14,12},{1,3},{3,1},... | collective-permute-start | bytes 1572872 | tf_op jit(solution)/shard_map/ppermute | solution.py:545
  182.5 20.8 %collective-permute-start.27 = (bf16[256,1024]{1,0:T(8,128)(2,1)S(1)}, bf16[256,1024]{1,0:T(8,128)(2,1)S(1)}, u32[]{:S(2)}, u32[]{:S(2)}) collective-permute-start(bf16[256,1024]{1,0:T(8,128)(2,1)S(1)} %broadcast_select_fusion.refs_14_.refs_12_.refs_8_), channel_id=1, source_target_pairs={{0,16},{16,0},{1,17},{17,1},{2,18},{18,2},{3,19},{19,3},{4,20},{20... | collective-permute-start | bytes 1572872 | tf_op jit(solution)/shard_map/ppermute | solution.py:542
  184.3 24.5 %collective-permute-start.26 = (bf16[256,1024]{1,0:T(8,128)(2,1)S(1)}, bf16[256,1024]{1,0:T(8,128)(2,1)}, u32[]{:S(2)}, u32[]{:S(2)}) collective-permute-start(bf16[256,1024]{1,0:T(8,128)(2,1)S(1)} %broadcast_select_fusion.1.refs_12_.refs_10_.refs_6_), channel_id=1, source_target_pairs={{0,16},{16,0},{1,17},{17,1},{2,18},{18,2},{3,19},{19,3},{4,20},{20... | collective-permute-start | bytes 1572872 | tf_op jit(solution)/shard_map/ppermute | solution.py:542
  194.6 23.2 %collective-permute-start.25 = (bf16[256,1024]{1,0:T(8,128)(2,1)S(1)}, bf16[256,1024]{1,0:T(8,128)(2,1)}, u32[]{:S(2)}, u32[]{:S(2)}) collective-permute-start(bf16[256,1024]{1,0:T(8,128)(2,1)S(1)} %broadcast_select_fusion.2.refs_10_.refs_8_.refs_4_), channel_id=1, source_target_pairs={{0,16},{16,0},{1,17},{17,1},{2,18},{18,2},{3,19},{19,3},{4,20},{20... | collective-permute-start | bytes 1572872 | tf_op jit(solution)/shard_map/ppermute | solution.py:542
  202.8 16.3 %collective-permute-start.22 = (bf16[256,1024]{1,0:T(8,128)(2,1)}, bf16[256,1024]{1,0:T(8,128)(2,1)}, u32[]{:S(2)}, u32[]{:S(2)}) collective-permute-start(bf16[256,1024]{1,0:T(8,128)(2,1)} %collective-permute-done.16.refs_1_), channel_id=1, source_target_pairs={{0,1},{1,0},{2,3},{3,2},{4,5},{5,4},{6,7},{7,6},{8,9},{9,8},{10,11... | collective-permute-start | bytes 1572872 | tf_op jit(solution)/shard_map/ppermute | solution.py:640
  202.8 16.3 %collective-permute-start.23 = (bf16[256,1024]{1,0:T(8,128)(2,1)}, bf16[256,1024]{1,0:T(8,128)(2,1)}, u32[]{:S(2)}, u32[]{:S(2)}) collective-permute-start(bf16[256,1024]{1,0:T(8,128)(2,1)} %collective-permute-done.17.refs_2_), channel_id=1, source_target_pairs={{0,1},{1,0},{2,3},{3,2},{4,5},{5,4},{6,7},{7,6},{8,9},{9,8},{10,11... | collective-permute-start | bytes 1572872 | tf_op jit(solution)/shard_map/ppermute | solution.py:640
  203.3 41.3 %copy-start.20 = (bf16[256,1024]{1,0:T(8,128)(2,1)}, bf16[256,1024]{1,0:T(8,128)(2,1)S(1)}, u32[]{:S(2)}) copy-start(bf16[256,1024]{1,0:T(8,128)(2,1)S(1)} %collective-permute-done.27.refs_15_.refs_13_.refs_9_) | copy-start | bytes 1572868
  203.3 15.8 %collective-permute-start.24 = (bf16[256,1024]{1,0:T(8,128)(2,1)}, bf16[256,1024]{1,0:T(8,128)(2,1)}, u32[]{:S(2)}, u32[]{:S(2)}) collective-permute-start(bf16[256,1024]{1,0:T(8,128)(2,1)} %collective-permute-done.18.refs_3_), channel_id=1, source_target_pairs={{0,1},{1,0},{2,3},{3,2},{4,5},{5,4},{6,7},{7,6},{8,9},{9,8},{10,11... | collective-permute-start | bytes 1572872 | tf_op jit(solution)/shard_map/ppermute | solution.py:640
  208.8 32.4 %collective-permute-start.20 = (bf16[256,1024]{1,0:T(8,128)(2,1)}, bf16[256,1024]{1,0:T(8,128)(2,1)S(1)}, u32[]{:S(2)}, u32[]{:S(2)}) collective-permute-start(bf16[256,1024]{1,0:T(8,128)(2,1)} %collective-permute-done.17.refs_2_), channel_id=1, source_target_pairs={{0,2},{2,0},{4,6},{6,4},{8,10},{10,8},{12,14},{14,12},{1,3},{3,1},... | collective-permute-start | bytes 1572872 | tf_op jit(solution)/shard_map/ppermute | solution.py:545
  217.8 23.3 %collective-permute-start.21 = (bf16[256,1024]{1,0:T(8,128)(2,1)}, bf16[256,1024]{1,0:T(8,128)(2,1)S(1)}, u32[]{:S(2)}, u32[]{:S(2)}) collective-permute-start(bf16[256,1024]{1,0:T(8,128)(2,1)} %collective-permute-done.18.refs_3_), channel_id=1, source_target_pairs={{0,2},{2,0},{4,6},{6,4},{8,10},{10,8},{12,14},{14,12},{1,3},{3,1},... | collective-permute-start | bytes 1572872 | tf_op jit(solution)/shard_map/ppermute | solution.py:545
  219.1 22.1 %collective-permute-start.19 = (bf16[256,1024]{1,0:T(8,128)(2,1)}, bf16[256,1024]{1,0:T(8,128)(2,1)S(1)}, u32[]{:S(2)}, u32[]{:S(2)}) collective-permute-start(bf16[256,1024]{1,0:T(8,128)(2,1)} %copy-done.25), channel_id=1, source_target_pairs={{8,0},{10,2},{12,4},{14,6},{0,8},{2,10},{4,12},{6,14},{9,1},{11,3}... | collective-permute-start | bytes 1572872 | tf_op jit(solution)/shard_map/ppermute | solution.py:548
  221.2 8.7 %copy-start.7 = (bf16[512,512]{1,0:T(8,128)(2,1)S(1)}, bf16[512,512]{1,0:T(8,128)(2,1)}, u32[]{:S(2)}) copy-start(bf16[512,512]{1,0:T(8,128)(2,1)} %get-tuple-element.118.refs_0_) | copy-start | bytes 1572868
  241.2 1.9 collective-permute-start.30
  241.2 2.6 collective-permute-start.31
  241.7 2.9 collective-permute-start.29
  241.7 26.1 %collective-permute-start.28 = (bf16[256,1024]{1,0:T(8,128)(2,1)S(1)}, bf16[256,1024]{1,0:T(8,128)(2,1)S(1)}, u32[]{:S(2)}, u32[]{:S(2)}) collective-permute-start(bf16[256,1024]{1,0:T(8,128)(2,1)S(1)} %collective-permute-done.19.refs_0_), channel_id=1, source_target_pairs={{0,2},{2,0},{4,6},{6,4},{8,10},{10,8},{12,14},{14,12},{1,3},{3,1},... | collective-permute-start | bytes 1572872 | tf_op jit(solution)/shard_map/ppermute | solution.py:545
  259.4 10.4 %copy-start.21 = (bf16[256,1024]{1,0:T(8,128)(2,1)S(1)}, bf16[256,1024]{1,0:T(8,128)(2,1)}, u32[]{:S(2)}) copy-start(bf16[256,1024]{1,0:T(8,128)(2,1)} %copy-done.20) | copy-start | bytes 1572868
  267.9 2.0 collective-permute-start.32
  278.8 14.3 %collective-permute-start.33 = (bf16[512,512]{1,0:T(8,128)(2,1)}, bf16[512,512]{1,0:T(8,128)(2,1)}, u32[]{:S(2)}, u32[]{:S(2)}) collective-permute-start(bf16[512,512]{1,0:T(8,128)(2,1)} %decode_rows.11), channel_id=1, source_target_pairs={{0,2},{2,0},{4,6},{6,4},{8,10},{10,8},{12,14},{14,12},{1,3},{3,1},... | collective-permute-start | bytes 1572872 | tf_op jit(solution)/shard_map/ppermute | solution.py:658
  (28 other events, 88.9 us)

commit v5 on v4

--- a/solution.py
+++ b/solution.py
@@ -176,6 +176,7 @@
 
 LANES = 128
 EXTRA = 16
+BIG = 56
 LOG2E = 1.4426950408889634
 EXP2_SCALE = LOG2E * HEAD_DIM**-0.5
 NT = (((1,), (1,)), ((), ()))
@@ -211,7 +212,7 @@
         in_specs=[column, column, whole(extra.shape)],
         out_specs=pl.BlockSpec(block, lambda h: (h, 0)),
         out_shape=jax.ShapeDtypeStruct((heads * block[0], block[1]), keys.dtype),
-        compiler_params=params(16),
+        compiler_params=params(BIG),
         cost_estimate=cost(0, 8 * tokens * width),
         name="pack_heads",
     )(keys, values, extra)
@@ -258,7 +259,7 @@
         in_specs=[block, whole(kv.shape), pl.BlockSpec(memory_space=pltpu.SMEM)],
         out_specs=block,
         out_shape=jax.ShapeDtypeStruct((latents, HEAD_DIM), jnp.bfloat16),
-        compiler_params=params(32),
+        compiler_params=params(BIG),
         cost_estimate=cost(
             16 * latents * tokens * pos * HEAD_DIM, 2 * kv.size, latents * tokens * pos
         ),
@@ -308,7 +309,7 @@
         functools.partial(project_kernel, heads, far),
         grid_spec=grid_spec,
         out_shape=jax.ShapeDtypeStruct((rows, out_cols), jnp.float32),
-        compiler_params=params(32),
+        compiler_params=params(BIG),
         cost_estimate=cost(2 * rows * width * out_cols, 2 * width * out_cols + 4 * rows * out_cols),
         name="project_rows",
     )(ids, attended, *weights)
@@ -346,7 +347,7 @@
             jax.ShapeDtypeStruct((rows, half), jnp.bfloat16),
             jax.ShapeDtypeStruct((rows, half), jnp.bfloat16),
         ],
-        compiler_params=params(32),
+        compiler_params=params(BIG),
         cost_estimate=cost(6 * rows * width, 13 * rows * width),
         name="norm_rows",
     )(place.reshape(1), mine, theirs, latent_array, gain)
@@ -399,33 +400,39 @@
         functools.partial(latents_kernel, pieces),
         grid_spec=grid_spec,
         out_shape=jax.ShapeDtypeStruct((rows * pieces, width), jnp.bfloat16),
-        compiler_params=params(40),
+        compiler_params=params(BIG),
         cost_estimate=cost(2 * rows * pieces * total * width, 2 * total * width),
         name="latent_keys_values",
     )(ids, *mine, *theirs, *bands)
 
 
-def decode_kernel(first, last, *refs):
-    q_ref, k_ref, v_ref = refs[:3]
-    rest = refs[3:]
-    if not first:
-        old_max_ref, old_acc_ref = rest[:2]
-        rest = rest[2:]
-    latents = k_ref.shape[0]
-    chunk = 512 if latents % 512 == 0 else 256 if latents % 256 == 0 else latents
-    ones = jnp.ones((chunk, LANES), jnp.bfloat16)
+def row_chunks(lengths, size):
+    chunks, open_chunk, room = [], [], size
+    for i, length in enumerate(lengths):
+        start = 0
+        while start < length:
+            take = min(room, length - start)
+            open_chunk.append((i, start, start + take))
+            start, room = start + take, room - take
+            if room == 0:
+                chunks.append(open_chunk)
+                open_chunk, room = [], size
+    return chunks + ([open_chunk] if open_chunk else [])
+
+
+def decode_kernel(parts, q_ref, *refs):
+    k_refs, v_refs, out_ref = refs[:parts], refs[parts : 2 * parts], refs[-1]
+
+    def gathered(sources, chunk, cols):
+        rows = [sources[i][start:stop, cols] for i, start, stop in chunk]
+        return rows[0] if len(rows) == 1 else jnp.concatenate(rows)
+
     for h in range(q_ref.shape[1] // HEAD_DIM):
         cols = slice(h * HEAD_DIM, (h + 1) * HEAD_DIM)
-        wide = slice(2 * h * HEAD_DIM, 2 * (h + 1) * HEAD_DIM)
-        if first:
-            top, acc = None, None
-        else:
-            top, acc = old_max_ref[:, cols][:, :1], old_acc_ref[:, wide]
-        for start in range(0, latents, chunk):
-            band = slice(start, start + chunk)
-            scores = lax.dot_general(
-                q_ref[:, cols], k_ref[band, cols], NT, preferred_element_type=jnp.float32
-            )
+        top = acc = None
+        for chunk in row_chunks([k.shape[0] for k in k_refs], 512):
+            keys, values = gathered(k_refs, chunk, cols), gathered(v_refs, chunk, cols)
+            scores = lax.dot_general(q_ref[:, cols], keys, NT, preferred_element_type=jnp.float32)
             scores = scores * EXP2_SCALE
             new_top = jnp.max(scores, axis=1, keepdims=True)
             if top is not None:
@@ -433,70 +440,41 @@
             weights = jnp.exp2(scores - new_top).astype(jnp.bfloat16)
             summed = jnp.dot(
                 weights,
-                jnp.concatenate([v_ref[band, cols], ones], axis=1),
+                jnp.concatenate([values, jnp.ones((keys.shape[0], LANES), jnp.bfloat16)], axis=1),
                 preferred_element_type=jnp.float32,
             )
             if top is not None:
                 summed = summed + acc * jnp.exp2(top - new_top)
             top, acc = new_top, summed
-        if last:
-            (out_ref,) = rest
-            out_ref[:, cols] = (acc[:, :HEAD_DIM] / acc[:, HEAD_DIM:]).astype(out_ref.dtype)
-        else:
-            max_ref, acc_ref = rest
-            max_ref[:, cols] = jnp.broadcast_to(top, (top.shape[0], HEAD_DIM))
-            acc_ref[:, wide] = acc
-
-
-def decode(queries, keys_values, state, out_type):
-    first, last = state is None, out_type is not None
+        out_ref[:, cols] = (acc[:, :HEAD_DIM] / acc[:, HEAD_DIM:]).astype(out_ref.dtype)
+
+
+def decode(queries, keys_values, out_type):
     tokens, width = queries.shape
-    latents = keys_values.shape[0]
+    latents = sum(v.shape[0] for v in keys_values)
     pair = min(2 * HEAD_DIM, width)
     steps = width // pair
     narrow = pl.BlockSpec((tokens, pair), lambda i: (0, i))
-    wide = pl.BlockSpec((tokens, 2 * pair), lambda i: (0, i))
-    in_specs = [
-        narrow,
-        pl.BlockSpec((latents, pair), lambda i: (0, i)),
-        pl.BlockSpec((latents, pair), lambda i: (0, steps + i)),
-    ]
-    args = [queries, keys_values, keys_values]
-    if not first:
-        in_specs += [narrow, wide]
-        args += list(state)
-    if last:
-        out_specs = narrow
-        out_shape = jax.ShapeDtypeStruct((tokens, width), out_type)
-    else:
-        out_specs = [narrow, wide]
-        out_shape = [
-            jax.ShapeDtypeStruct((tokens, width), jnp.float32),
-            jax.ShapeDtypeStruct((tokens, 2 * width), jnp.float32),
-        ]
+    keys = [pl.BlockSpec((v.shape[0], pair), lambda i: (0, i)) for v in keys_values]
+    values = [pl.BlockSpec((v.shape[0], pair), lambda i: (0, steps + i)) for v in keys_values]
     return pl.pallas_call(
-        functools.partial(decode_kernel, first, last),
+        functools.partial(decode_kernel, len(keys_values)),
         grid=(steps,),
-        in_specs=in_specs,
-        out_specs=out_specs,
-        out_shape=out_shape,
-        compiler_params=params(40),
+        in_specs=[narrow, *keys, *values],
+        out_specs=narrow,
+        out_shape=jax.ShapeDtypeStruct((tokens, width), out_type),
+        compiler_params=params(BIG),
         cost_estimate=cost(
             16 * tokens * latents * width,
-            4 * latents * width + 16 * tokens * width,
+            4 * latents * width + 6 * tokens * width,
             tokens * latents * (width // HEAD_DIM),
         ),
         name="decode_rows",
-    )(*args)
+    )(queries, *keys_values, *keys_values)
 
 
 def swap_perm(size):
     return [(i, i ^ 1) for i in range(size)]
-
-
-def shift_perm(size, k):
-    far = size // 2
-    return [(((z + k) % far) * 2 + y, z * 2 + y) for z in range(far) for y in range(2)]
 
 
 def hop_perm(size, step, way):
@@ -544,17 +522,23 @@
     def over_near(value):
         return lax.ppermute(value, "pos", near)
 
-    def over_far(value, k):
-        return lax.ppermute(value, "pos", shift_perm(pos, k))
-
-    shifts = sorted(range(far), key=lambda k: min(k, far - k))
+    def hop(step, pair):
+        return [
+            lax.ppermute(v, "pos", hop_perm(pos, step, way)) for v, way in zip(pair, (1, -1))
+        ]
+
+    def by_shift(hops, k):
+        return jnp.where(z + k < far, hops[k][1], hops[far - k][0])
+
     out_half = w_out.shape[0] // 2
     out_sent = lax.dynamic_slice_in_dim(w_out, x * out_half, out_half, 0)
-    out_far = [over_far(out_sent, k) for k in shifts[1:]]
+    out_hops = {0: [out_sent, out_sent]}
+    for step in range(1, far):
+        out_hops[step] = hop(step, out_hops[step - 1])
     out_near = over_near(w_out)
     out_ids = [p, p ^ 1]
     for j in range(2):
-        out_ids += [((z + k) % far) * 2 + (y ^ j) for k in shifts[1:]]
+        out_ids += [((z + k) % far) * 2 + (y ^ j) for k in range(1, far)]
     out_ids = jnp.stack([*out_ids, x, 1 - x]).astype(jnp.int32)
 
     part = half_width // 2
@@ -590,71 +574,99 @@
     kv = lax.all_to_all(payload, "pos", 0, 0, tiled=True)
     head_queries = lax.dynamic_slice_in_dim(latent_queries, p * HEAD_DIM, HEAD_DIM, 1)
     head_bias = lax.dynamic_slice_in_dim(enc_bias, p, 1, 1)[:, 0]
+    def kept_queries():
+        counts = kv.reshape(pos, tokens + EXTRA, pair)[:, tokens + id_rows, : 2 * mods]
+        counts = counts.astype(jnp.int32)
+        counts = counts[:, :mods] * 16 + counts[:, mods:]
+        earlier = jnp.arange(pos, dtype=jnp.int32)[:, None] < p
+        before = jnp.sum(jnp.where(earlier, counts, 0), axis=0)
+        within = jnp.cumsum(q_onehot, axis=0) - q_onehot
+        ranked = jnp.sum((within + before[None, :]) * q_onehot, axis=1)
+        limits = jnp.sum(q_onehot * query_counts[None, :], axis=1)
+        return ranked < limits
+
     kv_sent = jnp.where(x == 0, kv_own, kv_near)
-    kv, kv_sent, near_queries, out_far, out_near = lax.optimization_barrier(
-        (kv, kv_sent, near_queries, out_far, out_near)
-    )
-    out_far = jnp.concatenate(out_far)
+    hops = {0: [kv_sent, kv_sent]}
+    hops[1] = hop(1, hops[0])
+    kv, hops, near_queries, out_hops, out_near = lax.optimization_barrier(
+        (kv, hops, near_queries, out_hops, out_near)
+    )
+    out_far = jnp.concatenate([by_shift(out_hops, k) for k in range(1, far)])
     out_bands = [out_far, over_near(out_far), over_groups(out_far)]
-
-    def hop(step, pair):
-        return [
-            lax.ppermute(v, "pos", hop_perm(pos, step, way)) for v, way in zip(pair, (1, -1))
-        ]
-
-    hops = {1: hop(1, [kv_sent, kv_sent])}
+    hops[2] = hop(2, hops[1])
     attended = encode(head_queries, kv, head_bias, pos)
-    attended, hops[1], out_bands = lax.optimization_barrier((attended, hops[1], out_bands))
+    attended, hops, out_bands = lax.optimization_barrier((attended, hops, out_bands))
     out_far, out_across, out_other = out_bands
     out_bands = [w_out, out_near, out_far, out_other, out_across, over_near(out_other)]
-    hops[2] = hop(2, hops[1])
-    attended = lax.all_to_all(attended, "pos", 0, 0, tiled=True)
-    attended, hops[2], out_bands = lax.optimization_barrier((attended, hops[2], out_bands))
+    moved = {k: by_shift(hops, k) for k in range(1, far) if max(k, far - k) < 3}
+    swapped = {k: over_groups(v) for k, v in moved.items()}
     for step in range(3, far):
         hops[step] = hop(step, hops[step - 1])
+    attended = lax.all_to_all(attended, "pos", 0, 0, tiled=True)
+    kept = kept_queries()
+    attended, hops, out_bands, kept, swapped = lax.optimization_barrier(
+        (attended, hops, out_bands, kept, swapped)
+    )
+    for k in range(1, far):
+        if k not in moved:
+            moved[k] = by_shift(hops, k)
+            swapped[k] = over_groups(moved[k])
     partial_value = project(out_ids, attended, out_bands, rows)
     theirs = lax.ppermute(partial_value, "head", swap_perm(2))
-    theirs, hops = lax.optimization_barrier((theirs, hops))
     own_cols, normed, normed_other = normalise(
         place, partial_value, theirs, latent_array, norm_gain[None, :]
     )
     kv_bands = [kv_own, kv_near]
     kv_at = [p, p ^ 1]
     for k in range(1, far):
-        moved = jnp.where(z + k < far, hops[k][1], hops[far - k][0])
-        kv_bands += [moved, over_groups(moved)]
+        kv_bands += [moved[k], swapped[k]]
         there = ((z + k) % far) * 2
         kv_at += [there + (y ^ x), there + (1 - (y ^ x))]
     kv_ids = jnp.stack([place, *kv_at]).astype(jnp.int32)
 
-    counts = kv.reshape(pos, tokens + EXTRA, pair)[:, tokens + id_rows, : 2 * mods]
-    counts = counts.astype(jnp.int32)
-    counts = counts[:, :mods] * 16 + counts[:, mods:]
-    earlier = jnp.arange(pos, dtype=jnp.int32)[:, None] < p
-    before = jnp.sum(jnp.where(earlier, counts, 0), axis=0)
-    within = jnp.cumsum(q_onehot, axis=0) - q_onehot
-    ranked = jnp.sum((within + before[None, :]) * q_onehot, axis=1)
-    limits = jnp.sum(q_onehot * query_counts[None, :], axis=1)
-    kept = ranked < limits
     def cores(values):
         return [lax.ppermute(v, "head", swap_perm(2)) for v in values]
 
-    def fold(mine, other, states, types):
-        keys_values = latent_keys_values(kv_ids, mine, other, kv_bands)
-        return [
-            decode(q, keys_values, state, kind)
-            for q, state, kind in zip((near_queries, own_queries), states, types)
-        ]
-
-    first = [normed, over_near(normed), *[over_far(normed, k) for k in shifts[1:-1]]]
-    first, kept = lax.optimization_barrier((first, kept))
-    second = [over_far(first[0], shifts[-1]), *[over_near(v) for v in first[2:]]]
-    states = fold(first, [normed_other, *cores(first[1:])], [None, None], [None, None])
-    second, states = lax.optimization_barrier((second, states))
-    last = over_near(second[0])
-    states = fold(second, cores(second), states, [None, None])
-    last, states = lax.optimization_barrier((last, states))
-    near_state, own_state = fold([last], cores([last]), states, [jnp.bfloat16, jnp.float32])
+    def fold(mine, other):
+        return latent_keys_values(kv_ids, mine, other, kv_bands)
+
+    def arrival(hops, j):
+        picked = None
+        for at in range(far):
+            came = [
+                (step, way)
+                for step in range(1, far)
+                for way in (1, 0)
+                if (at + step < far if way else at >= step)
+            ]
+            step, way = came[j - 1]
+            value = hops[step][way]
+            picked = value if picked is None else jnp.where(z == at, value, picked)
+        return picked
+
+    came = {0: [normed, normed]}
+    came[1] = hop(1, came[0])
+    came, normed_near, kv_bands = lax.optimization_barrier((came, over_near(normed), kv_bands))
+    mine, other = [normed, normed_near], [normed_other, *cores([normed_near])]
+    keys_values = []
+    for step in range(1, far):
+        fresh = arrival(came, step)
+        if step + 1 < far:
+            came[step + 1] = hop(step + 1, came[step])
+        fresh_near = over_near(fresh)
+        mine.append(fresh)
+        other += cores([fresh])
+        if step > 1:
+            keys_values.append(fold(mine, other))
+            mine, other = [], []
+        came, fresh_near, mine, other, keys_values = lax.optimization_barrier(
+            (came, fresh_near, mine, other, keys_values)
+        )
+        mine.append(fresh_near)
+        other += cores([fresh_near])
+    keys_values.append(fold(mine, other))
+    near_state = decode(near_queries, keys_values, jnp.bfloat16)
+    own_state = decode(own_queries, keys_values, jnp.float32)
     from_near = lax.ppermute(near_state, "pos", near).astype(jnp.float32)
     decoded = jnp.where(
         y == 0,

time: 297 us -> 278 us (0.936)
  waiting for transfers between devices: 132 us -> 100 us
  starting transfers between devices: 48.4 us -> 72.6 us
  local copies, waits for them, and re-layouts: 27.6 us -> 15.1 us
  other arithmetic: 9 us -> 15.4 us
  Pallas kernels: 75.5 us -> 71.6 us
    ppermute x6 -> x0, waiting for transfers between devices: 36.5 us -> none  [over_far(): return lax.ppermute(value, 'pos', shift_perm(pos, k))]
    ppermute x6 -> x18, starting transfers between devices: 9.83 us -> 44.9 us  [hop(): lax.ppermute(v, 'pos', hop_perm(pos, step, way))]
    ppermute x6 -> x18, waiting for transfers between devices: 31.7 us -> 55.9 us  [hop(): lax.ppermute(v, 'pos', hop_perm(pos, step, way))]
    ppermute x9, waiting for transfers between devices: 35.9 us -> 14.8 us  [over_near(): return lax.ppermute(value, 'pos', near)]
    pallas_call x6 -> x2, Pallas kernels: 33.8 us -> 16.7 us  [decode(): pl.pallas_call(functools.partial(decode_kernel, len(keys_values)), grid=(...]
    unnamed x82 -> x60, local copies, waits for them, and re-layouts: 18.8 us -> 6.56 us
    ppermute x6 -> x0, starting transfers between devices: 10.8 us -> none  [over_far(): return lax.ppermute(value, 'pos', shift_perm(pos, k))]
    pallas_call x3, Pallas kernels: 18.3 us -> 24.7 us  [latent_keys_values(): pl.pallas_call(functools.partial(latents_kernel, pieces), grid_spec=grid_...]
  transfers between devices with their start and end apart: 36 -> 42, of which waited for: 18 -> 17; matrix products, arithmetic and copies ran while one was open for 6% -> 6% of each run, Pallas kernels for 19% -> 17%
where the time goes in v5:
time: 278 us; the launch traced here: 276 us
  waiting for transfers between devices  100 us (36%)
  starting transfers between devices  72.6 us (26%)
  Pallas kernels  71.6 us (26%)
  other arithmetic  15.4 us (6%)
  local copies, waits for them, and re-layouts  15.1 us (5%)
    ppermute x18, waiting for transfers between devices, hop(): lax.ppermute(v, 'pos', hop_perm(pos, step, way))  55.9 us
    ppermute x18, starting transfers between devices, hop(): lax.ppermute(v, 'pos', hop_perm(pos, step, way))  44.9 us
    pallas_call x3, Pallas kernels, latent_keys_values(): pl.pallas_call(functools.partial(latents_kernel, pieces), grid_spec=grid_...  24.7 us
    ppermute x4, waiting for transfers between devices, over_groups(): return lax.ppermute(value, 'groups', swap_perm(groups))  20.5 us
    pallas_call x2, Pallas kernels, decode(): pl.pallas_call(functools.partial(decode_kernel, len(keys_values)), grid=(...  16.7 us
    ppermute x9, waiting for transfers between devices, over_near(): return lax.ppermute(value, 'pos', near)  14.8 us
    pallas_call x1, Pallas kernels, encode(): pl.pallas_call(functools.partial(encode_kernel, pos, tokens), grid=(laten...  14.1 us
    ppermute x9, starting transfers between devices, over_near(): return lax.ppermute(value, 'pos', near)  9.12 us
  transfers between devices with their start and end apart: 42, of which 17 were waited for; matrix products, arithmetic and copies ran while one was open for 6% of the time, Pallas kernels for 17%

profile of v5, /device:TPU:0, one launch (start us, length us, event | category | flops | bytes accessed | tf_op | source)
XLA Modules:
  0.0 276.5 jit_solution(4779512327199191316)
XLA Ops:
  2.9 5.9 %pack_heads.1 = bf16[4224,256]{1,0:T(8,128)(2,1)} custom-call(bf16[512,1024]{1,0:T(8,128)(2,1)} %k_ref.1, bf16[512,1024]{1,0:T(8,128)(2,1)} %v_ref.1, bf16[16,256]{1,0:T(8,128)(2,1)} %fusion.6.extra_ref), custom_call_target="tpu_custom_call" | custom-call | bytes 4194304 | tf_op jit(solution)/shard_map/pack_heads/pallas_call | solution.py:209
  8.8 7.4 %all-to-all-start = ((bf16[8,528,256]{2,1,0:T(8,128)(2,1)}), bf16[8,528,256]{2,1,0:T(8,128)(2,1)S(1)}, u32[]{:S(2)}, u32[]{:S(2)}) async-start(bf16[8,528,256]{2,1,0:T(8,128)(2,1)} %bitcast.43), calls=%async_computation | async-start | bytes 4325376 | tf_op jit(solution)/shard_map/all_to_all | solution.py:574
  17.0 4.6 %collective-permute-start.4 = (bf16[512,256]{1,0:T(8,128)(2,1)}, bf16[512,256]{1,0:T(8,128)(2,1)}, u32[]{:S(2)}, u32[]{:S(2)}) collective-permute-start(bf16[512,256]{1,0:T(8,128)(2,1)} %constant_dynamic-slice_fusion.2), channel_id=1, source_target_pairs={{0,4},{2,6},{4,8},{6,10},{8,12},{10,14},{1,5},{3,7},{5,9},{7,11},{... | collective-permute-start | bytes 786440 | tf_op jit(solution)/shard_map/ppermute | solution.py:527
  21.6 1.3 collective-permute-start.5
  22.9 2.1 constant_dynamic-slice_fusion.6
  25.8 1.5 collective-permute-start
  29.4 1.5 collective-permute-start.10
  30.9 27.0 %collective-permute-done.4 = bf16[512,256]{1,0:T(8,128)(2,1)} collective-permute-done((bf16[512,256]{1,0:T(8,128)(2,1)}, bf16[512,256]{1,0:T(8,128)(2,1)}, u32[]{:S(2)}, u32[]{:S(2)}) %collective-permute-start.4) | collective-permute-done | bytes 262176 | tf_op jit(solution)/shard_map/ppermute | solution.py:527
  57.9 1.4 collective-permute-start.6
  59.3 1.3 collective-permute-start.7
  60.6 2.4 pad_maximum_fusion.1
  63.1 20.1 %collective-permute-start.1 = (bf16[256,1024]{1,0:T(8,128)(2,1)}, bf16[256,1024]{1,0:T(8,128)(2,1)}, u32[]{:S(2)}, u32[]{:S(2)}) collective-permute-start(bf16[256,1024]{1,0:T(8,128)(2,1)} %get-tuple-element.137), channel_id=1, source_target_pairs={{0,4},{2,6},{4,8},{6,10},{8,12},{10,14},{1,5},{3,7},{5,9},{7,11},{... | collective-permute-start | bytes 1572872 | tf_op jit(solution)/shard_map/ppermute | solution.py:527
  83.2 1.3 collective-permute-start.2
  86.1 1.3 collective-permute-start.9
  88.5 1.9 constant_dynamic-slice_fusion.8.q_ref
  90.4 13.9 %collective-permute-done.9 = bf16[512,256]{1,0:T(8,128)(2,1)} collective-permute-done((bf16[512,256]{1,0:T(8,128)(2,1)}, bf16[512,256]{1,0:T(8,128)(2,1)}, u32[]{:S(2)}, u32[]{:S(2)}) %collective-permute-start.9) | collective-permute-done | bytes 262176 | tf_op jit(solution)/shard_map/ppermute | solution.py:527
  104.3 1.2 broadcast_select_fusion.7
  108.4 1.5 collective-permute-start.14
  110.6 1.3 collective-permute-start.12
  111.9 14.1 %encode_head.1 = bf16[2048,128]{1,0:T(8,128)(2,1)} custom-call(bf16[2048,128]{1,0:T(8,128)(2,1)} %constant_dynamic-slice_fusion.8.q_ref, bf16[4224,256]{1,0:T(8,128)(2,1)} %bitcast.44, f32[3]{0:T(128)} %fusion.9.bias_ref), custom_call_target="tpu_custom_call" | custom-call | flops 17179869184 | bytes 2162688 | tf_op jit(solution)/shard_map/encode_head/pallas_call | solution.py:256
  127.7 4.6 %all-to-all-start.1 = ((bf16[8,256,128]{2,1,0:T(8,128)(2,1)}), bf16[8,256,128]{2,1,0:T(8,128)(2,1)S(1)}, u32[]{:S(2)}, u32[]{:S(2)}) async-start(bf16[8,256,128]{2,1,0:T(8,128)(2,1)} %bitcast.46), calls=%async_computation.1 | async-start | bytes 1048576 | tf_op jit(solution)/shard_map/all_to_all | solution.py:605
  133.0 2.0 collective-permute-start.17
  135.7 1.3 collective-permute-start.16
  137.0 1.1 broadcast_select_fusion.3.refs_14_.refs_8_.refs_6_
  139.7 9.2 %collective-permute-done.18.refs_15_.refs_9_.refs_7_ = bf16[256,1024]{1,0:T(8,128)(2,1)S(1)} collective-permute-done((bf16[256,1024]{1,0:T(8,128)(2,1)S(1)}, bf16[256,1024]{1,0:T(8,128)(2,1)S(1)}, u32[]{:S(2)}, u32[]{:S(2)}) %collective-permute-start.18) | collective-permute-done | bytes 524320 | tf_op jit(solution)/shard_map/ppermute | solution.py:520
  148.9 4.3 %collective-permute-done.16 = bf16[256,1024]{1,0:T(8,128)(2,1)S(1)} collective-permute-done((bf16[256,1024]{1,0:T(8,128)(2,1)}, bf16[256,1024]{1,0:T(8,128)(2,1)S(1)}, u32[]{:S(2)}, u32[]{:S(2)}) %collective-permute-start.16) | collective-permute-done | bytes 524320 | tf_op jit(solution)/shard_map/ppermute | solution.py:527
  156.1 5.6 %project_rows.1.mine_ref = f32[256,2048]{1,0:T(8,128)} custom-call(s32[10]{0:T(128)} %stack.67.ids_ref, bf16[2048,128]{1,0:T(8,128)(2,1)} %bitcast.45, bf16[1024,256]{1,0:T(8,128)(2,1)} %refs_0_, bf16[1024,256]{1,0:T(8,128)(2,1)} %collective-permute-done.10.refs_1_, bf16[1536,256]{1,0:T(8,128)(2,1)} %copy-done.1, bf16[1536,256]{1,0:T(8,128)(2,1)} %copy-done.13, ...), custom_call_target="tpu_custom_call" | custom-call | flops 1073741824 | bytes 6291456 | tf_op jit(solution)/shard_map/project_rows/pallas_call | solution.py:308
  164.6 1.6 collective-permute-start.23
  166.2 1.3 copy-done.7
  167.5 4.5 %norm_rows.1 = (f32[256,1024]{1,0:T(8,128)}, bf16[256,1024]{1,0:T(8,128)(2,1)}, bf16[256,1024]{1,0:T(8,128)(2,1)}) custom-call(s32[1]{0:T(128)} %bitcast.ids_ref, f32[256,2048]{1,0:T(8,128)} %project_rows.1.mine_ref, f32[256,2048]{1,0:T(8,128)} %copy-done.7, bf16[256,2048]{1,0:T(8,128)(2,1)} %latent_ref.1, f32[1,2048]{1,0:T(1,128)} %bitcast.48), custom_call_target="tpu_custom_call" | custom-call | flops 3145728 | bytes 6815744 | tf_op jit(solution)/shard_map/norm_rows/pallas_call | solution.py:342
  172.0 3.6 %collective-permute-start.20 = (bf16[256,1024]{1,0:T(8,128)(2,1)}, bf16[256,1024]{1,0:T(8,128)(2,1)S(1)}, u32[]{:S(2)}, u32[]{:S(2)}) collective-permute-start(bf16[256,1024]{1,0:T(8,128)(2,1)} %get-tuple-element.107.refs_0_), channel_id=1, source_target_pairs={{0,4},{2,6},{4,8},{6,10},{8,12},{10,14},{1,5},{3,7},{5,9},{7,11},{... | collective-permute-start | bytes 1572872 | tf_op jit(solution)/shard_map/ppermute | solution.py:527
  175.7 1.3 collective-permute-start.21
  177.8 10.8 %collective-permute-done.23.refs_13_.refs_7_.refs_5_ = bf16[256,1024]{1,0:T(8,128)(2,1)} collective-permute-done((bf16[256,1024]{1,0:T(8,128)(2,1)S(1)}, bf16[256,1024]{1,0:T(8,128)(2,1)}, u32[]{:S(2)}, u32[]{:S(2)}) %collective-permute-start.23) | collective-permute-done | bytes 524320 | tf_op jit(solution)/shard_map/ppermute | solution.py:520
  188.6 2.8 %collective-permute-done.21 = bf16[256,1024]{1,0:T(8,128)(2,1)S(1)} collective-permute-done((bf16[256,1024]{1,0:T(8,128)(2,1)}, bf16[256,1024]{1,0:T(8,128)(2,1)S(1)}, u32[]{:S(2)}, u32[]{:S(2)}) %collective-permute-start.21) | collective-permute-done | bytes 524320 | tf_op jit(solution)/shard_map/ppermute | solution.py:527
  192.6 1.3 collective-permute-start.26
  194.5 10.0 %collective-permute-done.27.refs_3_ = bf16[256,1024]{1,0:T(8,128)(2,1)} collective-permute-done((bf16[256,1024]{1,0:T(8,128)(2,1)S(1)}, bf16[256,1024]{1,0:T(8,128)(2,1)}, u32[]{:S(2)}, u32[]{:S(2)}) %collective-permute-start.27) | collective-permute-done | bytes 524320 | tf_op jit(solution)/shard_map/ppermute | solution.py:523
  204.5 6.8 %collective-permute-done.26 = bf16[256,1024]{1,0:T(8,128)(2,1)S(1)} collective-permute-done((bf16[256,1024]{1,0:T(8,128)(2,1)S(1)}, bf16[256,1024]{1,0:T(8,128)(2,1)S(1)}, u32[]{:S(2)}, u32[]{:S(2)}) %collective-permute-start.26) | collective-permute-done | bytes 524320 | tf_op jit(solution)/shard_map/ppermute | solution.py:527
  212.0 1.5 collective-permute-start.32
  214.1 1.5 collective-permute-start.31
  216.3 12.4 %latent_keys_values.3.refs_0_.refs_3_ = bf16[1280,1024]{1,0:T(8,128)(2,1)} custom-call(s32[9]{0:T(128)} %stack.74.ids_ref, bf16[256,1024]{1,0:T(8,128)(2,1)} %get-tuple-element.107.refs_0_, bf16[256,1024]{1,0:T(8,128)(2,1)} %copy-done.27, bf16[256,1024]{1,0:T(8,128)(2,1)} %copy-done.19, bf16[256,1024]{1,0:T(8,128)(2,1)} %collective-permute-done.27.refs_3_, ...), custom_call_target="tpu_custom_call" | custom-call | flops 5368709120 | bytes 4194304 | tf_op jit(solution)/shard_map/latent_keys_values/pallas_call | solution.py:399
  233.5 7.0 %latent_keys_values.4.refs_1_.refs_4_ = bf16[512,1024]{1,0:T(8,128)(2,1)} custom-call(s32[9]{0:T(128)} %stack.74.ids_ref, bf16[256,1024]{1,0:T(8,128)(2,1)} %collective-permute-done.32.refs_0_, bf16[256,1024]{1,0:T(8,128)(2,1)} %copy-done.23, bf16[256,1024]{1,0:T(8,128)(2,1)} %copy-done.29, bf16[256,1024]{1,0:T(8,128)(2,1)} %copy-done.28, ...), custom_call_target="tpu_custom_call" | custom-call | flops 2147483648 | bytes 4194304 | tf_op jit(solution)/shard_map/latent_keys_values/pallas_call | solution.py:399
  240.5 3.7 %collective-permute-done.35.refs_0_ = bf16[256,1024]{1,0:T(8,128)(2,1)S(1)} collective-permute-done((bf16[256,1024]{1,0:T(8,128)(2,1)S(1)}, bf16[256,1024]{1,0:T(8,128)(2,1)S(1)}, u32[]{:S(2)}, u32[]{:S(2)}) %collective-permute-start.35) | collective-permute-done | bytes 524320 | tf_op jit(solution)/shard_map/ppermute | solution.py:523
  244.3 1.9 collective-permute-done.38.refs_1_
  247.0 5.3 %latent_keys_values.5.refs_2_.refs_5_ = bf16[256,1024]{1,0:T(8,128)(2,1)} custom-call(s32[9]{0:T(128)} %stack.74.ids_ref, bf16[256,1024]{1,0:T(8,128)(2,1)} %copy-done.16, bf16[256,1024]{1,0:T(8,128)(2,1)} %copy-done.17, bf16[256,1024]{1,0:T(8,128)(2,1)} %get-tuple-element.114.refs_10_.refs_4_.refs_2_, bf16[256,1024]{1,0:T(8,128)(2,1)} %copy-done.3, ...), custom_call_target="tpu_custom_call" | custom-call | flops 1073741824 | bytes 4194304 | tf_op jit(solution)/shard_map/latent_keys_values/pallas_call | solution.py:399
  252.3 8.3 %decode_rows.3 = bf16[512,512]{1,0:T(8,128)(2,1)} custom-call(bf16[512,512]{1,0:T(8,128)(2,1)} %collective-permute-done.3.q_ref, bf16[1280,1024]{1,0:T(8,128)(2,1)} %latent_keys_values.3.refs_0_.refs_3_, bf16[512,1024]{1,0:T(8,128)(2,1)} %latent_keys_values.4.refs_1_.refs_4_, bf16[256,1024]{1,0:T(8,128)(2,1)} %latent_keys_values.5.refs_2_.refs_5_, ...), custom_call_target="tpu_custom_call" | custom-call | flops 8589934592 | bytes 5767168 | tf_op jit(solution)/shard_map/decode_rows/pallas_call | solution.py:460
  261.2 8.4 %decode_rows.2 = f32[512,512]{1,0:T(8,128)} custom-call(bf16[512,512]{1,0:T(8,128)(2,1)} %get-tuple-element.134.q_ref, bf16[1280,1024]{1,0:T(8,128)(2,1)} %latent_keys_values.3.refs_0_.refs_3_, bf16[512,1024]{1,0:T(8,128)(2,1)} %latent_keys_values.4.refs_1_.refs_4_, bf16[256,1024]{1,0:T(8,128)(2,1)} %latent_keys_values.5.refs_2_.refs_5_, ...), custom_call_target="tpu_custom_call" | custom-call | flops 8589934592 | bytes 5767168 | tf_op jit(solution)/shard_map/decode_rows/pallas_call | solution.py:460
  269.6 5.2 %collective-permute-done.39 = bf16[512,512]{1,0:T(8,128)(2,1)S(1)} collective-permute-done((bf16[512,512]{1,0:T(8,128)(2,1)}, bf16[512,512]{1,0:T(8,128)(2,1)S(1)}, u32[]{:S(2)}, u32[]{:S(2)}) %collective-permute-start.39) | collective-permute-done | bytes 524320 | tf_op jit(solution)/shard_map/ppermute | solution.py:670
  274.9 1.6 fusion
  (144 shorter events, 33.4 us)
Async XLA Ops:
  0.6 26.6 %copy-start = (bf16[3,1024]{1,0:T(4,128)(2,1)S(1)}, bf16[3,1024]{1,0:T(4,128)(2,1)}, u32[]{:S(2)}) copy-start(bf16[3,1024]{1,0:T(4,128)(2,1)} %param.25) | copy-start | bytes 18436
  8.8 95.5 %all-to-all-start = ((bf16[8,528,256]{2,1,0:T(8,128)(2,1)}), bf16[8,528,256]{2,1,0:T(8,128)(2,1)S(1)}, u32[]{:S(2)}, u32[]{:S(2)}) async-start(bf16[8,528,256]{2,1,0:T(8,128)(2,1)} %bitcast.43), calls=%async_computation | async-start | bytes 4325376 | tf_op jit(solution)/shard_map/all_to_all | solution.py:574
  17.0 41.0 %collective-permute-start.4 = (bf16[512,256]{1,0:T(8,128)(2,1)}, bf16[512,256]{1,0:T(8,128)(2,1)}, u32[]{:S(2)}, u32[]{:S(2)}) collective-permute-start(bf16[512,256]{1,0:T(8,128)(2,1)} %constant_dynamic-slice_fusion.2), channel_id=1, source_target_pairs={{0,4},{2,6},{4,8},{6,10},{8,12},{10,14},{1,5},{3,7},{5,9},{7,11},{... | collective-permute-start | bytes 786440 | tf_op jit(solution)/shard_map/ppermute | solution.py:527
  21.6 37.7 %collective-permute-start.5 = (bf16[512,256]{1,0:T(8,128)(2,1)}, bf16[512,256]{1,0:T(8,128)(2,1)}, u32[]{:S(2)}, u32[]{:S(2)}) collective-permute-start(bf16[512,256]{1,0:T(8,128)(2,1)} %constant_dynamic-slice_fusion.2), channel_id=1, source_target_pairs={{12,8},{14,10},{8,4},{10,6},{4,0},{6,2},{13,9},{15,11},{9,5},{11,7... | collective-permute-start | bytes 786440 | tf_op jit(solution)/shard_map/ppermute | solution.py:527
  25.8 34.8 %collective-permute-start = (bf16[256,1024]{1,0:T(8,128)(2,1)}, bf16[256,1024]{1,0:T(8,128)(2,1)S(1)}, u32[]{:S(2)}, u32[]{:S(2)}) collective-permute-start(bf16[256,1024]{1,0:T(8,128)(2,1)} %pad_maximum_fusion.2), channel_id=1, source_target_pairs={{0,2},{2,0},{4,6},{6,4},{8,10},{10,8},{12,14},{14,12},{1,3},{3,1},... | collective-permute-start | bytes 1572872 | tf_op jit(solution)/shard_map/ppermute | solution.py:523
  27.8 60.0 %copy-start.25 = (f32[3,8]{1,0:T(4,128)S(1)}, f32[3,8]{1,0:T(4,128)}, u32[]{:S(2)}) copy-start(f32[3,8]{1,0:T(4,128)} %param.26) | copy-start | bytes 292
  28.9 54.3 %collective-permute-start.3 = (bf16[512,512]{1,0:T(8,128)(2,1)}, bf16[512,512]{1,0:T(8,128)(2,1)}, u32[]{:S(2)}, u32[]{:S(2)}) collective-permute-start(bf16[512,512]{1,0:T(8,128)(2,1)} %get-tuple-element.135), channel_id=1, source_target_pairs={{0,2},{2,0},{4,6},{6,4},{8,10},{10,8},{12,14},{14,12},{1,3},{3,1},... | collective-permute-start | bytes 1572872 | tf_op jit(solution)/shard_map/ppermute | solution.py:523
  29.4 60.9 %collective-permute-start.10 = (bf16[1024,256]{1,0:T(8,128)(2,1)S(1)}, bf16[1024,256]{1,0:T(8,128)(2,1)}, u32[]{:S(2)}, u32[]{:S(2)}) collective-permute-start(bf16[1024,256]{1,0:T(8,128)(2,1)S(1)} %copy-done.9), channel_id=1, source_target_pairs={{0,2},{2,0},{4,6},{6,4},{8,10},{10,8},{12,14},{14,12},{1,3},{3,1},... | collective-permute-start | bytes 1572872 | tf_op jit(solution)/shard_map/ppermute | solution.py:523
  57.9 27.5 %collective-permute-start.6 = (bf16[512,256]{1,0:T(8,128)(2,1)}, bf16[512,256]{1,0:T(8,128)(2,1)}, u32[]{:S(2)}, u32[]{:S(2)}) collective-permute-start(bf16[512,256]{1,0:T(8,128)(2,1)} %collective-permute-done.4), channel_id=1, source_target_pairs={{4,8},{6,10},{8,12},{10,14},{5,9},{7,11},{9,13},{11,15},{20,24},{2... | collective-permute-start | bytes 786440 | tf_op jit(solution)/shard_map/ppermute | solution.py:527
  59.3 26.8 %collective-permute-start.7 = (bf16[512,256]{1,0:T(8,128)(2,1)}, bf16[512,256]{1,0:T(8,128)(2,1)}, u32[]{:S(2)}, u32[]{:S(2)}) collective-permute-start(bf16[512,256]{1,0:T(8,128)(2,1)} %collective-permute-done.5), channel_id=1, source_target_pairs={{8,4},{10,6},{4,0},{6,2},{9,5},{11,7},{5,1},{7,3},{24,20},{26,22},... | collective-permute-start | bytes 786440 | tf_op jit(solution)/shard_map/ppermute | solution.py:527
  60.6 45.9 %copy-start.3 = (bf16[256,1024]{1,0:T(8,128)(2,1)}, bf16[256,1024]{1,0:T(8,128)(2,1)S(1)}, u32[]{:S(2)}) copy-start(bf16[256,1024]{1,0:T(8,128)(2,1)S(1)} %collective-permute-done.refs_11_.refs_5_.refs_3_) | copy-start | bytes 1572868
  63.1 41.2 %collective-permute-start.1 = (bf16[256,1024]{1,0:T(8,128)(2,1)}, bf16[256,1024]{1,0:T(8,128)(2,1)}, u32[]{:S(2)}, u32[]{:S(2)}) collective-permute-start(bf16[256,1024]{1,0:T(8,128)(2,1)} %get-tuple-element.137), channel_id=1, source_target_pairs={{0,4},{2,6},{4,8},{6,10},{8,12},{10,14},{1,5},{3,7},{5,9},{7,11},{... | collective-permute-start | bytes 1572872 | tf_op jit(solution)/shard_map/ppermute | solution.py:527
  83.2 21.1 %collective-permute-start.2 = (bf16[256,1024]{1,0:T(8,128)(2,1)}, bf16[256,1024]{1,0:T(8,128)(2,1)}, u32[]{:S(2)}, u32[]{:S(2)}) collective-permute-start(bf16[256,1024]{1,0:T(8,128)(2,1)} %get-tuple-element.137), channel_id=1, source_target_pairs={{12,8},{14,10},{8,4},{10,6},{4,0},{6,2},{13,9},{15,11},{9,5},{11,7... | collective-permute-start | bytes 1572872 | tf_op jit(solution)/shard_map/ppermute | solution.py:527
  85.4 5.0 %collective-permute-start.8 = (bf16[512,256]{1,0:T(8,128)(2,1)}, bf16[512,256]{1,0:T(8,128)(2,1)S(1)}, u32[]{:S(2)}, u32[]{:S(2)}) collective-permute-start(bf16[512,256]{1,0:T(8,128)(2,1)} %collective-permute-done.6), channel_id=1, source_target_pairs={{8,12},{10,14},{9,13},{11,15},{24,28},{26,30},{25,29},{27,31}} | collective-permute-start | bytes 786440 | tf_op jit(solution)/shard_map/ppermute | solution.py:527
  86.1 18.2 %collective-permute-start.9 = (bf16[512,256]{1,0:T(8,128)(2,1)}, bf16[512,256]{1,0:T(8,128)(2,1)}, u32[]{:S(2)}, u32[]{:S(2)}) collective-permute-start(bf16[512,256]{1,0:T(8,128)(2,1)} %collective-permute-done.7), channel_id=1, source_target_pairs={{4,0},{6,2},{5,1},{7,3},{20,16},{22,18},{21,17},{23,19}} | collective-permute-start | bytes 786440 | tf_op jit(solution)/shard_map/ppermute | solution.py:527
  107.6 18.4 %collective-permute-start.13 = (bf16[1536,256]{1,0:T(8,128)(2,1)S(1)}, bf16[1536,256]{1,0:T(8,128)(2,1)S(1)}, u32[]{:S(2)}, u32[]{:S(2)}) collective-permute-start(bf16[1536,256]{1,0:T(8,128)(2,1)S(1)} %pad_maximum_fusion.refs_2_), channel_id=1, source_target_pairs={{0,2},{2,0},{4,6},{6,4},{8,10},{10,8},{12,14},{14,12},{1,3},{3,1},... | collective-permute-start | bytes 2359304 | tf_op jit(solution)/shard_map/ppermute | solution.py:523
  108.4 17.7 %collective-permute-start.14 = (bf16[1536,256]{1,0:T(8,128)(2,1)S(1)}, bf16[1536,256]{1,0:T(8,128)(2,1)S(1)}, u32[]{:S(2)}, u32[]{:S(2)}) collective-permute-start(bf16[1536,256]{1,0:T(8,128)(2,1)S(1)} %pad_maximum_fusion.refs_2_), channel_id=1, source_target_pairs={{0,16},{16,0},{1,17},{17,1},{2,18},{18,2},{3,19},{19,3},{4,20},{20... | collective-permute-start | bytes 2359304 | tf_op jit(solution)/shard_map/ppermute | solution.py:520
  109.9 16.1 %collective-permute-start.11 = (bf16[256,1024]{1,0:T(8,128)(2,1)}, bf16[256,1024]{1,0:T(8,128)(2,1)S(1)}, u32[]{:S(2)}, u32[]{:S(2)}) collective-permute-start(bf16[256,1024]{1,0:T(8,128)(2,1)} %collective-permute-done.1), channel_id=1, source_target_pairs={{4,8},{6,10},{8,12},{10,14},{5,9},{7,11},{9,13},{11,15},{20,24},{2... | collective-permute-start | bytes 1572872 | tf_op jit(solution)/shard_map/ppermute | solution.py:527
  110.6 15.4 %collective-permute-start.12 = (bf16[256,1024]{1,0:T(8,128)(2,1)}, bf16[256,1024]{1,0:T(8,128)(2,1)S(1)}, u32[]{:S(2)}, u32[]{:S(2)}) collective-permute-start(bf16[256,1024]{1,0:T(8,128)(2,1)} %collective-permute-done.2), channel_id=1, source_target_pairs={{8,4},{10,6},{4,0},{6,2},{9,5},{11,7},{5,1},{7,3},{24,20},{26,22},... | collective-permute-start | bytes 1572872 | tf_op jit(solution)/shard_map/ppermute | solution.py:527
  126.0 29.0 %copy-start.12 = (bf16[1536,256]{1,0:T(8,128)(2,1)}, bf16[1536,256]{1,0:T(8,128)(2,1)S(1)}, u32[]{:S(2)}) copy-start(bf16[1536,256]{1,0:T(8,128)(2,1)S(1)} %collective-permute-done.13.refs_4_) | copy-start | bytes 2359300
  127.7 27.3 %all-to-all-start.1 = ((bf16[8,256,128]{2,1,0:T(8,128)(2,1)}), bf16[8,256,128]{2,1,0:T(8,128)(2,1)S(1)}, u32[]{:S(2)}, u32[]{:S(2)}) async-start(bf16[8,256,128]{2,1,0:T(8,128)(2,1)} %bitcast.46), calls=%async_computation.1 | async-start | bytes 1048576 | tf_op jit(solution)/shard_map/all_to_all | solution.py:605
  133.0 22.0 %collective-permute-start.17 = (bf16[1536,256]{1,0:T(8,128)(2,1)}, bf16[1536,256]{1,0:T(8,128)(2,1)S(1)}, u32[]{:S(2)}, u32[]{:S(2)}) collective-permute-start(bf16[1536,256]{1,0:T(8,128)(2,1)} %copy-done.13), channel_id=1, source_target_pairs={{0,2},{2,0},{4,6},{6,4},{8,10},{10,8},{12,14},{14,12},{1,3},{3,1},... | collective-permute-start | bytes 2359304 | tf_op jit(solution)/shard_map/ppermute | solution.py:523
  135.0 13.9 %collective-permute-start.15 = (bf16[256,1024]{1,0:T(8,128)(2,1)S(1)}, bf16[256,1024]{1,0:T(8,128)(2,1)S(1)}, u32[]{:S(2)}, u32[]{:S(2)}) collective-permute-start(bf16[256,1024]{1,0:T(8,128)(2,1)S(1)} %collective-permute-done.11), channel_id=1, source_target_pairs={{8,12},{10,14},{9,13},{11,15},{24,28},{26,30},{25,29},{27,31}} | collective-permute-start | bytes 1572872 | tf_op jit(solution)/shard_map/ppermute | solution.py:527
  135.7 17.5 %collective-permute-start.16 = (bf16[256,1024]{1,0:T(8,128)(2,1)}, bf16[256,1024]{1,0:T(8,128)(2,1)S(1)}, u32[]{:S(2)}, u32[]{:S(2)}) collective-permute-start(bf16[256,1024]{1,0:T(8,128)(2,1)} %copy-done.18), channel_id=1, source_target_pairs={{4,0},{6,2},{5,1},{7,3},{20,16},{22,18},{21,17},{23,19}} | collective-permute-start | bytes 1572872 | tf_op jit(solution)/shard_map/ppermute | solution.py:527
  138.1 23.6 %copy-start.4 = (bf16[256,1024]{1,0:T(8,128)(2,1)}, bf16[256,1024]{1,0:T(8,128)(2,1)S(1)}, u32[]{:S(2)}) copy-start(bf16[256,1024]{1,0:T(8,128)(2,1)S(1)} %broadcast_select_fusion.3.refs_14_.refs_8_.refs_6_) | copy-start | bytes 1572868
  138.2 10.8 %collective-permute-start.18 = (bf16[256,1024]{1,0:T(8,128)(2,1)S(1)}, bf16[256,1024]{1,0:T(8,128)(2,1)S(1)}, u32[]{:S(2)}, u32[]{:S(2)}) collective-permute-start(bf16[256,1024]{1,0:T(8,128)(2,1)S(1)} %broadcast_select_fusion.3.refs_14_.refs_8_.refs_6_), channel_id=1, source_target_pairs={{0,16},{16,0},{1,17},{17,1},{2,18},{18,2},{3,19},{19,3},{4,20},{20... | collective-permute-start | bytes 1572872 | tf_op jit(solution)/shard_map/ppermute | solution.py:520
  161.8 4.4 %collective-permute-start.19 = (f32[256,2048]{1,0:T(8,128)}, f32[256,2048]{1,0:T(8,128)S(1)}, u32[]{:S(2)}, u32[]{:S(2)}) collective-permute-start(f32[256,2048]{1,0:T(8,128)} %project_rows.1.mine_ref), channel_id=1, source_target_pairs={{0,1},{1,0},{2,3},{3,2},{4,5},{5,4},{6,7},{7,6},{8,9},{9,8},{10,11... | collective-permute-start | bytes 6291464 | tf_op jit(solution)/shard_map/ppermute | solution.py:615
  162.9 14.9 %collective-permute-start.24 = (bf16[256,1024]{1,0:T(8,128)(2,1)S(1)}, bf16[256,1024]{1,0:T(8,128)(2,1)}, u32[]{:S(2)}, u32[]{:S(2)}) collective-permute-start(bf16[256,1024]{1,0:T(8,128)(2,1)S(1)} %broadcast_select_fusion.1.refs_16_.refs_10_.refs_8_), channel_id=1, source_target_pairs={{0,16},{16,0},{1,17},{17,1},{2,18},{18,2},{3,19},{19,3},{4,20},{20... | collective-permute-start | bytes 1572872 | tf_op jit(solution)/shard_map/ppermute | solution.py:520
  164.6 24.0 %collective-permute-start.23 = (bf16[256,1024]{1,0:T(8,128)(2,1)S(1)}, bf16[256,1024]{1,0:T(8,128)(2,1)}, u32[]{:S(2)}, u32[]{:S(2)}) collective-permute-start(bf16[256,1024]{1,0:T(8,128)(2,1)S(1)} %broadcast_select_fusion.2.refs_12_.refs_6_.refs_4_), channel_id=1, source_target_pairs={{0,16},{16,0},{1,17},{17,1},{2,18},{18,2},{3,19},{19,3},{4,20},{20... | collective-permute-start | bytes 1572872 | tf_op jit(solution)/shard_map/ppermute | solution.py:520
  172.0 16.6 %collective-permute-start.20 = (bf16[256,1024]{1,0:T(8,128)(2,1)}, bf16[256,1024]{1,0:T(8,128)(2,1)S(1)}, u32[]{:S(2)}, u32[]{:S(2)}) collective-permute-start(bf16[256,1024]{1,0:T(8,128)(2,1)} %get-tuple-element.107.refs_0_), channel_id=1, source_target_pairs={{0,4},{2,6},{4,8},{6,10},{8,12},{10,14},{1,5},{3,7},{5,9},{7,11},{... | collective-permute-start | bytes 1572872 | tf_op jit(solution)/shard_map/ppermute | solution.py:527
  175.7 15.8 %collective-permute-start.21 = (bf16[256,1024]{1,0:T(8,128)(2,1)}, bf16[256,1024]{1,0:T(8,128)(2,1)S(1)}, u32[]{:S(2)}, u32[]{:S(2)}) collective-permute-start(bf16[256,1024]{1,0:T(8,128)(2,1)} %get-tuple-element.107.refs_0_), channel_id=1, source_target_pairs={{12,8},{14,10},{8,4},{10,6},{4,0},{6,2},{13,9},{15,11},{9,5},{11,7... | collective-permute-start | bytes 1572872 | tf_op jit(solution)/shard_map/ppermute | solution.py:527
  177.0 14.5 %collective-permute-start.22 = (bf16[256,1024]{1,0:T(8,128)(2,1)}, bf16[256,1024]{1,0:T(8,128)(2,1)S(1)}, u32[]{:S(2)}, u32[]{:S(2)}) collective-permute-start(bf16[256,1024]{1,0:T(8,128)(2,1)} %get-tuple-element.107.refs_0_), channel_id=1, source_target_pairs={{0,2},{2,0},{4,6},{6,4},{8,10},{10,8},{12,14},{14,12},{1,3},{3,1},... | collective-permute-start | bytes 1572872 | tf_op jit(solution)/shard_map/ppermute | solution.py:523
  191.5 24.7 %copy-start.19 = (bf16[256,1024]{1,0:T(8,128)(2,1)}, bf16[256,1024]{1,0:T(8,128)(2,1)S(1)}, u32[]{:S(2)}) copy-start(bf16[256,1024]{1,0:T(8,128)(2,1)S(1)} %broadcast_select_fusion.refs_2_) | copy-start | bytes 1572868
  191.5 13.0 %collective-permute-start.27 = (bf16[256,1024]{1,0:T(8,128)(2,1)S(1)}, bf16[256,1024]{1,0:T(8,128)(2,1)}, u32[]{:S(2)}, u32[]{:S(2)}) collective-permute-start(bf16[256,1024]{1,0:T(8,128)(2,1)S(1)} %broadcast_select_fusion.refs_2_), channel_id=1, source_target_pairs={{0,2},{2,0},{4,6},{6,4},{8,10},{10,8},{12,14},{14,12},{1,3},{3,1},... | collective-permute-start | bytes 1572872 | tf_op jit(solution)/shard_map/ppermute | solution.py:523
  191.9 12.6 %collective-permute-start.29 = (bf16[256,1024]{1,0:T(8,128)(2,1)S(1)}, bf16[256,1024]{1,0:T(8,128)(2,1)}, u32[]{:S(2)}, u32[]{:S(2)}) collective-permute-start(bf16[256,1024]{1,0:T(8,128)(2,1)S(1)} %broadcast_select_fusion.refs_2_), channel_id=1, source_target_pairs={{0,1},{1,0},{2,3},{3,2},{4,5},{5,4},{6,7},{7,6},{8,9},{9,8},{10,11... | collective-permute-start | bytes 1572872 | tf_op jit(solution)/shard_map/ppermute | solution.py:628
  191.9 12.6 %collective-permute-start.25 = (bf16[256,1024]{1,0:T(8,128)(2,1)S(1)}, bf16[256,1024]{1,0:T(8,128)(2,1)S(1)}, u32[]{:S(2)}, u32[]{:S(2)}) collective-permute-start(bf16[256,1024]{1,0:T(8,128)(2,1)S(1)} %collective-permute-done.20), channel_id=1, source_target_pairs={{4,8},{6,10},{8,12},{10,14},{5,9},{7,11},{9,13},{11,15},{20,24},{2... | collective-permute-start | bytes 1572872 | tf_op jit(solution)/shard_map/ppermute | solution.py:527
  192.6 18.7 %collective-permute-start.26 = (bf16[256,1024]{1,0:T(8,128)(2,1)S(1)}, bf16[256,1024]{1,0:T(8,128)(2,1)S(1)}, u32[]{:S(2)}, u32[]{:S(2)}) collective-permute-start(bf16[256,1024]{1,0:T(8,128)(2,1)S(1)} %collective-permute-done.21), channel_id=1, source_target_pairs={{8,4},{10,6},{4,0},{6,2},{9,5},{11,7},{5,1},{7,3},{24,20},{26,22},... | collective-permute-start | bytes 1572872 | tf_op jit(solution)/shard_map/ppermute | solution.py:527
  193.9 17.4 %collective-permute-start.28 = (bf16[256,1024]{1,0:T(8,128)(2,1)S(1)}, bf16[256,1024]{1,0:T(8,128)(2,1)}, u32[]{:S(2)}, u32[]{:S(2)}) collective-permute-start(bf16[256,1024]{1,0:T(8,128)(2,1)S(1)} %collective-permute-done.22.refs_1_), channel_id=1, source_target_pairs={{0,1},{1,0},{2,3},{3,2},{4,5},{5,4},{6,7},{7,6},{8,9},{9,8},{10,11... | collective-permute-start | bytes 1572872 | tf_op jit(solution)/shard_map/ppermute | solution.py:628
  211.4 4.8 %collective-permute-start.34 = (bf16[256,1024]{1,0:T(8,128)(2,1)S(1)}, bf16[256,1024]{1,0:T(8,128)(2,1)}, u32[]{:S(2)}, u32[]{:S(2)}) collective-permute-start(bf16[256,1024]{1,0:T(8,128)(2,1)S(1)} %fusion.1.refs_4_), channel_id=1, source_target_pairs={{0,1},{1,0},{2,3},{3,2},{4,5},{5,4},{6,7},{7,6},{8,9},{9,8},{10,11... | collective-permute-start | bytes 1572872 | tf_op jit(solution)/shard_map/ppermute | solution.py:628
  211.5 4.8 %collective-permute-start.33 = (bf16[256,1024]{1,0:T(8,128)(2,1)}, bf16[256,1024]{1,0:T(8,128)(2,1)}, u32[]{:S(2)}, u32[]{:S(2)}) collective-permute-start(bf16[256,1024]{1,0:T(8,128)(2,1)} %collective-permute-done.27.refs_3_), channel_id=1, source_target_pairs={{0,1},{1,0},{2,3},{3,2},{4,5},{5,4},{6,7},{7,6},{8,9},{9,8},{10,11... | collective-permute-start | bytes 1572872 | tf_op jit(solution)/shard_map/ppermute | solution.py:628
  212.0 16.6 %collective-permute-start.32 = (bf16[256,1024]{1,0:T(8,128)(2,1)S(1)}, bf16[256,1024]{1,0:T(8,128)(2,1)}, u32[]{:S(2)}, u32[]{:S(2)}) collective-permute-start(bf16[256,1024]{1,0:T(8,128)(2,1)S(1)} %fusion.1.refs_4_), channel_id=1, source_target_pairs={{0,2},{2,0},{4,6},{6,4},{8,10},{10,8},{12,14},{14,12},{1,3},{3,1},... | collective-permute-start | bytes 1572872 | tf_op jit(solution)/shard_map/ppermute | solution.py:523
  213.5 15.2 %collective-permute-start.30 = (bf16[256,1024]{1,0:T(8,128)(2,1)S(1)}, bf16[256,1024]{1,0:T(8,128)(2,1)S(1)}, u32[]{:S(2)}, u32[]{:S(2)}) collective-permute-start(bf16[256,1024]{1,0:T(8,128)(2,1)S(1)} %collective-permute-done.25), channel_id=1, source_target_pairs={{8,12},{10,14},{9,13},{11,15},{24,28},{26,30},{25,29},{27,31}} | collective-permute-start | bytes 1572872 | tf_op jit(solution)/shard_map/ppermute | solution.py:527
  214.1 15.5 %collective-permute-start.31 = (bf16[256,1024]{1,0:T(8,128)(2,1)S(1)}, bf16[256,1024]{1,0:T(8,128)(2,1)S(1)}, u32[]{:S(2)}, u32[]{:S(2)}) collective-permute-start(bf16[256,1024]{1,0:T(8,128)(2,1)S(1)} %collective-permute-done.26), channel_id=1, source_target_pairs={{4,0},{6,2},{5,1},{7,3},{20,16},{22,18},{21,17},{23,19}} | collective-permute-start | bytes 1572872 | tf_op jit(solution)/shard_map/ppermute | solution.py:527
  229.8 2.0 collective-permute-start.37
  229.9 2.9 %collective-permute-start.36 = (bf16[256,1024]{1,0:T(8,128)(2,1)}, bf16[256,1024]{1,0:T(8,128)(2,1)S(1)}, u32[]{:S(2)}, u32[]{:S(2)}) collective-permute-start(bf16[256,1024]{1,0:T(8,128)(2,1)} %collective-permute-done.32.refs_0_), channel_id=1, source_target_pairs={{0,1},{1,0},{2,3},{3,2},{4,5},{5,4},{6,7},{7,6},{8,9},{9,8},{10,11... | collective-permute-start | bytes 1572872 | tf_op jit(solution)/shard_map/ppermute | solution.py:628
  230.4 13.9 %collective-permute-start.35 = (bf16[256,1024]{1,0:T(8,128)(2,1)S(1)}, bf16[256,1024]{1,0:T(8,128)(2,1)S(1)}, u32[]{:S(2)}, u32[]{:S(2)}) collective-permute-start(bf16[256,1024]{1,0:T(8,128)(2,1)S(1)} %select_select_fusion.1.refs_1_), channel_id=1, source_target_pairs={{0,2},{2,0},{4,6},{6,4},{8,10},{10,8},{12,14},{14,12},{1,3},{3,1},... | collective-permute-start | bytes 1572872 | tf_op jit(solution)/shard_map/ppermute | solution.py:523
  244.3 1.9 collective-permute-start.38
  260.6 14.2 %collective-permute-start.39 = (bf16[512,512]{1,0:T(8,128)(2,1)}, bf16[512,512]{1,0:T(8,128)(2,1)S(1)}, u32[]{:S(2)}, u32[]{:S(2)}) collective-permute-start(bf16[512,512]{1,0:T(8,128)(2,1)} %decode_rows.3), channel_id=1, source_target_pairs={{0,2},{2,0},{4,6},{6,4},{8,10},{10,8},{12,14},{14,12},{1,3},{3,1},... | collective-permute-start | bytes 1572872 | tf_op jit(solution)/shard_map/ppermute | solution.py:670
  (24 other events, 133.2 us)

commit v6 on v5

--- a/solution.py
+++ b/solution.py
@@ -194,125 +194,170 @@
     return pl.BlockSpec(shape, lambda *args: (0,) * len(shape))
 
 
-def pack_kernel(k_ref, v_ref, extra_ref, out_ref):
+def encode_kernel(ids_ref, q_ref, k_ref, v_ref, extra_ref, near_ref, bias_ref, out_ref):
+    rows, width = q_ref.shape
     tokens = k_ref.shape[0]
-    out_ref[:tokens, :HEAD_DIM] = k_ref[...]
-    out_ref[:tokens, HEAD_DIM:] = v_ref[...]
-    out_ref[tokens:, :] = extra_ref[...]
-
-
-def pack(keys, values, extra):
-    tokens, width = keys.shape
     heads = width // HEAD_DIM
-    column = pl.BlockSpec((tokens, HEAD_DIM), lambda h: (0, h))
-    block = (tokens + EXTRA, 2 * HEAD_DIM)
+    ones = jnp.ones((tokens, LANES), jnp.bfloat16)
+    kinds = [
+        extra_ref[...].astype(jnp.float32)[:1, :tokens],
+        near_ref[tokens:, :].astype(jnp.float32)[:1, :tokens],
+    ]
+    lane = lax.broadcasted_iota(jnp.int32, (rows, LANES), 1)
+    lse_all = jnp.zeros((rows, LANES), jnp.float32)
+    for h in range(heads):
+        cols = slice(h * HEAD_DIM, (h + 1) * HEAD_DIM)
+        late = slice(width + h * HEAD_DIM, width + (h + 1) * HEAD_DIM)
+        pairs = [
+            (k_ref[:, cols], v_ref[:, cols]),
+            (near_ref[:tokens, cols], near_ref[:tokens, late]),
+        ]
+        top = acc = None
+        for (keys, values), kind in zip(pairs, kinds):
+            bias = jnp.zeros_like(kind)
+            for m in range(bias_ref.shape[0]):
+                bias = jnp.where(kind == m, bias_ref[m, h] * LOG2E, bias)
+            scores = lax.dot_general(q_ref[:, cols], keys, NT, preferred_element_type=jnp.float32)
+            scores = scores * EXP2_SCALE + bias
+            new_top = jnp.max(scores, axis=1, keepdims=True)
+            if top is not None:
+                new_top = jnp.maximum(top, new_top)
+            weights = jnp.exp2(scores - new_top).astype(jnp.bfloat16)
+            summed = jnp.dot(
+                weights, jnp.concatenate([values, ones], axis=1), preferred_element_type=jnp.float32
+            )
+            if top is not None:
+                summed = summed + acc * jnp.exp2(top - new_top)
+            top, acc = new_top, summed
+        totals = acc[:, HEAD_DIM:]
+        out_ref[:rows, cols] = (acc[:, :HEAD_DIM] / totals).astype(jnp.bfloat16)
+        lse_all = jnp.where(lane % heads == h, top + jnp.log2(totals), lse_all)
+    lse = lse_all.T[:EXTRA, :]
+    high = lse.astype(jnp.bfloat16).astype(jnp.float32)
+    mid = (lse - high).astype(jnp.bfloat16).astype(jnp.float32)
+    low = lse - high - mid
+    row = lax.broadcasted_iota(jnp.int32, lse.shape, 0)
+    terms = jnp.where(row < heads, high, jnp.where(row < 2 * heads, mid, low))
+    out_ref[rows:, :] = terms.astype(jnp.bfloat16)
+
+
+def encode(ids, queries, keys, values, extra, near, bias, rows):
+    tokens = keys.shape[0]
+    width = keys.shape[1] // 2
+    half = pl.BlockSpec((tokens, width), lambda i, ids: (0, ids[1]))
+    grid_spec = pltpu.PrefetchScalarGridSpec(
+        num_scalar_prefetch=1,
+        grid=(1,),
+        in_specs=[
+            pl.BlockSpec((rows, width), lambda i, ids: (ids[0], ids[1])),
+            half,
+            half,
+            whole(extra.shape),
+            whole(near.shape),
+            pl.BlockSpec(memory_space=pltpu.SMEM),
+        ],
+        out_specs=whole((rows + EXTRA, width)),
+    )
     return pl.pallas_call(
-        pack_kernel,
-        grid=(heads,),
-        in_specs=[column, column, whole(extra.shape)],
-        out_specs=pl.BlockSpec(block, lambda h: (h, 0)),
-        out_shape=jax.ShapeDtypeStruct((heads * block[0], block[1]), keys.dtype),
-        compiler_params=params(BIG),
-        cost_estimate=cost(0, 8 * tokens * width),
-        name="pack_heads",
-    )(keys, values, extra)
-
-
-def encode_kernel(pos, tokens, q_ref, kv_ref, bias_ref, out_ref):
-    rows = q_ref.shape[0]
-    queries = q_ref[...]
-    ones = jnp.ones((tokens, LANES), jnp.bfloat16)
-    row_bits = kv_ref.shape[1]
-    top = jnp.full((rows, 1), -jnp.inf, jnp.float32)
-    acc = jnp.zeros((rows, 2 * HEAD_DIM), jnp.float32)
-    for j in range(pos):
-        base = j * (tokens + EXTRA)
-        band = slice(base, base + tokens)
-        scores = lax.dot_general(
-            queries, kv_ref[band, :HEAD_DIM], NT, preferred_element_type=jnp.float32
+        encode_kernel,
+        grid_spec=grid_spec,
+        out_shape=jax.ShapeDtypeStruct((rows + EXTRA, width), jnp.bfloat16),
+        compiler_params=params(32),
+        cost_estimate=cost(16 * rows * tokens * width, 8 * tokens * width, rows * tokens * 8),
+        name="encode_rows",
+    )(ids, queries, keys, values, extra, near, bias)
+
+
+def merge_kernel(count, ids_ref, *refs):
+    parts, (mine_ref, near_ref, all_ref) = refs[:count], refs[count:]
+    rows, width = all_ref.shape
+    heads = width // HEAD_DIM
+    stats = [v[rows:, :].astype(jnp.float32).T for v in parts]
+    for h in range(heads):
+        cols = slice(h * HEAD_DIM, (h + 1) * HEAD_DIM)
+        lses = [
+            s[:, h : h + 1] + s[:, heads + h : heads + h + 1] + s[:, 2 * heads + h : 2 * heads + h + 1]
+            for s in stats
+        ]
+        top = functools.reduce(jnp.maximum, lses)
+        factors = [jnp.exp2(v - top) for v in lses]
+        inverse = 1.0 / functools.reduce(jnp.add, factors)
+        merged = functools.reduce(
+            jnp.add,
+            [v[:rows, cols].astype(jnp.float32) * (f * inverse) for v, f in zip(parts, factors)],
         )
-        tail = kv_ref[base + tokens : base + tokens + EXTRA, :].astype(jnp.float32)
-        kind = jnp.concatenate([tail[r : r + 1] for r in range(tokens // row_bits)], axis=1)
-        bias = jnp.zeros_like(kind)
-        for m in range(bias_ref.shape[0]):
-            bias = jnp.where(kind == m, bias_ref[m] * LOG2E, bias)
-        scores = scores * EXP2_SCALE + bias
-        new_top = jnp.maximum(top, jnp.max(scores, axis=1, keepdims=True))
-        weights = jnp.exp2(scores - new_top).astype(jnp.bfloat16)
-        acc = acc * jnp.exp2(top - new_top) + jnp.dot(
-            weights,
-            jnp.concatenate([kv_ref[band, HEAD_DIM:], ones], axis=1),
-            preferred_element_type=jnp.float32,
-        )
-        top = new_top
-    out_ref[...] = (acc[:, :HEAD_DIM] / acc[:, HEAD_DIM:]).astype(jnp.bfloat16)
-
-
-def encode(queries, kv, bias, pos):
-    latents = queries.shape[0]
-    tokens = kv.shape[0] // pos - EXTRA
-    rows = min(512, latents)
-    block = pl.BlockSpec((rows, HEAD_DIM), lambda i: (i, 0))
+        all_ref[:, cols] = merged.astype(jnp.bfloat16)
+    own = rows // 2
+    mine_ref[...] = all_ref[pl.ds(pl.multiple_of(ids_ref[0] * own, own), own), :]
+    near_ref[...] = all_ref[pl.ds(pl.multiple_of((1 - ids_ref[0]) * own, own), own), :]
+
+
+def merge(which, parts):
+    long, width = parts[0].shape
+    rows = long - EXTRA
+    grid_spec = pltpu.PrefetchScalarGridSpec(
+        num_scalar_prefetch=1,
+        grid=(1,),
+        in_specs=[whole(v.shape) for v in parts],
+        out_specs=[whole((rows // 2, width))] * 2,
+        scratch_shapes=[pltpu.VMEM((rows, width), jnp.bfloat16)],
+    )
     return pl.pallas_call(
-        functools.partial(encode_kernel, pos, tokens),
-        grid=(latents // rows,),
-        in_specs=[block, whole(kv.shape), pl.BlockSpec(memory_space=pltpu.SMEM)],
-        out_specs=block,
-        out_shape=jax.ShapeDtypeStruct((latents, HEAD_DIM), jnp.bfloat16),
-        compiler_params=params(BIG),
-        cost_estimate=cost(
-            16 * latents * tokens * pos * HEAD_DIM, 2 * kv.size, latents * tokens * pos
-        ),
-        name="encode_head",
-    )(queries, kv, bias)
-
-
-def project_kernel(heads, far, ids_ref, att_in_ref, *refs):
-    w_refs, out_ref, att_ref = refs[:-2], refs[-2], refs[-1]
-    rows = att_ref.shape[0]
-    for h in range(heads):
-        att_ref[:, h * HEAD_DIM : (h + 1) * HEAD_DIM] = att_in_ref[h * rows : (h + 1) * rows, :]
-    cols = w_refs[0].shape[1]
+        functools.partial(merge_kernel, len(parts)),
+        grid_spec=grid_spec,
+        out_shape=[jax.ShapeDtypeStruct((rows // 2, width), jnp.bfloat16)] * 2,
+        compiler_params=params(32),
+        cost_estimate=cost(8 * rows * width, 10 * rows * width),
+        name="merge_rows",
+    )(which.reshape(1), *parts)
+
+
+def project_kernel(far, ids_ref, mine_ref, near_ref, *refs):
+    w_ref, far_ref, far_other_ref, near_w_ref, near_other_ref, out_ref, att_ref = refs
+    part = mine_ref.shape[1]
+    first = ids_ref[2 * far]
+    att_ref[:, pl.ds(pl.multiple_of(first * part, part), part)] = mine_ref[...]
+    att_ref[:, pl.ds(pl.multiple_of((1 - first) * part, part), part)] = near_ref[...]
+    cols = w_ref.shape[1]
     depth = att_ref.shape[1] // 2
+    share = ids_ref[2 * far + 1]
+    halves = [
+        att_ref[:, pl.ds(pl.multiple_of(v * depth, depth), depth)] for v in (share, 1 - share)
+    ]
 
     def place(slot, value):
         out_ref[:, pl.ds(pl.multiple_of(ids_ref[slot] * cols, cols), cols)] = value
 
-    for slot in range(2):
-        place(slot, jnp.dot(att_ref[...], w_refs[slot][...], preferred_element_type=jnp.float32))
-    mine, theirs = [
-        att_ref[:, pl.ds(pl.multiple_of(ids_ref[2 * far + k] * depth, depth), depth)]
-        for k in range(2)
-    ]
-    for j in range(2):
-        for k in range(far - 1):
-            band = slice(k * depth, (k + 1) * depth)
-            total = jnp.dot(
-                mine, w_refs[2 + 2 * j][band, :], preferred_element_type=jnp.float32
-            ) + jnp.dot(theirs, w_refs[3 + 2 * j][band, :], preferred_element_type=jnp.float32)
-            place(2 + j * (far - 1) + k, total)
-
-
-def project(ids, attended, weights, rows):
-    heads = attended.shape[0] // rows
+    place(0, jnp.dot(att_ref[...], w_ref[...], preferred_element_type=jnp.float32))
+    for slot in range(1, 2 * far):
+        refs = (far_ref, far_other_ref) if slot < far else (near_w_ref, near_other_ref)
+        start = (slot - 1 if slot < far else slot - far) * (depth + EXTRA)
+        terms = [
+            jnp.dot(v, w[start : start + depth, :], preferred_element_type=jnp.float32)
+            for v, w in zip(halves, refs)
+        ]
+        place(slot, terms[0] + terms[1])
+
+
+def project(ids, mine, near, weights):
+    rows, part = mine.shape
     far = (ids.shape[0] - 2) // 2
-    width = heads * HEAD_DIM
     out_cols = 2 * far * weights[0].shape[1]
     grid_spec = pltpu.PrefetchScalarGridSpec(
         num_scalar_prefetch=1,
         grid=(1,),
-        in_specs=[whole(v.shape) for v in (attended, *weights)],
+        in_specs=[whole(v.shape) for v in (mine, near, *weights)],
         out_specs=whole((rows, out_cols)),
-        scratch_shapes=[pltpu.VMEM((rows, width), jnp.bfloat16)],
+        scratch_shapes=[pltpu.VMEM((rows, 2 * part), jnp.bfloat16)],
     )
     return pl.pallas_call(
-        functools.partial(project_kernel, heads, far),
+        functools.partial(project_kernel, far),
         grid_spec=grid_spec,
         out_shape=jax.ShapeDtypeStruct((rows, out_cols), jnp.float32),
         compiler_params=params(BIG),
-        cost_estimate=cost(2 * rows * width * out_cols, 2 * width * out_cols + 4 * rows * out_cols),
+        cost_estimate=cost(4 * rows * part * out_cols, 4 * part * out_cols + 4 * rows * out_cols),
         name="project_rows",
-    )(ids, attended, *weights)
+    )(ids, mine, near, *weights)
 
 
 def norm_kernel(
@@ -364,13 +409,17 @@
     def arrange():
         for j in range(slots):
             at = ids_ref[1 + j]
+            start = pl.multiple_of((at % (slots // 2)) * depth, depth)
+
+            def copy(pieces):
+                for r, piece in enumerate(pieces):
+                    normed_ref[r * rows : (r + 1) * rows, j * depth : (j + 1) * depth] = piece[
+                        :, pl.ds(start, depth)
+                    ]
+
             is_mine = at // (slots // 2) == ids_ref[0]
-            start = pl.multiple_of((at % (slots // 2)) * depth, depth)
-            for r in range(pieces):
-                both = [v[r][:, pl.ds(start, depth)] for v in (mine, theirs)]
-                normed_ref[r * rows : (r + 1) * rows, j * depth : (j + 1) * depth] = jnp.where(
-                    is_mine, both[0], both[1]
-                )
+            pl.when(is_mine)(functools.partial(copy, mine))
+            pl.when(jnp.logical_not(is_mine))(functools.partial(copy, theirs))
 
     for j, band in enumerate(w_refs):
         w_ref[j * depth : (j + 1) * depth, :] = band[...]
@@ -477,6 +526,11 @@
     return [(i, i ^ 1) for i in range(size)]
 
 
+def shift_perm(size, k):
+    far = size // 2
+    return [(((z + k) % far) * 2 + y, z * 2 + y) for z in range(far) for y in range(2)]
+
+
 def hop_perm(size, step, way):
     far = size // 2
     moves = [(z, z + 1) for z in range(step - 1, far - 1)]
@@ -503,7 +557,6 @@
     query_counts,
 ):
     groups, pos = sizes
-    far = pos // 2
     p = lax.axis_index("pos")
     place = lax.axis_index("head")
     rows = latent_array.shape[0]
@@ -511,8 +564,6 @@
     heads = half_width // HEAD_DIM
     mods = enc_bias.shape[0]
     modality = jnp.arange(mods, dtype=jnp.int32)
-    pair = 2 * HEAD_DIM
-
     far, z, y, x = pos // 2, p // 2, p % 2, lax.axis_index("groups") % 2
     near = swap_perm(pos)
 
@@ -521,6 +572,9 @@
 
     def over_near(value):
         return lax.ppermute(value, "pos", near)
+
+    def over_far(value, k):
+        return lax.ppermute(value, "pos", shift_perm(pos, k))
 
     def hop(step, pair):
         return [
@@ -530,96 +584,97 @@
     def by_shift(hops, k):
         return jnp.where(z + k < far, hops[k][1], hops[far - k][0])
 
-    out_half = w_out.shape[0] // 2
-    out_sent = lax.dynamic_slice_in_dim(w_out, x * out_half, out_half, 0)
-    out_hops = {0: [out_sent, out_sent]}
-    for step in range(1, far):
-        out_hops[step] = hop(step, out_hops[step - 1])
-    out_near = over_near(w_out)
-    out_ids = [p, p ^ 1]
-    for j in range(2):
-        out_ids += [((z + k) % far) * 2 + (y ^ j) for k in range(1, far)]
-    out_ids = jnp.stack([*out_ids, x, 1 - x]).astype(jnp.int32)
-
-    part = half_width // 2
+    q_onehot = (query_ids[:, None] == modality[None, :]).astype(jnp.int32)
+    local_counts = jnp.sum(q_onehot, axis=0)
 
     def columns(arrays, which):
+        part = half_width // 2
         return jnp.concatenate(
             [lax.dynamic_slice_in_dim(v, which * part, part, 1) for v in arrays], axis=1
         )
 
+    extra = jnp.pad(input_ids[None, :], ((0, EXTRA - 1), (0, half_width - tokens)))
+    extra = extra.astype(jnp.bfloat16)
+    near_inputs = over_near(
+        jnp.concatenate([columns((enc_keys, enc_values), 1 - y), extra], axis=0)
+    )
+
+    out_half, out_cols = w_out.shape[0] // 2, w_out.shape[1]
+    counted = jnp.concatenate([local_counts // 16, local_counts % 16])
+    counted = jnp.pad(counted[None, :], ((0, EXTRA - 1), (0, out_cols - 2 * mods)))
+    counted = counted.astype(jnp.bfloat16)
+
+    def half_of_out(which):
+        own = lax.dynamic_slice_in_dim(w_out, which * out_half, out_half, 0)
+        return jnp.concatenate([own, counted])
+
+    out_sent = half_of_out(x)
+    out_far = [over_far(out_sent, k) for k in range(1, far)]
+    places = [((z + k) % far) * 2 + (y ^ j) for j in range(2) for k in range(far)]
+    kv_for_near = columns((w_key, w_value), 1 - y)
+    near_inputs, out_far, out_sent, kv_for_near = lax.optimization_barrier(
+        (near_inputs, out_far, out_sent, kv_for_near)
+    )
+    out_far = jnp.concatenate(out_far)
+    out_near = over_near(jnp.concatenate([out_sent, out_far]))
+    out_far_other = over_groups(out_far)
+
     kv_own = columns((w_key, w_value), y)
-    kv_near = over_near(columns((w_key, w_value), 1 - y))
-    lookup = jnp.dot(
-        (query_ids[:, None] == modality[None, :]).astype(jnp.bfloat16),
-        query_table,
-        preferred_element_type=jnp.float32,
-    )
-    queries = (query_features.astype(jnp.float32) + lookup).astype(jnp.bfloat16)
-    own_queries = columns((queries,), y)
-    near_queries = over_near(columns((queries,), 1 - y))
-
-
-    q_onehot = (query_ids[:, None] == modality[None, :]).astype(jnp.int32)
-    local_counts = jnp.sum(q_onehot, axis=0)
-    id_rows = tokens // pair
-    counted = jnp.concatenate([local_counts // 16, local_counts % 16])
-    extra = jnp.concatenate(
-        [
-            input_ids.reshape(id_rows, pair),
-            jnp.pad(counted[None, :], ((0, EXTRA - id_rows - 1), (0, pair - 2 * mods))),
-        ]
-    ).astype(jnp.bfloat16)
-    payload = pack(enc_keys, enc_values, extra)
-    kv = lax.all_to_all(payload, "pos", 0, 0, tiled=True)
-    head_queries = lax.dynamic_slice_in_dim(latent_queries, p * HEAD_DIM, HEAD_DIM, 1)
-    head_bias = lax.dynamic_slice_in_dim(enc_bias, p, 1, 1)[:, 0]
+    kv_near = over_near(kv_for_near)
+
+    ids = [jnp.stack([(z - k) % far, y]).astype(jnp.int32) for k in range(far)]
+    head_bias = lax.dynamic_slice_in_dim(enc_bias, y * (heads // 2), heads // 2, 1)
+    order = sorted(range(1, far), key=lambda k: -min(k, far - k)) + [0]
+    results = {}
+    for k in order:
+        result = encode(
+            ids[k], latent_queries, enc_keys, enc_values, extra, near_inputs, head_bias, 2 * rows
+        )
+        results[k], near_inputs = lax.optimization_barrier((result, near_inputs))
+    parts = [over_far(results[k], k) for k in order[:-1]]
+    result, out_far_other = lax.optimization_barrier((results[0], out_far_other))
+    parts.append(result)
+    out_near_other = over_near(jnp.concatenate([half_of_out(1 - x), out_far_other]))
+
     def kept_queries():
-        counts = kv.reshape(pos, tokens + EXTRA, pair)[:, tokens + id_rows, : 2 * mods]
+        far_counts = out_far.reshape(far - 1, out_half + EXTRA, out_cols)[:, out_half, : 2 * mods]
+        near_counts = out_near.reshape(far, out_half + EXTRA, out_cols)[:, out_half, : 2 * mods]
+        counts = jnp.concatenate([counted[:1, : 2 * mods], far_counts, near_counts])
         counts = counts.astype(jnp.int32)
         counts = counts[:, :mods] * 16 + counts[:, mods:]
-        earlier = jnp.arange(pos, dtype=jnp.int32)[:, None] < p
+        earlier = jnp.stack(places)[:, None] < p
         before = jnp.sum(jnp.where(earlier, counts, 0), axis=0)
         within = jnp.cumsum(q_onehot, axis=0) - q_onehot
         ranked = jnp.sum((within + before[None, :]) * q_onehot, axis=1)
         limits = jnp.sum(q_onehot * query_counts[None, :], axis=1)
         return ranked < limits
 
+    parts, out_near, out_far_other, out_near_other, kv_near = lax.optimization_barrier(
+        (parts, out_near, out_far_other, out_near_other, kv_near)
+    )
     kv_sent = jnp.where(x == 0, kv_own, kv_near)
     hops = {0: [kv_sent, kv_sent]}
     hops[1] = hop(1, hops[0])
-    kv, hops, near_queries, out_hops, out_near = lax.optimization_barrier(
-        (kv, hops, near_queries, out_hops, out_near)
-    )
-    out_far = jnp.concatenate([by_shift(out_hops, k) for k in range(1, far)])
-    out_bands = [out_far, over_near(out_far), over_groups(out_far)]
+    attended, for_near = merge(y, parts)
+    from_near = over_near(for_near)
+    kept = kept_queries()
+    from_near, hops, kept = lax.optimization_barrier((from_near, hops, kept))
     hops[2] = hop(2, hops[1])
-    attended = encode(head_queries, kv, head_bias, pos)
-    attended, hops, out_bands = lax.optimization_barrier((attended, hops, out_bands))
-    out_far, out_across, out_other = out_bands
-    out_bands = [w_out, out_near, out_far, out_other, out_across, over_near(out_other)]
-    moved = {k: by_shift(hops, k) for k in range(1, far) if max(k, far - k) < 3}
-    swapped = {k: over_groups(v) for k, v in moved.items()}
-    for step in range(3, far):
-        hops[step] = hop(step, hops[step - 1])
-    attended = lax.all_to_all(attended, "pos", 0, 0, tiled=True)
-    kept = kept_queries()
-    attended, hops, out_bands, kept, swapped = lax.optimization_barrier(
-        (attended, hops, out_bands, kept, swapped)
-    )
-    for k in range(1, far):
-        if k not in moved:
-            moved[k] = by_shift(hops, k)
-            swapped[k] = over_groups(moved[k])
-    partial_value = project(out_ids, attended, out_bands, rows)
+    out_ids = jnp.stack([*places, y, x]).astype(jnp.int32)
+    weights = [w_out, out_far, out_far_other, out_near, out_near_other]
+    partial_value = project(out_ids, attended, from_near, weights)
     theirs = lax.ppermute(partial_value, "head", swap_perm(2))
+    theirs, hops = lax.optimization_barrier((theirs, hops))
     own_cols, normed, normed_other = normalise(
         place, partial_value, theirs, latent_array, norm_gain[None, :]
     )
-    kv_bands = [kv_own, kv_near]
+    lookup = jnp.dot(q_onehot.astype(jnp.bfloat16), query_table, preferred_element_type=jnp.float32)
+    queries = (query_features.astype(jnp.float32) + lookup).astype(jnp.bfloat16)
+    own_queries = columns((queries,), y)
+    near_queries = over_near(columns((queries,), 1 - y))
+
     kv_at = [p, p ^ 1]
     for k in range(1, far):
-        kv_bands += [moved[k], swapped[k]]
         there = ((z + k) % far) * 2
         kv_at += [there + (y ^ x), there + (1 - (y ^ x))]
     kv_ids = jnp.stack([place, *kv_at]).astype(jnp.int32)
@@ -646,7 +701,20 @@
 
     came = {0: [normed, normed]}
     came[1] = hop(1, came[0])
-    came, normed_near, kv_bands = lax.optimization_barrier((came, over_near(normed), kv_bands))
+    moved = {k: by_shift(hops, k) for k in range(1, far) if max(k, far - k) < 3}
+    swapped = {k: over_groups(v) for k, v in moved.items()}
+    for step in range(3, far):
+        hops[step] = hop(step, hops[step - 1])
+    came, normed_near, hops, swapped = lax.optimization_barrier(
+        (came, over_near(normed), hops, swapped)
+    )
+    for k in range(1, far):
+        if k not in moved:
+            moved[k] = by_shift(hops, k)
+            swapped[k] = over_groups(moved[k])
+    kv_bands = [kv_own, kv_near]
+    for k in range(1, far):
+        kv_bands += [moved[k], swapped[k]]
     mine, other = [normed, normed_near], [normed_other, *cores([normed_near])]
     keys_values = []
     for step in range(1, far):
@@ -659,8 +727,8 @@
         if step > 1:
             keys_values.append(fold(mine, other))
             mine, other = [], []
-        came, fresh_near, mine, other, keys_values = lax.optimization_barrier(
-            (came, fresh_near, mine, other, keys_values)
+        came, fresh_near, mine, other, keys_values, near_queries = lax.optimization_barrier(
+            (came, fresh_near, mine, other, keys_values, near_queries)
         )
         mine.append(fresh_near)
         other += cores([fresh_near])
@@ -685,9 +753,10 @@
         and pos % 2 == 0
         and pos > 2
         and groups % 2 == 0
-        and enc_keys.shape[1] == pos * HEAD_DIM
-        and enc_keys.shape[0] % (2 * HEAD_DIM) == 0
-        and enc_keys.shape[0] < 2048
+        and enc_keys.shape[1] % (4 * HEAD_DIM) == 0
+        and 3 * enc_keys.shape[1] <= 2 * HEAD_DIM * EXTRA
+        and enc_keys.shape[0] % LANES == 0
+        and enc_keys.shape[0] <= enc_keys.shape[1]
         and w_key.shape[0] % LANES == 0
         and w_out.shape[0] % (2 * LANES) == 0
         and w_out.shape[1] % LANES == 0

time: 278 us -> 301 us (1.083)
  waiting for transfers between devices: 100 us -> 148 us
  starting transfers between devices: 72.6 us -> 43.5 us
    ppermute x0 -> x6, waiting for transfers between devices: none -> 36.3 us  [over_far(): return lax.ppermute(value, 'pos', shift_perm(pos, k))]
    ppermute x9 -> x10, waiting for transfers between devices: 14.8 us -> 49.4 us  [over_near(): return lax.ppermute(value, 'pos', near)]
    ppermute x18 -> x12, starting transfers between devices: 44.9 us -> 16.5 us  [hop(): lax.ppermute(v, 'pos', hop_perm(pos, step, way))]
    ppermute x18 -> x12, waiting for transfers between devices: 55.9 us -> 39.2 us  [hop(): lax.ppermute(v, 'pos', hop_perm(pos, step, way))]
    all_to_all x2 -> x0, starting transfers between devices: 12.1 us -> none  [the longest x1 7.41 us: fast_on_device(): kv = lax.all_to_all(payload, 'pos', 0, 0, tiled=True)]
    ppermute x0 -> x6, starting transfers between devices: none -> 11.3 us  [over_far(): return lax.ppermute(value, 'pos', shift_perm(pos, k))]
    ppermute x4, waiting for transfers between devices: 20.5 us -> 13.9 us  [over_groups(): return lax.ppermute(value, 'groups', swap_perm(groups))]
    concatenate x2 -> x4, other arithmetic: 0.66 us -> 4.68 us  [the longest x1 2.38 us: fast_on_device(): out_near = over_near(jnp.concatenate([out_sent, out_far]))]
  transfers between devices with their start and end apart: 42 -> 41, of which waited for: 17 -> 20; matrix products, arithmetic and copies ran while one was open for 6% -> 6% of each run, Pallas kernels for 17% -> 17%
where the time goes in v6:
time: 301 us; the launch traced here: 300 us
  waiting for transfers between devices  148 us (49%)
  Pallas kernels  70.8 us (24%)
  starting transfers between devices  43.5 us (14%)
  local copies, waits for them, and re-layouts  17.9 us (6%)
  other arithmetic  17.8 us (6%)
    ppermute x10, waiting for transfers between devices, over_near(): return lax.ppermute(value, 'pos', near)  49.4 us
    ppermute x12, waiting for transfers between devices, hop(): lax.ppermute(v, 'pos', hop_perm(pos, step, way))  39.2 us
    ppermute x6, waiting for transfers between devices, over_far(): return lax.ppermute(value, 'pos', shift_perm(pos, k))  36.3 us
    pallas_call x3, Pallas kernels, latent_keys_values(): pl.pallas_call(functools.partial(latents_kernel, pieces), grid_spec=grid_...  24.2 us
    pallas_call x2, Pallas kernels, decode(): pl.pallas_call(functools.partial(decode_kernel, len(keys_values)), grid=(...  16.8 us
    pallas_call x4, Pallas kernels, encode(): pl.pallas_call(encode_kernel, grid_spec=grid_spec, out_shape=jax.ShapeDty...  16.7 us
    ppermute x12, starting transfers between devices, hop(): lax.ppermute(v, 'pos', hop_perm(pos, step, way))  16.5 us
    ppermute x4, waiting for transfers between devices, over_groups(): return lax.ppermute(value, 'groups', swap_perm(groups))  13.9 us
  transfers between devices with their start and end apart: 41, of which 20 were waited for; matrix products, arithmetic and copies ran while one was open for 6% of the time, Pallas kernels for 17%

profile of v6, /device:TPU:0, one launch (start us, length us, event | category | flops | bytes accessed | tf_op | source)
XLA Modules:
  0.0 300.1 jit_solution(11225562982036359232)
XLA Ops:
  1.4 1.3 constant_dynamic-slice_fusion.9
  3.9 3.0 collective-permute-start
  7.9 3.7 %collective-permute-start.1 = (bf16[528,256]{1,0:T(8,128)(2,1)S(1)}, bf16[528,256]{1,0:T(8,128)(2,1)}, u32[]{:S(2)}, u32[]{:S(2)}) collective-permute-start(bf16[528,256]{1,0:T(8,128)(2,1)S(1)} %pad_maximum_fusion.5), channel_id=1, source_target_pairs={{4,0},{6,2},{8,4},{10,6},{12,8},{14,10},{0,12},{2,14},{5,1},{7,3},... | collective-permute-start | bytes 811016 | tf_op jit(solution)/shard_map/ppermute | solution.py:577
  12.9 2.2 constant_dynamic-slice_fusion.2
  15.9 2.6 collective-permute-done.1
  18.5 15.9 %collective-permute-done.2 = bf16[528,256]{1,0:T(8,128)(2,1)} collective-permute-done((bf16[528,256]{1,0:T(8,128)(2,1)S(1)}, bf16[528,256]{1,0:T(8,128)(2,1)}, u32[]{:S(2)}, u32[]{:S(2)}) %collective-permute-start.2) | collective-permute-done | bytes 270368 | tf_op jit(solution)/shard_map/ppermute | solution.py:577
  37.3 1.6 collective-permute-start.7
  38.9 4.1 %encode_rows.4 = bf16[528,512]{1,0:T(8,128)(2,1)S(1)} custom-call(s32[2]{0:T(128)S(1)} %pad_add_fusion.ids_ref, bf16[2048,1024]{1,0:T(8,128)(2,1)S(1)} %copy-done.1, bf16[512,1024]{1,0:T(8,128)(2,1)S(1)} %copy-done.2, bf16[512,1024]{1,0:T(8,128)(2,1)S(1)} %copy-done.3, bf16[16,1024]{1,0:T(8,128)(2,1)S(1)} %pad.10.extra_ref, ...), custom_call_target="tpu_custom_call" | custom-call | flops 2147483648 | bytes 2097152 | tf_op jit(solution)/shard_map/encode_rows/pallas_call | solution.py:261
  43.8 4.1 %encode_rows.5 = bf16[528,512]{1,0:T(8,128)(2,1)S(1)} custom-call(s32[2]{0:T(128)S(1)} %get-tuple-element.150.ids_ref, bf16[2048,1024]{1,0:T(8,128)(2,1)S(1)} %copy-done.1, bf16[512,1024]{1,0:T(8,128)(2,1)S(1)} %copy-done.2, bf16[512,1024]{1,0:T(8,128)(2,1)S(1)} %copy-done.3, bf16[16,1024]{1,0:T(8,128)(2,1)S(1)} %pad.10.extra_ref, ...), custom_call_target="tpu_custom_call" | custom-call | flops 2147483648 | bytes 2097152 | tf_op jit(solution)/shard_map/encode_rows/pallas_call | solution.py:261
  48.8 4.1 %encode_rows.6 = bf16[528,512]{1,0:T(8,128)(2,1)S(1)} custom-call(s32[2]{0:T(128)S(1)} %get-tuple-element.151.ids_ref, bf16[2048,1024]{1,0:T(8,128)(2,1)S(1)} %copy-done.1, bf16[512,1024]{1,0:T(8,128)(2,1)S(1)} %copy-done.2, bf16[512,1024]{1,0:T(8,128)(2,1)S(1)} %copy-done.3, bf16[16,1024]{1,0:T(8,128)(2,1)S(1)} %pad.10.extra_ref, ...), custom_call_target="tpu_custom_call" | custom-call | flops 2147483648 | bytes 2097152 | tf_op jit(solution)/shard_map/encode_rows/pallas_call | solution.py:261
  53.8 4.3 %encode_rows.7.refs_3_ = bf16[528,512]{1,0:T(8,128)(2,1)S(1)} custom-call(s32[2]{0:T(128)S(1)} %pad_add_fusion.3.ids_ref, bf16[2048,1024]{1,0:T(8,128)(2,1)S(1)} %copy-done.1, bf16[512,1024]{1,0:T(8,128)(2,1)S(1)} %copy-done.2, bf16[512,1024]{1,0:T(8,128)(2,1)S(1)} %copy-done.3, bf16[16,1024]{1,0:T(8,128)(2,1)S(1)} %pad.10.extra_ref, ...), custom_call_target="tpu_custom_call" | custom-call | flops 2147483648 | bytes 2097152 | tf_op jit(solution)/shard_map/encode_rows/pallas_call | solution.py:261
  58.1 2.4 pad_maximum_fusion.1
  61.0 1.5 collective-permute-start.10
  65.1 3.1 %collective-permute-start.5 = (bf16[528,512]{1,0:T(8,128)(2,1)S(1)}, bf16[528,512]{1,0:T(8,128)(2,1)S(1)}, u32[]{:S(2)}, u32[]{:S(2)}) collective-permute-start(bf16[528,512]{1,0:T(8,128)(2,1)S(1)} %copy-done.9), channel_id=1, source_target_pairs={{4,0},{6,2},{8,4},{10,6},{12,8},{14,10},{0,12},{2,14},{5,1},{7,3},... | collective-permute-start | bytes 1622024 | tf_op jit(solution)/shard_map/ppermute | solution.py:577
  68.1 30.7 %collective-permute-done.10.refs_11_.refs_5_.refs_3_ = bf16[256,1024]{1,0:T(8,128)(2,1)} collective-permute-done((bf16[256,1024]{1,0:T(8,128)(2,1)}, bf16[256,1024]{1,0:T(8,128)(2,1)}, u32[]{:S(2)}, u32[]{:S(2)}) %collective-permute-start.10) | collective-permute-done | bytes 524320 | tf_op jit(solution)/shard_map/ppermute | solution.py:574
  98.9 2.8 collective-permute-start.4
  103.8 17.9 %collective-permute-done.4.refs_0_ = bf16[528,512]{1,0:T(8,128)(2,1)} collective-permute-done((bf16[528,512]{1,0:T(8,128)(2,1)S(1)}, bf16[528,512]{1,0:T(8,128)(2,1)}, u32[]{:S(2)}, u32[]{:S(2)}) %collective-permute-start.4) | collective-permute-done | bytes 540704 | tf_op jit(solution)/shard_map/ppermute | solution.py:577
  121.8 2.0 pad_maximum_fusion.4
  123.7 2.1 collective-permute-start.12
  128.6 2.9 merge_rows.1
  132.9 7.5 %collective-permute-done.11.near_ref = bf16[256,512]{1,0:T(8,128)(2,1)S(1)} collective-permute-done((bf16[256,512]{1,0:T(8,128)(2,1)S(1)}, bf16[256,512]{1,0:T(8,128)(2,1)S(1)}, u32[]{:S(2)}, u32[]{:S(2)}) %collective-permute-start.11) | collective-permute-done | bytes 262176 | tf_op jit(solution)/shard_map/ppermute | solution.py:574
  141.6 5.7 %project_rows.1.mine_ref = f32[256,2048]{1,0:T(8,128)} custom-call(s32[10]{0:T(128)} %stack.110.ids_ref, bf16[256,512]{1,0:T(8,128)(2,1)} %copy-done.12, bf16[256,512]{1,0:T(8,128)(2,1)} %copy-done.32, bf16[1024,256]{1,0:T(8,128)(2,1)} %refs_0_.1, bf16[1584,256]{1,0:T(8,128)(2,1)} %copy-done.19, bf16[1584,256]{1,0:T(8,128)(2,1)} %copy-done.13, ...), custom_call_target="tpu_custom_call" | custom-call | flops 1073741824 | bytes 6291456 | tf_op jit(solution)/shard_map/project_rows/pallas_call | solution.py:353
  149.3 16.1 %collective-permute-done.16 = bf16[256,1024]{1,0:T(8,128)(2,1)} collective-permute-done((bf16[256,1024]{1,0:T(8,128)(2,1)}, bf16[256,1024]{1,0:T(8,128)(2,1)}, u32[]{:S(2)}, u32[]{:S(2)}) %collective-permute-start.16) | collective-permute-done | bytes 524320 | tf_op jit(solution)/shard_map/ppermute | solution.py:581
  165.4 1.5 broadcast_select_fusion.3.refs_14_.refs_8_.refs_6_
  167.7 4.6 %norm_rows.1 = (f32[256,1024]{1,0:T(8,128)}, bf16[256,1024]{1,0:T(8,128)(2,1)}, bf16[256,1024]{1,0:T(8,128)(2,1)}) custom-call(s32[1]{0:T(128)} %bitcast.ids_ref, f32[256,2048]{1,0:T(8,128)} %project_rows.1.mine_ref, f32[256,2048]{1,0:T(8,128)} %copy-done.17, bf16[256,2048]{1,0:T(8,128)(2,1)} %latent_ref.1, f32[1,2048]{1,0:T(1,128)} %bitcast.49), custom_call_target="tpu_custom_call" | custom-call | flops 3145728 | bytes 6815744 | tf_op jit(solution)/shard_map/norm_rows/pallas_call | solution.py:387
  172.3 3.7 %collective-permute-start.17 = (bf16[256,1024]{1,0:T(8,128)(2,1)}, bf16[256,1024]{1,0:T(8,128)(2,1)S(1)}, u32[]{:S(2)}, u32[]{:S(2)}) collective-permute-start(bf16[256,1024]{1,0:T(8,128)(2,1)} %get-tuple-element.112.refs_0_), channel_id=1, source_target_pairs={{0,4},{2,6},{4,8},{6,10},{8,12},{10,14},{1,5},{3,7},{5,9},{7,11},{... | collective-permute-start | bytes 1572872 | tf_op jit(solution)/shard_map/ppermute | solution.py:581
  178.6 2.1 collective-permute-done.22.refs_15_.refs_9_.refs_7_
  183.4 3.4 %collective-permute-done.17 = bf16[256,1024]{1,0:T(8,128)(2,1)S(1)} collective-permute-done((bf16[256,1024]{1,0:T(8,128)(2,1)}, bf16[256,1024]{1,0:T(8,128)(2,1)S(1)}, u32[]{:S(2)}, u32[]{:S(2)}) %collective-permute-start.17) | collective-permute-done | bytes 524320 | tf_op jit(solution)/shard_map/ppermute | solution.py:581
  187.3 5.8 %collective-permute-done.18 = bf16[256,1024]{1,0:T(8,128)(2,1)} collective-permute-done((bf16[256,1024]{1,0:T(8,128)(2,1)}, bf16[256,1024]{1,0:T(8,128)(2,1)}, u32[]{:S(2)}, u32[]{:S(2)}) %collective-permute-start.18) | collective-permute-done | bytes 524320 | tf_op jit(solution)/shard_map/ppermute | solution.py:581
  193.1 8.9 %collective-permute-done.21 = bf16[256,1024]{1,0:T(8,128)(2,1)S(1)} collective-permute-done((bf16[256,1024]{1,0:T(8,128)(2,1)}, bf16[256,1024]{1,0:T(8,128)(2,1)S(1)}, u32[]{:S(2)}, u32[]{:S(2)}) %collective-permute-start.21) | collective-permute-done | bytes 524320 | tf_op jit(solution)/shard_map/ppermute | solution.py:581
  204.5 1.3 collective-permute-start.24
  206.4 1.3 broadcast_select_fusion.1.refs_12_.refs_6_.refs_4_
  207.8 7.3 %collective-permute-done.25.refs_3_ = bf16[256,1024]{1,0:T(8,128)(2,1)} collective-permute-done((bf16[256,1024]{1,0:T(8,128)(2,1)S(1)}, bf16[256,1024]{1,0:T(8,128)(2,1)}, u32[]{:S(2)}, u32[]{:S(2)}) %collective-permute-start.25) | collective-permute-done | bytes 524320 | tf_op jit(solution)/shard_map/ppermute | solution.py:574
  215.1 1.3 collective-permute-start.35
  217.1 3.8 %collective-permute-done.24 = bf16[256,1024]{1,0:T(8,128)(2,1)S(1)} collective-permute-done((bf16[256,1024]{1,0:T(8,128)(2,1)}, bf16[256,1024]{1,0:T(8,128)(2,1)S(1)}, u32[]{:S(2)}, u32[]{:S(2)}) %collective-permute-start.24) | collective-permute-done | bytes 524320 | tf_op jit(solution)/shard_map/ppermute | solution.py:581
  223.1 1.5 collective-permute-start.31
  224.6 5.3 %collective-permute-done.35.refs_17_.refs_11_.refs_9_ = bf16[256,1024]{1,0:T(8,128)(2,1)S(1)} collective-permute-done((bf16[256,1024]{1,0:T(8,128)(2,1)S(1)}, bf16[256,1024]{1,0:T(8,128)(2,1)S(1)}, u32[]{:S(2)}, u32[]{:S(2)}) %collective-permute-start.35) | collective-permute-done | bytes 524320 | tf_op jit(solution)/shard_map/ppermute | solution.py:571
  230.6 6.5 %collective-permute-done.34.refs_13_.refs_7_.refs_5_ = bf16[256,1024]{1,0:T(8,128)(2,1)S(1)} collective-permute-done((bf16[256,1024]{1,0:T(8,128)(2,1)S(1)}, bf16[256,1024]{1,0:T(8,128)(2,1)S(1)}, u32[]{:S(2)}, u32[]{:S(2)}) %collective-permute-start.34) | collective-permute-done | bytes 524320 | tf_op jit(solution)/shard_map/ppermute | solution.py:571
  238.0 1.5 collective-permute-start.30
  240.1 12.0 %latent_keys_values.3.refs_0_.refs_3_ = bf16[1280,1024]{1,0:T(8,128)(2,1)} custom-call(s32[9]{0:T(128)} %stack.128.ids_ref, bf16[256,1024]{1,0:T(8,128)(2,1)} %get-tuple-element.112.refs_0_, bf16[256,1024]{1,0:T(8,128)(2,1)} %copy-done.37, bf16[256,1024]{1,0:T(8,128)(2,1)} %copy-done.28, bf16[256,1024]{1,0:T(8,128)(2,1)} %collective-permute-done.25.refs_3_, ...), custom_call_target="tpu_custom_call" | custom-call | flops 5368709120 | bytes 4194304 | tf_op jit(solution)/shard_map/latent_keys_values/pallas_call | solution.py:448
  257.1 6.9 %latent_keys_values.4.refs_1_.refs_4_ = bf16[512,1024]{1,0:T(8,128)(2,1)} custom-call(s32[9]{0:T(128)} %stack.128.ids_ref, bf16[256,1024]{1,0:T(8,128)(2,1)} %collective-permute-done.31.refs_0_, bf16[256,1024]{1,0:T(8,128)(2,1)} %copy-done.31, bf16[256,1024]{1,0:T(8,128)(2,1)} %copy-done.41, bf16[256,1024]{1,0:T(8,128)(2,1)} %copy-done.40, ...), custom_call_target="tpu_custom_call" | custom-call | flops 2147483648 | bytes 4194304 | tf_op jit(solution)/shard_map/latent_keys_values/pallas_call | solution.py:448
  264.0 3.9 %collective-permute-done.36.refs_0_ = bf16[256,1024]{1,0:T(8,128)(2,1)S(1)} collective-permute-done((bf16[256,1024]{1,0:T(8,128)(2,1)S(1)}, bf16[256,1024]{1,0:T(8,128)(2,1)S(1)}, u32[]{:S(2)}, u32[]{:S(2)}) %collective-permute-start.36) | collective-permute-done | bytes 524320 | tf_op jit(solution)/shard_map/ppermute | solution.py:574
  267.9 1.9 collective-permute-done.39.refs_1_
  270.6 5.3 %latent_keys_values.5.refs_2_.refs_5_ = bf16[256,1024]{1,0:T(8,128)(2,1)} custom-call(s32[9]{0:T(128)} %stack.128.ids_ref, bf16[256,1024]{1,0:T(8,128)(2,1)} %copy-done.26, bf16[256,1024]{1,0:T(8,128)(2,1)} %copy-done.27, bf16[256,1024]{1,0:T(8,128)(2,1)} %get-tuple-element.140.refs_10_.refs_4_.refs_2_, ...), custom_call_target="tpu_custom_call" | custom-call | flops 1073741824 | bytes 4194304 | tf_op jit(solution)/shard_map/latent_keys_values/pallas_call | solution.py:448
  275.9 8.3 %decode_rows.3 = bf16[512,512]{1,0:T(8,128)(2,1)} custom-call(bf16[512,512]{1,0:T(8,128)(2,1)} %copy-done.36, bf16[1280,1024]{1,0:T(8,128)(2,1)} %latent_keys_values.3.refs_0_.refs_3_, bf16[512,1024]{1,0:T(8,128)(2,1)} %latent_keys_values.4.refs_1_.refs_4_, bf16[256,1024]{1,0:T(8,128)(2,1)} %latent_keys_values.5.refs_2_.refs_5_, ...), custom_call_target="tpu_custom_call" | custom-call | flops 8589934592 | bytes 5767168 | tf_op jit(solution)/shard_map/decode_rows/pallas_call | solution.py:509
  284.5 8.4 %decode_rows.2 = f32[512,512]{1,0:T(8,128)} custom-call(bf16[512,512]{1,0:T(8,128)(2,1)} %get-tuple-element.138.q_ref, bf16[1280,1024]{1,0:T(8,128)(2,1)} %latent_keys_values.3.refs_0_.refs_3_, bf16[512,1024]{1,0:T(8,128)(2,1)} %latent_keys_values.4.refs_1_.refs_4_, bf16[256,1024]{1,0:T(8,128)(2,1)} %latent_keys_values.5.refs_2_.refs_5_, ...), custom_call_target="tpu_custom_call" | custom-call | flops 8589934592 | bytes 5767168 | tf_op jit(solution)/shard_map/decode_rows/pallas_call | solution.py:509
  292.9 5.4 %collective-permute-done.40 = bf16[512,512]{1,0:T(8,128)(2,1)S(1)} collective-permute-done((bf16[512,512]{1,0:T(8,128)(2,1)}, bf16[512,512]{1,0:T(8,128)(2,1)S(1)}, u32[]{:S(2)}, u32[]{:S(2)}) %collective-permute-start.40) | collective-permute-done | bytes 524320 | tf_op jit(solution)/shard_map/ppermute | solution.py:738
  298.5 1.6 fusion
  (180 shorter events, 43.9 us)
Async XLA Ops:
  0.6 181.3 %copy-start = (bf16[3,1024]{1,0:T(4,128)(2,1)S(1)}, bf16[3,1024]{1,0:T(4,128)(2,1)}, u32[]{:S(2)}) copy-start(bf16[3,1024]{1,0:T(4,128)(2,1)} %param.25) | copy-start | bytes 18436
  3.9 30.5 %collective-permute-start = (bf16[528,1024]{1,0:T(8,128)(2,1)}, bf16[528,1024]{1,0:T(8,128)(2,1)S(1)}, u32[]{:S(2)}, u32[]{:S(2)}) collective-permute-start(bf16[528,1024]{1,0:T(8,128)(2,1)} %pad_maximum_fusion), channel_id=1, source_target_pairs={{0,2},{2,0},{4,6},{6,4},{8,10},{10,8},{12,14},{14,12},{1,3},{3,1},... | collective-permute-start | bytes 3244040 | tf_op jit(solution)/shard_map/ppermute | solution.py:574
  7.1 31.8 %copy-start.3 = (bf16[512,1024]{1,0:T(8,128)(2,1)S(1)}, bf16[512,1024]{1,0:T(8,128)(2,1)}, u32[]{:S(2)}) copy-start(bf16[512,1024]{1,0:T(8,128)(2,1)} %v_ref.7) | copy-start | bytes 3145732
  7.9 10.6 %collective-permute-start.1 = (bf16[528,256]{1,0:T(8,128)(2,1)S(1)}, bf16[528,256]{1,0:T(8,128)(2,1)}, u32[]{:S(2)}, u32[]{:S(2)}) collective-permute-start(bf16[528,256]{1,0:T(8,128)(2,1)S(1)} %pad_maximum_fusion.5), channel_id=1, source_target_pairs={{4,0},{6,2},{8,4},{10,6},{12,8},{14,10},{0,12},{2,14},{5,1},{7,3},... | collective-permute-start | bytes 811016 | tf_op jit(solution)/shard_map/ppermute | solution.py:577
  11.5 22.8 %collective-permute-start.2 = (bf16[528,256]{1,0:T(8,128)(2,1)S(1)}, bf16[528,256]{1,0:T(8,128)(2,1)}, u32[]{:S(2)}, u32[]{:S(2)}) collective-permute-start(bf16[528,256]{1,0:T(8,128)(2,1)S(1)} %pad_maximum_fusion.5), channel_id=1, source_target_pairs={{8,0},{10,2},{12,4},{14,6},{0,8},{2,10},{4,12},{6,14},{9,1},{11,3}... | collective-permute-start | bytes 811016 | tf_op jit(solution)/shard_map/ppermute | solution.py:577
  11.5 22.8 %collective-permute-start.3 = (bf16[528,256]{1,0:T(8,128)(2,1)S(1)}, bf16[528,256]{1,0:T(8,128)(2,1)}, u32[]{:S(2)}, u32[]{:S(2)}) collective-permute-start(bf16[528,256]{1,0:T(8,128)(2,1)S(1)} %pad_maximum_fusion.5), channel_id=1, source_target_pairs={{12,0},{14,2},{0,4},{2,6},{4,8},{6,10},{8,12},{10,14},{13,1},{15,3... | collective-permute-start | bytes 811016 | tf_op jit(solution)/shard_map/ppermute | solution.py:577
  37.3 25.2 %collective-permute-start.7 = (bf16[1584,256]{1,0:T(8,128)(2,1)S(1)}, bf16[1584,256]{1,0:T(8,128)(2,1)S(1)}, u32[]{:S(2)}, u32[]{:S(2)}) collective-permute-start(bf16[1584,256]{1,0:T(8,128)(2,1)S(1)} %constant_dynamic-update-slice_fusion.refs_1_), channel_id=1, source_target_pairs={{0,16},{16,0},{1,17},{17,1},{2,18},{18,2},{3,19},{19,3},{4,20},{20... | collective-permute-start | bytes 2433032 | tf_op jit(solution)/shard_map/ppermute | solution.py:571
  58.1 40.8 %copy-start.7 = (bf16[528,512]{1,0:T(8,128)(2,1)S(1)}, bf16[528,512]{1,0:T(8,128)(2,1)}, u32[]{:S(2)}) copy-start(bf16[528,512]{1,0:T(8,128)(2,1)} %copy-done.6) | copy-start | bytes 1622020
  60.5 61.2 %copy-start.23 = (bf16[256,512]{1,0:T(8,128)(2,1)S(1)}, bf16[256,512]{1,0:T(8,128)(2,1)}, u32[]{:S(2)}) copy-start(bf16[256,512]{1,0:T(8,128)(2,1)} %get-tuple-element.144) | copy-start | bytes 786436
  60.5 61.2 %collective-permute-start.8 = (bf16[2112,256]{1,0:T(8,128)(2,1)}, bf16[2112,256]{1,0:T(8,128)(2,1)}, u32[]{:S(2)}, u32[]{:S(2)}) collective-permute-start(bf16[2112,256]{1,0:T(8,128)(2,1)} %pad_maximum_fusion.1), channel_id=1, source_target_pairs={{0,2},{2,0},{4,6},{6,4},{8,10},{10,8},{12,14},{14,12},{1,3},{3,1},... | collective-permute-start | bytes 3244040 | tf_op jit(solution)/shard_map/ppermute | solution.py:574
  61.0 37.8 %collective-permute-start.10 = (bf16[256,1024]{1,0:T(8,128)(2,1)}, bf16[256,1024]{1,0:T(8,128)(2,1)}, u32[]{:S(2)}, u32[]{:S(2)}) collective-permute-start(bf16[256,1024]{1,0:T(8,128)(2,1)} %pad_maximum_fusion.3), channel_id=1, source_target_pairs={{0,2},{2,0},{4,6},{6,4},{8,10},{10,8},{12,14},{14,12},{1,3},{3,1},... | collective-permute-start | bytes 1572872 | tf_op jit(solution)/shard_map/ppermute | solution.py:574
  63.8 57.9 %collective-permute-start.9 = (bf16[2112,256]{1,0:T(8,128)(2,1)}, bf16[2112,256]{1,0:T(8,128)(2,1)}, u32[]{:S(2)}, u32[]{:S(2)}) collective-permute-start(bf16[2112,256]{1,0:T(8,128)(2,1)} %pad_maximum_fusion.2), channel_id=1, source_target_pairs={{0,2},{2,0},{4,6},{6,4},{8,10},{10,8},{12,14},{14,12},{1,3},{3,1},... | collective-permute-start | bytes 3244040 | tf_op jit(solution)/shard_map/ppermute | solution.py:574
  64.3 64.3 %copy-start.5 = (bf16[528,512]{1,0:T(8,128)(2,1)S(1)}, bf16[528,512]{1,0:T(8,128)(2,1)}, u32[]{:S(2)}) copy-start(bf16[528,512]{1,0:T(8,128)(2,1)} %copy-done.4) | copy-start | bytes 1622020
  64.3 39.5 %collective-permute-start.6 = (bf16[528,512]{1,0:T(8,128)(2,1)S(1)}, bf16[528,512]{1,0:T(8,128)(2,1)S(1)}, u32[]{:S(2)}, u32[]{:S(2)}) collective-permute-start(bf16[528,512]{1,0:T(8,128)(2,1)S(1)} %copy-done.11), channel_id=1, source_target_pairs={{12,0},{14,2},{0,4},{2,6},{4,8},{6,10},{8,12},{10,14},{13,1},{15,3... | collective-permute-start | bytes 1622024 | tf_op jit(solution)/shard_map/ppermute | solution.py:577
  65.1 38.8 %collective-permute-start.5 = (bf16[528,512]{1,0:T(8,128)(2,1)S(1)}, bf16[528,512]{1,0:T(8,128)(2,1)S(1)}, u32[]{:S(2)}, u32[]{:S(2)}) collective-permute-start(bf16[528,512]{1,0:T(8,128)(2,1)S(1)} %copy-done.9), channel_id=1, source_target_pairs={{4,0},{6,2},{8,4},{10,6},{12,8},{14,10},{0,12},{2,14},{5,1},{7,3},... | collective-permute-start | bytes 1622024 | tf_op jit(solution)/shard_map/ppermute | solution.py:577
  98.9 22.9 %collective-permute-start.4 = (bf16[528,512]{1,0:T(8,128)(2,1)S(1)}, bf16[528,512]{1,0:T(8,128)(2,1)}, u32[]{:S(2)}, u32[]{:S(2)}) collective-permute-start(bf16[528,512]{1,0:T(8,128)(2,1)S(1)} %copy-done.7), channel_id=1, source_target_pairs={{8,0},{10,2},{12,4},{14,6},{0,8},{2,10},{4,12},{6,14},{9,1},{11,3}... | collective-permute-start | bytes 1622024 | tf_op jit(solution)/shard_map/ppermute | solution.py:577
  123.7 16.6 %collective-permute-start.12 = (bf16[256,1024]{1,0:T(8,128)(2,1)S(1)}, bf16[256,1024]{1,0:T(8,128)(2,1)}, u32[]{:S(2)}, u32[]{:S(2)}) collective-permute-start(bf16[256,1024]{1,0:T(8,128)(2,1)S(1)} %get-tuple-element.141), channel_id=1, source_target_pairs={{0,4},{2,6},{4,8},{6,10},{8,12},{10,14},{1,5},{3,7},{5,9},{7,11},{... | collective-permute-start | bytes 1572872 | tf_op jit(solution)/shard_map/ppermute | solution.py:581
  125.8 15.8 %collective-permute-start.13 = (bf16[256,1024]{1,0:T(8,128)(2,1)S(1)}, bf16[256,1024]{1,0:T(8,128)(2,1)}, u32[]{:S(2)}, u32[]{:S(2)}) collective-permute-start(bf16[256,1024]{1,0:T(8,128)(2,1)S(1)} %get-tuple-element.141), channel_id=1, source_target_pairs={{12,8},{14,10},{8,4},{10,6},{4,0},{6,2},{13,9},{15,11},{9,5},{11,7... | collective-permute-start | bytes 1572872 | tf_op jit(solution)/shard_map/ppermute | solution.py:581
  132.2 8.2 %collective-permute-start.11 = (bf16[256,512]{1,0:T(8,128)(2,1)S(1)}, bf16[256,512]{1,0:T(8,128)(2,1)S(1)}, u32[]{:S(2)}, u32[]{:S(2)}) collective-permute-start(bf16[256,512]{1,0:T(8,128)(2,1)S(1)} %get-tuple-element.89), channel_id=1, source_target_pairs={{0,2},{2,0},{4,6},{6,4},{8,10},{10,8},{12,14},{14,12},{1,3},{3,1},... | collective-permute-start | bytes 786440 | tf_op jit(solution)/shard_map/ppermute | solution.py:574
  147.3 18.1 %collective-permute-start.14 = (f32[256,2048]{1,0:T(8,128)}, f32[256,2048]{1,0:T(8,128)S(1)}, u32[]{:S(2)}, u32[]{:S(2)}) collective-permute-start(f32[256,2048]{1,0:T(8,128)} %project_rows.1.mine_ref), channel_id=1, source_target_pairs={{0,1},{1,0},{2,3},{3,2},{4,5},{5,4},{6,7},{7,6},{8,9},{9,8},{10,11... | collective-permute-start | bytes 6291464 | tf_op jit(solution)/shard_map/ppermute | solution.py:666
  147.3 2.0 collective-permute-start.15
  148.0 17.4 %collective-permute-start.16 = (bf16[256,1024]{1,0:T(8,128)(2,1)}, bf16[256,1024]{1,0:T(8,128)(2,1)}, u32[]{:S(2)}, u32[]{:S(2)}) collective-permute-start(bf16[256,1024]{1,0:T(8,128)(2,1)} %collective-permute-done.13), channel_id=1, source_target_pairs={{8,4},{10,6},{4,0},{6,2},{9,5},{11,7},{5,1},{7,3},{24,20},{26,22},... | collective-permute-start | bytes 1572872 | tf_op jit(solution)/shard_map/ppermute | solution.py:581
  166.9 13.7 %collective-permute-start.22 = (bf16[256,1024]{1,0:T(8,128)(2,1)S(1)}, bf16[256,1024]{1,0:T(8,128)(2,1)}, u32[]{:S(2)}, u32[]{:S(2)}) collective-permute-start(bf16[256,1024]{1,0:T(8,128)(2,1)S(1)} %broadcast_select_fusion.3.refs_14_.refs_8_.refs_6_), channel_id=1, source_target_pairs={{0,16},{16,0},{1,17},{17,1},{2,18},{18,2},{3,19},{19,3},{4,20},{20... | collective-permute-start | bytes 1572872 | tf_op jit(solution)/shard_map/ppermute | solution.py:571
  172.3 14.4 %collective-permute-start.17 = (bf16[256,1024]{1,0:T(8,128)(2,1)}, bf16[256,1024]{1,0:T(8,128)(2,1)S(1)}, u32[]{:S(2)}, u32[]{:S(2)}) collective-permute-start(bf16[256,1024]{1,0:T(8,128)(2,1)} %get-tuple-element.112.refs_0_), channel_id=1, source_target_pairs={{0,4},{2,6},{4,8},{6,10},{8,12},{10,14},{1,5},{3,7},{5,9},{7,11},{... | collective-permute-start | bytes 1572872 | tf_op jit(solution)/shard_map/ppermute | solution.py:581
  176.0 17.1 %collective-permute-start.18 = (bf16[256,1024]{1,0:T(8,128)(2,1)}, bf16[256,1024]{1,0:T(8,128)(2,1)}, u32[]{:S(2)}, u32[]{:S(2)}) collective-permute-start(bf16[256,1024]{1,0:T(8,128)(2,1)} %get-tuple-element.112.refs_0_), channel_id=1, source_target_pairs={{12,8},{14,10},{8,4},{10,6},{4,0},{6,2},{13,9},{15,11},{9,5},{11,7... | collective-permute-start | bytes 1572872 | tf_op jit(solution)/shard_map/ppermute | solution.py:581
  177.3 15.8 %collective-permute-start.19 = (bf16[256,1024]{1,0:T(8,128)(2,1)}, bf16[256,1024]{1,0:T(8,128)(2,1)S(1)}, u32[]{:S(2)}, u32[]{:S(2)}) collective-permute-start(bf16[256,1024]{1,0:T(8,128)(2,1)} %get-tuple-element.112.refs_0_), channel_id=1, source_target_pairs={{0,2},{2,0},{4,6},{6,4},{8,10},{10,8},{12,14},{14,12},{1,3},{3,1},... | collective-permute-start | bytes 1572872 | tf_op jit(solution)/shard_map/ppermute | solution.py:574
  177.9 15.2 %collective-permute-start.20 = (bf16[256,1024]{1,0:T(8,128)(2,1)}, bf16[256,1024]{1,0:T(8,128)(2,1)S(1)}, u32[]{:S(2)}, u32[]{:S(2)}) collective-permute-start(bf16[256,1024]{1,0:T(8,128)(2,1)} %copy-done.29), channel_id=1, source_target_pairs={{8,12},{10,14},{9,13},{11,15},{24,28},{26,30},{25,29},{27,31}} | collective-permute-start | bytes 1572872 | tf_op jit(solution)/shard_map/ppermute | solution.py:581
  180.7 21.4 %collective-permute-start.21 = (bf16[256,1024]{1,0:T(8,128)(2,1)}, bf16[256,1024]{1,0:T(8,128)(2,1)S(1)}, u32[]{:S(2)}, u32[]{:S(2)}) collective-permute-start(bf16[256,1024]{1,0:T(8,128)(2,1)} %collective-permute-done.16), channel_id=1, source_target_pairs={{4,0},{6,2},{5,1},{7,3},{20,16},{22,18},{21,17},{23,19}} | collective-permute-start | bytes 1572872 | tf_op jit(solution)/shard_map/ppermute | solution.py:581
  186.7 19.0 %collective-permute-start.28 = (bf16[512,512]{1,0:T(8,128)(2,1)S(1)}, bf16[512,512]{1,0:T(8,128)(2,1)S(1)}, u32[]{:S(2)}, u32[]{:S(2)}) collective-permute-start(bf16[512,512]{1,0:T(8,128)(2,1)S(1)} %get-tuple-element.139), channel_id=1, source_target_pairs={{0,2},{2,0},{4,6},{6,4},{8,10},{10,8},{12,14},{14,12},{1,3},{3,1},... | collective-permute-start | bytes 1572872 | tf_op jit(solution)/shard_map/ppermute | solution.py:574
  203.2 11.9 %collective-permute-start.25 = (bf16[256,1024]{1,0:T(8,128)(2,1)S(1)}, bf16[256,1024]{1,0:T(8,128)(2,1)}, u32[]{:S(2)}, u32[]{:S(2)}) collective-permute-start(bf16[256,1024]{1,0:T(8,128)(2,1)S(1)} %broadcast_select_fusion.2.refs_2_), channel_id=1, source_target_pairs={{0,2},{2,0},{4,6},{6,4},{8,10},{10,8},{12,14},{14,12},{1,3},{3,1},... | collective-permute-start | bytes 1572872 | tf_op jit(solution)/shard_map/ppermute | solution.py:574
  203.7 12.7 %collective-permute-start.27 = (bf16[256,1024]{1,0:T(8,128)(2,1)S(1)}, bf16[256,1024]{1,0:T(8,128)(2,1)S(1)}, u32[]{:S(2)}, u32[]{:S(2)}) collective-permute-start(bf16[256,1024]{1,0:T(8,128)(2,1)S(1)} %broadcast_select_fusion.2.refs_2_), channel_id=1, source_target_pairs={{0,1},{1,0},{2,3},{3,2},{4,5},{5,4},{6,7},{7,6},{8,9},{9,8},{10,11... | collective-permute-start | bytes 1572872 | tf_op jit(solution)/shard_map/ppermute | solution.py:683
  203.8 13.4 %collective-permute-start.23 = (bf16[256,1024]{1,0:T(8,128)(2,1)S(1)}, bf16[256,1024]{1,0:T(8,128)(2,1)S(1)}, u32[]{:S(2)}, u32[]{:S(2)}) collective-permute-start(bf16[256,1024]{1,0:T(8,128)(2,1)S(1)} %collective-permute-done.17), channel_id=1, source_target_pairs={{4,8},{6,10},{8,12},{10,14},{5,9},{7,11},{9,13},{11,15},{20,24},{2... | collective-permute-start | bytes 1572872 | tf_op jit(solution)/shard_map/ppermute | solution.py:581
  204.5 16.4 %collective-permute-start.24 = (bf16[256,1024]{1,0:T(8,128)(2,1)}, bf16[256,1024]{1,0:T(8,128)(2,1)S(1)}, u32[]{:S(2)}, u32[]{:S(2)}) collective-permute-start(bf16[256,1024]{1,0:T(8,128)(2,1)} %collective-permute-done.18), channel_id=1, source_target_pairs={{8,4},{10,6},{4,0},{6,2},{9,5},{11,7},{5,1},{7,3},{24,20},{26,22},... | collective-permute-start | bytes 1572872 | tf_op jit(solution)/shard_map/ppermute | solution.py:581
  205.8 15.1 %collective-permute-start.26 = (bf16[256,1024]{1,0:T(8,128)(2,1)}, bf16[256,1024]{1,0:T(8,128)(2,1)S(1)}, u32[]{:S(2)}, u32[]{:S(2)}) collective-permute-start(bf16[256,1024]{1,0:T(8,128)(2,1)} %copy-done.37), channel_id=1, source_target_pairs={{0,1},{1,0},{2,3},{3,2},{4,5},{5,4},{6,7},{7,6},{8,9},{9,8},{10,11... | collective-permute-start | bytes 1572872 | tf_op jit(solution)/shard_map/ppermute | solution.py:683
  206.4 33.7 %copy-start.15 = (bf16[256,1024]{1,0:T(8,128)(2,1)}, bf16[256,1024]{1,0:T(8,128)(2,1)S(1)}, u32[]{:S(2)}) copy-start(bf16[256,1024]{1,0:T(8,128)(2,1)S(1)} %broadcast_select_fusion.refs_16_.refs_10_.refs_8_) | copy-start | bytes 1572868
  207.7 32.4 %copy-start.16 = (bf16[256,1024]{1,0:T(8,128)(2,1)}, bf16[256,1024]{1,0:T(8,128)(2,1)S(1)}, u32[]{:S(2)}) copy-start(bf16[256,1024]{1,0:T(8,128)(2,1)S(1)} %broadcast_select_fusion.1.refs_12_.refs_6_.refs_4_) | copy-start | bytes 1572868
  215.1 14.9 %collective-permute-start.35 = (bf16[256,1024]{1,0:T(8,128)(2,1)S(1)}, bf16[256,1024]{1,0:T(8,128)(2,1)S(1)}, u32[]{:S(2)}, u32[]{:S(2)}) collective-permute-start(bf16[256,1024]{1,0:T(8,128)(2,1)S(1)} %broadcast_select_fusion.refs_16_.refs_10_.refs_8_), channel_id=1, source_target_pairs={{0,16},{16,0},{1,17},{17,1},{2,18},{18,2},{3,19},{19,3},{4,20},{20... | collective-permute-start | bytes 1572872 | tf_op jit(solution)/shard_map/ppermute | solution.py:571
  216.4 20.7 %collective-permute-start.34 = (bf16[256,1024]{1,0:T(8,128)(2,1)S(1)}, bf16[256,1024]{1,0:T(8,128)(2,1)S(1)}, u32[]{:S(2)}, u32[]{:S(2)}) collective-permute-start(bf16[256,1024]{1,0:T(8,128)(2,1)S(1)} %broadcast_select_fusion.1.refs_12_.refs_6_.refs_4_), channel_id=1, source_target_pairs={{0,16},{16,0},{1,17},{17,1},{2,18},{18,2},{3,19},{19,3},{4,20},{20... | collective-permute-start | bytes 1572872 | tf_op jit(solution)/shard_map/ppermute | solution.py:571
  222.6 17.5 %collective-permute-start.33 = (bf16[256,1024]{1,0:T(8,128)(2,1)}, bf16[256,1024]{1,0:T(8,128)(2,1)}, u32[]{:S(2)}, u32[]{:S(2)}) collective-permute-start(bf16[256,1024]{1,0:T(8,128)(2,1)} %fusion.1.refs_4_), channel_id=1, source_target_pairs={{0,1},{1,0},{2,3},{3,2},{4,5},{5,4},{6,7},{7,6},{8,9},{9,8},{10,11... | collective-permute-start | bytes 1572872 | tf_op jit(solution)/shard_map/ppermute | solution.py:683
  222.6 17.5 %collective-permute-start.32 = (bf16[256,1024]{1,0:T(8,128)(2,1)}, bf16[256,1024]{1,0:T(8,128)(2,1)}, u32[]{:S(2)}, u32[]{:S(2)}) collective-permute-start(bf16[256,1024]{1,0:T(8,128)(2,1)} %collective-permute-done.25.refs_3_), channel_id=1, source_target_pairs={{0,1},{1,0},{2,3},{3,2},{4,5},{5,4},{6,7},{7,6},{8,9},{9,8},{10,11... | collective-permute-start | bytes 1572872 | tf_op jit(solution)/shard_map/ppermute | solution.py:683
  223.1 29.1 %collective-permute-start.31 = (bf16[256,1024]{1,0:T(8,128)(2,1)}, bf16[256,1024]{1,0:T(8,128)(2,1)}, u32[]{:S(2)}, u32[]{:S(2)}) collective-permute-start(bf16[256,1024]{1,0:T(8,128)(2,1)} %fusion.1.refs_4_), channel_id=1, source_target_pairs={{0,2},{2,0},{4,6},{6,4},{8,10},{10,8},{12,14},{14,12},{1,3},{3,1},... | collective-permute-start | bytes 1572872 | tf_op jit(solution)/shard_map/ppermute | solution.py:574
  229.9 22.2 %collective-permute-start.29 = (bf16[256,1024]{1,0:T(8,128)(2,1)S(1)}, bf16[256,1024]{1,0:T(8,128)(2,1)S(1)}, u32[]{:S(2)}, u32[]{:S(2)}) collective-permute-start(bf16[256,1024]{1,0:T(8,128)(2,1)S(1)} %collective-permute-done.23), channel_id=1, source_target_pairs={{8,12},{10,14},{9,13},{11,15},{24,28},{26,30},{25,29},{27,31}} | collective-permute-start | bytes 1572872 | tf_op jit(solution)/shard_map/ppermute | solution.py:581
  238.0 14.2 %collective-permute-start.30 = (bf16[256,1024]{1,0:T(8,128)(2,1)S(1)}, bf16[256,1024]{1,0:T(8,128)(2,1)}, u32[]{:S(2)}, u32[]{:S(2)}) collective-permute-start(bf16[256,1024]{1,0:T(8,128)(2,1)S(1)} %collective-permute-done.24), channel_id=1, source_target_pairs={{4,0},{6,2},{5,1},{7,3},{20,16},{22,18},{21,17},{23,19}} | collective-permute-start | bytes 1572872 | tf_op jit(solution)/shard_map/ppermute | solution.py:581
  253.4 2.0 collective-permute-start.38
  253.5 2.9 collective-permute-start.37
  254.0 13.9 %collective-permute-start.36 = (bf16[256,1024]{1,0:T(8,128)(2,1)S(1)}, bf16[256,1024]{1,0:T(8,128)(2,1)S(1)}, u32[]{:S(2)}, u32[]{:S(2)}) collective-permute-start(bf16[256,1024]{1,0:T(8,128)(2,1)S(1)} %select_select_fusion.1.refs_1_), channel_id=1, source_target_pairs={{0,2},{2,0},{4,6},{6,4},{8,10},{10,8},{12,14},{14,12},{1,3},{3,1},... | collective-permute-start | bytes 1572872 | tf_op jit(solution)/shard_map/ppermute | solution.py:574
  267.9 1.9 collective-permute-start.39
  284.2 14.2 %collective-permute-start.40 = (bf16[512,512]{1,0:T(8,128)(2,1)}, bf16[512,512]{1,0:T(8,128)(2,1)S(1)}, u32[]{:S(2)}, u32[]{:S(2)}) collective-permute-start(bf16[512,512]{1,0:T(8,128)(2,1)} %decode_rows.3), channel_id=1, source_target_pairs={{0,2},{2,0},{4,6},{6,4},{8,10},{10,8},{12,14},{14,12},{1,3},{3,1},... | collective-permute-start | bytes 1572872 | tf_op jit(solution)/shard_map/ppermute | solution.py:738
  (35 other events, 239.2 us)

commit v7 on v6

--- a/solution.py
+++ b/solution.py
@@ -241,36 +241,40 @@
     out_ref[rows:, :] = terms.astype(jnp.bfloat16)
 
 
-def encode(ids, queries, keys, values, extra, near, bias, rows):
+def encode(which, queries, keys, values, extra, near, bias, rows):
     tokens = keys.shape[0]
     width = keys.shape[1] // 2
-    half = pl.BlockSpec((tokens, width), lambda i, ids: (0, ids[1]))
+    blocks = queries.shape[0] // rows
+    half = pl.BlockSpec((tokens, width), lambda i, ids: (0, ids[0]))
     grid_spec = pltpu.PrefetchScalarGridSpec(
         num_scalar_prefetch=1,
-        grid=(1,),
+        grid=(blocks,),
         in_specs=[
-            pl.BlockSpec((rows, width), lambda i, ids: (ids[0], ids[1])),
+            pl.BlockSpec((rows, width), lambda i, ids: (i, ids[0])),
             half,
             half,
             whole(extra.shape),
             whole(near.shape),
             pl.BlockSpec(memory_space=pltpu.SMEM),
         ],
-        out_specs=whole((rows + EXTRA, width)),
+        out_specs=pl.BlockSpec((rows + EXTRA, width), lambda i, ids: (i, 0)),
     )
     return pl.pallas_call(
         encode_kernel,
         grid_spec=grid_spec,
-        out_shape=jax.ShapeDtypeStruct((rows + EXTRA, width), jnp.bfloat16),
+        out_shape=jax.ShapeDtypeStruct((blocks * (rows + EXTRA), width), jnp.bfloat16),
         compiler_params=params(32),
-        cost_estimate=cost(16 * rows * tokens * width, 8 * tokens * width, rows * tokens * 8),
+        cost_estimate=cost(
+            16 * blocks * rows * tokens * width, 8 * tokens * width, blocks * rows * tokens * 8
+        ),
         name="encode_rows",
-    )(ids, queries, keys, values, extra, near, bias)
-
-
-def merge_kernel(count, ids_ref, *refs):
-    parts, (mine_ref, near_ref, all_ref) = refs[:count], refs[count:]
+    )(which.reshape(1), queries, keys, values, extra, near, bias)
+
+
+def merge_kernel(count, ids_ref, parts_ref, mine_ref, near_ref, all_ref):
     rows, width = all_ref.shape
+    long = rows + EXTRA
+    parts = [parts_ref.at[i * long : (i + 1) * long, :] for i in range(count)]
     heads = width // HEAD_DIM
     stats = [v[rows:, :].astype(jnp.float32).T for v in parts]
     for h in range(heads):
@@ -292,24 +296,24 @@
     near_ref[...] = all_ref[pl.ds(pl.multiple_of((1 - ids_ref[0]) * own, own), own), :]
 
 
-def merge(which, parts):
-    long, width = parts[0].shape
+def merge(which, parts, count):
+    long, width = parts.shape[0] // count, parts.shape[1]
     rows = long - EXTRA
     grid_spec = pltpu.PrefetchScalarGridSpec(
         num_scalar_prefetch=1,
         grid=(1,),
-        in_specs=[whole(v.shape) for v in parts],
+        in_specs=[whole(parts.shape)],
         out_specs=[whole((rows // 2, width))] * 2,
         scratch_shapes=[pltpu.VMEM((rows, width), jnp.bfloat16)],
     )
     return pl.pallas_call(
-        functools.partial(merge_kernel, len(parts)),
+        functools.partial(merge_kernel, count),
         grid_spec=grid_spec,
         out_shape=[jax.ShapeDtypeStruct((rows // 2, width), jnp.bfloat16)] * 2,
         compiler_params=params(32),
         cost_estimate=cost(8 * rows * width, 10 * rows * width),
         name="merge_rows",
-    )(which.reshape(1), *parts)
+    )(which.reshape(1), parts)
 
 
 def project_kernel(far, ids_ref, mine_ref, near_ref, *refs):
@@ -616,25 +620,23 @@
         (near_inputs, out_far, out_sent, kv_for_near)
     )
     out_far = jnp.concatenate(out_far)
-    out_near = over_near(jnp.concatenate([out_sent, out_far]))
     out_far_other = over_groups(out_far)
 
     kv_own = columns((w_key, w_value), y)
     kv_near = over_near(kv_for_near)
 
-    ids = [jnp.stack([(z - k) % far, y]).astype(jnp.int32) for k in range(far)]
     head_bias = lax.dynamic_slice_in_dim(enc_bias, y * (heads // 2), heads // 2, 1)
-    order = sorted(range(1, far), key=lambda k: -min(k, far - k)) + [0]
-    results = {}
-    for k in order:
-        result = encode(
-            ids[k], latent_queries, enc_keys, enc_values, extra, near_inputs, head_bias, 2 * rows
-        )
-        results[k], near_inputs = lax.optimization_barrier((result, near_inputs))
-    parts = [over_far(results[k], k) for k in order[:-1]]
-    result, out_far_other = lax.optimization_barrier((results[0], out_far_other))
-    parts.append(result)
+    parts = encode(
+        y, latent_queries, enc_keys, enc_values, extra, near_inputs, head_bias, 2 * rows
+    )
+    kv_near, out_sent, _ = lax.optimization_barrier((kv_near, out_sent, parts))
+    kv_sent = jnp.where(x == 0, kv_own, kv_near)
+    hops = {0: [kv_sent, kv_sent]}
+    hops[1] = hop(1, hops[0])
+    out_near = over_near(jnp.concatenate([out_sent, out_far]))
     out_near_other = over_near(jnp.concatenate([half_of_out(1 - x), out_far_other]))
+    columns_of_slice = [[2 * i + j for i in range(far)] for j in range(2)]
+    parts = lax.all_to_all(parts, "pos", 0, 0, axis_index_groups=columns_of_slice, tiled=True)
 
     def kept_queries():
         far_counts = out_far.reshape(far - 1, out_half + EXTRA, out_cols)[:, out_half, : 2 * mods]
@@ -649,17 +651,16 @@
         limits = jnp.sum(q_onehot * query_counts[None, :], axis=1)
         return ranked < limits
 
-    parts, out_near, out_far_other, out_near_other, kv_near = lax.optimization_barrier(
-        (parts, out_near, out_far_other, out_near_other, kv_near)
-    )
-    kv_sent = jnp.where(x == 0, kv_own, kv_near)
-    hops = {0: [kv_sent, kv_sent]}
-    hops[1] = hop(1, hops[0])
-    attended, for_near = merge(y, parts)
+    parts, out_near, out_far_other, out_near_other, hops = lax.optimization_barrier(
+        (parts, out_near, out_far_other, out_near_other, hops)
+    )
+    hops[2] = hop(2, hops[1])
+    attended, for_near = merge(y, parts, far)
     from_near = over_near(for_near)
     kept = kept_queries()
     from_near, hops, kept = lax.optimization_barrier((from_near, hops, kept))
-    hops[2] = hop(2, hops[1])
+    for step in range(3, far):
+        hops[step] = hop(step, hops[step - 1])
     out_ids = jnp.stack([*places, y, x]).astype(jnp.int32)
     weights = [w_out, out_far, out_far_other, out_near, out_near_other]
     partial_value = project(out_ids, attended, from_near, weights)
@@ -701,20 +702,9 @@
 
     came = {0: [normed, normed]}
     came[1] = hop(1, came[0])
-    moved = {k: by_shift(hops, k) for k in range(1, far) if max(k, far - k) < 3}
+    moved = {k: by_shift(hops, k) for k in range(1, far)}
     swapped = {k: over_groups(v) for k, v in moved.items()}
-    for step in range(3, far):
-        hops[step] = hop(step, hops[step - 1])
-    came, normed_near, hops, swapped = lax.optimization_barrier(
-        (came, over_near(normed), hops, swapped)
-    )
-    for k in range(1, far):
-        if k not in moved:
-            moved[k] = by_shift(hops, k)
-            swapped[k] = over_groups(moved[k])
-    kv_bands = [kv_own, kv_near]
-    for k in range(1, far):
-        kv_bands += [moved[k], swapped[k]]
+    came, normed_near, moved = lax.optimization_barrier((came, over_near(normed), moved))
     mine, other = [normed, normed_near], [normed_other, *cores([normed_near])]
     keys_values = []
     for step in range(1, far):
@@ -727,9 +717,14 @@
         if step > 1:
             keys_values.append(fold(mine, other))
             mine, other = [], []
-        came, fresh_near, mine, other, keys_values, near_queries = lax.optimization_barrier(
-            (came, fresh_near, mine, other, keys_values, near_queries)
+        came, fresh_near, mine, other, keys_values, swapped, near_queries = (
+            lax.optimization_barrier(
+                (came, fresh_near, mine, other, keys_values, swapped, near_queries)
+            )
         )
+        kv_bands = [kv_own, kv_near]
+        for k in range(1, far):
+            kv_bands += [moved[k], swapped[k]]
         mine.append(fresh_near)
         other += cores([fresh_near])
     keys_values.append(fold(mine, other))

time: 301 us -> 274 us (0.910)
  waiting for transfers between devices: 148 us -> 126 us
  Pallas kernels: 70.8 us -> 66.1 us
    ppermute x10, waiting for transfers between devices: 49.4 us -> 25.8 us  [over_near(): return lax.ppermute(value, 'pos', near)]
    ppermute x6 -> x3, waiting for transfers between devices: 36.3 us -> 18.8 us  [over_far(): return lax.ppermute(value, 'pos', shift_perm(pos, k))]
    ppermute x12, waiting for transfers between devices: 39.2 us -> 49.6 us  [hop(): lax.ppermute(v, 'pos', hop_perm(pos, step, way))]
    ppermute x4, waiting for transfers between devices: 13.9 us -> 22.8 us  [over_groups(): return lax.ppermute(value, 'groups', swap_perm(groups))]
    ppermute x6 -> x3, starting transfers between devices: 11.3 us -> 4.67 us  [over_far(): return lax.ppermute(value, 'pos', shift_perm(pos, k))]
    all_to_all x0 -> x1, starting transfers between devices: none -> 4.06 us  [fast_on_device(): lax.all_to_all(parts, 'pos', 0, 0, axis_index_groups=columns_of_slice, ti...]
    pallas_call x4 -> x1, Pallas kernels: 16.7 us -> 12.8 us  [encode(): pl.pallas_call(encode_kernel, grid_spec=grid_spec, out_shape=jax.ShapeDty...]
    unnamed x88 -> x66, local copies, waits for them, and re-layouts: 8.63 us -> 9.25 us
  transfers between devices with their start and end apart: 41 -> 39, of which waited for: 20 -> 21; matrix products, arithmetic and copies ran while one was open for 6% -> 9% of each run, Pallas kernels for 17% -> 12%
where the time goes in v7:
time: 274 us; the launch traced here: 272 us
  waiting for transfers between devices  126 us (46%)
  Pallas kernels  66.1 us (24%)
  starting transfers between devices  42.8 us (16%)
  local copies, waits for them, and re-layouts  18.6 us (7%)
  other arithmetic  17.2 us (6%)
    ppermute x12, waiting for transfers between devices, hop(): lax.ppermute(v, 'pos', hop_perm(pos, step, way))  49.6 us
    ppermute x10, waiting for transfers between devices, over_near(): return lax.ppermute(value, 'pos', near)  25.8 us
    pallas_call x3, Pallas kernels, latent_keys_values(): pl.pallas_call(functools.partial(latents_kernel, pieces), grid_spec=grid_...  24.3 us
    ppermute x4, waiting for transfers between devices, over_groups(): return lax.ppermute(value, 'groups', swap_perm(groups))  22.8 us
    ppermute x3, waiting for transfers between devices, over_far(): return lax.ppermute(value, 'pos', shift_perm(pos, k))  18.8 us
    pallas_call x2, Pallas kernels, decode(): pl.pallas_call(functools.partial(decode_kernel, len(keys_values)), grid=(...  16.7 us
    ppermute x12, starting transfers between devices, hop(): lax.ppermute(v, 'pos', hop_perm(pos, step, way))  16.7 us
    pallas_call x1, Pallas kernels, encode(): pl.pallas_call(encode_kernel, grid_spec=grid_spec, out_shape=jax.ShapeDty...  12.8 us
  transfers between devices with their start and end apart: 39, of which 21 were waited for; matrix products, arithmetic and copies ran while one was open for 9% of the time, Pallas kernels for 12%

profile of v7, /device:TPU:0, one launch (start us, length us, event | category | flops | bytes accessed | tf_op | source)
XLA Modules:
  0.0 272.3 jit_solution(7436919519380837002)
XLA Ops:
  1.4 1.3 constant_dynamic-slice_fusion.9
  3.9 3.0 %collective-permute-start = (bf16[528,1024]{1,0:T(8,128)(2,1)}, bf16[528,1024]{1,0:T(8,128)(2,1)S(1)}, u32[]{:S(2)}, u32[]{:S(2)}) collective-permute-start(bf16[528,1024]{1,0:T(8,128)(2,1)} %pad_maximum_fusion), channel_id=1, source_target_pairs={{0,2},{2,0},{4,6},{6,4},{8,10},{10,8},{12,14},{14,12},{1,3},{3,1},... | collective-permute-start | bytes 3244040 | tf_op jit(solution)/shard_map/ppermute | solution.py:578
  7.8 3.7 %collective-permute-start.1 = (bf16[528,256]{1,0:T(8,128)(2,1)S(1)}, bf16[528,256]{1,0:T(8,128)(2,1)}, u32[]{:S(2)}, u32[]{:S(2)}) collective-permute-start(bf16[528,256]{1,0:T(8,128)(2,1)S(1)} %pad_maximum_fusion.5), channel_id=1, source_target_pairs={{4,0},{6,2},{8,4},{10,6},{12,8},{14,10},{0,12},{2,14},{5,1},{7,3},... | collective-permute-start | bytes 811016 | tf_op jit(solution)/shard_map/ppermute | solution.py:581
  12.6 2.0 constant_dynamic-slice_fusion.2
  15.5 3.0 %collective-permute-done.1 = bf16[528,256]{1,0:T(8,128)(2,1)} collective-permute-done((bf16[528,256]{1,0:T(8,128)(2,1)S(1)}, bf16[528,256]{1,0:T(8,128)(2,1)}, u32[]{:S(2)}, u32[]{:S(2)}) %collective-permute-start.1) | collective-permute-done | bytes 270368 | tf_op jit(solution)/shard_map/ppermute | solution.py:581
  18.5 15.9 %collective-permute-done.2 = bf16[528,256]{1,0:T(8,128)(2,1)} collective-permute-done((bf16[528,256]{1,0:T(8,128)(2,1)S(1)}, bf16[528,256]{1,0:T(8,128)(2,1)}, u32[]{:S(2)}, u32[]{:S(2)}) %collective-permute-start.2) | collective-permute-done | bytes 270368 | tf_op jit(solution)/shard_map/ppermute | solution.py:581
  34.4 2.2 copy-done.5
  36.6 12.8 %encode_rows.1 = bf16[2112,512]{1,0:T(8,128)(2,1)S(1)} custom-call(s32[1]{0:T(128)} %bitcast.9.ids_ref, bf16[2048,1024]{1,0:T(8,128)(2,1)S(1)} %copy-done.5, bf16[512,1024]{1,0:T(8,128)(2,1)S(1)} %copy-done.2, bf16[512,1024]{1,0:T(8,128)(2,1)S(1)} %copy-done.3, bf16[16,1024]{1,0:T(8,128)(2,1)S(1)} %pad.10.extra_ref, ...), custom_call_target="tpu_custom_call" | custom-call | flops 8589934592 | bytes 2097152 | tf_op jit(solution)/shard_map/encode_rows/pallas_call | solution.py:262
  50.7 4.1 %all-to-all-start = ((bf16[4,528,512]{2,1,0:T(8,128)(2,1)}), bf16[4,528,512]{2,1,0:T(8,128)(2,1)S(1)}, u32[]{:S(2)}, u32[]{:S(2)}) async-start(bf16[4,528,512]{2,1,0:T(8,128)(2,1)} %bitcast.46), calls=%async_computation | async-start | bytes 4325376 | tf_op jit(solution)/shard_map/all_to_all | solution.py:639
  58.2 1.6 collective-permute-start.6
  59.8 8.0 %collective-permute-done.4.refs_11_.refs_5_.refs_3_ = bf16[256,1024]{1,0:T(8,128)(2,1)S(1)} collective-permute-done((bf16[256,1024]{1,0:T(8,128)(2,1)}, bf16[256,1024]{1,0:T(8,128)(2,1)S(1)}, u32[]{:S(2)}, u32[]{:S(2)}) %collective-permute-start.4) | collective-permute-done | bytes 524320 | tf_op jit(solution)/shard_map/ppermute | solution.py:578
  67.8 2.4 pad_maximum_fusion.1
  70.7 6.2 %collective-permute-done.6.refs_2_ = bf16[1584,256]{1,0:T(8,128)(2,1)S(1)} collective-permute-done((bf16[1584,256]{1,0:T(8,128)(2,1)S(1)}, bf16[1584,256]{1,0:T(8,128)(2,1)S(1)}, u32[]{:S(2)}, u32[]{:S(2)}) %collective-permute-start.6) | collective-permute-done | bytes 811040 | tf_op jit(solution)/shard_map/ppermute | solution.py:575
  78.2 1.5 collective-permute-start.7
  79.7 2.3 pad_maximum_fusion.4
  82.0 3.7 %collective-permute-start.8 = (bf16[256,1024]{1,0:T(8,128)(2,1)}, bf16[256,1024]{1,0:T(8,128)(2,1)S(1)}, u32[]{:S(2)}, u32[]{:S(2)}) collective-permute-start(bf16[256,1024]{1,0:T(8,128)(2,1)} %get-tuple-element.145), channel_id=1, source_target_pairs={{0,4},{2,6},{4,8},{6,10},{8,12},{10,14},{1,5},{3,7},{5,9},{7,11},{... | collective-permute-start | bytes 1572872 | tf_op jit(solution)/shard_map/ppermute | solution.py:585
  89.1 11.3 %collective-permute-done.8 = bf16[256,1024]{1,0:T(8,128)(2,1)S(1)} collective-permute-done((bf16[256,1024]{1,0:T(8,128)(2,1)}, bf16[256,1024]{1,0:T(8,128)(2,1)S(1)}, u32[]{:S(2)}, u32[]{:S(2)}) %collective-permute-start.8) | collective-permute-done | bytes 524320 | tf_op jit(solution)/shard_map/ppermute | solution.py:585
  100.5 8.7 %collective-permute-done.9 = bf16[256,1024]{1,0:T(8,128)(2,1)S(1)} collective-permute-done((bf16[256,1024]{1,0:T(8,128)(2,1)}, bf16[256,1024]{1,0:T(8,128)(2,1)S(1)}, u32[]{:S(2)}, u32[]{:S(2)}) %collective-permute-start.9) | collective-permute-done | bytes 524320 | tf_op jit(solution)/shard_map/ppermute | solution.py:585
  109.2 8.3 %collective-permute-done.7.refs_4_ = bf16[2112,256]{1,0:T(8,128)(2,1)} collective-permute-done((bf16[2112,256]{1,0:T(8,128)(2,1)}, bf16[2112,256]{1,0:T(8,128)(2,1)}, u32[]{:S(2)}, u32[]{:S(2)}) %collective-permute-start.7) | collective-permute-done | bytes 1081376 | tf_op jit(solution)/shard_map/ppermute | solution.py:578
  117.5 1.5 collective-permute-start.11
  121.7 1.9 merge_rows.1
  125.0 5.7 %collective-permute-done.10.near_ref = bf16[256,512]{1,0:T(8,128)(2,1)S(1)} collective-permute-done((bf16[256,512]{1,0:T(8,128)(2,1)S(1)}, bf16[256,512]{1,0:T(8,128)(2,1)S(1)}, u32[]{:S(2)}, u32[]{:S(2)}) %collective-permute-start.10) | collective-permute-done | bytes 262176 | tf_op jit(solution)/shard_map/ppermute | solution.py:578
  130.7 3.2 %collective-permute-done.12 = bf16[256,1024]{1,0:T(8,128)(2,1)} collective-permute-done((bf16[256,1024]{1,0:T(8,128)(2,1)S(1)}, bf16[256,1024]{1,0:T(8,128)(2,1)}, u32[]{:S(2)}, u32[]{:S(2)}) %collective-permute-start.12) | collective-permute-done | bytes 524320 | tf_op jit(solution)/shard_map/ppermute | solution.py:585
  133.9 5.8 %project_rows.1.mine_ref = f32[256,2048]{1,0:T(8,128)} custom-call(s32[10]{0:T(128)} %stack.82.ids_ref, bf16[256,512]{1,0:T(8,128)(2,1)} %copy-done.4, bf16[256,512]{1,0:T(8,128)(2,1)} %copy-done.25, bf16[1024,256]{1,0:T(8,128)(2,1)} %refs_0_.1, bf16[1584,256]{1,0:T(8,128)(2,1)} %copy-done.13, bf16[1584,256]{1,0:T(8,128)(2,1)} %copy-done.6, ...), custom_call_target="tpu_custom_call" | custom-call | flops 1073741824 | bytes 6291456 | tf_op jit(solution)/shard_map/project_rows/pallas_call | solution.py:357
  143.9 13.1 %collective-permute-done.15 = bf16[256,1024]{1,0:T(8,128)(2,1)} collective-permute-done((bf16[256,1024]{1,0:T(8,128)(2,1)}, bf16[256,1024]{1,0:T(8,128)(2,1)}, u32[]{:S(2)}, u32[]{:S(2)}) %collective-permute-start.15) | collective-permute-done | bytes 524320 | tf_op jit(solution)/shard_map/ppermute | solution.py:585
  157.0 1.4 copy-done.11
  158.4 4.5 %norm_rows.1 = (f32[256,1024]{1,0:T(8,128)}, bf16[256,1024]{1,0:T(8,128)(2,1)}, bf16[256,1024]{1,0:T(8,128)(2,1)}) custom-call(s32[1]{0:T(128)} %bitcast.ids_ref, f32[256,2048]{1,0:T(8,128)} %project_rows.1.mine_ref, f32[256,2048]{1,0:T(8,128)} %copy-done.11, bf16[256,2048]{1,0:T(8,128)(2,1)} %latent_ref.1, f32[1,2048]{1,0:T(1,128)} %bitcast.49), custom_call_target="tpu_custom_call" | custom-call | flops 3145728 | bytes 6815744 | tf_op jit(solution)/shard_map/norm_rows/pallas_call | solution.py:391
  162.9 1.6 collective-permute-start.16
  167.5 1.6 collective-permute-start.26
  170.3 5.6 %collective-permute-done.16 = bf16[256,1024]{1,0:T(8,128)(2,1)S(1)} collective-permute-done((bf16[256,1024]{1,0:T(8,128)(2,1)}, bf16[256,1024]{1,0:T(8,128)(2,1)S(1)}, u32[]{:S(2)}, u32[]{:S(2)}) %collective-permute-start.16) | collective-permute-done | bytes 524320 | tf_op jit(solution)/shard_map/ppermute | solution.py:585
  176.0 1.5 collective-permute-start.25
  177.5 3.1 %collective-permute-done.17 = bf16[256,1024]{1,0:T(8,128)(2,1)} collective-permute-done((bf16[256,1024]{1,0:T(8,128)(2,1)}, bf16[256,1024]{1,0:T(8,128)(2,1)}, u32[]{:S(2)}, u32[]{:S(2)}) %collective-permute-start.17) | collective-permute-done | bytes 524320 | tf_op jit(solution)/shard_map/ppermute | solution.py:585
  180.6 1.5 collective-permute-start.24
  182.1 1.9 broadcast_select_fusion.refs_2_
  185.3 8.5 %collective-permute-done.25.refs_15_.refs_9_.refs_7_ = bf16[256,1024]{1,0:T(8,128)(2,1)} collective-permute-done((bf16[256,1024]{1,0:T(8,128)(2,1)S(1)}, bf16[256,1024]{1,0:T(8,128)(2,1)}, u32[]{:S(2)}, u32[]{:S(2)}) %collective-permute-start.25) | collective-permute-done | bytes 524320 | tf_op jit(solution)/shard_map/ppermute | solution.py:575
  193.8 1.5 collective-permute-start.20
  195.3 8.0 %collective-permute-done.24.refs_13_.refs_7_.refs_5_ = bf16[256,1024]{1,0:T(8,128)(2,1)} collective-permute-done((bf16[256,1024]{1,0:T(8,128)(2,1)S(1)}, bf16[256,1024]{1,0:T(8,128)(2,1)}, u32[]{:S(2)}, u32[]{:S(2)}) %collective-permute-start.24) | collective-permute-done | bytes 524320 | tf_op jit(solution)/shard_map/ppermute | solution.py:575
  203.3 3.2 %collective-permute-done.20 = bf16[256,1024]{1,0:T(8,128)(2,1)S(1)} collective-permute-done((bf16[256,1024]{1,0:T(8,128)(2,1)}, bf16[256,1024]{1,0:T(8,128)(2,1)S(1)}, u32[]{:S(2)}, u32[]{:S(2)}) %collective-permute-start.20) | collective-permute-done | bytes 524320 | tf_op jit(solution)/shard_map/ppermute | solution.py:585
  207.9 1.5 collective-permute-start.30
  212.1 12.1 %latent_keys_values.3.refs_0_.refs_3_ = bf16[1280,1024]{1,0:T(8,128)(2,1)} custom-call(s32[9]{0:T(128)} %stack.92.ids_ref, bf16[256,1024]{1,0:T(8,128)(2,1)} %get-tuple-element.109.refs_0_, bf16[256,1024]{1,0:T(8,128)(2,1)} %collective-permute-done.18.refs_1_, bf16[256,1024]{1,0:T(8,128)(2,1)} %broadcast_select_fusion.refs_2_, ...), custom_call_target="tpu_custom_call" | custom-call | flops 5368709120 | bytes 4194304 | tf_op jit(solution)/shard_map/latent_keys_values/pallas_call | solution.py:452
  229.4 6.9 %latent_keys_values.4.refs_1_.refs_4_ = bf16[512,1024]{1,0:T(8,128)(2,1)} custom-call(s32[9]{0:T(128)} %stack.92.ids_ref, bf16[256,1024]{1,0:T(8,128)(2,1)} %collective-permute-done.30.refs_0_, bf16[256,1024]{1,0:T(8,128)(2,1)} %copy-done.24, bf16[256,1024]{1,0:T(8,128)(2,1)} %copy-done.30, bf16[256,1024]{1,0:T(8,128)(2,1)} %copy-done.29, ...), custom_call_target="tpu_custom_call" | custom-call | flops 2147483648 | bytes 4194304 | tf_op jit(solution)/shard_map/latent_keys_values/pallas_call | solution.py:452
  236.3 3.9 %collective-permute-done.33.refs_0_ = bf16[256,1024]{1,0:T(8,128)(2,1)S(1)} collective-permute-done((bf16[256,1024]{1,0:T(8,128)(2,1)S(1)}, bf16[256,1024]{1,0:T(8,128)(2,1)S(1)}, u32[]{:S(2)}, u32[]{:S(2)}) %collective-permute-start.33) | collective-permute-done | bytes 524320 | tf_op jit(solution)/shard_map/ppermute | solution.py:578
  240.1 1.9 collective-permute-done.36.refs_1_
  242.8 5.3 %latent_keys_values.5.refs_2_.refs_5_ = bf16[256,1024]{1,0:T(8,128)(2,1)} custom-call(s32[9]{0:T(128)} %stack.92.ids_ref, bf16[256,1024]{1,0:T(8,128)(2,1)} %copy-done.19, bf16[256,1024]{1,0:T(8,128)(2,1)} %copy-done.20, bf16[256,1024]{1,0:T(8,128)(2,1)} %get-tuple-element.144.refs_10_.refs_4_.refs_2_, bf16[256,1024]{1,0:T(8,128)(2,1)} %copy-done.7, ...), custom_call_target="tpu_custom_call" | custom-call | flops 1073741824 | bytes 4194304 | tf_op jit(solution)/shard_map/latent_keys_values/pallas_call | solution.py:452
  248.2 8.3 %decode_rows.3 = bf16[512,512]{1,0:T(8,128)(2,1)} custom-call(bf16[512,512]{1,0:T(8,128)(2,1)} %collective-permute-done.27.q_ref, bf16[1280,1024]{1,0:T(8,128)(2,1)} %latent_keys_values.3.refs_0_.refs_3_, bf16[512,1024]{1,0:T(8,128)(2,1)} %latent_keys_values.4.refs_1_.refs_4_, bf16[256,1024]{1,0:T(8,128)(2,1)} %latent_keys_values.5.refs_2_.refs_5_, ...), custom_call_target="tpu_custom_call" | custom-call | flops 8589934592 | bytes 5767168 | tf_op jit(solution)/shard_map/decode_rows/pallas_call | solution.py:513
  257.0 8.4 %decode_rows.2 = f32[512,512]{1,0:T(8,128)} custom-call(bf16[512,512]{1,0:T(8,128)(2,1)} %get-tuple-element.142.q_ref, bf16[1280,1024]{1,0:T(8,128)(2,1)} %latent_keys_values.3.refs_0_.refs_3_, bf16[512,1024]{1,0:T(8,128)(2,1)} %latent_keys_values.4.refs_1_.refs_4_, bf16[256,1024]{1,0:T(8,128)(2,1)} %latent_keys_values.5.refs_2_.refs_5_, ...), custom_call_target="tpu_custom_call" | custom-call | flops 8589934592 | bytes 5767168 | tf_op jit(solution)/shard_map/decode_rows/pallas_call | solution.py:513
  265.4 5.2 %collective-permute-done.37 = bf16[512,512]{1,0:T(8,128)(2,1)S(1)} collective-permute-done((bf16[512,512]{1,0:T(8,128)(2,1)}, bf16[512,512]{1,0:T(8,128)(2,1)S(1)}, u32[]{:S(2)}, u32[]{:S(2)}) %collective-permute-start.37) | collective-permute-done | bytes 524320 | tf_op jit(solution)/shard_map/ppermute | solution.py:733
  270.8 1.6 fusion
  (148 shorter events, 39.1 us)
Async XLA Ops:
  0.6 141.1 %copy-start = (bf16[3,1024]{1,0:T(4,128)(2,1)S(1)}, bf16[3,1024]{1,0:T(4,128)(2,1)}, u32[]{:S(2)}) copy-start(bf16[3,1024]{1,0:T(4,128)(2,1)} %param.25) | copy-start | bytes 18436
  3.9 30.5 %collective-permute-start = (bf16[528,1024]{1,0:T(8,128)(2,1)}, bf16[528,1024]{1,0:T(8,128)(2,1)S(1)}, u32[]{:S(2)}, u32[]{:S(2)}) collective-permute-start(bf16[528,1024]{1,0:T(8,128)(2,1)} %pad_maximum_fusion), channel_id=1, source_target_pairs={{0,2},{2,0},{4,6},{6,4},{8,10},{10,8},{12,14},{14,12},{1,3},{3,1},... | collective-permute-start | bytes 3244040 | tf_op jit(solution)/shard_map/ppermute | solution.py:578
  7.8 26.5 %copy-start.2 = (bf16[512,1024]{1,0:T(8,128)(2,1)S(1)}, bf16[512,1024]{1,0:T(8,128)(2,1)}, u32[]{:S(2)}) copy-start(bf16[512,1024]{1,0:T(8,128)(2,1)} %k_ref.1) | copy-start | bytes 3145732
  7.8 26.5 %copy-start.3 = (bf16[512,1024]{1,0:T(8,128)(2,1)S(1)}, bf16[512,1024]{1,0:T(8,128)(2,1)}, u32[]{:S(2)}) copy-start(bf16[512,1024]{1,0:T(8,128)(2,1)} %v_ref.1) | copy-start | bytes 3145732
  7.8 41.6 %copy-start.14 = (bf16[528,256]{1,0:T(8,128)(2,1)}, bf16[528,256]{1,0:T(8,128)(2,1)S(1)}, u32[]{:S(2)}) copy-start(bf16[528,256]{1,0:T(8,128)(2,1)S(1)} %pad_maximum_fusion.5) | copy-start | bytes 811012
  7.8 10.6 %collective-permute-start.1 = (bf16[528,256]{1,0:T(8,128)(2,1)S(1)}, bf16[528,256]{1,0:T(8,128)(2,1)}, u32[]{:S(2)}, u32[]{:S(2)}) collective-permute-start(bf16[528,256]{1,0:T(8,128)(2,1)S(1)} %pad_maximum_fusion.5), channel_id=1, source_target_pairs={{4,0},{6,2},{8,4},{10,6},{12,8},{14,10},{0,12},{2,14},{5,1},{7,3},... | collective-permute-start | bytes 811016 | tf_op jit(solution)/shard_map/ppermute | solution.py:581
  11.5 22.8 %collective-permute-start.2 = (bf16[528,256]{1,0:T(8,128)(2,1)S(1)}, bf16[528,256]{1,0:T(8,128)(2,1)}, u32[]{:S(2)}, u32[]{:S(2)}) collective-permute-start(bf16[528,256]{1,0:T(8,128)(2,1)S(1)} %pad_maximum_fusion.5), channel_id=1, source_target_pairs={{8,0},{10,2},{12,4},{14,6},{0,8},{2,10},{4,12},{6,14},{9,1},{11,3}... | collective-permute-start | bytes 811016 | tf_op jit(solution)/shard_map/ppermute | solution.py:581
  11.5 22.8 %collective-permute-start.3 = (bf16[528,256]{1,0:T(8,128)(2,1)S(1)}, bf16[528,256]{1,0:T(8,128)(2,1)}, u32[]{:S(2)}, u32[]{:S(2)}) collective-permute-start(bf16[528,256]{1,0:T(8,128)(2,1)S(1)} %pad_maximum_fusion.5), channel_id=1, source_target_pairs={{12,0},{14,2},{0,4},{2,6},{4,8},{6,10},{8,12},{10,14},{13,1},{15,3... | collective-permute-start | bytes 811016 | tf_op jit(solution)/shard_map/ppermute | solution.py:581
  50.7 66.8 %all-to-all-start = ((bf16[4,528,512]{2,1,0:T(8,128)(2,1)}), bf16[4,528,512]{2,1,0:T(8,128)(2,1)S(1)}, u32[]{:S(2)}, u32[]{:S(2)}) async-start(bf16[4,528,512]{2,1,0:T(8,128)(2,1)} %bitcast.46), calls=%async_computation | async-start | bytes 4325376 | tf_op jit(solution)/shard_map/all_to_all | solution.py:639
  54.8 13.0 %collective-permute-start.4 = (bf16[256,1024]{1,0:T(8,128)(2,1)}, bf16[256,1024]{1,0:T(8,128)(2,1)S(1)}, u32[]{:S(2)}, u32[]{:S(2)}) collective-permute-start(bf16[256,1024]{1,0:T(8,128)(2,1)} %pad_maximum_fusion.3), channel_id=1, source_target_pairs={{0,2},{2,0},{4,6},{6,4},{8,10},{10,8},{12,14},{14,12},{1,3},{3,1},... | collective-permute-start | bytes 1572872 | tf_op jit(solution)/shard_map/ppermute | solution.py:578
  58.2 18.7 %collective-permute-start.6 = (bf16[1584,256]{1,0:T(8,128)(2,1)S(1)}, bf16[1584,256]{1,0:T(8,128)(2,1)S(1)}, u32[]{:S(2)}, u32[]{:S(2)}) collective-permute-start(bf16[1584,256]{1,0:T(8,128)(2,1)S(1)} %constant_dynamic-update-slice_fusion.refs_1_), channel_id=1, source_target_pairs={{0,16},{16,0},{1,17},{17,1},{2,18},{18,2},{3,19},{19,3},{4,20},{20... | collective-permute-start | bytes 2433032 | tf_op jit(solution)/shard_map/ppermute | solution.py:575
  70.2 38.9 %collective-permute-start.5 = (bf16[2112,256]{1,0:T(8,128)(2,1)}, bf16[2112,256]{1,0:T(8,128)(2,1)}, u32[]{:S(2)}, u32[]{:S(2)}) collective-permute-start(bf16[2112,256]{1,0:T(8,128)(2,1)} %pad_maximum_fusion.1), channel_id=1, source_target_pairs={{0,2},{2,0},{4,6},{6,4},{8,10},{10,8},{12,14},{14,12},{1,3},{3,1},... | collective-permute-start | bytes 3244040 | tf_op jit(solution)/shard_map/ppermute | solution.py:578
  78.2 39.3 %collective-permute-start.7 = (bf16[2112,256]{1,0:T(8,128)(2,1)}, bf16[2112,256]{1,0:T(8,128)(2,1)}, u32[]{:S(2)}, u32[]{:S(2)}) collective-permute-start(bf16[2112,256]{1,0:T(8,128)(2,1)} %pad_maximum_fusion.2), channel_id=1, source_target_pairs={{0,2},{2,0},{4,6},{6,4},{8,10},{10,8},{12,14},{14,12},{1,3},{3,1},... | collective-permute-start | bytes 3244040 | tf_op jit(solution)/shard_map/ppermute | solution.py:578
  79.7 45.2 %copy-start.28 = (s32[3]{0:T(128)S(1)}, s32[3]{0:T(128)}, u32[]{:S(2)}) copy-start(s32[3]{0:T(128)} %param.27) | copy-start | bytes 40
  82.0 18.5 %collective-permute-start.8 = (bf16[256,1024]{1,0:T(8,128)(2,1)}, bf16[256,1024]{1,0:T(8,128)(2,1)S(1)}, u32[]{:S(2)}, u32[]{:S(2)}) collective-permute-start(bf16[256,1024]{1,0:T(8,128)(2,1)} %get-tuple-element.145), channel_id=1, source_target_pairs={{0,4},{2,6},{4,8},{6,10},{8,12},{10,14},{1,5},{3,7},{5,9},{7,11},{... | collective-permute-start | bytes 1572872 | tf_op jit(solution)/shard_map/ppermute | solution.py:585
  85.7 23.5 %collective-permute-start.9 = (bf16[256,1024]{1,0:T(8,128)(2,1)}, bf16[256,1024]{1,0:T(8,128)(2,1)S(1)}, u32[]{:S(2)}, u32[]{:S(2)}) collective-permute-start(bf16[256,1024]{1,0:T(8,128)(2,1)} %get-tuple-element.145), channel_id=1, source_target_pairs={{12,8},{14,10},{8,4},{10,6},{4,0},{6,2},{13,9},{15,11},{9,5},{11,7... | collective-permute-start | bytes 1572872 | tf_op jit(solution)/shard_map/ppermute | solution.py:585
  109.1 30.6 %copy-start.21 = (bf16[256,1024]{1,0:T(8,128)(2,1)}, bf16[256,1024]{1,0:T(8,128)(2,1)S(1)}, u32[]{:S(2)}) copy-start(bf16[256,1024]{1,0:T(8,128)(2,1)S(1)} %collective-permute-done.9) | copy-start | bytes 1572868
  117.5 13.2 %collective-permute-start.11 = (bf16[256,1024]{1,0:T(8,128)(2,1)S(1)}, bf16[256,1024]{1,0:T(8,128)(2,1)}, u32[]{:S(2)}, u32[]{:S(2)}) collective-permute-start(bf16[256,1024]{1,0:T(8,128)(2,1)S(1)} %collective-permute-done.8), channel_id=1, source_target_pairs={{4,8},{6,10},{8,12},{10,14},{5,9},{7,11},{9,13},{11,15},{20,24},{2... | collective-permute-start | bytes 1572872 | tf_op jit(solution)/shard_map/ppermute | solution.py:585
  119.0 14.9 %collective-permute-start.12 = (bf16[256,1024]{1,0:T(8,128)(2,1)S(1)}, bf16[256,1024]{1,0:T(8,128)(2,1)}, u32[]{:S(2)}, u32[]{:S(2)}) collective-permute-start(bf16[256,1024]{1,0:T(8,128)(2,1)S(1)} %collective-permute-done.9), channel_id=1, source_target_pairs={{8,4},{10,6},{4,0},{6,2},{9,5},{11,7},{5,1},{7,3},{24,20},{26,22},... | collective-permute-start | bytes 1572872 | tf_op jit(solution)/shard_map/ppermute | solution.py:585
  124.3 6.4 %collective-permute-start.10 = (bf16[256,512]{1,0:T(8,128)(2,1)S(1)}, bf16[256,512]{1,0:T(8,128)(2,1)S(1)}, u32[]{:S(2)}, u32[]{:S(2)}) collective-permute-start(bf16[256,512]{1,0:T(8,128)(2,1)S(1)} %get-tuple-element.81), channel_id=1, source_target_pairs={{0,2},{2,0},{4,6},{6,4},{8,10},{10,8},{12,14},{14,12},{1,3},{3,1},... | collective-permute-start | bytes 786440 | tf_op jit(solution)/shard_map/ppermute | solution.py:578
  139.7 17.2 %collective-permute-start.13 = (f32[256,2048]{1,0:T(8,128)}, f32[256,2048]{1,0:T(8,128)S(1)}, u32[]{:S(2)}, u32[]{:S(2)}) collective-permute-start(f32[256,2048]{1,0:T(8,128)} %project_rows.1.mine_ref), channel_id=1, source_target_pairs={{0,1},{1,0},{2,3},{3,2},{4,5},{5,4},{6,7},{7,6},{8,9},{9,8},{10,11... | collective-permute-start | bytes 6291464 | tf_op jit(solution)/shard_map/ppermute | solution.py:667
  139.7 4.1 %collective-permute-start.14 = (bf16[256,1024]{1,0:T(8,128)(2,1)}, bf16[256,1024]{1,0:T(8,128)(2,1)S(1)}, u32[]{:S(2)}, u32[]{:S(2)}) collective-permute-start(bf16[256,1024]{1,0:T(8,128)(2,1)} %collective-permute-done.11), channel_id=1, source_target_pairs={{8,12},{10,14},{9,13},{11,15},{24,28},{26,30},{25,29},{27,31}} | collective-permute-start | bytes 1572872 | tf_op jit(solution)/shard_map/ppermute | solution.py:585
  140.4 16.5 %collective-permute-start.15 = (bf16[256,1024]{1,0:T(8,128)(2,1)}, bf16[256,1024]{1,0:T(8,128)(2,1)}, u32[]{:S(2)}, u32[]{:S(2)}) collective-permute-start(bf16[256,1024]{1,0:T(8,128)(2,1)} %collective-permute-done.12), channel_id=1, source_target_pairs={{4,0},{6,2},{5,1},{7,3},{20,16},{22,18},{21,17},{23,19}} | collective-permute-start | bytes 1572872 | tf_op jit(solution)/shard_map/ppermute | solution.py:585
  143.4 41.2 %collective-permute-start.27 = (bf16[512,512]{1,0:T(8,128)(2,1)}, bf16[512,512]{1,0:T(8,128)(2,1)}, u32[]{:S(2)}, u32[]{:S(2)}) collective-permute-start(bf16[512,512]{1,0:T(8,128)(2,1)} %get-tuple-element.143), channel_id=1, source_target_pairs={{0,2},{2,0},{4,6},{6,4},{8,10},{10,8},{12,14},{14,12},{1,3},{3,1},... | collective-permute-start | bytes 1572872 | tf_op jit(solution)/shard_map/ppermute | solution.py:578
  162.9 13.1 %collective-permute-start.16 = (bf16[256,1024]{1,0:T(8,128)(2,1)}, bf16[256,1024]{1,0:T(8,128)(2,1)S(1)}, u32[]{:S(2)}, u32[]{:S(2)}) collective-permute-start(bf16[256,1024]{1,0:T(8,128)(2,1)} %get-tuple-element.109.refs_0_), channel_id=1, source_target_pairs={{0,4},{2,6},{4,8},{6,10},{8,12},{10,14},{1,5},{3,7},{5,9},{7,11},{... | collective-permute-start | bytes 1572872 | tf_op jit(solution)/shard_map/ppermute | solution.py:585
  164.5 16.1 %collective-permute-start.17 = (bf16[256,1024]{1,0:T(8,128)(2,1)}, bf16[256,1024]{1,0:T(8,128)(2,1)}, u32[]{:S(2)}, u32[]{:S(2)}) collective-permute-start(bf16[256,1024]{1,0:T(8,128)(2,1)} %get-tuple-element.109.refs_0_), channel_id=1, source_target_pairs={{12,8},{14,10},{8,4},{10,6},{4,0},{6,2},{13,9},{15,11},{9,5},{11,7... | collective-permute-start | bytes 1572872 | tf_op jit(solution)/shard_map/ppermute | solution.py:585
  165.8 16.3 %collective-permute-start.18 = (bf16[256,1024]{1,0:T(8,128)(2,1)}, bf16[256,1024]{1,0:T(8,128)(2,1)}, u32[]{:S(2)}, u32[]{:S(2)}) collective-permute-start(bf16[256,1024]{1,0:T(8,128)(2,1)} %get-tuple-element.109.refs_0_), channel_id=1, source_target_pairs={{0,2},{2,0},{4,6},{6,4},{8,10},{10,8},{12,14},{14,12},{1,3},{3,1},... | collective-permute-start | bytes 1572872 | tf_op jit(solution)/shard_map/ppermute | solution.py:578
  167.5 17.0 %collective-permute-start.26 = (bf16[256,1024]{1,0:T(8,128)(2,1)S(1)}, bf16[256,1024]{1,0:T(8,128)(2,1)S(1)}, u32[]{:S(2)}, u32[]{:S(2)}) collective-permute-start(bf16[256,1024]{1,0:T(8,128)(2,1)S(1)} %broadcast_select_fusion.1.refs_16_.refs_10_.refs_8_), channel_id=1, source_target_pairs={{0,16},{16,0},{1,17},{17,1},{2,18},{18,2},{3,19},{19,3},{4,20},{20... | collective-permute-start | bytes 1572872 | tf_op jit(solution)/shard_map/ppermute | solution.py:575
  170.2 37.2 %copy-start.9 = (bf16[256,1024]{1,0:T(8,128)(2,1)}, bf16[256,1024]{1,0:T(8,128)(2,1)S(1)}, u32[]{:S(2)}) copy-start(bf16[256,1024]{1,0:T(8,128)(2,1)S(1)} %broadcast_select_fusion.2.refs_14_.refs_8_.refs_6_) | copy-start | bytes 1572868
  170.3 41.8 %copy-start.10 = (bf16[256,1024]{1,0:T(8,128)(2,1)}, bf16[256,1024]{1,0:T(8,128)(2,1)S(1)}, u32[]{:S(2)}) copy-start(bf16[256,1024]{1,0:T(8,128)(2,1)S(1)} %broadcast_select_fusion.3.refs_12_.refs_6_.refs_4_) | copy-start | bytes 1572868
  176.0 17.8 %collective-permute-start.25 = (bf16[256,1024]{1,0:T(8,128)(2,1)S(1)}, bf16[256,1024]{1,0:T(8,128)(2,1)}, u32[]{:S(2)}, u32[]{:S(2)}) collective-permute-start(bf16[256,1024]{1,0:T(8,128)(2,1)S(1)} %broadcast_select_fusion.2.refs_14_.refs_8_.refs_6_), channel_id=1, source_target_pairs={{0,16},{16,0},{1,17},{17,1},{2,18},{18,2},{3,19},{19,3},{4,20},{20... | collective-permute-start | bytes 1572872 | tf_op jit(solution)/shard_map/ppermute | solution.py:575
  180.6 22.7 %collective-permute-start.24 = (bf16[256,1024]{1,0:T(8,128)(2,1)S(1)}, bf16[256,1024]{1,0:T(8,128)(2,1)}, u32[]{:S(2)}, u32[]{:S(2)}) collective-permute-start(bf16[256,1024]{1,0:T(8,128)(2,1)S(1)} %broadcast_select_fusion.3.refs_12_.refs_6_.refs_4_), channel_id=1, source_target_pairs={{0,16},{16,0},{1,17},{17,1},{2,18},{18,2},{3,19},{19,3},{4,20},{20... | collective-permute-start | bytes 1572872 | tf_op jit(solution)/shard_map/ppermute | solution.py:575
  184.0 19.3 %collective-permute-start.21 = (bf16[256,1024]{1,0:T(8,128)(2,1)}, bf16[256,1024]{1,0:T(8,128)(2,1)}, u32[]{:S(2)}, u32[]{:S(2)}) collective-permute-start(bf16[256,1024]{1,0:T(8,128)(2,1)} %broadcast_select_fusion.refs_2_), channel_id=1, source_target_pairs={{0,2},{2,0},{4,6},{6,4},{8,10},{10,8},{12,14},{14,12},{1,3},{3,1},... | collective-permute-start | bytes 1572872 | tf_op jit(solution)/shard_map/ppermute | solution.py:578
  184.6 18.7 %collective-permute-start.23 = (bf16[256,1024]{1,0:T(8,128)(2,1)}, bf16[256,1024]{1,0:T(8,128)(2,1)}, u32[]{:S(2)}, u32[]{:S(2)}) collective-permute-start(bf16[256,1024]{1,0:T(8,128)(2,1)} %broadcast_select_fusion.refs_2_), channel_id=1, source_target_pairs={{0,1},{1,0},{2,3},{3,2},{4,5},{5,4},{6,7},{7,6},{8,9},{9,8},{10,11... | collective-permute-start | bytes 1572872 | tf_op jit(solution)/shard_map/ppermute | solution.py:684
  184.6 27.6 %copy-start.18 = (bf16[256,1024]{1,0:T(8,128)(2,1)}, bf16[256,1024]{1,0:T(8,128)(2,1)S(1)}, u32[]{:S(2)}) copy-start(bf16[256,1024]{1,0:T(8,128)(2,1)S(1)} %collective-permute-done.26.refs_17_.refs_11_.refs_9_) | copy-start | bytes 1572868
  184.6 18.7 %collective-permute-start.19 = (bf16[256,1024]{1,0:T(8,128)(2,1)S(1)}, bf16[256,1024]{1,0:T(8,128)(2,1)S(1)}, u32[]{:S(2)}, u32[]{:S(2)}) collective-permute-start(bf16[256,1024]{1,0:T(8,128)(2,1)S(1)} %collective-permute-done.16), channel_id=1, source_target_pairs={{4,8},{6,10},{8,12},{10,14},{5,9},{7,11},{9,13},{11,15},{20,24},{2... | collective-permute-start | bytes 1572872 | tf_op jit(solution)/shard_map/ppermute | solution.py:585
  193.8 12.7 %collective-permute-start.20 = (bf16[256,1024]{1,0:T(8,128)(2,1)}, bf16[256,1024]{1,0:T(8,128)(2,1)S(1)}, u32[]{:S(2)}, u32[]{:S(2)}) collective-permute-start(bf16[256,1024]{1,0:T(8,128)(2,1)} %collective-permute-done.17), channel_id=1, source_target_pairs={{8,4},{10,6},{4,0},{6,2},{9,5},{11,7},{5,1},{7,3},{24,20},{26,22},... | collective-permute-start | bytes 1572872 | tf_op jit(solution)/shard_map/ppermute | solution.py:585
  203.3 3.2 %collective-permute-start.22 = (bf16[256,1024]{1,0:T(8,128)(2,1)}, bf16[256,1024]{1,0:T(8,128)(2,1)}, u32[]{:S(2)}, u32[]{:S(2)}) collective-permute-start(bf16[256,1024]{1,0:T(8,128)(2,1)} %collective-permute-done.18.refs_1_), channel_id=1, source_target_pairs={{0,1},{1,0},{2,3},{3,2},{4,5},{5,4},{6,7},{7,6},{8,9},{9,8},{10,11... | collective-permute-start | bytes 1572872 | tf_op jit(solution)/shard_map/ppermute | solution.py:684
  207.4 4.7 %collective-permute-start.32 = (bf16[256,1024]{1,0:T(8,128)(2,1)}, bf16[256,1024]{1,0:T(8,128)(2,1)}, u32[]{:S(2)}, u32[]{:S(2)}) collective-permute-start(bf16[256,1024]{1,0:T(8,128)(2,1)} %fusion.1.refs_4_), channel_id=1, source_target_pairs={{0,1},{1,0},{2,3},{3,2},{4,5},{5,4},{6,7},{7,6},{8,9},{9,8},{10,11... | collective-permute-start | bytes 1572872 | tf_op jit(solution)/shard_map/ppermute | solution.py:684
  207.4 4.7 %collective-permute-start.31 = (bf16[256,1024]{1,0:T(8,128)(2,1)}, bf16[256,1024]{1,0:T(8,128)(2,1)}, u32[]{:S(2)}, u32[]{:S(2)}) collective-permute-start(bf16[256,1024]{1,0:T(8,128)(2,1)} %collective-permute-done.21.refs_3_), channel_id=1, source_target_pairs={{0,1},{1,0},{2,3},{3,2},{4,5},{5,4},{6,7},{7,6},{8,9},{9,8},{10,11... | collective-permute-start | bytes 1572872 | tf_op jit(solution)/shard_map/ppermute | solution.py:684
  207.9 16.3 %collective-permute-start.30 = (bf16[256,1024]{1,0:T(8,128)(2,1)}, bf16[256,1024]{1,0:T(8,128)(2,1)}, u32[]{:S(2)}, u32[]{:S(2)}) collective-permute-start(bf16[256,1024]{1,0:T(8,128)(2,1)} %fusion.1.refs_4_), channel_id=1, source_target_pairs={{0,2},{2,0},{4,6},{6,4},{8,10},{10,8},{12,14},{14,12},{1,3},{3,1},... | collective-permute-start | bytes 1572872 | tf_op jit(solution)/shard_map/ppermute | solution.py:578
  209.4 14.8 %collective-permute-start.28 = (bf16[256,1024]{1,0:T(8,128)(2,1)S(1)}, bf16[256,1024]{1,0:T(8,128)(2,1)S(1)}, u32[]{:S(2)}, u32[]{:S(2)}) collective-permute-start(bf16[256,1024]{1,0:T(8,128)(2,1)S(1)} %collective-permute-done.19), channel_id=1, source_target_pairs={{8,12},{10,14},{9,13},{11,15},{24,28},{26,30},{25,29},{27,31}} | collective-permute-start | bytes 1572872 | tf_op jit(solution)/shard_map/ppermute | solution.py:585
  210.1 15.4 %collective-permute-start.29 = (bf16[256,1024]{1,0:T(8,128)(2,1)S(1)}, bf16[256,1024]{1,0:T(8,128)(2,1)S(1)}, u32[]{:S(2)}, u32[]{:S(2)}) collective-permute-start(bf16[256,1024]{1,0:T(8,128)(2,1)S(1)} %collective-permute-done.20), channel_id=1, source_target_pairs={{4,0},{6,2},{5,1},{7,3},{20,16},{22,18},{21,17},{23,19}} | collective-permute-start | bytes 1572872 | tf_op jit(solution)/shard_map/ppermute | solution.py:585
  225.7 2.0 collective-permute-start.35
  225.7 2.9 %collective-permute-start.34 = (bf16[256,1024]{1,0:T(8,128)(2,1)}, bf16[256,1024]{1,0:T(8,128)(2,1)S(1)}, u32[]{:S(2)}, u32[]{:S(2)}) collective-permute-start(bf16[256,1024]{1,0:T(8,128)(2,1)} %collective-permute-done.30.refs_0_), channel_id=1, source_target_pairs={{0,1},{1,0},{2,3},{3,2},{4,5},{5,4},{6,7},{7,6},{8,9},{9,8},{10,11... | collective-permute-start | bytes 1572872 | tf_op jit(solution)/shard_map/ppermute | solution.py:684
  226.2 13.9 %collective-permute-start.33 = (bf16[256,1024]{1,0:T(8,128)(2,1)S(1)}, bf16[256,1024]{1,0:T(8,128)(2,1)S(1)}, u32[]{:S(2)}, u32[]{:S(2)}) collective-permute-start(bf16[256,1024]{1,0:T(8,128)(2,1)S(1)} %select_select_fusion.1.refs_1_), channel_id=1, source_target_pairs={{0,2},{2,0},{4,6},{6,4},{8,10},{10,8},{12,14},{14,12},{1,3},{3,1},... | collective-permute-start | bytes 1572872 | tf_op jit(solution)/shard_map/ppermute | solution.py:578
  240.1 1.9 collective-permute-start.36
  256.5 14.2 %collective-permute-start.37 = (bf16[512,512]{1,0:T(8,128)(2,1)}, bf16[512,512]{1,0:T(8,128)(2,1)S(1)}, u32[]{:S(2)}, u32[]{:S(2)}) collective-permute-start(bf16[512,512]{1,0:T(8,128)(2,1)} %decode_rows.3), channel_id=1, source_target_pairs={{0,2},{2,0},{4,6},{6,4},{8,10},{10,8},{12,14},{14,12},{1,3},{3,1},... | collective-permute-start | bytes 1572872 | tf_op jit(solution)/shard_map/ppermute | solution.py:733
  (22 other events, 157.1 us)

commit v8 on v7

--- a/solution.py
+++ b/solution.py
@@ -263,7 +263,7 @@
         encode_kernel,
         grid_spec=grid_spec,
         out_shape=jax.ShapeDtypeStruct((blocks * (rows + EXTRA), width), jnp.bfloat16),
-        compiler_params=params(32),
+        compiler_params=params(BIG),
         cost_estimate=cost(
             16 * blocks * rows * tokens * width, 8 * tokens * width, blocks * rows * tokens * 8
         ),
@@ -425,8 +425,10 @@
             pl.when(is_mine)(functools.partial(copy, mine))
             pl.when(jnp.logical_not(is_mine))(functools.partial(copy, theirs))
 
-    for j, band in enumerate(w_refs):
-        w_ref[j * depth : (j + 1) * depth, :] = band[...]
+    start = 0
+    for band in w_refs:
+        w_ref[start : start + band.shape[0], :] = band[...]
+        start += band.shape[0]
     out_ref[...] = jnp.dot(
         normed_ref[...], w_ref[...], preferred_element_type=jnp.float32
     ).astype(jnp.bfloat16)
@@ -435,14 +437,14 @@
 def latent_keys_values(ids, mine, theirs, bands):
     pieces = len(mine)
     rows, half = mine[0].shape
-    depth, width = bands[0].shape
+    width = bands[0].shape[1]
     block = min(512, width)
-    total = depth * len(bands)
+    total = sum(band.shape[0] for band in bands)
     grid_spec = pltpu.PrefetchScalarGridSpec(
         num_scalar_prefetch=1,
         grid=(width // block,),
         in_specs=[whole((rows, half))] * (2 * pieces)
-        + [pl.BlockSpec((depth, block), lambda i, ids: (0, i))] * len(bands),
+        + [pl.BlockSpec((band.shape[0], block), lambda i, ids: (0, i)) for band in bands],
         out_specs=pl.BlockSpec((rows * pieces, block), lambda i, ids: (0, i)),
         scratch_shapes=[
             pltpu.VMEM((rows * pieces, total), jnp.bfloat16),
@@ -473,8 +475,8 @@
     return chunks + ([open_chunk] if open_chunk else [])
 
 
-def decode_kernel(parts, q_ref, *refs):
-    k_refs, v_refs, out_ref = refs[:parts], refs[parts : 2 * parts], refs[-1]
+def decode_kernel(parts, first, last, q_ref, *refs):
+    k_refs, v_refs, rest = refs[:parts], refs[parts : 2 * parts], refs[2 * parts :]
 
     def gathered(sources, chunk, cols):
         rows = [sources[i][start:stop, cols] for i, start, stop in chunk]
@@ -482,7 +484,10 @@
 
     for h in range(q_ref.shape[1] // HEAD_DIM):
         cols = slice(h * HEAD_DIM, (h + 1) * HEAD_DIM)
+        wide = slice(2 * h * HEAD_DIM, 2 * (h + 1) * HEAD_DIM)
         top = acc = None
+        if not first:
+            top, acc = rest[0][:, cols][:, :1], rest[1][:, wide]
         for chunk in row_chunks([k.shape[0] for k in k_refs], 512):
             keys, values = gathered(k_refs, chunk, cols), gathered(v_refs, chunk, cols)
             scores = lax.dot_general(q_ref[:, cols], keys, NT, preferred_element_type=jnp.float32)
@@ -499,23 +504,37 @@
             if top is not None:
                 summed = summed + acc * jnp.exp2(top - new_top)
             top, acc = new_top, summed
-        out_ref[:, cols] = (acc[:, :HEAD_DIM] / acc[:, HEAD_DIM:]).astype(out_ref.dtype)
-
-
-def decode(queries, keys_values, out_type):
+        if last:
+            out_ref = rest[-1]
+            out_ref[:, cols] = (acc[:, :HEAD_DIM] / acc[:, HEAD_DIM:]).astype(out_ref.dtype)
+        else:
+            rest[-2][:, cols] = jnp.broadcast_to(top, (top.shape[0], HEAD_DIM))
+            rest[-1][:, wide] = acc
+
+
+def decode(queries, keys_values, state, out_type):
+    first, last = state is None, out_type is not None
     tokens, width = queries.shape
     latents = sum(v.shape[0] for v in keys_values)
     pair = min(2 * HEAD_DIM, width)
     steps = width // pair
     narrow = pl.BlockSpec((tokens, pair), lambda i: (0, i))
+    wide = pl.BlockSpec((tokens, 2 * pair), lambda i: (0, i))
     keys = [pl.BlockSpec((v.shape[0], pair), lambda i: (0, i)) for v in keys_values]
     values = [pl.BlockSpec((v.shape[0], pair), lambda i: (0, steps + i)) for v in keys_values]
+    if last:
+        out_specs, out_shape = narrow, jax.ShapeDtypeStruct((tokens, width), out_type)
+    else:
+        out_specs = [narrow, wide]
+        out_shape = [
+            jax.ShapeDtypeStruct((tokens, n * width), jnp.float32) for n in (1, 2)
+        ]
     return pl.pallas_call(
-        functools.partial(decode_kernel, len(keys_values)),
+        functools.partial(decode_kernel, len(keys_values), first, last),
         grid=(steps,),
-        in_specs=[narrow, *keys, *values],
-        out_specs=narrow,
-        out_shape=jax.ShapeDtypeStruct((tokens, width), out_type),
+        in_specs=[narrow, *keys, *values, *([] if first else [narrow, wide])],
+        out_specs=out_specs,
+        out_shape=out_shape,
         compiler_params=params(BIG),
         cost_estimate=cost(
             16 * tokens * latents * width,
@@ -523,7 +542,7 @@
             tokens * latents * (width // HEAD_DIM),
         ),
         name="decode_rows",
-    )(queries, *keys_values, *keys_values)
+    )(queries, *keys_values, *keys_values, *([] if first else state))
 
 
 def swap_perm(size):
@@ -658,14 +677,14 @@
     attended, for_near = merge(y, parts, far)
     from_near = over_near(for_near)
     kept = kept_queries()
-    from_near, hops, kept = lax.optimization_barrier((from_near, hops, kept))
-    for step in range(3, far):
-        hops[step] = hop(step, hops[step - 1])
+    from_near, kept = lax.optimization_barrier((from_near, kept))
     out_ids = jnp.stack([*places, y, x]).astype(jnp.int32)
     weights = [w_out, out_far, out_far_other, out_near, out_near_other]
     partial_value = project(out_ids, attended, from_near, weights)
+    partial_value, hops = lax.optimization_barrier((partial_value, hops))
+    for step in range(3, far):
+        hops[step] = hop(step, hops[step - 1])
     theirs = lax.ppermute(partial_value, "head", swap_perm(2))
-    theirs, hops = lax.optimization_barrier((theirs, hops))
     own_cols, normed, normed_other = normalise(
         place, partial_value, theirs, latent_array, norm_gain[None, :]
     )
@@ -675,9 +694,8 @@
     near_queries = over_near(columns((queries,), 1 - y))
 
     kv_at = [p, p ^ 1]
-    for k in range(1, far):
-        there = ((z + k) % far) * 2
-        kv_at += [there + (y ^ x), there + (1 - (y ^ x))]
+    for other in (x, 1 - x):
+        kv_at += [((z + k) % far) * 2 + (y ^ other) for k in range(1, far)]
     kv_ids = jnp.stack([place, *kv_at]).astype(jnp.int32)
 
     def cores(values):
@@ -702,11 +720,12 @@
 
     came = {0: [normed, normed]}
     came[1] = hop(1, came[0])
-    moved = {k: by_shift(hops, k) for k in range(1, far)}
-    swapped = {k: over_groups(v) for k, v in moved.items()}
-    came, normed_near, moved = lax.optimization_barrier((came, over_near(normed), moved))
+    normed_near = over_near(normed)
+    came, hops = lax.optimization_barrier((came, hops))
+    kv_moved = jnp.concatenate([by_shift(hops, k) for k in range(1, far)])
+    kv_bands = [kv_own, kv_near, kv_moved, over_groups(kv_moved)]
     mine, other = [normed, normed_near], [normed_other, *cores([normed_near])]
-    keys_values = []
+    keys_values, near_state = [], None
     for step in range(1, far):
         fresh = arrival(came, step)
         if step + 1 < far:
@@ -717,19 +736,22 @@
         if step > 1:
             keys_values.append(fold(mine, other))
             mine, other = [], []
-        came, fresh_near, mine, other, keys_values, swapped, near_queries = (
-            lax.optimization_barrier(
-                (came, fresh_near, mine, other, keys_values, swapped, near_queries)
+        if step == 2 and far > 3:
+            near_state = decode(near_queries, keys_values, None, None)
+        if step + 1 < far:
+            came, keys_values, near_state = lax.optimization_barrier(
+                (came, keys_values, near_state)
             )
-        )
-        kv_bands = [kv_own, kv_near]
-        for k in range(1, far):
-            kv_bands += [moved[k], swapped[k]]
+        else:
+            fresh_near, keys_values = lax.optimization_barrier((fresh_near, keys_values))
         mine.append(fresh_near)
         other += cores([fresh_near])
     keys_values.append(fold(mine, other))
-    near_state = decode(near_queries, keys_values, jnp.bfloat16)
-    own_state = decode(own_queries, keys_values, jnp.float32)
+    own_state = decode(own_queries, keys_values, None, jnp.float32)
+    if far > 3:
+        near_state = decode(near_queries, keys_values[1:], near_state, jnp.bfloat16)
+    else:
+        near_state = decode(near_queries, keys_values, None, jnp.bfloat16)
     from_near = lax.ppermute(near_state, "pos", near).astype(jnp.float32)
     decoded = jnp.where(
         y == 0,

time: 274 us -> 274 us (level)
  Pallas kernels: 66.1 us -> 74.5 us
  waiting for transfers between devices: 126 us -> 121 us
  local copies, waits for them, and re-layouts: 18.6 us -> 13.9 us
    ppermute x4 -> x2, waiting for transfers between devices: 22.8 us -> 5.17 us  [over_groups(): return lax.ppermute(value, 'groups', swap_perm(groups))]
    ppermute x10, waiting for transfers between devices: 25.8 us -> 41 us  [over_near(): return lax.ppermute(value, 'pos', near)]
    pallas_call x2 -> x3, Pallas kernels: 16.7 us -> 24.2 us  [decode(): pl.pallas_call(functools.partial(decode_kernel, len(keys_values), first,...]
    ppermute x12, starting transfers between devices: 16.7 us -> 22.9 us  [hop(): lax.ppermute(v, 'pos', hop_perm(pos, step, way))]
    unnamed x66 -> x70, local copies, waits for them, and re-layouts: 9.25 us -> 5.33 us
    ppermute x12, waiting for transfers between devices: 49.6 us -> 46.5 us  [hop(): lax.ppermute(v, 'pos', hop_perm(pos, step, way))]
    ppermute x4 -> x2, starting transfers between devices: 6.1 us -> 3.12 us  [over_groups(): return lax.ppermute(value, 'groups', swap_perm(groups))]
  transfers between devices with their start and end apart: 39 -> 37, of which waited for: 21 -> 20; matrix products, arithmetic and copies ran while one was open for 9% -> 8% of each run, Pallas kernels for 12% -> 16%
where the time goes in v8:
time: 274 us; the launch traced here: 273 us
  waiting for transfers between devices  121 us (44%)
  Pallas kernels  74.5 us (27%)
  starting transfers between devices  45.5 us (17%)
  other arithmetic  16.4 us (6%)
  local copies, waits for them, and re-layouts  13.9 us (5%)
    ppermute x12, waiting for transfers between devices, hop(): lax.ppermute(v, 'pos', hop_perm(pos, step, way))  46.5 us
    ppermute x10, waiting for transfers between devices, over_near(): return lax.ppermute(value, 'pos', near)  41 us
    pallas_call x3, Pallas kernels, decode(): pl.pallas_call(functools.partial(decode_kernel, len(keys_values), first,...  24.2 us
    pallas_call x3, Pallas kernels, latent_keys_values(): pl.pallas_call(functools.partial(latents_kernel, pieces), grid_spec=grid_...  23.5 us
    ppermute x12, starting transfers between devices, hop(): lax.ppermute(v, 'pos', hop_perm(pos, step, way))  22.9 us
    ppermute x3, waiting for transfers between devices, over_far(): return lax.ppermute(value, 'pos', shift_perm(pos, k))  18.3 us
    pallas_call x1, Pallas kernels, encode(): pl.pallas_call(encode_kernel, grid_spec=grid_spec, out_shape=jax.ShapeDty...  14.6 us
    ppermute x10, starting transfers between devices, over_near(): return lax.ppermute(value, 'pos', near)  9.63 us
  transfers between devices with their start and end apart: 37, of which 20 were waited for; matrix products, arithmetic and copies ran while one was open for 8% of the time, Pallas kernels for 16%

profile of v8, /device:TPU:0, one launch (start us, length us, event | category | flops | bytes accessed | tf_op | source)
XLA Modules:
  0.0 273.3 jit_solution(12507081805180088292)
XLA Ops:
  1.4 1.3 constant_dynamic-slice_fusion.9
  2.9 3.0 %collective-permute-start = (bf16[528,1024]{1,0:T(8,128)(2,1)S(1)}, bf16[528,1024]{1,0:T(8,128)(2,1)}, u32[]{:S(2)}, u32[]{:S(2)}) collective-permute-start(bf16[528,1024]{1,0:T(8,128)(2,1)S(1)} %pad_maximum_fusion.1), channel_id=1, source_target_pairs={{0,2},{2,0},{4,6},{6,4},{8,10},{10,8},{12,14},{14,12},{1,3},{3,1},... | collective-permute-start | bytes 3244040 | tf_op jit(solution)/shard_map/ppermute | solution.py:597
  7.0 3.7 %collective-permute-start.1 = (bf16[528,256]{1,0:T(8,128)(2,1)S(1)}, bf16[528,256]{1,0:T(8,128)(2,1)S(1)}, u32[]{:S(2)}, u32[]{:S(2)}) collective-permute-start(bf16[528,256]{1,0:T(8,128)(2,1)S(1)} %pad_maximum_fusion.6), channel_id=1, source_target_pairs={{4,0},{6,2},{8,4},{10,6},{12,8},{14,10},{0,12},{2,14},{5,1},{7,3},... | collective-permute-start | bytes 811016 | tf_op jit(solution)/shard_map/ppermute | solution.py:600
  12.3 1.9 constant_dynamic-slice_fusion.2
  15.1 2.5 collective-permute-done.1
  17.6 15.8 %collective-permute-done.2 = bf16[528,256]{1,0:T(8,128)(2,1)S(1)} collective-permute-done((bf16[528,256]{1,0:T(8,128)(2,1)S(1)}, bf16[528,256]{1,0:T(8,128)(2,1)S(1)}, u32[]{:S(2)}, u32[]{:S(2)}) %collective-permute-start.2) | collective-permute-done | bytes 270368 | tf_op jit(solution)/shard_map/ppermute | solution.py:600
  33.4 14.6 %encode_rows.1 = bf16[2112,512]{1,0:T(8,128)(2,1)} custom-call(s32[1]{0:T(128)} %bitcast.9.ids_ref, bf16[2048,1024]{1,0:T(8,128)(2,1)} %q_ref.1, bf16[512,1024]{1,0:T(8,128)(2,1)} %k_ref.1, bf16[512,1024]{1,0:T(8,128)(2,1)} %v_ref.1, bf16[16,1024]{1,0:T(8,128)(2,1)} %copy-done.26, bf16[528,1024]{1,0:T(8,128)(2,1)} %collective-permute-done.near_ref, ...), custom_call_target="tpu_custom_call" | custom-call | flops 8589934592 | bytes 2097152 | tf_op jit(solution)/shard_map/encode_rows/pallas_call | solution.py:262
  48.0 4.0 %all-to-all-start = ((bf16[4,528,512]{2,1,0:T(8,128)(2,1)}), bf16[4,528,512]{2,1,0:T(8,128)(2,1)S(1)}, u32[]{:S(2)}, u32[]{:S(2)}) async-start(bf16[4,528,512]{2,1,0:T(8,128)(2,1)} %bitcast.46), calls=%async_computation | async-start | bytes 4325376 | tf_op jit(solution)/shard_map/all_to_all | solution.py:658
  52.6 1.6 collective-permute-start.6
  54.1 10.8 %collective-permute-done.4.refs_11_.refs_5_.refs_3_ = bf16[256,1024]{1,0:T(8,128)(2,1)S(1)} collective-permute-done((bf16[256,1024]{1,0:T(8,128)(2,1)}, bf16[256,1024]{1,0:T(8,128)(2,1)S(1)}, u32[]{:S(2)}, u32[]{:S(2)}) %collective-permute-start.4) | collective-permute-done | bytes 524320 | tf_op jit(solution)/shard_map/ppermute | solution.py:597
  64.9 2.4 pad_maximum_fusion.2
  67.9 3.4 %collective-permute-done.6.refs_2_ = bf16[1584,256]{1,0:T(8,128)(2,1)S(1)} collective-permute-done((bf16[1584,256]{1,0:T(8,128)(2,1)S(1)}, bf16[1584,256]{1,0:T(8,128)(2,1)S(1)}, u32[]{:S(2)}, u32[]{:S(2)}) %collective-permute-start.6) | collective-permute-done | bytes 811040 | tf_op jit(solution)/shard_map/ppermute | solution.py:594
  72.5 1.5 collective-permute-start.7
  74.0 2.3 pad_maximum_fusion.5
  76.3 3.7 %collective-permute-start.8 = (bf16[256,1024]{1,0:T(8,128)(2,1)}, bf16[256,1024]{1,0:T(8,128)(2,1)S(1)}, u32[]{:S(2)}, u32[]{:S(2)}) collective-permute-start(bf16[256,1024]{1,0:T(8,128)(2,1)} %get-tuple-element.105), channel_id=1, source_target_pairs={{0,4},{2,6},{4,8},{6,10},{8,12},{10,14},{1,5},{3,7},{5,9},{7,11},{... | collective-permute-start | bytes 1572872 | tf_op jit(solution)/shard_map/ppermute | solution.py:604
  82.8 14.8 %collective-permute-done.8 = bf16[256,1024]{1,0:T(8,128)(2,1)S(1)} collective-permute-done((bf16[256,1024]{1,0:T(8,128)(2,1)}, bf16[256,1024]{1,0:T(8,128)(2,1)S(1)}, u32[]{:S(2)}, u32[]{:S(2)}) %collective-permute-start.8) | collective-permute-done | bytes 524320 | tf_op jit(solution)/shard_map/ppermute | solution.py:604
  97.6 5.7 %collective-permute-done.9 = bf16[256,1024]{1,0:T(8,128)(2,1)S(1)} collective-permute-done((bf16[256,1024]{1,0:T(8,128)(2,1)}, bf16[256,1024]{1,0:T(8,128)(2,1)S(1)}, u32[]{:S(2)}, u32[]{:S(2)}) %collective-permute-start.9) | collective-permute-done | bytes 524320 | tf_op jit(solution)/shard_map/ppermute | solution.py:604
  103.4 11.3 %collective-permute-done.7.refs_4_ = bf16[2112,256]{1,0:T(8,128)(2,1)} collective-permute-done((bf16[2112,256]{1,0:T(8,128)(2,1)}, bf16[2112,256]{1,0:T(8,128)(2,1)}, u32[]{:S(2)}, u32[]{:S(2)}) %collective-permute-start.7) | collective-permute-done | bytes 1081376 | tf_op jit(solution)/shard_map/ppermute | solution.py:597
  114.6 1.5 collective-permute-start.11
  119.6 1.9 merge_rows.1
  122.8 5.7 %collective-permute-done.10.near_ref = bf16[256,512]{1,0:T(8,128)(2,1)S(1)} collective-permute-done((bf16[256,512]{1,0:T(8,128)(2,1)S(1)}, bf16[256,512]{1,0:T(8,128)(2,1)S(1)}, u32[]{:S(2)}, u32[]{:S(2)}) %collective-permute-start.10) | collective-permute-done | bytes 262176 | tf_op jit(solution)/shard_map/ppermute | solution.py:597
  129.2 5.7 %project_rows.1.mine_ref = f32[256,2048]{1,0:T(8,128)} custom-call(s32[10]{0:T(128)} %stack.82.ids_ref, bf16[256,512]{1,0:T(8,128)(2,1)} %copy-done.2, bf16[256,512]{1,0:T(8,128)(2,1)} %copy-done.25, bf16[1024,256]{1,0:T(8,128)(2,1)} %refs_0_.1, bf16[1584,256]{1,0:T(8,128)(2,1)} %copy-done.8, bf16[1584,256]{1,0:T(8,128)(2,1)} %copy-done.4, ...), custom_call_target="tpu_custom_call" | custom-call | flops 1073741824 | bytes 6291456 | tf_op jit(solution)/shard_map/project_rows/pallas_call | solution.py:357
  135.0 1.5 collective-permute-start.16
  137.7 1.6 collective-permute-done.13.theirs_ref
  139.4 1.4 copy-done.6
  140.7 4.6 %norm_rows.1 = (f32[256,1024]{1,0:T(8,128)}, bf16[256,1024]{1,0:T(8,128)(2,1)}, bf16[256,1024]{1,0:T(8,128)(2,1)}) custom-call(s32[1]{0:T(128)} %bitcast.ids_ref, f32[256,2048]{1,0:T(8,128)} %project_rows.1.mine_ref, f32[256,2048]{1,0:T(8,128)} %copy-done.6, bf16[256,2048]{1,0:T(8,128)(2,1)} %latent_ref.1, f32[1,2048]{1,0:T(1,128)} %bitcast.49), custom_call_target="tpu_custom_call" | custom-call | flops 3145728 | bytes 6815744 | tf_op jit(solution)/shard_map/norm_rows/pallas_call | solution.py:391
  145.3 7.0 %collective-permute-start.14 = (bf16[256,1024]{1,0:T(8,128)(2,1)}, bf16[256,1024]{1,0:T(8,128)(2,1)S(1)}, u32[]{:S(2)}, u32[]{:S(2)}) collective-permute-start(bf16[256,1024]{1,0:T(8,128)(2,1)} %get-tuple-element.71.refs_0_), channel_id=1, source_target_pairs={{0,4},{2,6},{4,8},{6,10},{8,12},{10,14},{1,5},{3,7},{5,9},{7,11},{... | collective-permute-start | bytes 1572872 | tf_op jit(solution)/shard_map/ppermute | solution.py:604
  154.2 1.3 collective-permute-done.17
  155.5 8.5 %collective-permute-done.14 = bf16[256,1024]{1,0:T(8,128)(2,1)S(1)} collective-permute-done((bf16[256,1024]{1,0:T(8,128)(2,1)}, bf16[256,1024]{1,0:T(8,128)(2,1)S(1)}, u32[]{:S(2)}, u32[]{:S(2)}) %collective-permute-start.14) | collective-permute-done | bytes 524320 | tf_op jit(solution)/shard_map/ppermute | solution.py:604
  164.1 5.1 %collective-permute-done.15 = bf16[256,1024]{1,0:T(8,128)(2,1)S(1)} collective-permute-done((bf16[256,1024]{1,0:T(8,128)(2,1)}, bf16[256,1024]{1,0:T(8,128)(2,1)S(1)}, u32[]{:S(2)}, u32[]{:S(2)}) %collective-permute-start.15) | collective-permute-done | bytes 524320 | tf_op jit(solution)/shard_map/ppermute | solution.py:604
  171.7 1.6 collective-permute-start.28
  175.3 1.9 broadcast_select_fusion.3.refs_2_
  178.3 11.0 %collective-permute-done.19 = bf16[256,1024]{1,0:T(8,128)(2,1)S(1)} collective-permute-done((bf16[256,1024]{1,0:T(8,128)(2,1)}, bf16[256,1024]{1,0:T(8,128)(2,1)S(1)}, u32[]{:S(2)}, u32[]{:S(2)}) %collective-permute-start.19) | collective-permute-done | bytes 524320 | tf_op jit(solution)/shard_map/ppermute | solution.py:604
  193.4 1.5 collective-permute-start.29
  196.4 1.3 collective-permute-start.21
  197.7 8.0 %collective-permute-done.31.refs_0_ = bf16[256,1024]{1,0:T(8,128)(2,1)} collective-permute-done((bf16[256,1024]{1,0:T(8,128)(2,1)}, bf16[256,1024]{1,0:T(8,128)(2,1)}, u32[]{:S(2)}, u32[]{:S(2)}) %collective-permute-start.31) | collective-permute-done | bytes 524320 | tf_op jit(solution)/shard_map/ppermute | solution.py:597
  205.7 1.8 collective-permute-done.28.refs_13_.refs_7_.refs_5_
  207.5 11.7 %latent_keys_values.3.refs_0_.refs_1_.refs_3_ = bf16[1280,1024]{1,0:T(8,128)(2,1)} custom-call(s32[9]{0:T(128)} %stack.92.ids_ref, bf16[256,1024]{1,0:T(8,128)(2,1)} %get-tuple-element.71.refs_0_, bf16[256,1024]{1,0:T(8,128)(2,1)} %collective-permute-done.22.refs_1_, bf16[256,1024]{1,0:T(8,128)(2,1)} %broadcast_select_fusion.3.refs_2_, ...), custom_call_target="tpu_custom_call" | custom-call | flops 5368709120 | bytes 4194304 | tf_op jit(solution)/shard_map/latent_keys_values/pallas_call | solution.py:454
  219.3 6.0 %decode_rows.3 = (f32[512,512]{1,0:T(8,128)}, f32[512,1024]{1,0:T(8,128)}) custom-call(bf16[512,512]{1,0:T(8,128)(2,1)} %collective-permute-done.29.q_ref, bf16[1280,1024]{1,0:T(8,128)(2,1)} %latent_keys_values.3.refs_0_.refs_1_.refs_3_, bf16[1280,1024]{1,0:T(8,128)(2,1)} %latent_keys_values.3.refs_0_.refs_1_.refs_3_), custom_call_target="tpu_custom_call" | custom-call | flops 5368709120 | bytes 4194304 | tf_op jit(solution)/shard_map/decode_rows/pallas_call | solution.py:532
  225.9 1.4 collective-permute-done.33.refs_3_
  228.2 6.7 %latent_keys_values.4.refs_1_.refs_4_.refs_0_.refs_2_ = bf16[512,1024]{1,0:T(8,128)(2,1)} custom-call(s32[9]{0:T(128)} %stack.92.ids_ref, bf16[256,1024]{1,0:T(8,128)(2,1)} %collective-permute-done.31.refs_0_, bf16[256,1024]{1,0:T(8,128)(2,1)} %copy-done.24, bf16[256,1024]{1,0:T(8,128)(2,1)} %copy-done.31, bf16[256,1024]{1,0:T(8,128)(2,1)} %copy-done.32, ...), custom_call_target="tpu_custom_call" | custom-call | flops 2147483648 | bytes 4194304 | tf_op jit(solution)/shard_map/latent_keys_values/pallas_call | solution.py:454
  234.9 4.9 %collective-permute-done.30.refs_0_ = bf16[256,1024]{1,0:T(8,128)(2,1)S(1)} collective-permute-done((bf16[256,1024]{1,0:T(8,128)(2,1)S(1)}, bf16[256,1024]{1,0:T(8,128)(2,1)S(1)}, u32[]{:S(2)}, u32[]{:S(2)}) %collective-permute-start.30) | collective-permute-done | bytes 524320 | tf_op jit(solution)/shard_map/ppermute | solution.py:597
  239.8 1.9 collective-permute-done.34.refs_1_
  242.5 5.1 %latent_keys_values.5.refs_2_.refs_5_.refs_1_.refs_3_ = bf16[256,1024]{1,0:T(8,128)(2,1)} custom-call(s32[9]{0:T(128)} %stack.92.ids_ref, bf16[256,1024]{1,0:T(8,128)(2,1)} %copy-done.16, bf16[256,1024]{1,0:T(8,128)(2,1)} %copy-done.17, bf16[256,1024]{1,0:T(8,128)(2,1)} %get-tuple-element.104.refs_10_.refs_4_.refs_2_, bf16[256,1024]{1,0:T(8,128)(2,1)} %copy-done.5, ...), custom_call_target="tpu_custom_call" | custom-call | flops 1073741824 | bytes 4194304 | tf_op jit(solution)/shard_map/latent_keys_values/pallas_call | solution.py:454
  247.6 9.8 %decode_rows.5 = bf16[512,512]{1,0:T(8,128)(2,1)} custom-call(bf16[512,512]{1,0:T(8,128)(2,1)} %collective-permute-done.29.q_ref, bf16[512,1024]{1,0:T(8,128)(2,1)} %latent_keys_values.4.refs_1_.refs_4_.refs_0_.refs_2_, bf16[256,1024]{1,0:T(8,128)(2,1)} %latent_keys_values.5.refs_2_.refs_5_.refs_1_.refs_3_, ...), custom_call_target="tpu_custom_call" | custom-call | flops 3221225472 | bytes 3145728 | tf_op jit(solution)/shard_map/decode_rows/pallas_call | solution.py:532
  257.8 8.4 %decode_rows.4 = f32[512,512]{1,0:T(8,128)} custom-call(bf16[512,512]{1,0:T(8,128)(2,1)} %get-tuple-element.102.q_ref, bf16[1280,1024]{1,0:T(8,128)(2,1)} %latent_keys_values.3.refs_0_.refs_1_.refs_3_, bf16[512,1024]{1,0:T(8,128)(2,1)} %latent_keys_values.4.refs_1_.refs_4_.refs_0_.refs_2_, ...), custom_call_target="tpu_custom_call" | custom-call | flops 8589934592 | bytes 5767168 | tf_op jit(solution)/shard_map/decode_rows/pallas_call | solution.py:532
  266.2 5.4 %collective-permute-done.35 = bf16[512,512]{1,0:T(8,128)(2,1)S(1)} collective-permute-done((bf16[512,512]{1,0:T(8,128)(2,1)}, bf16[512,512]{1,0:T(8,128)(2,1)S(1)}, u32[]{:S(2)}, u32[]{:S(2)}) %collective-permute-start.35) | collective-permute-done | bytes 524320 | tf_op jit(solution)/shard_map/ppermute | solution.py:755
  271.8 1.6 fusion
  (150 shorter events, 32.1 us)
Async XLA Ops:
  0.6 190.6 %copy-start = (bf16[3,1024]{1,0:T(4,128)(2,1)S(1)}, bf16[3,1024]{1,0:T(4,128)(2,1)}, u32[]{:S(2)}) copy-start(bf16[3,1024]{1,0:T(4,128)(2,1)} %param.25) | copy-start | bytes 18436
  2.9 30.4 %collective-permute-start = (bf16[528,1024]{1,0:T(8,128)(2,1)S(1)}, bf16[528,1024]{1,0:T(8,128)(2,1)}, u32[]{:S(2)}, u32[]{:S(2)}) collective-permute-start(bf16[528,1024]{1,0:T(8,128)(2,1)S(1)} %pad_maximum_fusion.1), channel_id=1, source_target_pairs={{0,2},{2,0},{4,6},{6,4},{8,10},{10,8},{12,14},{14,12},{1,3},{3,1},... | collective-permute-start | bytes 3244040 | tf_op jit(solution)/shard_map/ppermute | solution.py:597
  7.0 41.0 %copy-start.9 = (bf16[528,256]{1,0:T(8,128)(2,1)}, bf16[528,256]{1,0:T(8,128)(2,1)S(1)}, u32[]{:S(2)}) copy-start(bf16[528,256]{1,0:T(8,128)(2,1)S(1)} %pad_maximum_fusion.6) | copy-start | bytes 811012
  7.0 10.6 %collective-permute-start.1 = (bf16[528,256]{1,0:T(8,128)(2,1)S(1)}, bf16[528,256]{1,0:T(8,128)(2,1)S(1)}, u32[]{:S(2)}, u32[]{:S(2)}) collective-permute-start(bf16[528,256]{1,0:T(8,128)(2,1)S(1)} %pad_maximum_fusion.6), channel_id=1, source_target_pairs={{4,0},{6,2},{8,4},{10,6},{12,8},{14,10},{0,12},{2,14},{5,1},{7,3},... | collective-permute-start | bytes 811016 | tf_op jit(solution)/shard_map/ppermute | solution.py:600
  10.6 22.7 %collective-permute-start.2 = (bf16[528,256]{1,0:T(8,128)(2,1)S(1)}, bf16[528,256]{1,0:T(8,128)(2,1)S(1)}, u32[]{:S(2)}, u32[]{:S(2)}) collective-permute-start(bf16[528,256]{1,0:T(8,128)(2,1)S(1)} %pad_maximum_fusion.6), channel_id=1, source_target_pairs={{8,0},{10,2},{12,4},{14,6},{0,8},{2,10},{4,12},{6,14},{9,1},{11,3}... | collective-permute-start | bytes 811016 | tf_op jit(solution)/shard_map/ppermute | solution.py:600
  10.6 22.7 %collective-permute-start.3 = (bf16[528,256]{1,0:T(8,128)(2,1)S(1)}, bf16[528,256]{1,0:T(8,128)(2,1)S(1)}, u32[]{:S(2)}, u32[]{:S(2)}) collective-permute-start(bf16[528,256]{1,0:T(8,128)(2,1)S(1)} %pad_maximum_fusion.6), channel_id=1, source_target_pairs={{12,0},{14,2},{0,4},{2,6},{4,8},{6,10},{8,12},{10,14},{13,1},{15,3... | collective-permute-start | bytes 811016 | tf_op jit(solution)/shard_map/ppermute | solution.py:600
  17.6 34.9 %copy-start.10 = (bf16[528,256]{1,0:T(8,128)(2,1)}, bf16[528,256]{1,0:T(8,128)(2,1)S(1)}, u32[]{:S(2)}) copy-start(bf16[528,256]{1,0:T(8,128)(2,1)S(1)} %collective-permute-done.1) | copy-start | bytes 811012
  48.0 66.7 %all-to-all-start = ((bf16[4,528,512]{2,1,0:T(8,128)(2,1)}), bf16[4,528,512]{2,1,0:T(8,128)(2,1)S(1)}, u32[]{:S(2)}, u32[]{:S(2)}) async-start(bf16[4,528,512]{2,1,0:T(8,128)(2,1)} %bitcast.46), calls=%async_computation | async-start | bytes 4325376 | tf_op jit(solution)/shard_map/all_to_all | solution.py:658
  51.9 19.3 %copy-start.14 = (bf16[512,256]{1,0:T(8,128)(2,1)S(1)}, bf16[512,256]{1,0:T(8,128)(2,1)}, u32[]{:S(2)}) copy-start(bf16[512,256]{1,0:T(8,128)(2,1)} %get-tuple-element.110) | copy-start | bytes 786436
  51.9 13.0 %collective-permute-start.4 = (bf16[256,1024]{1,0:T(8,128)(2,1)}, bf16[256,1024]{1,0:T(8,128)(2,1)S(1)}, u32[]{:S(2)}, u32[]{:S(2)}) collective-permute-start(bf16[256,1024]{1,0:T(8,128)(2,1)} %pad_maximum_fusion.4), channel_id=1, source_target_pairs={{0,2},{2,0},{4,6},{6,4},{8,10},{10,8},{12,14},{14,12},{1,3},{3,1},... | collective-permute-start | bytes 1572872 | tf_op jit(solution)/shard_map/ppermute | solution.py:597
  52.6 19.9 %copy-start.8 = (bf16[1584,256]{1,0:T(8,128)(2,1)}, bf16[1584,256]{1,0:T(8,128)(2,1)S(1)}, u32[]{:S(2)}) copy-start(bf16[1584,256]{1,0:T(8,128)(2,1)S(1)} %constant_dynamic-update-slice_fusion.refs_1_) | copy-start | bytes 2433028
  52.6 18.7 %collective-permute-start.6 = (bf16[1584,256]{1,0:T(8,128)(2,1)S(1)}, bf16[1584,256]{1,0:T(8,128)(2,1)S(1)}, u32[]{:S(2)}, u32[]{:S(2)}) collective-permute-start(bf16[1584,256]{1,0:T(8,128)(2,1)S(1)} %constant_dynamic-update-slice_fusion.refs_1_), channel_id=1, source_target_pairs={{0,16},{16,0},{1,17},{17,1},{2,18},{18,2},{3,19},{19,3},{4,20},{20... | collective-permute-start | bytes 2433032 | tf_op jit(solution)/shard_map/ppermute | solution.py:594
  67.4 36.0 %collective-permute-start.5 = (bf16[2112,256]{1,0:T(8,128)(2,1)}, bf16[2112,256]{1,0:T(8,128)(2,1)}, u32[]{:S(2)}, u32[]{:S(2)}) collective-permute-start(bf16[2112,256]{1,0:T(8,128)(2,1)} %pad_maximum_fusion.2), channel_id=1, source_target_pairs={{0,2},{2,0},{4,6},{6,4},{8,10},{10,8},{12,14},{14,12},{1,3},{3,1},... | collective-permute-start | bytes 3244040 | tf_op jit(solution)/shard_map/ppermute | solution.py:597
  72.5 42.1 %collective-permute-start.7 = (bf16[2112,256]{1,0:T(8,128)(2,1)}, bf16[2112,256]{1,0:T(8,128)(2,1)}, u32[]{:S(2)}, u32[]{:S(2)}) collective-permute-start(bf16[2112,256]{1,0:T(8,128)(2,1)} %pad_maximum_fusion.3), channel_id=1, source_target_pairs={{0,2},{2,0},{4,6},{6,4},{8,10},{10,8},{12,14},{14,12},{1,3},{3,1},... | collective-permute-start | bytes 3244040 | tf_op jit(solution)/shard_map/ppermute | solution.py:597
  74.0 48.7 %copy-start.29 = (s32[3]{0:T(128)S(1)}, s32[3]{0:T(128)}, u32[]{:S(2)}) copy-start(s32[3]{0:T(128)} %param.27) | copy-start | bytes 40
  76.3 21.3 %collective-permute-start.8 = (bf16[256,1024]{1,0:T(8,128)(2,1)}, bf16[256,1024]{1,0:T(8,128)(2,1)S(1)}, u32[]{:S(2)}, u32[]{:S(2)}) collective-permute-start(bf16[256,1024]{1,0:T(8,128)(2,1)} %get-tuple-element.105), channel_id=1, source_target_pairs={{0,4},{2,6},{4,8},{6,10},{8,12},{10,14},{1,5},{3,7},{5,9},{7,11},{... | collective-permute-start | bytes 1572872 | tf_op jit(solution)/shard_map/ppermute | solution.py:604
  80.0 23.4 %collective-permute-start.9 = (bf16[256,1024]{1,0:T(8,128)(2,1)}, bf16[256,1024]{1,0:T(8,128)(2,1)S(1)}, u32[]{:S(2)}, u32[]{:S(2)}) collective-permute-start(bf16[256,1024]{1,0:T(8,128)(2,1)} %get-tuple-element.105), channel_id=1, source_target_pairs={{12,8},{14,10},{8,4},{10,6},{4,0},{6,2},{13,9},{15,11},{9,5},{11,7... | collective-permute-start | bytes 1572872 | tf_op jit(solution)/shard_map/ppermute | solution.py:604
  97.6 37.3 %copy-start.18 = (bf16[256,1024]{1,0:T(8,128)(2,1)}, bf16[256,1024]{1,0:T(8,128)(2,1)S(1)}, u32[]{:S(2)}) copy-start(bf16[256,1024]{1,0:T(8,128)(2,1)S(1)} %collective-permute-done.8) | copy-start | bytes 1572868
  103.4 31.5 %copy-start.20 = (bf16[256,1024]{1,0:T(8,128)(2,1)}, bf16[256,1024]{1,0:T(8,128)(2,1)S(1)}, u32[]{:S(2)}) copy-start(bf16[256,1024]{1,0:T(8,128)(2,1)S(1)} %collective-permute-done.9) | copy-start | bytes 1572868
  114.6 20.3 %collective-permute-start.11 = (bf16[256,1024]{1,0:T(8,128)(2,1)S(1)}, bf16[256,1024]{1,0:T(8,128)(2,1)}, u32[]{:S(2)}, u32[]{:S(2)}) collective-permute-start(bf16[256,1024]{1,0:T(8,128)(2,1)S(1)} %collective-permute-done.8), channel_id=1, source_target_pairs={{4,8},{6,10},{8,12},{10,14},{5,9},{7,11},{9,13},{11,15},{20,24},{2... | collective-permute-start | bytes 1572872 | tf_op jit(solution)/shard_map/ppermute | solution.py:604
  116.1 18.8 %collective-permute-start.12 = (bf16[256,1024]{1,0:T(8,128)(2,1)S(1)}, bf16[256,1024]{1,0:T(8,128)(2,1)}, u32[]{:S(2)}, u32[]{:S(2)}) collective-permute-start(bf16[256,1024]{1,0:T(8,128)(2,1)S(1)} %collective-permute-done.9), channel_id=1, source_target_pairs={{8,4},{10,6},{4,0},{6,2},{9,5},{11,7},{5,1},{7,3},{24,20},{26,22},... | collective-permute-start | bytes 1572872 | tf_op jit(solution)/shard_map/ppermute | solution.py:604
  122.1 6.4 %collective-permute-start.10 = (bf16[256,512]{1,0:T(8,128)(2,1)S(1)}, bf16[256,512]{1,0:T(8,128)(2,1)S(1)}, u32[]{:S(2)}, u32[]{:S(2)}) collective-permute-start(bf16[256,512]{1,0:T(8,128)(2,1)S(1)} %get-tuple-element.61), channel_id=1, source_target_pairs={{0,2},{2,0},{4,6},{6,4},{8,10},{10,8},{12,14},{14,12},{1,3},{3,1},... | collective-permute-start | bytes 786440 | tf_op jit(solution)/shard_map/ppermute | solution.py:597
  134.9 4.4 %collective-permute-start.13 = (f32[256,2048]{1,0:T(8,128)}, f32[256,2048]{1,0:T(8,128)S(1)}, u32[]{:S(2)}, u32[]{:S(2)}) collective-permute-start(f32[256,2048]{1,0:T(8,128)} %project_rows.1.mine_ref), channel_id=1, source_target_pairs={{0,1},{1,0},{2,3},{3,2},{4,5},{5,4},{6,7},{7,6},{8,9},{9,8},{10,11... | collective-permute-start | bytes 6291464 | tf_op jit(solution)/shard_map/ppermute | solution.py:687
  135.0 19.2 %collective-permute-start.16 = (bf16[256,1024]{1,0:T(8,128)(2,1)}, bf16[256,1024]{1,0:T(8,128)(2,1)}, u32[]{:S(2)}, u32[]{:S(2)}) collective-permute-start(bf16[256,1024]{1,0:T(8,128)(2,1)} %collective-permute-done.11), channel_id=1, source_target_pairs={{8,12},{10,14},{9,13},{11,15},{24,28},{26,30},{25,29},{27,31}} | collective-permute-start | bytes 1572872 | tf_op jit(solution)/shard_map/ppermute | solution.py:604
  136.5 19.1 %collective-permute-start.17 = (bf16[256,1024]{1,0:T(8,128)(2,1)}, bf16[256,1024]{1,0:T(8,128)(2,1)}, u32[]{:S(2)}, u32[]{:S(2)}) collective-permute-start(bf16[256,1024]{1,0:T(8,128)(2,1)} %collective-permute-done.12), channel_id=1, source_target_pairs={{4,0},{6,2},{5,1},{7,3},{20,16},{22,18},{21,17},{23,19}} | collective-permute-start | bytes 1572872 | tf_op jit(solution)/shard_map/ppermute | solution.py:604
  140.7 28.4 %copy-start.21 = (bf16[256,1024]{1,0:T(8,128)(2,1)S(1)}, bf16[256,1024]{1,0:T(8,128)(2,1)}, u32[]{:S(2)}) copy-start(bf16[256,1024]{1,0:T(8,128)(2,1)} %copy-done.20) | copy-start | bytes 1572868
  145.3 25.1 %copy-start.19 = (bf16[256,1024]{1,0:T(8,128)(2,1)S(1)}, bf16[256,1024]{1,0:T(8,128)(2,1)}, u32[]{:S(2)}) copy-start(bf16[256,1024]{1,0:T(8,128)(2,1)} %copy-done.18) | copy-start | bytes 1572868
  145.3 18.7 %collective-permute-start.14 = (bf16[256,1024]{1,0:T(8,128)(2,1)}, bf16[256,1024]{1,0:T(8,128)(2,1)S(1)}, u32[]{:S(2)}, u32[]{:S(2)}) collective-permute-start(bf16[256,1024]{1,0:T(8,128)(2,1)} %get-tuple-element.71.refs_0_), channel_id=1, source_target_pairs={{0,4},{2,6},{4,8},{6,10},{8,12},{10,14},{1,5},{3,7},{5,9},{7,11},{... | collective-permute-start | bytes 1572872 | tf_op jit(solution)/shard_map/ppermute | solution.py:604
  152.3 16.8 %collective-permute-start.15 = (bf16[256,1024]{1,0:T(8,128)(2,1)}, bf16[256,1024]{1,0:T(8,128)(2,1)S(1)}, u32[]{:S(2)}, u32[]{:S(2)}) collective-permute-start(bf16[256,1024]{1,0:T(8,128)(2,1)} %get-tuple-element.71.refs_0_), channel_id=1, source_target_pairs={{12,8},{14,10},{8,4},{10,6},{4,0},{6,2},{13,9},{15,11},{9,5},{11,7... | collective-permute-start | bytes 1572872 | tf_op jit(solution)/shard_map/ppermute | solution.py:604
  153.6 24.1 %collective-permute-start.22 = (bf16[256,1024]{1,0:T(8,128)(2,1)}, bf16[256,1024]{1,0:T(8,128)(2,1)}, u32[]{:S(2)}, u32[]{:S(2)}) collective-permute-start(bf16[256,1024]{1,0:T(8,128)(2,1)} %get-tuple-element.71.refs_0_), channel_id=1, source_target_pairs={{0,2},{2,0},{4,6},{6,4},{8,10},{10,8},{12,14},{14,12},{1,3},{3,1},... | collective-permute-start | bytes 1572872 | tf_op jit(solution)/shard_map/ppermute | solution.py:597
  171.7 19.9 %copy-start.3 = (bf16[768,1024]{1,0:T(8,128)(2,1)}, bf16[768,1024]{1,0:T(8,128)(2,1)S(1)}, u32[]{:S(2)}) copy-start(bf16[768,1024]{1,0:T(8,128)(2,1)S(1)} %pad_maximum_fusion.refs_12_.refs_6_.refs_4_) | copy-start | bytes 4718596
  171.7 35.8 %collective-permute-start.28 = (bf16[768,1024]{1,0:T(8,128)(2,1)S(1)}, bf16[768,1024]{1,0:T(8,128)(2,1)}, u32[]{:S(2)}, u32[]{:S(2)}) collective-permute-start(bf16[768,1024]{1,0:T(8,128)(2,1)S(1)} %pad_maximum_fusion.refs_12_.refs_6_.refs_4_), channel_id=1, source_target_pairs={{0,16},{16,0},{1,17},{17,1},{2,18},{18,2},{3,19},{19,3},{4,20},{20... | collective-permute-start | bytes 4718600 | tf_op jit(solution)/shard_map/ppermute | solution.py:594
  173.3 4.5 %collective-permute-start.18 = (bf16[256,1024]{1,0:T(8,128)(2,1)S(1)}, bf16[256,1024]{1,0:T(8,128)(2,1)S(1)}, u32[]{:S(2)}, u32[]{:S(2)}) collective-permute-start(bf16[256,1024]{1,0:T(8,128)(2,1)S(1)} %collective-permute-done.14), channel_id=1, source_target_pairs={{4,8},{6,10},{8,12},{10,14},{5,9},{7,11},{9,13},{11,15},{20,24},{2... | collective-permute-start | bytes 1572872 | tf_op jit(solution)/shard_map/ppermute | solution.py:604
  174.0 15.3 %collective-permute-start.19 = (bf16[256,1024]{1,0:T(8,128)(2,1)}, bf16[256,1024]{1,0:T(8,128)(2,1)S(1)}, u32[]{:S(2)}, u32[]{:S(2)}) collective-permute-start(bf16[256,1024]{1,0:T(8,128)(2,1)} %copy-done.22), channel_id=1, source_target_pairs={{8,4},{10,6},{4,0},{6,2},{9,5},{11,7},{5,1},{7,3},{24,20},{26,22},... | collective-permute-start | bytes 1572872 | tf_op jit(solution)/shard_map/ppermute | solution.py:604
  177.3 13.2 %collective-permute-start.23 = (bf16[256,1024]{1,0:T(8,128)(2,1)}, bf16[256,1024]{1,0:T(8,128)(2,1)}, u32[]{:S(2)}, u32[]{:S(2)}) collective-permute-start(bf16[256,1024]{1,0:T(8,128)(2,1)} %broadcast_select_fusion.3.refs_2_), channel_id=1, source_target_pairs={{0,2},{2,0},{4,6},{6,4},{8,10},{10,8},{12,14},{14,12},{1,3},{3,1},... | collective-permute-start | bytes 1572872 | tf_op jit(solution)/shard_map/ppermute | solution.py:597
  177.8 12.9 %collective-permute-start.25 = (bf16[256,1024]{1,0:T(8,128)(2,1)}, bf16[256,1024]{1,0:T(8,128)(2,1)}, u32[]{:S(2)}, u32[]{:S(2)}) collective-permute-start(bf16[256,1024]{1,0:T(8,128)(2,1)} %broadcast_select_fusion.3.refs_2_), channel_id=1, source_target_pairs={{0,1},{1,0},{2,3},{3,2},{4,5},{5,4},{6,7},{7,6},{8,9},{9,8},{10,11... | collective-permute-start | bytes 1572872 | tf_op jit(solution)/shard_map/ppermute | solution.py:702
  177.8 14.8 %collective-permute-start.24 = (bf16[256,1024]{1,0:T(8,128)(2,1)}, bf16[256,1024]{1,0:T(8,128)(2,1)S(1)}, u32[]{:S(2)}, u32[]{:S(2)}) collective-permute-start(bf16[256,1024]{1,0:T(8,128)(2,1)} %collective-permute-done.22.refs_1_), channel_id=1, source_target_pairs={{0,1},{1,0},{2,3},{3,2},{4,5},{5,4},{6,7},{7,6},{8,9},{9,8},{10,11... | collective-permute-start | bytes 1572872 | tf_op jit(solution)/shard_map/ppermute | solution.py:702
  190.2 5.4 %collective-permute-start.27 = (bf16[256,1024]{1,0:T(8,128)(2,1)}, bf16[256,1024]{1,0:T(8,128)(2,1)}, u32[]{:S(2)}, u32[]{:S(2)}) collective-permute-start(bf16[256,1024]{1,0:T(8,128)(2,1)} %fusion.1.refs_4_), channel_id=1, source_target_pairs={{0,1},{1,0},{2,3},{3,2},{4,5},{5,4},{6,7},{7,6},{8,9},{9,8},{10,11... | collective-permute-start | bytes 1572872 | tf_op jit(solution)/shard_map/ppermute | solution.py:702
  190.4 6.0 %collective-permute-start.26 = (bf16[256,1024]{1,0:T(8,128)(2,1)}, bf16[256,1024]{1,0:T(8,128)(2,1)}, u32[]{:S(2)}, u32[]{:S(2)}) collective-permute-start(bf16[256,1024]{1,0:T(8,128)(2,1)} %collective-permute-done.23.refs_3_), channel_id=1, source_target_pairs={{0,1},{1,0},{2,3},{3,2},{4,5},{5,4},{6,7},{7,6},{8,9},{9,8},{10,11... | collective-permute-start | bytes 1572872 | tf_op jit(solution)/shard_map/ppermute | solution.py:702
  190.7 15.1 %collective-permute-start.31 = (bf16[256,1024]{1,0:T(8,128)(2,1)}, bf16[256,1024]{1,0:T(8,128)(2,1)}, u32[]{:S(2)}, u32[]{:S(2)}) collective-permute-start(bf16[256,1024]{1,0:T(8,128)(2,1)} %fusion.1.refs_4_), channel_id=1, source_target_pairs={{0,2},{2,0},{4,6},{6,4},{8,10},{10,8},{12,14},{14,12},{1,3},{3,1},... | collective-permute-start | bytes 1572872 | tf_op jit(solution)/shard_map/ppermute | solution.py:597
  193.4 25.9 %collective-permute-start.29 = (bf16[512,512]{1,0:T(8,128)(2,1)S(1)}, bf16[512,512]{1,0:T(8,128)(2,1)}, u32[]{:S(2)}, u32[]{:S(2)}) collective-permute-start(bf16[512,512]{1,0:T(8,128)(2,1)S(1)} %get-tuple-element.103), channel_id=1, source_target_pairs={{0,2},{2,0},{4,6},{6,4},{8,10},{10,8},{12,14},{14,12},{1,3},{3,1},... | collective-permute-start | bytes 1572872 | tf_op jit(solution)/shard_map/ppermute | solution.py:597
  195.5 29.7 %collective-permute-start.20 = (bf16[256,1024]{1,0:T(8,128)(2,1)S(1)}, bf16[256,1024]{1,0:T(8,128)(2,1)S(1)}, u32[]{:S(2)}, u32[]{:S(2)}) collective-permute-start(bf16[256,1024]{1,0:T(8,128)(2,1)S(1)} %collective-permute-done.18), channel_id=1, source_target_pairs={{8,12},{10,14},{9,13},{11,15},{24,28},{26,30},{25,29},{27,31}} | collective-permute-start | bytes 1572872 | tf_op jit(solution)/shard_map/ppermute | solution.py:604
  196.4 28.9 %collective-permute-start.21 = (bf16[256,1024]{1,0:T(8,128)(2,1)S(1)}, bf16[256,1024]{1,0:T(8,128)(2,1)S(1)}, u32[]{:S(2)}, u32[]{:S(2)}) collective-permute-start(bf16[256,1024]{1,0:T(8,128)(2,1)S(1)} %collective-permute-done.19), channel_id=1, source_target_pairs={{4,0},{6,2},{5,1},{7,3},{20,16},{22,18},{21,17},{23,19}} | collective-permute-start | bytes 1572872 | tf_op jit(solution)/shard_map/ppermute | solution.py:604
  205.7 20.2 %collective-permute-start.32 = (bf16[256,1024]{1,0:T(8,128)(2,1)}, bf16[256,1024]{1,0:T(8,128)(2,1)S(1)}, u32[]{:S(2)}, u32[]{:S(2)}) collective-permute-start(bf16[256,1024]{1,0:T(8,128)(2,1)} %collective-permute-done.31.refs_0_), channel_id=1, source_target_pairs={{0,1},{1,0},{2,3},{3,2},{4,5},{5,4},{6,7},{7,6},{8,9},{9,8},{10,11... | collective-permute-start | bytes 1572872 | tf_op jit(solution)/shard_map/ppermute | solution.py:702
  225.4 2.0 collective-permute-start.33
  225.5 14.3 %collective-permute-start.30 = (bf16[256,1024]{1,0:T(8,128)(2,1)S(1)}, bf16[256,1024]{1,0:T(8,128)(2,1)S(1)}, u32[]{:S(2)}, u32[]{:S(2)}) collective-permute-start(bf16[256,1024]{1,0:T(8,128)(2,1)S(1)} %select_select_fusion.1.refs_1_), channel_id=1, source_target_pairs={{0,2},{2,0},{4,6},{6,4},{8,10},{10,8},{12,14},{14,12},{1,3},{3,1},... | collective-permute-start | bytes 1572872 | tf_op jit(solution)/shard_map/ppermute | solution.py:597
  239.8 1.9 collective-permute-start.34
  257.4 14.2 %collective-permute-start.35 = (bf16[512,512]{1,0:T(8,128)(2,1)}, bf16[512,512]{1,0:T(8,128)(2,1)S(1)}, u32[]{:S(2)}, u32[]{:S(2)}) collective-permute-start(bf16[512,512]{1,0:T(8,128)(2,1)} %decode_rows.5), channel_id=1, source_target_pairs={{0,2},{2,0},{4,6},{6,4},{8,10},{10,8},{12,14},{14,12},{1,3},{3,1},... | collective-permute-start | bytes 1572872 | tf_op jit(solution)/shard_map/ppermute | solution.py:755
  (22 other events, 115.5 us)

commit v9 on v7

--- a/solution.py
+++ b/solution.py
@@ -263,7 +263,7 @@
         encode_kernel,
         grid_spec=grid_spec,
         out_shape=jax.ShapeDtypeStruct((blocks * (rows + EXTRA), width), jnp.bfloat16),
-        compiler_params=params(32),
+        compiler_params=params(BIG),
         cost_estimate=cost(
             16 * blocks * rows * tokens * width, 8 * tokens * width, blocks * rows * tokens * 8
         ),
@@ -425,8 +425,10 @@
             pl.when(is_mine)(functools.partial(copy, mine))
             pl.when(jnp.logical_not(is_mine))(functools.partial(copy, theirs))
 
-    for j, band in enumerate(w_refs):
-        w_ref[j * depth : (j + 1) * depth, :] = band[...]
+    start = 0
+    for band in w_refs:
+        w_ref[start : start + band.shape[0], :] = band[...]
+        start += band.shape[0]
     out_ref[...] = jnp.dot(
         normed_ref[...], w_ref[...], preferred_element_type=jnp.float32
     ).astype(jnp.bfloat16)
@@ -435,14 +437,14 @@
 def latent_keys_values(ids, mine, theirs, bands):
     pieces = len(mine)
     rows, half = mine[0].shape
-    depth, width = bands[0].shape
+    width = bands[0].shape[1]
     block = min(512, width)
-    total = depth * len(bands)
+    total = sum(band.shape[0] for band in bands)
     grid_spec = pltpu.PrefetchScalarGridSpec(
         num_scalar_prefetch=1,
         grid=(width // block,),
         in_specs=[whole((rows, half))] * (2 * pieces)
-        + [pl.BlockSpec((depth, block), lambda i, ids: (0, i))] * len(bands),
+        + [pl.BlockSpec((band.shape[0], block), lambda i, ids: (0, i)) for band in bands],
         out_specs=pl.BlockSpec((rows * pieces, block), lambda i, ids: (0, i)),
         scratch_shapes=[
             pltpu.VMEM((rows * pieces, total), jnp.bfloat16),
@@ -629,10 +631,12 @@
     parts = encode(
         y, latent_queries, enc_keys, enc_values, extra, near_inputs, head_bias, 2 * rows
     )
-    kv_near, out_sent, _ = lax.optimization_barrier((kv_near, out_sent, parts))
+    kv_near, out_sent, parts = lax.optimization_barrier((kv_near, out_sent, parts))
     kv_sent = jnp.where(x == 0, kv_own, kv_near)
     hops = {0: [kv_sent, kv_sent]}
     hops[1] = hop(1, hops[0])
+    early = [k for k in range(1, far) if max(k, far - k) < 3]
+    rest = [k for k in range(1, far) if k not in early]
     out_near = over_near(jnp.concatenate([out_sent, out_far]))
     out_near_other = over_near(jnp.concatenate([half_of_out(1 - x), out_far_other]))
     columns_of_slice = [[2 * i + j for i in range(far)] for j in range(2)]
@@ -651,33 +655,36 @@
         limits = jnp.sum(q_onehot * query_counts[None, :], axis=1)
         return ranked < limits
 
-    parts, out_near, out_far_other, out_near_other, hops = lax.optimization_barrier(
-        (parts, out_near, out_far_other, out_near_other, hops)
-    )
-    hops[2] = hop(2, hops[1])
-    attended, for_near = merge(y, parts, far)
-    from_near = over_near(for_near)
-    kept = kept_queries()
-    from_near, hops, kept = lax.optimization_barrier((from_near, hops, kept))
-    for step in range(3, far):
-        hops[step] = hop(step, hops[step - 1])
-    out_ids = jnp.stack([*places, y, x]).astype(jnp.int32)
-    weights = [w_out, out_far, out_far_other, out_near, out_near_other]
-    partial_value = project(out_ids, attended, from_near, weights)
-    theirs = lax.ppermute(partial_value, "head", swap_perm(2))
-    theirs, hops = lax.optimization_barrier((theirs, hops))
-    own_cols, normed, normed_other = normalise(
-        place, partial_value, theirs, latent_array, norm_gain[None, :]
-    )
     lookup = jnp.dot(q_onehot.astype(jnp.bfloat16), query_table, preferred_element_type=jnp.float32)
     queries = (query_features.astype(jnp.float32) + lookup).astype(jnp.bfloat16)
     own_queries = columns((queries,), y)
     near_queries = over_near(columns((queries,), 1 - y))
 
+    parts, out_near, out_far_other, out_near_other, hops, near_queries = lax.optimization_barrier(
+        (parts, out_near, out_far_other, out_near_other, hops, near_queries)
+    )
+    attended, for_near = merge(y, parts, far)
+    for_near, hops = lax.optimization_barrier((for_near, hops))
+    hops[2] = hop(2, hops[1])
+    from_near = over_near(for_near)
+    kept = kept_queries()
+    out_ids = jnp.stack([*places, y, x]).astype(jnp.int32)
+    weights = [w_out, out_far, out_far_other, out_near, out_near_other]
+    partial_value = project(out_ids, attended, from_near, weights)
+    partial_value, hops = lax.optimization_barrier((partial_value, hops))
+    kv_bands = [kv_own, kv_near]
+    for k in early:
+        kv_moved = by_shift(hops, k)
+        kv_bands += [kv_moved, over_groups(kv_moved)]
+    for step in range(3, far):
+        hops[step] = hop(step, hops[step - 1])
+    theirs = lax.ppermute(partial_value, "head", swap_perm(2))
+    own_cols, normed, normed_other = normalise(
+        place, partial_value, theirs, latent_array, norm_gain[None, :]
+    )
     kv_at = [p, p ^ 1]
-    for k in range(1, far):
-        there = ((z + k) % far) * 2
-        kv_at += [there + (y ^ x), there + (1 - (y ^ x))]
+    for k in early + rest:
+        kv_at += [((z + k) % far) * 2 + (y ^ other) for other in (x, 1 - x)]
     kv_ids = jnp.stack([place, *kv_at]).astype(jnp.int32)
 
     def cores(values):
@@ -702,32 +709,28 @@
 
     came = {0: [normed, normed]}
     came[1] = hop(1, came[0])
-    moved = {k: by_shift(hops, k) for k in range(1, far)}
-    swapped = {k: over_groups(v) for k, v in moved.items()}
-    came, normed_near, moved = lax.optimization_barrier((came, over_near(normed), moved))
-    mine, other = [normed, normed_near], [normed_other, *cores([normed_near])]
-    keys_values = []
+    normed_near = over_near(normed)
+    came, hops, kv_bands, kept = lax.optimization_barrier((came, hops, kv_bands, kept))
+    mine, other = [normed, normed_near], [normed_other]
     for step in range(1, far):
         fresh = arrival(came, step)
+        fresh_near = over_near(fresh)
         if step + 1 < far:
             came[step + 1] = hop(step + 1, came[step])
-        fresh_near = over_near(fresh)
-        mine.append(fresh)
-        other += cores([fresh])
-        if step > 1:
-            keys_values.append(fold(mine, other))
-            mine, other = [], []
-        came, fresh_near, mine, other, keys_values, swapped, near_queries = (
-            lax.optimization_barrier(
-                (came, fresh_near, mine, other, keys_values, swapped, near_queries)
+            k = rest[step - 1]
+            kv_moved = by_shift(hops, k)
+            kv_bands += [kv_moved, over_groups(kv_moved)]
+            came, mine, kv_bands, fresh, fresh_near = lax.optimization_barrier(
+                (came, mine, kv_bands, fresh, fresh_near)
             )
-        )
-        kv_bands = [kv_own, kv_near]
-        for k in range(1, far):
-            kv_bands += [moved[k], swapped[k]]
-        mine.append(fresh_near)
-        other += cores([fresh_near])
-    keys_values.append(fold(mine, other))
+            other += cores(mine[-1:] + [fresh])
+            mine += [fresh, fresh_near]
+    mine, other, fresh = lax.optimization_barrier((mine, other, fresh))
+    keys_values = [fold(mine[:-1], other)]
+    last = [mine[-1], fresh]
+    keys_values.append(fold(last, cores(last)))
+    fresh_near, keys_values = lax.optimization_barrier((fresh_near, keys_values))
+    keys_values.append(fold([fresh_near], cores([fresh_near])))
     near_state = decode(near_queries, keys_values, jnp.bfloat16)
     own_state = decode(own_queries, keys_values, jnp.float32)
     from_near = lax.ppermute(near_state, "pos", near).astype(jnp.float32)
@@ -746,7 +749,7 @@
     fits = (
         head == 2
         and pos % 2 == 0
-        and pos > 2
+        and pos > 4
         and groups % 2 == 0
         and enc_keys.shape[1] % (4 * HEAD_DIM) == 0
         and 3 * enc_keys.shape[1] <= 2 * HEAD_DIM * EXTRA

time: 274 us -> 266 us (0.971)
  waiting for transfers between devices: 126 us -> 111 us
  starting transfers between devices: 42.8 us -> 55.7 us
  local copies, waits for them, and re-layouts: 18.6 us -> 14.7 us
    ppermute x12, waiting for transfers between devices: 49.6 us -> 18.8 us  [hop(): lax.ppermute(v, 'pos', hop_perm(pos, step, way))]
    ppermute x10, waiting for transfers between devices: 25.8 us -> 51 us  [over_near(): return lax.ppermute(value, 'pos', near)]
    ppermute x12, starting transfers between devices: 16.7 us -> 22.7 us  [hop(): lax.ppermute(v, 'pos', hop_perm(pos, step, way))]
    ppermute x10, starting transfers between devices: 9.64 us -> 15.1 us  [over_near(): return lax.ppermute(value, 'pos', near)]
    ppermute x4, waiting for transfers between devices: 22.8 us -> 18.2 us  [over_groups(): return lax.ppermute(value, 'groups', swap_perm(groups))]
    ppermute x3, waiting for transfers between devices: 18.8 us -> 14.4 us  [over_far(): return lax.ppermute(value, 'pos', shift_perm(pos, k))]
    unnamed x66 -> x78, local copies, waits for them, and re-layouts: 9.25 us -> 7.01 us
  transfers between devices with their start and end apart: 39 -> 39, of which waited for: 21 -> 17; matrix products, arithmetic and copies ran while one was open for 9% -> 8% of each run, Pallas kernels for 12% -> 20%
where the time goes in v9:
time: 266 us; the launch traced here: 265 us
  waiting for transfers between devices  111 us (42%)
  Pallas kernels  67.6 us (25%)
  starting transfers between devices  55.7 us (21%)
  local copies, waits for them, and re-layouts  14.7 us (6%)
  other arithmetic  14.5 us (5%)
    ppermute x10, waiting for transfers between devices, over_near(): return lax.ppermute(value, 'pos', near)  51 us
    pallas_call x3, Pallas kernels, latent_keys_values(): pl.pallas_call(functools.partial(latents_kernel, pieces), grid_spec=grid_...  24.3 us
    ppermute x12, starting transfers between devices, hop(): lax.ppermute(v, 'pos', hop_perm(pos, step, way))  22.7 us
    ppermute x12, waiting for transfers between devices, hop(): lax.ppermute(v, 'pos', hop_perm(pos, step, way))  18.8 us
    ppermute x4, waiting for transfers between devices, over_groups(): return lax.ppermute(value, 'groups', swap_perm(groups))  18.2 us
    pallas_call x2, Pallas kernels, decode(): pl.pallas_call(functools.partial(decode_kernel, len(keys_values)), grid=(...  16.8 us
    ppermute x10, starting transfers between devices, over_near(): return lax.ppermute(value, 'pos', near)  15.1 us
    pallas_call x1, Pallas kernels, encode(): pl.pallas_call(encode_kernel, grid_spec=grid_spec, out_shape=jax.ShapeDty...  14.4 us
  transfers between devices with their start and end apart: 39, of which 17 were waited for; matrix products, arithmetic and copies ran while one was open for 8% of the time, Pallas kernels for 20%

profile of v9, /device:TPU:0, one launch (start us, length us, event | category | flops | bytes accessed | tf_op | source)
XLA Modules:
  0.0 265.2 jit_solution(6089644683281998392)
XLA Ops:
  1.4 1.3 constant_dynamic-slice_fusion.9
  2.9 3.0 %collective-permute-start = (bf16[528,1024]{1,0:T(8,128)(2,1)S(1)}, bf16[528,1024]{1,0:T(8,128)(2,1)}, u32[]{:S(2)}, u32[]{:S(2)}) collective-permute-start(bf16[528,1024]{1,0:T(8,128)(2,1)S(1)} %pad_maximum_fusion), channel_id=1, source_target_pairs={{0,2},{2,0},{4,6},{6,4},{8,10},{10,8},{12,14},{14,12},{1,3},{3,1},... | collective-permute-start | bytes 3244040 | tf_op jit(solution)/shard_map/ppermute | solution.py:580
  7.0 1.6 collective-permute-start.3
  8.6 2.6 collective-permute-start.2
  11.2 1.3 collective-permute-start.1
  14.2 4.2 %collective-permute-done.3 = bf16[528,256]{1,0:T(8,128)(2,1)S(1)} collective-permute-done((bf16[528,256]{1,0:T(8,128)(2,1)S(1)}, bf16[528,256]{1,0:T(8,128)(2,1)S(1)}, u32[]{:S(2)}, u32[]{:S(2)}) %collective-permute-start.3) | collective-permute-done | bytes 270368 | tf_op jit(solution)/shard_map/ppermute | solution.py:583
  18.4 10.2 %collective-permute-done.2 = bf16[528,256]{1,0:T(8,128)(2,1)S(1)} collective-permute-done((bf16[528,256]{1,0:T(8,128)(2,1)S(1)}, bf16[528,256]{1,0:T(8,128)(2,1)S(1)}, u32[]{:S(2)}, u32[]{:S(2)}) %collective-permute-start.2) | collective-permute-done | bytes 270368 | tf_op jit(solution)/shard_map/ppermute | solution.py:583
  28.6 1.4 collective-permute-done.near_ref
  29.9 1.7 collective-permute-start.4
  31.7 14.4 %encode_rows.1 = bf16[2112,512]{1,0:T(8,128)(2,1)} custom-call(s32[1]{0:T(128)} %bitcast.9.ids_ref, bf16[2048,1024]{1,0:T(8,128)(2,1)} %q_ref.1, bf16[512,1024]{1,0:T(8,128)(2,1)} %k_ref.1, bf16[512,1024]{1,0:T(8,128)(2,1)} %v_ref.1, bf16[16,1024]{1,0:T(8,128)(2,1)} %copy-done.27, bf16[528,1024]{1,0:T(8,128)(2,1)} %collective-permute-done.near_ref, ...), custom_call_target="tpu_custom_call" | custom-call | flops 8589934592 | bytes 2097152 | tf_op jit(solution)/shard_map/encode_rows/pallas_call | solution.py:262
  46.1 6.0 %all-to-all-start = ((bf16[4,528,512]{2,1,0:T(8,128)(2,1)}), bf16[4,528,512]{2,1,0:T(8,128)(2,1)S(1)}, u32[]{:S(2)}, u32[]{:S(2)}) async-start(bf16[4,528,512]{2,1,0:T(8,128)(2,1)} %bitcast.46), calls=%async_computation | async-start | bytes 4325376 | tf_op jit(solution)/shard_map/all_to_all | solution.py:643
  53.2 1.6 collective-permute-start.6
  54.8 2.0 pad_maximum_fusion.1
  56.8 1.5 collective-permute-start.5
  58.3 13.3 %collective-permute-done.6.refs_2_ = bf16[1584,256]{1,0:T(8,128)(2,1)S(1)} collective-permute-done((bf16[1584,256]{1,0:T(8,128)(2,1)S(1)}, bf16[1584,256]{1,0:T(8,128)(2,1)S(1)}, u32[]{:S(2)}, u32[]{:S(2)}) %collective-permute-start.6) | collective-permute-done | bytes 811040 | tf_op jit(solution)/shard_map/ppermute | solution.py:577
  72.8 1.5 collective-permute-start.7
  78.7 5.2 %collective-permute-start.8 = (bf16[256,1024]{1,0:T(8,128)(2,1)S(1)}, bf16[256,1024]{1,0:T(8,128)(2,1)S(1)}, u32[]{:S(2)}, u32[]{:S(2)}) collective-permute-start(bf16[256,1024]{1,0:T(8,128)(2,1)S(1)} %get-tuple-element.179), channel_id=1, source_target_pairs={{0,4},{2,6},{4,8},{6,10},{8,12},{10,14},{1,5},{3,7},{5,9},{7,11},{... | collective-permute-start | bytes 1572872 | tf_op jit(solution)/shard_map/ppermute | solution.py:587
  83.9 31.4 %collective-permute-done.10.q_ref = bf16[512,512]{1,0:T(8,128)(2,1)} collective-permute-done((bf16[512,512]{1,0:T(8,128)(2,1)}, bf16[512,512]{1,0:T(8,128)(2,1)}, u32[]{:S(2)}, u32[]{:S(2)}) %collective-permute-start.10) | collective-permute-done | bytes 524320 | tf_op jit(solution)/shard_map/ppermute | solution.py:580
  115.4 1.9 merge_rows.1
  118.0 1.5 collective-permute-start.12
  120.8 1.6 collective-permute-start.11
  123.0 4.2 %collective-permute-done.11.near_ref = bf16[256,512]{1,0:T(8,128)(2,1)S(1)} collective-permute-done((bf16[256,512]{1,0:T(8,128)(2,1)S(1)}, bf16[256,512]{1,0:T(8,128)(2,1)S(1)}, u32[]{:S(2)}, u32[]{:S(2)}) %collective-permute-start.11) | collective-permute-done | bytes 262176 | tf_op jit(solution)/shard_map/ppermute | solution.py:580
  127.9 5.7 %project_rows.1.mine_ref = f32[256,2048]{1,0:T(8,128)} custom-call(s32[10]{0:T(128)} %stack.82.ids_ref, bf16[256,512]{1,0:T(8,128)(2,1)} %copy-done.1, bf16[256,512]{1,0:T(8,128)(2,1)} %copy-done.26, bf16[1024,256]{1,0:T(8,128)(2,1)} %refs_0_.1, bf16[1584,256]{1,0:T(8,128)(2,1)} %copy-done.9, bf16[1584,256]{1,0:T(8,128)(2,1)} %copy-done.2, ...), custom_call_target="tpu_custom_call" | custom-call | flops 1073741824 | bytes 6291456 | tf_op jit(solution)/shard_map/project_rows/pallas_call | solution.py:357
  137.0 1.3 collective-permute-start.18
  140.6 1.3 copy-done.7
  141.9 4.6 %norm_rows.1 = (f32[256,1024]{1,0:T(8,128)}, bf16[256,1024]{1,0:T(8,128)(2,1)}, bf16[256,1024]{1,0:T(8,128)(2,1)}) custom-call(s32[1]{0:T(128)} %bitcast.ids_ref, f32[256,2048]{1,0:T(8,128)} %project_rows.1.mine_ref, f32[256,2048]{1,0:T(8,128)} %copy-done.7, bf16[256,2048]{1,0:T(8,128)(2,1)} %latent_ref.1, f32[1,2048]{1,0:T(1,128)} %bitcast.49), custom_call_target="tpu_custom_call" | custom-call | flops 3145728 | bytes 6815744 | tf_op jit(solution)/shard_map/norm_rows/pallas_call | solution.py:391
  147.8 6.3 %collective-permute-start.15 = (bf16[256,1024]{1,0:T(8,128)(2,1)}, bf16[256,1024]{1,0:T(8,128)(2,1)S(1)}, u32[]{:S(2)}, u32[]{:S(2)}) collective-permute-start(bf16[256,1024]{1,0:T(8,128)(2,1)} %get-tuple-element.150.refs_0_), channel_id=1, source_target_pairs={{0,4},{2,6},{4,8},{6,10},{8,12},{10,14},{1,5},{3,7},{5,9},{7,11},{... | collective-permute-start | bytes 1572872 | tf_op jit(solution)/shard_map/ppermute | solution.py:587
  155.7 1.6 collective-permute-start.22
  157.3 9.1 %collective-permute-done.16 = bf16[256,1024]{1,0:T(8,128)(2,1)} collective-permute-done((bf16[256,1024]{1,0:T(8,128)(2,1)}, bf16[256,1024]{1,0:T(8,128)(2,1)}, u32[]{:S(2)}, u32[]{:S(2)}) %collective-permute-start.16) | collective-permute-done | bytes 524320 | tf_op jit(solution)/shard_map/ppermute | solution.py:587
  166.4 1.9 broadcast_select_fusion.2.refs_2_
  168.3 1.5 collective-permute-start.24
  172.5 1.3 collective-permute-start.21
  176.3 6.1 %collective-permute-done.24.refs_3_ = bf16[256,1024]{1,0:T(8,128)(2,1)} collective-permute-done((bf16[256,1024]{1,0:T(8,128)(2,1)}, bf16[256,1024]{1,0:T(8,128)(2,1)}, u32[]{:S(2)}, u32[]{:S(2)}) %collective-permute-start.24) | collective-permute-done | bytes 524320 | tf_op jit(solution)/shard_map/ppermute | solution.py:580
  182.3 3.5 %collective-permute-done.23.refs_15_.refs_9_.refs_7_ = bf16[256,1024]{1,0:T(8,128)(2,1)S(1)} collective-permute-done((bf16[256,1024]{1,0:T(8,128)(2,1)S(1)}, bf16[256,1024]{1,0:T(8,128)(2,1)S(1)}, u32[]{:S(2)}, u32[]{:S(2)}) %collective-permute-start.23) | collective-permute-done | bytes 524320 | tf_op jit(solution)/shard_map/ppermute | solution.py:577
  185.9 5.8 %collective-permute-done.21 = bf16[256,1024]{1,0:T(8,128)(2,1)S(1)} collective-permute-done((bf16[256,1024]{1,0:T(8,128)(2,1)}, bf16[256,1024]{1,0:T(8,128)(2,1)S(1)}, u32[]{:S(2)}, u32[]{:S(2)}) %collective-permute-start.21) | collective-permute-done | bytes 524320 | tf_op jit(solution)/shard_map/ppermute | solution.py:587
  194.4 1.3 collective-permute-done.27.refs_17_.refs_11_.refs_9_
  195.7 7.9 %collective-permute-done.28.refs_0_ = bf16[256,1024]{1,0:T(8,128)(2,1)} collective-permute-done((bf16[256,1024]{1,0:T(8,128)(2,1)S(1)}, bf16[256,1024]{1,0:T(8,128)(2,1)}, u32[]{:S(2)}, u32[]{:S(2)}) %collective-permute-start.28) | collective-permute-done | bytes 524320 | tf_op jit(solution)/shard_map/ppermute | solution.py:580
  203.6 2.7 %collective-permute-done.26 = bf16[256,1024]{1,0:T(8,128)(2,1)S(1)} collective-permute-done((bf16[256,1024]{1,0:T(8,128)(2,1)S(1)}, bf16[256,1024]{1,0:T(8,128)(2,1)S(1)}, u32[]{:S(2)}, u32[]{:S(2)}) %collective-permute-start.26) | collective-permute-done | bytes 524320 | tf_op jit(solution)/shard_map/ppermute | solution.py:587
  207.7 1.4 collective-permute-done.32.refs_8_
  210.8 1.5 collective-permute-start.29
  212.4 12.1 %latent_keys_values.3.refs_0_.refs_3_ = bf16[1280,1024]{1,0:T(8,128)(2,1)} custom-call(s32[9]{0:T(128)} %stack.92.ids_ref, bf16[256,1024]{1,0:T(8,128)(2,1)} %get-tuple-element.150.refs_0_, bf16[256,1024]{1,0:T(8,128)(2,1)} %collective-permute-done.22.refs_1_, bf16[256,1024]{1,0:T(8,128)(2,1)} %broadcast_select_fusion.2.refs_2_, ...), custom_call_target="tpu_custom_call" | custom-call | flops 5368709120 | bytes 4194304 | tf_op jit(solution)/shard_map/latent_keys_values/pallas_call | solution.py:454
  226.1 6.9 %latent_keys_values.4.refs_1_.refs_4_ = bf16[512,1024]{1,0:T(8,128)(2,1)} custom-call(s32[9]{0:T(128)} %stack.92.ids_ref, bf16[256,1024]{1,0:T(8,128)(2,1)} %collective-permute-done.28.refs_0_, bf16[256,1024]{1,0:T(8,128)(2,1)} %select_select_fusion.1.refs_1_, bf16[256,1024]{1,0:T(8,128)(2,1)} %copy-done.35, bf16[256,1024]{1,0:T(8,128)(2,1)} %copy-done.36, ...), custom_call_target="tpu_custom_call" | custom-call | flops 2147483648 | bytes 4194304 | tf_op jit(solution)/shard_map/latent_keys_values/pallas_call | solution.py:454
  233.1 1.9 collective-permute-done.36.refs_1_
  235.7 5.3 %latent_keys_values.5.refs_2_.refs_5_ = bf16[256,1024]{1,0:T(8,128)(2,1)} custom-call(s32[9]{0:T(128)} %stack.92.ids_ref, bf16[256,1024]{1,0:T(8,128)(2,1)} %copy-done.19, bf16[256,1024]{1,0:T(8,128)(2,1)} %copy-done.20, bf16[256,1024]{1,0:T(8,128)(2,1)} %get-tuple-element.160.refs_10_.refs_4_.refs_2_, bf16[256,1024]{1,0:T(8,128)(2,1)} %copy-done.3, ...), custom_call_target="tpu_custom_call" | custom-call | flops 1073741824 | bytes 4194304 | tf_op jit(solution)/shard_map/latent_keys_values/pallas_call | solution.py:454
  241.0 8.3 %decode_rows.3 = bf16[512,512]{1,0:T(8,128)(2,1)} custom-call(bf16[512,512]{1,0:T(8,128)(2,1)} %collective-permute-done.10.q_ref, bf16[1280,1024]{1,0:T(8,128)(2,1)} %latent_keys_values.3.refs_0_.refs_3_, bf16[512,1024]{1,0:T(8,128)(2,1)} %latent_keys_values.4.refs_1_.refs_4_, bf16[256,1024]{1,0:T(8,128)(2,1)} %latent_keys_values.5.refs_2_.refs_5_, ...), custom_call_target="tpu_custom_call" | custom-call | flops 8589934592 | bytes 5767168 | tf_op jit(solution)/shard_map/decode_rows/pallas_call | solution.py:515
  249.7 8.4 %decode_rows.2 = f32[512,512]{1,0:T(8,128)} custom-call(bf16[512,512]{1,0:T(8,128)(2,1)} %get-tuple-element.176.q_ref, bf16[1280,1024]{1,0:T(8,128)(2,1)} %latent_keys_values.3.refs_0_.refs_3_, bf16[512,1024]{1,0:T(8,128)(2,1)} %latent_keys_values.4.refs_1_.refs_4_, bf16[256,1024]{1,0:T(8,128)(2,1)} %latent_keys_values.5.refs_2_.refs_5_, ...), custom_call_target="tpu_custom_call" | custom-call | flops 8589934592 | bytes 5767168 | tf_op jit(solution)/shard_map/decode_rows/pallas_call | solution.py:515
  258.1 5.4 %collective-permute-done.37 = bf16[512,512]{1,0:T(8,128)(2,1)S(1)} collective-permute-done((bf16[512,512]{1,0:T(8,128)(2,1)}, bf16[512,512]{1,0:T(8,128)(2,1)S(1)}, u32[]{:S(2)}, u32[]{:S(2)}) %collective-permute-start.37) | collective-permute-done | bytes 524320 | tf_op jit(solution)/shard_map/ppermute | solution.py:736
  263.7 1.6 fusion
  (160 shorter events, 35.9 us)
Async XLA Ops:
  0.6 73.7 %copy-start = (bf16[3,1024]{1,0:T(4,128)(2,1)S(1)}, bf16[3,1024]{1,0:T(4,128)(2,1)}, u32[]{:S(2)}) copy-start(bf16[3,1024]{1,0:T(4,128)(2,1)} %param.25) | copy-start | bytes 18436
  2.9 27.0 %collective-permute-start = (bf16[528,1024]{1,0:T(8,128)(2,1)S(1)}, bf16[528,1024]{1,0:T(8,128)(2,1)}, u32[]{:S(2)}, u32[]{:S(2)}) collective-permute-start(bf16[528,1024]{1,0:T(8,128)(2,1)S(1)} %pad_maximum_fusion), channel_id=1, source_target_pairs={{0,2},{2,0},{4,6},{6,4},{8,10},{10,8},{12,14},{14,12},{1,3},{3,1},... | collective-permute-start | bytes 3244040 | tf_op jit(solution)/shard_map/ppermute | solution.py:580
  7.0 11.4 %collective-permute-start.3 = (bf16[528,256]{1,0:T(8,128)(2,1)S(1)}, bf16[528,256]{1,0:T(8,128)(2,1)S(1)}, u32[]{:S(2)}, u32[]{:S(2)}) collective-permute-start(bf16[528,256]{1,0:T(8,128)(2,1)S(1)} %pad_maximum_fusion.5), channel_id=1, source_target_pairs={{12,0},{14,2},{0,4},{2,6},{4,8},{6,10},{8,12},{10,14},{13,1},{15,3... | collective-permute-start | bytes 811016 | tf_op jit(solution)/shard_map/ppermute | solution.py:583
  8.6 19.9 %collective-permute-start.2 = (bf16[528,256]{1,0:T(8,128)(2,1)S(1)}, bf16[528,256]{1,0:T(8,128)(2,1)S(1)}, u32[]{:S(2)}, u32[]{:S(2)}) collective-permute-start(bf16[528,256]{1,0:T(8,128)(2,1)S(1)} %pad_maximum_fusion.5), channel_id=1, source_target_pairs={{8,0},{10,2},{12,4},{14,6},{0,8},{2,10},{4,12},{6,14},{9,1},{11,3}... | collective-permute-start | bytes 811016 | tf_op jit(solution)/shard_map/ppermute | solution.py:583
  11.2 17.4 %collective-permute-start.1 = (bf16[528,256]{1,0:T(8,128)(2,1)S(1)}, bf16[528,256]{1,0:T(8,128)(2,1)S(1)}, u32[]{:S(2)}, u32[]{:S(2)}) collective-permute-start(bf16[528,256]{1,0:T(8,128)(2,1)S(1)} %pad_maximum_fusion.5), channel_id=1, source_target_pairs={{4,0},{6,2},{8,4},{10,6},{12,8},{14,10},{0,12},{2,14},{5,1},{7,3},... | collective-permute-start | bytes 811016 | tf_op jit(solution)/shard_map/ppermute | solution.py:583
  29.9 16.1 %collective-permute-start.4 = (bf16[256,1024]{1,0:T(8,128)(2,1)S(1)}, bf16[256,1024]{1,0:T(8,128)(2,1)S(1)}, u32[]{:S(2)}, u32[]{:S(2)}) collective-permute-start(bf16[256,1024]{1,0:T(8,128)(2,1)S(1)} %pad_maximum_fusion.3), channel_id=1, source_target_pairs={{0,2},{2,0},{4,6},{6,4},{8,10},{10,8},{12,14},{14,12},{1,3},{3,1},... | collective-permute-start | bytes 1572872 | tf_op jit(solution)/shard_map/ppermute | solution.py:580
  46.1 30.3 %copy-start.3 = (bf16[256,1024]{1,0:T(8,128)(2,1)}, bf16[256,1024]{1,0:T(8,128)(2,1)S(1)}, u32[]{:S(2)}) copy-start(bf16[256,1024]{1,0:T(8,128)(2,1)S(1)} %collective-permute-done.4.refs_11_.refs_5_.refs_3_) | copy-start | bytes 1572868
  46.1 69.3 %all-to-all-start = ((bf16[4,528,512]{2,1,0:T(8,128)(2,1)}), bf16[4,528,512]{2,1,0:T(8,128)(2,1)S(1)}, u32[]{:S(2)}, u32[]{:S(2)}) async-start(bf16[4,528,512]{2,1,0:T(8,128)(2,1)} %bitcast.46), calls=%async_computation | async-start | bytes 4325376 | tf_op jit(solution)/shard_map/all_to_all | solution.py:643
  52.1 19.5 %copy-start.12 = (bf16[512,256]{1,0:T(8,128)(2,1)S(1)}, bf16[512,256]{1,0:T(8,128)(2,1)}, u32[]{:S(2)}) copy-start(bf16[512,256]{1,0:T(8,128)(2,1)} %get-tuple-element.184) | copy-start | bytes 786436
  53.2 19.6 %copy-start.9 = (bf16[1584,256]{1,0:T(8,128)(2,1)}, bf16[1584,256]{1,0:T(8,128)(2,1)S(1)}, u32[]{:S(2)}) copy-start(bf16[1584,256]{1,0:T(8,128)(2,1)S(1)} %constant_dynamic-update-slice_fusion.refs_1_) | copy-start | bytes 2433028
  53.2 21.1 %copy-start.13 = (bf16[512,1024]{1,0:T(8,128)(2,1)S(1)}, bf16[512,1024]{1,0:T(8,128)(2,1)}, u32[]{:S(2)}) copy-start(bf16[512,1024]{1,0:T(8,128)(2,1)} %param.23) | copy-start | bytes 3145732
  53.2 18.4 %collective-permute-start.6 = (bf16[1584,256]{1,0:T(8,128)(2,1)S(1)}, bf16[1584,256]{1,0:T(8,128)(2,1)S(1)}, u32[]{:S(2)}, u32[]{:S(2)}) collective-permute-start(bf16[1584,256]{1,0:T(8,128)(2,1)S(1)} %constant_dynamic-update-slice_fusion.refs_1_), channel_id=1, source_target_pairs={{0,16},{16,0},{1,17},{17,1},{2,18},{18,2},{3,19},{19,3},{4,20},{20... | collective-permute-start | bytes 2433032 | tf_op jit(solution)/shard_map/ppermute | solution.py:577
  56.8 58.6 %collective-permute-start.5 = (bf16[2112,256]{1,0:T(8,128)(2,1)}, bf16[2112,256]{1,0:T(8,128)(2,1)}, u32[]{:S(2)}, u32[]{:S(2)}) collective-permute-start(bf16[2112,256]{1,0:T(8,128)(2,1)} %pad_maximum_fusion.1), channel_id=1, source_target_pairs={{0,2},{2,0},{4,6},{6,4},{8,10},{10,8},{12,14},{14,12},{1,3},{3,1},... | collective-permute-start | bytes 3244040 | tf_op jit(solution)/shard_map/ppermute | solution.py:580
  72.8 42.6 %collective-permute-start.7 = (bf16[2112,256]{1,0:T(8,128)(2,1)}, bf16[2112,256]{1,0:T(8,128)(2,1)}, u32[]{:S(2)}, u32[]{:S(2)}) collective-permute-start(bf16[2112,256]{1,0:T(8,128)(2,1)} %pad_maximum_fusion.2), channel_id=1, source_target_pairs={{0,2},{2,0},{4,6},{6,4},{8,10},{10,8},{12,14},{14,12},{1,3},{3,1},... | collective-permute-start | bytes 3244040 | tf_op jit(solution)/shard_map/ppermute | solution.py:580
  75.9 39.5 %collective-permute-start.10 = (bf16[512,512]{1,0:T(8,128)(2,1)}, bf16[512,512]{1,0:T(8,128)(2,1)}, u32[]{:S(2)}, u32[]{:S(2)}) collective-permute-start(bf16[512,512]{1,0:T(8,128)(2,1)} %get-tuple-element.177), channel_id=1, source_target_pairs={{0,2},{2,0},{4,6},{6,4},{8,10},{10,8},{12,14},{14,12},{1,3},{3,1},... | collective-permute-start | bytes 1572872 | tf_op jit(solution)/shard_map/ppermute | solution.py:580
  77.4 37.9 %collective-permute-start.9 = (bf16[256,1024]{1,0:T(8,128)(2,1)S(1)}, bf16[256,1024]{1,0:T(8,128)(2,1)}, u32[]{:S(2)}, u32[]{:S(2)}) collective-permute-start(bf16[256,1024]{1,0:T(8,128)(2,1)S(1)} %get-tuple-element.179), channel_id=1, source_target_pairs={{12,8},{14,10},{8,4},{10,6},{4,0},{6,2},{13,9},{15,11},{9,5},{11,7... | collective-permute-start | bytes 1572872 | tf_op jit(solution)/shard_map/ppermute | solution.py:587
  78.7 36.6 %collective-permute-start.8 = (bf16[256,1024]{1,0:T(8,128)(2,1)S(1)}, bf16[256,1024]{1,0:T(8,128)(2,1)S(1)}, u32[]{:S(2)}, u32[]{:S(2)}) collective-permute-start(bf16[256,1024]{1,0:T(8,128)(2,1)S(1)} %get-tuple-element.179), channel_id=1, source_target_pairs={{0,4},{2,6},{4,8},{6,10},{8,12},{10,14},{1,5},{3,7},{5,9},{7,11},{... | collective-permute-start | bytes 1572872 | tf_op jit(solution)/shard_map/ppermute | solution.py:587
  115.4 31.1 %copy-start.21 = (bf16[256,1024]{1,0:T(8,128)(2,1)}, bf16[256,1024]{1,0:T(8,128)(2,1)S(1)}, u32[]{:S(2)}) copy-start(bf16[256,1024]{1,0:T(8,128)(2,1)S(1)} %collective-permute-done.8) | copy-start | bytes 1572868
  118.0 15.6 %collective-permute-start.12 = (bf16[256,1024]{1,0:T(8,128)(2,1)S(1)}, bf16[256,1024]{1,0:T(8,128)(2,1)}, u32[]{:S(2)}, u32[]{:S(2)}) collective-permute-start(bf16[256,1024]{1,0:T(8,128)(2,1)S(1)} %collective-permute-done.8), channel_id=1, source_target_pairs={{4,8},{6,10},{8,12},{10,14},{5,9},{7,11},{9,13},{11,15},{20,24},{2... | collective-permute-start | bytes 1572872 | tf_op jit(solution)/shard_map/ppermute | solution.py:587
  119.5 15.3 %collective-permute-start.13 = (bf16[256,1024]{1,0:T(8,128)(2,1)}, bf16[256,1024]{1,0:T(8,128)(2,1)}, u32[]{:S(2)}, u32[]{:S(2)}) collective-permute-start(bf16[256,1024]{1,0:T(8,128)(2,1)} %collective-permute-done.9), channel_id=1, source_target_pairs={{8,4},{10,6},{4,0},{6,2},{9,5},{11,7},{5,1},{7,3},{24,20},{26,22},... | collective-permute-start | bytes 1572872 | tf_op jit(solution)/shard_map/ppermute | solution.py:587
  120.8 6.4 %collective-permute-start.11 = (bf16[256,512]{1,0:T(8,128)(2,1)S(1)}, bf16[256,512]{1,0:T(8,128)(2,1)S(1)}, u32[]{:S(2)}, u32[]{:S(2)}) collective-permute-start(bf16[256,512]{1,0:T(8,128)(2,1)S(1)} %get-tuple-element.102), channel_id=1, source_target_pairs={{0,2},{2,0},{4,6},{6,4},{8,10},{10,8},{12,14},{14,12},{1,3},{3,1},... | collective-permute-start | bytes 786440 | tf_op jit(solution)/shard_map/ppermute | solution.py:580
  134.8 5.8 %collective-permute-start.14 = (f32[256,2048]{1,0:T(8,128)}, f32[256,2048]{1,0:T(8,128)S(1)}, u32[]{:S(2)}, u32[]{:S(2)}) collective-permute-start(f32[256,2048]{1,0:T(8,128)} %project_rows.1.mine_ref), channel_id=1, source_target_pairs={{0,1},{1,0},{2,3},{3,2},{4,5},{5,4},{6,7},{7,6},{8,9},{9,8},{10,11... | collective-permute-start | bytes 6291464 | tf_op jit(solution)/shard_map/ppermute | solution.py:681
  136.3 21.0 %collective-permute-start.17 = (bf16[256,1024]{1,0:T(8,128)(2,1)}, bf16[256,1024]{1,0:T(8,128)(2,1)S(1)}, u32[]{:S(2)}, u32[]{:S(2)}) collective-permute-start(bf16[256,1024]{1,0:T(8,128)(2,1)} %collective-permute-done.12), channel_id=1, source_target_pairs={{8,12},{10,14},{9,13},{11,15},{24,28},{26,30},{25,29},{27,31}} | collective-permute-start | bytes 1572872 | tf_op jit(solution)/shard_map/ppermute | solution.py:587
  137.0 20.3 %collective-permute-start.18 = (bf16[256,1024]{1,0:T(8,128)(2,1)}, bf16[256,1024]{1,0:T(8,128)(2,1)S(1)}, u32[]{:S(2)}, u32[]{:S(2)}) collective-permute-start(bf16[256,1024]{1,0:T(8,128)(2,1)} %collective-permute-done.13), channel_id=1, source_target_pairs={{4,0},{6,2},{5,1},{7,3},{20,16},{22,18},{21,17},{23,19}} | collective-permute-start | bytes 1572872 | tf_op jit(solution)/shard_map/ppermute | solution.py:587
  139.4 16.2 %collective-permute-start.19 = (bf16[256,1024]{1,0:T(8,128)(2,1)S(1)}, bf16[256,1024]{1,0:T(8,128)(2,1)S(1)}, u32[]{:S(2)}, u32[]{:S(2)}) collective-permute-start(bf16[256,1024]{1,0:T(8,128)(2,1)S(1)} %broadcast_select_fusion.3.refs_12_.refs_6_.refs_4_), channel_id=1, source_target_pairs={{0,16},{16,0},{1,17},{17,1},{2,18},{18,2},{3,19},{19,3},{4,20},{20... | collective-permute-start | bytes 1572872 | tf_op jit(solution)/shard_map/ppermute | solution.py:577
  146.5 19.9 %collective-permute-start.16 = (bf16[256,1024]{1,0:T(8,128)(2,1)}, bf16[256,1024]{1,0:T(8,128)(2,1)}, u32[]{:S(2)}, u32[]{:S(2)}) collective-permute-start(bf16[256,1024]{1,0:T(8,128)(2,1)} %get-tuple-element.150.refs_0_), channel_id=1, source_target_pairs={{12,8},{14,10},{8,4},{10,6},{4,0},{6,2},{13,9},{15,11},{9,5},{11,7... | collective-permute-start | bytes 1572872 | tf_op jit(solution)/shard_map/ppermute | solution.py:587
  147.8 18.6 %collective-permute-start.15 = (bf16[256,1024]{1,0:T(8,128)(2,1)}, bf16[256,1024]{1,0:T(8,128)(2,1)S(1)}, u32[]{:S(2)}, u32[]{:S(2)}) collective-permute-start(bf16[256,1024]{1,0:T(8,128)(2,1)} %get-tuple-element.150.refs_0_), channel_id=1, source_target_pairs={{0,4},{2,6},{4,8},{6,10},{8,12},{10,14},{1,5},{3,7},{5,9},{7,11},{... | collective-permute-start | bytes 1572872 | tf_op jit(solution)/shard_map/ppermute | solution.py:587
  155.7 19.3 %collective-permute-start.22 = (bf16[256,1024]{1,0:T(8,128)(2,1)}, bf16[256,1024]{1,0:T(8,128)(2,1)}, u32[]{:S(2)}, u32[]{:S(2)}) collective-permute-start(bf16[256,1024]{1,0:T(8,128)(2,1)} %get-tuple-element.150.refs_0_), channel_id=1, source_target_pairs={{0,2},{2,0},{4,6},{6,4},{8,10},{10,8},{12,14},{14,12},{1,3},{3,1},... | collective-permute-start | bytes 1572872 | tf_op jit(solution)/shard_map/ppermute | solution.py:580
  168.3 14.0 %collective-permute-start.24 = (bf16[256,1024]{1,0:T(8,128)(2,1)}, bf16[256,1024]{1,0:T(8,128)(2,1)}, u32[]{:S(2)}, u32[]{:S(2)}) collective-permute-start(bf16[256,1024]{1,0:T(8,128)(2,1)} %broadcast_select_fusion.2.refs_2_), channel_id=1, source_target_pairs={{0,2},{2,0},{4,6},{6,4},{8,10},{10,8},{12,14},{14,12},{1,3},{3,1},... | collective-permute-start | bytes 1572872 | tf_op jit(solution)/shard_map/ppermute | solution.py:580
  170.9 36.7 %copy-start.5 = (bf16[256,1024]{1,0:T(8,128)(2,1)}, bf16[256,1024]{1,0:T(8,128)(2,1)S(1)}, u32[]{:S(2)}) copy-start(bf16[256,1024]{1,0:T(8,128)(2,1)S(1)} %broadcast_select_fusion.1.refs_14_.refs_8_.refs_6_) | copy-start | bytes 1572868
  171.0 14.9 %collective-permute-start.23 = (bf16[256,1024]{1,0:T(8,128)(2,1)S(1)}, bf16[256,1024]{1,0:T(8,128)(2,1)S(1)}, u32[]{:S(2)}, u32[]{:S(2)}) collective-permute-start(bf16[256,1024]{1,0:T(8,128)(2,1)S(1)} %broadcast_select_fusion.1.refs_14_.refs_8_.refs_6_), channel_id=1, source_target_pairs={{0,16},{16,0},{1,17},{17,1},{2,18},{18,2},{3,19},{19,3},{4,20},{20... | collective-permute-start | bytes 1572872 | tf_op jit(solution)/shard_map/ppermute | solution.py:577
  171.8 14.0 %collective-permute-start.20 = (bf16[256,1024]{1,0:T(8,128)(2,1)S(1)}, bf16[256,1024]{1,0:T(8,128)(2,1)S(1)}, u32[]{:S(2)}, u32[]{:S(2)}) collective-permute-start(bf16[256,1024]{1,0:T(8,128)(2,1)S(1)} %collective-permute-done.15), channel_id=1, source_target_pairs={{4,8},{6,10},{8,12},{10,14},{5,9},{7,11},{9,13},{11,15},{20,24},{2... | collective-permute-start | bytes 1572872 | tf_op jit(solution)/shard_map/ppermute | solution.py:587
  172.5 19.1 %collective-permute-start.21 = (bf16[256,1024]{1,0:T(8,128)(2,1)}, bf16[256,1024]{1,0:T(8,128)(2,1)S(1)}, u32[]{:S(2)}, u32[]{:S(2)}) collective-permute-start(bf16[256,1024]{1,0:T(8,128)(2,1)} %collective-permute-done.16), channel_id=1, source_target_pairs={{8,4},{10,6},{4,0},{6,2},{9,5},{11,7},{5,1},{7,3},{24,20},{26,22},... | collective-permute-start | bytes 1572872 | tf_op jit(solution)/shard_map/ppermute | solution.py:587
  175.0 32.7 %copy-start.6 = (bf16[256,1024]{1,0:T(8,128)(2,1)}, bf16[256,1024]{1,0:T(8,128)(2,1)S(1)}, u32[]{:S(2)}) copy-start(bf16[256,1024]{1,0:T(8,128)(2,1)S(1)} %broadcast_select_fusion.refs_16_.refs_10_.refs_8_) | copy-start | bytes 1572868
  175.0 20.7 %collective-permute-start.27 = (bf16[256,1024]{1,0:T(8,128)(2,1)S(1)}, bf16[256,1024]{1,0:T(8,128)(2,1)S(1)}, u32[]{:S(2)}, u32[]{:S(2)}) collective-permute-start(bf16[256,1024]{1,0:T(8,128)(2,1)S(1)} %broadcast_select_fusion.refs_16_.refs_10_.refs_8_), channel_id=1, source_target_pairs={{0,16},{16,0},{1,17},{17,1},{2,18},{18,2},{3,19},{19,3},{4,20},{20... | collective-permute-start | bytes 1572872 | tf_op jit(solution)/shard_map/ppermute | solution.py:577
  185.9 21.8 %copy-start.17 = (bf16[256,1024]{1,0:T(8,128)(2,1)}, bf16[256,1024]{1,0:T(8,128)(2,1)S(1)}, u32[]{:S(2)}) copy-start(bf16[256,1024]{1,0:T(8,128)(2,1)S(1)} %collective-permute-done.23.refs_15_.refs_9_.refs_7_) | copy-start | bytes 1572868
  191.7 11.9 %collective-permute-start.28 = (bf16[256,1024]{1,0:T(8,128)(2,1)S(1)}, bf16[256,1024]{1,0:T(8,128)(2,1)}, u32[]{:S(2)}, u32[]{:S(2)}) collective-permute-start(bf16[256,1024]{1,0:T(8,128)(2,1)S(1)} %fusion.1.refs_4_), channel_id=1, source_target_pairs={{0,2},{2,0},{4,6},{6,4},{8,10},{10,8},{12,14},{14,12},{1,3},{3,1},... | collective-permute-start | bytes 1572872 | tf_op jit(solution)/shard_map/ppermute | solution.py:580
  192.3 11.3 %collective-permute-start.25 = (bf16[256,1024]{1,0:T(8,128)(2,1)S(1)}, bf16[256,1024]{1,0:T(8,128)(2,1)S(1)}, u32[]{:S(2)}, u32[]{:S(2)}) collective-permute-start(bf16[256,1024]{1,0:T(8,128)(2,1)S(1)} %collective-permute-done.20), channel_id=1, source_target_pairs={{8,12},{10,14},{9,13},{11,15},{24,28},{26,30},{25,29},{27,31}} | collective-permute-start | bytes 1572872 | tf_op jit(solution)/shard_map/ppermute | solution.py:587
  193.0 13.3 %collective-permute-start.26 = (bf16[256,1024]{1,0:T(8,128)(2,1)S(1)}, bf16[256,1024]{1,0:T(8,128)(2,1)S(1)}, u32[]{:S(2)}, u32[]{:S(2)}) collective-permute-start(bf16[256,1024]{1,0:T(8,128)(2,1)S(1)} %collective-permute-done.21), channel_id=1, source_target_pairs={{4,0},{6,2},{5,1},{7,3},{20,16},{22,18},{21,17},{23,19}} | collective-permute-start | bytes 1572872 | tf_op jit(solution)/shard_map/ppermute | solution.py:587
  194.3 13.4 %collective-permute-start.30 = (bf16[256,1024]{1,0:T(8,128)(2,1)}, bf16[256,1024]{1,0:T(8,128)(2,1)S(1)}, u32[]{:S(2)}, u32[]{:S(2)}) collective-permute-start(bf16[256,1024]{1,0:T(8,128)(2,1)} %collective-permute-done.22.refs_1_), channel_id=1, source_target_pairs={{0,1},{1,0},{2,3},{3,2},{4,5},{5,4},{6,7},{7,6},{8,9},{9,8},{10,11... | collective-permute-start | bytes 1572872 | tf_op jit(solution)/shard_map/ppermute | solution.py:691
  195.7 12.0 %collective-permute-start.31 = (bf16[256,1024]{1,0:T(8,128)(2,1)}, bf16[256,1024]{1,0:T(8,128)(2,1)S(1)}, u32[]{:S(2)}, u32[]{:S(2)}) collective-permute-start(bf16[256,1024]{1,0:T(8,128)(2,1)} %broadcast_select_fusion.2.refs_2_), channel_id=1, source_target_pairs={{0,1},{1,0},{2,3},{3,2},{4,5},{5,4},{6,7},{7,6},{8,9},{9,8},{10,11... | collective-permute-start | bytes 1572872 | tf_op jit(solution)/shard_map/ppermute | solution.py:691
  206.3 2.8 %collective-permute-start.32 = (bf16[256,1024]{1,0:T(8,128)(2,1)}, bf16[256,1024]{1,0:T(8,128)(2,1)S(1)}, u32[]{:S(2)}, u32[]{:S(2)}) collective-permute-start(bf16[256,1024]{1,0:T(8,128)(2,1)} %collective-permute-done.24.refs_3_), channel_id=1, source_target_pairs={{0,1},{1,0},{2,3},{3,2},{4,5},{5,4},{6,7},{7,6},{8,9},{9,8},{10,11... | collective-permute-start | bytes 1572872 | tf_op jit(solution)/shard_map/ppermute | solution.py:691
  206.3 2.8 %collective-permute-start.33 = (bf16[256,1024]{1,0:T(8,128)(2,1)S(1)}, bf16[256,1024]{1,0:T(8,128)(2,1)S(1)}, u32[]{:S(2)}, u32[]{:S(2)}) collective-permute-start(bf16[256,1024]{1,0:T(8,128)(2,1)S(1)} %fusion.1.refs_4_), channel_id=1, source_target_pairs={{0,1},{1,0},{2,3},{3,2},{4,5},{5,4},{6,7},{7,6},{8,9},{9,8},{10,11... | collective-permute-start | bytes 1572872 | tf_op jit(solution)/shard_map/ppermute | solution.py:691
  209.2 15.3 %collective-permute-start.34 = (bf16[256,1024]{1,0:T(8,128)(2,1)}, bf16[256,1024]{1,0:T(8,128)(2,1)S(1)}, u32[]{:S(2)}, u32[]{:S(2)}) collective-permute-start(bf16[256,1024]{1,0:T(8,128)(2,1)} %collective-permute-done.28.refs_0_), channel_id=1, source_target_pairs={{0,1},{1,0},{2,3},{3,2},{4,5},{5,4},{6,7},{7,6},{8,9},{9,8},{10,11... | collective-permute-start | bytes 1572872 | tf_op jit(solution)/shard_map/ppermute | solution.py:691
  210.1 14.3 %collective-permute-start.35 = (bf16[256,1024]{1,0:T(8,128)(2,1)}, bf16[256,1024]{1,0:T(8,128)(2,1)S(1)}, u32[]{:S(2)}, u32[]{:S(2)}) collective-permute-start(bf16[256,1024]{1,0:T(8,128)(2,1)} %select_select_fusion.1.refs_1_), channel_id=1, source_target_pairs={{0,1},{1,0},{2,3},{3,2},{4,5},{5,4},{6,7},{7,6},{8,9},{9,8},{10,11... | collective-permute-start | bytes 1572872 | tf_op jit(solution)/shard_map/ppermute | solution.py:691
  210.8 22.1 %collective-permute-start.29 = (bf16[256,1024]{1,0:T(8,128)(2,1)}, bf16[256,1024]{1,0:T(8,128)(2,1)S(1)}, u32[]{:S(2)}, u32[]{:S(2)}) collective-permute-start(bf16[256,1024]{1,0:T(8,128)(2,1)} %select_select_fusion.1.refs_1_), channel_id=1, source_target_pairs={{0,2},{2,0},{4,6},{6,4},{8,10},{10,8},{12,14},{14,12},{1,3},{3,1},... | collective-permute-start | bytes 1572872 | tf_op jit(solution)/shard_map/ppermute | solution.py:580
  232.9 2.0 collective-permute-start.36
  249.4 14.2 %collective-permute-start.37 = (bf16[512,512]{1,0:T(8,128)(2,1)}, bf16[512,512]{1,0:T(8,128)(2,1)S(1)}, u32[]{:S(2)}, u32[]{:S(2)}) collective-permute-start(bf16[512,512]{1,0:T(8,128)(2,1)} %decode_rows.3), channel_id=1, source_target_pairs={{0,2},{2,0},{4,6},{6,4},{8,10},{10,8},{12,14},{14,12},{1,3},{3,1},... | collective-permute-start | bytes 1572872 | tf_op jit(solution)/shard_map/ppermute | solution.py:736
  (28 other events, 174.1 us)

commit v10 on v9

--- a/solution.py
+++ b/solution.py
@@ -332,15 +332,21 @@
     def place(slot, value):
         out_ref[:, pl.ds(pl.multiple_of(ids_ref[slot] * cols, cols), cols)] = value
 
-    place(0, jnp.dot(att_ref[...], w_ref[...], preferred_element_type=jnp.float32))
-    for slot in range(1, 2 * far):
-        refs = (far_ref, far_other_ref) if slot < far else (near_w_ref, near_other_ref)
-        start = (slot - 1 if slot < far else slot - far) * (depth + EXTRA)
-        terms = [
-            jnp.dot(v, w[start : start + depth, :], preferred_element_type=jnp.float32)
-            for v, w in zip(halves, refs)
-        ]
-        place(slot, terms[0] + terms[1])
+    for slot, own_ref in ((0, w_ref), (far, near_w_ref)):
+        own = own_ref[: 2 * depth, :]
+        place(slot, jnp.dot(att_ref[...], own, preferred_element_type=jnp.float32))
+    for k in range(far - 1):
+        start = k * (depth + EXTRA)
+        band = slice(start, start + depth)
+        near_band = slice(start + 2 * depth + EXTRA, start + 3 * depth + EXTRA)
+        for slot, weights in (
+            (1 + k, (far_ref[band, :], far_other_ref[band, :])),
+            (far + 1 + k, (near_w_ref[near_band, :], near_other_ref[band, :])),
+        ):
+            terms = [
+                jnp.dot(v, w, preferred_element_type=jnp.float32) for v, w in zip(halves, weights)
+            ]
+            place(slot, terms[0] + terms[1])
 
 
 def project(ids, mine, near, weights):
@@ -425,9 +431,10 @@
             pl.when(is_mine)(functools.partial(copy, mine))
             pl.when(jnp.logical_not(is_mine))(functools.partial(copy, theirs))
 
-    start = 0
+    start, block = 0, w_ref.shape[1]
     for band in w_refs:
-        w_ref[start : start + band.shape[0], :] = band[...]
+        columns = pl.ds(pl.multiple_of(pl.program_id(0) * block, block), block)
+        w_ref[start : start + band.shape[0], :] = band[:, columns]
         start += band.shape[0]
     out_ref[...] = jnp.dot(
         normed_ref[...], w_ref[...], preferred_element_type=jnp.float32
@@ -443,8 +450,7 @@
     grid_spec = pltpu.PrefetchScalarGridSpec(
         num_scalar_prefetch=1,
         grid=(width // block,),
-        in_specs=[whole((rows, half))] * (2 * pieces)
-        + [pl.BlockSpec((band.shape[0], block), lambda i, ids: (0, i)) for band in bands],
+        in_specs=[pl.BlockSpec(memory_space=pltpu.VMEM)] * (2 * pieces + len(bands)),
         out_specs=pl.BlockSpec((rows * pieces, block), lambda i, ids: (0, i)),
         scratch_shapes=[
             pltpu.VMEM((rows * pieces, total), jnp.bfloat16),
@@ -455,7 +461,7 @@
         functools.partial(latents_kernel, pieces),
         grid_spec=grid_spec,
         out_shape=jax.ShapeDtypeStruct((rows * pieces, width), jnp.bfloat16),
-        compiler_params=params(BIG),
+        compiler_params=params(24),
         cost_estimate=cost(2 * rows * pieces * total * width, 2 * total * width),
         name="latent_keys_values",
     )(ids, *mine, *theirs, *bands)
@@ -610,16 +616,14 @@
     counted = jnp.pad(counted[None, :], ((0, EXTRA - 1), (0, out_cols - 2 * mods)))
     counted = counted.astype(jnp.bfloat16)
 
-    def half_of_out(which):
-        own = lax.dynamic_slice_in_dim(w_out, which * out_half, out_half, 0)
-        return jnp.concatenate([own, counted])
-
-    out_sent = half_of_out(x)
+    out_sent = jnp.concatenate(
+        [lax.dynamic_slice_in_dim(w_out, x * out_half, out_half, 0), counted]
+    )
     out_far = [over_far(out_sent, k) for k in range(1, far)]
     places = [((z + k) % far) * 2 + (y ^ j) for j in range(2) for k in range(far)]
     kv_for_near = columns((w_key, w_value), 1 - y)
-    near_inputs, out_far, out_sent, kv_for_near = lax.optimization_barrier(
-        (near_inputs, out_far, out_sent, kv_for_near)
+    near_inputs, out_far, kv_for_near = lax.optimization_barrier(
+        (near_inputs, out_far, kv_for_near)
     )
     out_far = jnp.concatenate(out_far)
     out_far_other = over_groups(out_far)
@@ -631,20 +635,23 @@
     parts = encode(
         y, latent_queries, enc_keys, enc_values, extra, near_inputs, head_bias, 2 * rows
     )
-    kv_near, out_sent, parts = lax.optimization_barrier((kv_near, out_sent, parts))
+    kv_near, out_far, parts = lax.optimization_barrier((kv_near, out_far, parts))
     kv_sent = jnp.where(x == 0, kv_own, kv_near)
     hops = {0: [kv_sent, kv_sent]}
     hops[1] = hop(1, hops[0])
     early = [k for k in range(1, far) if max(k, far - k) < 3]
     rest = [k for k in range(1, far) if k not in early]
-    out_near = over_near(jnp.concatenate([out_sent, out_far]))
-    out_near_other = over_near(jnp.concatenate([half_of_out(1 - x), out_far_other]))
+    out_near = over_near(jnp.concatenate([w_out, counted, out_far]))
+    out_near_other = over_groups(out_near[w_out.shape[0] + EXTRA :])
     columns_of_slice = [[2 * i + j for i in range(far)] for j in range(2)]
     parts = lax.all_to_all(parts, "pos", 0, 0, axis_index_groups=columns_of_slice, tiled=True)
 
     def kept_queries():
         far_counts = out_far.reshape(far - 1, out_half + EXTRA, out_cols)[:, out_half, : 2 * mods]
-        near_counts = out_near.reshape(far, out_half + EXTRA, out_cols)[:, out_half, : 2 * mods]
+        near_counts = out_near.reshape(-1, EXTRA, out_cols)[:, 0, : 2 * mods]
+        at = [w_out.shape[0] // EXTRA]
+        at += [at[0] + k * (out_half // EXTRA + 1) for k in range(1, far)]
+        near_counts = jnp.concatenate([near_counts[i : i + 1] for i in at])
         counts = jnp.concatenate([counted[:1, : 2 * mods], far_counts, near_counts])
         counts = counts.astype(jnp.int32)
         counts = counts[:, :mods] * 16 + counts[:, mods:]
@@ -711,7 +718,7 @@
     came[1] = hop(1, came[0])
     normed_near = over_near(normed)
     came, hops, kv_bands, kept = lax.optimization_barrier((came, hops, kv_bands, kept))
-    mine, other = [normed, normed_near], [normed_other]
+    mine, other, keys_values = [normed, normed_near], [normed_other], []
     for step in range(1, far):
         fresh = arrival(came, step)
         fresh_near = over_near(fresh)
@@ -720,15 +727,21 @@
             k = rest[step - 1]
             kv_moved = by_shift(hops, k)
             kv_bands += [kv_moved, over_groups(kv_moved)]
-            came, mine, kv_bands, fresh, fresh_near = lax.optimization_barrier(
-                (came, mine, kv_bands, fresh, fresh_near)
+            if step > 1:
+                keys_values.append(fold(mine, other))
+                mine, other = [], []
+            came, mine, other, kv_bands, keys_values, fresh, fresh_near = (
+                lax.optimization_barrier(
+                    (came, mine, other, kv_bands, keys_values, fresh, fresh_near)
+                )
             )
-            other += cores(mine[-1:] + [fresh])
-            mine += [fresh, fresh_near]
-    mine, other, fresh = lax.optimization_barrier((mine, other, fresh))
-    keys_values = [fold(mine[:-1], other)]
-    last = [mine[-1], fresh]
-    keys_values.append(fold(last, cores(last)))
+            if step == 1:
+                mine += [fresh, fresh_near]
+                other += cores(mine[1:])
+            else:
+                mine += [fresh, fresh_near]
+                other += cores([fresh, fresh_near])
+    keys_values.append(fold([*mine, fresh], [*other, *cores([fresh])]))
     fresh_near, keys_values = lax.optimization_barrier((fresh_near, keys_values))
     keys_values.append(fold([fresh_near], cores([fresh_near])))
     near_state = decode(near_queries, keys_values, jnp.bfloat16)

time: 266 us -> 260 us (0.977)
  Pallas kernels: 67.6 us -> 62.1 us
  waiting for transfers between devices: 111 us -> 107 us
  local copies, waits for them, and re-layouts: 14.7 us -> 18.4 us
    ppermute x12, waiting for transfers between devices: 18.8 us -> 30.8 us  [hop(): lax.ppermute(v, 'pos', hop_perm(pos, step, way))]
    ppermute x4 -> x5, waiting for transfers between devices: 18.2 us -> 6.92 us  [over_groups(): return lax.ppermute(value, 'groups', swap_perm(groups))]
    ppermute x10 -> x9, waiting for transfers between devices: 51 us -> 40.8 us  [over_near(): return lax.ppermute(value, 'pos', near)]
    ppermute x3, waiting for transfers between devices: 14.4 us -> 20.4 us  [over_far(): return lax.ppermute(value, 'pos', shift_perm(pos, k))]
    pallas_call x3, Pallas kernels: 24.3 us -> 18.8 us  [latent_keys_values(): pl.pallas_call(functools.partial(latents_kernel, pieces), grid_spec=grid_...]
    unnamed x78 -> x41, local copies, waits for them, and re-layouts: 7.01 us -> 9.25 us
    ppermute x4 -> x5, starting transfers between devices: 4.87 us -> 6.77 us  [over_groups(): return lax.ppermute(value, 'groups', swap_perm(groups))]
    ppermute x10 -> x9, starting transfers between devices: 15.1 us -> 13.6 us  [over_near(): return lax.ppermute(value, 'pos', near)]
  transfers between devices with their start and end apart: 39 -> 39, of which waited for: 17 -> 18; matrix products, arithmetic and copies ran while one was open for 8% -> 9% of each run, Pallas kernels for 20% -> 19%
where the time goes in v10:
time: 260 us; the launch traced here: 258 us
  waiting for transfers between devices  107 us (41%)
  Pallas kernels  62.1 us (24%)
  starting transfers between devices  54.3 us (21%)
  local copies, waits for them, and re-layouts  18.4 us (7%)
  other arithmetic  14.7 us (6%)
    ppermute x9, waiting for transfers between devices, over_near(): return lax.ppermute(value, 'pos', near)  40.8 us
    ppermute x12, waiting for transfers between devices, hop(): lax.ppermute(v, 'pos', hop_perm(pos, step, way))  30.8 us
    ppermute x12, starting transfers between devices, hop(): lax.ppermute(v, 'pos', hop_perm(pos, step, way))  23.3 us
    ppermute x3, waiting for transfers between devices, over_far(): return lax.ppermute(value, 'pos', shift_perm(pos, k))  20.4 us
    pallas_call x3, Pallas kernels, latent_keys_values(): pl.pallas_call(functools.partial(latents_kernel, pieces), grid_spec=grid_...  18.8 us
    pallas_call x2, Pallas kernels, decode(): pl.pallas_call(functools.partial(decode_kernel, len(keys_values)), grid=(...  16.8 us
    pallas_call x1, Pallas kernels, encode(): pl.pallas_call(encode_kernel, grid_spec=grid_spec, out_shape=jax.ShapeDty...  14.4 us
    ppermute x9, starting transfers between devices, over_near(): return lax.ppermute(value, 'pos', near)  13.6 us
  transfers between devices with their start and end apart: 39, of which 18 were waited for; matrix products, arithmetic and copies ran while one was open for 9% of the time, Pallas kernels for 19%

profile of v10, /device:TPU:0, one launch (start us, length us, event | category | flops | bytes accessed | tf_op | source)
XLA Modules:
  0.0 258.5 jit_solution(12734160195582325520)
XLA Ops:
  1.4 1.3 constant_dynamic-slice_fusion.8
  2.9 3.0 %collective-permute-start = (bf16[528,1024]{1,0:T(8,128)(2,1)S(1)}, bf16[528,1024]{1,0:T(8,128)(2,1)}, u32[]{:S(2)}, u32[]{:S(2)}) collective-permute-start(bf16[528,1024]{1,0:T(8,128)(2,1)S(1)} %pad_maximum_fusion.1), channel_id=1, source_target_pairs={{0,2},{2,0},{4,6},{6,4},{8,10},{10,8},{12,14},{14,12},{1,3},{3,1},... | collective-permute-start | bytes 3244040 | tf_op jit(solution)/shard_map/ppermute | solution.py:586
  6.9 3.6 %collective-permute-start.1 = (bf16[528,256]{1,0:T(8,128)(2,1)}, bf16[528,256]{1,0:T(8,128)(2,1)S(1)}, u32[]{:S(2)}, u32[]{:S(2)}) collective-permute-start(bf16[528,256]{1,0:T(8,128)(2,1)} %pad_maximum_fusion.4), channel_id=1, source_target_pairs={{4,0},{6,2},{8,4},{10,6},{12,8},{14,10},{0,12},{2,14},{5,1},{7,3},... | collective-permute-start | bytes 811016 | tf_op jit(solution)/shard_map/ppermute | solution.py:589
  13.2 4.6 %collective-permute-done.1 = bf16[528,256]{1,0:T(8,128)(2,1)S(1)} collective-permute-done((bf16[528,256]{1,0:T(8,128)(2,1)}, bf16[528,256]{1,0:T(8,128)(2,1)S(1)}, u32[]{:S(2)}, u32[]{:S(2)}) %collective-permute-start.1) | collective-permute-done | bytes 270368 | tf_op jit(solution)/shard_map/ppermute | solution.py:589
  17.8 15.8 %collective-permute-done.2 = bf16[528,256]{1,0:T(8,128)(2,1)} collective-permute-done((bf16[528,256]{1,0:T(8,128)(2,1)}, bf16[528,256]{1,0:T(8,128)(2,1)}, u32[]{:S(2)}, u32[]{:S(2)}) %collective-permute-start.2) | collective-permute-done | bytes 270368 | tf_op jit(solution)/shard_map/ppermute | solution.py:589
  34.8 1.7 constant_dynamic-update-slice_fusion.1
  36.5 1.7 constant_dynamic-update-slice_fusion.refs_1_
  38.2 14.4 %encode_rows.1 = bf16[2112,512]{1,0:T(8,128)(2,1)} custom-call(s32[1]{0:T(128)} %bitcast.9.ids_ref, bf16[2048,1024]{1,0:T(8,128)(2,1)} %q_ref.1, bf16[512,1024]{1,0:T(8,128)(2,1)} %k_ref.1, bf16[512,1024]{1,0:T(8,128)(2,1)} %v_ref.1, bf16[16,1024]{1,0:T(8,128)(2,1)} %copy-done.15, bf16[528,1024]{1,0:T(8,128)(2,1)} %collective-permute-done.near_ref, ...), custom_call_target="tpu_custom_call" | custom-call | flops 8589934592 | bytes 2097152 | tf_op jit(solution)/shard_map/encode_rows/pallas_call | solution.py:262
  52.7 4.1 %all-to-all-start = ((bf16[4,528,512]{2,1,0:T(8,128)(2,1)}), bf16[4,528,512]{2,1,0:T(8,128)(2,1)S(1)}, u32[]{:S(2)}, u32[]{:S(2)}) async-start(bf16[4,528,512]{2,1,0:T(8,128)(2,1)} %bitcast.52), calls=%async_computation | async-start | bytes 4325376 | tf_op jit(solution)/shard_map/all_to_all | solution.py:647
  58.0 1.6 collective-permute-start.5
  60.1 1.6 collective-permute-start.6
  61.7 26.5 %collective-permute-done.5.refs_3_ = bf16[2624,256]{1,0:T(8,128)(2,1)S(1)} collective-permute-done((bf16[2624,256]{1,0:T(8,128)(2,1)S(1)}, bf16[2624,256]{1,0:T(8,128)(2,1)S(1)}, u32[]{:S(2)}, u32[]{:S(2)}) %collective-permute-start.5) | collective-permute-done | bytes 1343520 | tf_op jit(solution)/shard_map/ppermute | solution.py:586
  89.2 1.5 collective-permute-start.7
  91.7 1.5 collective-permute-start.10
  94.4 4.5 %collective-permute-start.8 = (bf16[256,1024]{1,0:T(8,128)(2,1)S(1)}, bf16[256,1024]{1,0:T(8,128)(2,1)}, u32[]{:S(2)}, u32[]{:S(2)}) collective-permute-start(bf16[256,1024]{1,0:T(8,128)(2,1)S(1)} %get-tuple-element.153), channel_id=1, source_target_pairs={{0,4},{2,6},{4,8},{6,10},{8,12},{10,14},{1,5},{3,7},{5,9},{7,11},{... | collective-permute-start | bytes 1572872 | tf_op jit(solution)/shard_map/ppermute | solution.py:593
  100.2 3.2 %collective-permute-done.10.q_ref = bf16[512,512]{1,0:T(8,128)(2,1)} collective-permute-done((bf16[512,512]{1,0:T(8,128)(2,1)}, bf16[512,512]{1,0:T(8,128)(2,1)}, u32[]{:S(2)}, u32[]{:S(2)}) %collective-permute-start.10) | collective-permute-done | bytes 524320 | tf_op jit(solution)/shard_map/ppermute | solution.py:586
  103.3 3.0 %collective-permute-done.8 = bf16[256,1024]{1,0:T(8,128)(2,1)} collective-permute-done((bf16[256,1024]{1,0:T(8,128)(2,1)S(1)}, bf16[256,1024]{1,0:T(8,128)(2,1)}, u32[]{:S(2)}, u32[]{:S(2)}) %collective-permute-start.8) | collective-permute-done | bytes 524320 | tf_op jit(solution)/shard_map/ppermute | solution.py:593
  106.3 10.5 %collective-permute-done.9 = bf16[256,1024]{1,0:T(8,128)(2,1)} collective-permute-done((bf16[256,1024]{1,0:T(8,128)(2,1)S(1)}, bf16[256,1024]{1,0:T(8,128)(2,1)}, u32[]{:S(2)}, u32[]{:S(2)}) %collective-permute-start.9) | collective-permute-done | bytes 524320 | tf_op jit(solution)/shard_map/ppermute | solution.py:593
  116.8 1.9 merge_rows.1
  121.4 1.6 collective-permute-start.11
  123.6 6.1 %collective-permute-done.11.near_ref = bf16[256,512]{1,0:T(8,128)(2,1)S(1)} collective-permute-done((bf16[256,512]{1,0:T(8,128)(2,1)S(1)}, bf16[256,512]{1,0:T(8,128)(2,1)S(1)}, u32[]{:S(2)}, u32[]{:S(2)}) %collective-permute-start.11) | collective-permute-done | bytes 262176 | tf_op jit(solution)/shard_map/ppermute | solution.py:586
  130.3 5.7 %project_rows.1.mine_ref = f32[256,2048]{1,0:T(8,128)} custom-call(s32[10]{0:T(128)} %stack.82.ids_ref, bf16[256,512]{1,0:T(8,128)(2,1)} %copy-done.2, bf16[256,512]{1,0:T(8,128)(2,1)} %copy-done.14, bf16[1024,256]{1,0:T(8,128)(2,1)} %refs_0_.1, bf16[1584,256]{1,0:T(8,128)(2,1)} %constant_dynamic-update-slice_fusion.refs_1_, ...), custom_call_target="tpu_custom_call" | custom-call | flops 1073741824 | bytes 6291456 | tf_op jit(solution)/shard_map/project_rows/pallas_call | solution.py:363
  137.6 1.5 collective-permute-start.17
  140.4 1.6 collective-permute-start.19
  142.0 4.5 %norm_rows.1 = (f32[256,1024]{1,0:T(8,128)}, bf16[256,1024]{1,0:T(8,128)(2,1)}, bf16[256,1024]{1,0:T(8,128)(2,1)}) custom-call(s32[1]{0:T(128)} %bitcast.ids_ref, f32[256,2048]{1,0:T(8,128)} %project_rows.1.mine_ref, f32[256,2048]{1,0:T(8,128)} %collective-permute-done.14.theirs_ref, bf16[256,2048]{1,0:T(8,128)(2,1)} %latent_ref.1, f32[1,2048]{1,0:T(1,128)} %bitcast.54), custom_call_target="tpu_custom_call" | custom-call | flops 3145728 | bytes 6815744 | tf_op jit(solution)/shard_map/norm_rows/pallas_call | solution.py:397
  146.6 6.1 %collective-permute-start.15 = (bf16[256,1024]{1,0:T(8,128)(2,1)}, bf16[256,1024]{1,0:T(8,128)(2,1)}, u32[]{:S(2)}, u32[]{:S(2)}) collective-permute-start(bf16[256,1024]{1,0:T(8,128)(2,1)} %get-tuple-element.120.refs_0_), channel_id=1, source_target_pairs={{0,4},{2,6},{4,8},{6,10},{8,12},{10,14},{1,5},{3,7},{5,9},{7,11},{... | collective-permute-start | bytes 1572872 | tf_op jit(solution)/shard_map/ppermute | solution.py:593
  155.6 1.6 collective-permute-start.22
  157.2 6.2 %collective-permute-done.15 = bf16[256,1024]{1,0:T(8,128)(2,1)} collective-permute-done((bf16[256,1024]{1,0:T(8,128)(2,1)}, bf16[256,1024]{1,0:T(8,128)(2,1)}, u32[]{:S(2)}, u32[]{:S(2)}) %collective-permute-start.15) | collective-permute-done | bytes 524320 | tf_op jit(solution)/shard_map/ppermute | solution.py:593
  163.5 4.9 %collective-permute-done.16 = bf16[256,1024]{1,0:T(8,128)(2,1)} collective-permute-done((bf16[256,1024]{1,0:T(8,128)(2,1)}, bf16[256,1024]{1,0:T(8,128)(2,1)}, u32[]{:S(2)}, u32[]{:S(2)}) %collective-permute-start.16) | collective-permute-done | bytes 524320 | tf_op jit(solution)/shard_map/ppermute | solution.py:593
  168.4 1.5 collective-permute-start.20
  172.8 1.9 broadcast_select_fusion.2.refs_2_
  174.7 1.5 collective-permute-start.24
  177.3 1.6 collective-permute-start.27
  178.9 6.3 %collective-permute-done.21 = bf16[256,1024]{1,0:T(8,128)(2,1)} collective-permute-done((bf16[256,1024]{1,0:T(8,128)(2,1)}, bf16[256,1024]{1,0:T(8,128)(2,1)}, u32[]{:S(2)}, u32[]{:S(2)}) %collective-permute-start.21) | collective-permute-done | bytes 524320 | tf_op jit(solution)/shard_map/ppermute | solution.py:593
  185.2 2.1 collective-permute-done.23.refs_13_.refs_11_.refs_7_
  187.8 1.4 collective-permute-start.25
  189.3 2.1 fusion.1.refs_0_
  191.4 4.8 %collective-permute-done.27.refs_15_.refs_13_.refs_9_ = bf16[256,1024]{1,0:T(8,128)(2,1)} collective-permute-done((bf16[256,1024]{1,0:T(8,128)(2,1)S(1)}, bf16[256,1024]{1,0:T(8,128)(2,1)}, u32[]{:S(2)}, u32[]{:S(2)}) %collective-permute-start.27) | collective-permute-done | bytes 524320 | tf_op jit(solution)/shard_map/ppermute | solution.py:583
  197.5 1.6 collective-permute-start.31
  201.3 8.5 %latent_keys_values.3.refs_0_.refs_3_ = bf16[1024,1024]{1,0:T(8,128)(2,1)S(1)} custom-call(s32[9]{0:T(128)S(1)} %stack.92.ids_ref, bf16[256,1024]{1,0:T(8,128)(2,1)S(1)} %copy-done.3, bf16[256,1024]{1,0:T(8,128)(2,1)} %collective-permute-done.22.refs_1_, bf16[256,1024]{1,0:T(8,128)(2,1)} %broadcast_select_fusion.2.refs_2_, ...), custom_call_target="tpu_custom_call" | custom-call | flops 4294967296 | bytes 4194304 | tf_op jit(solution)/shard_map/latent_keys_values/pallas_call | solution.py:460
  214.8 6.4 %latent_keys_values.4.refs_1_.refs_4_ = bf16[768,1024]{1,0:T(8,128)(2,1)S(1)} custom-call(s32[9]{0:T(128)S(1)} %stack.92.ids_ref, bf16[256,1024]{1,0:T(8,128)(2,1)} %fusion.1.refs_0_, bf16[256,1024]{1,0:T(8,128)(2,1)} %collective-permute-done.31.refs_1_, bf16[256,1024]{1,0:T(8,128)(2,1)S(1)} %select_select_fusion.1.refs_2_, ...), custom_call_target="tpu_custom_call" | custom-call | flops 3221225472 | bytes 4194304 | tf_op jit(solution)/shard_map/latent_keys_values/pallas_call | solution.py:460
  222.4 5.0 %collective-permute-done.32.refs_0_ = bf16[256,1024]{1,0:T(8,128)(2,1)} collective-permute-done((bf16[256,1024]{1,0:T(8,128)(2,1)S(1)}, bf16[256,1024]{1,0:T(8,128)(2,1)}, u32[]{:S(2)}, u32[]{:S(2)}) %collective-permute-start.32) | collective-permute-done | bytes 524320 | tf_op jit(solution)/shard_map/ppermute | solution.py:586
  227.4 2.2 collective-permute-done.36.refs_1_
  229.6 3.8 %latent_keys_values.5.refs_2_.refs_5_ = bf16[256,1024]{1,0:T(8,128)(2,1)S(1)} custom-call(s32[9]{0:T(128)S(1)} %stack.92.ids_ref, bf16[256,1024]{1,0:T(8,128)(2,1)} %collective-permute-done.32.refs_0_, bf16[256,1024]{1,0:T(8,128)(2,1)} %collective-permute-done.36.refs_1_, bf16[256,1024]{1,0:T(8,128)(2,1)S(1)} %get-tuple-element.132.refs_8_.refs_6_.refs_2_, ...), custom_call_target="tpu_custom_call" | custom-call | flops 1073741824 | bytes 4194304 | tf_op jit(solution)/shard_map/latent_keys_values/pallas_call | solution.py:460
  234.3 8.3 %decode_rows.3 = bf16[512,512]{1,0:T(8,128)(2,1)} custom-call(bf16[512,512]{1,0:T(8,128)(2,1)} %collective-permute-done.10.q_ref, bf16[1024,1024]{1,0:T(8,128)(2,1)} %copy-done.6, bf16[768,1024]{1,0:T(8,128)(2,1)} %copy-done.5, bf16[256,1024]{1,0:T(8,128)(2,1)} %copy-done.1, bf16[1024,1024]{1,0:T(8,128)(2,1)} %copy-done.6, bf16[768,1024]{1,0:T(8,128)(2,1)} %copy-done.5, ...), custom_call_target="tpu_custom_call" | custom-call | flops 8589934592 | bytes 5767168 | tf_op jit(solution)/shard_map/decode_rows/pallas_call | solution.py:521
  243.2 8.5 %decode_rows.2 = f32[512,512]{1,0:T(8,128)} custom-call(bf16[512,512]{1,0:T(8,128)(2,1)} %get-tuple-element.150.q_ref, bf16[1024,1024]{1,0:T(8,128)(2,1)} %copy-done.6, bf16[768,1024]{1,0:T(8,128)(2,1)} %copy-done.5, bf16[256,1024]{1,0:T(8,128)(2,1)} %copy-done.1, bf16[1024,1024]{1,0:T(8,128)(2,1)} %copy-done.6, bf16[768,1024]{1,0:T(8,128)(2,1)} %copy-done.5, ...), custom_call_target="tpu_custom_call" | custom-call | flops 8589934592 | bytes 5767168 | tf_op jit(solution)/shard_map/decode_rows/pallas_call | solution.py:521
  251.7 5.1 %collective-permute-done.37 = bf16[512,512]{1,0:T(8,128)(2,1)S(1)} collective-permute-done((bf16[512,512]{1,0:T(8,128)(2,1)}, bf16[512,512]{1,0:T(8,128)(2,1)S(1)}, u32[]{:S(2)}, u32[]{:S(2)}) %collective-permute-start.37) | collective-permute-done | bytes 524320 | tf_op jit(solution)/shard_map/ppermute | solution.py:749
  256.9 1.6 fusion
  (124 shorter events, 37.7 us)
Async XLA Ops:
  0.6 59.0 %copy-start = (bf16[3,1024]{1,0:T(4,128)(2,1)S(1)}, bf16[3,1024]{1,0:T(4,128)(2,1)}, u32[]{:S(2)}) copy-start(bf16[3,1024]{1,0:T(4,128)(2,1)} %param.25) | copy-start | bytes 18436
  1.4 4.6 %copy-start.16 = (s32[512]{0:T(512)S(1)}, s32[512]{0:T(512)}, u32[]{:S(2)}) copy-start(s32[512]{0:T(512)} %param.24) | copy-start | bytes 6148
  1.4 4.8 %copy-start.8 = (bf16[1024,256]{1,0:T(8,128)(2,1)S(1)}, bf16[1024,256]{1,0:T(8,128)(2,1)}, u32[]{:S(2)}) copy-start(bf16[1024,256]{1,0:T(8,128)(2,1)} %refs_0_.1) | copy-start | bytes 1572868
  2.7 8.8 %copy-start.17 = (f32[3,8]{1,0:T(4,128)S(1)}, f32[3,8]{1,0:T(4,128)}, u32[]{:S(2)}) copy-start(f32[3,8]{1,0:T(4,128)} %param.26) | copy-start | bytes 292
  2.7 9.5 %copy-start.12 = (bf16[256,1024]{1,0:T(8,128)(2,1)S(1)}, bf16[256,1024]{1,0:T(8,128)(2,1)}, u32[]{:S(2)}) copy-start(bf16[256,1024]{1,0:T(8,128)(2,1)} %param.22) | copy-start | bytes 1572868
  2.8 9.5 %copy-start.13 = (bf16[256,1024]{1,0:T(8,128)(2,1)S(1)}, bf16[256,1024]{1,0:T(8,128)(2,1)}, u32[]{:S(2)}) copy-start(bf16[256,1024]{1,0:T(8,128)(2,1)} %param.21) | copy-start | bytes 1572868
  2.9 30.7 %collective-permute-start = (bf16[528,1024]{1,0:T(8,128)(2,1)S(1)}, bf16[528,1024]{1,0:T(8,128)(2,1)}, u32[]{:S(2)}, u32[]{:S(2)}) collective-permute-start(bf16[528,1024]{1,0:T(8,128)(2,1)S(1)} %pad_maximum_fusion.1), channel_id=1, source_target_pairs={{0,2},{2,0},{4,6},{6,4},{8,10},{10,8},{12,14},{14,12},{1,3},{3,1},... | collective-permute-start | bytes 3244040 | tf_op jit(solution)/shard_map/ppermute | solution.py:586
  6.9 10.9 %collective-permute-start.1 = (bf16[528,256]{1,0:T(8,128)(2,1)}, bf16[528,256]{1,0:T(8,128)(2,1)S(1)}, u32[]{:S(2)}, u32[]{:S(2)}) collective-permute-start(bf16[528,256]{1,0:T(8,128)(2,1)} %pad_maximum_fusion.4), channel_id=1, source_target_pairs={{4,0},{6,2},{8,4},{10,6},{12,8},{14,10},{0,12},{2,14},{5,1},{7,3},... | collective-permute-start | bytes 811016 | tf_op jit(solution)/shard_map/ppermute | solution.py:589
  10.5 23.0 %collective-permute-start.2 = (bf16[528,256]{1,0:T(8,128)(2,1)}, bf16[528,256]{1,0:T(8,128)(2,1)}, u32[]{:S(2)}, u32[]{:S(2)}) collective-permute-start(bf16[528,256]{1,0:T(8,128)(2,1)} %pad_maximum_fusion.4), channel_id=1, source_target_pairs={{8,0},{10,2},{12,4},{14,6},{0,8},{2,10},{4,12},{6,14},{9,1},{11,3}... | collective-permute-start | bytes 811016 | tf_op jit(solution)/shard_map/ppermute | solution.py:589
  10.6 23.0 %collective-permute-start.3 = (bf16[528,256]{1,0:T(8,128)(2,1)}, bf16[528,256]{1,0:T(8,128)(2,1)}, u32[]{:S(2)}, u32[]{:S(2)}) collective-permute-start(bf16[528,256]{1,0:T(8,128)(2,1)} %pad_maximum_fusion.4), channel_id=1, source_target_pairs={{12,0},{14,2},{0,4},{2,6},{4,8},{6,10},{8,12},{10,14},{13,1},{15,3... | collective-permute-start | bytes 811016 | tf_op jit(solution)/shard_map/ppermute | solution.py:589
  33.6 19.1 %collective-permute-start.4 = (bf16[256,1024]{1,0:T(8,128)(2,1)S(1)}, bf16[256,1024]{1,0:T(8,128)(2,1)S(1)}, u32[]{:S(2)}, u32[]{:S(2)}) collective-permute-start(bf16[256,1024]{1,0:T(8,128)(2,1)S(1)} %pad_maximum_fusion.2), channel_id=1, source_target_pairs={{0,2},{2,0},{4,6},{6,4},{8,10},{10,8},{12,14},{14,12},{1,3},{3,1},... | collective-permute-start | bytes 1572872 | tf_op jit(solution)/shard_map/ppermute | solution.py:586
  52.7 64.1 %all-to-all-start = ((bf16[4,528,512]{2,1,0:T(8,128)(2,1)}), bf16[4,528,512]{2,1,0:T(8,128)(2,1)S(1)}, u32[]{:S(2)}, u32[]{:S(2)}) async-start(bf16[4,528,512]{2,1,0:T(8,128)(2,1)} %bitcast.52), calls=%async_computation | async-start | bytes 4325376 | tf_op jit(solution)/shard_map/all_to_all | solution.py:647
  58.0 30.1 %collective-permute-start.5 = (bf16[2624,256]{1,0:T(8,128)(2,1)S(1)}, bf16[2624,256]{1,0:T(8,128)(2,1)S(1)}, u32[]{:S(2)}, u32[]{:S(2)}) collective-permute-start(bf16[2624,256]{1,0:T(8,128)(2,1)S(1)} %pad_maximum_fusion), channel_id=1, source_target_pairs={{0,2},{2,0},{4,6},{6,4},{8,10},{10,8},{12,14},{14,12},{1,3},{3,1},... | collective-permute-start | bytes 4030472 | tf_op jit(solution)/shard_map/ppermute | solution.py:586
  60.1 33.1 %copy-start.11 = (bf16[256,512]{1,0:T(8,128)(2,1)S(1)}, bf16[256,512]{1,0:T(8,128)(2,1)}, u32[]{:S(2)}) copy-start(bf16[256,512]{1,0:T(8,128)(2,1)} %get-tuple-element.156) | copy-start | bytes 786436
  60.1 43.2 %collective-permute-start.6 = (bf16[1584,256]{1,0:T(8,128)(2,1)}, bf16[1584,256]{1,0:T(8,128)(2,1)}, u32[]{:S(2)}, u32[]{:S(2)}) collective-permute-start(bf16[1584,256]{1,0:T(8,128)(2,1)} %constant_dynamic-update-slice_fusion.refs_1_), channel_id=1, source_target_pairs={{0,16},{16,0},{1,17},{17,1},{2,18},{18,2},{3,19},{19,3},{4,20},{20... | collective-permute-start | bytes 2433032 | tf_op jit(solution)/shard_map/ppermute | solution.py:583
  89.2 27.6 %collective-permute-start.7 = (bf16[1584,256]{1,0:T(8,128)(2,1)}, bf16[1584,256]{1,0:T(8,128)(2,1)}, u32[]{:S(2)}, u32[]{:S(2)}) collective-permute-start(bf16[1584,256]{1,0:T(8,128)(2,1)} %slice.62), channel_id=1, source_target_pairs={{0,16},{16,0},{1,17},{17,1},{2,18},{18,2},{3,19},{19,3},{4,20},{20... | collective-permute-start | bytes 2433032 | tf_op jit(solution)/shard_map/ppermute | solution.py:583
  91.7 11.6 %collective-permute-start.10 = (bf16[512,512]{1,0:T(8,128)(2,1)}, bf16[512,512]{1,0:T(8,128)(2,1)}, u32[]{:S(2)}, u32[]{:S(2)}) collective-permute-start(bf16[512,512]{1,0:T(8,128)(2,1)} %get-tuple-element.151), channel_id=1, source_target_pairs={{0,2},{2,0},{4,6},{6,4},{8,10},{10,8},{12,14},{14,12},{1,3},{3,1},... | collective-permute-start | bytes 1572872 | tf_op jit(solution)/shard_map/ppermute | solution.py:586
  94.4 11.9 %collective-permute-start.8 = (bf16[256,1024]{1,0:T(8,128)(2,1)S(1)}, bf16[256,1024]{1,0:T(8,128)(2,1)}, u32[]{:S(2)}, u32[]{:S(2)}) collective-permute-start(bf16[256,1024]{1,0:T(8,128)(2,1)S(1)} %get-tuple-element.153), channel_id=1, source_target_pairs={{0,4},{2,6},{4,8},{6,10},{8,12},{10,14},{1,5},{3,7},{5,9},{7,11},{... | collective-permute-start | bytes 1572872 | tf_op jit(solution)/shard_map/ppermute | solution.py:593
  98.9 17.9 %collective-permute-start.9 = (bf16[256,1024]{1,0:T(8,128)(2,1)S(1)}, bf16[256,1024]{1,0:T(8,128)(2,1)}, u32[]{:S(2)}, u32[]{:S(2)}) collective-permute-start(bf16[256,1024]{1,0:T(8,128)(2,1)S(1)} %get-tuple-element.153), channel_id=1, source_target_pairs={{12,8},{14,10},{8,4},{10,6},{4,0},{6,2},{13,9},{15,11},{9,5},{11,7... | collective-permute-start | bytes 1572872 | tf_op jit(solution)/shard_map/ppermute | solution.py:593
  119.4 16.7 %collective-permute-start.12 = (bf16[256,1024]{1,0:T(8,128)(2,1)}, bf16[256,1024]{1,0:T(8,128)(2,1)S(1)}, u32[]{:S(2)}, u32[]{:S(2)}) collective-permute-start(bf16[256,1024]{1,0:T(8,128)(2,1)} %collective-permute-done.8), channel_id=1, source_target_pairs={{4,8},{6,10},{8,12},{10,14},{5,9},{7,11},{9,13},{11,15},{20,24},{2... | collective-permute-start | bytes 1572872 | tf_op jit(solution)/shard_map/ppermute | solution.py:593
  120.1 16.0 %collective-permute-start.13 = (bf16[256,1024]{1,0:T(8,128)(2,1)}, bf16[256,1024]{1,0:T(8,128)(2,1)S(1)}, u32[]{:S(2)}, u32[]{:S(2)}) collective-permute-start(bf16[256,1024]{1,0:T(8,128)(2,1)} %collective-permute-done.9), channel_id=1, source_target_pairs={{8,4},{10,6},{4,0},{6,2},{9,5},{11,7},{5,1},{7,3},{24,20},{26,22},... | collective-permute-start | bytes 1572872 | tf_op jit(solution)/shard_map/ppermute | solution.py:593
  121.4 8.3 %collective-permute-start.11 = (bf16[256,512]{1,0:T(8,128)(2,1)S(1)}, bf16[256,512]{1,0:T(8,128)(2,1)S(1)}, u32[]{:S(2)}, u32[]{:S(2)}) collective-permute-start(bf16[256,512]{1,0:T(8,128)(2,1)S(1)} %get-tuple-element.86), channel_id=1, source_target_pairs={{0,2},{2,0},{4,6},{6,4},{8,10},{10,8},{12,14},{14,12},{1,3},{3,1},... | collective-permute-start | bytes 786440 | tf_op jit(solution)/shard_map/ppermute | solution.py:586
  136.0 6.0 %collective-permute-start.14 = (f32[256,2048]{1,0:T(8,128)}, f32[256,2048]{1,0:T(8,128)}, u32[]{:S(2)}, u32[]{:S(2)}) collective-permute-start(f32[256,2048]{1,0:T(8,128)} %project_rows.1.mine_ref), channel_id=1, source_target_pairs={{0,1},{1,0},{2,3},{3,2},{4,5},{5,4},{6,7},{7,6},{8,9},{9,8},{10,11... | collective-permute-start | bytes 6291464 | tf_op jit(solution)/shard_map/ppermute | solution.py:688
  137.6 18.0 %collective-permute-start.17 = (bf16[256,1024]{1,0:T(8,128)(2,1)S(1)}, bf16[256,1024]{1,0:T(8,128)(2,1)}, u32[]{:S(2)}, u32[]{:S(2)}) collective-permute-start(bf16[256,1024]{1,0:T(8,128)(2,1)S(1)} %collective-permute-done.12), channel_id=1, source_target_pairs={{8,12},{10,14},{9,13},{11,15},{24,28},{26,30},{25,29},{27,31}} | collective-permute-start | bytes 1572872 | tf_op jit(solution)/shard_map/ppermute | solution.py:593
  139.1 18.1 %collective-permute-start.18 = (bf16[256,1024]{1,0:T(8,128)(2,1)S(1)}, bf16[256,1024]{1,0:T(8,128)(2,1)}, u32[]{:S(2)}, u32[]{:S(2)}) collective-permute-start(bf16[256,1024]{1,0:T(8,128)(2,1)S(1)} %collective-permute-done.13), channel_id=1, source_target_pairs={{4,0},{6,2},{5,1},{7,3},{20,16},{22,18},{21,17},{23,19}} | collective-permute-start | bytes 1572872 | tf_op jit(solution)/shard_map/ppermute | solution.py:593
  140.4 16.8 %collective-permute-start.19 = (bf16[256,1024]{1,0:T(8,128)(2,1)S(1)}, bf16[256,1024]{1,0:T(8,128)(2,1)S(1)}, u32[]{:S(2)}, u32[]{:S(2)}) collective-permute-start(bf16[256,1024]{1,0:T(8,128)(2,1)S(1)} %broadcast_select_fusion.3.refs_10_.refs_8_.refs_4_), channel_id=1, source_target_pairs={{0,16},{16,0},{1,17},{17,1},{2,18},{18,2},{3,19},{19,3},{4,20},{20... | collective-permute-start | bytes 1572872 | tf_op jit(solution)/shard_map/ppermute | solution.py:583
  142.0 13.5 %copy-start.18 = (s32[3]{0:T(128)S(1)}, s32[3]{0:T(128)}, u32[]{:S(2)}) copy-start(s32[3]{0:T(128)} %param.27) | copy-start | bytes 40
  146.6 16.9 %collective-permute-start.15 = (bf16[256,1024]{1,0:T(8,128)(2,1)}, bf16[256,1024]{1,0:T(8,128)(2,1)}, u32[]{:S(2)}, u32[]{:S(2)}) collective-permute-start(bf16[256,1024]{1,0:T(8,128)(2,1)} %get-tuple-element.120.refs_0_), channel_id=1, source_target_pairs={{0,4},{2,6},{4,8},{6,10},{8,12},{10,14},{1,5},{3,7},{5,9},{7,11},{... | collective-permute-start | bytes 1572872 | tf_op jit(solution)/shard_map/ppermute | solution.py:593
  152.7 15.7 %collective-permute-start.16 = (bf16[256,1024]{1,0:T(8,128)(2,1)}, bf16[256,1024]{1,0:T(8,128)(2,1)}, u32[]{:S(2)}, u32[]{:S(2)}) collective-permute-start(bf16[256,1024]{1,0:T(8,128)(2,1)} %get-tuple-element.120.refs_0_), channel_id=1, source_target_pairs={{12,8},{14,10},{8,4},{10,6},{4,0},{6,2},{13,9},{15,11},{9,5},{11,7... | collective-permute-start | bytes 1572872 | tf_op jit(solution)/shard_map/ppermute | solution.py:593
  155.6 21.7 %collective-permute-start.22 = (bf16[256,1024]{1,0:T(8,128)(2,1)}, bf16[256,1024]{1,0:T(8,128)(2,1)}, u32[]{:S(2)}, u32[]{:S(2)}) collective-permute-start(bf16[256,1024]{1,0:T(8,128)(2,1)} %get-tuple-element.120.refs_0_), channel_id=1, source_target_pairs={{0,2},{2,0},{4,6},{6,4},{8,10},{10,8},{12,14},{14,12},{1,3},{3,1},... | collective-permute-start | bytes 1572872 | tf_op jit(solution)/shard_map/ppermute | solution.py:586
  168.4 10.6 %collective-permute-start.20 = (bf16[256,1024]{1,0:T(8,128)(2,1)}, bf16[256,1024]{1,0:T(8,128)(2,1)}, u32[]{:S(2)}, u32[]{:S(2)}) collective-permute-start(bf16[256,1024]{1,0:T(8,128)(2,1)} %collective-permute-done.15), channel_id=1, source_target_pairs={{4,8},{6,10},{8,12},{10,14},{5,9},{7,11},{9,13},{11,15},{20,24},{2... | collective-permute-start | bytes 1572872 | tf_op jit(solution)/shard_map/ppermute | solution.py:593
  169.8 15.3 %collective-permute-start.21 = (bf16[256,1024]{1,0:T(8,128)(2,1)}, bf16[256,1024]{1,0:T(8,128)(2,1)}, u32[]{:S(2)}, u32[]{:S(2)}) collective-permute-start(bf16[256,1024]{1,0:T(8,128)(2,1)} %collective-permute-done.16), channel_id=1, source_target_pairs={{8,4},{10,6},{4,0},{6,2},{9,5},{11,7},{5,1},{7,3},{24,20},{26,22},... | collective-permute-start | bytes 1572872 | tf_op jit(solution)/shard_map/ppermute | solution.py:593
  172.2 15.0 %collective-permute-start.23 = (bf16[256,1024]{1,0:T(8,128)(2,1)S(1)}, bf16[256,1024]{1,0:T(8,128)(2,1)}, u32[]{:S(2)}, u32[]{:S(2)}) collective-permute-start(bf16[256,1024]{1,0:T(8,128)(2,1)S(1)} %broadcast_select_fusion.1.refs_12_.refs_10_.refs_6_), channel_id=1, source_target_pairs={{0,16},{16,0},{1,17},{17,1},{2,18},{18,2},{3,19},{19,3},{4,20},{20... | collective-permute-start | bytes 1572872 | tf_op jit(solution)/shard_map/ppermute | solution.py:583
  174.7 12.6 %collective-permute-start.24 = (bf16[256,1024]{1,0:T(8,128)(2,1)}, bf16[256,1024]{1,0:T(8,128)(2,1)}, u32[]{:S(2)}, u32[]{:S(2)}) collective-permute-start(bf16[256,1024]{1,0:T(8,128)(2,1)} %broadcast_select_fusion.2.refs_2_), channel_id=1, source_target_pairs={{0,2},{2,0},{4,6},{6,4},{8,10},{10,8},{12,14},{14,12},{1,3},{3,1},... | collective-permute-start | bytes 1572872 | tf_op jit(solution)/shard_map/ppermute | solution.py:586
  177.3 18.8 %collective-permute-start.27 = (bf16[256,1024]{1,0:T(8,128)(2,1)S(1)}, bf16[256,1024]{1,0:T(8,128)(2,1)}, u32[]{:S(2)}, u32[]{:S(2)}) collective-permute-start(bf16[256,1024]{1,0:T(8,128)(2,1)S(1)} %broadcast_select_fusion.refs_14_.refs_12_.refs_8_), channel_id=1, source_target_pairs={{0,16},{16,0},{1,17},{17,1},{2,18},{18,2},{3,19},{19,3},{4,20},{20... | collective-permute-start | bytes 1572872 | tf_op jit(solution)/shard_map/ppermute | solution.py:583
  187.3 10.2 %collective-permute-start.28 = (bf16[256,1024]{1,0:T(8,128)(2,1)}, bf16[256,1024]{1,0:T(8,128)(2,1)}, u32[]{:S(2)}, u32[]{:S(2)}) collective-permute-start(bf16[256,1024]{1,0:T(8,128)(2,1)} %collective-permute-done.22.refs_1_), channel_id=1, source_target_pairs={{0,1},{1,0},{2,3},{3,2},{4,5},{5,4},{6,7},{7,6},{8,9},{9,8},{10,11... | collective-permute-start | bytes 1572872 | tf_op jit(solution)/shard_map/ppermute | solution.py:698
  187.3 11.8 %collective-permute-start.29 = (bf16[256,1024]{1,0:T(8,128)(2,1)}, bf16[256,1024]{1,0:T(8,128)(2,1)}, u32[]{:S(2)}, u32[]{:S(2)}) collective-permute-start(bf16[256,1024]{1,0:T(8,128)(2,1)} %broadcast_select_fusion.2.refs_2_), channel_id=1, source_target_pairs={{0,1},{1,0},{2,3},{3,2},{4,5},{5,4},{6,7},{7,6},{8,9},{9,8},{10,11... | collective-permute-start | bytes 1572872 | tf_op jit(solution)/shard_map/ppermute | solution.py:698
  187.8 11.3 %collective-permute-start.30 = (bf16[256,1024]{1,0:T(8,128)(2,1)}, bf16[256,1024]{1,0:T(8,128)(2,1)}, u32[]{:S(2)}, u32[]{:S(2)}) collective-permute-start(bf16[256,1024]{1,0:T(8,128)(2,1)} %collective-permute-done.24.refs_3_), channel_id=1, source_target_pairs={{0,1},{1,0},{2,3},{3,2},{4,5},{5,4},{6,7},{7,6},{8,9},{9,8},{10,11... | collective-permute-start | bytes 1572872 | tf_op jit(solution)/shard_map/ppermute | solution.py:698
  187.8 23.3 %collective-permute-start.25 = (bf16[256,1024]{1,0:T(8,128)(2,1)}, bf16[256,1024]{1,0:T(8,128)(2,1)}, u32[]{:S(2)}, u32[]{:S(2)}) collective-permute-start(bf16[256,1024]{1,0:T(8,128)(2,1)} %collective-permute-done.20), channel_id=1, source_target_pairs={{8,12},{10,14},{9,13},{11,15},{24,28},{26,30},{25,29},{27,31}} | collective-permute-start | bytes 1572872 | tf_op jit(solution)/shard_map/ppermute | solution.py:593
  196.2 14.9 %collective-permute-start.26 = (bf16[256,1024]{1,0:T(8,128)(2,1)}, bf16[256,1024]{1,0:T(8,128)(2,1)}, u32[]{:S(2)}, u32[]{:S(2)}) collective-permute-start(bf16[256,1024]{1,0:T(8,128)(2,1)} %collective-permute-done.21), channel_id=1, source_target_pairs={{4,0},{6,2},{5,1},{7,3},{20,16},{22,18},{21,17},{23,19}} | collective-permute-start | bytes 1572872 | tf_op jit(solution)/shard_map/ppermute | solution.py:593
  197.5 13.6 %collective-permute-start.31 = (bf16[256,1024]{1,0:T(8,128)(2,1)}, bf16[256,1024]{1,0:T(8,128)(2,1)}, u32[]{:S(2)}, u32[]{:S(2)}) collective-permute-start(bf16[256,1024]{1,0:T(8,128)(2,1)} %fusion.1.refs_0_), channel_id=1, source_target_pairs={{0,2},{2,0},{4,6},{6,4},{8,10},{10,8},{12,14},{14,12},{1,3},{3,1},... | collective-permute-start | bytes 1572872 | tf_op jit(solution)/shard_map/ppermute | solution.py:586
  211.1 2.5 collective-permute-start.33
  211.2 2.9 %collective-permute-start.34 = (bf16[256,1024]{1,0:T(8,128)(2,1)}, bf16[256,1024]{1,0:T(8,128)(2,1)S(1)}, u32[]{:S(2)}, u32[]{:S(2)}) collective-permute-start(bf16[256,1024]{1,0:T(8,128)(2,1)} %collective-permute-done.31.refs_1_), channel_id=1, source_target_pairs={{0,1},{1,0},{2,3},{3,2},{4,5},{5,4},{6,7},{7,6},{8,9},{9,8},{10,11... | collective-permute-start | bytes 1572872 | tf_op jit(solution)/shard_map/ppermute | solution.py:698
  212.9 2.0 collective-permute-start.35
  213.0 14.4 %collective-permute-start.32 = (bf16[256,1024]{1,0:T(8,128)(2,1)S(1)}, bf16[256,1024]{1,0:T(8,128)(2,1)}, u32[]{:S(2)}, u32[]{:S(2)}) collective-permute-start(bf16[256,1024]{1,0:T(8,128)(2,1)S(1)} %select_select_fusion.1.refs_2_), channel_id=1, source_target_pairs={{0,2},{2,0},{4,6},{6,4},{8,10},{10,8},{12,14},{14,12},{1,3},{3,1},... | collective-permute-start | bytes 1572872 | tf_op jit(solution)/shard_map/ppermute | solution.py:586
  227.4 2.3 collective-permute-start.36
  242.6 14.2 %collective-permute-start.37 = (bf16[512,512]{1,0:T(8,128)(2,1)}, bf16[512,512]{1,0:T(8,128)(2,1)S(1)}, u32[]{:S(2)}, u32[]{:S(2)}) collective-permute-start(bf16[512,512]{1,0:T(8,128)(2,1)} %decode_rows.3), channel_id=1, source_target_pairs={{0,2},{2,0},{4,6},{6,4},{8,10},{10,8},{12,14},{14,12},{1,3},{3,1},... | collective-permute-start | bytes 1572872 | tf_op jit(solution)/shard_map/ppermute | solution.py:749
  251.7 5.2 %copy-start.9 = (f32[512,512]{1,0:T(8,128)S(1)}, f32[512,512]{1,0:T(8,128)}, u32[]{:S(2)}) copy-start(f32[512,512]{1,0:T(8,128)} %decode_rows.2) | copy-start | bytes 3145732
  (10 other events, 14.8 us)

commit v11 on v10

--- a/solution.py
+++ b/solution.py
@@ -194,43 +194,49 @@
     return pl.BlockSpec(shape, lambda *args: (0,) * len(shape))
 
 
-def encode_kernel(ids_ref, q_ref, k_ref, v_ref, extra_ref, near_ref, bias_ref, out_ref):
+def stats_of(ref, heads):
+    long = ref.shape[0]
+    terms = ref[long - EXTRA : long, :].astype(jnp.float32).T
+    return [
+        terms[:, h : h + 1] + terms[:, heads + h : heads + h + 1] + terms[:, 2 * heads + h : 2 * heads + h + 1]
+        for h in range(heads)
+    ]
+
+
+def encode_kernel(count, ids_ref, q_ref, k_ref, v_ref, extra_ref, bias_ref, *refs):
+    out_ref = refs[-1]
     rows, width = q_ref.shape
     tokens = k_ref.shape[0]
     heads = width // HEAD_DIM
     ones = jnp.ones((tokens, LANES), jnp.bfloat16)
-    kinds = [
-        extra_ref[...].astype(jnp.float32)[:1, :tokens],
-        near_ref[tokens:, :].astype(jnp.float32)[:1, :tokens],
-    ]
+    kind = extra_ref[...].astype(jnp.float32)[:1, :tokens]
     lane = lax.broadcasted_iota(jnp.int32, (rows, LANES), 1)
     lse_all = jnp.zeros((rows, LANES), jnp.float32)
+    earlier = stats_of(refs[0], heads) if len(refs) > 1 else None
     for h in range(heads):
         cols = slice(h * HEAD_DIM, (h + 1) * HEAD_DIM)
-        late = slice(width + h * HEAD_DIM, width + (h + 1) * HEAD_DIM)
-        pairs = [
-            (k_ref[:, cols], v_ref[:, cols]),
-            (near_ref[:tokens, cols], near_ref[:tokens, late]),
-        ]
-        top = acc = None
-        for (keys, values), kind in zip(pairs, kinds):
-            bias = jnp.zeros_like(kind)
-            for m in range(bias_ref.shape[0]):
-                bias = jnp.where(kind == m, bias_ref[m, h] * LOG2E, bias)
-            scores = lax.dot_general(q_ref[:, cols], keys, NT, preferred_element_type=jnp.float32)
-            scores = scores * EXP2_SCALE + bias
-            new_top = jnp.max(scores, axis=1, keepdims=True)
-            if top is not None:
-                new_top = jnp.maximum(top, new_top)
-            weights = jnp.exp2(scores - new_top).astype(jnp.bfloat16)
-            summed = jnp.dot(
-                weights, jnp.concatenate([values, ones], axis=1), preferred_element_type=jnp.float32
-            )
-            if top is not None:
-                summed = summed + acc * jnp.exp2(top - new_top)
-            top, acc = new_top, summed
-        totals = acc[:, HEAD_DIM:]
-        out_ref[:rows, cols] = (acc[:, :HEAD_DIM] / totals).astype(jnp.bfloat16)
+        bias = jnp.zeros_like(kind)
+        for m in range(count):
+            bias = jnp.where(kind == m, bias_ref[m, h] * LOG2E, bias)
+        scores = lax.dot_general(
+            q_ref[:, cols], k_ref[:, cols], NT, preferred_element_type=jnp.float32
+        )
+        scores = scores * EXP2_SCALE + bias
+        top = jnp.max(scores, axis=1, keepdims=True)
+        if earlier is not None:
+            top = jnp.maximum(top, earlier[h])
+        weights = jnp.exp2(scores - top).astype(jnp.bfloat16)
+        acc = jnp.dot(
+            weights,
+            jnp.concatenate([v_ref[:, cols], ones], axis=1),
+            preferred_element_type=jnp.float32,
+        )
+        summed, totals = acc[:, :HEAD_DIM], acc[:, HEAD_DIM:]
+        if earlier is not None:
+            fade = jnp.exp2(earlier[h] - top)
+            summed = summed + refs[0][:rows, cols].astype(jnp.float32) * fade
+            totals = totals + fade
+        out_ref[:rows, cols] = (summed / totals).astype(jnp.bfloat16)
         lse_all = jnp.where(lane % heads == h, top + jnp.log2(totals), lse_all)
     lse = lse_all.T[:EXTRA, :]
     high = lse.astype(jnp.bfloat16).astype(jnp.float32)
@@ -241,34 +247,34 @@
     out_ref[rows:, :] = terms.astype(jnp.bfloat16)
 
 
-def encode(which, queries, keys, values, extra, near, bias, rows):
-    tokens = keys.shape[0]
-    width = keys.shape[1] // 2
+def encode(which, queries, keys, values, extra, bias, rows, earlier=None):
+    tokens = extra.shape[1] // 2
+    width = queries.shape[1] // 2
     blocks = queries.shape[0] // rows
-    half = pl.BlockSpec((tokens, width), lambda i, ids: (0, ids[0]))
+    packed = pl.BlockSpec((rows + EXTRA, width), lambda i, ids: (i, 0))
     grid_spec = pltpu.PrefetchScalarGridSpec(
         num_scalar_prefetch=1,
         grid=(blocks,),
         in_specs=[
             pl.BlockSpec((rows, width), lambda i, ids: (i, ids[0])),
-            half,
-            half,
-            whole(extra.shape),
-            whole(near.shape),
+            pl.BlockSpec((tokens, width), lambda i, ids: (0, ids[1])),
+            pl.BlockSpec((tokens, width), lambda i, ids: (0, ids[2])),
+            pl.BlockSpec((EXTRA, extra.shape[1]), lambda i, ids: (ids[3], 0)),
             pl.BlockSpec(memory_space=pltpu.SMEM),
+            *([] if earlier is None else [packed]),
         ],
-        out_specs=pl.BlockSpec((rows + EXTRA, width), lambda i, ids: (i, 0)),
+        out_specs=packed,
     )
     return pl.pallas_call(
-        encode_kernel,
+        functools.partial(encode_kernel, bias.shape[0]),
         grid_spec=grid_spec,
         out_shape=jax.ShapeDtypeStruct((blocks * (rows + EXTRA), width), jnp.bfloat16),
         compiler_params=params(BIG),
         cost_estimate=cost(
-            16 * blocks * rows * tokens * width, 8 * tokens * width, blocks * rows * tokens * 8
+            8 * blocks * rows * tokens * width, 8 * tokens * width, blocks * rows * tokens * 4
         ),
         name="encode_rows",
-    )(which.reshape(1), queries, keys, values, extra, near, bias)
+    )(which, queries, keys, values, extra, bias, *([] if earlier is None else [earlier]))
 
 
 def merge_kernel(count, ids_ref, parts_ref, mine_ref, near_ref, all_ref):
@@ -276,13 +282,10 @@
     long = rows + EXTRA
     parts = [parts_ref.at[i * long : (i + 1) * long, :] for i in range(count)]
     heads = width // HEAD_DIM
-    stats = [v[rows:, :].astype(jnp.float32).T for v in parts]
+    stats = [stats_of(v, heads) for v in parts]
     for h in range(heads):
         cols = slice(h * HEAD_DIM, (h + 1) * HEAD_DIM)
-        lses = [
-            s[:, h : h + 1] + s[:, heads + h : heads + h + 1] + s[:, 2 * heads + h : 2 * heads + h + 1]
-            for s in stats
-        ]
+        lses = [s[h] for s in stats]
         top = functools.reduce(jnp.maximum, lses)
         factors = [jnp.exp2(v - top) for v in lses]
         inverse = 1.0 / functools.reduce(jnp.add, factors)
@@ -411,7 +414,7 @@
 def latents_kernel(pieces, ids_ref, *refs):
     mine, theirs = refs[:pieces], refs[pieces : 2 * pieces]
     w_refs, (out_ref, normed_ref, w_ref) = refs[2 * pieces : -3], refs[-3:]
-    rows, half = mine[0].shape
+    half = mine[0].shape[1]
     slots = ids_ref.shape[0] - 1
     depth = 2 * half // slots
 
@@ -422,10 +425,11 @@
             start = pl.multiple_of((at % (slots // 2)) * depth, depth)
 
             def copy(pieces):
-                for r, piece in enumerate(pieces):
-                    normed_ref[r * rows : (r + 1) * rows, j * depth : (j + 1) * depth] = piece[
-                        :, pl.ds(start, depth)
-                    ]
+                row = 0
+                for piece in pieces:
+                    band = slice(row, row + piece.shape[0])
+                    row += piece.shape[0]
+                    normed_ref[band, j * depth : (j + 1) * depth] = piece[:, pl.ds(start, depth)]
 
             is_mine = at // (slots // 2) == ids_ref[0]
             pl.when(is_mine)(functools.partial(copy, mine))
@@ -443,7 +447,7 @@
 
 def latent_keys_values(ids, mine, theirs, bands):
     pieces = len(mine)
-    rows, half = mine[0].shape
+    rows = sum(v.shape[0] for v in mine)
     width = bands[0].shape[1]
     block = min(512, width)
     total = sum(band.shape[0] for band in bands)
@@ -451,18 +455,18 @@
         num_scalar_prefetch=1,
         grid=(width // block,),
         in_specs=[pl.BlockSpec(memory_space=pltpu.VMEM)] * (2 * pieces + len(bands)),
-        out_specs=pl.BlockSpec((rows * pieces, block), lambda i, ids: (0, i)),
+        out_specs=pl.BlockSpec((rows, block), lambda i, ids: (0, i)),
         scratch_shapes=[
-            pltpu.VMEM((rows * pieces, total), jnp.bfloat16),
+            pltpu.VMEM((rows, total), jnp.bfloat16),
             pltpu.VMEM((total, block), jnp.bfloat16),
         ],
     )
     return pl.pallas_call(
         functools.partial(latents_kernel, pieces),
         grid_spec=grid_spec,
-        out_shape=jax.ShapeDtypeStruct((rows * pieces, width), jnp.bfloat16),
+        out_shape=jax.ShapeDtypeStruct((rows, width), jnp.bfloat16),
         compiler_params=params(24),
-        cost_estimate=cost(2 * rows * pieces * total * width, 2 * total * width),
+        cost_estimate=cost(2 * rows * total * width, 2 * total * width),
         name="latent_keys_values",
     )(ids, *mine, *theirs, *bands)
 
@@ -622,18 +626,26 @@
     out_far = [over_far(out_sent, k) for k in range(1, far)]
     places = [((z + k) % far) * 2 + (y ^ j) for j in range(2) for k in range(far)]
     kv_for_near = columns((w_key, w_value), 1 - y)
-    near_inputs, out_far, kv_for_near = lax.optimization_barrier(
-        (near_inputs, out_far, kv_for_near)
-    )
-    out_far = jnp.concatenate(out_far)
-    out_far_other = over_groups(out_far)
+    head_bias = lax.dynamic_slice_in_dim(enc_bias, y * (heads // 2), heads // 2, 1)
+    which = jnp.stack([y, y, y, 0 * y]).astype(jnp.int32)
+    parts = encode(which, latent_queries, enc_keys, enc_values, extra, head_bias, 2 * rows)
+    near_inputs, out_far, kv_for_near, parts = lax.optimization_barrier(
+        (near_inputs, out_far, kv_for_near, parts)
+    )
 
     kv_own = columns((w_key, w_value), y)
     kv_near = over_near(kv_for_near)
 
-    head_bias = lax.dynamic_slice_in_dim(enc_bias, y * (heads // 2), heads // 2, 1)
+    which = jnp.stack([y, 0 * y, 0 * y + 1, 0 * y + tokens // EXTRA]).astype(jnp.int32)
     parts = encode(
-        y, latent_queries, enc_keys, enc_values, extra, near_inputs, head_bias, 2 * rows
+        which,
+        latent_queries,
+        near_inputs,
+        near_inputs,
+        near_inputs,
+        head_bias,
+        2 * rows,
+        parts,
     )
     kv_near, out_far, parts = lax.optimization_barrier((kv_near, out_far, parts))
     kv_sent = jnp.where(x == 0, kv_own, kv_near)
@@ -641,7 +653,10 @@
     hops[1] = hop(1, hops[0])
     early = [k for k in range(1, far) if max(k, far - k) < 3]
     rest = [k for k in range(1, far) if k not in early]
+    out_far = jnp.concatenate(out_far)
+    out_far_other = over_groups(out_far)
     out_near = over_near(jnp.concatenate([w_out, counted, out_far]))
+    out_near, hops = lax.optimization_barrier((out_near, hops))
     out_near_other = over_groups(out_near[w_out.shape[0] + EXTRA :])
     columns_of_slice = [[2 * i + j for i in range(far)] for j in range(2)]
     parts = lax.all_to_all(parts, "pos", 0, 0, axis_index_groups=columns_of_slice, tiled=True)
@@ -724,8 +739,7 @@
         fresh_near = over_near(fresh)
         if step + 1 < far:
             came[step + 1] = hop(step + 1, came[step])
-            k = rest[step - 1]
-            kv_moved = by_shift(hops, k)
+            kv_moved = by_shift(hops, rest[step - 1])
             kv_bands += [kv_moved, over_groups(kv_moved)]
             if step > 1:
                 keys_values.append(fold(mine, other))
@@ -736,17 +750,17 @@
                 )
             )
             if step == 1:
-                mine += [fresh, fresh_near]
-                other += cores(mine[1:])
+                mine = [normed, jnp.concatenate([normed_near, fresh, fresh_near])]
+                other = [normed_other, *cores(mine[1:])]
             else:
                 mine += [fresh, fresh_near]
-                other += cores([fresh, fresh_near])
-    keys_values.append(fold([*mine, fresh], [*other, *cores([fresh])]))
+    mine = [jnp.concatenate([*mine, fresh])]
+    keys_values.append(fold(mine, cores(mine)))
     fresh_near, keys_values = lax.optimization_barrier((fresh_near, keys_values))
     keys_values.append(fold([fresh_near], cores([fresh_near])))
     near_state = decode(near_queries, keys_values, jnp.bfloat16)
     own_state = decode(own_queries, keys_values, jnp.float32)
-    from_near = lax.ppermute(near_state, "pos", near).astype(jnp.float32)
+    from_near = over_near(near_state).astype(jnp.float32)
     decoded = jnp.where(
         y == 0,
         jnp.concatenate([own_state, from_near], axis=1),

time: 260 us -> 283 us (1.088)
  waiting for transfers between devices: 107 us -> 117 us
  Pallas kernels: 62.1 us -> 71.4 us
  local copies, waits for them, and re-layouts: 18.4 us -> 25.1 us
  starting transfers between devices: 54.3 us -> 50.4 us
    ppermute x12, waiting for transfers between devices: 30.8 us -> 68.1 us  [hop(): lax.ppermute(v, 'pos', hop_perm(pos, step, way))]
    ppermute x9 -> x10, waiting for transfers between devices: 40.8 us -> 25 us  [over_near(): return lax.ppermute(value, 'pos', near)]
    ppermute x3, waiting for transfers between devices: 20.4 us -> 9.98 us  [over_far(): return lax.ppermute(value, 'pos', shift_perm(pos, k))]
    pallas_call x1 -> x2, Pallas kernels: 14.4 us -> 24.7 us  [encode(): pl.pallas_call(functools.partial(encode_kernel, bias.shape[0]), grid_spec...]
    unnamed x41 -> x67, local copies, waits for them, and re-layouts: 9.25 us -> 16 us
    ppermute x1 -> x0, waiting for transfers between devices: 5.09 us -> none  [fast_on_device(): from_near = lax.ppermute(near_state, 'pos', near).astype(jnp.float32)]
    ppermute x9 -> x10, starting transfers between devices: 13.6 us -> 12 us  [over_near(): return lax.ppermute(value, 'pos', near)]
  transfers between devices with their start and end apart: 39 -> 35, of which waited for: 18 -> 15; matrix products, arithmetic and copies ran while one was open for 9% -> 8% of each run, Pallas kernels for 19% -> 20%
where the time goes in v11:
time: 283 us; the launch traced here: 281 us
  waiting for transfers between devices  117 us (41%)
  Pallas kernels  71.4 us (25%)
  starting transfers between devices  50.4 us (18%)
  local copies, waits for them, and re-layouts  25.1 us (9%)
  other arithmetic  15.9 us (6%)
    ppermute x12, waiting for transfers between devices, hop(): lax.ppermute(v, 'pos', hop_perm(pos, step, way))  68.1 us
    ppermute x10, waiting for transfers between devices, over_near(): return lax.ppermute(value, 'pos', near)  25 us
    pallas_call x2, Pallas kernels, encode(): pl.pallas_call(functools.partial(encode_kernel, bias.shape[0]), grid_spec...  24.7 us
    ppermute x12, starting transfers between devices, hop(): lax.ppermute(v, 'pos', hop_perm(pos, step, way))  22.9 us
    pallas_call x3, Pallas kernels, latent_keys_values(): pl.pallas_call(functools.partial(latents_kernel, pieces), grid_spec=grid_...  17.9 us
    pallas_call x2, Pallas kernels, decode(): pl.pallas_call(functools.partial(decode_kernel, len(keys_values)), grid=(...  16.7 us
    unnamed x67, local copies, waits for them, and re-layouts  16 us
    ppermute x10, starting transfers between devices, over_near(): return lax.ppermute(value, 'pos', near)  12 us
  transfers between devices with their start and end apart: 35, of which 15 were waited for; matrix products, arithmetic and copies ran while one was open for 8% of the time, Pallas kernels for 20%

profile of v11, /device:TPU:0, one launch (start us, length us, event | category | flops | bytes accessed | tf_op | source)
XLA Modules:
  0.0 281.0 jit_solution(134621879187164997)
XLA Ops:
  1.4 1.3 constant_dynamic-slice_fusion.8
  2.9 3.0 %collective-permute-start = (bf16[528,1024]{1,0:T(8,128)(2,1)S(1)}, bf16[528,1024]{1,0:T(8,128)(2,1)}, u32[]{:S(2)}, u32[]{:S(2)}) collective-permute-start(bf16[528,1024]{1,0:T(8,128)(2,1)S(1)} %pad_maximum_fusion.1), channel_id=1, source_target_pairs={{0,2},{2,0},{4,6},{6,4},{8,10},{10,8},{12,14},{14,12},{1,3},{3,1},... | collective-permute-start | bytes 3244040 | tf_op jit(solution)/shard_map/ppermute | solution.py:590
  8.3 3.6 %collective-permute-start.1 = (bf16[528,256]{1,0:T(8,128)(2,1)}, bf16[528,256]{1,0:T(8,128)(2,1)}, u32[]{:S(2)}, u32[]{:S(2)}) collective-permute-start(bf16[528,256]{1,0:T(8,128)(2,1)} %pad_maximum_fusion.4), channel_id=1, source_target_pairs={{4,0},{6,2},{8,4},{10,6},{12,8},{14,10},{0,12},{2,14},{5,1},{7,3},... | collective-permute-start | bytes 811016 | tf_op jit(solution)/shard_map/ppermute | solution.py:593
  15.1 9.9 %encode_rows.2.refs_0_ = bf16[2112,512]{1,0:T(8,128)(2,1)} custom-call(s32[4]{0:T(128)} %pad_add_fusion.ids_ref, bf16[2048,1024]{1,0:T(8,128)(2,1)} %q_ref.3, bf16[512,1024]{1,0:T(8,128)(2,1)} %k_ref.1, bf16[512,1024]{1,0:T(8,128)(2,1)} %v_ref.1, bf16[16,1024]{1,0:T(8,128)(2,1)} %copy-done.25, f32[3,4]{1,0:T(4,128)} %constant_dynamic-slice_fusion.4.bias_ref), custom_call_target="tpu_custom_call" | custom-call | flops 4294967296 | bytes 2097152 | tf_op jit(solution)/shard_map/encode_rows/pallas_call | solution.py:268
  25.0 10.0 %collective-permute-done.2 = bf16[528,256]{1,0:T(8,128)(2,1)} collective-permute-done((bf16[528,256]{1,0:T(8,128)(2,1)}, bf16[528,256]{1,0:T(8,128)(2,1)}, u32[]{:S(2)}, u32[]{:S(2)}) %collective-permute-start.2) | collective-permute-done | bytes 270368 | tf_op jit(solution)/shard_map/ppermute | solution.py:593
  36.7 14.8 %encode_rows.3 = bf16[2112,512]{1,0:T(8,128)(2,1)} custom-call(s32[4]{0:T(128)} %pad_add_fusion.1.ids_ref, bf16[2048,1024]{1,0:T(8,128)(2,1)} %q_ref.3, bf16[528,1024]{1,0:T(8,128)(2,1)} %collective-permute-done.k_ref.v_ref.extra_ref, bf16[528,1024]{1,0:T(8,128)(2,1)} %collective-permute-done.k_ref.v_ref.extra_ref, ...), custom_call_target="tpu_custom_call" | custom-call | flops 4294967296 | bytes 2097152 | tf_op jit(solution)/shard_map/encode_rows/pallas_call | solution.py:268
  51.6 3.9 %all-to-all-start = ((bf16[4,528,512]{2,1,0:T(8,128)(2,1)}), bf16[4,528,512]{2,1,0:T(8,128)(2,1)S(1)}, u32[]{:S(2)}, u32[]{:S(2)}) async-start(bf16[4,528,512]{2,1,0:T(8,128)(2,1)} %bitcast.51), calls=%async_computation | async-start | bytes 4325376 | tf_op jit(solution)/shard_map/all_to_all | solution.py:662
  55.5 1.8 constant_dynamic-update-slice_fusion.7
  57.3 1.8 constant_dynamic-update-slice_fusion.6
  62.2 4.7 %collective-permute-start.6 = (bf16[256,1024]{1,0:T(8,128)(2,1)S(1)}, bf16[256,1024]{1,0:T(8,128)(2,1)}, u32[]{:S(2)}, u32[]{:S(2)}) collective-permute-start(bf16[256,1024]{1,0:T(8,128)(2,1)S(1)} %get-tuple-element.159), channel_id=1, source_target_pairs={{0,4},{2,6},{4,8},{6,10},{8,12},{10,14},{1,5},{3,7},{5,9},{7,11},{... | collective-permute-start | bytes 1572872 | tf_op jit(solution)/shard_map/ppermute | solution.py:597
  66.9 1.3 collective-permute-start.7
  68.2 1.6 collective-permute-start.8
  69.8 31.0 %collective-permute-done.6 = bf16[256,1024]{1,0:T(8,128)(2,1)} collective-permute-done((bf16[256,1024]{1,0:T(8,128)(2,1)S(1)}, bf16[256,1024]{1,0:T(8,128)(2,1)}, u32[]{:S(2)}, u32[]{:S(2)}) %collective-permute-start.6) | collective-permute-done | bytes 524320 | tf_op jit(solution)/shard_map/ppermute | solution.py:597
  102.0 1.6 collective-permute-start.9
  105.9 10.6 %collective-permute-done.10.q_ref = bf16[512,512]{1,0:T(8,128)(2,1)S(1)} collective-permute-done((bf16[512,512]{1,0:T(8,128)(2,1)S(1)}, bf16[512,512]{1,0:T(8,128)(2,1)S(1)}, u32[]{:S(2)}, u32[]{:S(2)}) %collective-permute-start.10) | collective-permute-done | bytes 524320 | tf_op jit(solution)/shard_map/ppermute | solution.py:590
  118.2 1.9 collective-permute-done.9.refs_4_
  120.2 1.9 merge_rows.1
  123.4 1.3 collective-permute-start.13
  126.4 4.8 %collective-permute-done.11.near_ref = bf16[256,512]{1,0:T(8,128)(2,1)S(1)} collective-permute-done((bf16[256,512]{1,0:T(8,128)(2,1)S(1)}, bf16[256,512]{1,0:T(8,128)(2,1)S(1)}, u32[]{:S(2)}, u32[]{:S(2)}) %collective-permute-start.11) | collective-permute-done | bytes 262176 | tf_op jit(solution)/shard_map/ppermute | solution.py:590
  131.9 5.7 %project_rows.1.mine_ref = f32[256,2048]{1,0:T(8,128)} custom-call(s32[10]{0:T(128)} %stack.92.ids_ref, bf16[256,512]{1,0:T(8,128)(2,1)} %copy-done.6, bf16[256,512]{1,0:T(8,128)(2,1)} %copy-done.24, bf16[1024,256]{1,0:T(8,128)(2,1)} %refs_0_.1, bf16[1584,256]{1,0:T(8,128)(2,1)} %get-tuple-element.164.refs_1_, bf16[1584,256]{1,0:T(8,128)(2,1)} %copy-done.19, ...), custom_call_target="tpu_custom_call" | custom-call | flops 1073741824 | bytes 6291456 | tf_op jit(solution)/shard_map/project_rows/pallas_call | solution.py:366
  137.6 15.2 %collective-permute-done.13 = bf16[256,1024]{1,0:T(8,128)(2,1)S(1)} collective-permute-done((bf16[256,1024]{1,0:T(8,128)(2,1)}, bf16[256,1024]{1,0:T(8,128)(2,1)S(1)}, u32[]{:S(2)}, u32[]{:S(2)}) %collective-permute-start.13) | collective-permute-done | bytes 524320 | tf_op jit(solution)/shard_map/ppermute | solution.py:597
  154.2 1.5 collective-permute-start.17
  155.7 1.3 collective-permute-start.18
  157.0 1.6 collective-permute-start.19
  158.6 4.6 %norm_rows.1 = (f32[256,1024]{1,0:T(8,128)}, bf16[256,1024]{1,0:T(8,128)(2,1)}, bf16[256,1024]{1,0:T(8,128)(2,1)}) custom-call(s32[1]{0:T(128)} %bitcast.ids_ref, f32[256,2048]{1,0:T(8,128)} %project_rows.1.mine_ref, f32[256,2048]{1,0:T(8,128)} %collective-permute-done.14.theirs_ref, bf16[256,2048]{1,0:T(8,128)(2,1)} %latent_ref.1, f32[1,2048]{1,0:T(1,128)} %bitcast.53), custom_call_target="tpu_custom_call" | custom-call | flops 3145728 | bytes 6815744 | tf_op jit(solution)/shard_map/norm_rows/pallas_call | solution.py:400
  163.2 6.2 %collective-permute-start.15 = (bf16[256,1024]{1,0:T(8,128)(2,1)}, bf16[256,1024]{1,0:T(8,128)(2,1)}, u32[]{:S(2)}, u32[]{:S(2)}) collective-permute-start(bf16[256,1024]{1,0:T(8,128)(2,1)} %get-tuple-element.103.refs_0_), channel_id=1, source_target_pairs={{0,4},{2,6},{4,8},{6,10},{8,12},{10,14},{1,5},{3,7},{5,9},{7,11},{... | collective-permute-start | bytes 1572872 | tf_op jit(solution)/shard_map/ppermute | solution.py:597
  169.4 1.3 collective-permute-start.16
  173.4 6.9 %collective-permute-done.15 = bf16[256,1024]{1,0:T(8,128)(2,1)} collective-permute-done((bf16[256,1024]{1,0:T(8,128)(2,1)}, bf16[256,1024]{1,0:T(8,128)(2,1)}, u32[]{:S(2)}, u32[]{:S(2)}) %collective-permute-start.15) | collective-permute-done | bytes 524320 | tf_op jit(solution)/shard_map/ppermute | solution.py:597
  180.3 5.0 %collective-permute-done.16 = bf16[256,1024]{1,0:T(8,128)(2,1)} collective-permute-done((bf16[256,1024]{1,0:T(8,128)(2,1)}, bf16[256,1024]{1,0:T(8,128)(2,1)}, u32[]{:S(2)}, u32[]{:S(2)}) %collective-permute-start.16) | collective-permute-done | bytes 524320 | tf_op jit(solution)/shard_map/ppermute | solution.py:597
  186.0 1.3 collective-permute-start.21
  192.0 10.0 %collective-permute-done.21 = bf16[256,1024]{1,0:T(8,128)(2,1)S(1)} collective-permute-done((bf16[256,1024]{1,0:T(8,128)(2,1)}, bf16[256,1024]{1,0:T(8,128)(2,1)S(1)}, u32[]{:S(2)}, u32[]{:S(2)}) %collective-permute-start.21) | collective-permute-done | bytes 524320 | tf_op jit(solution)/shard_map/ppermute | solution.py:597
  205.5 1.6 collective-permute-start.27
  207.1 1.5 collective-permute-start.25
  208.5 1.3 collective-permute-start.26
  209.8 2.1 fusion.1
  213.0 7.0 %collective-permute-done.27.refs_11_.refs_9_ = bf16[256,1024]{1,0:T(8,128)(2,1)} collective-permute-done((bf16[256,1024]{1,0:T(8,128)(2,1)S(1)}, bf16[256,1024]{1,0:T(8,128)(2,1)}, u32[]{:S(2)}, u32[]{:S(2)}) %collective-permute-start.27) | collective-permute-done | bytes 524320 | tf_op jit(solution)/shard_map/ppermute | solution.py:587
  223.1 8.3 %latent_keys_values.3.refs_0_.refs_3_ = bf16[1024,1024]{1,0:T(8,128)(2,1)S(1)} custom-call(s32[9]{0:T(128)S(1)} %stack.104.ids_ref, bf16[256,1024]{1,0:T(8,128)(2,1)S(1)} %copy-done.7, bf16[768,1024]{1,0:T(8,128)(2,1)} %constant_dynamic-update-slice_fusion.8.refs_1_, bf16[256,1024]{1,0:T(8,128)(2,1)S(1)} %copy-done.8, ...), custom_call_target="tpu_custom_call" | custom-call | flops 4294967296 | bytes 4194304 | tf_op jit(solution)/shard_map/latent_keys_values/pallas_call | solution.py:464
  231.5 1.6 select_select_fusion.1
  233.2 1.4 pad_maximum_fusion.refs_0_
  235.6 2.4 collective-permute-done.31.refs_1_
  238.0 5.9 %latent_keys_values.4.refs_1_.refs_4_ = bf16[768,1024]{1,0:T(8,128)(2,1)S(1)} custom-call(s32[9]{0:T(128)S(1)} %stack.104.ids_ref, bf16[768,1024]{1,0:T(8,128)(2,1)S(1)} %pad_maximum_fusion.refs_0_, bf16[768,1024]{1,0:T(8,128)(2,1)S(1)} %collective-permute-done.31.refs_1_, bf16[256,1024]{1,0:T(8,128)(2,1)S(1)} %get-tuple-element.138.refs_4_.refs_2_, ...), custom_call_target="tpu_custom_call" | custom-call | flops 3221225472 | bytes 4194304 | tf_op jit(solution)/shard_map/latent_keys_values/pallas_call | solution.py:464
  245.1 4.0 %collective-permute-done.30.refs_0_ = bf16[256,1024]{1,0:T(8,128)(2,1)} collective-permute-done((bf16[256,1024]{1,0:T(8,128)(2,1)S(1)}, bf16[256,1024]{1,0:T(8,128)(2,1)}, u32[]{:S(2)}, u32[]{:S(2)}) %collective-permute-start.30) | collective-permute-done | bytes 524320 | tf_op jit(solution)/shard_map/ppermute | solution.py:590
  249.1 2.2 collective-permute-done.32.refs_1_
  252.4 3.7 %latent_keys_values.5.refs_2_.refs_5_ = bf16[256,1024]{1,0:T(8,128)(2,1)S(1)} custom-call(s32[9]{0:T(128)S(1)} %stack.104.ids_ref, bf16[256,1024]{1,0:T(8,128)(2,1)} %collective-permute-done.30.refs_0_, bf16[256,1024]{1,0:T(8,128)(2,1)} %collective-permute-done.32.refs_1_, bf16[256,1024]{1,0:T(8,128)(2,1)S(1)} %get-tuple-element.138.refs_4_.refs_2_, ...), custom_call_target="tpu_custom_call" | custom-call | flops 1073741824 | bytes 4194304 | tf_op jit(solution)/shard_map/latent_keys_values/pallas_call | solution.py:464
  256.8 8.3 %decode_rows.3 = bf16[512,512]{1,0:T(8,128)(2,1)} custom-call(bf16[512,512]{1,0:T(8,128)(2,1)} %copy-done.29, bf16[1024,1024]{1,0:T(8,128)(2,1)} %copy-done.10, bf16[768,1024]{1,0:T(8,128)(2,1)} %copy-done.9, bf16[256,1024]{1,0:T(8,128)(2,1)} %copy-done.5, bf16[1024,1024]{1,0:T(8,128)(2,1)} %copy-done.10, bf16[768,1024]{1,0:T(8,128)(2,1)} %copy-done.9, ...), custom_call_target="tpu_custom_call" | custom-call | flops 8589934592 | bytes 5767168 | tf_op jit(solution)/shard_map/decode_rows/pallas_call | solution.py:525
  266.0 8.4 %decode_rows.2 = f32[512,512]{1,0:T(8,128)} custom-call(bf16[512,512]{1,0:T(8,128)(2,1)} %get-tuple-element.156.q_ref, bf16[1024,1024]{1,0:T(8,128)(2,1)} %copy-done.10, bf16[768,1024]{1,0:T(8,128)(2,1)} %copy-done.9, bf16[256,1024]{1,0:T(8,128)(2,1)} %copy-done.5, bf16[1024,1024]{1,0:T(8,128)(2,1)} %copy-done.10, bf16[768,1024]{1,0:T(8,128)(2,1)} %copy-done.9, ...), custom_call_target="tpu_custom_call" | custom-call | flops 8589934592 | bytes 5767168 | tf_op jit(solution)/shard_map/decode_rows/pallas_call | solution.py:525
  274.4 4.9 %collective-permute-done.33 = bf16[512,512]{1,0:T(8,128)(2,1)S(1)} collective-permute-done((bf16[512,512]{1,0:T(8,128)(2,1)}, bf16[512,512]{1,0:T(8,128)(2,1)S(1)}, u32[]{:S(2)}, u32[]{:S(2)}) %collective-permute-start.33) | collective-permute-done | bytes 524320 | tf_op jit(solution)/shard_map/ppermute | solution.py:590
  279.4 1.6 fusion
  (145 shorter events, 42.6 us)
Async XLA Ops:
  0.6 102.9 %copy-start = (bf16[3,1024]{1,0:T(4,128)(2,1)S(1)}, bf16[3,1024]{1,0:T(4,128)(2,1)}, u32[]{:S(2)}) copy-start(bf16[3,1024]{1,0:T(4,128)(2,1)} %param.25) | copy-start | bytes 18436
  2.7 4.1 %copy-start.26 = (s32[512]{0:T(512)S(1)}, s32[512]{0:T(512)}, u32[]{:S(2)}) copy-start(s32[512]{0:T(512)} %param.24) | copy-start | bytes 6148
  2.8 10.7 %copy-start.27 = (f32[3,8]{1,0:T(4,128)S(1)}, f32[3,8]{1,0:T(4,128)}, u32[]{:S(2)}) copy-start(f32[3,8]{1,0:T(4,128)} %param.26) | copy-start | bytes 292
  2.9 11.3 %copy-start.20 = (bf16[256,1024]{1,0:T(8,128)(2,1)S(1)}, bf16[256,1024]{1,0:T(8,128)(2,1)}, u32[]{:S(2)}) copy-start(bf16[256,1024]{1,0:T(8,128)(2,1)} %param.22) | copy-start | bytes 1572868
  2.9 11.3 %copy-start.21 = (bf16[256,1024]{1,0:T(8,128)(2,1)S(1)}, bf16[256,1024]{1,0:T(8,128)(2,1)}, u32[]{:S(2)}) copy-start(bf16[256,1024]{1,0:T(8,128)(2,1)} %param.21) | copy-start | bytes 1572868
  2.9 32.1 %collective-permute-start = (bf16[528,1024]{1,0:T(8,128)(2,1)S(1)}, bf16[528,1024]{1,0:T(8,128)(2,1)}, u32[]{:S(2)}, u32[]{:S(2)}) collective-permute-start(bf16[528,1024]{1,0:T(8,128)(2,1)S(1)} %pad_maximum_fusion.1), channel_id=1, source_target_pairs={{0,2},{2,0},{4,6},{6,4},{8,10},{10,8},{12,14},{14,12},{1,3},{3,1},... | collective-permute-start | bytes 3244040 | tf_op jit(solution)/shard_map/ppermute | solution.py:590
  8.3 16.7 %collective-permute-start.1 = (bf16[528,256]{1,0:T(8,128)(2,1)}, bf16[528,256]{1,0:T(8,128)(2,1)}, u32[]{:S(2)}, u32[]{:S(2)}) collective-permute-start(bf16[528,256]{1,0:T(8,128)(2,1)} %pad_maximum_fusion.4), channel_id=1, source_target_pairs={{4,0},{6,2},{8,4},{10,6},{12,8},{14,10},{0,12},{2,14},{5,1},{7,3},... | collective-permute-start | bytes 811016 | tf_op jit(solution)/shard_map/ppermute | solution.py:593
  11.9 23.0 %collective-permute-start.2 = (bf16[528,256]{1,0:T(8,128)(2,1)}, bf16[528,256]{1,0:T(8,128)(2,1)}, u32[]{:S(2)}, u32[]{:S(2)}) collective-permute-start(bf16[528,256]{1,0:T(8,128)(2,1)} %pad_maximum_fusion.4), channel_id=1, source_target_pairs={{8,0},{10,2},{12,4},{14,6},{0,8},{2,10},{4,12},{6,14},{9,1},{11,3}... | collective-permute-start | bytes 811016 | tf_op jit(solution)/shard_map/ppermute | solution.py:593
  11.9 23.0 %collective-permute-start.3 = (bf16[528,256]{1,0:T(8,128)(2,1)}, bf16[528,256]{1,0:T(8,128)(2,1)S(1)}, u32[]{:S(2)}, u32[]{:S(2)}) collective-permute-start(bf16[528,256]{1,0:T(8,128)(2,1)} %pad_maximum_fusion.4), channel_id=1, source_target_pairs={{12,0},{14,2},{0,4},{2,6},{4,8},{6,10},{8,12},{10,14},{13,1},{15,3... | collective-permute-start | bytes 811016 | tf_op jit(solution)/shard_map/ppermute | solution.py:593
  35.0 16.6 %copy-start.22 = (bf16[528,256]{1,0:T(8,128)(2,1)}, bf16[528,256]{1,0:T(8,128)(2,1)S(1)}, u32[]{:S(2)}) copy-start(bf16[528,256]{1,0:T(8,128)(2,1)S(1)} %collective-permute-done.3) | copy-start | bytes 811012
  35.0 16.6 %collective-permute-start.4 = (bf16[256,1024]{1,0:T(8,128)(2,1)S(1)}, bf16[256,1024]{1,0:T(8,128)(2,1)S(1)}, u32[]{:S(2)}, u32[]{:S(2)}) collective-permute-start(bf16[256,1024]{1,0:T(8,128)(2,1)S(1)} %pad_maximum_fusion.2), channel_id=1, source_target_pairs={{0,2},{2,0},{4,6},{6,4},{8,10},{10,8},{12,14},{14,12},{1,3},{3,1},... | collective-permute-start | bytes 1572872 | tf_op jit(solution)/shard_map/ppermute | solution.py:590
  51.6 68.6 %all-to-all-start = ((bf16[4,528,512]{2,1,0:T(8,128)(2,1)}), bf16[4,528,512]{2,1,0:T(8,128)(2,1)S(1)}, u32[]{:S(2)}, u32[]{:S(2)}) async-start(bf16[4,528,512]{2,1,0:T(8,128)(2,1)} %bitcast.51), calls=%async_computation | async-start | bytes 4325376 | tf_op jit(solution)/shard_map/all_to_all | solution.py:662
  55.5 5.4 %copy-start.18 = (bf16[256,512]{1,0:T(8,128)(2,1)S(1)}, bf16[256,512]{1,0:T(8,128)(2,1)}, u32[]{:S(2)}) copy-start(bf16[256,512]{1,0:T(8,128)(2,1)} %get-tuple-element.162) | copy-start | bytes 786436
  59.9 40.9 %collective-permute-start.5 = (bf16[2624,256]{1,0:T(8,128)(2,1)}, bf16[2624,256]{1,0:T(8,128)(2,1)}, u32[]{:S(2)}, u32[]{:S(2)}) collective-permute-start(bf16[2624,256]{1,0:T(8,128)(2,1)} %get-tuple-element.165), channel_id=1, source_target_pairs={{0,2},{2,0},{4,6},{6,4},{8,10},{10,8},{12,14},{14,12},{1,3},{3,1},... | collective-permute-start | bytes 4030472 | tf_op jit(solution)/shard_map/ppermute | solution.py:590
  60.9 42.6 %copy-start.17 = (bf16[512,1024]{1,0:T(8,128)(2,1)S(1)}, bf16[512,1024]{1,0:T(8,128)(2,1)}, u32[]{:S(2)}) copy-start(bf16[512,1024]{1,0:T(8,128)(2,1)} %param.23) | copy-start | bytes 3145732
  62.2 38.6 %collective-permute-start.6 = (bf16[256,1024]{1,0:T(8,128)(2,1)S(1)}, bf16[256,1024]{1,0:T(8,128)(2,1)}, u32[]{:S(2)}, u32[]{:S(2)}) collective-permute-start(bf16[256,1024]{1,0:T(8,128)(2,1)S(1)} %get-tuple-element.159), channel_id=1, source_target_pairs={{0,4},{2,6},{4,8},{6,10},{8,12},{10,14},{1,5},{3,7},{5,9},{7,11},{... | collective-permute-start | bytes 1572872 | tf_op jit(solution)/shard_map/ppermute | solution.py:597
  66.9 33.9 %collective-permute-start.7 = (bf16[256,1024]{1,0:T(8,128)(2,1)S(1)}, bf16[256,1024]{1,0:T(8,128)(2,1)}, u32[]{:S(2)}, u32[]{:S(2)}) collective-permute-start(bf16[256,1024]{1,0:T(8,128)(2,1)S(1)} %get-tuple-element.159), channel_id=1, source_target_pairs={{12,8},{14,10},{8,4},{10,6},{4,0},{6,2},{13,9},{15,11},{9,5},{11,7... | collective-permute-start | bytes 1572872 | tf_op jit(solution)/shard_map/ppermute | solution.py:597
  68.2 48.3 %collective-permute-start.8 = (bf16[1584,256]{1,0:T(8,128)(2,1)}, bf16[1584,256]{1,0:T(8,128)(2,1)S(1)}, u32[]{:S(2)}, u32[]{:S(2)}) collective-permute-start(bf16[1584,256]{1,0:T(8,128)(2,1)} %get-tuple-element.164.refs_1_), channel_id=1, source_target_pairs={{0,16},{16,0},{1,17},{17,1},{2,18},{18,2},{3,19},{19,3},{4,20},{20... | collective-permute-start | bytes 2433032 | tf_op jit(solution)/shard_map/ppermute | solution.py:587
  102.0 18.2 %collective-permute-start.9 = (bf16[1584,256]{1,0:T(8,128)(2,1)S(1)}, bf16[1584,256]{1,0:T(8,128)(2,1)}, u32[]{:S(2)}, u32[]{:S(2)}) collective-permute-start(bf16[1584,256]{1,0:T(8,128)(2,1)S(1)} %slice.48), channel_id=1, source_target_pairs={{0,16},{16,0},{1,17},{17,1},{2,18},{18,2},{3,19},{19,3},{4,20},{20... | collective-permute-start | bytes 2433032 | tf_op jit(solution)/shard_map/ppermute | solution.py:587
  104.9 11.6 %collective-permute-start.10 = (bf16[512,512]{1,0:T(8,128)(2,1)S(1)}, bf16[512,512]{1,0:T(8,128)(2,1)S(1)}, u32[]{:S(2)}, u32[]{:S(2)}) collective-permute-start(bf16[512,512]{1,0:T(8,128)(2,1)S(1)} %get-tuple-element.157), channel_id=1, source_target_pairs={{0,2},{2,0},{4,6},{6,4},{8,10},{10,8},{12,14},{14,12},{1,3},{3,1},... | collective-permute-start | bytes 1572872 | tf_op jit(solution)/shard_map/ppermute | solution.py:590
  122.7 14.8 %collective-permute-start.12 = (bf16[256,1024]{1,0:T(8,128)(2,1)}, bf16[256,1024]{1,0:T(8,128)(2,1)S(1)}, u32[]{:S(2)}, u32[]{:S(2)}) collective-permute-start(bf16[256,1024]{1,0:T(8,128)(2,1)} %collective-permute-done.6), channel_id=1, source_target_pairs={{4,8},{6,10},{8,12},{10,14},{5,9},{7,11},{9,13},{11,15},{20,24},{2... | collective-permute-start | bytes 1572872 | tf_op jit(solution)/shard_map/ppermute | solution.py:597
  123.4 29.3 %collective-permute-start.13 = (bf16[256,1024]{1,0:T(8,128)(2,1)}, bf16[256,1024]{1,0:T(8,128)(2,1)S(1)}, u32[]{:S(2)}, u32[]{:S(2)}) collective-permute-start(bf16[256,1024]{1,0:T(8,128)(2,1)} %collective-permute-done.7), channel_id=1, source_target_pairs={{8,4},{10,6},{4,0},{6,2},{9,5},{11,7},{5,1},{7,3},{24,20},{26,22},... | collective-permute-start | bytes 1572872 | tf_op jit(solution)/shard_map/ppermute | solution.py:597
  124.7 6.4 %collective-permute-start.11 = (bf16[256,512]{1,0:T(8,128)(2,1)S(1)}, bf16[256,512]{1,0:T(8,128)(2,1)S(1)}, u32[]{:S(2)}, u32[]{:S(2)}) collective-permute-start(bf16[256,512]{1,0:T(8,128)(2,1)S(1)} %get-tuple-element.95), channel_id=1, source_target_pairs={{0,2},{2,0},{4,6},{6,4},{8,10},{10,8},{12,14},{14,12},{1,3},{3,1},... | collective-permute-start | bytes 786440 | tf_op jit(solution)/shard_map/ppermute | solution.py:590
  152.7 5.9 %collective-permute-start.14 = (f32[256,2048]{1,0:T(8,128)}, f32[256,2048]{1,0:T(8,128)}, u32[]{:S(2)}, u32[]{:S(2)}) collective-permute-start(f32[256,2048]{1,0:T(8,128)} %project_rows.1.mine_ref), channel_id=1, source_target_pairs={{0,1},{1,0},{2,3},{3,2},{4,5},{5,4},{6,7},{7,6},{8,9},{9,8},{10,11... | collective-permute-start | bytes 6291464 | tf_op jit(solution)/shard_map/ppermute | solution.py:703
  154.2 18.1 %collective-permute-start.17 = (bf16[256,1024]{1,0:T(8,128)(2,1)S(1)}, bf16[256,1024]{1,0:T(8,128)(2,1)}, u32[]{:S(2)}, u32[]{:S(2)}) collective-permute-start(bf16[256,1024]{1,0:T(8,128)(2,1)S(1)} %collective-permute-done.12), channel_id=1, source_target_pairs={{8,12},{10,14},{9,13},{11,15},{24,28},{26,30},{25,29},{27,31}} | collective-permute-start | bytes 1572872 | tf_op jit(solution)/shard_map/ppermute | solution.py:597
  155.7 17.7 %collective-permute-start.18 = (bf16[256,1024]{1,0:T(8,128)(2,1)S(1)}, bf16[256,1024]{1,0:T(8,128)(2,1)}, u32[]{:S(2)}, u32[]{:S(2)}) collective-permute-start(bf16[256,1024]{1,0:T(8,128)(2,1)S(1)} %collective-permute-done.13), channel_id=1, source_target_pairs={{4,0},{6,2},{5,1},{7,3},{20,16},{22,18},{21,17},{23,19}} | collective-permute-start | bytes 1572872 | tf_op jit(solution)/shard_map/ppermute | solution.py:597
  157.0 16.4 %collective-permute-start.19 = (bf16[256,1024]{1,0:T(8,128)(2,1)S(1)}, bf16[256,1024]{1,0:T(8,128)(2,1)S(1)}, u32[]{:S(2)}, u32[]{:S(2)}) collective-permute-start(bf16[256,1024]{1,0:T(8,128)(2,1)S(1)} %broadcast_select_fusion.3.refs_6_.refs_4_), channel_id=1, source_target_pairs={{0,16},{16,0},{1,17},{17,1},{2,18},{18,2},{3,19},{19,3},{4,20},{20... | collective-permute-start | bytes 1572872 | tf_op jit(solution)/shard_map/ppermute | solution.py:587
  158.6 13.6 %copy-start.28 = (s32[3]{0:T(128)S(1)}, s32[3]{0:T(128)}, u32[]{:S(2)}) copy-start(s32[3]{0:T(128)} %param.27) | copy-start | bytes 40
  163.2 17.2 %collective-permute-start.15 = (bf16[256,1024]{1,0:T(8,128)(2,1)}, bf16[256,1024]{1,0:T(8,128)(2,1)}, u32[]{:S(2)}, u32[]{:S(2)}) collective-permute-start(bf16[256,1024]{1,0:T(8,128)(2,1)} %get-tuple-element.103.refs_0_), channel_id=1, source_target_pairs={{0,4},{2,6},{4,8},{6,10},{8,12},{10,14},{1,5},{3,7},{5,9},{7,11},{... | collective-permute-start | bytes 1572872 | tf_op jit(solution)/shard_map/ppermute | solution.py:597
  169.4 15.9 %collective-permute-start.16 = (bf16[256,1024]{1,0:T(8,128)(2,1)}, bf16[256,1024]{1,0:T(8,128)(2,1)}, u32[]{:S(2)}, u32[]{:S(2)}) collective-permute-start(bf16[256,1024]{1,0:T(8,128)(2,1)} %get-tuple-element.103.refs_0_), channel_id=1, source_target_pairs={{12,8},{14,10},{8,4},{10,6},{4,0},{6,2},{13,9},{15,11},{9,5},{11,7... | collective-permute-start | bytes 1572872 | tf_op jit(solution)/shard_map/ppermute | solution.py:597
  172.3 18.8 %collective-permute-start.22 = (bf16[256,1024]{1,0:T(8,128)(2,1)}, bf16[256,1024]{1,0:T(8,128)(2,1)S(1)}, u32[]{:S(2)}, u32[]{:S(2)}) collective-permute-start(bf16[256,1024]{1,0:T(8,128)(2,1)} %get-tuple-element.103.refs_0_), channel_id=1, source_target_pairs={{0,2},{2,0},{4,6},{6,4},{8,10},{10,8},{12,14},{14,12},{1,3},{3,1},... | collective-permute-start | bytes 1572872 | tf_op jit(solution)/shard_map/ppermute | solution.py:590
  185.3 6.7 %collective-permute-start.20 = (bf16[256,1024]{1,0:T(8,128)(2,1)}, bf16[256,1024]{1,0:T(8,128)(2,1)S(1)}, u32[]{:S(2)}, u32[]{:S(2)}) collective-permute-start(bf16[256,1024]{1,0:T(8,128)(2,1)} %collective-permute-done.15), channel_id=1, source_target_pairs={{4,8},{6,10},{8,12},{10,14},{5,9},{7,11},{9,13},{11,15},{20,24},{2... | collective-permute-start | bytes 1572872 | tf_op jit(solution)/shard_map/ppermute | solution.py:597
  186.0 16.0 %collective-permute-start.21 = (bf16[256,1024]{1,0:T(8,128)(2,1)}, bf16[256,1024]{1,0:T(8,128)(2,1)S(1)}, u32[]{:S(2)}, u32[]{:S(2)}) collective-permute-start(bf16[256,1024]{1,0:T(8,128)(2,1)} %collective-permute-done.16), channel_id=1, source_target_pairs={{8,4},{10,6},{4,0},{6,2},{9,5},{11,7},{5,1},{7,3},{24,20},{26,22},... | collective-permute-start | bytes 1572872 | tf_op jit(solution)/shard_map/ppermute | solution.py:597
  188.4 13.6 %collective-permute-start.23 = (bf16[256,1024]{1,0:T(8,128)(2,1)S(1)}, bf16[256,1024]{1,0:T(8,128)(2,1)S(1)}, u32[]{:S(2)}, u32[]{:S(2)}) collective-permute-start(bf16[256,1024]{1,0:T(8,128)(2,1)S(1)} %broadcast_select_fusion.1.refs_8_.refs_6_), channel_id=1, source_target_pairs={{0,16},{16,0},{1,17},{17,1},{2,18},{18,2},{3,19},{19,3},{4,20},{20... | collective-permute-start | bytes 1572872 | tf_op jit(solution)/shard_map/ppermute | solution.py:587
  190.1 12.6 %collective-permute-start.24 = (bf16[256,1024]{1,0:T(8,128)(2,1)S(1)}, bf16[256,1024]{1,0:T(8,128)(2,1)S(1)}, u32[]{:S(2)}, u32[]{:S(2)}) collective-permute-start(bf16[256,1024]{1,0:T(8,128)(2,1)S(1)} %broadcast_select_fusion.2), channel_id=1, source_target_pairs={{0,2},{2,0},{4,6},{6,4},{8,10},{10,8},{12,14},{14,12},{1,3},{3,1},... | collective-permute-start | bytes 1572872 | tf_op jit(solution)/shard_map/ppermute | solution.py:590
  192.0 11.6 %copy-start.12 = (bf16[256,1024]{1,0:T(8,128)(2,1)}, bf16[256,1024]{1,0:T(8,128)(2,1)S(1)}, u32[]{:S(2)}) copy-start(bf16[256,1024]{1,0:T(8,128)(2,1)S(1)} %collective-permute-done.20) | copy-start | bytes 1572868
  204.4 15.6 %collective-permute-start.28 = (bf16[768,1024]{1,0:T(8,128)(2,1)}, bf16[768,1024]{1,0:T(8,128)(2,1)}, u32[]{:S(2)}, u32[]{:S(2)}) collective-permute-start(bf16[768,1024]{1,0:T(8,128)(2,1)} %constant_dynamic-update-slice_fusion.8.refs_1_), channel_id=1, source_target_pairs={{0,1},{1,0},{2,3},{3,2},{4,5},{5,4},{6,7},{7,6},{8,9},{9,8},{10,11... | collective-permute-start | bytes 4718600 | tf_op jit(solution)/shard_map/ppermute | solution.py:713
  205.5 14.5 %collective-permute-start.27 = (bf16[256,1024]{1,0:T(8,128)(2,1)S(1)}, bf16[256,1024]{1,0:T(8,128)(2,1)}, u32[]{:S(2)}, u32[]{:S(2)}) collective-permute-start(bf16[256,1024]{1,0:T(8,128)(2,1)S(1)} %broadcast_select_fusion.refs_10_.refs_8_), channel_id=1, source_target_pairs={{0,16},{16,0},{1,17},{17,1},{2,18},{18,2},{3,19},{19,3},{4,20},{20... | collective-permute-start | bytes 1572872 | tf_op jit(solution)/shard_map/ppermute | solution.py:587
  207.1 24.4 %collective-permute-start.25 = (bf16[256,1024]{1,0:T(8,128)(2,1)}, bf16[256,1024]{1,0:T(8,128)(2,1)}, u32[]{:S(2)}, u32[]{:S(2)}) collective-permute-start(bf16[256,1024]{1,0:T(8,128)(2,1)} %copy-done.12), channel_id=1, source_target_pairs={{8,12},{10,14},{9,13},{11,15},{24,28},{26,30},{25,29},{27,31}} | collective-permute-start | bytes 1572872 | tf_op jit(solution)/shard_map/ppermute | solution.py:597
  208.5 23.0 %collective-permute-start.26 = (bf16[256,1024]{1,0:T(8,128)(2,1)}, bf16[256,1024]{1,0:T(8,128)(2,1)}, u32[]{:S(2)}, u32[]{:S(2)}) collective-permute-start(bf16[256,1024]{1,0:T(8,128)(2,1)} %copy-done.14), channel_id=1, source_target_pairs={{4,0},{6,2},{5,1},{7,3},{20,16},{22,18},{21,17},{23,19}} | collective-permute-start | bytes 1572872 | tf_op jit(solution)/shard_map/ppermute | solution.py:597
  211.9 19.6 %collective-permute-start.29 = (bf16[256,1024]{1,0:T(8,128)(2,1)}, bf16[256,1024]{1,0:T(8,128)(2,1)}, u32[]{:S(2)}, u32[]{:S(2)}) collective-permute-start(bf16[256,1024]{1,0:T(8,128)(2,1)} %fusion.1), channel_id=1, source_target_pairs={{0,2},{2,0},{4,6},{6,4},{8,10},{10,8},{12,14},{14,12},{1,3},{3,1},... | collective-permute-start | bytes 1572872 | tf_op jit(solution)/shard_map/ppermute | solution.py:590
  223.1 8.4 %copy-start.13 = (bf16[256,1024]{1,0:T(8,128)(2,1)S(1)}, bf16[256,1024]{1,0:T(8,128)(2,1)}, u32[]{:S(2)}) copy-start(bf16[256,1024]{1,0:T(8,128)(2,1)} %copy-done.12) | copy-start | bytes 1572868
  223.1 8.4 %copy-start.15 = (bf16[256,1024]{1,0:T(8,128)(2,1)S(1)}, bf16[256,1024]{1,0:T(8,128)(2,1)}, u32[]{:S(2)}) copy-start(bf16[256,1024]{1,0:T(8,128)(2,1)} %copy-done.14) | copy-start | bytes 1572868
  234.6 3.5 %collective-permute-start.31 = (bf16[768,1024]{1,0:T(8,128)(2,1)S(1)}, bf16[768,1024]{1,0:T(8,128)(2,1)S(1)}, u32[]{:S(2)}, u32[]{:S(2)}) collective-permute-start(bf16[768,1024]{1,0:T(8,128)(2,1)S(1)} %pad_maximum_fusion.refs_0_), channel_id=1, source_target_pairs={{0,1},{1,0},{2,3},{3,2},{4,5},{5,4},{6,7},{7,6},{8,9},{9,8},{10,11... | collective-permute-start | bytes 4718600 | tf_op jit(solution)/shard_map/ppermute | solution.py:713
  234.6 14.4 %collective-permute-start.30 = (bf16[256,1024]{1,0:T(8,128)(2,1)S(1)}, bf16[256,1024]{1,0:T(8,128)(2,1)}, u32[]{:S(2)}, u32[]{:S(2)}) collective-permute-start(bf16[256,1024]{1,0:T(8,128)(2,1)S(1)} %select_select_fusion.1), channel_id=1, source_target_pairs={{0,2},{2,0},{4,6},{6,4},{8,10},{10,8},{12,14},{14,12},{1,3},{3,1},... | collective-permute-start | bytes 1572872 | tf_op jit(solution)/shard_map/ppermute | solution.py:590
  249.1 2.3 collective-permute-start.32
  265.1 14.2 %collective-permute-start.33 = (bf16[512,512]{1,0:T(8,128)(2,1)}, bf16[512,512]{1,0:T(8,128)(2,1)S(1)}, u32[]{:S(2)}, u32[]{:S(2)}) collective-permute-start(bf16[512,512]{1,0:T(8,128)(2,1)} %decode_rows.3), channel_id=1, source_target_pairs={{0,2},{2,0},{4,6},{6,4},{8,10},{10,8},{12,14},{14,12},{1,3},{3,1},... | collective-permute-start | bytes 1572872 | tf_op jit(solution)/shard_map/ppermute | solution.py:590
  274.4 5.0 %copy-start.16 = (f32[512,512]{1,0:T(8,128)S(1)}, f32[512,512]{1,0:T(8,128)}, u32[]{:S(2)}) copy-start(f32[512,512]{1,0:T(8,128)} %decode_rows.2) | copy-start | bytes 3145732
  (17 other events, 27.1 us)

commit v12 on v11

--- a/solution.py
+++ b/solution.py
@@ -212,7 +212,12 @@
     kind = extra_ref[...].astype(jnp.float32)[:1, :tokens]
     lane = lax.broadcasted_iota(jnp.int32, (rows, LANES), 1)
     lse_all = jnp.zeros((rows, LANES), jnp.float32)
-    earlier = stats_of(refs[0], heads) if len(refs) > 1 else None
+    earlier = None
+    if len(refs) > 1:
+        earlier = [
+            jnp.max(jnp.broadcast_to(v, (rows, LANES)), axis=1, keepdims=True)
+            for v in stats_of(refs[0], heads)
+        ]
     for h in range(heads):
         cols = slice(h * HEAD_DIM, (h + 1) * HEAD_DIM)
         bias = jnp.zeros_like(kind)
@@ -629,12 +634,14 @@
     head_bias = lax.dynamic_slice_in_dim(enc_bias, y * (heads // 2), heads // 2, 1)
     which = jnp.stack([y, y, y, 0 * y]).astype(jnp.int32)
     parts = encode(which, latent_queries, enc_keys, enc_values, extra, head_bias, 2 * rows)
-    near_inputs, out_far, kv_for_near, parts = lax.optimization_barrier(
-        (near_inputs, out_far, kv_for_near, parts)
-    )
-
     kv_own = columns((w_key, w_value), y)
-    kv_near = over_near(kv_for_near)
+    kv_near, out_far, parts = lax.optimization_barrier((over_near(kv_for_near), out_far, parts))
+    kv_sent = jnp.where(x == 0, kv_own, kv_near)
+    hops = {0: [kv_sent, kv_sent]}
+    hops[1] = hop(1, hops[0])
+    early = [k for k in range(1, far) if max(k, far - k) < 3]
+    rest = [k for k in range(1, far) if k not in early]
+    near_inputs, hops, parts = lax.optimization_barrier((near_inputs, hops, parts))
 
     which = jnp.stack([y, 0 * y, 0 * y + 1, 0 * y + tokens // EXTRA]).astype(jnp.int32)
     parts = encode(
@@ -647,16 +654,10 @@
         2 * rows,
         parts,
     )
-    kv_near, out_far, parts = lax.optimization_barrier((kv_near, out_far, parts))
-    kv_sent = jnp.where(x == 0, kv_own, kv_near)
-    hops = {0: [kv_sent, kv_sent]}
-    hops[1] = hop(1, hops[0])
-    early = [k for k in range(1, far) if max(k, far - k) < 3]
-    rest = [k for k in range(1, far) if k not in early]
+    out_far, parts = lax.optimization_barrier((out_far, parts))
     out_far = jnp.concatenate(out_far)
     out_far_other = over_groups(out_far)
     out_near = over_near(jnp.concatenate([w_out, counted, out_far]))
-    out_near, hops = lax.optimization_barrier((out_near, hops))
     out_near_other = over_groups(out_near[w_out.shape[0] + EXTRA :])
     columns_of_slice = [[2 * i + j for i in range(far)] for j in range(2)]
     parts = lax.all_to_all(parts, "pos", 0, 0, axis_index_groups=columns_of_slice, tiled=True)
@@ -732,15 +733,26 @@
     came = {0: [normed, normed]}
     came[1] = hop(1, came[0])
     normed_near = over_near(normed)
-    came, hops, kv_bands, kept = lax.optimization_barrier((came, hops, kv_bands, kept))
+    hops, _ = lax.optimization_barrier((hops, normed))
+
+    def add_band(k):
+        moved = by_shift(hops, k)
+        return [*kv_bands, moved, over_groups(moved)]
+
+    kv_bands = add_band(rest[0])
+    came, kv_bands, kept, normed_near = lax.optimization_barrier(
+        (came, kv_bands, kept, normed_near)
+    )
     mine, other, keys_values = [normed, normed_near], [normed_other], []
     for step in range(1, far):
         fresh = arrival(came, step)
         fresh_near = over_near(fresh)
         if step + 1 < far:
             came[step + 1] = hop(step + 1, came[step])
-            kv_moved = by_shift(hops, rest[step - 1])
-            kv_bands += [kv_moved, over_groups(kv_moved)]
+            if step == 1:
+                other += cores([normed_near])
+            if step < len(rest):
+                kv_bands = add_band(rest[step])
             if step > 1:
                 keys_values.append(fold(mine, other))
                 mine, other = [], []
@@ -749,13 +761,9 @@
                     (came, mine, other, kv_bands, keys_values, fresh, fresh_near)
                 )
             )
-            if step == 1:
-                mine = [normed, jnp.concatenate([normed_near, fresh, fresh_near])]
-                other = [normed_other, *cores(mine[1:])]
-            else:
-                mine += [fresh, fresh_near]
-    mine = [jnp.concatenate([*mine, fresh])]
-    keys_values.append(fold(mine, cores(mine)))
+            mine += [fresh, fresh_near]
+            other += cores([fresh, fresh_near])
+    keys_values.append(fold([*mine, fresh], [*other, *cores([fresh])]))
     fresh_near, keys_values = lax.optimization_barrier((fresh_near, keys_values))
     keys_values.append(fold([fresh_near], cores([fresh_near])))
     near_state = decode(near_queries, keys_values, jnp.bfloat16)

time: 283 us -> 270 us (0.954)
  waiting for transfers between devices: 117 us -> 102 us
  local copies, waits for them, and re-layouts: 25.1 us -> 28.5 us
    ppermute x12, waiting for transfers between devices: 68.1 us -> 29 us  [hop(): lax.ppermute(v, 'pos', hop_perm(pos, step, way))]
    ppermute x10, waiting for transfers between devices: 25 us -> 51.6 us  [over_near(): return lax.ppermute(value, 'pos', near)]
    unnamed x67 -> x69, local copies, waits for them, and re-layouts: 16 us -> 20.3 us
  transfers between devices with their start and end apart: 35 -> 39, of which waited for: 15 -> 19; matrix products, arithmetic and copies ran while one was open for 8% -> 8% of each run, Pallas kernels for 20% -> 16%
where the time goes in v12:
time: 270 us; the launch traced here: 266 us
  waiting for transfers between devices  102 us (38%)
  Pallas kernels  69.3 us (26%)
  starting transfers between devices  51.9 us (19%)
  local copies, waits for them, and re-layouts  28.5 us (11%)
  other arithmetic  13.2 us (5%)
    ppermute x10, waiting for transfers between devices, over_near(): return lax.ppermute(value, 'pos', near)  51.6 us
    ppermute x12, waiting for transfers between devices, hop(): lax.ppermute(v, 'pos', hop_perm(pos, step, way))  29 us
    ppermute x12, starting transfers between devices, hop(): lax.ppermute(v, 'pos', hop_perm(pos, step, way))  23.9 us
    pallas_call x2, Pallas kernels, encode(): pl.pallas_call(functools.partial(encode_kernel, bias.shape[0]), grid_spec...  22.4 us
    unnamed x69, local copies, waits for them, and re-layouts  20.3 us
    pallas_call x3, Pallas kernels, latent_keys_values(): pl.pallas_call(functools.partial(latents_kernel, pieces), grid_spec=grid_...  18.1 us
    pallas_call x2, Pallas kernels, decode(): pl.pallas_call(functools.partial(decode_kernel, len(keys_values)), grid=(...  16.7 us
    ppermute x10, starting transfers between devices, over_near(): return lax.ppermute(value, 'pos', near)  10.4 us
  transfers between devices with their start and end apart: 39, of which 19 were waited for; matrix products, arithmetic and copies ran while one was open for 8% of the time, Pallas kernels for 16%

profile of v12, /device:TPU:0, one launch (start us, length us, event | category | flops | bytes accessed | tf_op | source)
XLA Modules:
  0.0 266.2 jit_solution(14055636324765921950)
XLA Ops:
  0.7 2.0 constant_dynamic-update-slice_fusion.4
  5.9 5.0 %collective-permute-start.1 = (bf16[528,256]{1,0:T(8,128)(2,1)}, bf16[528,256]{1,0:T(8,128)(2,1)}, u32[]{:S(2)}, u32[]{:S(2)}) collective-permute-start(bf16[528,256]{1,0:T(8,128)(2,1)} %pad_maximum_fusion.3), channel_id=1, source_target_pairs={{4,0},{6,2},{8,4},{10,6},{12,8},{14,10},{0,12},{2,14},{5,1},{7,3},... | collective-permute-start | bytes 811016 | tf_op jit(solution)/shard_map/ppermute | solution.py:598
  12.1 1.6 collective-permute-start
  17.1 9.8 %encode_rows.2.refs_0_ = bf16[2112,512]{1,0:T(8,128)(2,1)} custom-call(s32[4]{0:T(128)} %get-tuple-element.190.ids_ref, bf16[2048,1024]{1,0:T(8,128)(2,1)} %q_ref.3, bf16[512,1024]{1,0:T(8,128)(2,1)} %k_ref.1, bf16[512,1024]{1,0:T(8,128)(2,1)} %v_ref.1, bf16[16,1024]{1,0:T(8,128)(2,1)} %copy-done.26, f32[3,4]{1,0:T(4,128)} %constant_dynamic-slice_fusion.6.bias_ref), custom_call_target="tpu_custom_call" | custom-call | flops 4294967296 | bytes 2097152 | tf_op jit(solution)/shard_map/encode_rows/pallas_call | solution.py:273
  26.9 7.3 %collective-permute-done.2 = bf16[528,256]{1,0:T(8,128)(2,1)} collective-permute-done((bf16[528,256]{1,0:T(8,128)(2,1)}, bf16[528,256]{1,0:T(8,128)(2,1)}, u32[]{:S(2)}, u32[]{:S(2)}) %collective-permute-start.2) | collective-permute-done | bytes 270368 | tf_op jit(solution)/shard_map/ppermute | solution.py:598
  34.4 3.6 %collective-permute-start.5 = (bf16[256,1024]{1,0:T(8,128)(2,1)S(1)}, bf16[256,1024]{1,0:T(8,128)(2,1)}, u32[]{:S(2)}, u32[]{:S(2)}) collective-permute-start(bf16[256,1024]{1,0:T(8,128)(2,1)S(1)} %get-tuple-element.175), channel_id=1, source_target_pairs={{0,4},{2,6},{4,8},{6,10},{8,12},{10,14},{1,5},{3,7},{5,9},{7,11},{... | collective-permute-start | bytes 1572872 | tf_op jit(solution)/shard_map/ppermute | solution.py:602
  39.3 8.5 %collective-permute-done.5 = bf16[256,1024]{1,0:T(8,128)(2,1)} collective-permute-done((bf16[256,1024]{1,0:T(8,128)(2,1)S(1)}, bf16[256,1024]{1,0:T(8,128)(2,1)}, u32[]{:S(2)}, u32[]{:S(2)}) %collective-permute-start.5) | collective-permute-done | bytes 524320 | tf_op jit(solution)/shard_map/ppermute | solution.py:602
  47.8 5.0 %collective-permute-done.6 = bf16[256,1024]{1,0:T(8,128)(2,1)} collective-permute-done((bf16[256,1024]{1,0:T(8,128)(2,1)S(1)}, bf16[256,1024]{1,0:T(8,128)(2,1)}, u32[]{:S(2)}, u32[]{:S(2)}) %collective-permute-start.6) | collective-permute-done | bytes 524320 | tf_op jit(solution)/shard_map/ppermute | solution.py:602
  52.8 12.5 %encode_rows.3 = bf16[2112,512]{1,0:T(8,128)(2,1)} custom-call(s32[4]{0:T(128)} %get-tuple-element.191.ids_ref, bf16[2048,1024]{1,0:T(8,128)(2,1)} %q_ref.3, bf16[528,1024]{1,0:T(8,128)(2,1)} %collective-permute-done.4.k_ref.v_ref.extra_ref, bf16[528,1024]{1,0:T(8,128)(2,1)} %collective-permute-done.4.k_ref.v_ref.extra_ref, ...), custom_call_target="tpu_custom_call" | custom-call | flops 4294967296 | bytes 2097152 | tf_op jit(solution)/shard_map/encode_rows/pallas_call | solution.py:273
  65.3 3.6 %all-to-all-start = ((bf16[4,528,512]{2,1,0:T(8,128)(2,1)}), bf16[4,528,512]{2,1,0:T(8,128)(2,1)S(1)}, u32[]{:S(2)}, u32[]{:S(2)}) async-start(bf16[4,528,512]{2,1,0:T(8,128)(2,1)} %bitcast.52), calls=%async_computation | async-start | bytes 4325376 | tf_op jit(solution)/shard_map/all_to_all | solution.py:663
  69.0 1.8 constant_dynamic-update-slice_fusion.7
  70.8 1.7 constant_dynamic-update-slice_fusion.6
  72.5 1.7 constant_dynamic-update-slice_fusion.5
  74.1 1.5 collective-permute-start.7
  75.7 1.5 collective-permute-start.8
  77.2 26.6 %collective-permute-done.7.refs_3_ = bf16[2624,256]{1,0:T(8,128)(2,1)S(1)} collective-permute-done((bf16[2624,256]{1,0:T(8,128)(2,1)}, bf16[2624,256]{1,0:T(8,128)(2,1)S(1)}, u32[]{:S(2)}, u32[]{:S(2)}) %collective-permute-start.7) | collective-permute-done | bytes 1343520 | tf_op jit(solution)/shard_map/ppermute | solution.py:595
  104.9 1.5 collective-permute-start.9
  107.7 1.5 collective-permute-start.10
  109.3 9.1 %collective-permute-done.10.q_ref = bf16[512,512]{1,0:T(8,128)(2,1)S(1)} collective-permute-done((bf16[512,512]{1,0:T(8,128)(2,1)S(1)}, bf16[512,512]{1,0:T(8,128)(2,1)S(1)}, u32[]{:S(2)}, u32[]{:S(2)}) %collective-permute-start.10) | collective-permute-done | bytes 524320 | tf_op jit(solution)/shard_map/ppermute | solution.py:595
  120.1 1.9 collective-permute-done.9.refs_4_
  122.0 1.9 merge_rows.1
  126.6 1.6 collective-permute-start.11
  128.8 4.2 %collective-permute-done.11.near_ref = bf16[256,512]{1,0:T(8,128)(2,1)S(1)} collective-permute-done((bf16[256,512]{1,0:T(8,128)(2,1)S(1)}, bf16[256,512]{1,0:T(8,128)(2,1)S(1)}, u32[]{:S(2)}, u32[]{:S(2)}) %collective-permute-start.11) | collective-permute-done | bytes 262176 | tf_op jit(solution)/shard_map/ppermute | solution.py:595
  133.8 5.7 %project_rows.1.mine_ref = f32[256,2048]{1,0:T(8,128)} custom-call(s32[10]{0:T(128)} %stack.92.ids_ref, bf16[256,512]{1,0:T(8,128)(2,1)} %copy-done.6, bf16[256,512]{1,0:T(8,128)(2,1)} %copy-done.25, bf16[1024,256]{1,0:T(8,128)(2,1)} %refs_0_.1, bf16[1584,256]{1,0:T(8,128)(2,1)} %copy-done.18, bf16[1584,256]{1,0:T(8,128)(2,1)} %copy-done.21, ...), custom_call_target="tpu_custom_call" | custom-call | flops 1073741824 | bytes 6291456 | tf_op jit(solution)/shard_map/project_rows/pallas_call | solution.py:371
  140.6 1.5 collective-permute-start.18
  144.7 1.6 collective-permute-start.17
  146.2 4.5 %norm_rows.1 = (f32[256,1024]{1,0:T(8,128)}, bf16[256,1024]{1,0:T(8,128)(2,1)}, bf16[256,1024]{1,0:T(8,128)(2,1)}) custom-call(s32[1]{0:T(128)} %bitcast.ids_ref, f32[256,2048]{1,0:T(8,128)} %project_rows.1.mine_ref, f32[256,2048]{1,0:T(8,128)} %collective-permute-done.14.theirs_ref, bf16[256,2048]{1,0:T(8,128)(2,1)} %latent_ref.1, f32[1,2048]{1,0:T(1,128)} %bitcast.55), custom_call_target="tpu_custom_call" | custom-call | flops 3145728 | bytes 6815744 | tf_op jit(solution)/shard_map/norm_rows/pallas_call | solution.py:405
  150.7 8.3 %collective-permute-start.15 = (bf16[256,1024]{1,0:T(8,128)(2,1)}, bf16[256,1024]{1,0:T(8,128)(2,1)}, u32[]{:S(2)}, u32[]{:S(2)}) collective-permute-start(bf16[256,1024]{1,0:T(8,128)(2,1)} %get-tuple-element.141.refs_0_), channel_id=1, source_target_pairs={{0,4},{2,6},{4,8},{6,10},{8,12},{10,14},{1,5},{3,7},{5,9},{7,11},{... | collective-permute-start | bytes 1572872 | tf_op jit(solution)/shard_map/ppermute | solution.py:602
  160.3 1.6 collective-permute-start.21
  165.7 1.6 collective-permute-start.25
  167.2 2.9 %collective-permute-done.15 = bf16[256,1024]{1,0:T(8,128)(2,1)} collective-permute-done((bf16[256,1024]{1,0:T(8,128)(2,1)}, bf16[256,1024]{1,0:T(8,128)(2,1)}, u32[]{:S(2)}, u32[]{:S(2)}) %collective-permute-start.15) | collective-permute-done | bytes 524320 | tf_op jit(solution)/shard_map/ppermute | solution.py:602
  170.1 4.9 %collective-permute-done.16 = bf16[256,1024]{1,0:T(8,128)(2,1)} collective-permute-done((bf16[256,1024]{1,0:T(8,128)(2,1)}, bf16[256,1024]{1,0:T(8,128)(2,1)}, u32[]{:S(2)}, u32[]{:S(2)}) %collective-permute-start.16) | collective-permute-done | bytes 524320 | tf_op jit(solution)/shard_map/ppermute | solution.py:602
  175.0 3.1 %collective-permute-done.20.refs_13_.refs_11_.refs_7_ = bf16[256,1024]{1,0:T(8,128)(2,1)} collective-permute-done((bf16[256,1024]{1,0:T(8,128)(2,1)S(1)}, bf16[256,1024]{1,0:T(8,128)(2,1)}, u32[]{:S(2)}, u32[]{:S(2)}) %collective-permute-start.20) | collective-permute-done | bytes 524320 | tf_op jit(solution)/shard_map/ppermute | solution.py:592
  180.1 1.9 broadcast_select_fusion.1.refs_2_
  182.5 5.3 %collective-permute-done.25.refs_15_.refs_13_.refs_9_ = bf16[256,1024]{1,0:T(8,128)(2,1)S(1)} collective-permute-done((bf16[256,1024]{1,0:T(8,128)(2,1)S(1)}, bf16[256,1024]{1,0:T(8,128)(2,1)S(1)}, u32[]{:S(2)}, u32[]{:S(2)}) %collective-permute-start.25) | collective-permute-done | bytes 524320 | tf_op jit(solution)/shard_map/ppermute | solution.py:592
  188.6 6.0 %collective-permute-done.23 = bf16[256,1024]{1,0:T(8,128)(2,1)S(1)} collective-permute-done((bf16[256,1024]{1,0:T(8,128)(2,1)}, bf16[256,1024]{1,0:T(8,128)(2,1)S(1)}, u32[]{:S(2)}, u32[]{:S(2)}) %collective-permute-start.23) | collective-permute-done | bytes 524320 | tf_op jit(solution)/shard_map/ppermute | solution.py:602
  197.2 1.4 collective-permute-start.27
  199.9 2.1 fusion.1.refs_0_
  206.7 8.2 %latent_keys_values.3.refs_0_.refs_3_ = bf16[1024,1024]{1,0:T(8,128)(2,1)S(1)} custom-call(s32[9]{0:T(128)S(1)} %stack.104.ids_ref, bf16[256,1024]{1,0:T(8,128)(2,1)S(1)} %copy-done.7, bf16[256,1024]{1,0:T(8,128)(2,1)} %collective-permute-done.21.refs_1_, bf16[256,1024]{1,0:T(8,128)(2,1)} %broadcast_select_fusion.1.refs_2_, ...), custom_call_target="tpu_custom_call" | custom-call | flops 4294967296 | bytes 4194304 | tf_op jit(solution)/shard_map/latent_keys_values/pallas_call | solution.py:469
  216.3 1.8 collective-permute-done.28
  221.8 6.2 %latent_keys_values.4.refs_1_.refs_4_ = bf16[768,1024]{1,0:T(8,128)(2,1)S(1)} custom-call(s32[9]{0:T(128)S(1)} %stack.104.ids_ref, bf16[256,1024]{1,0:T(8,128)(2,1)} %fusion.1.refs_0_, bf16[256,1024]{1,0:T(8,128)(2,1)} %collective-permute-done.31.refs_1_, bf16[256,1024]{1,0:T(8,128)(2,1)S(1)} %select_select_fusion.1.refs_2_, ...), custom_call_target="tpu_custom_call" | custom-call | flops 3221225472 | bytes 4194304 | tf_op jit(solution)/shard_map/latent_keys_values/pallas_call | solution.py:469
  229.2 5.2 %collective-permute-done.32.refs_0_ = bf16[256,1024]{1,0:T(8,128)(2,1)} collective-permute-done((bf16[256,1024]{1,0:T(8,128)(2,1)S(1)}, bf16[256,1024]{1,0:T(8,128)(2,1)}, u32[]{:S(2)}, u32[]{:S(2)}) %collective-permute-start.32) | collective-permute-done | bytes 524320 | tf_op jit(solution)/shard_map/ppermute | solution.py:595
  234.3 2.2 collective-permute-done.36.refs_1_
  237.6 3.7 %latent_keys_values.5.refs_2_.refs_5_ = bf16[256,1024]{1,0:T(8,128)(2,1)S(1)} custom-call(s32[9]{0:T(128)S(1)} %stack.104.ids_ref, bf16[256,1024]{1,0:T(8,128)(2,1)} %collective-permute-done.32.refs_0_, bf16[256,1024]{1,0:T(8,128)(2,1)} %collective-permute-done.36.refs_1_, bf16[256,1024]{1,0:T(8,128)(2,1)S(1)} %get-tuple-element.154.refs_8_.refs_6_.refs_2_, ...), custom_call_target="tpu_custom_call" | custom-call | flops 1073741824 | bytes 4194304 | tf_op jit(solution)/shard_map/latent_keys_values/pallas_call | solution.py:469
  242.1 8.3 %decode_rows.3 = bf16[512,512]{1,0:T(8,128)(2,1)} custom-call(bf16[512,512]{1,0:T(8,128)(2,1)} %copy-done.31, bf16[1024,1024]{1,0:T(8,128)(2,1)} %copy-done.12, bf16[768,1024]{1,0:T(8,128)(2,1)} %copy-done.11, bf16[256,1024]{1,0:T(8,128)(2,1)} %copy-done.5, bf16[1024,1024]{1,0:T(8,128)(2,1)} %copy-done.12, bf16[768,1024]{1,0:T(8,128)(2,1)} %copy-done.11, ...), custom_call_target="tpu_custom_call" | custom-call | flops 8589934592 | bytes 5767168 | tf_op jit(solution)/shard_map/decode_rows/pallas_call | solution.py:530
  250.9 8.4 %decode_rows.2 = f32[512,512]{1,0:T(8,128)} custom-call(bf16[512,512]{1,0:T(8,128)(2,1)} %get-tuple-element.172.q_ref, bf16[1024,1024]{1,0:T(8,128)(2,1)} %copy-done.12, bf16[768,1024]{1,0:T(8,128)(2,1)} %copy-done.11, bf16[256,1024]{1,0:T(8,128)(2,1)} %copy-done.5, bf16[1024,1024]{1,0:T(8,128)(2,1)} %copy-done.12, bf16[768,1024]{1,0:T(8,128)(2,1)} %copy-done.11, ...), custom_call_target="tpu_custom_call" | custom-call | flops 8589934592 | bytes 5767168 | tf_op jit(solution)/shard_map/decode_rows/pallas_call | solution.py:530
  259.3 5.3 %collective-permute-done.37 = bf16[512,512]{1,0:T(8,128)(2,1)S(1)} collective-permute-done((bf16[512,512]{1,0:T(8,128)(2,1)}, bf16[512,512]{1,0:T(8,128)(2,1)S(1)}, u32[]{:S(2)}, u32[]{:S(2)}) %collective-permute-start.37) | collective-permute-done | bytes 524320 | tf_op jit(solution)/shard_map/ppermute | solution.py:595
  264.7 1.6 fusion
  (152 shorter events, 46.6 us)
Async XLA Ops:
  0.6 105.7 %copy-start = (bf16[3,1024]{1,0:T(4,128)(2,1)S(1)}, bf16[3,1024]{1,0:T(4,128)(2,1)}, u32[]{:S(2)}) copy-start(bf16[3,1024]{1,0:T(4,128)(2,1)} %param.25) | copy-start | bytes 18436
  0.6 11.3 %copy-start.22 = (bf16[256,1024]{1,0:T(8,128)(2,1)S(1)}, bf16[256,1024]{1,0:T(8,128)(2,1)}, u32[]{:S(2)}) copy-start(bf16[256,1024]{1,0:T(8,128)(2,1)} %param.22) | copy-start | bytes 1572868
  5.9 21.1 %collective-permute-start.1 = (bf16[528,256]{1,0:T(8,128)(2,1)}, bf16[528,256]{1,0:T(8,128)(2,1)}, u32[]{:S(2)}, u32[]{:S(2)}) collective-permute-start(bf16[528,256]{1,0:T(8,128)(2,1)} %pad_maximum_fusion.3), channel_id=1, source_target_pairs={{4,0},{6,2},{8,4},{10,6},{12,8},{14,10},{0,12},{2,14},{5,1},{7,3},... | collective-permute-start | bytes 811016 | tf_op jit(solution)/shard_map/ppermute | solution.py:598
  10.9 23.3 %collective-permute-start.2 = (bf16[528,256]{1,0:T(8,128)(2,1)}, bf16[528,256]{1,0:T(8,128)(2,1)}, u32[]{:S(2)}, u32[]{:S(2)}) collective-permute-start(bf16[528,256]{1,0:T(8,128)(2,1)} %pad_maximum_fusion.3), channel_id=1, source_target_pairs={{8,0},{10,2},{12,4},{14,6},{0,8},{2,10},{4,12},{6,14},{9,1},{11,3}... | collective-permute-start | bytes 811016 | tf_op jit(solution)/shard_map/ppermute | solution.py:598
  10.9 23.3 %collective-permute-start.3 = (bf16[528,256]{1,0:T(8,128)(2,1)}, bf16[528,256]{1,0:T(8,128)(2,1)S(1)}, u32[]{:S(2)}, u32[]{:S(2)}) collective-permute-start(bf16[528,256]{1,0:T(8,128)(2,1)} %pad_maximum_fusion.3), channel_id=1, source_target_pairs={{12,0},{14,2},{0,4},{2,6},{4,8},{6,10},{8,12},{10,14},{13,1},{15,3... | collective-permute-start | bytes 811016 | tf_op jit(solution)/shard_map/ppermute | solution.py:598
  12.1 22.1 %collective-permute-start = (bf16[256,1024]{1,0:T(8,128)(2,1)S(1)}, bf16[256,1024]{1,0:T(8,128)(2,1)S(1)}, u32[]{:S(2)}, u32[]{:S(2)}) collective-permute-start(bf16[256,1024]{1,0:T(8,128)(2,1)S(1)} %pad_maximum_fusion.1), channel_id=1, source_target_pairs={{0,2},{2,0},{4,6},{6,4},{8,10},{10,8},{12,14},{14,12},{1,3},{3,1},... | collective-permute-start | bytes 1572872 | tf_op jit(solution)/shard_map/ppermute | solution.py:595
  15.2 37.6 %collective-permute-start.4 = (bf16[528,1024]{1,0:T(8,128)(2,1)S(1)}, bf16[528,1024]{1,0:T(8,128)(2,1)}, u32[]{:S(2)}, u32[]{:S(2)}) collective-permute-start(bf16[528,1024]{1,0:T(8,128)(2,1)S(1)} %pad_maximum_fusion), channel_id=1, source_target_pairs={{0,2},{2,0},{4,6},{6,4},{8,10},{10,8},{12,14},{14,12},{1,3},{3,1},... | collective-permute-start | bytes 3244040 | tf_op jit(solution)/shard_map/ppermute | solution.py:595
  34.2 31.1 %copy-start.24 = (bf16[528,256]{1,0:T(8,128)(2,1)}, bf16[528,256]{1,0:T(8,128)(2,1)S(1)}, u32[]{:S(2)}) copy-start(bf16[528,256]{1,0:T(8,128)(2,1)S(1)} %collective-permute-done.3) | copy-start | bytes 811012
  34.4 13.4 %collective-permute-start.5 = (bf16[256,1024]{1,0:T(8,128)(2,1)S(1)}, bf16[256,1024]{1,0:T(8,128)(2,1)}, u32[]{:S(2)}, u32[]{:S(2)}) collective-permute-start(bf16[256,1024]{1,0:T(8,128)(2,1)S(1)} %get-tuple-element.175), channel_id=1, source_target_pairs={{0,4},{2,6},{4,8},{6,10},{8,12},{10,14},{1,5},{3,7},{5,9},{7,11},{... | collective-permute-start | bytes 1572872 | tf_op jit(solution)/shard_map/ppermute | solution.py:602
  38.0 14.8 %collective-permute-start.6 = (bf16[256,1024]{1,0:T(8,128)(2,1)S(1)}, bf16[256,1024]{1,0:T(8,128)(2,1)}, u32[]{:S(2)}, u32[]{:S(2)}) collective-permute-start(bf16[256,1024]{1,0:T(8,128)(2,1)S(1)} %get-tuple-element.175), channel_id=1, source_target_pairs={{12,8},{14,10},{8,4},{10,6},{4,0},{6,2},{13,9},{15,11},{9,5},{11,7... | collective-permute-start | bytes 1572872 | tf_op jit(solution)/shard_map/ppermute | solution.py:602
  65.3 56.7 %all-to-all-start = ((bf16[4,528,512]{2,1,0:T(8,128)(2,1)}), bf16[4,528,512]{2,1,0:T(8,128)(2,1)S(1)}, u32[]{:S(2)}, u32[]{:S(2)}) async-start(bf16[4,528,512]{2,1,0:T(8,128)(2,1)} %bitcast.52), calls=%async_computation | async-start | bytes 4325376 | tf_op jit(solution)/shard_map/all_to_all | solution.py:663
  69.0 37.4 %copy-start.20 = (bf16[512,1024]{1,0:T(8,128)(2,1)S(1)}, bf16[512,1024]{1,0:T(8,128)(2,1)}, u32[]{:S(2)}) copy-start(bf16[512,1024]{1,0:T(8,128)(2,1)} %param.23) | copy-start | bytes 3145732
  69.0 37.4 %copy-start.27 = (s32[512]{0:T(512)S(1)}, s32[512]{0:T(512)}, u32[]{:S(2)}) copy-start(s32[512]{0:T(512)} %param.24) | copy-start | bytes 6148
  74.1 44.3 %copy-start.18 = (bf16[1584,256]{1,0:T(8,128)(2,1)}, bf16[1584,256]{1,0:T(8,128)(2,1)S(1)}, u32[]{:S(2)}) copy-start(bf16[1584,256]{1,0:T(8,128)(2,1)S(1)} %get-tuple-element.180.refs_1_) | copy-start | bytes 2433028
  74.1 29.6 %collective-permute-start.7 = (bf16[2624,256]{1,0:T(8,128)(2,1)}, bf16[2624,256]{1,0:T(8,128)(2,1)S(1)}, u32[]{:S(2)}, u32[]{:S(2)}) collective-permute-start(bf16[2624,256]{1,0:T(8,128)(2,1)} %get-tuple-element.181), channel_id=1, source_target_pairs={{0,2},{2,0},{4,6},{6,4},{8,10},{10,8},{12,14},{14,12},{1,3},{3,1},... | collective-permute-start | bytes 4030472 | tf_op jit(solution)/shard_map/ppermute | solution.py:595
  75.7 42.7 %collective-permute-start.8 = (bf16[1584,256]{1,0:T(8,128)(2,1)S(1)}, bf16[1584,256]{1,0:T(8,128)(2,1)S(1)}, u32[]{:S(2)}, u32[]{:S(2)}) collective-permute-start(bf16[1584,256]{1,0:T(8,128)(2,1)S(1)} %get-tuple-element.180.refs_1_), channel_id=1, source_target_pairs={{0,16},{16,0},{1,17},{17,1},{2,18},{18,2},{3,19},{19,3},{4,20},{20... | collective-permute-start | bytes 2433032 | tf_op jit(solution)/shard_map/ppermute | solution.py:592
  104.9 17.2 %collective-permute-start.9 = (bf16[1584,256]{1,0:T(8,128)(2,1)S(1)}, bf16[1584,256]{1,0:T(8,128)(2,1)}, u32[]{:S(2)}, u32[]{:S(2)}) collective-permute-start(bf16[1584,256]{1,0:T(8,128)(2,1)S(1)} %slice.62), channel_id=1, source_target_pairs={{0,16},{16,0},{1,17},{17,1},{2,18},{18,2},{3,19},{19,3},{4,20},{20... | collective-permute-start | bytes 2433032 | tf_op jit(solution)/shard_map/ppermute | solution.py:592
  107.7 10.7 %collective-permute-start.10 = (bf16[512,512]{1,0:T(8,128)(2,1)S(1)}, bf16[512,512]{1,0:T(8,128)(2,1)S(1)}, u32[]{:S(2)}, u32[]{:S(2)}) collective-permute-start(bf16[512,512]{1,0:T(8,128)(2,1)S(1)} %get-tuple-element.173), channel_id=1, source_target_pairs={{0,2},{2,0},{4,6},{6,4},{8,10},{10,8},{12,14},{14,12},{1,3},{3,1},... | collective-permute-start | bytes 1572872 | tf_op jit(solution)/shard_map/ppermute | solution.py:595
  124.6 14.8 %collective-permute-start.12 = (bf16[256,1024]{1,0:T(8,128)(2,1)}, bf16[256,1024]{1,0:T(8,128)(2,1)S(1)}, u32[]{:S(2)}, u32[]{:S(2)}) collective-permute-start(bf16[256,1024]{1,0:T(8,128)(2,1)} %collective-permute-done.5), channel_id=1, source_target_pairs={{4,8},{6,10},{8,12},{10,14},{5,9},{7,11},{9,13},{11,15},{20,24},{2... | collective-permute-start | bytes 1572872 | tf_op jit(solution)/shard_map/ppermute | solution.py:602
  125.3 14.1 %collective-permute-start.13 = (bf16[256,1024]{1,0:T(8,128)(2,1)}, bf16[256,1024]{1,0:T(8,128)(2,1)S(1)}, u32[]{:S(2)}, u32[]{:S(2)}) collective-permute-start(bf16[256,1024]{1,0:T(8,128)(2,1)} %collective-permute-done.6), channel_id=1, source_target_pairs={{8,4},{10,6},{4,0},{6,2},{9,5},{11,7},{5,1},{7,3},{24,20},{26,22},... | collective-permute-start | bytes 1572872 | tf_op jit(solution)/shard_map/ppermute | solution.py:602
  126.6 6.4 %collective-permute-start.11 = (bf16[256,512]{1,0:T(8,128)(2,1)S(1)}, bf16[256,512]{1,0:T(8,128)(2,1)S(1)}, u32[]{:S(2)}, u32[]{:S(2)}) collective-permute-start(bf16[256,512]{1,0:T(8,128)(2,1)S(1)} %get-tuple-element.102), channel_id=1, source_target_pairs={{0,2},{2,0},{4,6},{6,4},{8,10},{10,8},{12,14},{14,12},{1,3},{3,1},... | collective-permute-start | bytes 786440 | tf_op jit(solution)/shard_map/ppermute | solution.py:595
  139.5 6.7 %collective-permute-start.14 = (f32[256,2048]{1,0:T(8,128)}, f32[256,2048]{1,0:T(8,128)}, u32[]{:S(2)}, u32[]{:S(2)}) collective-permute-start(f32[256,2048]{1,0:T(8,128)} %project_rows.1.mine_ref), channel_id=1, source_target_pairs={{0,1},{1,0},{2,3},{3,2},{4,5},{5,4},{6,7},{7,6},{8,9},{9,8},{10,11... | collective-permute-start | bytes 6291464 | tf_op jit(solution)/shard_map/ppermute | solution.py:704
  140.6 19.7 %collective-permute-start.18 = (bf16[256,1024]{1,0:T(8,128)(2,1)S(1)}, bf16[256,1024]{1,0:T(8,128)(2,1)}, u32[]{:S(2)}, u32[]{:S(2)}) collective-permute-start(bf16[256,1024]{1,0:T(8,128)(2,1)S(1)} %collective-permute-done.12), channel_id=1, source_target_pairs={{8,12},{10,14},{9,13},{11,15},{24,28},{26,30},{25,29},{27,31}} | collective-permute-start | bytes 1572872 | tf_op jit(solution)/shard_map/ppermute | solution.py:602
  142.1 19.8 %collective-permute-start.19 = (bf16[256,1024]{1,0:T(8,128)(2,1)S(1)}, bf16[256,1024]{1,0:T(8,128)(2,1)}, u32[]{:S(2)}, u32[]{:S(2)}) collective-permute-start(bf16[256,1024]{1,0:T(8,128)(2,1)S(1)} %collective-permute-done.13), channel_id=1, source_target_pairs={{4,0},{6,2},{5,1},{7,3},{20,16},{22,18},{21,17},{23,19}} | collective-permute-start | bytes 1572872 | tf_op jit(solution)/shard_map/ppermute | solution.py:602
  144.7 21.0 %collective-permute-start.17 = (bf16[256,1024]{1,0:T(8,128)(2,1)S(1)}, bf16[256,1024]{1,0:T(8,128)(2,1)S(1)}, u32[]{:S(2)}, u32[]{:S(2)}) collective-permute-start(bf16[256,1024]{1,0:T(8,128)(2,1)S(1)} %broadcast_select_fusion.3.refs_10_.refs_8_.refs_4_), channel_id=1, source_target_pairs={{0,16},{16,0},{1,17},{17,1},{2,18},{18,2},{3,19},{19,3},{4,20},{20... | collective-permute-start | bytes 1572872 | tf_op jit(solution)/shard_map/ppermute | solution.py:592
  146.2 18.2 %copy-start.30 = (s32[3]{0:T(128)S(1)}, s32[3]{0:T(128)}, u32[]{:S(2)}) copy-start(s32[3]{0:T(128)} %param.27) | copy-start | bytes 40
  150.7 19.3 %collective-permute-start.15 = (bf16[256,1024]{1,0:T(8,128)(2,1)}, bf16[256,1024]{1,0:T(8,128)(2,1)}, u32[]{:S(2)}, u32[]{:S(2)}) collective-permute-start(bf16[256,1024]{1,0:T(8,128)(2,1)} %get-tuple-element.141.refs_0_), channel_id=1, source_target_pairs={{0,4},{2,6},{4,8},{6,10},{8,12},{10,14},{1,5},{3,7},{5,9},{7,11},{... | collective-permute-start | bytes 1572872 | tf_op jit(solution)/shard_map/ppermute | solution.py:602
  159.0 16.0 %collective-permute-start.16 = (bf16[256,1024]{1,0:T(8,128)(2,1)}, bf16[256,1024]{1,0:T(8,128)(2,1)}, u32[]{:S(2)}, u32[]{:S(2)}) collective-permute-start(bf16[256,1024]{1,0:T(8,128)(2,1)} %get-tuple-element.141.refs_0_), channel_id=1, source_target_pairs={{12,8},{14,10},{8,4},{10,6},{4,0},{6,2},{13,9},{15,11},{9,5},{11,7... | collective-permute-start | bytes 1572872 | tf_op jit(solution)/shard_map/ppermute | solution.py:602
  160.3 17.7 %collective-permute-start.21 = (bf16[256,1024]{1,0:T(8,128)(2,1)}, bf16[256,1024]{1,0:T(8,128)(2,1)}, u32[]{:S(2)}, u32[]{:S(2)}) collective-permute-start(bf16[256,1024]{1,0:T(8,128)(2,1)} %get-tuple-element.141.refs_0_), channel_id=1, source_target_pairs={{0,2},{2,0},{4,6},{6,4},{8,10},{10,8},{12,14},{14,12},{1,3},{3,1},... | collective-permute-start | bytes 1572872 | tf_op jit(solution)/shard_map/ppermute | solution.py:595
  163.0 15.0 %collective-permute-start.20 = (bf16[256,1024]{1,0:T(8,128)(2,1)S(1)}, bf16[256,1024]{1,0:T(8,128)(2,1)}, u32[]{:S(2)}, u32[]{:S(2)}) collective-permute-start(bf16[256,1024]{1,0:T(8,128)(2,1)S(1)} %broadcast_select_fusion.2.refs_12_.refs_10_.refs_6_), channel_id=1, source_target_pairs={{0,16},{16,0},{1,17},{17,1},{2,18},{18,2},{3,19},{19,3},{4,20},{20... | collective-permute-start | bytes 1572872 | tf_op jit(solution)/shard_map/ppermute | solution.py:592
  165.7 22.1 %collective-permute-start.25 = (bf16[256,1024]{1,0:T(8,128)(2,1)S(1)}, bf16[256,1024]{1,0:T(8,128)(2,1)S(1)}, u32[]{:S(2)}, u32[]{:S(2)}) collective-permute-start(bf16[256,1024]{1,0:T(8,128)(2,1)S(1)} %broadcast_select_fusion.refs_14_.refs_12_.refs_8_), channel_id=1, source_target_pairs={{0,16},{16,0},{1,17},{17,1},{2,18},{18,2},{3,19},{19,3},{4,20},{20... | collective-permute-start | bytes 1572872 | tf_op jit(solution)/shard_map/ppermute | solution.py:592
  178.0 10.6 %collective-permute-start.22 = (bf16[256,1024]{1,0:T(8,128)(2,1)}, bf16[256,1024]{1,0:T(8,128)(2,1)S(1)}, u32[]{:S(2)}, u32[]{:S(2)}) collective-permute-start(bf16[256,1024]{1,0:T(8,128)(2,1)} %collective-permute-done.15), channel_id=1, source_target_pairs={{4,8},{6,10},{8,12},{10,14},{5,9},{7,11},{9,13},{11,15},{20,24},{2... | collective-permute-start | bytes 1572872 | tf_op jit(solution)/shard_map/ppermute | solution.py:602
  178.7 15.9 %collective-permute-start.23 = (bf16[256,1024]{1,0:T(8,128)(2,1)}, bf16[256,1024]{1,0:T(8,128)(2,1)S(1)}, u32[]{:S(2)}, u32[]{:S(2)}) collective-permute-start(bf16[256,1024]{1,0:T(8,128)(2,1)} %collective-permute-done.16), channel_id=1, source_target_pairs={{8,4},{10,6},{4,0},{6,2},{9,5},{11,7},{5,1},{7,3},{24,20},{26,22},... | collective-permute-start | bytes 1572872 | tf_op jit(solution)/shard_map/ppermute | solution.py:602
  180.0 14.6 %collective-permute-start.24 = (bf16[256,1024]{1,0:T(8,128)(2,1)}, bf16[256,1024]{1,0:T(8,128)(2,1)S(1)}, u32[]{:S(2)}, u32[]{:S(2)}) collective-permute-start(bf16[256,1024]{1,0:T(8,128)(2,1)} %collective-permute-done.21.refs_1_), channel_id=1, source_target_pairs={{0,1},{1,0},{2,3},{3,2},{4,5},{5,4},{6,7},{7,6},{8,9},{9,8},{10,11... | collective-permute-start | bytes 1572872 | tf_op jit(solution)/shard_map/ppermute | solution.py:714
  182.0 14.6 %collective-permute-start.26 = (bf16[256,1024]{1,0:T(8,128)(2,1)}, bf16[256,1024]{1,0:T(8,128)(2,1)}, u32[]{:S(2)}, u32[]{:S(2)}) collective-permute-start(bf16[256,1024]{1,0:T(8,128)(2,1)} %broadcast_select_fusion.1.refs_2_), channel_id=1, source_target_pairs={{0,2},{2,0},{4,6},{6,4},{8,10},{10,8},{12,14},{14,12},{1,3},{3,1},... | collective-permute-start | bytes 1572872 | tf_op jit(solution)/shard_map/ppermute | solution.py:595
  196.6 5.9 %collective-permute-start.29 = (bf16[256,1024]{1,0:T(8,128)(2,1)}, bf16[256,1024]{1,0:T(8,128)(2,1)}, u32[]{:S(2)}, u32[]{:S(2)}) collective-permute-start(bf16[256,1024]{1,0:T(8,128)(2,1)} %broadcast_select_fusion.1.refs_2_), channel_id=1, source_target_pairs={{0,1},{1,0},{2,3},{3,2},{4,5},{5,4},{6,7},{7,6},{8,9},{9,8},{10,11... | collective-permute-start | bytes 1572872 | tf_op jit(solution)/shard_map/ppermute | solution.py:714
  196.6 5.9 %collective-permute-start.30 = (bf16[256,1024]{1,0:T(8,128)(2,1)}, bf16[256,1024]{1,0:T(8,128)(2,1)}, u32[]{:S(2)}, u32[]{:S(2)}) collective-permute-start(bf16[256,1024]{1,0:T(8,128)(2,1)} %collective-permute-done.26.refs_3_), channel_id=1, source_target_pairs={{0,1},{1,0},{2,3},{3,2},{4,5},{5,4},{6,7},{7,6},{8,9},{9,8},{10,11... | collective-permute-start | bytes 1572872 | tf_op jit(solution)/shard_map/ppermute | solution.py:714
  197.2 19.1 %collective-permute-start.27 = (bf16[256,1024]{1,0:T(8,128)(2,1)}, bf16[256,1024]{1,0:T(8,128)(2,1)}, u32[]{:S(2)}, u32[]{:S(2)}) collective-permute-start(bf16[256,1024]{1,0:T(8,128)(2,1)} %copy-done.14), channel_id=1, source_target_pairs={{8,12},{10,14},{9,13},{11,15},{24,28},{26,30},{25,29},{27,31}} | collective-permute-start | bytes 1572872 | tf_op jit(solution)/shard_map/ppermute | solution.py:602
  198.6 19.5 %collective-permute-start.28 = (bf16[256,1024]{1,0:T(8,128)(2,1)}, bf16[256,1024]{1,0:T(8,128)(2,1)}, u32[]{:S(2)}, u32[]{:S(2)}) collective-permute-start(bf16[256,1024]{1,0:T(8,128)(2,1)} %copy-done.16), channel_id=1, source_target_pairs={{4,0},{6,2},{5,1},{7,3},{20,16},{22,18},{21,17},{23,19}} | collective-permute-start | bytes 1572872 | tf_op jit(solution)/shard_map/ppermute | solution.py:602
  202.0 16.1 %collective-permute-start.31 = (bf16[256,1024]{1,0:T(8,128)(2,1)}, bf16[256,1024]{1,0:T(8,128)(2,1)}, u32[]{:S(2)}, u32[]{:S(2)}) collective-permute-start(bf16[256,1024]{1,0:T(8,128)(2,1)} %fusion.1.refs_0_), channel_id=1, source_target_pairs={{0,2},{2,0},{4,6},{6,4},{8,10},{10,8},{12,14},{14,12},{1,3},{3,1},... | collective-permute-start | bytes 1572872 | tf_op jit(solution)/shard_map/ppermute | solution.py:595
  206.7 11.9 %copy-start.15 = (bf16[256,1024]{1,0:T(8,128)(2,1)S(1)}, bf16[256,1024]{1,0:T(8,128)(2,1)}, u32[]{:S(2)}) copy-start(bf16[256,1024]{1,0:T(8,128)(2,1)} %copy-done.14) | copy-start | bytes 1572868
  206.7 11.9 %copy-start.17 = (bf16[256,1024]{1,0:T(8,128)(2,1)S(1)}, bf16[256,1024]{1,0:T(8,128)(2,1)}, u32[]{:S(2)}) copy-start(bf16[256,1024]{1,0:T(8,128)(2,1)} %copy-done.16) | copy-start | bytes 1572868
  218.1 2.4 collective-permute-start.33
  218.1 2.9 %collective-permute-start.34 = (bf16[256,1024]{1,0:T(8,128)(2,1)}, bf16[256,1024]{1,0:T(8,128)(2,1)S(1)}, u32[]{:S(2)}, u32[]{:S(2)}) collective-permute-start(bf16[256,1024]{1,0:T(8,128)(2,1)} %collective-permute-done.31.refs_1_), channel_id=1, source_target_pairs={{0,1},{1,0},{2,3},{3,2},{4,5},{5,4},{6,7},{7,6},{8,9},{9,8},{10,11... | collective-permute-start | bytes 1572872 | tf_op jit(solution)/shard_map/ppermute | solution.py:714
  219.8 2.0 collective-permute-start.35
  219.9 14.4 %collective-permute-start.32 = (bf16[256,1024]{1,0:T(8,128)(2,1)S(1)}, bf16[256,1024]{1,0:T(8,128)(2,1)}, u32[]{:S(2)}, u32[]{:S(2)}) collective-permute-start(bf16[256,1024]{1,0:T(8,128)(2,1)S(1)} %select_select_fusion.1.refs_2_), channel_id=1, source_target_pairs={{0,2},{2,0},{4,6},{6,4},{8,10},{10,8},{12,14},{14,12},{1,3},{3,1},... | collective-permute-start | bytes 1572872 | tf_op jit(solution)/shard_map/ppermute | solution.py:595
  234.3 2.3 collective-permute-start.36
  250.4 14.2 %collective-permute-start.37 = (bf16[512,512]{1,0:T(8,128)(2,1)}, bf16[512,512]{1,0:T(8,128)(2,1)S(1)}, u32[]{:S(2)}, u32[]{:S(2)}) collective-permute-start(bf16[512,512]{1,0:T(8,128)(2,1)} %decode_rows.3), channel_id=1, source_target_pairs={{0,2},{2,0},{4,6},{6,4},{8,10},{10,8},{12,14},{14,12},{1,3},{3,1},... | collective-permute-start | bytes 1572872 | tf_op jit(solution)/shard_map/ppermute | solution.py:595
  (23 other events, 59.0 us)

commit v13 on v10

--- a/solution.py
+++ b/solution.py
@@ -625,8 +625,6 @@
     near_inputs, out_far, kv_for_near = lax.optimization_barrier(
         (near_inputs, out_far, kv_for_near)
     )
-    out_far = jnp.concatenate(out_far)
-    out_far_other = over_groups(out_far)
 
     kv_own = columns((w_key, w_value), y)
     kv_near = over_near(kv_for_near)
@@ -641,6 +639,8 @@
     hops[1] = hop(1, hops[0])
     early = [k for k in range(1, far) if max(k, far - k) < 3]
     rest = [k for k in range(1, far) if k not in early]
+    out_far = jnp.concatenate(out_far)
+    out_far_other = over_groups(out_far)
     out_near = over_near(jnp.concatenate([w_out, counted, out_far]))
     out_near_other = over_groups(out_near[w_out.shape[0] + EXTRA :])
     columns_of_slice = [[2 * i + j for i in range(far)] for j in range(2)]
@@ -667,8 +667,8 @@
     own_queries = columns((queries,), y)
     near_queries = over_near(columns((queries,), 1 - y))
 
-    parts, out_near, out_far_other, out_near_other, hops, near_queries = lax.optimization_barrier(
-        (parts, out_near, out_far_other, out_near_other, hops, near_queries)
+    parts, out_near, out_far_other, out_near_other, near_queries = lax.optimization_barrier(
+        (parts, out_near, out_far_other, out_near_other, near_queries)
     )
     attended, for_near = merge(y, parts, far)
     for_near, hops = lax.optimization_barrier((for_near, hops))

time: 260 us -> 255 us (0.981)
  waiting for transfers between devices: 107 us -> 98.3 us
    ppermute x12, waiting for transfers between devices: 30.8 us -> 22.6 us  [hop(): lax.ppermute(v, 'pos', hop_perm(pos, step, way))]
    ppermute x5, waiting for transfers between devices: 6.92 us -> 9.9 us  [over_groups(): return lax.ppermute(value, 'groups', swap_perm(groups))]
    unnamed x41 -> x47, local copies, waits for them, and re-layouts: 9.25 us -> 11.9 us
  transfers between devices with their start and end apart: 39 -> 39, of which waited for: 18 -> 18; matrix products, arithmetic and copies ran while one was open for 9% -> 10% of each run, Pallas kernels for 19% -> 20%
where the time goes in v13:
time: 255 us; the launch traced here: 253 us
  waiting for transfers between devices  98.3 us (39%)
  Pallas kernels  62 us (24%)
  starting transfers between devices  56.4 us (22%)
  local copies, waits for them, and re-layouts  20.1 us (8%)
  other arithmetic  14.2 us (6%)
    ppermute x9, waiting for transfers between devices, over_near(): return lax.ppermute(value, 'pos', near)  38.6 us
    ppermute x12, starting transfers between devices, hop(): lax.ppermute(v, 'pos', hop_perm(pos, step, way))  23.3 us
    ppermute x12, waiting for transfers between devices, hop(): lax.ppermute(v, 'pos', hop_perm(pos, step, way))  22.6 us
    ppermute x3, waiting for transfers between devices, over_far(): return lax.ppermute(value, 'pos', shift_perm(pos, k))  20.4 us
    pallas_call x3, Pallas kernels, latent_keys_values(): pl.pallas_call(functools.partial(latents_kernel, pieces), grid_spec=grid_...  18.8 us
    pallas_call x2, Pallas kernels, decode(): pl.pallas_call(functools.partial(decode_kernel, len(keys_values)), grid=(...  16.7 us
    ppermute x9, starting transfers between devices, over_near(): return lax.ppermute(value, 'pos', near)  14.5 us
    pallas_call x1, Pallas kernels, encode(): pl.pallas_call(encode_kernel, grid_spec=grid_spec, out_shape=jax.ShapeDty...  14.4 us
  transfers between devices with their start and end apart: 39, of which 18 were waited for; matrix products, arithmetic and copies ran while one was open for 10% of the time, Pallas kernels for 20%

profile of v13, /device:TPU:0, one launch (start us, length us, event | category | flops | bytes accessed | tf_op | source)
XLA Modules:
  0.0 252.7 jit_solution(15309271435731880719)
XLA Ops:
  2.9 3.0 %collective-permute-start = (bf16[528,1024]{1,0:T(8,128)(2,1)S(1)}, bf16[528,1024]{1,0:T(8,128)(2,1)}, u32[]{:S(2)}, u32[]{:S(2)}) collective-permute-start(bf16[528,1024]{1,0:T(8,128)(2,1)S(1)} %pad_maximum_fusion), channel_id=1, source_target_pairs={{0,2},{2,0},{4,6},{6,4},{8,10},{10,8},{12,14},{14,12},{1,3},{3,1},... | collective-permute-start | bytes 3244040 | tf_op jit(solution)/shard_map/ppermute | solution.py:586
  8.4 3.6 %collective-permute-start.1 = (bf16[528,256]{1,0:T(8,128)(2,1)}, bf16[528,256]{1,0:T(8,128)(2,1)}, u32[]{:S(2)}, u32[]{:S(2)}) collective-permute-start(bf16[528,256]{1,0:T(8,128)(2,1)} %pad_maximum_fusion.3), channel_id=1, source_target_pairs={{4,0},{6,2},{8,4},{10,6},{12,8},{14,10},{0,12},{2,14},{5,1},{7,3},... | collective-permute-start | bytes 811016 | tf_op jit(solution)/shard_map/ppermute | solution.py:589
  14.6 4.7 %collective-permute-done.1 = bf16[528,256]{1,0:T(8,128)(2,1)} collective-permute-done((bf16[528,256]{1,0:T(8,128)(2,1)}, bf16[528,256]{1,0:T(8,128)(2,1)}, u32[]{:S(2)}, u32[]{:S(2)}) %collective-permute-start.1) | collective-permute-done | bytes 270368 | tf_op jit(solution)/shard_map/ppermute | solution.py:589
  19.2 15.8 %collective-permute-done.2 = bf16[528,256]{1,0:T(8,128)(2,1)} collective-permute-done((bf16[528,256]{1,0:T(8,128)(2,1)}, bf16[528,256]{1,0:T(8,128)(2,1)}, u32[]{:S(2)}, u32[]{:S(2)}) %collective-permute-start.2) | collective-permute-done | bytes 270368 | tf_op jit(solution)/shard_map/ppermute | solution.py:589
  35.6 14.4 %encode_rows.1 = bf16[2112,512]{1,0:T(8,128)(2,1)} custom-call(s32[1]{0:T(128)} %bitcast.9.ids_ref, bf16[2048,1024]{1,0:T(8,128)(2,1)} %q_ref.1, bf16[512,1024]{1,0:T(8,128)(2,1)} %k_ref.1, bf16[512,1024]{1,0:T(8,128)(2,1)} %v_ref.1, bf16[16,1024]{1,0:T(8,128)(2,1)} %copy-done.17, bf16[528,1024]{1,0:T(8,128)(2,1)} %collective-permute-done.near_ref, ...), custom_call_target="tpu_custom_call" | custom-call | flops 8589934592 | bytes 2097152 | tf_op jit(solution)/shard_map/encode_rows/pallas_call | solution.py:262
  50.0 4.0 %all-to-all-start = ((bf16[4,528,512]{2,1,0:T(8,128)(2,1)}), bf16[4,528,512]{2,1,0:T(8,128)(2,1)S(1)}, u32[]{:S(2)}, u32[]{:S(2)}) async-start(bf16[4,528,512]{2,1,0:T(8,128)(2,1)} %bitcast.52), calls=%async_computation | async-start | bytes 4325376 | tf_op jit(solution)/shard_map/all_to_all | solution.py:647
  54.1 1.9 constant_dynamic-update-slice_fusion.7
  56.0 1.8 constant_dynamic-update-slice_fusion.6
  58.6 1.5 collective-permute-start.5
  60.6 1.6 collective-permute-start.6
  62.1 26.7 %collective-permute-done.5.refs_3_ = bf16[2624,256]{1,0:T(8,128)(2,1)S(1)} collective-permute-done((bf16[2624,256]{1,0:T(8,128)(2,1)}, bf16[2624,256]{1,0:T(8,128)(2,1)S(1)}, u32[]{:S(2)}, u32[]{:S(2)}) %collective-permute-start.5) | collective-permute-done | bytes 1343520 | tf_op jit(solution)/shard_map/ppermute | solution.py:586
  89.8 1.5 collective-permute-start.7
  92.4 1.5 collective-permute-start.8
  93.9 2.0 pad_maximum_fusion.2
  95.9 4.4 %collective-permute-start.9 = (bf16[256,1024]{1,0:T(8,128)(2,1)}, bf16[256,1024]{1,0:T(8,128)(2,1)}, u32[]{:S(2)}, u32[]{:S(2)}) collective-permute-start(bf16[256,1024]{1,0:T(8,128)(2,1)} %get-tuple-element.153), channel_id=1, source_target_pairs={{0,4},{2,6},{4,8},{6,10},{8,12},{10,14},{1,5},{3,7},{5,9},{7,11},{... | collective-permute-start | bytes 1572872 | tf_op jit(solution)/shard_map/ppermute | solution.py:593
  101.6 2.4 collective-permute-done.8.q_ref
  104.0 3.9 %collective-permute-done.7.refs_4_ = bf16[1584,256]{1,0:T(8,128)(2,1)} collective-permute-done((bf16[1584,256]{1,0:T(8,128)(2,1)}, bf16[1584,256]{1,0:T(8,128)(2,1)}, u32[]{:S(2)}, u32[]{:S(2)}) %collective-permute-start.7) | collective-permute-done | bytes 811040 | tf_op jit(solution)/shard_map/ppermute | solution.py:583
  107.8 1.9 merge_rows.1
  110.4 3.7 %collective-permute-done.10 = bf16[256,1024]{1,0:T(8,128)(2,1)} collective-permute-done((bf16[256,1024]{1,0:T(8,128)(2,1)}, bf16[256,1024]{1,0:T(8,128)(2,1)}, u32[]{:S(2)}, u32[]{:S(2)}) %collective-permute-start.10) | collective-permute-done | bytes 524320 | tf_op jit(solution)/shard_map/ppermute | solution.py:593
  116.1 1.6 collective-permute-start.11
  118.3 4.2 %collective-permute-done.11.near_ref = bf16[256,512]{1,0:T(8,128)(2,1)S(1)} collective-permute-done((bf16[256,512]{1,0:T(8,128)(2,1)S(1)}, bf16[256,512]{1,0:T(8,128)(2,1)S(1)}, u32[]{:S(2)}, u32[]{:S(2)}) %collective-permute-start.11) | collective-permute-done | bytes 262176 | tf_op jit(solution)/shard_map/ppermute | solution.py:586
  123.3 5.7 %project_rows.1.mine_ref = f32[256,2048]{1,0:T(8,128)} custom-call(s32[10]{0:T(128)} %stack.82.ids_ref, bf16[256,512]{1,0:T(8,128)(2,1)} %copy-done.2, bf16[256,512]{1,0:T(8,128)(2,1)} %copy-done.16, bf16[1024,256]{1,0:T(8,128)(2,1)} %refs_0_.1, bf16[1584,256]{1,0:T(8,128)(2,1)} %get-tuple-element.158.refs_1_, ...), custom_call_target="tpu_custom_call" | custom-call | flops 1073741824 | bytes 6291456 | tf_op jit(solution)/shard_map/project_rows/pallas_call | solution.py:363
  130.5 1.5 collective-permute-start.17
  133.3 2.0 collective-permute-start.19
  135.4 4.5 %norm_rows.1 = (f32[256,1024]{1,0:T(8,128)}, bf16[256,1024]{1,0:T(8,128)(2,1)}, bf16[256,1024]{1,0:T(8,128)(2,1)}) custom-call(s32[1]{0:T(128)} %bitcast.ids_ref, f32[256,2048]{1,0:T(8,128)} %project_rows.1.mine_ref, f32[256,2048]{1,0:T(8,128)} %collective-permute-done.14.theirs_ref, bf16[256,2048]{1,0:T(8,128)(2,1)} %latent_ref.1, f32[1,2048]{1,0:T(1,128)} %bitcast.54), custom_call_target="tpu_custom_call" | custom-call | flops 3145728 | bytes 6815744 | tf_op jit(solution)/shard_map/norm_rows/pallas_call | solution.py:397
  139.9 6.1 %collective-permute-start.15 = (bf16[256,1024]{1,0:T(8,128)(2,1)}, bf16[256,1024]{1,0:T(8,128)(2,1)}, u32[]{:S(2)}, u32[]{:S(2)}) collective-permute-start(bf16[256,1024]{1,0:T(8,128)(2,1)} %get-tuple-element.120.refs_0_), channel_id=1, source_target_pairs={{0,4},{2,6},{4,8},{6,10},{8,12},{10,14},{1,5},{3,7},{5,9},{7,11},{... | collective-permute-start | bytes 1572872 | tf_op jit(solution)/shard_map/ppermute | solution.py:593
  149.0 1.8 collective-permute-start.22
  150.8 6.2 %collective-permute-done.15 = bf16[256,1024]{1,0:T(8,128)(2,1)} collective-permute-done((bf16[256,1024]{1,0:T(8,128)(2,1)}, bf16[256,1024]{1,0:T(8,128)(2,1)}, u32[]{:S(2)}, u32[]{:S(2)}) %collective-permute-start.15) | collective-permute-done | bytes 524320 | tf_op jit(solution)/shard_map/ppermute | solution.py:593
  157.0 4.9 %collective-permute-done.16 = bf16[256,1024]{1,0:T(8,128)(2,1)} collective-permute-done((bf16[256,1024]{1,0:T(8,128)(2,1)}, bf16[256,1024]{1,0:T(8,128)(2,1)}, u32[]{:S(2)}, u32[]{:S(2)}) %collective-permute-start.16) | collective-permute-done | bytes 524320 | tf_op jit(solution)/shard_map/ppermute | solution.py:593
  161.9 1.5 collective-permute-start.20
  166.4 1.9 broadcast_select_fusion.2.refs_2_
  168.3 1.6 collective-permute-start.24
  171.0 1.6 collective-permute-start.27
  172.5 7.1 %collective-permute-done.21 = bf16[256,1024]{1,0:T(8,128)(2,1)} collective-permute-done((bf16[256,1024]{1,0:T(8,128)(2,1)}, bf16[256,1024]{1,0:T(8,128)(2,1)}, u32[]{:S(2)}, u32[]{:S(2)}) %collective-permute-start.21) | collective-permute-done | bytes 524320 | tf_op jit(solution)/shard_map/ppermute | solution.py:593
  181.7 1.5 collective-permute-start.25
  183.2 2.1 fusion.1.refs_0_
  185.3 4.8 %collective-permute-done.27.refs_15_.refs_13_.refs_9_ = bf16[256,1024]{1,0:T(8,128)(2,1)} collective-permute-done((bf16[256,1024]{1,0:T(8,128)(2,1)S(1)}, bf16[256,1024]{1,0:T(8,128)(2,1)}, u32[]{:S(2)}, u32[]{:S(2)}) %collective-permute-start.27) | collective-permute-done | bytes 524320 | tf_op jit(solution)/shard_map/ppermute | solution.py:583
  194.9 8.5 %latent_keys_values.3.refs_0_.refs_3_ = bf16[1024,1024]{1,0:T(8,128)(2,1)S(1)} custom-call(s32[9]{0:T(128)S(1)} %stack.92.ids_ref, bf16[256,1024]{1,0:T(8,128)(2,1)S(1)} %copy-done.3, bf16[256,1024]{1,0:T(8,128)(2,1)} %collective-permute-done.22.refs_1_, bf16[256,1024]{1,0:T(8,128)(2,1)} %broadcast_select_fusion.2.refs_2_, ...), custom_call_target="tpu_custom_call" | custom-call | flops 4294967296 | bytes 4194304 | tf_op jit(solution)/shard_map/latent_keys_values/pallas_call | solution.py:460
  207.2 1.6 collective-permute-start.32
  209.1 6.4 %latent_keys_values.4.refs_1_.refs_4_ = bf16[768,1024]{1,0:T(8,128)(2,1)S(1)} custom-call(s32[9]{0:T(128)S(1)} %stack.92.ids_ref, bf16[256,1024]{1,0:T(8,128)(2,1)} %fusion.1.refs_0_, bf16[256,1024]{1,0:T(8,128)(2,1)} %collective-permute-done.31.refs_1_, bf16[256,1024]{1,0:T(8,128)(2,1)S(1)} %select_select_fusion.1.refs_2_, ...), custom_call_target="tpu_custom_call" | custom-call | flops 3221225472 | bytes 4194304 | tf_op jit(solution)/shard_map/latent_keys_values/pallas_call | solution.py:460
  216.6 5.0 %collective-permute-done.32.refs_0_ = bf16[256,1024]{1,0:T(8,128)(2,1)} collective-permute-done((bf16[256,1024]{1,0:T(8,128)(2,1)S(1)}, bf16[256,1024]{1,0:T(8,128)(2,1)}, u32[]{:S(2)}, u32[]{:S(2)}) %collective-permute-start.32) | collective-permute-done | bytes 524320 | tf_op jit(solution)/shard_map/ppermute | solution.py:586
  221.6 2.2 collective-permute-done.36.refs_1_
  223.9 3.8 %latent_keys_values.5.refs_2_.refs_5_ = bf16[256,1024]{1,0:T(8,128)(2,1)S(1)} custom-call(s32[9]{0:T(128)S(1)} %stack.92.ids_ref, bf16[256,1024]{1,0:T(8,128)(2,1)} %collective-permute-done.32.refs_0_, bf16[256,1024]{1,0:T(8,128)(2,1)} %collective-permute-done.36.refs_1_, bf16[256,1024]{1,0:T(8,128)(2,1)S(1)} %get-tuple-element.132.refs_8_.refs_6_.refs_2_, ...), custom_call_target="tpu_custom_call" | custom-call | flops 1073741824 | bytes 4194304 | tf_op jit(solution)/shard_map/latent_keys_values/pallas_call | solution.py:460
  228.5 8.3 %decode_rows.3 = bf16[512,512]{1,0:T(8,128)(2,1)} custom-call(bf16[512,512]{1,0:T(8,128)(2,1)} %collective-permute-done.8.q_ref, bf16[1024,1024]{1,0:T(8,128)(2,1)} %copy-done.6, bf16[768,1024]{1,0:T(8,128)(2,1)} %copy-done.5, bf16[256,1024]{1,0:T(8,128)(2,1)} %copy-done.1, bf16[1024,1024]{1,0:T(8,128)(2,1)} %copy-done.6, bf16[768,1024]{1,0:T(8,128)(2,1)} %copy-done.5, ...), custom_call_target="tpu_custom_call" | custom-call | flops 8589934592 | bytes 5767168 | tf_op jit(solution)/shard_map/decode_rows/pallas_call | solution.py:521
  236.8 1.5 collective-permute-start.37
  238.3 8.4 %decode_rows.2 = f32[512,512]{1,0:T(8,128)} custom-call(bf16[512,512]{1,0:T(8,128)(2,1)} %get-tuple-element.150.q_ref, bf16[1024,1024]{1,0:T(8,128)(2,1)} %copy-done.6, bf16[768,1024]{1,0:T(8,128)(2,1)} %copy-done.5, bf16[256,1024]{1,0:T(8,128)(2,1)} %copy-done.1, bf16[1024,1024]{1,0:T(8,128)(2,1)} %copy-done.6, bf16[768,1024]{1,0:T(8,128)(2,1)} %copy-done.5, ...), custom_call_target="tpu_custom_call" | custom-call | flops 8589934592 | bytes 5767168 | tf_op jit(solution)/shard_map/decode_rows/pallas_call | solution.py:521
  246.7 4.2 %collective-permute-done.37 = bf16[512,512]{1,0:T(8,128)(2,1)S(1)} collective-permute-done((bf16[512,512]{1,0:T(8,128)(2,1)}, bf16[512,512]{1,0:T(8,128)(2,1)S(1)}, u32[]{:S(2)}, u32[]{:S(2)}) %collective-permute-start.37) | collective-permute-done | bytes 524320 | tf_op jit(solution)/shard_map/ppermute | solution.py:749
  251.1 1.6 fusion
  (128 shorter events, 39.3 us)
Async XLA Ops:
  0.6 59.5 %copy-start = (bf16[3,1024]{1,0:T(4,128)(2,1)S(1)}, bf16[3,1024]{1,0:T(4,128)(2,1)}, u32[]{:S(2)}) copy-start(bf16[3,1024]{1,0:T(4,128)(2,1)} %param.25) | copy-start | bytes 18436
  2.7 10.2 %copy-start.19 = (f32[3,8]{1,0:T(4,128)S(1)}, f32[3,8]{1,0:T(4,128)}, u32[]{:S(2)}) copy-start(f32[3,8]{1,0:T(4,128)} %param.26) | copy-start | bytes 292
  2.7 10.9 %copy-start.12 = (bf16[256,1024]{1,0:T(8,128)(2,1)S(1)}, bf16[256,1024]{1,0:T(8,128)(2,1)}, u32[]{:S(2)}) copy-start(bf16[256,1024]{1,0:T(8,128)(2,1)} %param.22) | copy-start | bytes 1572868
  2.8 10.9 %copy-start.13 = (bf16[256,1024]{1,0:T(8,128)(2,1)S(1)}, bf16[256,1024]{1,0:T(8,128)(2,1)}, u32[]{:S(2)}) copy-start(bf16[256,1024]{1,0:T(8,128)(2,1)} %param.21) | copy-start | bytes 1572868
  2.9 32.1 %collective-permute-start = (bf16[528,1024]{1,0:T(8,128)(2,1)S(1)}, bf16[528,1024]{1,0:T(8,128)(2,1)}, u32[]{:S(2)}, u32[]{:S(2)}) collective-permute-start(bf16[528,1024]{1,0:T(8,128)(2,1)S(1)} %pad_maximum_fusion), channel_id=1, source_target_pairs={{0,2},{2,0},{4,6},{6,4},{8,10},{10,8},{12,14},{14,12},{1,3},{3,1},... | collective-permute-start | bytes 3244040 | tf_op jit(solution)/shard_map/ppermute | solution.py:586
  8.4 10.9 %collective-permute-start.1 = (bf16[528,256]{1,0:T(8,128)(2,1)}, bf16[528,256]{1,0:T(8,128)(2,1)}, u32[]{:S(2)}, u32[]{:S(2)}) collective-permute-start(bf16[528,256]{1,0:T(8,128)(2,1)} %pad_maximum_fusion.3), channel_id=1, source_target_pairs={{4,0},{6,2},{8,4},{10,6},{12,8},{14,10},{0,12},{2,14},{5,1},{7,3},... | collective-permute-start | bytes 811016 | tf_op jit(solution)/shard_map/ppermute | solution.py:589
  12.0 23.0 %collective-permute-start.2 = (bf16[528,256]{1,0:T(8,128)(2,1)}, bf16[528,256]{1,0:T(8,128)(2,1)}, u32[]{:S(2)}, u32[]{:S(2)}) collective-permute-start(bf16[528,256]{1,0:T(8,128)(2,1)} %pad_maximum_fusion.3), channel_id=1, source_target_pairs={{8,0},{10,2},{12,4},{14,6},{0,8},{2,10},{4,12},{6,14},{9,1},{11,3}... | collective-permute-start | bytes 811016 | tf_op jit(solution)/shard_map/ppermute | solution.py:589
  12.0 23.0 %collective-permute-start.3 = (bf16[528,256]{1,0:T(8,128)(2,1)}, bf16[528,256]{1,0:T(8,128)(2,1)S(1)}, u32[]{:S(2)}, u32[]{:S(2)}) collective-permute-start(bf16[528,256]{1,0:T(8,128)(2,1)} %pad_maximum_fusion.3), channel_id=1, source_target_pairs={{12,0},{14,2},{0,4},{2,6},{4,8},{6,10},{8,12},{10,14},{13,1},{15,3... | collective-permute-start | bytes 811016 | tf_op jit(solution)/shard_map/ppermute | solution.py:589
  35.0 15.0 %copy-start.14 = (bf16[528,256]{1,0:T(8,128)(2,1)}, bf16[528,256]{1,0:T(8,128)(2,1)S(1)}, u32[]{:S(2)}) copy-start(bf16[528,256]{1,0:T(8,128)(2,1)S(1)} %collective-permute-done.3) | copy-start | bytes 811012
  35.0 15.0 %collective-permute-start.4 = (bf16[256,1024]{1,0:T(8,128)(2,1)S(1)}, bf16[256,1024]{1,0:T(8,128)(2,1)S(1)}, u32[]{:S(2)}, u32[]{:S(2)}) collective-permute-start(bf16[256,1024]{1,0:T(8,128)(2,1)S(1)} %pad_maximum_fusion.1), channel_id=1, source_target_pairs={{0,2},{2,0},{4,6},{6,4},{8,10},{10,8},{12,14},{14,12},{1,3},{3,1},... | collective-permute-start | bytes 1572872 | tf_op jit(solution)/shard_map/ppermute | solution.py:586
  50.0 7.7 %copy-start.15 = (bf16[528,256]{1,0:T(8,128)(2,1)S(1)}, bf16[528,256]{1,0:T(8,128)(2,1)}, u32[]{:S(2)}) copy-start(bf16[528,256]{1,0:T(8,128)(2,1)} %copy-done.14) | copy-start | bytes 811012
  50.0 57.8 %all-to-all-start = ((bf16[4,528,512]{2,1,0:T(8,128)(2,1)}), bf16[4,528,512]{2,1,0:T(8,128)(2,1)S(1)}, u32[]{:S(2)}, u32[]{:S(2)}) async-start(bf16[4,528,512]{2,1,0:T(8,128)(2,1)} %bitcast.52), calls=%async_computation | async-start | bytes 4325376 | tf_op jit(solution)/shard_map/all_to_all | solution.py:647
  54.1 6.0 %copy-start.10 = (bf16[512,1024]{1,0:T(8,128)(2,1)S(1)}, bf16[512,1024]{1,0:T(8,128)(2,1)}, u32[]{:S(2)}) copy-start(bf16[512,1024]{1,0:T(8,128)(2,1)} %param.23) | copy-start | bytes 3145732
  58.6 30.3 %collective-permute-start.5 = (bf16[2624,256]{1,0:T(8,128)(2,1)}, bf16[2624,256]{1,0:T(8,128)(2,1)S(1)}, u32[]{:S(2)}, u32[]{:S(2)}) collective-permute-start(bf16[2624,256]{1,0:T(8,128)(2,1)} %get-tuple-element.159), channel_id=1, source_target_pairs={{0,2},{2,0},{4,6},{6,4},{8,10},{10,8},{12,14},{14,12},{1,3},{3,1},... | collective-permute-start | bytes 4030472 | tf_op jit(solution)/shard_map/ppermute | solution.py:586
  60.6 33.3 %copy-start.11 = (bf16[256,512]{1,0:T(8,128)(2,1)S(1)}, bf16[256,512]{1,0:T(8,128)(2,1)}, u32[]{:S(2)}) copy-start(bf16[256,512]{1,0:T(8,128)(2,1)} %get-tuple-element.156) | copy-start | bytes 786436
  60.6 43.4 %collective-permute-start.6 = (bf16[1584,256]{1,0:T(8,128)(2,1)}, bf16[1584,256]{1,0:T(8,128)(2,1)}, u32[]{:S(2)}, u32[]{:S(2)}) collective-permute-start(bf16[1584,256]{1,0:T(8,128)(2,1)} %get-tuple-element.158.refs_1_), channel_id=1, source_target_pairs={{0,16},{16,0},{1,17},{17,1},{2,18},{18,2},{3,19},{19,3},{4,20},{20... | collective-permute-start | bytes 2433032 | tf_op jit(solution)/shard_map/ppermute | solution.py:583
  89.8 18.0 %collective-permute-start.7 = (bf16[1584,256]{1,0:T(8,128)(2,1)}, bf16[1584,256]{1,0:T(8,128)(2,1)}, u32[]{:S(2)}, u32[]{:S(2)}) collective-permute-start(bf16[1584,256]{1,0:T(8,128)(2,1)} %slice.62), channel_id=1, source_target_pairs={{0,16},{16,0},{1,17},{17,1},{2,18},{18,2},{3,19},{19,3},{4,20},{20... | collective-permute-start | bytes 2433032 | tf_op jit(solution)/shard_map/ppermute | solution.py:583
  92.4 11.6 %collective-permute-start.8 = (bf16[512,512]{1,0:T(8,128)(2,1)}, bf16[512,512]{1,0:T(8,128)(2,1)}, u32[]{:S(2)}, u32[]{:S(2)}) collective-permute-start(bf16[512,512]{1,0:T(8,128)(2,1)} %get-tuple-element.151), channel_id=1, source_target_pairs={{0,2},{2,0},{4,6},{6,4},{8,10},{10,8},{12,14},{14,12},{1,3},{3,1},... | collective-permute-start | bytes 1572872 | tf_op jit(solution)/shard_map/ppermute | solution.py:586
  95.9 14.6 %collective-permute-start.9 = (bf16[256,1024]{1,0:T(8,128)(2,1)}, bf16[256,1024]{1,0:T(8,128)(2,1)}, u32[]{:S(2)}, u32[]{:S(2)}) collective-permute-start(bf16[256,1024]{1,0:T(8,128)(2,1)} %get-tuple-element.153), channel_id=1, source_target_pairs={{0,4},{2,6},{4,8},{6,10},{8,12},{10,14},{1,5},{3,7},{5,9},{7,11},{... | collective-permute-start | bytes 1572872 | tf_op jit(solution)/shard_map/ppermute | solution.py:593
  100.3 13.8 %collective-permute-start.10 = (bf16[256,1024]{1,0:T(8,128)(2,1)}, bf16[256,1024]{1,0:T(8,128)(2,1)}, u32[]{:S(2)}, u32[]{:S(2)}) collective-permute-start(bf16[256,1024]{1,0:T(8,128)(2,1)} %get-tuple-element.153), channel_id=1, source_target_pairs={{12,8},{14,10},{8,4},{10,6},{4,0},{6,2},{13,9},{15,11},{9,5},{11,7... | collective-permute-start | bytes 1572872 | tf_op jit(solution)/shard_map/ppermute | solution.py:593
  114.1 14.8 %collective-permute-start.12 = (bf16[256,1024]{1,0:T(8,128)(2,1)}, bf16[256,1024]{1,0:T(8,128)(2,1)S(1)}, u32[]{:S(2)}, u32[]{:S(2)}) collective-permute-start(bf16[256,1024]{1,0:T(8,128)(2,1)} %collective-permute-done.9), channel_id=1, source_target_pairs={{4,8},{6,10},{8,12},{10,14},{5,9},{7,11},{9,13},{11,15},{20,24},{2... | collective-permute-start | bytes 1572872 | tf_op jit(solution)/shard_map/ppermute | solution.py:593
  114.8 14.1 %collective-permute-start.13 = (bf16[256,1024]{1,0:T(8,128)(2,1)}, bf16[256,1024]{1,0:T(8,128)(2,1)S(1)}, u32[]{:S(2)}, u32[]{:S(2)}) collective-permute-start(bf16[256,1024]{1,0:T(8,128)(2,1)} %collective-permute-done.10), channel_id=1, source_target_pairs={{8,4},{10,6},{4,0},{6,2},{9,5},{11,7},{5,1},{7,3},{24,20},{26,22},... | collective-permute-start | bytes 1572872 | tf_op jit(solution)/shard_map/ppermute | solution.py:593
  116.1 6.4 %collective-permute-start.11 = (bf16[256,512]{1,0:T(8,128)(2,1)S(1)}, bf16[256,512]{1,0:T(8,128)(2,1)S(1)}, u32[]{:S(2)}, u32[]{:S(2)}) collective-permute-start(bf16[256,512]{1,0:T(8,128)(2,1)S(1)} %get-tuple-element.86), channel_id=1, source_target_pairs={{0,2},{2,0},{4,6},{6,4},{8,10},{10,8},{12,14},{14,12},{1,3},{3,1},... | collective-permute-start | bytes 786440 | tf_op jit(solution)/shard_map/ppermute | solution.py:586
  129.0 6.4 %collective-permute-start.14 = (f32[256,2048]{1,0:T(8,128)}, f32[256,2048]{1,0:T(8,128)}, u32[]{:S(2)}, u32[]{:S(2)}) collective-permute-start(f32[256,2048]{1,0:T(8,128)} %project_rows.1.mine_ref), channel_id=1, source_target_pairs={{0,1},{1,0},{2,3},{3,2},{4,5},{5,4},{6,7},{7,6},{8,9},{9,8},{10,11... | collective-permute-start | bytes 6291464 | tf_op jit(solution)/shard_map/ppermute | solution.py:688
  130.5 18.5 %collective-permute-start.17 = (bf16[256,1024]{1,0:T(8,128)(2,1)S(1)}, bf16[256,1024]{1,0:T(8,128)(2,1)}, u32[]{:S(2)}, u32[]{:S(2)}) collective-permute-start(bf16[256,1024]{1,0:T(8,128)(2,1)S(1)} %collective-permute-done.12), channel_id=1, source_target_pairs={{8,12},{10,14},{9,13},{11,15},{24,28},{26,30},{25,29},{27,31}} | collective-permute-start | bytes 1572872 | tf_op jit(solution)/shard_map/ppermute | solution.py:593
  132.0 18.8 %collective-permute-start.18 = (bf16[256,1024]{1,0:T(8,128)(2,1)S(1)}, bf16[256,1024]{1,0:T(8,128)(2,1)}, u32[]{:S(2)}, u32[]{:S(2)}) collective-permute-start(bf16[256,1024]{1,0:T(8,128)(2,1)S(1)} %collective-permute-done.13), channel_id=1, source_target_pairs={{4,0},{6,2},{5,1},{7,3},{20,16},{22,18},{21,17},{23,19}} | collective-permute-start | bytes 1572872 | tf_op jit(solution)/shard_map/ppermute | solution.py:593
  133.3 17.5 %collective-permute-start.19 = (bf16[256,1024]{1,0:T(8,128)(2,1)S(1)}, bf16[256,1024]{1,0:T(8,128)(2,1)S(1)}, u32[]{:S(2)}, u32[]{:S(2)}) collective-permute-start(bf16[256,1024]{1,0:T(8,128)(2,1)S(1)} %broadcast_select_fusion.3.refs_10_.refs_8_.refs_4_), channel_id=1, source_target_pairs={{0,16},{16,0},{1,17},{17,1},{2,18},{18,2},{3,19},{19,3},{4,20},{20... | collective-permute-start | bytes 1572872 | tf_op jit(solution)/shard_map/ppermute | solution.py:583
  135.4 13.5 %copy-start.20 = (s32[3]{0:T(128)S(1)}, s32[3]{0:T(128)}, u32[]{:S(2)}) copy-start(s32[3]{0:T(128)} %param.27) | copy-start | bytes 40
  139.9 17.1 %collective-permute-start.15 = (bf16[256,1024]{1,0:T(8,128)(2,1)}, bf16[256,1024]{1,0:T(8,128)(2,1)}, u32[]{:S(2)}, u32[]{:S(2)}) collective-permute-start(bf16[256,1024]{1,0:T(8,128)(2,1)} %get-tuple-element.120.refs_0_), channel_id=1, source_target_pairs={{0,4},{2,6},{4,8},{6,10},{8,12},{10,14},{1,5},{3,7},{5,9},{7,11},{... | collective-permute-start | bytes 1572872 | tf_op jit(solution)/shard_map/ppermute | solution.py:593
  146.0 15.9 %collective-permute-start.16 = (bf16[256,1024]{1,0:T(8,128)(2,1)}, bf16[256,1024]{1,0:T(8,128)(2,1)}, u32[]{:S(2)}, u32[]{:S(2)}) collective-permute-start(bf16[256,1024]{1,0:T(8,128)(2,1)} %get-tuple-element.120.refs_0_), channel_id=1, source_target_pairs={{12,8},{14,10},{8,4},{10,6},{4,0},{6,2},{13,9},{15,11},{9,5},{11,7... | collective-permute-start | bytes 1572872 | tf_op jit(solution)/shard_map/ppermute | solution.py:593
  149.0 21.9 %collective-permute-start.22 = (bf16[256,1024]{1,0:T(8,128)(2,1)}, bf16[256,1024]{1,0:T(8,128)(2,1)}, u32[]{:S(2)}, u32[]{:S(2)}) collective-permute-start(bf16[256,1024]{1,0:T(8,128)(2,1)} %get-tuple-element.120.refs_0_), channel_id=1, source_target_pairs={{0,2},{2,0},{4,6},{6,4},{8,10},{10,8},{12,14},{14,12},{1,3},{3,1},... | collective-permute-start | bytes 1572872 | tf_op jit(solution)/shard_map/ppermute | solution.py:586
  161.9 10.6 %collective-permute-start.20 = (bf16[256,1024]{1,0:T(8,128)(2,1)}, bf16[256,1024]{1,0:T(8,128)(2,1)}, u32[]{:S(2)}, u32[]{:S(2)}) collective-permute-start(bf16[256,1024]{1,0:T(8,128)(2,1)} %collective-permute-done.15), channel_id=1, source_target_pairs={{4,8},{6,10},{8,12},{10,14},{5,9},{7,11},{9,13},{11,15},{20,24},{2... | collective-permute-start | bytes 1572872 | tf_op jit(solution)/shard_map/ppermute | solution.py:593
  163.4 16.2 %collective-permute-start.21 = (bf16[256,1024]{1,0:T(8,128)(2,1)}, bf16[256,1024]{1,0:T(8,128)(2,1)}, u32[]{:S(2)}, u32[]{:S(2)}) collective-permute-start(bf16[256,1024]{1,0:T(8,128)(2,1)} %collective-permute-done.16), channel_id=1, source_target_pairs={{8,4},{10,6},{4,0},{6,2},{9,5},{11,7},{5,1},{7,3},{24,20},{26,22},... | collective-permute-start | bytes 1572872 | tf_op jit(solution)/shard_map/ppermute | solution.py:593
  165.8 15.0 %collective-permute-start.23 = (bf16[256,1024]{1,0:T(8,128)(2,1)S(1)}, bf16[256,1024]{1,0:T(8,128)(2,1)}, u32[]{:S(2)}, u32[]{:S(2)}) collective-permute-start(bf16[256,1024]{1,0:T(8,128)(2,1)S(1)} %broadcast_select_fusion.1.refs_12_.refs_10_.refs_6_), channel_id=1, source_target_pairs={{0,16},{16,0},{1,17},{17,1},{2,18},{18,2},{3,19},{19,3},{4,20},{20... | collective-permute-start | bytes 1572872 | tf_op jit(solution)/shard_map/ppermute | solution.py:583
  168.3 12.9 %collective-permute-start.24 = (bf16[256,1024]{1,0:T(8,128)(2,1)}, bf16[256,1024]{1,0:T(8,128)(2,1)}, u32[]{:S(2)}, u32[]{:S(2)}) collective-permute-start(bf16[256,1024]{1,0:T(8,128)(2,1)} %broadcast_select_fusion.2.refs_2_), channel_id=1, source_target_pairs={{0,2},{2,0},{4,6},{6,4},{8,10},{10,8},{12,14},{14,12},{1,3},{3,1},... | collective-permute-start | bytes 1572872 | tf_op jit(solution)/shard_map/ppermute | solution.py:586
  171.0 19.1 %collective-permute-start.27 = (bf16[256,1024]{1,0:T(8,128)(2,1)S(1)}, bf16[256,1024]{1,0:T(8,128)(2,1)}, u32[]{:S(2)}, u32[]{:S(2)}) collective-permute-start(bf16[256,1024]{1,0:T(8,128)(2,1)S(1)} %broadcast_select_fusion.refs_14_.refs_12_.refs_8_), channel_id=1, source_target_pairs={{0,16},{16,0},{1,17},{17,1},{2,18},{18,2},{3,19},{19,3},{4,20},{20... | collective-permute-start | bytes 1572872 | tf_op jit(solution)/shard_map/ppermute | solution.py:583
  181.2 10.1 %collective-permute-start.28 = (bf16[256,1024]{1,0:T(8,128)(2,1)}, bf16[256,1024]{1,0:T(8,128)(2,1)}, u32[]{:S(2)}, u32[]{:S(2)}) collective-permute-start(bf16[256,1024]{1,0:T(8,128)(2,1)} %collective-permute-done.22.refs_1_), channel_id=1, source_target_pairs={{0,1},{1,0},{2,3},{3,2},{4,5},{5,4},{6,7},{7,6},{8,9},{9,8},{10,11... | collective-permute-start | bytes 1572872 | tf_op jit(solution)/shard_map/ppermute | solution.py:698
  181.2 11.6 %collective-permute-start.29 = (bf16[256,1024]{1,0:T(8,128)(2,1)}, bf16[256,1024]{1,0:T(8,128)(2,1)}, u32[]{:S(2)}, u32[]{:S(2)}) collective-permute-start(bf16[256,1024]{1,0:T(8,128)(2,1)} %broadcast_select_fusion.2.refs_2_), channel_id=1, source_target_pairs={{0,1},{1,0},{2,3},{3,2},{4,5},{5,4},{6,7},{7,6},{8,9},{9,8},{10,11... | collective-permute-start | bytes 1572872 | tf_op jit(solution)/shard_map/ppermute | solution.py:698
  181.7 11.1 %collective-permute-start.30 = (bf16[256,1024]{1,0:T(8,128)(2,1)}, bf16[256,1024]{1,0:T(8,128)(2,1)}, u32[]{:S(2)}, u32[]{:S(2)}) collective-permute-start(bf16[256,1024]{1,0:T(8,128)(2,1)} %collective-permute-done.24.refs_3_), channel_id=1, source_target_pairs={{0,1},{1,0},{2,3},{3,2},{4,5},{5,4},{6,7},{7,6},{8,9},{9,8},{10,11... | collective-permute-start | bytes 1572872 | tf_op jit(solution)/shard_map/ppermute | solution.py:698
  181.7 23.0 %collective-permute-start.25 = (bf16[256,1024]{1,0:T(8,128)(2,1)}, bf16[256,1024]{1,0:T(8,128)(2,1)}, u32[]{:S(2)}, u32[]{:S(2)}) collective-permute-start(bf16[256,1024]{1,0:T(8,128)(2,1)} %collective-permute-done.20), channel_id=1, source_target_pairs={{8,12},{10,14},{9,13},{11,15},{24,28},{26,30},{25,29},{27,31}} | collective-permute-start | bytes 1572872 | tf_op jit(solution)/shard_map/ppermute | solution.py:593
  190.1 15.4 %collective-permute-start.26 = (bf16[256,1024]{1,0:T(8,128)(2,1)}, bf16[256,1024]{1,0:T(8,128)(2,1)}, u32[]{:S(2)}, u32[]{:S(2)}) collective-permute-start(bf16[256,1024]{1,0:T(8,128)(2,1)} %collective-permute-done.21), channel_id=1, source_target_pairs={{4,0},{6,2},{5,1},{7,3},{20,16},{22,18},{21,17},{23,19}} | collective-permute-start | bytes 1572872 | tf_op jit(solution)/shard_map/ppermute | solution.py:593
  191.4 14.1 %collective-permute-start.31 = (bf16[256,1024]{1,0:T(8,128)(2,1)}, bf16[256,1024]{1,0:T(8,128)(2,1)}, u32[]{:S(2)}, u32[]{:S(2)}) collective-permute-start(bf16[256,1024]{1,0:T(8,128)(2,1)} %fusion.1.refs_0_), channel_id=1, source_target_pairs={{0,2},{2,0},{4,6},{6,4},{8,10},{10,8},{12,14},{14,12},{1,3},{3,1},... | collective-permute-start | bytes 1572872 | tf_op jit(solution)/shard_map/ppermute | solution.py:586
  205.4 3.3 %collective-permute-start.33 = (bf16[256,1024]{1,0:T(8,128)(2,1)}, bf16[256,1024]{1,0:T(8,128)(2,1)S(1)}, u32[]{:S(2)}, u32[]{:S(2)}) collective-permute-start(bf16[256,1024]{1,0:T(8,128)(2,1)} %fusion.1.refs_0_), channel_id=1, source_target_pairs={{0,1},{1,0},{2,3},{3,2},{4,5},{5,4},{6,7},{7,6},{8,9},{9,8},{10,11... | collective-permute-start | bytes 1572872 | tf_op jit(solution)/shard_map/ppermute | solution.py:698
  205.4 3.3 %collective-permute-start.34 = (bf16[256,1024]{1,0:T(8,128)(2,1)}, bf16[256,1024]{1,0:T(8,128)(2,1)S(1)}, u32[]{:S(2)}, u32[]{:S(2)}) collective-permute-start(bf16[256,1024]{1,0:T(8,128)(2,1)} %collective-permute-done.31.refs_1_), channel_id=1, source_target_pairs={{0,1},{1,0},{2,3},{3,2},{4,5},{5,4},{6,7},{7,6},{8,9},{9,8},{10,11... | collective-permute-start | bytes 1572872 | tf_op jit(solution)/shard_map/ppermute | solution.py:698
  207.1 2.0 collective-permute-start.35
  207.2 14.4 %collective-permute-start.32 = (bf16[256,1024]{1,0:T(8,128)(2,1)S(1)}, bf16[256,1024]{1,0:T(8,128)(2,1)}, u32[]{:S(2)}, u32[]{:S(2)}) collective-permute-start(bf16[256,1024]{1,0:T(8,128)(2,1)S(1)} %select_select_fusion.1.refs_2_), channel_id=1, source_target_pairs={{0,2},{2,0},{4,6},{6,4},{8,10},{10,8},{12,14},{14,12},{1,3},{3,1},... | collective-permute-start | bytes 1572872 | tf_op jit(solution)/shard_map/ppermute | solution.py:586
  221.6 2.3 collective-permute-start.36
  236.8 14.2 %collective-permute-start.37 = (bf16[512,512]{1,0:T(8,128)(2,1)}, bf16[512,512]{1,0:T(8,128)(2,1)S(1)}, u32[]{:S(2)}, u32[]{:S(2)}) collective-permute-start(bf16[512,512]{1,0:T(8,128)(2,1)} %decode_rows.3), channel_id=1, source_target_pairs={{0,2},{2,0},{4,6},{6,4},{8,10},{10,8},{12,14},{14,12},{1,3},{3,1},... | collective-permute-start | bytes 1572872 | tf_op jit(solution)/shard_map/ppermute | solution.py:749
  (12 other events, 25.6 us)

commit v14 on v13

--- a/solution.py
+++ b/solution.py
@@ -481,16 +481,25 @@
     return chunks + ([open_chunk] if open_chunk else [])
 
 
-def decode_kernel(parts, q_ref, *refs):
-    k_refs, v_refs, out_ref = refs[:parts], refs[parts : 2 * parts], refs[-1]
+def decode_kernel(parts, first, last, q_ref, *refs):
+    k_refs, v_refs, rest = refs[:parts], refs[parts : 2 * parts], refs[2 * parts :]
+    rows = q_ref.shape[0]
+    heads = q_ref.shape[1] // HEAD_DIM
+    lane = lax.broadcasted_iota(jnp.int32, (rows, LANES), 1)
+    lse_all = jnp.zeros((rows, LANES), jnp.float32)
 
     def gathered(sources, chunk, cols):
         rows = [sources[i][start:stop, cols] for i, start, stop in chunk]
         return rows[0] if len(rows) == 1 else jnp.concatenate(rows)
 
-    for h in range(q_ref.shape[1] // HEAD_DIM):
+    for h in range(heads):
         cols = slice(h * HEAD_DIM, (h + 1) * HEAD_DIM)
         top = acc = None
+        if not first:
+            top = jnp.max(
+                jnp.where(lane % heads == h, rest[1][...], -jnp.inf), axis=1, keepdims=True
+            )
+            acc = jnp.concatenate([rest[0][:, cols], jnp.ones((rows, LANES), jnp.float32)], axis=1)
         for chunk in row_chunks([k.shape[0] for k in k_refs], 512):
             keys, values = gathered(k_refs, chunk, cols), gathered(v_refs, chunk, cols)
             scores = lax.dot_general(q_ref[:, cols], keys, NT, preferred_element_type=jnp.float32)
@@ -507,23 +516,39 @@
             if top is not None:
                 summed = summed + acc * jnp.exp2(top - new_top)
             top, acc = new_top, summed
-        out_ref[:, cols] = (acc[:, :HEAD_DIM] / acc[:, HEAD_DIM:]).astype(out_ref.dtype)
-
-
-def decode(queries, keys_values, out_type):
+        totals = acc[:, HEAD_DIM:]
+        out_ref = rest[-1] if last else rest[-2]
+        out_ref[:, cols] = (acc[:, :HEAD_DIM] / totals).astype(out_ref.dtype)
+        if not last:
+            lse_all = jnp.where(lane % heads == h, top + jnp.log2(totals), lse_all)
+    if not last:
+        rest[-1][...] = lse_all
+
+
+def decode(queries, keys_values, state, out_type):
+    first, last = state is None, out_type is not None
     tokens, width = queries.shape
     latents = sum(v.shape[0] for v in keys_values)
     pair = min(2 * HEAD_DIM, width)
     steps = width // pair
     narrow = pl.BlockSpec((tokens, pair), lambda i: (0, i))
+    sums = pl.BlockSpec((tokens, LANES), lambda i: (0, i))
     keys = [pl.BlockSpec((v.shape[0], pair), lambda i: (0, i)) for v in keys_values]
     values = [pl.BlockSpec((v.shape[0], pair), lambda i: (0, steps + i)) for v in keys_values]
+    if last:
+        out_specs, out_shape = narrow, jax.ShapeDtypeStruct((tokens, width), out_type)
+    else:
+        out_specs = [narrow, sums]
+        out_shape = [
+            jax.ShapeDtypeStruct((tokens, width), jnp.float32),
+            jax.ShapeDtypeStruct((tokens, steps * LANES), jnp.float32),
+        ]
     return pl.pallas_call(
-        functools.partial(decode_kernel, len(keys_values)),
+        functools.partial(decode_kernel, len(keys_values), first, last),
         grid=(steps,),
-        in_specs=[narrow, *keys, *values],
-        out_specs=narrow,
-        out_shape=jax.ShapeDtypeStruct((tokens, width), out_type),
+        in_specs=[narrow, *keys, *values, *([] if first else [narrow, sums])],
+        out_specs=out_specs,
+        out_shape=out_shape,
         compiler_params=params(BIG),
         cost_estimate=cost(
             16 * tokens * latents * width,
@@ -531,7 +556,7 @@
             tokens * latents * (width // HEAD_DIM),
         ),
         name="decode_rows",
-    )(queries, *keys_values, *keys_values)
+    )(queries, *keys_values, *keys_values, *([] if first else state))
 
 
 def swap_perm(size):
@@ -671,7 +696,7 @@
         (parts, out_near, out_far_other, out_near_other, near_queries)
     )
     attended, for_near = merge(y, parts, far)
-    for_near, hops = lax.optimization_barrier((for_near, hops))
+    _, hops = lax.optimization_barrier((for_near, hops))
     hops[2] = hop(2, hops[1])
     from_near = over_near(for_near)
     kept = kept_queries()
@@ -742,10 +767,13 @@
                 mine += [fresh, fresh_near]
                 other += cores([fresh, fresh_near])
     keys_values.append(fold([*mine, fresh], [*other, *cores([fresh])]))
-    fresh_near, keys_values = lax.optimization_barrier((fresh_near, keys_values))
+    near_state = decode(near_queries, keys_values, None, None)
+    fresh_near, keys_values, near_state = lax.optimization_barrier(
+        (fresh_near, keys_values, near_state)
+    )
     keys_values.append(fold([fresh_near], cores([fresh_near])))
-    near_state = decode(near_queries, keys_values, jnp.bfloat16)
-    own_state = decode(own_queries, keys_values, jnp.float32)
+    near_state = decode(near_queries, keys_values[-1:], near_state, jnp.bfloat16)
+    own_state = decode(own_queries, keys_values, None, jnp.float32)
     from_near = lax.ppermute(near_state, "pos", near).astype(jnp.float32)
     decoded = jnp.where(
         y == 0,

time: 255 us -> 251 us (0.984)
  waiting for transfers between devices: 98.3 us -> 94.5 us
    ppermute x9, waiting for transfers between devices: 38.6 us -> 33.6 us  [over_near(): return lax.ppermute(value, 'pos', near)]
    pallas_call x2 -> x3, Pallas kernels: 16.7 us -> 19.2 us  [decode(): pl.pallas_call(functools.partial(decode_kernel, len(keys_values), first,...]
  transfers between devices with their start and end apart: 39 -> 39, of which waited for: 18 -> 17; matrix products, arithmetic and copies ran while one was open for 10% -> 10% of each run, Pallas kernels for 20% -> 23%
where the time goes in v14:
time: 251 us; the launch traced here: 250 us
  waiting for transfers between devices  94.5 us (38%)
  Pallas kernels  64.3 us (26%)
  starting transfers between devices  56.7 us (23%)
  local copies, waits for them, and re-layouts  18.9 us (8%)
  other arithmetic  14.3 us (6%)
    ppermute x9, waiting for transfers between devices, over_near(): return lax.ppermute(value, 'pos', near)  33.6 us
    ppermute x12, waiting for transfers between devices, hop(): lax.ppermute(v, 'pos', hop_perm(pos, step, way))  23.9 us
    ppermute x12, starting transfers between devices, hop(): lax.ppermute(v, 'pos', hop_perm(pos, step, way))  23.6 us
    ppermute x3, waiting for transfers between devices, over_far(): return lax.ppermute(value, 'pos', shift_perm(pos, k))  20.4 us
    pallas_call x3, Pallas kernels, decode(): pl.pallas_call(functools.partial(decode_kernel, len(keys_values), first,...  19.2 us
    pallas_call x3, Pallas kernels, latent_keys_values(): pl.pallas_call(functools.partial(latents_kernel, pieces), grid_spec=grid_...  18.6 us
    ppermute x9, starting transfers between devices, over_near(): return lax.ppermute(value, 'pos', near)  14.5 us
    pallas_call x1, Pallas kernels, encode(): pl.pallas_call(encode_kernel, grid_spec=grid_spec, out_shape=jax.ShapeDty...  14.4 us
  transfers between devices with their start and end apart: 39, of which 17 were waited for; matrix products, arithmetic and copies ran while one was open for 10% of the time, Pallas kernels for 23%

profile of v14, /device:TPU:0, one launch (start us, length us, event | category | flops | bytes accessed | tf_op | source)
XLA Modules:
  0.0 250.2 jit_solution(6946352236973533043)
XLA Ops:
  2.9 3.0 %collective-permute-start = (bf16[528,1024]{1,0:T(8,128)(2,1)S(1)}, bf16[528,1024]{1,0:T(8,128)(2,1)}, u32[]{:S(2)}, u32[]{:S(2)}) collective-permute-start(bf16[528,1024]{1,0:T(8,128)(2,1)S(1)} %pad_maximum_fusion), channel_id=1, source_target_pairs={{0,2},{2,0},{4,6},{6,4},{8,10},{10,8},{12,14},{14,12},{1,3},{3,1},... | collective-permute-start | bytes 3244040 | tf_op jit(solution)/shard_map/ppermute | solution.py:611
  8.4 3.6 %collective-permute-start.1 = (bf16[528,256]{1,0:T(8,128)(2,1)}, bf16[528,256]{1,0:T(8,128)(2,1)}, u32[]{:S(2)}, u32[]{:S(2)}) collective-permute-start(bf16[528,256]{1,0:T(8,128)(2,1)} %pad_maximum_fusion.3), channel_id=1, source_target_pairs={{4,0},{6,2},{8,4},{10,6},{12,8},{14,10},{0,12},{2,14},{5,1},{7,3},... | collective-permute-start | bytes 811016 | tf_op jit(solution)/shard_map/ppermute | solution.py:614
  14.6 4.6 %collective-permute-done.1 = bf16[528,256]{1,0:T(8,128)(2,1)} collective-permute-done((bf16[528,256]{1,0:T(8,128)(2,1)}, bf16[528,256]{1,0:T(8,128)(2,1)}, u32[]{:S(2)}, u32[]{:S(2)}) %collective-permute-start.1) | collective-permute-done | bytes 270368 | tf_op jit(solution)/shard_map/ppermute | solution.py:614
  19.2 15.8 %collective-permute-done.2 = bf16[528,256]{1,0:T(8,128)(2,1)} collective-permute-done((bf16[528,256]{1,0:T(8,128)(2,1)}, bf16[528,256]{1,0:T(8,128)(2,1)}, u32[]{:S(2)}, u32[]{:S(2)}) %collective-permute-start.2) | collective-permute-done | bytes 270368 | tf_op jit(solution)/shard_map/ppermute | solution.py:614
  35.6 14.4 %encode_rows.1 = bf16[2112,512]{1,0:T(8,128)(2,1)} custom-call(s32[1]{0:T(128)} %bitcast.9.ids_ref, bf16[2048,1024]{1,0:T(8,128)(2,1)} %q_ref.1, bf16[512,1024]{1,0:T(8,128)(2,1)} %k_ref.1, bf16[512,1024]{1,0:T(8,128)(2,1)} %v_ref.1, bf16[16,1024]{1,0:T(8,128)(2,1)} %copy-done.17, bf16[528,1024]{1,0:T(8,128)(2,1)} %collective-permute-done.near_ref, ...), custom_call_target="tpu_custom_call" | custom-call | flops 8589934592 | bytes 2097152 | tf_op jit(solution)/shard_map/encode_rows/pallas_call | solution.py:262
  50.0 4.0 %all-to-all-start = ((bf16[4,528,512]{2,1,0:T(8,128)(2,1)}), bf16[4,528,512]{2,1,0:T(8,128)(2,1)S(1)}, u32[]{:S(2)}, u32[]{:S(2)}) async-start(bf16[4,528,512]{2,1,0:T(8,128)(2,1)} %bitcast.52), calls=%async_computation | async-start | bytes 4325376 | tf_op jit(solution)/shard_map/all_to_all | solution.py:672
  54.1 1.9 constant_dynamic-update-slice_fusion.7
  55.9 1.8 constant_dynamic-update-slice_fusion.6
  58.6 1.5 collective-permute-start.5
  60.6 1.6 collective-permute-start.6
  62.1 26.7 %collective-permute-done.5.refs_3_ = bf16[2624,256]{1,0:T(8,128)(2,1)S(1)} collective-permute-done((bf16[2624,256]{1,0:T(8,128)(2,1)}, bf16[2624,256]{1,0:T(8,128)(2,1)S(1)}, u32[]{:S(2)}, u32[]{:S(2)}) %collective-permute-start.5) | collective-permute-done | bytes 1343520 | tf_op jit(solution)/shard_map/ppermute | solution.py:611
  89.8 1.5 collective-permute-start.7
  92.4 1.5 collective-permute-start.8
  93.9 2.0 pad_maximum_fusion.2
  95.9 4.4 %collective-permute-start.10 = (bf16[256,1024]{1,0:T(8,128)(2,1)}, bf16[256,1024]{1,0:T(8,128)(2,1)}, u32[]{:S(2)}, u32[]{:S(2)}) collective-permute-start(bf16[256,1024]{1,0:T(8,128)(2,1)} %get-tuple-element.159), channel_id=1, source_target_pairs={{0,4},{2,6},{4,8},{6,10},{8,12},{10,14},{1,5},{3,7},{5,9},{7,11},{... | collective-permute-start | bytes 1572872 | tf_op jit(solution)/shard_map/ppermute | solution.py:618
  101.6 2.4 collective-permute-done.8.q_ref
  104.0 3.9 %collective-permute-done.7.refs_4_ = bf16[1584,256]{1,0:T(8,128)(2,1)} collective-permute-done((bf16[1584,256]{1,0:T(8,128)(2,1)}, bf16[1584,256]{1,0:T(8,128)(2,1)}, u32[]{:S(2)}, u32[]{:S(2)}) %collective-permute-start.7) | collective-permute-done | bytes 811040 | tf_op jit(solution)/shard_map/ppermute | solution.py:608
  107.8 1.9 merge_rows.1
  110.4 3.7 %collective-permute-done.11 = bf16[256,1024]{1,0:T(8,128)(2,1)} collective-permute-done((bf16[256,1024]{1,0:T(8,128)(2,1)}, bf16[256,1024]{1,0:T(8,128)(2,1)}, u32[]{:S(2)}, u32[]{:S(2)}) %collective-permute-start.11) | collective-permute-done | bytes 524320 | tf_op jit(solution)/shard_map/ppermute | solution.py:618
  116.1 1.6 collective-permute-start.9
  118.4 4.2 %collective-permute-done.9.near_ref = bf16[256,512]{1,0:T(8,128)(2,1)S(1)} collective-permute-done((bf16[256,512]{1,0:T(8,128)(2,1)S(1)}, bf16[256,512]{1,0:T(8,128)(2,1)S(1)}, u32[]{:S(2)}, u32[]{:S(2)}) %collective-permute-start.9) | collective-permute-done | bytes 262176 | tf_op jit(solution)/shard_map/ppermute | solution.py:611
  123.3 5.7 %project_rows.1.mine_ref = f32[256,2048]{1,0:T(8,128)} custom-call(s32[10]{0:T(128)} %stack.82.ids_ref, bf16[256,512]{1,0:T(8,128)(2,1)} %copy-done.2, bf16[256,512]{1,0:T(8,128)(2,1)} %copy-done.16, bf16[1024,256]{1,0:T(8,128)(2,1)} %refs_0_.1, bf16[1584,256]{1,0:T(8,128)(2,1)} %get-tuple-element.164.refs_1_, ...), custom_call_target="tpu_custom_call" | custom-call | flops 1073741824 | bytes 6291456 | tf_op jit(solution)/shard_map/project_rows/pallas_call | solution.py:363
  130.5 1.5 collective-permute-start.17
  133.3 2.0 collective-permute-start.19
  135.3 4.6 %norm_rows.1 = (f32[256,1024]{1,0:T(8,128)}, bf16[256,1024]{1,0:T(8,128)(2,1)}, bf16[256,1024]{1,0:T(8,128)(2,1)}) custom-call(s32[1]{0:T(128)} %bitcast.ids_ref, f32[256,2048]{1,0:T(8,128)} %project_rows.1.mine_ref, f32[256,2048]{1,0:T(8,128)} %collective-permute-done.14.theirs_ref, bf16[256,2048]{1,0:T(8,128)(2,1)} %latent_ref.1, f32[1,2048]{1,0:T(1,128)} %bitcast.54), custom_call_target="tpu_custom_call" | custom-call | flops 3145728 | bytes 6815744 | tf_op jit(solution)/shard_map/norm_rows/pallas_call | solution.py:397
  139.9 6.2 %collective-permute-start.15 = (bf16[256,1024]{1,0:T(8,128)(2,1)}, bf16[256,1024]{1,0:T(8,128)(2,1)}, u32[]{:S(2)}, u32[]{:S(2)}) collective-permute-start(bf16[256,1024]{1,0:T(8,128)(2,1)} %get-tuple-element.122.refs_0_), channel_id=1, source_target_pairs={{0,4},{2,6},{4,8},{6,10},{8,12},{10,14},{1,5},{3,7},{5,9},{7,11},{... | collective-permute-start | bytes 1572872 | tf_op jit(solution)/shard_map/ppermute | solution.py:618
  149.0 1.8 collective-permute-start.22
  150.8 6.2 %collective-permute-done.15 = bf16[256,1024]{1,0:T(8,128)(2,1)} collective-permute-done((bf16[256,1024]{1,0:T(8,128)(2,1)}, bf16[256,1024]{1,0:T(8,128)(2,1)}, u32[]{:S(2)}, u32[]{:S(2)}) %collective-permute-start.15) | collective-permute-done | bytes 524320 | tf_op jit(solution)/shard_map/ppermute | solution.py:618
  157.1 4.9 %collective-permute-done.16 = bf16[256,1024]{1,0:T(8,128)(2,1)} collective-permute-done((bf16[256,1024]{1,0:T(8,128)(2,1)}, bf16[256,1024]{1,0:T(8,128)(2,1)}, u32[]{:S(2)}, u32[]{:S(2)}) %collective-permute-start.16) | collective-permute-done | bytes 524320 | tf_op jit(solution)/shard_map/ppermute | solution.py:618
  162.0 1.5 collective-permute-start.20
  166.4 1.9 broadcast_select_fusion.2.refs_2_
  168.3 1.6 collective-permute-start.24
  171.0 1.6 collective-permute-start.27
  172.5 7.1 %collective-permute-done.21 = bf16[256,1024]{1,0:T(8,128)(2,1)} collective-permute-done((bf16[256,1024]{1,0:T(8,128)(2,1)}, bf16[256,1024]{1,0:T(8,128)(2,1)}, u32[]{:S(2)}, u32[]{:S(2)}) %collective-permute-start.21) | collective-permute-done | bytes 524320 | tf_op jit(solution)/shard_map/ppermute | solution.py:618
  183.2 2.1 fusion.1.refs_0_
  185.3 4.8 %collective-permute-done.27.refs_15_.refs_13_.refs_9_ = bf16[256,1024]{1,0:T(8,128)(2,1)} collective-permute-done((bf16[256,1024]{1,0:T(8,128)(2,1)S(1)}, bf16[256,1024]{1,0:T(8,128)(2,1)}, u32[]{:S(2)}, u32[]{:S(2)}) %collective-permute-start.27) | collective-permute-done | bytes 524320 | tf_op jit(solution)/shard_map/ppermute | solution.py:608
  190.1 1.5 collective-permute-start.26
  195.1 8.3 %latent_keys_values.3.refs_0_.refs_2_.refs_3_ = bf16[1024,1024]{1,0:T(8,128)(2,1)S(1)} custom-call(s32[9]{0:T(128)S(1)} %stack.92.ids_ref, bf16[256,1024]{1,0:T(8,128)(2,1)S(1)} %copy-done.3, bf16[256,1024]{1,0:T(8,128)(2,1)} %collective-permute-done.22.refs_1_, bf16[256,1024]{1,0:T(8,128)(2,1)} %broadcast_select_fusion.2.refs_2_, ...), custom_call_target="tpu_custom_call" | custom-call | flops 4294967296 | bytes 4194304 | tf_op jit(solution)/shard_map/latent_keys_values/pallas_call | solution.py:460
  203.5 2.0 collective-permute-done.26
  207.2 1.6 collective-permute-start.32
  209.1 6.4 %latent_keys_values.4.refs_1_.refs_3_.refs_4_ = bf16[768,1024]{1,0:T(8,128)(2,1)S(1)} custom-call(s32[9]{0:T(128)S(1)} %stack.92.ids_ref, bf16[256,1024]{1,0:T(8,128)(2,1)} %fusion.1.refs_0_, bf16[256,1024]{1,0:T(8,128)(2,1)} %collective-permute-done.31.refs_1_, bf16[256,1024]{1,0:T(8,128)(2,1)S(1)} %select_select_fusion.1.refs_2_, ...), custom_call_target="tpu_custom_call" | custom-call | flops 3221225472 | bytes 4194304 | tf_op jit(solution)/shard_map/latent_keys_values/pallas_call | solution.py:460
  216.6 7.4 %decode_rows.3 = (f32[512,512]{1,0:T(8,128)}, f32[512,256]{1,0:T(8,128)}) custom-call(bf16[512,512]{1,0:T(8,128)(2,1)} %collective-permute-done.8.q_ref, bf16[1024,1024]{1,0:T(8,128)(2,1)} %copy-done.6, bf16[768,1024]{1,0:T(8,128)(2,1)} %copy-done.5, bf16[1024,1024]{1,0:T(8,128)(2,1)} %copy-done.6, bf16[768,1024]{1,0:T(8,128)(2,1)} %copy-done.5), custom_call_target="tpu_custom_call" | custom-call | flops 7516192768 | bytes 5242880 | tf_op jit(solution)/shard_map/decode_rows/pallas_call | solution.py:546
  224.2 2.1 collective-permute-done.36.refs_1_
  226.3 3.8 %latent_keys_values.5.refs_2_.refs_5_.refs_0_.refs_1_ = bf16[256,1024]{1,0:T(8,128)(2,1)S(1)} custom-call(s32[9]{0:T(128)S(1)} %stack.92.ids_ref, bf16[256,1024]{1,0:T(8,128)(2,1)} %collective-permute-done.32.refs_0_, bf16[256,1024]{1,0:T(8,128)(2,1)} %collective-permute-done.36.refs_1_, bf16[256,1024]{1,0:T(8,128)(2,1)S(1)} %get-tuple-element.134.refs_8_.refs_6_.refs_2_, ...), custom_call_target="tpu_custom_call" | custom-call | flops 1073741824 | bytes 4194304 | tf_op jit(solution)/shard_map/latent_keys_values/pallas_call | solution.py:460
  231.0 3.4 %decode_rows.5 = bf16[512,512]{1,0:T(8,128)(2,1)} custom-call(bf16[512,512]{1,0:T(8,128)(2,1)} %collective-permute-done.8.q_ref, bf16[256,1024]{1,0:T(8,128)(2,1)} %copy-done.1, bf16[256,1024]{1,0:T(8,128)(2,1)} %copy-done.1, f32[512,512]{1,0:T(8,128)} %get-tuple-element.148.refs_2_, f32[512,256]{1,0:T(8,128)} %get-tuple-element.149.refs_3_), custom_call_target="tpu_custom_call" | custom-call | flops 1073741824 | bytes 2097152 | tf_op jit(solution)/shard_map/decode_rows/pallas_call | solution.py:546
  235.8 8.4 %decode_rows.4 = f32[512,512]{1,0:T(8,128)} custom-call(bf16[512,512]{1,0:T(8,128)(2,1)} %get-tuple-element.156.q_ref, bf16[1024,1024]{1,0:T(8,128)(2,1)} %copy-done.6, bf16[768,1024]{1,0:T(8,128)(2,1)} %copy-done.5, bf16[256,1024]{1,0:T(8,128)(2,1)} %copy-done.1, bf16[1024,1024]{1,0:T(8,128)(2,1)} %copy-done.6, bf16[768,1024]{1,0:T(8,128)(2,1)} %copy-done.5, ...), custom_call_target="tpu_custom_call" | custom-call | flops 8589934592 | bytes 5767168 | tf_op jit(solution)/shard_map/decode_rows/pallas_call | solution.py:546
  244.2 4.3 %collective-permute-done.37 = bf16[512,512]{1,0:T(8,128)(2,1)S(1)} collective-permute-done((bf16[512,512]{1,0:T(8,128)(2,1)}, bf16[512,512]{1,0:T(8,128)(2,1)S(1)}, u32[]{:S(2)}, u32[]{:S(2)}) %collective-permute-start.37) | collective-permute-done | bytes 524320 | tf_op jit(solution)/shard_map/ppermute | solution.py:777
  248.7 1.6 fusion
  (129 shorter events, 39.3 us)
Async XLA Ops:
  0.6 59.5 %copy-start = (bf16[3,1024]{1,0:T(4,128)(2,1)S(1)}, bf16[3,1024]{1,0:T(4,128)(2,1)}, u32[]{:S(2)}) copy-start(bf16[3,1024]{1,0:T(4,128)(2,1)} %param.25) | copy-start | bytes 18436
  2.7 10.2 %copy-start.19 = (f32[3,8]{1,0:T(4,128)S(1)}, f32[3,8]{1,0:T(4,128)}, u32[]{:S(2)}) copy-start(f32[3,8]{1,0:T(4,128)} %param.26) | copy-start | bytes 292
  2.7 10.9 %copy-start.12 = (bf16[256,1024]{1,0:T(8,128)(2,1)S(1)}, bf16[256,1024]{1,0:T(8,128)(2,1)}, u32[]{:S(2)}) copy-start(bf16[256,1024]{1,0:T(8,128)(2,1)} %param.22) | copy-start | bytes 1572868
  2.8 10.9 %copy-start.13 = (bf16[256,1024]{1,0:T(8,128)(2,1)S(1)}, bf16[256,1024]{1,0:T(8,128)(2,1)}, u32[]{:S(2)}) copy-start(bf16[256,1024]{1,0:T(8,128)(2,1)} %param.21) | copy-start | bytes 1572868
  2.9 32.1 %collective-permute-start = (bf16[528,1024]{1,0:T(8,128)(2,1)S(1)}, bf16[528,1024]{1,0:T(8,128)(2,1)}, u32[]{:S(2)}, u32[]{:S(2)}) collective-permute-start(bf16[528,1024]{1,0:T(8,128)(2,1)S(1)} %pad_maximum_fusion), channel_id=1, source_target_pairs={{0,2},{2,0},{4,6},{6,4},{8,10},{10,8},{12,14},{14,12},{1,3},{3,1},... | collective-permute-start | bytes 3244040 | tf_op jit(solution)/shard_map/ppermute | solution.py:611
  8.4 10.9 %collective-permute-start.1 = (bf16[528,256]{1,0:T(8,128)(2,1)}, bf16[528,256]{1,0:T(8,128)(2,1)}, u32[]{:S(2)}, u32[]{:S(2)}) collective-permute-start(bf16[528,256]{1,0:T(8,128)(2,1)} %pad_maximum_fusion.3), channel_id=1, source_target_pairs={{4,0},{6,2},{8,4},{10,6},{12,8},{14,10},{0,12},{2,14},{5,1},{7,3},... | collective-permute-start | bytes 811016 | tf_op jit(solution)/shard_map/ppermute | solution.py:614
  12.0 23.0 %collective-permute-start.2 = (bf16[528,256]{1,0:T(8,128)(2,1)}, bf16[528,256]{1,0:T(8,128)(2,1)}, u32[]{:S(2)}, u32[]{:S(2)}) collective-permute-start(bf16[528,256]{1,0:T(8,128)(2,1)} %pad_maximum_fusion.3), channel_id=1, source_target_pairs={{8,0},{10,2},{12,4},{14,6},{0,8},{2,10},{4,12},{6,14},{9,1},{11,3}... | collective-permute-start | bytes 811016 | tf_op jit(solution)/shard_map/ppermute | solution.py:614
  12.0 23.0 %collective-permute-start.3 = (bf16[528,256]{1,0:T(8,128)(2,1)}, bf16[528,256]{1,0:T(8,128)(2,1)S(1)}, u32[]{:S(2)}, u32[]{:S(2)}) collective-permute-start(bf16[528,256]{1,0:T(8,128)(2,1)} %pad_maximum_fusion.3), channel_id=1, source_target_pairs={{12,0},{14,2},{0,4},{2,6},{4,8},{6,10},{8,12},{10,14},{13,1},{15,3... | collective-permute-start | bytes 811016 | tf_op jit(solution)/shard_map/ppermute | solution.py:614
  35.0 15.0 %copy-start.14 = (bf16[528,256]{1,0:T(8,128)(2,1)}, bf16[528,256]{1,0:T(8,128)(2,1)S(1)}, u32[]{:S(2)}) copy-start(bf16[528,256]{1,0:T(8,128)(2,1)S(1)} %collective-permute-done.3) | copy-start | bytes 811012
  35.0 15.0 %collective-permute-start.4 = (bf16[256,1024]{1,0:T(8,128)(2,1)S(1)}, bf16[256,1024]{1,0:T(8,128)(2,1)S(1)}, u32[]{:S(2)}, u32[]{:S(2)}) collective-permute-start(bf16[256,1024]{1,0:T(8,128)(2,1)S(1)} %pad_maximum_fusion.1), channel_id=1, source_target_pairs={{0,2},{2,0},{4,6},{6,4},{8,10},{10,8},{12,14},{14,12},{1,3},{3,1},... | collective-permute-start | bytes 1572872 | tf_op jit(solution)/shard_map/ppermute | solution.py:611
  50.0 7.7 %copy-start.15 = (bf16[528,256]{1,0:T(8,128)(2,1)S(1)}, bf16[528,256]{1,0:T(8,128)(2,1)}, u32[]{:S(2)}) copy-start(bf16[528,256]{1,0:T(8,128)(2,1)} %copy-done.14) | copy-start | bytes 811012
  50.0 57.8 %all-to-all-start = ((bf16[4,528,512]{2,1,0:T(8,128)(2,1)}), bf16[4,528,512]{2,1,0:T(8,128)(2,1)S(1)}, u32[]{:S(2)}, u32[]{:S(2)}) async-start(bf16[4,528,512]{2,1,0:T(8,128)(2,1)} %bitcast.52), calls=%async_computation | async-start | bytes 4325376 | tf_op jit(solution)/shard_map/all_to_all | solution.py:672
  54.1 6.0 %copy-start.10 = (bf16[512,1024]{1,0:T(8,128)(2,1)S(1)}, bf16[512,1024]{1,0:T(8,128)(2,1)}, u32[]{:S(2)}) copy-start(bf16[512,1024]{1,0:T(8,128)(2,1)} %param.23) | copy-start | bytes 3145732
  58.6 30.3 %collective-permute-start.5 = (bf16[2624,256]{1,0:T(8,128)(2,1)}, bf16[2624,256]{1,0:T(8,128)(2,1)S(1)}, u32[]{:S(2)}, u32[]{:S(2)}) collective-permute-start(bf16[2624,256]{1,0:T(8,128)(2,1)} %get-tuple-element.165), channel_id=1, source_target_pairs={{0,2},{2,0},{4,6},{6,4},{8,10},{10,8},{12,14},{14,12},{1,3},{3,1},... | collective-permute-start | bytes 4030472 | tf_op jit(solution)/shard_map/ppermute | solution.py:611
  60.6 33.3 %copy-start.11 = (bf16[256,512]{1,0:T(8,128)(2,1)S(1)}, bf16[256,512]{1,0:T(8,128)(2,1)}, u32[]{:S(2)}) copy-start(bf16[256,512]{1,0:T(8,128)(2,1)} %get-tuple-element.162) | copy-start | bytes 786436
  60.6 43.4 %collective-permute-start.6 = (bf16[1584,256]{1,0:T(8,128)(2,1)}, bf16[1584,256]{1,0:T(8,128)(2,1)}, u32[]{:S(2)}, u32[]{:S(2)}) collective-permute-start(bf16[1584,256]{1,0:T(8,128)(2,1)} %get-tuple-element.164.refs_1_), channel_id=1, source_target_pairs={{0,16},{16,0},{1,17},{17,1},{2,18},{18,2},{3,19},{19,3},{4,20},{20... | collective-permute-start | bytes 2433032 | tf_op jit(solution)/shard_map/ppermute | solution.py:608
  89.8 18.0 %collective-permute-start.7 = (bf16[1584,256]{1,0:T(8,128)(2,1)}, bf16[1584,256]{1,0:T(8,128)(2,1)}, u32[]{:S(2)}, u32[]{:S(2)}) collective-permute-start(bf16[1584,256]{1,0:T(8,128)(2,1)} %slice.62), channel_id=1, source_target_pairs={{0,16},{16,0},{1,17},{17,1},{2,18},{18,2},{3,19},{19,3},{4,20},{20... | collective-permute-start | bytes 2433032 | tf_op jit(solution)/shard_map/ppermute | solution.py:608
  92.4 11.6 %collective-permute-start.8 = (bf16[512,512]{1,0:T(8,128)(2,1)}, bf16[512,512]{1,0:T(8,128)(2,1)}, u32[]{:S(2)}, u32[]{:S(2)}) collective-permute-start(bf16[512,512]{1,0:T(8,128)(2,1)} %get-tuple-element.157), channel_id=1, source_target_pairs={{0,2},{2,0},{4,6},{6,4},{8,10},{10,8},{12,14},{14,12},{1,3},{3,1},... | collective-permute-start | bytes 1572872 | tf_op jit(solution)/shard_map/ppermute | solution.py:611
  95.9 14.6 %collective-permute-start.10 = (bf16[256,1024]{1,0:T(8,128)(2,1)}, bf16[256,1024]{1,0:T(8,128)(2,1)}, u32[]{:S(2)}, u32[]{:S(2)}) collective-permute-start(bf16[256,1024]{1,0:T(8,128)(2,1)} %get-tuple-element.159), channel_id=1, source_target_pairs={{0,4},{2,6},{4,8},{6,10},{8,12},{10,14},{1,5},{3,7},{5,9},{7,11},{... | collective-permute-start | bytes 1572872 | tf_op jit(solution)/shard_map/ppermute | solution.py:618
  100.3 13.8 %collective-permute-start.11 = (bf16[256,1024]{1,0:T(8,128)(2,1)}, bf16[256,1024]{1,0:T(8,128)(2,1)}, u32[]{:S(2)}, u32[]{:S(2)}) collective-permute-start(bf16[256,1024]{1,0:T(8,128)(2,1)} %get-tuple-element.159), channel_id=1, source_target_pairs={{12,8},{14,10},{8,4},{10,6},{4,0},{6,2},{13,9},{15,11},{9,5},{11,7... | collective-permute-start | bytes 1572872 | tf_op jit(solution)/shard_map/ppermute | solution.py:618
  114.1 14.8 %collective-permute-start.12 = (bf16[256,1024]{1,0:T(8,128)(2,1)}, bf16[256,1024]{1,0:T(8,128)(2,1)S(1)}, u32[]{:S(2)}, u32[]{:S(2)}) collective-permute-start(bf16[256,1024]{1,0:T(8,128)(2,1)} %collective-permute-done.10), channel_id=1, source_target_pairs={{4,8},{6,10},{8,12},{10,14},{5,9},{7,11},{9,13},{11,15},{20,24},{2... | collective-permute-start | bytes 1572872 | tf_op jit(solution)/shard_map/ppermute | solution.py:618
  114.8 14.1 %collective-permute-start.13 = (bf16[256,1024]{1,0:T(8,128)(2,1)}, bf16[256,1024]{1,0:T(8,128)(2,1)S(1)}, u32[]{:S(2)}, u32[]{:S(2)}) collective-permute-start(bf16[256,1024]{1,0:T(8,128)(2,1)} %collective-permute-done.11), channel_id=1, source_target_pairs={{8,4},{10,6},{4,0},{6,2},{9,5},{11,7},{5,1},{7,3},{24,20},{26,22},... | collective-permute-start | bytes 1572872 | tf_op jit(solution)/shard_map/ppermute | solution.py:618
  116.1 6.4 %collective-permute-start.9 = (bf16[256,512]{1,0:T(8,128)(2,1)S(1)}, bf16[256,512]{1,0:T(8,128)(2,1)S(1)}, u32[]{:S(2)}, u32[]{:S(2)}) collective-permute-start(bf16[256,512]{1,0:T(8,128)(2,1)S(1)} %get-tuple-element.87), channel_id=1, source_target_pairs={{0,2},{2,0},{4,6},{6,4},{8,10},{10,8},{12,14},{14,12},{1,3},{3,1},... | collective-permute-start | bytes 786440 | tf_op jit(solution)/shard_map/ppermute | solution.py:611
  129.0 6.4 %collective-permute-start.14 = (f32[256,2048]{1,0:T(8,128)}, f32[256,2048]{1,0:T(8,128)}, u32[]{:S(2)}, u32[]{:S(2)}) collective-permute-start(f32[256,2048]{1,0:T(8,128)} %project_rows.1.mine_ref), channel_id=1, source_target_pairs={{0,1},{1,0},{2,3},{3,2},{4,5},{5,4},{6,7},{7,6},{8,9},{9,8},{10,11... | collective-permute-start | bytes 6291464 | tf_op jit(solution)/shard_map/ppermute | solution.py:713
  130.5 18.5 %collective-permute-start.17 = (bf16[256,1024]{1,0:T(8,128)(2,1)S(1)}, bf16[256,1024]{1,0:T(8,128)(2,1)}, u32[]{:S(2)}, u32[]{:S(2)}) collective-permute-start(bf16[256,1024]{1,0:T(8,128)(2,1)S(1)} %collective-permute-done.12), channel_id=1, source_target_pairs={{8,12},{10,14},{9,13},{11,15},{24,28},{26,30},{25,29},{27,31}} | collective-permute-start | bytes 1572872 | tf_op jit(solution)/shard_map/ppermute | solution.py:618
  132.0 18.8 %collective-permute-start.18 = (bf16[256,1024]{1,0:T(8,128)(2,1)S(1)}, bf16[256,1024]{1,0:T(8,128)(2,1)}, u32[]{:S(2)}, u32[]{:S(2)}) collective-permute-start(bf16[256,1024]{1,0:T(8,128)(2,1)S(1)} %collective-permute-done.13), channel_id=1, source_target_pairs={{4,0},{6,2},{5,1},{7,3},{20,16},{22,18},{21,17},{23,19}} | collective-permute-start | bytes 1572872 | tf_op jit(solution)/shard_map/ppermute | solution.py:618
  133.3 17.5 %collective-permute-start.19 = (bf16[256,1024]{1,0:T(8,128)(2,1)S(1)}, bf16[256,1024]{1,0:T(8,128)(2,1)S(1)}, u32[]{:S(2)}, u32[]{:S(2)}) collective-permute-start(bf16[256,1024]{1,0:T(8,128)(2,1)S(1)} %broadcast_select_fusion.3.refs_10_.refs_8_.refs_4_), channel_id=1, source_target_pairs={{0,16},{16,0},{1,17},{17,1},{2,18},{18,2},{3,19},{19,3},{4,20},{20... | collective-permute-start | bytes 1572872 | tf_op jit(solution)/shard_map/ppermute | solution.py:608
  135.3 13.6 %copy-start.20 = (s32[3]{0:T(128)S(1)}, s32[3]{0:T(128)}, u32[]{:S(2)}) copy-start(s32[3]{0:T(128)} %param.27) | copy-start | bytes 40
  139.9 17.2 %collective-permute-start.15 = (bf16[256,1024]{1,0:T(8,128)(2,1)}, bf16[256,1024]{1,0:T(8,128)(2,1)}, u32[]{:S(2)}, u32[]{:S(2)}) collective-permute-start(bf16[256,1024]{1,0:T(8,128)(2,1)} %get-tuple-element.122.refs_0_), channel_id=1, source_target_pairs={{0,4},{2,6},{4,8},{6,10},{8,12},{10,14},{1,5},{3,7},{5,9},{7,11},{... | collective-permute-start | bytes 1572872 | tf_op jit(solution)/shard_map/ppermute | solution.py:618
  146.1 15.9 %collective-permute-start.16 = (bf16[256,1024]{1,0:T(8,128)(2,1)}, bf16[256,1024]{1,0:T(8,128)(2,1)}, u32[]{:S(2)}, u32[]{:S(2)}) collective-permute-start(bf16[256,1024]{1,0:T(8,128)(2,1)} %get-tuple-element.122.refs_0_), channel_id=1, source_target_pairs={{12,8},{14,10},{8,4},{10,6},{4,0},{6,2},{13,9},{15,11},{9,5},{11,7... | collective-permute-start | bytes 1572872 | tf_op jit(solution)/shard_map/ppermute | solution.py:618
  149.0 22.0 %collective-permute-start.22 = (bf16[256,1024]{1,0:T(8,128)(2,1)}, bf16[256,1024]{1,0:T(8,128)(2,1)}, u32[]{:S(2)}, u32[]{:S(2)}) collective-permute-start(bf16[256,1024]{1,0:T(8,128)(2,1)} %get-tuple-element.122.refs_0_), channel_id=1, source_target_pairs={{0,2},{2,0},{4,6},{6,4},{8,10},{10,8},{12,14},{14,12},{1,3},{3,1},... | collective-permute-start | bytes 1572872 | tf_op jit(solution)/shard_map/ppermute | solution.py:611
  162.0 10.6 %collective-permute-start.20 = (bf16[256,1024]{1,0:T(8,128)(2,1)}, bf16[256,1024]{1,0:T(8,128)(2,1)}, u32[]{:S(2)}, u32[]{:S(2)}) collective-permute-start(bf16[256,1024]{1,0:T(8,128)(2,1)} %collective-permute-done.15), channel_id=1, source_target_pairs={{4,8},{6,10},{8,12},{10,14},{5,9},{7,11},{9,13},{11,15},{20,24},{2... | collective-permute-start | bytes 1572872 | tf_op jit(solution)/shard_map/ppermute | solution.py:618
  163.5 16.2 %collective-permute-start.21 = (bf16[256,1024]{1,0:T(8,128)(2,1)}, bf16[256,1024]{1,0:T(8,128)(2,1)}, u32[]{:S(2)}, u32[]{:S(2)}) collective-permute-start(bf16[256,1024]{1,0:T(8,128)(2,1)} %collective-permute-done.16), channel_id=1, source_target_pairs={{8,4},{10,6},{4,0},{6,2},{9,5},{11,7},{5,1},{7,3},{24,20},{26,22},... | collective-permute-start | bytes 1572872 | tf_op jit(solution)/shard_map/ppermute | solution.py:618
  165.9 15.0 %collective-permute-start.23 = (bf16[256,1024]{1,0:T(8,128)(2,1)S(1)}, bf16[256,1024]{1,0:T(8,128)(2,1)}, u32[]{:S(2)}, u32[]{:S(2)}) collective-permute-start(bf16[256,1024]{1,0:T(8,128)(2,1)S(1)} %broadcast_select_fusion.1.refs_12_.refs_10_.refs_6_), channel_id=1, source_target_pairs={{0,16},{16,0},{1,17},{17,1},{2,18},{18,2},{3,19},{19,3},{4,20},{20... | collective-permute-start | bytes 1572872 | tf_op jit(solution)/shard_map/ppermute | solution.py:608
  168.3 12.9 %collective-permute-start.24 = (bf16[256,1024]{1,0:T(8,128)(2,1)}, bf16[256,1024]{1,0:T(8,128)(2,1)}, u32[]{:S(2)}, u32[]{:S(2)}) collective-permute-start(bf16[256,1024]{1,0:T(8,128)(2,1)} %broadcast_select_fusion.2.refs_2_), channel_id=1, source_target_pairs={{0,2},{2,0},{4,6},{6,4},{8,10},{10,8},{12,14},{14,12},{1,3},{3,1},... | collective-permute-start | bytes 1572872 | tf_op jit(solution)/shard_map/ppermute | solution.py:611
  171.0 19.1 %collective-permute-start.27 = (bf16[256,1024]{1,0:T(8,128)(2,1)S(1)}, bf16[256,1024]{1,0:T(8,128)(2,1)}, u32[]{:S(2)}, u32[]{:S(2)}) collective-permute-start(bf16[256,1024]{1,0:T(8,128)(2,1)S(1)} %broadcast_select_fusion.refs_14_.refs_12_.refs_8_), channel_id=1, source_target_pairs={{0,16},{16,0},{1,17},{17,1},{2,18},{18,2},{3,19},{19,3},{4,20},{20... | collective-permute-start | bytes 1572872 | tf_op jit(solution)/shard_map/ppermute | solution.py:608
  181.2 10.3 %collective-permute-start.28 = (bf16[256,1024]{1,0:T(8,128)(2,1)}, bf16[256,1024]{1,0:T(8,128)(2,1)}, u32[]{:S(2)}, u32[]{:S(2)}) collective-permute-start(bf16[256,1024]{1,0:T(8,128)(2,1)} %collective-permute-done.22.refs_1_), channel_id=1, source_target_pairs={{0,1},{1,0},{2,3},{3,2},{4,5},{5,4},{6,7},{7,6},{8,9},{9,8},{10,11... | collective-permute-start | bytes 1572872 | tf_op jit(solution)/shard_map/ppermute | solution.py:723
  181.2 11.8 %collective-permute-start.29 = (bf16[256,1024]{1,0:T(8,128)(2,1)}, bf16[256,1024]{1,0:T(8,128)(2,1)}, u32[]{:S(2)}, u32[]{:S(2)}) collective-permute-start(bf16[256,1024]{1,0:T(8,128)(2,1)} %broadcast_select_fusion.2.refs_2_), channel_id=1, source_target_pairs={{0,1},{1,0},{2,3},{3,2},{4,5},{5,4},{6,7},{7,6},{8,9},{9,8},{10,11... | collective-permute-start | bytes 1572872 | tf_op jit(solution)/shard_map/ppermute | solution.py:723
  181.7 11.3 %collective-permute-start.30 = (bf16[256,1024]{1,0:T(8,128)(2,1)}, bf16[256,1024]{1,0:T(8,128)(2,1)}, u32[]{:S(2)}, u32[]{:S(2)}) collective-permute-start(bf16[256,1024]{1,0:T(8,128)(2,1)} %collective-permute-done.24.refs_3_), channel_id=1, source_target_pairs={{0,1},{1,0},{2,3},{3,2},{4,5},{5,4},{6,7},{7,6},{8,9},{9,8},{10,11... | collective-permute-start | bytes 1572872 | tf_op jit(solution)/shard_map/ppermute | solution.py:723
  181.8 21.7 %collective-permute-start.25 = (bf16[256,1024]{1,0:T(8,128)(2,1)}, bf16[256,1024]{1,0:T(8,128)(2,1)}, u32[]{:S(2)}, u32[]{:S(2)}) collective-permute-start(bf16[256,1024]{1,0:T(8,128)(2,1)} %collective-permute-done.20), channel_id=1, source_target_pairs={{8,12},{10,14},{9,13},{11,15},{24,28},{26,30},{25,29},{27,31}} | collective-permute-start | bytes 1572872 | tf_op jit(solution)/shard_map/ppermute | solution.py:618
  190.1 15.3 %collective-permute-start.26 = (bf16[256,1024]{1,0:T(8,128)(2,1)}, bf16[256,1024]{1,0:T(8,128)(2,1)}, u32[]{:S(2)}, u32[]{:S(2)}) collective-permute-start(bf16[256,1024]{1,0:T(8,128)(2,1)} %collective-permute-done.21), channel_id=1, source_target_pairs={{4,0},{6,2},{5,1},{7,3},{20,16},{22,18},{21,17},{23,19}} | collective-permute-start | bytes 1572872 | tf_op jit(solution)/shard_map/ppermute | solution.py:618
  191.6 13.9 %collective-permute-start.31 = (bf16[256,1024]{1,0:T(8,128)(2,1)}, bf16[256,1024]{1,0:T(8,128)(2,1)}, u32[]{:S(2)}, u32[]{:S(2)}) collective-permute-start(bf16[256,1024]{1,0:T(8,128)(2,1)} %fusion.1.refs_0_), channel_id=1, source_target_pairs={{0,2},{2,0},{4,6},{6,4},{8,10},{10,8},{12,14},{14,12},{1,3},{3,1},... | collective-permute-start | bytes 1572872 | tf_op jit(solution)/shard_map/ppermute | solution.py:611
  205.4 3.3 %collective-permute-start.33 = (bf16[256,1024]{1,0:T(8,128)(2,1)}, bf16[256,1024]{1,0:T(8,128)(2,1)S(1)}, u32[]{:S(2)}, u32[]{:S(2)}) collective-permute-start(bf16[256,1024]{1,0:T(8,128)(2,1)} %fusion.1.refs_0_), channel_id=1, source_target_pairs={{0,1},{1,0},{2,3},{3,2},{4,5},{5,4},{6,7},{7,6},{8,9},{9,8},{10,11... | collective-permute-start | bytes 1572872 | tf_op jit(solution)/shard_map/ppermute | solution.py:723
  205.4 3.3 %collective-permute-start.34 = (bf16[256,1024]{1,0:T(8,128)(2,1)}, bf16[256,1024]{1,0:T(8,128)(2,1)S(1)}, u32[]{:S(2)}, u32[]{:S(2)}) collective-permute-start(bf16[256,1024]{1,0:T(8,128)(2,1)} %collective-permute-done.31.refs_1_), channel_id=1, source_target_pairs={{0,1},{1,0},{2,3},{3,2},{4,5},{5,4},{6,7},{7,6},{8,9},{9,8},{10,11... | collective-permute-start | bytes 1572872 | tf_op jit(solution)/shard_map/ppermute | solution.py:723
  207.1 2.0 collective-permute-start.35
  207.2 16.8 %collective-permute-start.32 = (bf16[256,1024]{1,0:T(8,128)(2,1)S(1)}, bf16[256,1024]{1,0:T(8,128)(2,1)}, u32[]{:S(2)}, u32[]{:S(2)}) collective-permute-start(bf16[256,1024]{1,0:T(8,128)(2,1)S(1)} %select_select_fusion.1.refs_2_), channel_id=1, source_target_pairs={{0,2},{2,0},{4,6},{6,4},{8,10},{10,8},{12,14},{14,12},{1,3},{3,1},... | collective-permute-start | bytes 1572872 | tf_op jit(solution)/shard_map/ppermute | solution.py:611
  224.0 2.3 collective-permute-start.36
  234.4 14.2 %collective-permute-start.37 = (bf16[512,512]{1,0:T(8,128)(2,1)}, bf16[512,512]{1,0:T(8,128)(2,1)S(1)}, u32[]{:S(2)}, u32[]{:S(2)}) collective-permute-start(bf16[512,512]{1,0:T(8,128)(2,1)} %decode_rows.5), channel_id=1, source_target_pairs={{0,2},{2,0},{4,6},{6,4},{8,10},{10,8},{12,14},{14,12},{1,3},{3,1},... | collective-permute-start | bytes 1572872 | tf_op jit(solution)/shard_map/ppermute | solution.py:777
  (12 other events, 29.7 us)

commit v15 on v14

--- a/solution.py
+++ b/solution.py
@@ -742,16 +742,17 @@
     came = {0: [normed, normed]}
     came[1] = hop(1, came[0])
     normed_near = over_near(normed)
-    came, hops, kv_bands, kept = lax.optimization_barrier((came, hops, kv_bands, kept))
+    hops, _ = lax.optimization_barrier((hops, normed))
+    for k in rest:
+        kv_moved = by_shift(hops, k)
+        kv_bands += [kv_moved, over_groups(kv_moved)]
+    came, kept = lax.optimization_barrier((came, kept))
     mine, other, keys_values = [normed, normed_near], [normed_other], []
     for step in range(1, far):
         fresh = arrival(came, step)
         fresh_near = over_near(fresh)
         if step + 1 < far:
             came[step + 1] = hop(step + 1, came[step])
-            k = rest[step - 1]
-            kv_moved = by_shift(hops, k)
-            kv_bands += [kv_moved, over_groups(kv_moved)]
             if step > 1:
                 keys_values.append(fold(mine, other))
                 mine, other = [], []

time: 251 us -> 250 us (level)
  local copies, waits for them, and re-layouts: 18.9 us -> 26.3 us
  waiting for transfers between devices: 94.5 us -> 89 us
    ppermute x12, waiting for transfers between devices: 23.9 us -> 16.4 us  [hop(): lax.ppermute(v, 'pos', hop_perm(pos, step, way))]
    unnamed x47 -> x69, local copies, waits for them, and re-layouts: 10.6 us -> 17.9 us
  transfers between devices with their start and end apart: 39 -> 39, of which waited for: 17 -> 15; matrix products, arithmetic and copies ran while one was open for 10% -> 9% of each run, Pallas kernels for 23% -> 23%
where the time goes in v15:
time: 250 us; the launch traced here: 249 us
  waiting for transfers between devices  89 us (36%)
  Pallas kernels  63.5 us (25%)
  starting transfers between devices  55 us (22%)
  local copies, waits for them, and re-layouts  26.3 us (11%)
  other arithmetic  13.3 us (5%)
    ppermute x9, waiting for transfers between devices, over_near(): return lax.ppermute(value, 'pos', near)  34 us
    ppermute x12, starting transfers between devices, hop(): lax.ppermute(v, 'pos', hop_perm(pos, step, way))  22 us
    ppermute x3, waiting for transfers between devices, over_far(): return lax.ppermute(value, 'pos', shift_perm(pos, k))  20.4 us
    pallas_call x3, Pallas kernels, decode(): pl.pallas_call(functools.partial(decode_kernel, len(keys_values), first,...  19.2 us
    unnamed x69, local copies, waits for them, and re-layouts  17.9 us
    pallas_call x3, Pallas kernels, latent_keys_values(): pl.pallas_call(functools.partial(latents_kernel, pieces), grid_spec=grid_...  17.6 us
    ppermute x12, waiting for transfers between devices, hop(): lax.ppermute(v, 'pos', hop_perm(pos, step, way))  16.4 us
    ppermute x9, starting transfers between devices, over_near(): return lax.ppermute(value, 'pos', near)  14.8 us
  transfers between devices with their start and end apart: 39, of which 15 were waited for; matrix products, arithmetic and copies ran while one was open for 9% of the time, Pallas kernels for 23%

profile of v15, /device:TPU:0, one launch (start us, length us, event | category | flops | bytes accessed | tf_op | source)
XLA Modules:
  0.0 248.5 jit_solution(8323878958137072056)
XLA Ops:
  1.4 1.3 constant_dynamic-slice_fusion.8
  2.9 3.0 %collective-permute-start = (bf16[528,1024]{1,0:T(8,128)(2,1)S(1)}, bf16[528,1024]{1,0:T(8,128)(2,1)}, u32[]{:S(2)}, u32[]{:S(2)}) collective-permute-start(bf16[528,1024]{1,0:T(8,128)(2,1)S(1)} %pad_maximum_fusion), channel_id=1, source_target_pairs={{0,2},{2,0},{4,6},{6,4},{8,10},{10,8},{12,14},{14,12},{1,3},{3,1},... | collective-permute-start | bytes 3244040 | tf_op jit(solution)/shard_map/ppermute | solution.py:611
  8.4 3.6 %collective-permute-start.1 = (bf16[528,256]{1,0:T(8,128)(2,1)}, bf16[528,256]{1,0:T(8,128)(2,1)}, u32[]{:S(2)}, u32[]{:S(2)}) collective-permute-start(bf16[528,256]{1,0:T(8,128)(2,1)} %pad_maximum_fusion.3), channel_id=1, source_target_pairs={{4,0},{6,2},{8,4},{10,6},{12,8},{14,10},{0,12},{2,14},{5,1},{7,3},... | collective-permute-start | bytes 811016 | tf_op jit(solution)/shard_map/ppermute | solution.py:614
  14.6 4.7 %collective-permute-done.1 = bf16[528,256]{1,0:T(8,128)(2,1)} collective-permute-done((bf16[528,256]{1,0:T(8,128)(2,1)}, bf16[528,256]{1,0:T(8,128)(2,1)}, u32[]{:S(2)}, u32[]{:S(2)}) %collective-permute-start.1) | collective-permute-done | bytes 270368 | tf_op jit(solution)/shard_map/ppermute | solution.py:614
  19.2 15.8 %collective-permute-done.2 = bf16[528,256]{1,0:T(8,128)(2,1)} collective-permute-done((bf16[528,256]{1,0:T(8,128)(2,1)}, bf16[528,256]{1,0:T(8,128)(2,1)}, u32[]{:S(2)}, u32[]{:S(2)}) %collective-permute-start.2) | collective-permute-done | bytes 270368 | tf_op jit(solution)/shard_map/ppermute | solution.py:614
  35.6 14.4 %encode_rows.1 = bf16[2112,512]{1,0:T(8,128)(2,1)} custom-call(s32[1]{0:T(128)} %bitcast.9.ids_ref, bf16[2048,1024]{1,0:T(8,128)(2,1)} %q_ref.1, bf16[512,1024]{1,0:T(8,128)(2,1)} %k_ref.1, bf16[512,1024]{1,0:T(8,128)(2,1)} %v_ref.1, bf16[16,1024]{1,0:T(8,128)(2,1)} %copy-done.28, bf16[528,1024]{1,0:T(8,128)(2,1)} %collective-permute-done.near_ref, ...), custom_call_target="tpu_custom_call" | custom-call | flops 8589934592 | bytes 2097152 | tf_op jit(solution)/shard_map/encode_rows/pallas_call | solution.py:262
  50.0 4.0 %all-to-all-start = ((bf16[4,528,512]{2,1,0:T(8,128)(2,1)}), bf16[4,528,512]{2,1,0:T(8,128)(2,1)S(1)}, u32[]{:S(2)}, u32[]{:S(2)}) async-start(bf16[4,528,512]{2,1,0:T(8,128)(2,1)} %bitcast.52), calls=%async_computation | async-start | bytes 4325376 | tf_op jit(solution)/shard_map/all_to_all | solution.py:672
  54.1 1.9 constant_dynamic-update-slice_fusion.7
  55.9 1.8 constant_dynamic-update-slice_fusion.6
  58.6 1.5 collective-permute-start.5
  60.6 1.6 collective-permute-start.6
  62.1 26.7 %collective-permute-done.5.refs_3_ = bf16[2624,256]{1,0:T(8,128)(2,1)S(1)} collective-permute-done((bf16[2624,256]{1,0:T(8,128)(2,1)}, bf16[2624,256]{1,0:T(8,128)(2,1)S(1)}, u32[]{:S(2)}, u32[]{:S(2)}) %collective-permute-start.5) | collective-permute-done | bytes 1343520 | tf_op jit(solution)/shard_map/ppermute | solution.py:611
  89.8 1.5 collective-permute-start.7
  92.4 1.5 collective-permute-start.8
  93.9 2.0 pad_maximum_fusion.2
  95.9 4.4 %collective-permute-start.10 = (bf16[256,1024]{1,0:T(8,128)(2,1)}, bf16[256,1024]{1,0:T(8,128)(2,1)}, u32[]{:S(2)}, u32[]{:S(2)}) collective-permute-start(bf16[256,1024]{1,0:T(8,128)(2,1)} %get-tuple-element.155), channel_id=1, source_target_pairs={{0,4},{2,6},{4,8},{6,10},{8,12},{10,14},{1,5},{3,7},{5,9},{7,11},{... | collective-permute-start | bytes 1572872 | tf_op jit(solution)/shard_map/ppermute | solution.py:618
  101.6 2.4 collective-permute-done.8.q_ref
  104.0 3.8 %collective-permute-done.7.refs_4_ = bf16[1584,256]{1,0:T(8,128)(2,1)} collective-permute-done((bf16[1584,256]{1,0:T(8,128)(2,1)}, bf16[1584,256]{1,0:T(8,128)(2,1)}, u32[]{:S(2)}, u32[]{:S(2)}) %collective-permute-start.7) | collective-permute-done | bytes 811040 | tf_op jit(solution)/shard_map/ppermute | solution.py:608
  107.9 1.9 merge_rows.1
  110.5 3.7 %collective-permute-done.11 = bf16[256,1024]{1,0:T(8,128)(2,1)} collective-permute-done((bf16[256,1024]{1,0:T(8,128)(2,1)}, bf16[256,1024]{1,0:T(8,128)(2,1)}, u32[]{:S(2)}, u32[]{:S(2)}) %collective-permute-start.11) | collective-permute-done | bytes 524320 | tf_op jit(solution)/shard_map/ppermute | solution.py:618
  116.1 1.6 collective-permute-start.9
  118.4 4.2 %collective-permute-done.9.near_ref = bf16[256,512]{1,0:T(8,128)(2,1)S(1)} collective-permute-done((bf16[256,512]{1,0:T(8,128)(2,1)S(1)}, bf16[256,512]{1,0:T(8,128)(2,1)S(1)}, u32[]{:S(2)}, u32[]{:S(2)}) %collective-permute-start.9) | collective-permute-done | bytes 262176 | tf_op jit(solution)/shard_map/ppermute | solution.py:611
  123.3 5.8 %project_rows.1.mine_ref = f32[256,2048]{1,0:T(8,128)} custom-call(s32[10]{0:T(128)} %stack.82.ids_ref, bf16[256,512]{1,0:T(8,128)(2,1)} %copy-done.8, bf16[256,512]{1,0:T(8,128)(2,1)} %copy-done.27, bf16[1024,256]{1,0:T(8,128)(2,1)} %refs_0_.1, bf16[1584,256]{1,0:T(8,128)(2,1)} %get-tuple-element.160.refs_1_, ...), custom_call_target="tpu_custom_call" | custom-call | flops 1073741824 | bytes 6291456 | tf_op jit(solution)/shard_map/project_rows/pallas_call | solution.py:363
  131.4 1.5 collective-permute-start.21
  135.2 2.0 collective-permute-start.20
  137.2 4.5 %norm_rows.1 = (f32[256,1024]{1,0:T(8,128)}, bf16[256,1024]{1,0:T(8,128)(2,1)}, bf16[256,1024]{1,0:T(8,128)(2,1)}) custom-call(s32[1]{0:T(128)} %bitcast.ids_ref, f32[256,2048]{1,0:T(8,128)} %project_rows.1.mine_ref, f32[256,2048]{1,0:T(8,128)} %collective-permute-done.14.theirs_ref, bf16[256,2048]{1,0:T(8,128)(2,1)} %latent_ref.1, f32[1,2048]{1,0:T(1,128)} %bitcast.54), custom_call_target="tpu_custom_call" | custom-call | flops 3145728 | bytes 6815744 | tf_op jit(solution)/shard_map/norm_rows/pallas_call | solution.py:397
  141.7 5.4 %collective-permute-start.15 = (bf16[256,1024]{1,0:T(8,128)(2,1)}, bf16[256,1024]{1,0:T(8,128)(2,1)S(1)}, u32[]{:S(2)}, u32[]{:S(2)}) collective-permute-start(bf16[256,1024]{1,0:T(8,128)(2,1)} %get-tuple-element.118.refs_0_), channel_id=1, source_target_pairs={{0,4},{2,6},{4,8},{6,10},{8,12},{10,14},{1,5},{3,7},{5,9},{7,11},{... | collective-permute-start | bytes 1572872 | tf_op jit(solution)/shard_map/ppermute | solution.py:618
  148.4 1.8 collective-permute-start.19
  153.7 5.3 %collective-permute-done.15 = bf16[256,1024]{1,0:T(8,128)(2,1)S(1)} collective-permute-done((bf16[256,1024]{1,0:T(8,128)(2,1)}, bf16[256,1024]{1,0:T(8,128)(2,1)S(1)}, u32[]{:S(2)}, u32[]{:S(2)}) %collective-permute-start.15) | collective-permute-done | bytes 524320 | tf_op jit(solution)/shard_map/ppermute | solution.py:618
  159.5 3.8 %collective-permute-done.16 = bf16[256,1024]{1,0:T(8,128)(2,1)S(1)} collective-permute-done((bf16[256,1024]{1,0:T(8,128)(2,1)}, bf16[256,1024]{1,0:T(8,128)(2,1)S(1)}, u32[]{:S(2)}, u32[]{:S(2)}) %collective-permute-start.16) | collective-permute-done | bytes 524320 | tf_op jit(solution)/shard_map/ppermute | solution.py:618
  166.1 1.6 collective-permute-start.25
  168.5 7.5 %collective-permute-done.24.refs_15_.refs_13_.refs_9_ = bf16[256,1024]{1,0:T(8,128)(2,1)S(1)} collective-permute-done((bf16[256,1024]{1,0:T(8,128)(2,1)S(1)}, bf16[256,1024]{1,0:T(8,128)(2,1)S(1)}, u32[]{:S(2)}, u32[]{:S(2)}) %collective-permute-start.24) | collective-permute-done | bytes 524320 | tf_op jit(solution)/shard_map/ppermute | solution.py:608
  177.6 3.6 %collective-permute-done.18 = bf16[256,1024]{1,0:T(8,128)(2,1)S(1)} collective-permute-done((bf16[256,1024]{1,0:T(8,128)(2,1)S(1)}, bf16[256,1024]{1,0:T(8,128)(2,1)S(1)}, u32[]{:S(2)}, u32[]{:S(2)}) %collective-permute-start.18) | collective-permute-done | bytes 524320 | tf_op jit(solution)/shard_map/ppermute | solution.py:618
  182.6 1.4 collective-permute-start.26
  184.0 1.5 collective-permute-start.27
  185.5 2.1 fusion.1.refs_0_
  187.6 1.5 collective-permute-start.31
  193.4 8.0 %latent_keys_values.3.refs_0_.refs_2_.refs_3_ = bf16[1024,1024]{1,0:T(8,128)(2,1)S(1)} custom-call(s32[9]{0:T(128)S(1)} %stack.92.ids_ref, bf16[256,1024]{1,0:T(8,128)(2,1)S(1)} %copy-done.9, bf16[256,1024]{1,0:T(8,128)(2,1)} %collective-permute-done.19.refs_1_, bf16[256,1024]{1,0:T(8,128)(2,1)} %broadcast_select_fusion.3.refs_2_, ...), custom_call_target="tpu_custom_call" | custom-call | flops 4294967296 | bytes 4194304 | tf_op jit(solution)/shard_map/latent_keys_values/pallas_call | solution.py:460
  204.1 1.6 collective-permute-start.32
  206.0 6.1 %latent_keys_values.4.refs_1_.refs_3_.refs_4_ = bf16[768,1024]{1,0:T(8,128)(2,1)S(1)} custom-call(s32[9]{0:T(128)S(1)} %stack.92.ids_ref, bf16[256,1024]{1,0:T(8,128)(2,1)} %fusion.1.refs_0_, bf16[256,1024]{1,0:T(8,128)(2,1)} %collective-permute-done.31.refs_1_, bf16[256,1024]{1,0:T(8,128)(2,1)S(1)} %select_select_fusion.1.refs_2_, ...), custom_call_target="tpu_custom_call" | custom-call | flops 3221225472 | bytes 4194304 | tf_op jit(solution)/shard_map/latent_keys_values/pallas_call | solution.py:460
  213.2 7.4 %decode_rows.3 = (f32[512,512]{1,0:T(8,128)}, f32[512,256]{1,0:T(8,128)}) custom-call(bf16[512,512]{1,0:T(8,128)(2,1)} %collective-permute-done.8.q_ref, bf16[1024,1024]{1,0:T(8,128)(2,1)} %copy-done.12, bf16[768,1024]{1,0:T(8,128)(2,1)} %copy-done.11, bf16[1024,1024]{1,0:T(8,128)(2,1)} %copy-done.12, bf16[768,1024]{1,0:T(8,128)(2,1)} %copy-done.11), custom_call_target="tpu_custom_call" | custom-call | flops 7516192768 | bytes 5242880 | tf_op jit(solution)/shard_map/decode_rows/pallas_call | solution.py:546
  220.8 2.1 collective-permute-done.36.refs_1_
  225.0 3.5 %latent_keys_values.5.refs_2_.refs_5_.refs_0_.refs_1_ = bf16[256,1024]{1,0:T(8,128)(2,1)S(1)} custom-call(s32[9]{0:T(128)S(1)} %stack.92.ids_ref, bf16[256,1024]{1,0:T(8,128)(2,1)} %collective-permute-done.32.refs_0_, bf16[256,1024]{1,0:T(8,128)(2,1)} %collective-permute-done.36.refs_1_, bf16[256,1024]{1,0:T(8,128)(2,1)S(1)} %get-tuple-element.130.refs_8_.refs_6_.refs_2_, ...), custom_call_target="tpu_custom_call" | custom-call | flops 1073741824 | bytes 4194304 | tf_op jit(solution)/shard_map/latent_keys_values/pallas_call | solution.py:460
  229.3 3.4 %decode_rows.5 = bf16[512,512]{1,0:T(8,128)(2,1)} custom-call(bf16[512,512]{1,0:T(8,128)(2,1)} %collective-permute-done.8.q_ref, bf16[256,1024]{1,0:T(8,128)(2,1)} %copy-done.7, bf16[256,1024]{1,0:T(8,128)(2,1)} %copy-done.7, f32[512,512]{1,0:T(8,128)} %get-tuple-element.144.refs_2_, f32[512,256]{1,0:T(8,128)} %get-tuple-element.145.refs_3_), custom_call_target="tpu_custom_call" | custom-call | flops 1073741824 | bytes 2097152 | tf_op jit(solution)/shard_map/decode_rows/pallas_call | solution.py:546
  232.7 1.4 collective-permute-start.37
  234.1 8.4 %decode_rows.4 = f32[512,512]{1,0:T(8,128)} custom-call(bf16[512,512]{1,0:T(8,128)(2,1)} %get-tuple-element.152.q_ref, bf16[1024,1024]{1,0:T(8,128)(2,1)} %copy-done.12, bf16[768,1024]{1,0:T(8,128)(2,1)} %copy-done.11, bf16[256,1024]{1,0:T(8,128)(2,1)} %copy-done.7, bf16[1024,1024]{1,0:T(8,128)(2,1)} %copy-done.12, bf16[768,1024]{1,0:T(8,128)(2,1)} %copy-done.11, ...), custom_call_target="tpu_custom_call" | custom-call | flops 8589934592 | bytes 5767168 | tf_op jit(solution)/shard_map/decode_rows/pallas_call | solution.py:546
  242.5 4.3 %collective-permute-done.37 = bf16[512,512]{1,0:T(8,128)(2,1)S(1)} collective-permute-done((bf16[512,512]{1,0:T(8,128)(2,1)}, bf16[512,512]{1,0:T(8,128)(2,1)S(1)}, u32[]{:S(2)}, u32[]{:S(2)}) %collective-permute-start.37) | collective-permute-done | bytes 524320 | tf_op jit(solution)/shard_map/ppermute | solution.py:778
  247.0 1.6 fusion
  (151 shorter events, 43.0 us)
Async XLA Ops:
  0.6 59.5 %copy-start = (bf16[3,1024]{1,0:T(4,128)(2,1)S(1)}, bf16[3,1024]{1,0:T(4,128)(2,1)}, u32[]{:S(2)}) copy-start(bf16[3,1024]{1,0:T(4,128)(2,1)} %param.25) | copy-start | bytes 18436
  2.7 10.2 %copy-start.30 = (f32[3,8]{1,0:T(4,128)S(1)}, f32[3,8]{1,0:T(4,128)}, u32[]{:S(2)}) copy-start(f32[3,8]{1,0:T(4,128)} %param.26) | copy-start | bytes 292
  2.7 10.9 %copy-start.23 = (bf16[256,1024]{1,0:T(8,128)(2,1)S(1)}, bf16[256,1024]{1,0:T(8,128)(2,1)}, u32[]{:S(2)}) copy-start(bf16[256,1024]{1,0:T(8,128)(2,1)} %param.22) | copy-start | bytes 1572868
  2.8 10.9 %copy-start.24 = (bf16[256,1024]{1,0:T(8,128)(2,1)S(1)}, bf16[256,1024]{1,0:T(8,128)(2,1)}, u32[]{:S(2)}) copy-start(bf16[256,1024]{1,0:T(8,128)(2,1)} %param.21) | copy-start | bytes 1572868
  2.9 32.1 %collective-permute-start = (bf16[528,1024]{1,0:T(8,128)(2,1)S(1)}, bf16[528,1024]{1,0:T(8,128)(2,1)}, u32[]{:S(2)}, u32[]{:S(2)}) collective-permute-start(bf16[528,1024]{1,0:T(8,128)(2,1)S(1)} %pad_maximum_fusion), channel_id=1, source_target_pairs={{0,2},{2,0},{4,6},{6,4},{8,10},{10,8},{12,14},{14,12},{1,3},{3,1},... | collective-permute-start | bytes 3244040 | tf_op jit(solution)/shard_map/ppermute | solution.py:611
  8.4 10.9 %collective-permute-start.1 = (bf16[528,256]{1,0:T(8,128)(2,1)}, bf16[528,256]{1,0:T(8,128)(2,1)}, u32[]{:S(2)}, u32[]{:S(2)}) collective-permute-start(bf16[528,256]{1,0:T(8,128)(2,1)} %pad_maximum_fusion.3), channel_id=1, source_target_pairs={{4,0},{6,2},{8,4},{10,6},{12,8},{14,10},{0,12},{2,14},{5,1},{7,3},... | collective-permute-start | bytes 811016 | tf_op jit(solution)/shard_map/ppermute | solution.py:614
  12.0 23.0 %collective-permute-start.2 = (bf16[528,256]{1,0:T(8,128)(2,1)}, bf16[528,256]{1,0:T(8,128)(2,1)}, u32[]{:S(2)}, u32[]{:S(2)}) collective-permute-start(bf16[528,256]{1,0:T(8,128)(2,1)} %pad_maximum_fusion.3), channel_id=1, source_target_pairs={{8,0},{10,2},{12,4},{14,6},{0,8},{2,10},{4,12},{6,14},{9,1},{11,3}... | collective-permute-start | bytes 811016 | tf_op jit(solution)/shard_map/ppermute | solution.py:614
  12.0 23.0 %collective-permute-start.3 = (bf16[528,256]{1,0:T(8,128)(2,1)}, bf16[528,256]{1,0:T(8,128)(2,1)S(1)}, u32[]{:S(2)}, u32[]{:S(2)}) collective-permute-start(bf16[528,256]{1,0:T(8,128)(2,1)} %pad_maximum_fusion.3), channel_id=1, source_target_pairs={{12,0},{14,2},{0,4},{2,6},{4,8},{6,10},{8,12},{10,14},{13,1},{15,3... | collective-permute-start | bytes 811016 | tf_op jit(solution)/shard_map/ppermute | solution.py:614
  35.0 15.0 %copy-start.25 = (bf16[528,256]{1,0:T(8,128)(2,1)}, bf16[528,256]{1,0:T(8,128)(2,1)S(1)}, u32[]{:S(2)}) copy-start(bf16[528,256]{1,0:T(8,128)(2,1)S(1)} %collective-permute-done.3) | copy-start | bytes 811012
  35.0 15.0 %collective-permute-start.4 = (bf16[256,1024]{1,0:T(8,128)(2,1)S(1)}, bf16[256,1024]{1,0:T(8,128)(2,1)S(1)}, u32[]{:S(2)}, u32[]{:S(2)}) collective-permute-start(bf16[256,1024]{1,0:T(8,128)(2,1)S(1)} %pad_maximum_fusion.1), channel_id=1, source_target_pairs={{0,2},{2,0},{4,6},{6,4},{8,10},{10,8},{12,14},{14,12},{1,3},{3,1},... | collective-permute-start | bytes 1572872 | tf_op jit(solution)/shard_map/ppermute | solution.py:611
  50.0 57.8 %all-to-all-start = ((bf16[4,528,512]{2,1,0:T(8,128)(2,1)}), bf16[4,528,512]{2,1,0:T(8,128)(2,1)S(1)}, u32[]{:S(2)}, u32[]{:S(2)}) async-start(bf16[4,528,512]{2,1,0:T(8,128)(2,1)} %bitcast.52), calls=%async_computation | async-start | bytes 4325376 | tf_op jit(solution)/shard_map/all_to_all | solution.py:672
  58.6 30.3 %collective-permute-start.5 = (bf16[2624,256]{1,0:T(8,128)(2,1)}, bf16[2624,256]{1,0:T(8,128)(2,1)S(1)}, u32[]{:S(2)}, u32[]{:S(2)}) collective-permute-start(bf16[2624,256]{1,0:T(8,128)(2,1)} %get-tuple-element.161), channel_id=1, source_target_pairs={{0,2},{2,0},{4,6},{6,4},{8,10},{10,8},{12,14},{14,12},{1,3},{3,1},... | collective-permute-start | bytes 4030472 | tf_op jit(solution)/shard_map/ppermute | solution.py:611
  60.6 33.4 %copy-start.22 = (bf16[256,512]{1,0:T(8,128)(2,1)S(1)}, bf16[256,512]{1,0:T(8,128)(2,1)}, u32[]{:S(2)}) copy-start(bf16[256,512]{1,0:T(8,128)(2,1)} %get-tuple-element.158) | copy-start | bytes 786436
  60.6 43.4 %collective-permute-start.6 = (bf16[1584,256]{1,0:T(8,128)(2,1)}, bf16[1584,256]{1,0:T(8,128)(2,1)}, u32[]{:S(2)}, u32[]{:S(2)}) collective-permute-start(bf16[1584,256]{1,0:T(8,128)(2,1)} %get-tuple-element.160.refs_1_), channel_id=1, source_target_pairs={{0,16},{16,0},{1,17},{17,1},{2,18},{18,2},{3,19},{19,3},{4,20},{20... | collective-permute-start | bytes 2433032 | tf_op jit(solution)/shard_map/ppermute | solution.py:608
  89.8 18.0 %collective-permute-start.7 = (bf16[1584,256]{1,0:T(8,128)(2,1)}, bf16[1584,256]{1,0:T(8,128)(2,1)}, u32[]{:S(2)}, u32[]{:S(2)}) collective-permute-start(bf16[1584,256]{1,0:T(8,128)(2,1)} %slice.62), channel_id=1, source_target_pairs={{0,16},{16,0},{1,17},{17,1},{2,18},{18,2},{3,19},{19,3},{4,20},{20... | collective-permute-start | bytes 2433032 | tf_op jit(solution)/shard_map/ppermute | solution.py:608
  92.4 11.6 %collective-permute-start.8 = (bf16[512,512]{1,0:T(8,128)(2,1)}, bf16[512,512]{1,0:T(8,128)(2,1)}, u32[]{:S(2)}, u32[]{:S(2)}) collective-permute-start(bf16[512,512]{1,0:T(8,128)(2,1)} %get-tuple-element.153), channel_id=1, source_target_pairs={{0,2},{2,0},{4,6},{6,4},{8,10},{10,8},{12,14},{14,12},{1,3},{3,1},... | collective-permute-start | bytes 1572872 | tf_op jit(solution)/shard_map/ppermute | solution.py:611
  95.9 14.5 %collective-permute-start.10 = (bf16[256,1024]{1,0:T(8,128)(2,1)}, bf16[256,1024]{1,0:T(8,128)(2,1)}, u32[]{:S(2)}, u32[]{:S(2)}) collective-permute-start(bf16[256,1024]{1,0:T(8,128)(2,1)} %get-tuple-element.155), channel_id=1, source_target_pairs={{0,4},{2,6},{4,8},{6,10},{8,12},{10,14},{1,5},{3,7},{5,9},{7,11},{... | collective-permute-start | bytes 1572872 | tf_op jit(solution)/shard_map/ppermute | solution.py:618
  100.4 13.8 %collective-permute-start.11 = (bf16[256,1024]{1,0:T(8,128)(2,1)}, bf16[256,1024]{1,0:T(8,128)(2,1)}, u32[]{:S(2)}, u32[]{:S(2)}) collective-permute-start(bf16[256,1024]{1,0:T(8,128)(2,1)} %get-tuple-element.155), channel_id=1, source_target_pairs={{12,8},{14,10},{8,4},{10,6},{4,0},{6,2},{13,9},{15,11},{9,5},{11,7... | collective-permute-start | bytes 1572872 | tf_op jit(solution)/shard_map/ppermute | solution.py:618
  114.1 15.0 %collective-permute-start.12 = (bf16[256,1024]{1,0:T(8,128)(2,1)}, bf16[256,1024]{1,0:T(8,128)(2,1)S(1)}, u32[]{:S(2)}, u32[]{:S(2)}) collective-permute-start(bf16[256,1024]{1,0:T(8,128)(2,1)} %collective-permute-done.10), channel_id=1, source_target_pairs={{4,8},{6,10},{8,12},{10,14},{5,9},{7,11},{9,13},{11,15},{20,24},{2... | collective-permute-start | bytes 1572872 | tf_op jit(solution)/shard_map/ppermute | solution.py:618
  114.8 14.3 %collective-permute-start.13 = (bf16[256,1024]{1,0:T(8,128)(2,1)}, bf16[256,1024]{1,0:T(8,128)(2,1)S(1)}, u32[]{:S(2)}, u32[]{:S(2)}) collective-permute-start(bf16[256,1024]{1,0:T(8,128)(2,1)} %collective-permute-done.11), channel_id=1, source_target_pairs={{8,4},{10,6},{4,0},{6,2},{9,5},{11,7},{5,1},{7,3},{24,20},{26,22},... | collective-permute-start | bytes 1572872 | tf_op jit(solution)/shard_map/ppermute | solution.py:618
  116.1 6.4 %collective-permute-start.9 = (bf16[256,512]{1,0:T(8,128)(2,1)S(1)}, bf16[256,512]{1,0:T(8,128)(2,1)S(1)}, u32[]{:S(2)}, u32[]{:S(2)}) collective-permute-start(bf16[256,512]{1,0:T(8,128)(2,1)S(1)} %get-tuple-element.85), channel_id=1, source_target_pairs={{0,2},{2,0},{4,6},{6,4},{8,10},{10,8},{12,14},{14,12},{1,3},{3,1},... | collective-permute-start | bytes 786440 | tf_op jit(solution)/shard_map/ppermute | solution.py:611
  123.3 11.8 %copy-start.31 = (s32[3]{0:T(128)S(1)}, s32[3]{0:T(128)}, u32[]{:S(2)}) copy-start(s32[3]{0:T(128)} %param.27) | copy-start | bytes 40
  129.1 8.1 %collective-permute-start.14 = (f32[256,2048]{1,0:T(8,128)}, f32[256,2048]{1,0:T(8,128)}, u32[]{:S(2)}, u32[]{:S(2)}) collective-permute-start(f32[256,2048]{1,0:T(8,128)} %project_rows.1.mine_ref), channel_id=1, source_target_pairs={{0,1},{1,0},{2,3},{3,2},{4,5},{5,4},{6,7},{7,6},{8,9},{9,8},{10,11... | collective-permute-start | bytes 6291464 | tf_op jit(solution)/shard_map/ppermute | solution.py:713
  131.4 17.0 %collective-permute-start.21 = (bf16[256,1024]{1,0:T(8,128)(2,1)S(1)}, bf16[256,1024]{1,0:T(8,128)(2,1)}, u32[]{:S(2)}, u32[]{:S(2)}) collective-permute-start(bf16[256,1024]{1,0:T(8,128)(2,1)S(1)} %collective-permute-done.12), channel_id=1, source_target_pairs={{8,12},{10,14},{9,13},{11,15},{24,28},{26,30},{25,29},{27,31}} | collective-permute-start | bytes 1572872 | tf_op jit(solution)/shard_map/ppermute | solution.py:618
  132.9 17.3 %collective-permute-start.22 = (bf16[256,1024]{1,0:T(8,128)(2,1)S(1)}, bf16[256,1024]{1,0:T(8,128)(2,1)}, u32[]{:S(2)}, u32[]{:S(2)}) collective-permute-start(bf16[256,1024]{1,0:T(8,128)(2,1)S(1)} %collective-permute-done.13), channel_id=1, source_target_pairs={{4,0},{6,2},{5,1},{7,3},{20,16},{22,18},{21,17},{23,19}} | collective-permute-start | bytes 1572872 | tf_op jit(solution)/shard_map/ppermute | solution.py:618
  135.2 29.6 %collective-permute-start.20 = (bf16[256,1024]{1,0:T(8,128)(2,1)S(1)}, bf16[256,1024]{1,0:T(8,128)(2,1)S(1)}, u32[]{:S(2)}, u32[]{:S(2)}) collective-permute-start(bf16[256,1024]{1,0:T(8,128)(2,1)S(1)} %broadcast_select_fusion.2.refs_10_.refs_8_.refs_4_), channel_id=1, source_target_pairs={{0,16},{16,0},{1,17},{17,1},{2,18},{18,2},{3,19},{19,3},{4,20},{20... | collective-permute-start | bytes 1572872 | tf_op jit(solution)/shard_map/ppermute | solution.py:608
  141.7 17.2 %collective-permute-start.15 = (bf16[256,1024]{1,0:T(8,128)(2,1)}, bf16[256,1024]{1,0:T(8,128)(2,1)S(1)}, u32[]{:S(2)}, u32[]{:S(2)}) collective-permute-start(bf16[256,1024]{1,0:T(8,128)(2,1)} %get-tuple-element.118.refs_0_), channel_id=1, source_target_pairs={{0,4},{2,6},{4,8},{6,10},{8,12},{10,14},{1,5},{3,7},{5,9},{7,11},{... | collective-permute-start | bytes 1572872 | tf_op jit(solution)/shard_map/ppermute | solution.py:618
  147.1 16.1 %collective-permute-start.16 = (bf16[256,1024]{1,0:T(8,128)(2,1)}, bf16[256,1024]{1,0:T(8,128)(2,1)S(1)}, u32[]{:S(2)}, u32[]{:S(2)}) collective-permute-start(bf16[256,1024]{1,0:T(8,128)(2,1)} %get-tuple-element.118.refs_0_), channel_id=1, source_target_pairs={{12,8},{14,10},{8,4},{10,6},{4,0},{6,2},{13,9},{15,11},{9,5},{11,7... | collective-permute-start | bytes 1572872 | tf_op jit(solution)/shard_map/ppermute | solution.py:618
  148.4 17.7 %collective-permute-start.19 = (bf16[256,1024]{1,0:T(8,128)(2,1)}, bf16[256,1024]{1,0:T(8,128)(2,1)}, u32[]{:S(2)}, u32[]{:S(2)}) collective-permute-start(bf16[256,1024]{1,0:T(8,128)(2,1)} %get-tuple-element.118.refs_0_), channel_id=1, source_target_pairs={{0,2},{2,0},{4,6},{6,4},{8,10},{10,8},{12,14},{14,12},{1,3},{3,1},... | collective-permute-start | bytes 1572872 | tf_op jit(solution)/shard_map/ppermute | solution.py:611
  151.4 16.4 %collective-permute-start.23 = (bf16[256,1024]{1,0:T(8,128)(2,1)S(1)}, bf16[256,1024]{1,0:T(8,128)(2,1)S(1)}, u32[]{:S(2)}, u32[]{:S(2)}) collective-permute-start(bf16[256,1024]{1,0:T(8,128)(2,1)S(1)} %broadcast_select_fusion.1.refs_12_.refs_10_.refs_6_), channel_id=1, source_target_pairs={{0,16},{16,0},{1,17},{17,1},{2,18},{18,2},{3,19},{19,3},{4,20},{20... | collective-permute-start | bytes 1572872 | tf_op jit(solution)/shard_map/ppermute | solution.py:608
  158.9 17.1 %copy-start.15 = (bf16[256,1024]{1,0:T(8,128)(2,1)}, bf16[256,1024]{1,0:T(8,128)(2,1)S(1)}, u32[]{:S(2)}) copy-start(bf16[256,1024]{1,0:T(8,128)(2,1)S(1)} %collective-permute-done.15) | copy-start | bytes 1572868
  158.9 17.1 %collective-permute-start.24 = (bf16[256,1024]{1,0:T(8,128)(2,1)S(1)}, bf16[256,1024]{1,0:T(8,128)(2,1)S(1)}, u32[]{:S(2)}, u32[]{:S(2)}) collective-permute-start(bf16[256,1024]{1,0:T(8,128)(2,1)S(1)} %broadcast_select_fusion.refs_14_.refs_12_.refs_8_), channel_id=1, source_target_pairs={{0,16},{16,0},{1,17},{17,1},{2,18},{18,2},{3,19},{19,3},{4,20},{20... | collective-permute-start | bytes 1572872 | tf_op jit(solution)/shard_map/ppermute | solution.py:608
  163.3 13.6 %collective-permute-start.17 = (bf16[256,1024]{1,0:T(8,128)(2,1)S(1)}, bf16[256,1024]{1,0:T(8,128)(2,1)S(1)}, u32[]{:S(2)}, u32[]{:S(2)}) collective-permute-start(bf16[256,1024]{1,0:T(8,128)(2,1)S(1)} %collective-permute-done.15), channel_id=1, source_target_pairs={{4,8},{6,10},{8,12},{10,14},{5,9},{7,11},{9,13},{11,15},{20,24},{2... | collective-permute-start | bytes 1572872 | tf_op jit(solution)/shard_map/ppermute | solution.py:618
  164.8 16.5 %collective-permute-start.18 = (bf16[256,1024]{1,0:T(8,128)(2,1)S(1)}, bf16[256,1024]{1,0:T(8,128)(2,1)S(1)}, u32[]{:S(2)}, u32[]{:S(2)}) collective-permute-start(bf16[256,1024]{1,0:T(8,128)(2,1)S(1)} %collective-permute-done.16), channel_id=1, source_target_pairs={{8,4},{10,6},{4,0},{6,2},{9,5},{11,7},{5,1},{7,3},{24,20},{26,22},... | collective-permute-start | bytes 1572872 | tf_op jit(solution)/shard_map/ppermute | solution.py:618
  166.1 16.0 %collective-permute-start.25 = (bf16[256,1024]{1,0:T(8,128)(2,1)}, bf16[256,1024]{1,0:T(8,128)(2,1)}, u32[]{:S(2)}, u32[]{:S(2)}) collective-permute-start(bf16[256,1024]{1,0:T(8,128)(2,1)} %broadcast_select_fusion.3.refs_2_), channel_id=1, source_target_pairs={{0,2},{2,0},{4,6},{6,4},{8,10},{10,8},{12,14},{14,12},{1,3},{3,1},... | collective-permute-start | bytes 1572872 | tf_op jit(solution)/shard_map/ppermute | solution.py:611
  182.1 5.5 %collective-permute-start.28 = (bf16[256,1024]{1,0:T(8,128)(2,1)}, bf16[256,1024]{1,0:T(8,128)(2,1)}, u32[]{:S(2)}, u32[]{:S(2)}) collective-permute-start(bf16[256,1024]{1,0:T(8,128)(2,1)} %collective-permute-done.19.refs_1_), channel_id=1, source_target_pairs={{0,1},{1,0},{2,3},{3,2},{4,5},{5,4},{6,7},{7,6},{8,9},{9,8},{10,11... | collective-permute-start | bytes 1572872 | tf_op jit(solution)/shard_map/ppermute | solution.py:723
  182.1 7.1 %collective-permute-start.29 = (bf16[256,1024]{1,0:T(8,128)(2,1)}, bf16[256,1024]{1,0:T(8,128)(2,1)}, u32[]{:S(2)}, u32[]{:S(2)}) collective-permute-start(bf16[256,1024]{1,0:T(8,128)(2,1)} %broadcast_select_fusion.3.refs_2_), channel_id=1, source_target_pairs={{0,1},{1,0},{2,3},{3,2},{4,5},{5,4},{6,7},{7,6},{8,9},{9,8},{10,11... | collective-permute-start | bytes 1572872 | tf_op jit(solution)/shard_map/ppermute | solution.py:723
  182.6 6.6 %collective-permute-start.30 = (bf16[256,1024]{1,0:T(8,128)(2,1)}, bf16[256,1024]{1,0:T(8,128)(2,1)}, u32[]{:S(2)}, u32[]{:S(2)}) collective-permute-start(bf16[256,1024]{1,0:T(8,128)(2,1)} %collective-permute-done.25.refs_3_), channel_id=1, source_target_pairs={{0,1},{1,0},{2,3},{3,2},{4,5},{5,4},{6,7},{7,6},{8,9},{9,8},{10,11... | collective-permute-start | bytes 1572872 | tf_op jit(solution)/shard_map/ppermute | solution.py:723
  182.6 18.9 %collective-permute-start.26 = (bf16[256,1024]{1,0:T(8,128)(2,1)}, bf16[256,1024]{1,0:T(8,128)(2,1)}, u32[]{:S(2)}, u32[]{:S(2)}) collective-permute-start(bf16[256,1024]{1,0:T(8,128)(2,1)} %copy-done.16), channel_id=1, source_target_pairs={{8,12},{10,14},{9,13},{11,15},{24,28},{26,30},{25,29},{27,31}} | collective-permute-start | bytes 1572872 | tf_op jit(solution)/shard_map/ppermute | solution.py:618
  184.0 17.4 %collective-permute-start.27 = (bf16[256,1024]{1,0:T(8,128)(2,1)}, bf16[256,1024]{1,0:T(8,128)(2,1)}, u32[]{:S(2)}, u32[]{:S(2)}) collective-permute-start(bf16[256,1024]{1,0:T(8,128)(2,1)} %copy-done.18), channel_id=1, source_target_pairs={{4,0},{6,2},{5,1},{7,3},{20,16},{22,18},{21,17},{23,19}} | collective-permute-start | bytes 1572872 | tf_op jit(solution)/shard_map/ppermute | solution.py:618
  187.6 14.7 %collective-permute-start.31 = (bf16[256,1024]{1,0:T(8,128)(2,1)}, bf16[256,1024]{1,0:T(8,128)(2,1)}, u32[]{:S(2)}, u32[]{:S(2)}) collective-permute-start(bf16[256,1024]{1,0:T(8,128)(2,1)} %fusion.1.refs_0_), channel_id=1, source_target_pairs={{0,2},{2,0},{4,6},{6,4},{8,10},{10,8},{12,14},{14,12},{1,3},{3,1},... | collective-permute-start | bytes 1572872 | tf_op jit(solution)/shard_map/ppermute | solution.py:611
  193.4 9.4 %copy-start.19 = (bf16[256,1024]{1,0:T(8,128)(2,1)S(1)}, bf16[256,1024]{1,0:T(8,128)(2,1)}, u32[]{:S(2)}) copy-start(bf16[256,1024]{1,0:T(8,128)(2,1)} %copy-done.18) | copy-start | bytes 1572868
  202.2 3.4 %collective-permute-start.33 = (bf16[256,1024]{1,0:T(8,128)(2,1)}, bf16[256,1024]{1,0:T(8,128)(2,1)S(1)}, u32[]{:S(2)}, u32[]{:S(2)}) collective-permute-start(bf16[256,1024]{1,0:T(8,128)(2,1)} %fusion.1.refs_0_), channel_id=1, source_target_pairs={{0,1},{1,0},{2,3},{3,2},{4,5},{5,4},{6,7},{7,6},{8,9},{9,8},{10,11... | collective-permute-start | bytes 1572872 | tf_op jit(solution)/shard_map/ppermute | solution.py:723
  202.2 3.4 %collective-permute-start.34 = (bf16[256,1024]{1,0:T(8,128)(2,1)}, bf16[256,1024]{1,0:T(8,128)(2,1)S(1)}, u32[]{:S(2)}, u32[]{:S(2)}) collective-permute-start(bf16[256,1024]{1,0:T(8,128)(2,1)} %collective-permute-done.31.refs_1_), channel_id=1, source_target_pairs={{0,1},{1,0},{2,3},{3,2},{4,5},{5,4},{6,7},{7,6},{8,9},{9,8},{10,11... | collective-permute-start | bytes 1572872 | tf_op jit(solution)/shard_map/ppermute | solution.py:723
  204.0 2.0 collective-permute-start.35
  204.1 16.5 %collective-permute-start.32 = (bf16[256,1024]{1,0:T(8,128)(2,1)S(1)}, bf16[256,1024]{1,0:T(8,128)(2,1)}, u32[]{:S(2)}, u32[]{:S(2)}) collective-permute-start(bf16[256,1024]{1,0:T(8,128)(2,1)S(1)} %select_select_fusion.1.refs_2_), channel_id=1, source_target_pairs={{0,2},{2,0},{4,6},{6,4},{8,10},{10,8},{12,14},{14,12},{1,3},{3,1},... | collective-permute-start | bytes 1572872 | tf_op jit(solution)/shard_map/ppermute | solution.py:611
  220.6 2.3 collective-permute-start.36
  232.7 14.2 %collective-permute-start.37 = (bf16[512,512]{1,0:T(8,128)(2,1)}, bf16[512,512]{1,0:T(8,128)(2,1)S(1)}, u32[]{:S(2)}, u32[]{:S(2)}) collective-permute-start(bf16[512,512]{1,0:T(8,128)(2,1)} %decode_rows.5), channel_id=1, source_target_pairs={{0,2},{2,0},{4,6},{6,4},{8,10},{10,8},{12,14},{14,12},{1,3},{3,1},... | collective-permute-start | bytes 1572872 | tf_op jit(solution)/shard_map/ppermute | solution.py:778
  (23 other events, 59.1 us)

commit v16 on v15

--- a/solution.py
+++ b/solution.py
@@ -431,10 +431,9 @@
             pl.when(is_mine)(functools.partial(copy, mine))
             pl.when(jnp.logical_not(is_mine))(functools.partial(copy, theirs))
 
-    start, block = 0, w_ref.shape[1]
+    start = 0
     for band in w_refs:
-        columns = pl.ds(pl.multiple_of(pl.program_id(0) * block, block), block)
-        w_ref[start : start + band.shape[0], :] = band[:, columns]
+        w_ref[start : start + band.shape[0], :] = band[...]
         start += band.shape[0]
     out_ref[...] = jnp.dot(
         normed_ref[...], w_ref[...], preferred_element_type=jnp.float32
@@ -450,7 +449,8 @@
     grid_spec = pltpu.PrefetchScalarGridSpec(
         num_scalar_prefetch=1,
         grid=(width // block,),
-        in_specs=[pl.BlockSpec(memory_space=pltpu.VMEM)] * (2 * pieces + len(bands)),
+        in_specs=[pl.BlockSpec(memory_space=pltpu.VMEM)] * (2 * pieces)
+        + [pl.BlockSpec((band.shape[0], block), lambda i, ids: (0, i)) for band in bands],
         out_specs=pl.BlockSpec((rows * pieces, block), lambda i, ids: (0, i)),
         scratch_shapes=[
             pltpu.VMEM((rows * pieces, total), jnp.bfloat16),
@@ -461,7 +461,7 @@
         functools.partial(latents_kernel, pieces),
         grid_spec=grid_spec,
         out_shape=jax.ShapeDtypeStruct((rows * pieces, width), jnp.bfloat16),
-        compiler_params=params(24),
+        compiler_params=params(28),
         cost_estimate=cost(2 * rows * pieces * total * width, 2 * total * width),
         name="latent_keys_values",
     )(ids, *mine, *theirs, *bands)

time: 250 us -> 250 us (level)
  no operation moved by 1% of the time
where the time goes in v16:
time: 250 us; the launch traced here: 249 us
  waiting for transfers between devices  88.8 us (36%)
  Pallas kernels  63.9 us (26%)
  starting transfers between devices  55 us (22%)
  local copies, waits for them, and re-layouts  26.3 us (11%)
  other arithmetic  13.3 us (5%)
    ppermute x9, waiting for transfers between devices, over_near(): return lax.ppermute(value, 'pos', near)  33.9 us
    ppermute x12, starting transfers between devices, hop(): lax.ppermute(v, 'pos', hop_perm(pos, step, way))  22 us
    ppermute x3, waiting for transfers between devices, over_far(): return lax.ppermute(value, 'pos', shift_perm(pos, k))  20.4 us
    pallas_call x3, Pallas kernels, decode(): pl.pallas_call(functools.partial(decode_kernel, len(keys_values), first,...  19.2 us
    pallas_call x3, Pallas kernels, latent_keys_values(): pl.pallas_call(functools.partial(latents_kernel, pieces), grid_spec=grid_...  18 us
    unnamed x69, local copies, waits for them, and re-layouts  17.9 us
    ppermute x12, waiting for transfers between devices, hop(): lax.ppermute(v, 'pos', hop_perm(pos, step, way))  16.4 us
    ppermute x9, starting transfers between devices, over_near(): return lax.ppermute(value, 'pos', near)  14.8 us
  transfers between devices with their start and end apart: 39, of which 15 were waited for; matrix products, arithmetic and copies ran while one was open for 9% of the time, Pallas kernels for 23%

profile of v16, /device:TPU:0, one launch (start us, length us, event | category | flops | bytes accessed | tf_op | source)
XLA Modules:
  0.0 248.9 jit_solution(15525276485813470312)
XLA Ops:
  1.4 1.3 constant_dynamic-slice_fusion.8
  2.9 3.0 %collective-permute-start = (bf16[528,1024]{1,0:T(8,128)(2,1)S(1)}, bf16[528,1024]{1,0:T(8,128)(2,1)}, u32[]{:S(2)}, u32[]{:S(2)}) collective-permute-start(bf16[528,1024]{1,0:T(8,128)(2,1)S(1)} %pad_maximum_fusion), channel_id=1, source_target_pairs={{0,2},{2,0},{4,6},{6,4},{8,10},{10,8},{12,14},{14,12},{1,3},{3,1},... | collective-permute-start | bytes 3244040 | tf_op jit(solution)/shard_map/ppermute | solution.py:611
  8.4 3.6 %collective-permute-start.1 = (bf16[528,256]{1,0:T(8,128)(2,1)}, bf16[528,256]{1,0:T(8,128)(2,1)}, u32[]{:S(2)}, u32[]{:S(2)}) collective-permute-start(bf16[528,256]{1,0:T(8,128)(2,1)} %pad_maximum_fusion.3), channel_id=1, source_target_pairs={{4,0},{6,2},{8,4},{10,6},{12,8},{14,10},{0,12},{2,14},{5,1},{7,3},... | collective-permute-start | bytes 811016 | tf_op jit(solution)/shard_map/ppermute | solution.py:614
  14.6 4.7 %collective-permute-done.1 = bf16[528,256]{1,0:T(8,128)(2,1)} collective-permute-done((bf16[528,256]{1,0:T(8,128)(2,1)}, bf16[528,256]{1,0:T(8,128)(2,1)}, u32[]{:S(2)}, u32[]{:S(2)}) %collective-permute-start.1) | collective-permute-done | bytes 270368 | tf_op jit(solution)/shard_map/ppermute | solution.py:614
  19.2 15.8 %collective-permute-done.2 = bf16[528,256]{1,0:T(8,128)(2,1)} collective-permute-done((bf16[528,256]{1,0:T(8,128)(2,1)}, bf16[528,256]{1,0:T(8,128)(2,1)}, u32[]{:S(2)}, u32[]{:S(2)}) %collective-permute-start.2) | collective-permute-done | bytes 270368 | tf_op jit(solution)/shard_map/ppermute | solution.py:614
  35.6 14.4 %encode_rows.1 = bf16[2112,512]{1,0:T(8,128)(2,1)} custom-call(s32[1]{0:T(128)} %bitcast.9.ids_ref, bf16[2048,1024]{1,0:T(8,128)(2,1)} %q_ref.1, bf16[512,1024]{1,0:T(8,128)(2,1)} %k_ref.1, bf16[512,1024]{1,0:T(8,128)(2,1)} %v_ref.1, bf16[16,1024]{1,0:T(8,128)(2,1)} %copy-done.28, bf16[528,1024]{1,0:T(8,128)(2,1)} %collective-permute-done.near_ref, ...), custom_call_target="tpu_custom_call" | custom-call | flops 8589934592 | bytes 2097152 | tf_op jit(solution)/shard_map/encode_rows/pallas_call | solution.py:262
  50.0 4.0 %all-to-all-start = ((bf16[4,528,512]{2,1,0:T(8,128)(2,1)}), bf16[4,528,512]{2,1,0:T(8,128)(2,1)S(1)}, u32[]{:S(2)}, u32[]{:S(2)}) async-start(bf16[4,528,512]{2,1,0:T(8,128)(2,1)} %bitcast.52), calls=%async_computation | async-start | bytes 4325376 | tf_op jit(solution)/shard_map/all_to_all | solution.py:672
  54.1 1.9 constant_dynamic-update-slice_fusion.7
  55.9 1.8 constant_dynamic-update-slice_fusion.6
  58.6 1.5 collective-permute-start.5
  60.6 1.6 collective-permute-start.6
  62.1 26.7 %collective-permute-done.5.refs_3_ = bf16[2624,256]{1,0:T(8,128)(2,1)S(1)} collective-permute-done((bf16[2624,256]{1,0:T(8,128)(2,1)}, bf16[2624,256]{1,0:T(8,128)(2,1)S(1)}, u32[]{:S(2)}, u32[]{:S(2)}) %collective-permute-start.5) | collective-permute-done | bytes 1343520 | tf_op jit(solution)/shard_map/ppermute | solution.py:611
  89.8 1.5 collective-permute-start.7
  92.4 1.5 collective-permute-start.8
  93.9 2.0 pad_maximum_fusion.2
  95.9 4.4 %collective-permute-start.10 = (bf16[256,1024]{1,0:T(8,128)(2,1)}, bf16[256,1024]{1,0:T(8,128)(2,1)}, u32[]{:S(2)}, u32[]{:S(2)}) collective-permute-start(bf16[256,1024]{1,0:T(8,128)(2,1)} %get-tuple-element.155), channel_id=1, source_target_pairs={{0,4},{2,6},{4,8},{6,10},{8,12},{10,14},{1,5},{3,7},{5,9},{7,11},{... | collective-permute-start | bytes 1572872 | tf_op jit(solution)/shard_map/ppermute | solution.py:618
  101.6 2.4 collective-permute-done.8.q_ref
  104.0 3.8 %collective-permute-done.7.refs_4_ = bf16[1584,256]{1,0:T(8,128)(2,1)} collective-permute-done((bf16[1584,256]{1,0:T(8,128)(2,1)}, bf16[1584,256]{1,0:T(8,128)(2,1)}, u32[]{:S(2)}, u32[]{:S(2)}) %collective-permute-start.7) | collective-permute-done | bytes 811040 | tf_op jit(solution)/shard_map/ppermute | solution.py:608
  107.9 1.9 merge_rows.1
  110.5 3.7 %collective-permute-done.11 = bf16[256,1024]{1,0:T(8,128)(2,1)} collective-permute-done((bf16[256,1024]{1,0:T(8,128)(2,1)}, bf16[256,1024]{1,0:T(8,128)(2,1)}, u32[]{:S(2)}, u32[]{:S(2)}) %collective-permute-start.11) | collective-permute-done | bytes 524320 | tf_op jit(solution)/shard_map/ppermute | solution.py:618
  116.1 1.6 collective-permute-start.9
  118.4 4.2 %collective-permute-done.9.near_ref = bf16[256,512]{1,0:T(8,128)(2,1)S(1)} collective-permute-done((bf16[256,512]{1,0:T(8,128)(2,1)S(1)}, bf16[256,512]{1,0:T(8,128)(2,1)S(1)}, u32[]{:S(2)}, u32[]{:S(2)}) %collective-permute-start.9) | collective-permute-done | bytes 262176 | tf_op jit(solution)/shard_map/ppermute | solution.py:611
  123.3 5.8 %project_rows.1.mine_ref = f32[256,2048]{1,0:T(8,128)} custom-call(s32[10]{0:T(128)} %stack.82.ids_ref, bf16[256,512]{1,0:T(8,128)(2,1)} %copy-done.8, bf16[256,512]{1,0:T(8,128)(2,1)} %copy-done.27, bf16[1024,256]{1,0:T(8,128)(2,1)} %refs_0_.1, bf16[1584,256]{1,0:T(8,128)(2,1)} %get-tuple-element.160.refs_1_, ...), custom_call_target="tpu_custom_call" | custom-call | flops 1073741824 | bytes 6291456 | tf_op jit(solution)/shard_map/project_rows/pallas_call | solution.py:363
  131.4 1.5 collective-permute-start.21
  135.2 2.0 collective-permute-start.20
  137.2 4.5 %norm_rows.1 = (f32[256,1024]{1,0:T(8,128)}, bf16[256,1024]{1,0:T(8,128)(2,1)}, bf16[256,1024]{1,0:T(8,128)(2,1)}) custom-call(s32[1]{0:T(128)} %bitcast.ids_ref, f32[256,2048]{1,0:T(8,128)} %project_rows.1.mine_ref, f32[256,2048]{1,0:T(8,128)} %collective-permute-done.14.theirs_ref, bf16[256,2048]{1,0:T(8,128)(2,1)} %latent_ref.1, f32[1,2048]{1,0:T(1,128)} %bitcast.54), custom_call_target="tpu_custom_call" | custom-call | flops 3145728 | bytes 6815744 | tf_op jit(solution)/shard_map/norm_rows/pallas_call | solution.py:397
  141.7 5.4 %collective-permute-start.15 = (bf16[256,1024]{1,0:T(8,128)(2,1)}, bf16[256,1024]{1,0:T(8,128)(2,1)S(1)}, u32[]{:S(2)}, u32[]{:S(2)}) collective-permute-start(bf16[256,1024]{1,0:T(8,128)(2,1)} %get-tuple-element.118.refs_0_), channel_id=1, source_target_pairs={{0,4},{2,6},{4,8},{6,10},{8,12},{10,14},{1,5},{3,7},{5,9},{7,11},{... | collective-permute-start | bytes 1572872 | tf_op jit(solution)/shard_map/ppermute | solution.py:618
  148.4 1.8 collective-permute-start.19
  153.7 5.3 %collective-permute-done.15 = bf16[256,1024]{1,0:T(8,128)(2,1)S(1)} collective-permute-done((bf16[256,1024]{1,0:T(8,128)(2,1)}, bf16[256,1024]{1,0:T(8,128)(2,1)S(1)}, u32[]{:S(2)}, u32[]{:S(2)}) %collective-permute-start.15) | collective-permute-done | bytes 524320 | tf_op jit(solution)/shard_map/ppermute | solution.py:618
  159.5 3.8 %collective-permute-done.16 = bf16[256,1024]{1,0:T(8,128)(2,1)S(1)} collective-permute-done((bf16[256,1024]{1,0:T(8,128)(2,1)}, bf16[256,1024]{1,0:T(8,128)(2,1)S(1)}, u32[]{:S(2)}, u32[]{:S(2)}) %collective-permute-start.16) | collective-permute-done | bytes 524320 | tf_op jit(solution)/shard_map/ppermute | solution.py:618
  166.1 1.6 collective-permute-start.25
  168.5 7.5 %collective-permute-done.24.refs_15_.refs_13_.refs_9_ = bf16[256,1024]{1,0:T(8,128)(2,1)S(1)} collective-permute-done((bf16[256,1024]{1,0:T(8,128)(2,1)S(1)}, bf16[256,1024]{1,0:T(8,128)(2,1)S(1)}, u32[]{:S(2)}, u32[]{:S(2)}) %collective-permute-start.24) | collective-permute-done | bytes 524320 | tf_op jit(solution)/shard_map/ppermute | solution.py:608
  177.6 3.6 %collective-permute-done.18 = bf16[256,1024]{1,0:T(8,128)(2,1)S(1)} collective-permute-done((bf16[256,1024]{1,0:T(8,128)(2,1)S(1)}, bf16[256,1024]{1,0:T(8,128)(2,1)S(1)}, u32[]{:S(2)}, u32[]{:S(2)}) %collective-permute-start.18) | collective-permute-done | bytes 524320 | tf_op jit(solution)/shard_map/ppermute | solution.py:618
  182.6 1.4 collective-permute-start.26
  184.0 1.5 collective-permute-start.27
  185.5 2.1 fusion.1.refs_0_
  187.6 1.5 collective-permute-start.31
  193.4 8.2 %latent_keys_values.3.refs_0_.refs_2_.refs_3_ = bf16[1024,1024]{1,0:T(8,128)(2,1)S(1)} custom-call(s32[9]{0:T(128)S(1)} %stack.92.ids_ref, bf16[256,1024]{1,0:T(8,128)(2,1)S(1)} %copy-done.9, bf16[256,1024]{1,0:T(8,128)(2,1)} %collective-permute-done.19.refs_1_, bf16[256,1024]{1,0:T(8,128)(2,1)} %broadcast_select_fusion.3.refs_2_, ...), custom_call_target="tpu_custom_call" | custom-call | flops 4294967296 | bytes 4194304 | tf_op jit(solution)/shard_map/latent_keys_values/pallas_call | solution.py:460
  204.1 1.6 collective-permute-start.32
  206.0 6.2 %latent_keys_values.4.refs_1_.refs_3_.refs_4_ = bf16[768,1024]{1,0:T(8,128)(2,1)S(1)} custom-call(s32[9]{0:T(128)S(1)} %stack.92.ids_ref, bf16[256,1024]{1,0:T(8,128)(2,1)} %fusion.1.refs_0_, bf16[256,1024]{1,0:T(8,128)(2,1)} %collective-permute-done.31.refs_1_, bf16[256,1024]{1,0:T(8,128)(2,1)S(1)} %select_select_fusion.1.refs_2_, ...), custom_call_target="tpu_custom_call" | custom-call | flops 3221225472 | bytes 4194304 | tf_op jit(solution)/shard_map/latent_keys_values/pallas_call | solution.py:460
  213.3 7.4 %decode_rows.3 = (f32[512,512]{1,0:T(8,128)}, f32[512,256]{1,0:T(8,128)}) custom-call(bf16[512,512]{1,0:T(8,128)(2,1)} %collective-permute-done.8.q_ref, bf16[1024,1024]{1,0:T(8,128)(2,1)} %copy-done.12, bf16[768,1024]{1,0:T(8,128)(2,1)} %copy-done.11, bf16[1024,1024]{1,0:T(8,128)(2,1)} %copy-done.12, bf16[768,1024]{1,0:T(8,128)(2,1)} %copy-done.11), custom_call_target="tpu_custom_call" | custom-call | flops 7516192768 | bytes 5242880 | tf_op jit(solution)/shard_map/decode_rows/pallas_call | solution.py:546
  220.9 2.1 collective-permute-done.36.refs_1_
  225.1 3.7 %latent_keys_values.5.refs_2_.refs_5_.refs_0_.refs_1_ = bf16[256,1024]{1,0:T(8,128)(2,1)S(1)} custom-call(s32[9]{0:T(128)S(1)} %stack.92.ids_ref, bf16[256,1024]{1,0:T(8,128)(2,1)} %collective-permute-done.32.refs_0_, bf16[256,1024]{1,0:T(8,128)(2,1)} %collective-permute-done.36.refs_1_, bf16[256,1024]{1,0:T(8,128)(2,1)S(1)} %get-tuple-element.130.refs_8_.refs_6_.refs_2_, ...), custom_call_target="tpu_custom_call" | custom-call | flops 1073741824 | bytes 4194304 | tf_op jit(solution)/shard_map/latent_keys_values/pallas_call | solution.py:460
  229.6 3.4 %decode_rows.5 = bf16[512,512]{1,0:T(8,128)(2,1)} custom-call(bf16[512,512]{1,0:T(8,128)(2,1)} %collective-permute-done.8.q_ref, bf16[256,1024]{1,0:T(8,128)(2,1)} %copy-done.7, bf16[256,1024]{1,0:T(8,128)(2,1)} %copy-done.7, f32[512,512]{1,0:T(8,128)} %get-tuple-element.144.refs_2_, f32[512,256]{1,0:T(8,128)} %get-tuple-element.145.refs_3_), custom_call_target="tpu_custom_call" | custom-call | flops 1073741824 | bytes 2097152 | tf_op jit(solution)/shard_map/decode_rows/pallas_call | solution.py:546
  233.0 1.5 collective-permute-start.37
  234.5 8.4 %decode_rows.4 = f32[512,512]{1,0:T(8,128)} custom-call(bf16[512,512]{1,0:T(8,128)(2,1)} %get-tuple-element.152.q_ref, bf16[1024,1024]{1,0:T(8,128)(2,1)} %copy-done.12, bf16[768,1024]{1,0:T(8,128)(2,1)} %copy-done.11, bf16[256,1024]{1,0:T(8,128)(2,1)} %copy-done.7, bf16[1024,1024]{1,0:T(8,128)(2,1)} %copy-done.12, bf16[768,1024]{1,0:T(8,128)(2,1)} %copy-done.11, ...), custom_call_target="tpu_custom_call" | custom-call | flops 8589934592 | bytes 5767168 | tf_op jit(solution)/shard_map/decode_rows/pallas_call | solution.py:546
  242.9 4.3 %collective-permute-done.37 = bf16[512,512]{1,0:T(8,128)(2,1)S(1)} collective-permute-done((bf16[512,512]{1,0:T(8,128)(2,1)}, bf16[512,512]{1,0:T(8,128)(2,1)S(1)}, u32[]{:S(2)}, u32[]{:S(2)}) %collective-permute-start.37) | collective-permute-done | bytes 524320 | tf_op jit(solution)/shard_map/ppermute | solution.py:778
  247.3 1.6 fusion
  (151 shorter events, 42.9 us)
Async XLA Ops:
  0.6 59.5 %copy-start = (bf16[3,1024]{1,0:T(4,128)(2,1)S(1)}, bf16[3,1024]{1,0:T(4,128)(2,1)}, u32[]{:S(2)}) copy-start(bf16[3,1024]{1,0:T(4,128)(2,1)} %param.25) | copy-start | bytes 18436
  2.7 10.2 %copy-start.30 = (f32[3,8]{1,0:T(4,128)S(1)}, f32[3,8]{1,0:T(4,128)}, u32[]{:S(2)}) copy-start(f32[3,8]{1,0:T(4,128)} %param.26) | copy-start | bytes 292
  2.7 10.9 %copy-start.23 = (bf16[256,1024]{1,0:T(8,128)(2,1)S(1)}, bf16[256,1024]{1,0:T(8,128)(2,1)}, u32[]{:S(2)}) copy-start(bf16[256,1024]{1,0:T(8,128)(2,1)} %param.22) | copy-start | bytes 1572868
  2.8 10.9 %copy-start.24 = (bf16[256,1024]{1,0:T(8,128)(2,1)S(1)}, bf16[256,1024]{1,0:T(8,128)(2,1)}, u32[]{:S(2)}) copy-start(bf16[256,1024]{1,0:T(8,128)(2,1)} %param.21) | copy-start | bytes 1572868
  2.9 32.1 %collective-permute-start = (bf16[528,1024]{1,0:T(8,128)(2,1)S(1)}, bf16[528,1024]{1,0:T(8,128)(2,1)}, u32[]{:S(2)}, u32[]{:S(2)}) collective-permute-start(bf16[528,1024]{1,0:T(8,128)(2,1)S(1)} %pad_maximum_fusion), channel_id=1, source_target_pairs={{0,2},{2,0},{4,6},{6,4},{8,10},{10,8},{12,14},{14,12},{1,3},{3,1},... | collective-permute-start | bytes 3244040 | tf_op jit(solution)/shard_map/ppermute | solution.py:611
  8.4 10.9 %collective-permute-start.1 = (bf16[528,256]{1,0:T(8,128)(2,1)}, bf16[528,256]{1,0:T(8,128)(2,1)}, u32[]{:S(2)}, u32[]{:S(2)}) collective-permute-start(bf16[528,256]{1,0:T(8,128)(2,1)} %pad_maximum_fusion.3), channel_id=1, source_target_pairs={{4,0},{6,2},{8,4},{10,6},{12,8},{14,10},{0,12},{2,14},{5,1},{7,3},... | collective-permute-start | bytes 811016 | tf_op jit(solution)/shard_map/ppermute | solution.py:614
  12.0 23.0 %collective-permute-start.2 = (bf16[528,256]{1,0:T(8,128)(2,1)}, bf16[528,256]{1,0:T(8,128)(2,1)}, u32[]{:S(2)}, u32[]{:S(2)}) collective-permute-start(bf16[528,256]{1,0:T(8,128)(2,1)} %pad_maximum_fusion.3), channel_id=1, source_target_pairs={{8,0},{10,2},{12,4},{14,6},{0,8},{2,10},{4,12},{6,14},{9,1},{11,3}... | collective-permute-start | bytes 811016 | tf_op jit(solution)/shard_map/ppermute | solution.py:614
  12.0 23.0 %collective-permute-start.3 = (bf16[528,256]{1,0:T(8,128)(2,1)}, bf16[528,256]{1,0:T(8,128)(2,1)S(1)}, u32[]{:S(2)}, u32[]{:S(2)}) collective-permute-start(bf16[528,256]{1,0:T(8,128)(2,1)} %pad_maximum_fusion.3), channel_id=1, source_target_pairs={{12,0},{14,2},{0,4},{2,6},{4,8},{6,10},{8,12},{10,14},{13,1},{15,3... | collective-permute-start | bytes 811016 | tf_op jit(solution)/shard_map/ppermute | solution.py:614
  35.0 15.0 %copy-start.25 = (bf16[528,256]{1,0:T(8,128)(2,1)}, bf16[528,256]{1,0:T(8,128)(2,1)S(1)}, u32[]{:S(2)}) copy-start(bf16[528,256]{1,0:T(8,128)(2,1)S(1)} %collective-permute-done.3) | copy-start | bytes 811012
  35.0 15.0 %collective-permute-start.4 = (bf16[256,1024]{1,0:T(8,128)(2,1)S(1)}, bf16[256,1024]{1,0:T(8,128)(2,1)S(1)}, u32[]{:S(2)}, u32[]{:S(2)}) collective-permute-start(bf16[256,1024]{1,0:T(8,128)(2,1)S(1)} %pad_maximum_fusion.1), channel_id=1, source_target_pairs={{0,2},{2,0},{4,6},{6,4},{8,10},{10,8},{12,14},{14,12},{1,3},{3,1},... | collective-permute-start | bytes 1572872 | tf_op jit(solution)/shard_map/ppermute | solution.py:611
  50.0 57.8 %all-to-all-start = ((bf16[4,528,512]{2,1,0:T(8,128)(2,1)}), bf16[4,528,512]{2,1,0:T(8,128)(2,1)S(1)}, u32[]{:S(2)}, u32[]{:S(2)}) async-start(bf16[4,528,512]{2,1,0:T(8,128)(2,1)} %bitcast.52), calls=%async_computation | async-start | bytes 4325376 | tf_op jit(solution)/shard_map/all_to_all | solution.py:672
  58.6 30.3 %collective-permute-start.5 = (bf16[2624,256]{1,0:T(8,128)(2,1)}, bf16[2624,256]{1,0:T(8,128)(2,1)S(1)}, u32[]{:S(2)}, u32[]{:S(2)}) collective-permute-start(bf16[2624,256]{1,0:T(8,128)(2,1)} %get-tuple-element.161), channel_id=1, source_target_pairs={{0,2},{2,0},{4,6},{6,4},{8,10},{10,8},{12,14},{14,12},{1,3},{3,1},... | collective-permute-start | bytes 4030472 | tf_op jit(solution)/shard_map/ppermute | solution.py:611
  60.6 33.4 %copy-start.22 = (bf16[256,512]{1,0:T(8,128)(2,1)S(1)}, bf16[256,512]{1,0:T(8,128)(2,1)}, u32[]{:S(2)}) copy-start(bf16[256,512]{1,0:T(8,128)(2,1)} %get-tuple-element.158) | copy-start | bytes 786436
  60.6 43.4 %collective-permute-start.6 = (bf16[1584,256]{1,0:T(8,128)(2,1)}, bf16[1584,256]{1,0:T(8,128)(2,1)}, u32[]{:S(2)}, u32[]{:S(2)}) collective-permute-start(bf16[1584,256]{1,0:T(8,128)(2,1)} %get-tuple-element.160.refs_1_), channel_id=1, source_target_pairs={{0,16},{16,0},{1,17},{17,1},{2,18},{18,2},{3,19},{19,3},{4,20},{20... | collective-permute-start | bytes 2433032 | tf_op jit(solution)/shard_map/ppermute | solution.py:608
  89.8 18.0 %collective-permute-start.7 = (bf16[1584,256]{1,0:T(8,128)(2,1)}, bf16[1584,256]{1,0:T(8,128)(2,1)}, u32[]{:S(2)}, u32[]{:S(2)}) collective-permute-start(bf16[1584,256]{1,0:T(8,128)(2,1)} %slice.62), channel_id=1, source_target_pairs={{0,16},{16,0},{1,17},{17,1},{2,18},{18,2},{3,19},{19,3},{4,20},{20... | collective-permute-start | bytes 2433032 | tf_op jit(solution)/shard_map/ppermute | solution.py:608
  92.4 11.6 %collective-permute-start.8 = (bf16[512,512]{1,0:T(8,128)(2,1)}, bf16[512,512]{1,0:T(8,128)(2,1)}, u32[]{:S(2)}, u32[]{:S(2)}) collective-permute-start(bf16[512,512]{1,0:T(8,128)(2,1)} %get-tuple-element.153), channel_id=1, source_target_pairs={{0,2},{2,0},{4,6},{6,4},{8,10},{10,8},{12,14},{14,12},{1,3},{3,1},... | collective-permute-start | bytes 1572872 | tf_op jit(solution)/shard_map/ppermute | solution.py:611
  95.9 14.5 %collective-permute-start.10 = (bf16[256,1024]{1,0:T(8,128)(2,1)}, bf16[256,1024]{1,0:T(8,128)(2,1)}, u32[]{:S(2)}, u32[]{:S(2)}) collective-permute-start(bf16[256,1024]{1,0:T(8,128)(2,1)} %get-tuple-element.155), channel_id=1, source_target_pairs={{0,4},{2,6},{4,8},{6,10},{8,12},{10,14},{1,5},{3,7},{5,9},{7,11},{... | collective-permute-start | bytes 1572872 | tf_op jit(solution)/shard_map/ppermute | solution.py:618
  100.4 13.8 %collective-permute-start.11 = (bf16[256,1024]{1,0:T(8,128)(2,1)}, bf16[256,1024]{1,0:T(8,128)(2,1)}, u32[]{:S(2)}, u32[]{:S(2)}) collective-permute-start(bf16[256,1024]{1,0:T(8,128)(2,1)} %get-tuple-element.155), channel_id=1, source_target_pairs={{12,8},{14,10},{8,4},{10,6},{4,0},{6,2},{13,9},{15,11},{9,5},{11,7... | collective-permute-start | bytes 1572872 | tf_op jit(solution)/shard_map/ppermute | solution.py:618
  114.1 15.0 %collective-permute-start.12 = (bf16[256,1024]{1,0:T(8,128)(2,1)}, bf16[256,1024]{1,0:T(8,128)(2,1)S(1)}, u32[]{:S(2)}, u32[]{:S(2)}) collective-permute-start(bf16[256,1024]{1,0:T(8,128)(2,1)} %collective-permute-done.10), channel_id=1, source_target_pairs={{4,8},{6,10},{8,12},{10,14},{5,9},{7,11},{9,13},{11,15},{20,24},{2... | collective-permute-start | bytes 1572872 | tf_op jit(solution)/shard_map/ppermute | solution.py:618
  114.8 14.3 %collective-permute-start.13 = (bf16[256,1024]{1,0:T(8,128)(2,1)}, bf16[256,1024]{1,0:T(8,128)(2,1)S(1)}, u32[]{:S(2)}, u32[]{:S(2)}) collective-permute-start(bf16[256,1024]{1,0:T(8,128)(2,1)} %collective-permute-done.11), channel_id=1, source_target_pairs={{8,4},{10,6},{4,0},{6,2},{9,5},{11,7},{5,1},{7,3},{24,20},{26,22},... | collective-permute-start | bytes 1572872 | tf_op jit(solution)/shard_map/ppermute | solution.py:618
  116.1 6.4 %collective-permute-start.9 = (bf16[256,512]{1,0:T(8,128)(2,1)S(1)}, bf16[256,512]{1,0:T(8,128)(2,1)S(1)}, u32[]{:S(2)}, u32[]{:S(2)}) collective-permute-start(bf16[256,512]{1,0:T(8,128)(2,1)S(1)} %get-tuple-element.85), channel_id=1, source_target_pairs={{0,2},{2,0},{4,6},{6,4},{8,10},{10,8},{12,14},{14,12},{1,3},{3,1},... | collective-permute-start | bytes 786440 | tf_op jit(solution)/shard_map/ppermute | solution.py:611
  123.3 11.8 %copy-start.31 = (s32[3]{0:T(128)S(1)}, s32[3]{0:T(128)}, u32[]{:S(2)}) copy-start(s32[3]{0:T(128)} %param.27) | copy-start | bytes 40
  129.1 8.1 %collective-permute-start.14 = (f32[256,2048]{1,0:T(8,128)}, f32[256,2048]{1,0:T(8,128)}, u32[]{:S(2)}, u32[]{:S(2)}) collective-permute-start(f32[256,2048]{1,0:T(8,128)} %project_rows.1.mine_ref), channel_id=1, source_target_pairs={{0,1},{1,0},{2,3},{3,2},{4,5},{5,4},{6,7},{7,6},{8,9},{9,8},{10,11... | collective-permute-start | bytes 6291464 | tf_op jit(solution)/shard_map/ppermute | solution.py:713
  131.4 17.0 %collective-permute-start.21 = (bf16[256,1024]{1,0:T(8,128)(2,1)S(1)}, bf16[256,1024]{1,0:T(8,128)(2,1)}, u32[]{:S(2)}, u32[]{:S(2)}) collective-permute-start(bf16[256,1024]{1,0:T(8,128)(2,1)S(1)} %collective-permute-done.12), channel_id=1, source_target_pairs={{8,12},{10,14},{9,13},{11,15},{24,28},{26,30},{25,29},{27,31}} | collective-permute-start | bytes 1572872 | tf_op jit(solution)/shard_map/ppermute | solution.py:618
  132.9 17.3 %collective-permute-start.22 = (bf16[256,1024]{1,0:T(8,128)(2,1)S(1)}, bf16[256,1024]{1,0:T(8,128)(2,1)}, u32[]{:S(2)}, u32[]{:S(2)}) collective-permute-start(bf16[256,1024]{1,0:T(8,128)(2,1)S(1)} %collective-permute-done.13), channel_id=1, source_target_pairs={{4,0},{6,2},{5,1},{7,3},{20,16},{22,18},{21,17},{23,19}} | collective-permute-start | bytes 1572872 | tf_op jit(solution)/shard_map/ppermute | solution.py:618
  135.2 29.6 %collective-permute-start.20 = (bf16[256,1024]{1,0:T(8,128)(2,1)S(1)}, bf16[256,1024]{1,0:T(8,128)(2,1)S(1)}, u32[]{:S(2)}, u32[]{:S(2)}) collective-permute-start(bf16[256,1024]{1,0:T(8,128)(2,1)S(1)} %broadcast_select_fusion.2.refs_10_.refs_8_.refs_4_), channel_id=1, source_target_pairs={{0,16},{16,0},{1,17},{17,1},{2,18},{18,2},{3,19},{19,3},{4,20},{20... | collective-permute-start | bytes 1572872 | tf_op jit(solution)/shard_map/ppermute | solution.py:608
  141.7 17.2 %collective-permute-start.15 = (bf16[256,1024]{1,0:T(8,128)(2,1)}, bf16[256,1024]{1,0:T(8,128)(2,1)S(1)}, u32[]{:S(2)}, u32[]{:S(2)}) collective-permute-start(bf16[256,1024]{1,0:T(8,128)(2,1)} %get-tuple-element.118.refs_0_), channel_id=1, source_target_pairs={{0,4},{2,6},{4,8},{6,10},{8,12},{10,14},{1,5},{3,7},{5,9},{7,11},{... | collective-permute-start | bytes 1572872 | tf_op jit(solution)/shard_map/ppermute | solution.py:618
  147.1 16.1 %collective-permute-start.16 = (bf16[256,1024]{1,0:T(8,128)(2,1)}, bf16[256,1024]{1,0:T(8,128)(2,1)S(1)}, u32[]{:S(2)}, u32[]{:S(2)}) collective-permute-start(bf16[256,1024]{1,0:T(8,128)(2,1)} %get-tuple-element.118.refs_0_), channel_id=1, source_target_pairs={{12,8},{14,10},{8,4},{10,6},{4,0},{6,2},{13,9},{15,11},{9,5},{11,7... | collective-permute-start | bytes 1572872 | tf_op jit(solution)/shard_map/ppermute | solution.py:618
  148.4 17.7 %collective-permute-start.19 = (bf16[256,1024]{1,0:T(8,128)(2,1)}, bf16[256,1024]{1,0:T(8,128)(2,1)}, u32[]{:S(2)}, u32[]{:S(2)}) collective-permute-start(bf16[256,1024]{1,0:T(8,128)(2,1)} %get-tuple-element.118.refs_0_), channel_id=1, source_target_pairs={{0,2},{2,0},{4,6},{6,4},{8,10},{10,8},{12,14},{14,12},{1,3},{3,1},... | collective-permute-start | bytes 1572872 | tf_op jit(solution)/shard_map/ppermute | solution.py:611
  151.4 16.4 %collective-permute-start.23 = (bf16[256,1024]{1,0:T(8,128)(2,1)S(1)}, bf16[256,1024]{1,0:T(8,128)(2,1)S(1)}, u32[]{:S(2)}, u32[]{:S(2)}) collective-permute-start(bf16[256,1024]{1,0:T(8,128)(2,1)S(1)} %broadcast_select_fusion.1.refs_12_.refs_10_.refs_6_), channel_id=1, source_target_pairs={{0,16},{16,0},{1,17},{17,1},{2,18},{18,2},{3,19},{19,3},{4,20},{20... | collective-permute-start | bytes 1572872 | tf_op jit(solution)/shard_map/ppermute | solution.py:608
  158.9 17.1 %copy-start.15 = (bf16[256,1024]{1,0:T(8,128)(2,1)}, bf16[256,1024]{1,0:T(8,128)(2,1)S(1)}, u32[]{:S(2)}) copy-start(bf16[256,1024]{1,0:T(8,128)(2,1)S(1)} %collective-permute-done.15) | copy-start | bytes 1572868
  158.9 17.1 %collective-permute-start.24 = (bf16[256,1024]{1,0:T(8,128)(2,1)S(1)}, bf16[256,1024]{1,0:T(8,128)(2,1)S(1)}, u32[]{:S(2)}, u32[]{:S(2)}) collective-permute-start(bf16[256,1024]{1,0:T(8,128)(2,1)S(1)} %broadcast_select_fusion.refs_14_.refs_12_.refs_8_), channel_id=1, source_target_pairs={{0,16},{16,0},{1,17},{17,1},{2,18},{18,2},{3,19},{19,3},{4,20},{20... | collective-permute-start | bytes 1572872 | tf_op jit(solution)/shard_map/ppermute | solution.py:608
  163.3 13.6 %collective-permute-start.17 = (bf16[256,1024]{1,0:T(8,128)(2,1)S(1)}, bf16[256,1024]{1,0:T(8,128)(2,1)S(1)}, u32[]{:S(2)}, u32[]{:S(2)}) collective-permute-start(bf16[256,1024]{1,0:T(8,128)(2,1)S(1)} %collective-permute-done.15), channel_id=1, source_target_pairs={{4,8},{6,10},{8,12},{10,14},{5,9},{7,11},{9,13},{11,15},{20,24},{2... | collective-permute-start | bytes 1572872 | tf_op jit(solution)/shard_map/ppermute | solution.py:618
  164.8 16.5 %collective-permute-start.18 = (bf16[256,1024]{1,0:T(8,128)(2,1)S(1)}, bf16[256,1024]{1,0:T(8,128)(2,1)S(1)}, u32[]{:S(2)}, u32[]{:S(2)}) collective-permute-start(bf16[256,1024]{1,0:T(8,128)(2,1)S(1)} %collective-permute-done.16), channel_id=1, source_target_pairs={{8,4},{10,6},{4,0},{6,2},{9,5},{11,7},{5,1},{7,3},{24,20},{26,22},... | collective-permute-start | bytes 1572872 | tf_op jit(solution)/shard_map/ppermute | solution.py:618
  166.1 16.0 %collective-permute-start.25 = (bf16[256,1024]{1,0:T(8,128)(2,1)}, bf16[256,1024]{1,0:T(8,128)(2,1)}, u32[]{:S(2)}, u32[]{:S(2)}) collective-permute-start(bf16[256,1024]{1,0:T(8,128)(2,1)} %broadcast_select_fusion.3.refs_2_), channel_id=1, source_target_pairs={{0,2},{2,0},{4,6},{6,4},{8,10},{10,8},{12,14},{14,12},{1,3},{3,1},... | collective-permute-start | bytes 1572872 | tf_op jit(solution)/shard_map/ppermute | solution.py:611
  182.1 5.5 %collective-permute-start.28 = (bf16[256,1024]{1,0:T(8,128)(2,1)}, bf16[256,1024]{1,0:T(8,128)(2,1)}, u32[]{:S(2)}, u32[]{:S(2)}) collective-permute-start(bf16[256,1024]{1,0:T(8,128)(2,1)} %collective-permute-done.19.refs_1_), channel_id=1, source_target_pairs={{0,1},{1,0},{2,3},{3,2},{4,5},{5,4},{6,7},{7,6},{8,9},{9,8},{10,11... | collective-permute-start | bytes 1572872 | tf_op jit(solution)/shard_map/ppermute | solution.py:723
  182.1 7.1 %collective-permute-start.29 = (bf16[256,1024]{1,0:T(8,128)(2,1)}, bf16[256,1024]{1,0:T(8,128)(2,1)}, u32[]{:S(2)}, u32[]{:S(2)}) collective-permute-start(bf16[256,1024]{1,0:T(8,128)(2,1)} %broadcast_select_fusion.3.refs_2_), channel_id=1, source_target_pairs={{0,1},{1,0},{2,3},{3,2},{4,5},{5,4},{6,7},{7,6},{8,9},{9,8},{10,11... | collective-permute-start | bytes 1572872 | tf_op jit(solution)/shard_map/ppermute | solution.py:723
  182.6 6.6 %collective-permute-start.30 = (bf16[256,1024]{1,0:T(8,128)(2,1)}, bf16[256,1024]{1,0:T(8,128)(2,1)}, u32[]{:S(2)}, u32[]{:S(2)}) collective-permute-start(bf16[256,1024]{1,0:T(8,128)(2,1)} %collective-permute-done.25.refs_3_), channel_id=1, source_target_pairs={{0,1},{1,0},{2,3},{3,2},{4,5},{5,4},{6,7},{7,6},{8,9},{9,8},{10,11... | collective-permute-start | bytes 1572872 | tf_op jit(solution)/shard_map/ppermute | solution.py:723
  182.6 19.0 %collective-permute-start.26 = (bf16[256,1024]{1,0:T(8,128)(2,1)}, bf16[256,1024]{1,0:T(8,128)(2,1)}, u32[]{:S(2)}, u32[]{:S(2)}) collective-permute-start(bf16[256,1024]{1,0:T(8,128)(2,1)} %copy-done.16), channel_id=1, source_target_pairs={{8,12},{10,14},{9,13},{11,15},{24,28},{26,30},{25,29},{27,31}} | collective-permute-start | bytes 1572872 | tf_op jit(solution)/shard_map/ppermute | solution.py:618
  184.0 17.5 %collective-permute-start.27 = (bf16[256,1024]{1,0:T(8,128)(2,1)}, bf16[256,1024]{1,0:T(8,128)(2,1)}, u32[]{:S(2)}, u32[]{:S(2)}) collective-permute-start(bf16[256,1024]{1,0:T(8,128)(2,1)} %copy-done.18), channel_id=1, source_target_pairs={{4,0},{6,2},{5,1},{7,3},{20,16},{22,18},{21,17},{23,19}} | collective-permute-start | bytes 1572872 | tf_op jit(solution)/shard_map/ppermute | solution.py:618
  187.6 14.7 %collective-permute-start.31 = (bf16[256,1024]{1,0:T(8,128)(2,1)}, bf16[256,1024]{1,0:T(8,128)(2,1)}, u32[]{:S(2)}, u32[]{:S(2)}) collective-permute-start(bf16[256,1024]{1,0:T(8,128)(2,1)} %fusion.1.refs_0_), channel_id=1, source_target_pairs={{0,2},{2,0},{4,6},{6,4},{8,10},{10,8},{12,14},{14,12},{1,3},{3,1},... | collective-permute-start | bytes 1572872 | tf_op jit(solution)/shard_map/ppermute | solution.py:611
  193.4 9.4 %copy-start.19 = (bf16[256,1024]{1,0:T(8,128)(2,1)S(1)}, bf16[256,1024]{1,0:T(8,128)(2,1)}, u32[]{:S(2)}) copy-start(bf16[256,1024]{1,0:T(8,128)(2,1)} %copy-done.18) | copy-start | bytes 1572868
  202.2 3.4 %collective-permute-start.33 = (bf16[256,1024]{1,0:T(8,128)(2,1)}, bf16[256,1024]{1,0:T(8,128)(2,1)S(1)}, u32[]{:S(2)}, u32[]{:S(2)}) collective-permute-start(bf16[256,1024]{1,0:T(8,128)(2,1)} %fusion.1.refs_0_), channel_id=1, source_target_pairs={{0,1},{1,0},{2,3},{3,2},{4,5},{5,4},{6,7},{7,6},{8,9},{9,8},{10,11... | collective-permute-start | bytes 1572872 | tf_op jit(solution)/shard_map/ppermute | solution.py:723
  202.2 3.4 %collective-permute-start.34 = (bf16[256,1024]{1,0:T(8,128)(2,1)}, bf16[256,1024]{1,0:T(8,128)(2,1)S(1)}, u32[]{:S(2)}, u32[]{:S(2)}) collective-permute-start(bf16[256,1024]{1,0:T(8,128)(2,1)} %collective-permute-done.31.refs_1_), channel_id=1, source_target_pairs={{0,1},{1,0},{2,3},{3,2},{4,5},{5,4},{6,7},{7,6},{8,9},{9,8},{10,11... | collective-permute-start | bytes 1572872 | tf_op jit(solution)/shard_map/ppermute | solution.py:723
  204.0 2.0 collective-permute-start.35
  204.1 16.7 %collective-permute-start.32 = (bf16[256,1024]{1,0:T(8,128)(2,1)S(1)}, bf16[256,1024]{1,0:T(8,128)(2,1)}, u32[]{:S(2)}, u32[]{:S(2)}) collective-permute-start(bf16[256,1024]{1,0:T(8,128)(2,1)S(1)} %select_select_fusion.1.refs_2_), channel_id=1, source_target_pairs={{0,2},{2,0},{4,6},{6,4},{8,10},{10,8},{12,14},{14,12},{1,3},{3,1},... | collective-permute-start | bytes 1572872 | tf_op jit(solution)/shard_map/ppermute | solution.py:611
  220.8 2.3 collective-permute-start.36
  233.0 14.2 %collective-permute-start.37 = (bf16[512,512]{1,0:T(8,128)(2,1)}, bf16[512,512]{1,0:T(8,128)(2,1)S(1)}, u32[]{:S(2)}, u32[]{:S(2)}) collective-permute-start(bf16[512,512]{1,0:T(8,128)(2,1)} %decode_rows.5), channel_id=1, source_target_pairs={{0,2},{2,0},{4,6},{6,4},{8,10},{10,8},{12,14},{14,12},{1,3},{3,1},... | collective-permute-start | bytes 1572872 | tf_op jit(solution)/shard_map/ppermute | solution.py:778
  (23 other events, 59.0 us)

commit v17 on v16

--- a/solution.py
+++ b/solution.py
@@ -461,7 +461,7 @@
         functools.partial(latents_kernel, pieces),
         grid_spec=grid_spec,
         out_shape=jax.ShapeDtypeStruct((rows * pieces, width), jnp.bfloat16),
-        compiler_params=params(28),
+        compiler_params=params(57),
         cost_estimate=cost(2 * rows * pieces * total * width, 2 * total * width),
         name="latent_keys_values",
     )(ids, *mine, *theirs, *bands)

time: 250 us -> 253 us (1.012)
  waiting for transfers between devices: 88.8 us -> 97.3 us
  local copies, waits for them, and re-layouts: 26.3 us -> 18.3 us
  Pallas kernels: 63.9 us -> 70.4 us
    unnamed x69, local copies, waits for them, and re-layouts: 17.9 us -> 10.4 us
    pallas_call x3, Pallas kernels: 18 us -> 24.3 us  [latent_keys_values(): pl.pallas_call(functools.partial(latents_kernel, pieces), grid_spec=grid_...]
    ppermute x12, waiting for transfers between devices: 16.4 us -> 22.4 us  [hop(): lax.ppermute(v, 'pos', hop_perm(pos, step, way))]
  transfers between devices with their start and end apart: 39 -> 39, of which waited for: 15 -> 16; matrix products, arithmetic and copies ran while one was open for 9% -> 8% of each run, Pallas kernels for 23% -> 24%
where the time goes in v17:
time: 253 us
  waiting for transfers between devices  97.3 us (38%)
  Pallas kernels  70.4 us (28%)
  starting transfers between devices  53.6 us (21%)
  local copies, waits for them, and re-layouts  18.3 us (7%)
  other arithmetic  11.5 us (5%)
    ppermute x9, waiting for transfers between devices, over_near(): return lax.ppermute(value, 'pos', near)  36.1 us
    pallas_call x3, Pallas kernels, latent_keys_values(): pl.pallas_call(functools.partial(latents_kernel, pieces), grid_spec=grid_...  24.3 us
    ppermute x12, waiting for transfers between devices, hop(): lax.ppermute(v, 'pos', hop_perm(pos, step, way))  22.4 us
    ppermute x12, starting transfers between devices, hop(): lax.ppermute(v, 'pos', hop_perm(pos, step, way))  21.8 us
    ppermute x3, waiting for transfers between devices, over_far(): return lax.ppermute(value, 'pos', shift_perm(pos, k))  21.2 us
    pallas_call x3, Pallas kernels, decode(): pl.pallas_call(functools.partial(decode_kernel, len(keys_values), first,...  19.3 us
    ppermute x9, starting transfers between devices, over_near(): return lax.ppermute(value, 'pos', near)  15.2 us
    pallas_call x1, Pallas kernels, encode(): pl.pallas_call(encode_kernel, grid_spec=grid_spec, out_shape=jax.ShapeDty...  14.4 us
  transfers between devices with their start and end apart: 39, of which 16 were waited for; matrix products, arithmetic and copies ran while one was open for 8% of the time, Pallas kernels for 24%

profile of v17, /device:TPU:0, one launch (start us, length us, event | category | flops | bytes accessed | tf_op | source)
XLA Modules:
  0.0 252.6 jit_solution(5877522437386673540)
XLA Ops:
  1.4 1.3 constant_dynamic-slice_fusion.8
  2.9 3.0 %collective-permute-start = (bf16[528,1024]{1,0:T(8,128)(2,1)S(1)}, bf16[528,1024]{1,0:T(8,128)(2,1)}, u32[]{:S(2)}, u32[]{:S(2)}) collective-permute-start(bf16[528,1024]{1,0:T(8,128)(2,1)S(1)} %pad_maximum_fusion), channel_id=1, source_target_pairs={{0,2},{2,0},{4,6},{6,4},{8,10},{10,8},{12,14},{14,12},{1,3},{3,1},... | collective-permute-start | bytes 3244040 | tf_op jit(solution)/shard_map/ppermute | solution.py:611
  8.4 3.6 %collective-permute-start.1 = (bf16[528,256]{1,0:T(8,128)(2,1)}, bf16[528,256]{1,0:T(8,128)(2,1)}, u32[]{:S(2)}, u32[]{:S(2)}) collective-permute-start(bf16[528,256]{1,0:T(8,128)(2,1)} %pad_maximum_fusion.3), channel_id=1, source_target_pairs={{4,0},{6,2},{8,4},{10,6},{12,8},{14,10},{0,12},{2,14},{5,1},{7,3},... | collective-permute-start | bytes 811016 | tf_op jit(solution)/shard_map/ppermute | solution.py:614
  13.8 5.4 %collective-permute-done.1 = bf16[528,256]{1,0:T(8,128)(2,1)} collective-permute-done((bf16[528,256]{1,0:T(8,128)(2,1)}, bf16[528,256]{1,0:T(8,128)(2,1)}, u32[]{:S(2)}, u32[]{:S(2)}) %collective-permute-start.1) | collective-permute-done | bytes 270368 | tf_op jit(solution)/shard_map/ppermute | solution.py:614
  19.2 15.8 %collective-permute-done.2 = bf16[528,256]{1,0:T(8,128)(2,1)} collective-permute-done((bf16[528,256]{1,0:T(8,128)(2,1)}, bf16[528,256]{1,0:T(8,128)(2,1)}, u32[]{:S(2)}, u32[]{:S(2)}) %collective-permute-start.2) | collective-permute-done | bytes 270368 | tf_op jit(solution)/shard_map/ppermute | solution.py:614
  35.5 14.4 %encode_rows.1 = bf16[2112,512]{1,0:T(8,128)(2,1)} custom-call(s32[1]{0:T(128)} %bitcast.9.ids_ref, bf16[2048,1024]{1,0:T(8,128)(2,1)} %q_ref.1, bf16[512,1024]{1,0:T(8,128)(2,1)} %k_ref.1, bf16[512,1024]{1,0:T(8,128)(2,1)} %v_ref.1, bf16[16,1024]{1,0:T(8,128)(2,1)} %copy-done.24, bf16[528,1024]{1,0:T(8,128)(2,1)} %collective-permute-done.near_ref, ...), custom_call_target="tpu_custom_call" | custom-call | flops 8589934592 | bytes 2097152 | tf_op jit(solution)/shard_map/encode_rows/pallas_call | solution.py:262
  50.0 4.0 %all-to-all-start = ((bf16[4,528,512]{2,1,0:T(8,128)(2,1)}), bf16[4,528,512]{2,1,0:T(8,128)(2,1)S(1)}, u32[]{:S(2)}, u32[]{:S(2)}) async-start(bf16[4,528,512]{2,1,0:T(8,128)(2,1)} %bitcast.52), calls=%async_computation | async-start | bytes 4325376 | tf_op jit(solution)/shard_map/all_to_all | solution.py:672
  53.9 1.9 constant_dynamic-update-slice_fusion.7
  55.8 1.8 constant_dynamic-update-slice_fusion.6
  58.4 1.5 collective-permute-start.5
  60.4 1.6 collective-permute-start.6
  62.0 26.7 %collective-permute-done.5.refs_3_ = bf16[2624,256]{1,0:T(8,128)(2,1)S(1)} collective-permute-done((bf16[2624,256]{1,0:T(8,128)(2,1)}, bf16[2624,256]{1,0:T(8,128)(2,1)S(1)}, u32[]{:S(2)}, u32[]{:S(2)}) %collective-permute-start.5) | collective-permute-done | bytes 1343520 | tf_op jit(solution)/shard_map/ppermute | solution.py:611
  89.7 1.5 collective-permute-start.7
  92.3 1.5 collective-permute-start.8
  95.0 3.7 %collective-permute-start.10 = (bf16[256,1024]{1,0:T(8,128)(2,1)}, bf16[256,1024]{1,0:T(8,128)(2,1)S(1)}, u32[]{:S(2)}, u32[]{:S(2)}) collective-permute-start(bf16[256,1024]{1,0:T(8,128)(2,1)} %get-tuple-element.155), channel_id=1, source_target_pairs={{0,4},{2,6},{4,8},{6,10},{8,12},{10,14},{1,5},{3,7},{5,9},{7,11},{... | collective-permute-start | bytes 1572872 | tf_op jit(solution)/shard_map/ppermute | solution.py:618
  98.6 1.3 collective-permute-start.11
  99.9 3.9 %collective-permute-done.8.q_ref = bf16[512,512]{1,0:T(8,128)(2,1)} collective-permute-done((bf16[512,512]{1,0:T(8,128)(2,1)}, bf16[512,512]{1,0:T(8,128)(2,1)}, u32[]{:S(2)}, u32[]{:S(2)}) %collective-permute-start.8) | collective-permute-done | bytes 524320 | tf_op jit(solution)/shard_map/ppermute | solution.py:611
  103.9 3.8 %collective-permute-done.7.refs_4_ = bf16[1584,256]{1,0:T(8,128)(2,1)} collective-permute-done((bf16[1584,256]{1,0:T(8,128)(2,1)}, bf16[1584,256]{1,0:T(8,128)(2,1)}, u32[]{:S(2)}, u32[]{:S(2)}) %collective-permute-start.7) | collective-permute-done | bytes 811040 | tf_op jit(solution)/shard_map/ppermute | solution.py:608
  107.7 1.9 merge_rows.1
  110.3 3.5 %collective-permute-done.11 = bf16[256,1024]{1,0:T(8,128)(2,1)S(1)} collective-permute-done((bf16[256,1024]{1,0:T(8,128)(2,1)}, bf16[256,1024]{1,0:T(8,128)(2,1)S(1)}, u32[]{:S(2)}, u32[]{:S(2)}) %collective-permute-start.11) | collective-permute-done | bytes 524320 | tf_op jit(solution)/shard_map/ppermute | solution.py:618
  113.9 1.4 collective-permute-start.12
  116.6 1.6 collective-permute-start.9
  118.8 5.0 %collective-permute-done.9.near_ref = bf16[256,512]{1,0:T(8,128)(2,1)S(1)} collective-permute-done((bf16[256,512]{1,0:T(8,128)(2,1)S(1)}, bf16[256,512]{1,0:T(8,128)(2,1)S(1)}, u32[]{:S(2)}, u32[]{:S(2)}) %collective-permute-start.9) | collective-permute-done | bytes 262176 | tf_op jit(solution)/shard_map/ppermute | solution.py:611
  124.5 5.8 %project_rows.1.mine_ref = f32[256,2048]{1,0:T(8,128)} custom-call(s32[10]{0:T(128)} %stack.82.ids_ref, bf16[256,512]{1,0:T(8,128)(2,1)} %copy-done.1, bf16[256,512]{1,0:T(8,128)(2,1)} %copy-done.23, bf16[1024,256]{1,0:T(8,128)(2,1)} %refs_0_.1, bf16[1584,256]{1,0:T(8,128)(2,1)} %get-tuple-element.160.refs_1_, ...), custom_call_target="tpu_custom_call" | custom-call | flops 1073741824 | bytes 6291456 | tf_op jit(solution)/shard_map/project_rows/pallas_call | solution.py:363
  132.7 1.5 collective-permute-start.21
  137.5 2.0 collective-permute-start.20
  139.5 1.3 copy-done.8
  140.8 4.6 %norm_rows.1 = (f32[256,1024]{1,0:T(8,128)}, bf16[256,1024]{1,0:T(8,128)(2,1)}, bf16[256,1024]{1,0:T(8,128)(2,1)}) custom-call(s32[1]{0:T(128)} %bitcast.ids_ref, f32[256,2048]{1,0:T(8,128)} %project_rows.1.mine_ref, f32[256,2048]{1,0:T(8,128)} %copy-done.8, bf16[256,2048]{1,0:T(8,128)(2,1)} %latent_ref.1, f32[1,2048]{1,0:T(1,128)} %bitcast.54), custom_call_target="tpu_custom_call" | custom-call | flops 3145728 | bytes 6815744 | tf_op jit(solution)/shard_map/norm_rows/pallas_call | solution.py:397
  145.5 5.4 %collective-permute-start.15 = (bf16[256,1024]{1,0:T(8,128)(2,1)}, bf16[256,1024]{1,0:T(8,128)(2,1)S(1)}, u32[]{:S(2)}, u32[]{:S(2)}) collective-permute-start(bf16[256,1024]{1,0:T(8,128)(2,1)} %get-tuple-element.118.refs_0_), channel_id=1, source_target_pairs={{0,4},{2,6},{4,8},{6,10},{8,12},{10,14},{1,5},{3,7},{5,9},{7,11},{... | collective-permute-start | bytes 1572872 | tf_op jit(solution)/shard_map/ppermute | solution.py:618
  152.2 1.8 collective-permute-start.19
  155.4 7.0 %collective-permute-done.15 = bf16[256,1024]{1,0:T(8,128)(2,1)S(1)} collective-permute-done((bf16[256,1024]{1,0:T(8,128)(2,1)}, bf16[256,1024]{1,0:T(8,128)(2,1)S(1)}, u32[]{:S(2)}, u32[]{:S(2)}) %collective-permute-start.15) | collective-permute-done | bytes 524320 | tf_op jit(solution)/shard_map/ppermute | solution.py:618
  162.8 4.1 %collective-permute-done.16 = bf16[256,1024]{1,0:T(8,128)(2,1)S(1)} collective-permute-done((bf16[256,1024]{1,0:T(8,128)(2,1)}, bf16[256,1024]{1,0:T(8,128)(2,1)S(1)}, u32[]{:S(2)}, u32[]{:S(2)}) %collective-permute-start.16) | collective-permute-done | bytes 524320 | tf_op jit(solution)/shard_map/ppermute | solution.py:618
  169.8 1.8 collective-permute-start.25
  171.6 7.0 %collective-permute-done.24.refs_15_.refs_13_.refs_9_ = bf16[256,1024]{1,0:T(8,128)(2,1)S(1)} collective-permute-done((bf16[256,1024]{1,0:T(8,128)(2,1)S(1)}, bf16[256,1024]{1,0:T(8,128)(2,1)S(1)}, u32[]{:S(2)}, u32[]{:S(2)}) %collective-permute-start.24) | collective-permute-done | bytes 524320 | tf_op jit(solution)/shard_map/ppermute | solution.py:608
  178.6 6.4 %collective-permute-done.18 = bf16[256,1024]{1,0:T(8,128)(2,1)S(1)} collective-permute-done((bf16[256,1024]{1,0:T(8,128)(2,1)S(1)}, bf16[256,1024]{1,0:T(8,128)(2,1)S(1)}, u32[]{:S(2)}, u32[]{:S(2)}) %collective-permute-start.18) | collective-permute-done | bytes 524320 | tf_op jit(solution)/shard_map/ppermute | solution.py:618
  185.6 1.4 collective-permute-start.26
  189.3 1.7 collective-permute-start.31
  191.6 10.3 %latent_keys_values.3.refs_0_.refs_2_.refs_3_ = bf16[1024,1024]{1,0:T(8,128)(2,1)} custom-call(s32[9]{0:T(128)} %stack.92.ids_ref, bf16[256,1024]{1,0:T(8,128)(2,1)} %get-tuple-element.118.refs_0_, bf16[256,1024]{1,0:T(8,128)(2,1)} %collective-permute-done.19.refs_1_, bf16[256,1024]{1,0:T(8,128)(2,1)} %broadcast_select_fusion.3.refs_2_, ...), custom_call_target="tpu_custom_call" | custom-call | flops 4294967296 | bytes 4194304 | tf_op jit(solution)/shard_map/latent_keys_values/pallas_call | solution.py:460
  202.0 1.4 collective-permute-done.27
  205.6 1.8 collective-permute-start.32
  209.2 8.6 %latent_keys_values.4.refs_1_.refs_3_.refs_4_ = bf16[768,1024]{1,0:T(8,128)(2,1)} custom-call(s32[9]{0:T(128)} %stack.92.ids_ref, bf16[256,1024]{1,0:T(8,128)(2,1)} %fusion.1.refs_0_, bf16[256,1024]{1,0:T(8,128)(2,1)} %copy-done.28, bf16[256,1024]{1,0:T(8,128)(2,1)} %copy-done.22, bf16[256,1024]{1,0:T(8,128)(2,1)} %copy-done.29, ...), custom_call_target="tpu_custom_call" | custom-call | flops 3221225472 | bytes 4194304 | tf_op jit(solution)/shard_map/latent_keys_values/pallas_call | solution.py:460
  217.8 7.4 %decode_rows.3 = (f32[512,512]{1,0:T(8,128)}, f32[512,256]{1,0:T(8,128)}) custom-call(bf16[512,512]{1,0:T(8,128)(2,1)} %collective-permute-done.8.q_ref, bf16[1024,1024]{1,0:T(8,128)(2,1)} %latent_keys_values.3.refs_0_.refs_2_.refs_3_, bf16[768,1024]{1,0:T(8,128)(2,1)} %latent_keys_values.4.refs_1_.refs_3_.refs_4_, ...), custom_call_target="tpu_custom_call" | custom-call | flops 7516192768 | bytes 5242880 | tf_op jit(solution)/shard_map/decode_rows/pallas_call | solution.py:546
  225.4 1.8 collective-permute-done.36.refs_1_
  228.0 5.3 %latent_keys_values.5.refs_2_.refs_5_.refs_0_.refs_1_ = bf16[256,1024]{1,0:T(8,128)(2,1)} custom-call(s32[9]{0:T(128)} %stack.92.ids_ref, bf16[256,1024]{1,0:T(8,128)(2,1)} %copy-done.14, bf16[256,1024]{1,0:T(8,128)(2,1)} %copy-done.15, bf16[256,1024]{1,0:T(8,128)(2,1)} %get-tuple-element.130.refs_8_.refs_6_.refs_2_, bf16[256,1024]{1,0:T(8,128)(2,1)} %copy-done.4, ...), custom_call_target="tpu_custom_call" | custom-call | flops 1073741824 | bytes 4194304 | tf_op jit(solution)/shard_map/latent_keys_values/pallas_call | solution.py:460
  233.3 3.4 %decode_rows.5 = bf16[512,512]{1,0:T(8,128)(2,1)} custom-call(bf16[512,512]{1,0:T(8,128)(2,1)} %collective-permute-done.8.q_ref, bf16[256,1024]{1,0:T(8,128)(2,1)} %latent_keys_values.5.refs_2_.refs_5_.refs_0_.refs_1_, bf16[256,1024]{1,0:T(8,128)(2,1)} %latent_keys_values.5.refs_2_.refs_5_.refs_0_.refs_1_, f32[512,512]{1,0:T(8,128)} %get-tuple-element.144.refs_2_, ...), custom_call_target="tpu_custom_call" | custom-call | flops 1073741824 | bytes 2097152 | tf_op jit(solution)/shard_map/decode_rows/pallas_call | solution.py:546
  237.6 8.5 %decode_rows.4 = f32[512,512]{1,0:T(8,128)} custom-call(bf16[512,512]{1,0:T(8,128)(2,1)} %get-tuple-element.152.q_ref, bf16[1024,1024]{1,0:T(8,128)(2,1)} %latent_keys_values.3.refs_0_.refs_2_.refs_3_, bf16[768,1024]{1,0:T(8,128)(2,1)} %latent_keys_values.4.refs_1_.refs_3_.refs_4_, bf16[256,1024]{1,0:T(8,128)(2,1)} %latent_keys_values.5.refs_2_.refs_5_.refs_0_.refs_1_, ...), custom_call_target="tpu_custom_call" | custom-call | flops 8589934592 | bytes 5767168 | tf_op jit(solution)/shard_map/decode_rows/pallas_call | solution.py:546
  246.1 4.8 %collective-permute-done.37 = bf16[512,512]{1,0:T(8,128)(2,1)S(1)} collective-permute-done((bf16[512,512]{1,0:T(8,128)(2,1)}, bf16[512,512]{1,0:T(8,128)(2,1)S(1)}, u32[]{:S(2)}, u32[]{:S(2)}) %collective-permute-start.37) | collective-permute-done | bytes 524320 | tf_op jit(solution)/shard_map/ppermute | solution.py:778
  251.0 1.6 fusion
  (151 shorter events, 34.6 us)
Async XLA Ops:
  0.6 59.3 %copy-start = (bf16[3,1024]{1,0:T(4,128)(2,1)S(1)}, bf16[3,1024]{1,0:T(4,128)(2,1)}, u32[]{:S(2)}) copy-start(bf16[3,1024]{1,0:T(4,128)(2,1)} %param.25) | copy-start | bytes 18436
  2.9 32.1 %collective-permute-start = (bf16[528,1024]{1,0:T(8,128)(2,1)S(1)}, bf16[528,1024]{1,0:T(8,128)(2,1)}, u32[]{:S(2)}, u32[]{:S(2)}) collective-permute-start(bf16[528,1024]{1,0:T(8,128)(2,1)S(1)} %pad_maximum_fusion), channel_id=1, source_target_pairs={{0,2},{2,0},{4,6},{6,4},{8,10},{10,8},{12,14},{14,12},{1,3},{3,1},... | collective-permute-start | bytes 3244040 | tf_op jit(solution)/shard_map/ppermute | solution.py:611
  8.4 10.9 %collective-permute-start.1 = (bf16[528,256]{1,0:T(8,128)(2,1)}, bf16[528,256]{1,0:T(8,128)(2,1)}, u32[]{:S(2)}, u32[]{:S(2)}) collective-permute-start(bf16[528,256]{1,0:T(8,128)(2,1)} %pad_maximum_fusion.3), channel_id=1, source_target_pairs={{4,0},{6,2},{8,4},{10,6},{12,8},{14,10},{0,12},{2,14},{5,1},{7,3},... | collective-permute-start | bytes 811016 | tf_op jit(solution)/shard_map/ppermute | solution.py:614
  12.0 23.0 %collective-permute-start.2 = (bf16[528,256]{1,0:T(8,128)(2,1)}, bf16[528,256]{1,0:T(8,128)(2,1)}, u32[]{:S(2)}, u32[]{:S(2)}) collective-permute-start(bf16[528,256]{1,0:T(8,128)(2,1)} %pad_maximum_fusion.3), channel_id=1, source_target_pairs={{8,0},{10,2},{12,4},{14,6},{0,8},{2,10},{4,12},{6,14},{9,1},{11,3}... | collective-permute-start | bytes 811016 | tf_op jit(solution)/shard_map/ppermute | solution.py:614
  12.0 23.0 %collective-permute-start.3 = (bf16[528,256]{1,0:T(8,128)(2,1)}, bf16[528,256]{1,0:T(8,128)(2,1)S(1)}, u32[]{:S(2)}, u32[]{:S(2)}) collective-permute-start(bf16[528,256]{1,0:T(8,128)(2,1)} %pad_maximum_fusion.3), channel_id=1, source_target_pairs={{12,0},{14,2},{0,4},{2,6},{4,8},{6,10},{8,12},{10,14},{13,1},{15,3... | collective-permute-start | bytes 811016 | tf_op jit(solution)/shard_map/ppermute | solution.py:614
  35.0 14.9 %collective-permute-start.4 = (bf16[256,1024]{1,0:T(8,128)(2,1)S(1)}, bf16[256,1024]{1,0:T(8,128)(2,1)S(1)}, u32[]{:S(2)}, u32[]{:S(2)}) collective-permute-start(bf16[256,1024]{1,0:T(8,128)(2,1)S(1)} %pad_maximum_fusion.1), channel_id=1, source_target_pairs={{0,2},{2,0},{4,6},{6,4},{8,10},{10,8},{12,14},{14,12},{1,3},{3,1},... | collective-permute-start | bytes 1572872 | tf_op jit(solution)/shard_map/ppermute | solution.py:611
  49.9 43.8 %copy-start.4 = (bf16[256,1024]{1,0:T(8,128)(2,1)}, bf16[256,1024]{1,0:T(8,128)(2,1)S(1)}, u32[]{:S(2)}) copy-start(bf16[256,1024]{1,0:T(8,128)(2,1)S(1)} %collective-permute-done.4.refs_9_.refs_7_.refs_3_) | copy-start | bytes 1572868
  50.0 57.8 %all-to-all-start = ((bf16[4,528,512]{2,1,0:T(8,128)(2,1)}), bf16[4,528,512]{2,1,0:T(8,128)(2,1)S(1)}, u32[]{:S(2)}, u32[]{:S(2)}) async-start(bf16[4,528,512]{2,1,0:T(8,128)(2,1)} %bitcast.52), calls=%async_computation | async-start | bytes 4325376 | tf_op jit(solution)/shard_map/all_to_all | solution.py:672
  58.4 30.3 %collective-permute-start.5 = (bf16[2624,256]{1,0:T(8,128)(2,1)}, bf16[2624,256]{1,0:T(8,128)(2,1)S(1)}, u32[]{:S(2)}, u32[]{:S(2)}) collective-permute-start(bf16[2624,256]{1,0:T(8,128)(2,1)} %get-tuple-element.161), channel_id=1, source_target_pairs={{0,2},{2,0},{4,6},{6,4},{8,10},{10,8},{12,14},{14,12},{1,3},{3,1},... | collective-permute-start | bytes 4030472 | tf_op jit(solution)/shard_map/ppermute | solution.py:611
  60.4 43.4 %collective-permute-start.6 = (bf16[1584,256]{1,0:T(8,128)(2,1)}, bf16[1584,256]{1,0:T(8,128)(2,1)}, u32[]{:S(2)}, u32[]{:S(2)}) collective-permute-start(bf16[1584,256]{1,0:T(8,128)(2,1)} %get-tuple-element.160.refs_1_), channel_id=1, source_target_pairs={{0,16},{16,0},{1,17},{17,1},{2,18},{18,2},{3,19},{19,3},{4,20},{20... | collective-permute-start | bytes 2433032 | tf_op jit(solution)/shard_map/ppermute | solution.py:608
  89.7 18.0 %collective-permute-start.7 = (bf16[1584,256]{1,0:T(8,128)(2,1)}, bf16[1584,256]{1,0:T(8,128)(2,1)}, u32[]{:S(2)}, u32[]{:S(2)}) collective-permute-start(bf16[1584,256]{1,0:T(8,128)(2,1)} %slice.62), channel_id=1, source_target_pairs={{0,16},{16,0},{1,17},{17,1},{2,18},{18,2},{3,19},{19,3},{4,20},{20... | collective-permute-start | bytes 2433032 | tf_op jit(solution)/shard_map/ppermute | solution.py:608
  92.3 11.6 %collective-permute-start.8 = (bf16[512,512]{1,0:T(8,128)(2,1)}, bf16[512,512]{1,0:T(8,128)(2,1)}, u32[]{:S(2)}, u32[]{:S(2)}) collective-permute-start(bf16[512,512]{1,0:T(8,128)(2,1)} %get-tuple-element.153), channel_id=1, source_target_pairs={{0,2},{2,0},{4,6},{6,4},{8,10},{10,8},{12,14},{14,12},{1,3},{3,1},... | collective-permute-start | bytes 1572872 | tf_op jit(solution)/shard_map/ppermute | solution.py:611
  95.0 15.3 %collective-permute-start.10 = (bf16[256,1024]{1,0:T(8,128)(2,1)}, bf16[256,1024]{1,0:T(8,128)(2,1)S(1)}, u32[]{:S(2)}, u32[]{:S(2)}) collective-permute-start(bf16[256,1024]{1,0:T(8,128)(2,1)} %get-tuple-element.155), channel_id=1, source_target_pairs={{0,4},{2,6},{4,8},{6,10},{8,12},{10,14},{1,5},{3,7},{5,9},{7,11},{... | collective-permute-start | bytes 1572872 | tf_op jit(solution)/shard_map/ppermute | solution.py:618
  98.6 15.2 %collective-permute-start.11 = (bf16[256,1024]{1,0:T(8,128)(2,1)}, bf16[256,1024]{1,0:T(8,128)(2,1)S(1)}, u32[]{:S(2)}, u32[]{:S(2)}) collective-permute-start(bf16[256,1024]{1,0:T(8,128)(2,1)} %get-tuple-element.155), channel_id=1, source_target_pairs={{12,8},{14,10},{8,4},{10,6},{4,0},{6,2},{13,9},{15,11},{9,5},{11,7... | collective-permute-start | bytes 1572872 | tf_op jit(solution)/shard_map/ppermute | solution.py:618
  110.3 20.0 %copy-start.16 = (bf16[256,1024]{1,0:T(8,128)(2,1)}, bf16[256,1024]{1,0:T(8,128)(2,1)S(1)}, u32[]{:S(2)}) copy-start(bf16[256,1024]{1,0:T(8,128)(2,1)S(1)} %collective-permute-done.10) | copy-start | bytes 1572868
  113.9 16.5 %copy-start.18 = (bf16[256,1024]{1,0:T(8,128)(2,1)}, bf16[256,1024]{1,0:T(8,128)(2,1)S(1)}, u32[]{:S(2)}) copy-start(bf16[256,1024]{1,0:T(8,128)(2,1)S(1)} %collective-permute-done.11) | copy-start | bytes 1572868
  113.9 16.5 %collective-permute-start.12 = (bf16[256,1024]{1,0:T(8,128)(2,1)S(1)}, bf16[256,1024]{1,0:T(8,128)(2,1)}, u32[]{:S(2)}, u32[]{:S(2)}) collective-permute-start(bf16[256,1024]{1,0:T(8,128)(2,1)S(1)} %collective-permute-done.10), channel_id=1, source_target_pairs={{4,8},{6,10},{8,12},{10,14},{5,9},{7,11},{9,13},{11,15},{20,24},{2... | collective-permute-start | bytes 1572872 | tf_op jit(solution)/shard_map/ppermute | solution.py:618
  115.3 15.0 %collective-permute-start.13 = (bf16[256,1024]{1,0:T(8,128)(2,1)S(1)}, bf16[256,1024]{1,0:T(8,128)(2,1)}, u32[]{:S(2)}, u32[]{:S(2)}) collective-permute-start(bf16[256,1024]{1,0:T(8,128)(2,1)S(1)} %collective-permute-done.11), channel_id=1, source_target_pairs={{8,4},{10,6},{4,0},{6,2},{9,5},{11,7},{5,1},{7,3},{24,20},{26,22},... | collective-permute-start | bytes 1572872 | tf_op jit(solution)/shard_map/ppermute | solution.py:618
  116.6 7.2 %collective-permute-start.9 = (bf16[256,512]{1,0:T(8,128)(2,1)S(1)}, bf16[256,512]{1,0:T(8,128)(2,1)S(1)}, u32[]{:S(2)}, u32[]{:S(2)}) collective-permute-start(bf16[256,512]{1,0:T(8,128)(2,1)S(1)} %get-tuple-element.85), channel_id=1, source_target_pairs={{0,2},{2,0},{4,6},{6,4},{8,10},{10,8},{12,14},{14,12},{1,3},{3,1},... | collective-permute-start | bytes 786440 | tf_op jit(solution)/shard_map/ppermute | solution.py:611
  130.4 9.2 %collective-permute-start.14 = (f32[256,2048]{1,0:T(8,128)}, f32[256,2048]{1,0:T(8,128)S(1)}, u32[]{:S(2)}, u32[]{:S(2)}) collective-permute-start(f32[256,2048]{1,0:T(8,128)} %project_rows.1.mine_ref), channel_id=1, source_target_pairs={{0,1},{1,0},{2,3},{3,2},{4,5},{5,4},{6,7},{7,6},{8,9},{9,8},{10,11... | collective-permute-start | bytes 6291464 | tf_op jit(solution)/shard_map/ppermute | solution.py:713
  132.7 19.5 %collective-permute-start.21 = (bf16[256,1024]{1,0:T(8,128)(2,1)}, bf16[256,1024]{1,0:T(8,128)(2,1)}, u32[]{:S(2)}, u32[]{:S(2)}) collective-permute-start(bf16[256,1024]{1,0:T(8,128)(2,1)} %collective-permute-done.12), channel_id=1, source_target_pairs={{8,12},{10,14},{9,13},{11,15},{24,28},{26,30},{25,29},{27,31}} | collective-permute-start | bytes 1572872 | tf_op jit(solution)/shard_map/ppermute | solution.py:618
  134.1 19.8 %collective-permute-start.22 = (bf16[256,1024]{1,0:T(8,128)(2,1)}, bf16[256,1024]{1,0:T(8,128)(2,1)}, u32[]{:S(2)}, u32[]{:S(2)}) collective-permute-start(bf16[256,1024]{1,0:T(8,128)(2,1)} %collective-permute-done.13), channel_id=1, source_target_pairs={{4,0},{6,2},{5,1},{7,3},{20,16},{22,18},{21,17},{23,19}} | collective-permute-start | bytes 1572872 | tf_op jit(solution)/shard_map/ppermute | solution.py:618
  137.5 31.0 %collective-permute-start.20 = (bf16[256,1024]{1,0:T(8,128)(2,1)S(1)}, bf16[256,1024]{1,0:T(8,128)(2,1)S(1)}, u32[]{:S(2)}, u32[]{:S(2)}) collective-permute-start(bf16[256,1024]{1,0:T(8,128)(2,1)S(1)} %broadcast_select_fusion.2.refs_10_.refs_8_.refs_4_), channel_id=1, source_target_pairs={{0,16},{16,0},{1,17},{17,1},{2,18},{18,2},{3,19},{19,3},{4,20},{20... | collective-permute-start | bytes 1572872 | tf_op jit(solution)/shard_map/ppermute | solution.py:608
  140.8 13.4 %copy-start.17 = (bf16[256,1024]{1,0:T(8,128)(2,1)S(1)}, bf16[256,1024]{1,0:T(8,128)(2,1)}, u32[]{:S(2)}) copy-start(bf16[256,1024]{1,0:T(8,128)(2,1)} %copy-done.16) | copy-start | bytes 1572868
  145.5 17.0 %collective-permute-start.15 = (bf16[256,1024]{1,0:T(8,128)(2,1)}, bf16[256,1024]{1,0:T(8,128)(2,1)S(1)}, u32[]{:S(2)}, u32[]{:S(2)}) collective-permute-start(bf16[256,1024]{1,0:T(8,128)(2,1)} %get-tuple-element.118.refs_0_), channel_id=1, source_target_pairs={{0,4},{2,6},{4,8},{6,10},{8,12},{10,14},{1,5},{3,7},{5,9},{7,11},{... | collective-permute-start | bytes 1572872 | tf_op jit(solution)/shard_map/ppermute | solution.py:618
  150.9 16.1 %collective-permute-start.16 = (bf16[256,1024]{1,0:T(8,128)(2,1)}, bf16[256,1024]{1,0:T(8,128)(2,1)S(1)}, u32[]{:S(2)}, u32[]{:S(2)}) collective-permute-start(bf16[256,1024]{1,0:T(8,128)(2,1)} %get-tuple-element.118.refs_0_), channel_id=1, source_target_pairs={{12,8},{14,10},{8,4},{10,6},{4,0},{6,2},{13,9},{15,11},{9,5},{11,7... | collective-permute-start | bytes 1572872 | tf_op jit(solution)/shard_map/ppermute | solution.py:618
  152.2 17.6 %collective-permute-start.19 = (bf16[256,1024]{1,0:T(8,128)(2,1)}, bf16[256,1024]{1,0:T(8,128)(2,1)}, u32[]{:S(2)}, u32[]{:S(2)}) collective-permute-start(bf16[256,1024]{1,0:T(8,128)(2,1)} %get-tuple-element.118.refs_0_), channel_id=1, source_target_pairs={{0,2},{2,0},{4,6},{6,4},{8,10},{10,8},{12,14},{14,12},{1,3},{3,1},... | collective-permute-start | bytes 1572872 | tf_op jit(solution)/shard_map/ppermute | solution.py:611
  154.1 35.2 %copy-start.6 = (bf16[256,1024]{1,0:T(8,128)(2,1)}, bf16[256,1024]{1,0:T(8,128)(2,1)S(1)}, u32[]{:S(2)}) copy-start(bf16[256,1024]{1,0:T(8,128)(2,1)S(1)} %broadcast_select_fusion.1.refs_12_.refs_10_.refs_6_) | copy-start | bytes 1572868
  154.1 17.5 %collective-permute-start.23 = (bf16[256,1024]{1,0:T(8,128)(2,1)S(1)}, bf16[256,1024]{1,0:T(8,128)(2,1)S(1)}, u32[]{:S(2)}, u32[]{:S(2)}) collective-permute-start(bf16[256,1024]{1,0:T(8,128)(2,1)S(1)} %broadcast_select_fusion.1.refs_12_.refs_10_.refs_6_), channel_id=1, source_target_pairs={{0,16},{16,0},{1,17},{17,1},{2,18},{18,2},{3,19},{19,3},{4,20},{20... | collective-permute-start | bytes 1572872 | tf_op jit(solution)/shard_map/ppermute | solution.py:608
  155.4 36.2 %copy-start.7 = (bf16[256,1024]{1,0:T(8,128)(2,1)}, bf16[256,1024]{1,0:T(8,128)(2,1)S(1)}, u32[]{:S(2)}) copy-start(bf16[256,1024]{1,0:T(8,128)(2,1)S(1)} %broadcast_select_fusion.refs_14_.refs_12_.refs_8_) | copy-start | bytes 1572868
  162.4 16.2 %collective-permute-start.24 = (bf16[256,1024]{1,0:T(8,128)(2,1)S(1)}, bf16[256,1024]{1,0:T(8,128)(2,1)S(1)}, u32[]{:S(2)}, u32[]{:S(2)}) collective-permute-start(bf16[256,1024]{1,0:T(8,128)(2,1)S(1)} %broadcast_select_fusion.refs_14_.refs_12_.refs_8_), channel_id=1, source_target_pairs={{0,16},{16,0},{1,17},{17,1},{2,18},{18,2},{3,19},{19,3},{4,20},{20... | collective-permute-start | bytes 1572872 | tf_op jit(solution)/shard_map/ppermute | solution.py:608
  166.9 11.7 %collective-permute-start.17 = (bf16[256,1024]{1,0:T(8,128)(2,1)S(1)}, bf16[256,1024]{1,0:T(8,128)(2,1)S(1)}, u32[]{:S(2)}, u32[]{:S(2)}) collective-permute-start(bf16[256,1024]{1,0:T(8,128)(2,1)S(1)} %collective-permute-done.15), channel_id=1, source_target_pairs={{4,8},{6,10},{8,12},{10,14},{5,9},{7,11},{9,13},{11,15},{20,24},{2... | collective-permute-start | bytes 1572872 | tf_op jit(solution)/shard_map/ppermute | solution.py:618
  168.5 23.1 %copy-start.11 = (bf16[256,1024]{1,0:T(8,128)(2,1)}, bf16[256,1024]{1,0:T(8,128)(2,1)S(1)}, u32[]{:S(2)}) copy-start(bf16[256,1024]{1,0:T(8,128)(2,1)S(1)} %collective-permute-done.20.refs_11_.refs_9_.refs_5_) | copy-start | bytes 1572868
  168.5 16.5 %collective-permute-start.18 = (bf16[256,1024]{1,0:T(8,128)(2,1)S(1)}, bf16[256,1024]{1,0:T(8,128)(2,1)S(1)}, u32[]{:S(2)}, u32[]{:S(2)}) collective-permute-start(bf16[256,1024]{1,0:T(8,128)(2,1)S(1)} %collective-permute-done.16), channel_id=1, source_target_pairs={{8,4},{10,6},{4,0},{6,2},{9,5},{11,7},{5,1},{7,3},{24,20},{26,22},... | collective-permute-start | bytes 1572872 | tf_op jit(solution)/shard_map/ppermute | solution.py:618
  169.8 15.2 %collective-permute-start.25 = (bf16[256,1024]{1,0:T(8,128)(2,1)}, bf16[256,1024]{1,0:T(8,128)(2,1)}, u32[]{:S(2)}, u32[]{:S(2)}) collective-permute-start(bf16[256,1024]{1,0:T(8,128)(2,1)} %broadcast_select_fusion.3.refs_2_), channel_id=1, source_target_pairs={{0,2},{2,0},{4,6},{6,4},{8,10},{10,8},{12,14},{14,12},{1,3},{3,1},... | collective-permute-start | bytes 1572872 | tf_op jit(solution)/shard_map/ppermute | solution.py:611
  171.6 13.4 %copy-start.12 = (bf16[256,1024]{1,0:T(8,128)(2,1)}, bf16[256,1024]{1,0:T(8,128)(2,1)S(1)}, u32[]{:S(2)}) copy-start(bf16[256,1024]{1,0:T(8,128)(2,1)S(1)} %collective-permute-done.23.refs_13_.refs_11_.refs_7_) | copy-start | bytes 1572868
  185.0 4.3 %collective-permute-start.28 = (bf16[256,1024]{1,0:T(8,128)(2,1)}, bf16[256,1024]{1,0:T(8,128)(2,1)}, u32[]{:S(2)}, u32[]{:S(2)}) collective-permute-start(bf16[256,1024]{1,0:T(8,128)(2,1)} %collective-permute-done.19.refs_1_), channel_id=1, source_target_pairs={{0,1},{1,0},{2,3},{3,2},{4,5},{5,4},{6,7},{7,6},{8,9},{9,8},{10,11... | collective-permute-start | bytes 1572872 | tf_op jit(solution)/shard_map/ppermute | solution.py:723
  185.1 6.5 %collective-permute-start.29 = (bf16[256,1024]{1,0:T(8,128)(2,1)}, bf16[256,1024]{1,0:T(8,128)(2,1)}, u32[]{:S(2)}, u32[]{:S(2)}) collective-permute-start(bf16[256,1024]{1,0:T(8,128)(2,1)} %broadcast_select_fusion.3.refs_2_), channel_id=1, source_target_pairs={{0,1},{1,0},{2,3},{3,2},{4,5},{5,4},{6,7},{7,6},{8,9},{9,8},{10,11... | collective-permute-start | bytes 1572872 | tf_op jit(solution)/shard_map/ppermute | solution.py:723
  185.6 6.0 %collective-permute-start.30 = (bf16[256,1024]{1,0:T(8,128)(2,1)}, bf16[256,1024]{1,0:T(8,128)(2,1)}, u32[]{:S(2)}, u32[]{:S(2)}) collective-permute-start(bf16[256,1024]{1,0:T(8,128)(2,1)} %collective-permute-done.25.refs_3_), channel_id=1, source_target_pairs={{0,1},{1,0},{2,3},{3,2},{4,5},{5,4},{6,7},{7,6},{8,9},{9,8},{10,11... | collective-permute-start | bytes 1572872 | tf_op jit(solution)/shard_map/ppermute | solution.py:723
  185.6 16.3 %collective-permute-start.26 = (bf16[256,1024]{1,0:T(8,128)(2,1)S(1)}, bf16[256,1024]{1,0:T(8,128)(2,1)}, u32[]{:S(2)}, u32[]{:S(2)}) collective-permute-start(bf16[256,1024]{1,0:T(8,128)(2,1)S(1)} %collective-permute-done.17), channel_id=1, source_target_pairs={{8,12},{10,14},{9,13},{11,15},{24,28},{26,30},{25,29},{27,31}} | collective-permute-start | bytes 1572872 | tf_op jit(solution)/shard_map/ppermute | solution.py:618
  187.1 16.3 %collective-permute-start.27 = (bf16[256,1024]{1,0:T(8,128)(2,1)S(1)}, bf16[256,1024]{1,0:T(8,128)(2,1)}, u32[]{:S(2)}, u32[]{:S(2)}) collective-permute-start(bf16[256,1024]{1,0:T(8,128)(2,1)S(1)} %collective-permute-done.18), channel_id=1, source_target_pairs={{4,0},{6,2},{5,1},{7,3},{20,16},{22,18},{21,17},{23,19}} | collective-permute-start | bytes 1572872 | tf_op jit(solution)/shard_map/ppermute | solution.py:618
  189.3 14.5 %collective-permute-start.31 = (bf16[256,1024]{1,0:T(8,128)(2,1)}, bf16[256,1024]{1,0:T(8,128)(2,1)S(1)}, u32[]{:S(2)}, u32[]{:S(2)}) collective-permute-start(bf16[256,1024]{1,0:T(8,128)(2,1)} %fusion.1.refs_0_), channel_id=1, source_target_pairs={{0,2},{2,0},{4,6},{6,4},{8,10},{10,8},{12,14},{14,12},{1,3},{3,1},... | collective-permute-start | bytes 1572872 | tf_op jit(solution)/shard_map/ppermute | solution.py:611
  203.8 3.6 %collective-permute-start.33 = (bf16[256,1024]{1,0:T(8,128)(2,1)}, bf16[256,1024]{1,0:T(8,128)(2,1)S(1)}, u32[]{:S(2)}, u32[]{:S(2)}) collective-permute-start(bf16[256,1024]{1,0:T(8,128)(2,1)} %fusion.1.refs_0_), channel_id=1, source_target_pairs={{0,1},{1,0},{2,3},{3,2},{4,5},{5,4},{6,7},{7,6},{8,9},{9,8},{10,11... | collective-permute-start | bytes 1572872 | tf_op jit(solution)/shard_map/ppermute | solution.py:723
  203.8 3.6 %collective-permute-start.34 = (bf16[256,1024]{1,0:T(8,128)(2,1)S(1)}, bf16[256,1024]{1,0:T(8,128)(2,1)S(1)}, u32[]{:S(2)}, u32[]{:S(2)}) collective-permute-start(bf16[256,1024]{1,0:T(8,128)(2,1)S(1)} %collective-permute-done.31.refs_1_), channel_id=1, source_target_pairs={{0,1},{1,0},{2,3},{3,2},{4,5},{5,4},{6,7},{7,6},{8,9},{9,8},{10,11... | collective-permute-start | bytes 1572872 | tf_op jit(solution)/shard_map/ppermute | solution.py:723
  205.5 2.0 collective-permute-start.35
  205.6 19.6 %collective-permute-start.32 = (bf16[256,1024]{1,0:T(8,128)(2,1)S(1)}, bf16[256,1024]{1,0:T(8,128)(2,1)S(1)}, u32[]{:S(2)}, u32[]{:S(2)}) collective-permute-start(bf16[256,1024]{1,0:T(8,128)(2,1)S(1)} %select_select_fusion.1.refs_2_), channel_id=1, source_target_pairs={{0,2},{2,0},{4,6},{6,4},{8,10},{10,8},{12,14},{14,12},{1,3},{3,1},... | collective-permute-start | bytes 1572872 | tf_op jit(solution)/shard_map/ppermute | solution.py:611
  225.2 2.0 collective-permute-start.36
  236.7 14.2 %collective-permute-start.37 = (bf16[512,512]{1,0:T(8,128)(2,1)}, bf16[512,512]{1,0:T(8,128)(2,1)S(1)}, u32[]{:S(2)}, u32[]{:S(2)}) collective-permute-start(bf16[512,512]{1,0:T(8,128)(2,1)} %decode_rows.5), channel_id=1, source_target_pairs={{0,2},{2,0},{4,6},{6,4},{8,10},{10,8},{12,14},{14,12},{1,3},{3,1},... | collective-permute-start | bytes 1572872 | tf_op jit(solution)/shard_map/ppermute | solution.py:778
  (23 other events, 110.6 us)

commit v18 on v15

--- a/solution.py
+++ b/solution.py
@@ -692,8 +692,8 @@
     own_queries = columns((queries,), y)
     near_queries = over_near(columns((queries,), 1 - y))
 
-    parts, out_near, out_far_other, out_near_other, near_queries = lax.optimization_barrier(
-        (parts, out_near, out_far_other, out_near_other, near_queries)
+    parts, out_near, out_far_other, out_near_other = lax.optimization_barrier(
+        (parts, out_near, out_far_other, out_near_other)
     )
     attended, for_near = merge(y, parts, far)
     _, hops = lax.optimization_barrier((for_near, hops))
@@ -703,7 +703,9 @@
     out_ids = jnp.stack([*places, y, x]).astype(jnp.int32)
     weights = [w_out, out_far, out_far_other, out_near, out_near_other]
     partial_value = project(out_ids, attended, from_near, weights)
-    partial_value, hops = lax.optimization_barrier((partial_value, hops))
+    partial_value, hops, near_queries = lax.optimization_barrier(
+        (partial_value, hops, near_queries)
+    )
     kv_bands = [kv_own, kv_near]
     for k in early:
         kv_moved = by_shift(hops, k)

time: 250 us -> 250 us (level)
  transfers between devices with their start and end apart: 39 -> 39, of which waited for: 15 -> 14; matrix products, arithmetic and copies ran while one was open for 9% -> 9% of each run, Pallas kernels for 23% -> 23%
where the time goes in v18:
time: 250 us; the launch traced here: 249 us
  waiting for transfers between devices  88 us (35%)
  Pallas kernels  63.5 us (25%)
  starting transfers between devices  54.8 us (22%)
  local copies, waits for them, and re-layouts  27.2 us (11%)
  other arithmetic  13.4 us (5%)
    ppermute x9, waiting for transfers between devices, over_near(): return lax.ppermute(value, 'pos', near)  32.4 us
    ppermute x12, starting transfers between devices, hop(): lax.ppermute(v, 'pos', hop_perm(pos, step, way))  22 us
    ppermute x3, waiting for transfers between devices, over_far(): return lax.ppermute(value, 'pos', shift_perm(pos, k))  20.4 us
    pallas_call x3, Pallas kernels, decode(): pl.pallas_call(functools.partial(decode_kernel, len(keys_values), first,...  19.2 us
    unnamed x69, local copies, waits for them, and re-layouts  19 us
    pallas_call x3, Pallas kernels, latent_keys_values(): pl.pallas_call(functools.partial(latents_kernel, pieces), grid_spec=grid_...  17.6 us
    ppermute x12, waiting for transfers between devices, hop(): lax.ppermute(v, 'pos', hop_perm(pos, step, way))  15.2 us
    ppermute x9, starting transfers between devices, over_near(): return lax.ppermute(value, 'pos', near)  14.5 us
  transfers between devices with their start and end apart: 39, of which 14 were waited for; matrix products, arithmetic and copies ran while one was open for 9% of the time, Pallas kernels for 23%

profile of v18, /device:TPU:0, one launch (start us, length us, event | category | flops | bytes accessed | tf_op | source)
XLA Modules:
  0.0 248.5 jit_solution(6695743724449594437)
XLA Ops:
  1.4 1.3 constant_dynamic-slice_fusion.8
  2.9 3.0 %collective-permute-start = (bf16[528,1024]{1,0:T(8,128)(2,1)S(1)}, bf16[528,1024]{1,0:T(8,128)(2,1)}, u32[]{:S(2)}, u32[]{:S(2)}) collective-permute-start(bf16[528,1024]{1,0:T(8,128)(2,1)S(1)} %pad_maximum_fusion), channel_id=1, source_target_pairs={{0,2},{2,0},{4,6},{6,4},{8,10},{10,8},{12,14},{14,12},{1,3},{3,1},... | collective-permute-start | bytes 3244040 | tf_op jit(solution)/shard_map/ppermute | solution.py:611
  8.4 3.6 %collective-permute-start.1 = (bf16[528,256]{1,0:T(8,128)(2,1)}, bf16[528,256]{1,0:T(8,128)(2,1)}, u32[]{:S(2)}, u32[]{:S(2)}) collective-permute-start(bf16[528,256]{1,0:T(8,128)(2,1)} %pad_maximum_fusion.3), channel_id=1, source_target_pairs={{4,0},{6,2},{8,4},{10,6},{12,8},{14,10},{0,12},{2,14},{5,1},{7,3},... | collective-permute-start | bytes 811016 | tf_op jit(solution)/shard_map/ppermute | solution.py:614
  14.6 4.6 %collective-permute-done.1 = bf16[528,256]{1,0:T(8,128)(2,1)} collective-permute-done((bf16[528,256]{1,0:T(8,128)(2,1)}, bf16[528,256]{1,0:T(8,128)(2,1)}, u32[]{:S(2)}, u32[]{:S(2)}) %collective-permute-start.1) | collective-permute-done | bytes 270368 | tf_op jit(solution)/shard_map/ppermute | solution.py:614
  19.2 15.8 %collective-permute-done.2 = bf16[528,256]{1,0:T(8,128)(2,1)} collective-permute-done((bf16[528,256]{1,0:T(8,128)(2,1)}, bf16[528,256]{1,0:T(8,128)(2,1)}, u32[]{:S(2)}, u32[]{:S(2)}) %collective-permute-start.2) | collective-permute-done | bytes 270368 | tf_op jit(solution)/shard_map/ppermute | solution.py:614
  35.6 14.5 %encode_rows.1 = bf16[2112,512]{1,0:T(8,128)(2,1)} custom-call(s32[1]{0:T(128)} %bitcast.9.ids_ref, bf16[2048,1024]{1,0:T(8,128)(2,1)} %q_ref.1, bf16[512,1024]{1,0:T(8,128)(2,1)} %k_ref.1, bf16[512,1024]{1,0:T(8,128)(2,1)} %v_ref.1, bf16[16,1024]{1,0:T(8,128)(2,1)} %copy-done.28, bf16[528,1024]{1,0:T(8,128)(2,1)} %collective-permute-done.near_ref, ...), custom_call_target="tpu_custom_call" | custom-call | flops 8589934592 | bytes 2097152 | tf_op jit(solution)/shard_map/encode_rows/pallas_call | solution.py:262
  50.1 4.0 %all-to-all-start = ((bf16[4,528,512]{2,1,0:T(8,128)(2,1)}), bf16[4,528,512]{2,1,0:T(8,128)(2,1)S(1)}, u32[]{:S(2)}, u32[]{:S(2)}) async-start(bf16[4,528,512]{2,1,0:T(8,128)(2,1)} %bitcast.52), calls=%async_computation | async-start | bytes 4325376 | tf_op jit(solution)/shard_map/all_to_all | solution.py:672
  54.1 1.8 constant_dynamic-update-slice_fusion.7
  55.9 1.8 constant_dynamic-update-slice_fusion.6
  58.5 1.5 collective-permute-start.5
  60.1 1.5 collective-permute-start.6
  61.6 27.2 %collective-permute-done.5.refs_3_ = bf16[2624,256]{1,0:T(8,128)(2,1)S(1)} collective-permute-done((bf16[2624,256]{1,0:T(8,128)(2,1)}, bf16[2624,256]{1,0:T(8,128)(2,1)S(1)}, u32[]{:S(2)}, u32[]{:S(2)}) %collective-permute-start.5) | collective-permute-done | bytes 1343520 | tf_op jit(solution)/shard_map/ppermute | solution.py:611
  90.8 1.5 collective-permute-start.7
  92.3 2.1 pad_maximum_fusion.2
  94.5 4.4 %collective-permute-start.9 = (bf16[256,1024]{1,0:T(8,128)(2,1)}, bf16[256,1024]{1,0:T(8,128)(2,1)}, u32[]{:S(2)}, u32[]{:S(2)}) collective-permute-start(bf16[256,1024]{1,0:T(8,128)(2,1)} %get-tuple-element.155), channel_id=1, source_target_pairs={{0,4},{2,6},{4,8},{6,10},{8,12},{10,14},{1,5},{3,7},{5,9},{7,11},{... | collective-permute-start | bytes 1572872 | tf_op jit(solution)/shard_map/ppermute | solution.py:618
  101.8 1.5 collective-permute-start.13
  103.3 5.6 %collective-permute-done.7.refs_4_ = bf16[1584,256]{1,0:T(8,128)(2,1)} collective-permute-done((bf16[1584,256]{1,0:T(8,128)(2,1)}, bf16[1584,256]{1,0:T(8,128)(2,1)}, u32[]{:S(2)}, u32[]{:S(2)}) %collective-permute-start.7) | collective-permute-done | bytes 811040 | tf_op jit(solution)/shard_map/ppermute | solution.py:608
  108.9 1.9 merge_rows.1
  111.5 2.7 %collective-permute-done.10 = bf16[256,1024]{1,0:T(8,128)(2,1)} collective-permute-done((bf16[256,1024]{1,0:T(8,128)(2,1)}, bf16[256,1024]{1,0:T(8,128)(2,1)}, u32[]{:S(2)}, u32[]{:S(2)}) %collective-permute-start.10) | collective-permute-done | bytes 524320 | tf_op jit(solution)/shard_map/ppermute | solution.py:618
  116.1 1.6 collective-permute-start.8
  118.4 4.3 %collective-permute-done.8.near_ref = bf16[256,512]{1,0:T(8,128)(2,1)S(1)} collective-permute-done((bf16[256,512]{1,0:T(8,128)(2,1)S(1)}, bf16[256,512]{1,0:T(8,128)(2,1)S(1)}, u32[]{:S(2)}, u32[]{:S(2)}) %collective-permute-start.8) | collective-permute-done | bytes 262176 | tf_op jit(solution)/shard_map/ppermute | solution.py:611
  123.5 5.8 %project_rows.1.mine_ref = f32[256,2048]{1,0:T(8,128)} custom-call(s32[10]{0:T(128)} %stack.82.ids_ref, bf16[256,512]{1,0:T(8,128)(2,1)} %copy-done.8, bf16[256,512]{1,0:T(8,128)(2,1)} %copy-done.27, bf16[1024,256]{1,0:T(8,128)(2,1)} %refs_0_.1, bf16[1584,256]{1,0:T(8,128)(2,1)} %get-tuple-element.160.refs_1_, ...), custom_call_target="tpu_custom_call" | custom-call | flops 1073741824 | bytes 6291456 | tf_op jit(solution)/shard_map/project_rows/pallas_call | solution.py:363
  131.6 1.5 collective-permute-start.21
  135.4 2.3 collective-permute-start.20
  137.7 4.5 %norm_rows.1 = (f32[256,1024]{1,0:T(8,128)}, bf16[256,1024]{1,0:T(8,128)(2,1)}, bf16[256,1024]{1,0:T(8,128)(2,1)}) custom-call(s32[1]{0:T(128)} %bitcast.ids_ref, f32[256,2048]{1,0:T(8,128)} %project_rows.1.mine_ref, f32[256,2048]{1,0:T(8,128)} %collective-permute-done.14.theirs_ref, bf16[256,2048]{1,0:T(8,128)(2,1)} %latent_ref.1, f32[1,2048]{1,0:T(1,128)} %bitcast.54), custom_call_target="tpu_custom_call" | custom-call | flops 3145728 | bytes 6815744 | tf_op jit(solution)/shard_map/norm_rows/pallas_call | solution.py:397
  142.3 5.4 %collective-permute-start.15 = (bf16[256,1024]{1,0:T(8,128)(2,1)}, bf16[256,1024]{1,0:T(8,128)(2,1)S(1)}, u32[]{:S(2)}, u32[]{:S(2)}) collective-permute-start(bf16[256,1024]{1,0:T(8,128)(2,1)} %get-tuple-element.118.refs_0_), channel_id=1, source_target_pairs={{0,4},{2,6},{4,8},{6,10},{8,12},{10,14},{1,5},{3,7},{5,9},{7,11},{... | collective-permute-start | bytes 1572872 | tf_op jit(solution)/shard_map/ppermute | solution.py:618
  147.6 1.3 collective-permute-start.16
  148.9 1.6 collective-permute-start.19
  153.9 5.2 %collective-permute-done.15 = bf16[256,1024]{1,0:T(8,128)(2,1)S(1)} collective-permute-done((bf16[256,1024]{1,0:T(8,128)(2,1)}, bf16[256,1024]{1,0:T(8,128)(2,1)S(1)}, u32[]{:S(2)}, u32[]{:S(2)}) %collective-permute-start.15) | collective-permute-done | bytes 524320 | tf_op jit(solution)/shard_map/ppermute | solution.py:618
  159.5 3.7 %collective-permute-done.16 = bf16[256,1024]{1,0:T(8,128)(2,1)S(1)} collective-permute-done((bf16[256,1024]{1,0:T(8,128)(2,1)}, bf16[256,1024]{1,0:T(8,128)(2,1)S(1)}, u32[]{:S(2)}, u32[]{:S(2)}) %collective-permute-start.16) | collective-permute-done | bytes 524320 | tf_op jit(solution)/shard_map/ppermute | solution.py:618
  166.1 1.6 collective-permute-start.25
  168.4 7.7 %collective-permute-done.24.refs_15_.refs_13_.refs_9_ = bf16[256,1024]{1,0:T(8,128)(2,1)S(1)} collective-permute-done((bf16[256,1024]{1,0:T(8,128)(2,1)S(1)}, bf16[256,1024]{1,0:T(8,128)(2,1)S(1)}, u32[]{:S(2)}, u32[]{:S(2)}) %collective-permute-start.24) | collective-permute-done | bytes 524320 | tf_op jit(solution)/shard_map/ppermute | solution.py:608
  177.7 3.5 %collective-permute-done.18 = bf16[256,1024]{1,0:T(8,128)(2,1)S(1)} collective-permute-done((bf16[256,1024]{1,0:T(8,128)(2,1)S(1)}, bf16[256,1024]{1,0:T(8,128)(2,1)S(1)}, u32[]{:S(2)}, u32[]{:S(2)}) %collective-permute-start.18) | collective-permute-done | bytes 524320 | tf_op jit(solution)/shard_map/ppermute | solution.py:618
  182.5 1.4 collective-permute-start.26
  184.0 1.5 collective-permute-start.27
  185.5 2.1 fusion.1.refs_0_
  187.5 1.5 collective-permute-start.31
  193.3 8.0 %latent_keys_values.3.refs_0_.refs_2_.refs_3_ = bf16[1024,1024]{1,0:T(8,128)(2,1)S(1)} custom-call(s32[9]{0:T(128)S(1)} %stack.92.ids_ref, bf16[256,1024]{1,0:T(8,128)(2,1)S(1)} %copy-done.9, bf16[256,1024]{1,0:T(8,128)(2,1)} %collective-permute-done.19.refs_1_, bf16[256,1024]{1,0:T(8,128)(2,1)} %broadcast_select_fusion.3.refs_2_, ...), custom_call_target="tpu_custom_call" | custom-call | flops 4294967296 | bytes 4194304 | tf_op jit(solution)/shard_map/latent_keys_values/pallas_call | solution.py:460
  204.0 1.6 collective-permute-start.32
  205.9 6.1 %latent_keys_values.4.refs_1_.refs_3_.refs_4_ = bf16[768,1024]{1,0:T(8,128)(2,1)S(1)} custom-call(s32[9]{0:T(128)S(1)} %stack.92.ids_ref, bf16[256,1024]{1,0:T(8,128)(2,1)} %fusion.1.refs_0_, bf16[256,1024]{1,0:T(8,128)(2,1)} %collective-permute-done.31.refs_1_, bf16[256,1024]{1,0:T(8,128)(2,1)S(1)} %select_select_fusion.1.refs_2_, ...), custom_call_target="tpu_custom_call" | custom-call | flops 3221225472 | bytes 4194304 | tf_op jit(solution)/shard_map/latent_keys_values/pallas_call | solution.py:460
  213.1 7.4 %decode_rows.3 = (f32[512,512]{1,0:T(8,128)}, f32[512,256]{1,0:T(8,128)}) custom-call(bf16[512,512]{1,0:T(8,128)(2,1)} %collective-permute-done.13.q_ref, bf16[1024,1024]{1,0:T(8,128)(2,1)} %copy-done.12, bf16[768,1024]{1,0:T(8,128)(2,1)} %copy-done.11, bf16[1024,1024]{1,0:T(8,128)(2,1)} %copy-done.12, bf16[768,1024]{1,0:T(8,128)(2,1)} %copy-done.11), custom_call_target="tpu_custom_call" | custom-call | flops 7516192768 | bytes 5242880 | tf_op jit(solution)/shard_map/decode_rows/pallas_call | solution.py:546
  220.8 2.1 collective-permute-done.36.refs_1_
  225.0 3.5 %latent_keys_values.5.refs_2_.refs_5_.refs_0_.refs_1_ = bf16[256,1024]{1,0:T(8,128)(2,1)S(1)} custom-call(s32[9]{0:T(128)S(1)} %stack.92.ids_ref, bf16[256,1024]{1,0:T(8,128)(2,1)} %collective-permute-done.32.refs_0_, bf16[256,1024]{1,0:T(8,128)(2,1)} %collective-permute-done.36.refs_1_, bf16[256,1024]{1,0:T(8,128)(2,1)S(1)} %get-tuple-element.130.refs_8_.refs_6_.refs_2_, ...), custom_call_target="tpu_custom_call" | custom-call | flops 1073741824 | bytes 4194304 | tf_op jit(solution)/shard_map/latent_keys_values/pallas_call | solution.py:460
  229.2 3.4 %decode_rows.5 = bf16[512,512]{1,0:T(8,128)(2,1)} custom-call(bf16[512,512]{1,0:T(8,128)(2,1)} %collective-permute-done.13.q_ref, bf16[256,1024]{1,0:T(8,128)(2,1)} %copy-done.7, bf16[256,1024]{1,0:T(8,128)(2,1)} %copy-done.7, f32[512,512]{1,0:T(8,128)} %get-tuple-element.144.refs_2_, f32[512,256]{1,0:T(8,128)} %get-tuple-element.145.refs_3_), custom_call_target="tpu_custom_call" | custom-call | flops 1073741824 | bytes 2097152 | tf_op jit(solution)/shard_map/decode_rows/pallas_call | solution.py:546
  232.6 1.5 collective-permute-start.37
  234.1 8.4 %decode_rows.4 = f32[512,512]{1,0:T(8,128)} custom-call(bf16[512,512]{1,0:T(8,128)(2,1)} %get-tuple-element.152.q_ref, bf16[1024,1024]{1,0:T(8,128)(2,1)} %copy-done.12, bf16[768,1024]{1,0:T(8,128)(2,1)} %copy-done.11, bf16[256,1024]{1,0:T(8,128)(2,1)} %copy-done.7, bf16[1024,1024]{1,0:T(8,128)(2,1)} %copy-done.12, bf16[768,1024]{1,0:T(8,128)(2,1)} %copy-done.11, ...), custom_call_target="tpu_custom_call" | custom-call | flops 8589934592 | bytes 5767168 | tf_op jit(solution)/shard_map/decode_rows/pallas_call | solution.py:546
  242.5 4.3 %collective-permute-done.37 = bf16[512,512]{1,0:T(8,128)(2,1)S(1)} collective-permute-done((bf16[512,512]{1,0:T(8,128)(2,1)}, bf16[512,512]{1,0:T(8,128)(2,1)S(1)}, u32[]{:S(2)}, u32[]{:S(2)}) %collective-permute-start.37) | collective-permute-done | bytes 524320 | tf_op jit(solution)/shard_map/ppermute | solution.py:780
  246.9 1.6 fusion
  (151 shorter events, 42.6 us)
Async XLA Ops:
  0.6 99.6 %copy-start = (bf16[3,1024]{1,0:T(4,128)(2,1)S(1)}, bf16[3,1024]{1,0:T(4,128)(2,1)}, u32[]{:S(2)}) copy-start(bf16[3,1024]{1,0:T(4,128)(2,1)} %param.25) | copy-start | bytes 18436
  2.7 10.2 %copy-start.30 = (f32[3,8]{1,0:T(4,128)S(1)}, f32[3,8]{1,0:T(4,128)}, u32[]{:S(2)}) copy-start(f32[3,8]{1,0:T(4,128)} %param.26) | copy-start | bytes 292
  2.7 10.9 %copy-start.23 = (bf16[256,1024]{1,0:T(8,128)(2,1)S(1)}, bf16[256,1024]{1,0:T(8,128)(2,1)}, u32[]{:S(2)}) copy-start(bf16[256,1024]{1,0:T(8,128)(2,1)} %param.22) | copy-start | bytes 1572868
  2.8 10.9 %copy-start.24 = (bf16[256,1024]{1,0:T(8,128)(2,1)S(1)}, bf16[256,1024]{1,0:T(8,128)(2,1)}, u32[]{:S(2)}) copy-start(bf16[256,1024]{1,0:T(8,128)(2,1)} %param.21) | copy-start | bytes 1572868
  2.9 32.1 %collective-permute-start = (bf16[528,1024]{1,0:T(8,128)(2,1)S(1)}, bf16[528,1024]{1,0:T(8,128)(2,1)}, u32[]{:S(2)}, u32[]{:S(2)}) collective-permute-start(bf16[528,1024]{1,0:T(8,128)(2,1)S(1)} %pad_maximum_fusion), channel_id=1, source_target_pairs={{0,2},{2,0},{4,6},{6,4},{8,10},{10,8},{12,14},{14,12},{1,3},{3,1},... | collective-permute-start | bytes 3244040 | tf_op jit(solution)/shard_map/ppermute | solution.py:611
  8.4 10.9 %collective-permute-start.1 = (bf16[528,256]{1,0:T(8,128)(2,1)}, bf16[528,256]{1,0:T(8,128)(2,1)}, u32[]{:S(2)}, u32[]{:S(2)}) collective-permute-start(bf16[528,256]{1,0:T(8,128)(2,1)} %pad_maximum_fusion.3), channel_id=1, source_target_pairs={{4,0},{6,2},{8,4},{10,6},{12,8},{14,10},{0,12},{2,14},{5,1},{7,3},... | collective-permute-start | bytes 811016 | tf_op jit(solution)/shard_map/ppermute | solution.py:614
  12.0 23.0 %collective-permute-start.2 = (bf16[528,256]{1,0:T(8,128)(2,1)}, bf16[528,256]{1,0:T(8,128)(2,1)}, u32[]{:S(2)}, u32[]{:S(2)}) collective-permute-start(bf16[528,256]{1,0:T(8,128)(2,1)} %pad_maximum_fusion.3), channel_id=1, source_target_pairs={{8,0},{10,2},{12,4},{14,6},{0,8},{2,10},{4,12},{6,14},{9,1},{11,3}... | collective-permute-start | bytes 811016 | tf_op jit(solution)/shard_map/ppermute | solution.py:614
  12.0 23.0 %collective-permute-start.3 = (bf16[528,256]{1,0:T(8,128)(2,1)}, bf16[528,256]{1,0:T(8,128)(2,1)S(1)}, u32[]{:S(2)}, u32[]{:S(2)}) collective-permute-start(bf16[528,256]{1,0:T(8,128)(2,1)} %pad_maximum_fusion.3), channel_id=1, source_target_pairs={{12,0},{14,2},{0,4},{2,6},{4,8},{6,10},{8,12},{10,14},{13,1},{15,3... | collective-permute-start | bytes 811016 | tf_op jit(solution)/shard_map/ppermute | solution.py:614
  35.0 15.0 %copy-start.25 = (bf16[528,256]{1,0:T(8,128)(2,1)}, bf16[528,256]{1,0:T(8,128)(2,1)S(1)}, u32[]{:S(2)}) copy-start(bf16[528,256]{1,0:T(8,128)(2,1)S(1)} %collective-permute-done.3) | copy-start | bytes 811012
  35.0 15.0 %collective-permute-start.4 = (bf16[256,1024]{1,0:T(8,128)(2,1)S(1)}, bf16[256,1024]{1,0:T(8,128)(2,1)S(1)}, u32[]{:S(2)}, u32[]{:S(2)}) collective-permute-start(bf16[256,1024]{1,0:T(8,128)(2,1)S(1)} %pad_maximum_fusion.1), channel_id=1, source_target_pairs={{0,2},{2,0},{4,6},{6,4},{8,10},{10,8},{12,14},{14,12},{1,3},{3,1},... | collective-permute-start | bytes 1572872 | tf_op jit(solution)/shard_map/ppermute | solution.py:611
  50.1 58.8 %all-to-all-start = ((bf16[4,528,512]{2,1,0:T(8,128)(2,1)}), bf16[4,528,512]{2,1,0:T(8,128)(2,1)S(1)}, u32[]{:S(2)}, u32[]{:S(2)}) async-start(bf16[4,528,512]{2,1,0:T(8,128)(2,1)} %bitcast.52), calls=%async_computation | async-start | bytes 4325376 | tf_op jit(solution)/shard_map/all_to_all | solution.py:672
  54.1 38.2 %copy-start.22 = (bf16[256,512]{1,0:T(8,128)(2,1)S(1)}, bf16[256,512]{1,0:T(8,128)(2,1)}, u32[]{:S(2)}) copy-start(bf16[256,512]{1,0:T(8,128)(2,1)} %get-tuple-element.158) | copy-start | bytes 786436
  58.5 30.3 %collective-permute-start.5 = (bf16[2624,256]{1,0:T(8,128)(2,1)}, bf16[2624,256]{1,0:T(8,128)(2,1)S(1)}, u32[]{:S(2)}, u32[]{:S(2)}) collective-permute-start(bf16[2624,256]{1,0:T(8,128)(2,1)} %get-tuple-element.161), channel_id=1, source_target_pairs={{0,2},{2,0},{4,6},{6,4},{8,10},{10,8},{12,14},{14,12},{1,3},{3,1},... | collective-permute-start | bytes 4030472 | tf_op jit(solution)/shard_map/ppermute | solution.py:611
  60.1 43.2 %collective-permute-start.6 = (bf16[1584,256]{1,0:T(8,128)(2,1)}, bf16[1584,256]{1,0:T(8,128)(2,1)}, u32[]{:S(2)}, u32[]{:S(2)}) collective-permute-start(bf16[1584,256]{1,0:T(8,128)(2,1)} %get-tuple-element.160.refs_1_), channel_id=1, source_target_pairs={{0,16},{16,0},{1,17},{17,1},{2,18},{18,2},{3,19},{19,3},{4,20},{20... | collective-permute-start | bytes 2433032 | tf_op jit(solution)/shard_map/ppermute | solution.py:608
  90.8 18.0 %collective-permute-start.7 = (bf16[1584,256]{1,0:T(8,128)(2,1)}, bf16[1584,256]{1,0:T(8,128)(2,1)}, u32[]{:S(2)}, u32[]{:S(2)}) collective-permute-start(bf16[1584,256]{1,0:T(8,128)(2,1)} %slice.62), channel_id=1, source_target_pairs={{0,16},{16,0},{1,17},{17,1},{2,18},{18,2},{3,19},{19,3},{4,20},{20... | collective-permute-start | bytes 2433032 | tf_op jit(solution)/shard_map/ppermute | solution.py:608
  94.5 17.0 %collective-permute-start.9 = (bf16[256,1024]{1,0:T(8,128)(2,1)}, bf16[256,1024]{1,0:T(8,128)(2,1)}, u32[]{:S(2)}, u32[]{:S(2)}) collective-permute-start(bf16[256,1024]{1,0:T(8,128)(2,1)} %get-tuple-element.155), channel_id=1, source_target_pairs={{0,4},{2,6},{4,8},{6,10},{8,12},{10,14},{1,5},{3,7},{5,9},{7,11},{... | collective-permute-start | bytes 1572872 | tf_op jit(solution)/shard_map/ppermute | solution.py:618
  98.9 15.3 %collective-permute-start.10 = (bf16[256,1024]{1,0:T(8,128)(2,1)}, bf16[256,1024]{1,0:T(8,128)(2,1)}, u32[]{:S(2)}, u32[]{:S(2)}) collective-permute-start(bf16[256,1024]{1,0:T(8,128)(2,1)} %get-tuple-element.155), channel_id=1, source_target_pairs={{12,8},{14,10},{8,4},{10,6},{4,0},{6,2},{13,9},{15,11},{9,5},{11,7... | collective-permute-start | bytes 1572872 | tf_op jit(solution)/shard_map/ppermute | solution.py:618
  101.8 27.5 %collective-permute-start.13 = (bf16[512,512]{1,0:T(8,128)(2,1)}, bf16[512,512]{1,0:T(8,128)(2,1)}, u32[]{:S(2)}, u32[]{:S(2)}) collective-permute-start(bf16[512,512]{1,0:T(8,128)(2,1)} %get-tuple-element.153), channel_id=1, source_target_pairs={{0,2},{2,0},{4,6},{6,4},{8,10},{10,8},{12,14},{14,12},{1,3},{3,1},... | collective-permute-start | bytes 1572872 | tf_op jit(solution)/shard_map/ppermute | solution.py:611
  114.2 15.1 %collective-permute-start.11 = (bf16[256,1024]{1,0:T(8,128)(2,1)}, bf16[256,1024]{1,0:T(8,128)(2,1)S(1)}, u32[]{:S(2)}, u32[]{:S(2)}) collective-permute-start(bf16[256,1024]{1,0:T(8,128)(2,1)} %collective-permute-done.9), channel_id=1, source_target_pairs={{4,8},{6,10},{8,12},{10,14},{5,9},{7,11},{9,13},{11,15},{20,24},{2... | collective-permute-start | bytes 1572872 | tf_op jit(solution)/shard_map/ppermute | solution.py:618
  114.8 14.4 %collective-permute-start.12 = (bf16[256,1024]{1,0:T(8,128)(2,1)}, bf16[256,1024]{1,0:T(8,128)(2,1)S(1)}, u32[]{:S(2)}, u32[]{:S(2)}) collective-permute-start(bf16[256,1024]{1,0:T(8,128)(2,1)} %collective-permute-done.10), channel_id=1, source_target_pairs={{8,4},{10,6},{4,0},{6,2},{9,5},{11,7},{5,1},{7,3},{24,20},{26,22},... | collective-permute-start | bytes 1572872 | tf_op jit(solution)/shard_map/ppermute | solution.py:618
  116.1 6.6 %collective-permute-start.8 = (bf16[256,512]{1,0:T(8,128)(2,1)S(1)}, bf16[256,512]{1,0:T(8,128)(2,1)S(1)}, u32[]{:S(2)}, u32[]{:S(2)}) collective-permute-start(bf16[256,512]{1,0:T(8,128)(2,1)S(1)} %get-tuple-element.85), channel_id=1, source_target_pairs={{0,2},{2,0},{4,6},{6,4},{8,10},{10,8},{12,14},{14,12},{1,3},{3,1},... | collective-permute-start | bytes 786440 | tf_op jit(solution)/shard_map/ppermute | solution.py:611
  123.5 11.7 %copy-start.31 = (s32[3]{0:T(128)S(1)}, s32[3]{0:T(128)}, u32[]{:S(2)}) copy-start(s32[3]{0:T(128)} %param.27) | copy-start | bytes 40
  129.3 8.4 %collective-permute-start.14 = (f32[256,2048]{1,0:T(8,128)}, f32[256,2048]{1,0:T(8,128)}, u32[]{:S(2)}, u32[]{:S(2)}) collective-permute-start(f32[256,2048]{1,0:T(8,128)} %project_rows.1.mine_ref), channel_id=1, source_target_pairs={{0,1},{1,0},{2,3},{3,2},{4,5},{5,4},{6,7},{7,6},{8,9},{9,8},{10,11... | collective-permute-start | bytes 6291464 | tf_op jit(solution)/shard_map/ppermute | solution.py:715
  131.6 17.3 %collective-permute-start.21 = (bf16[256,1024]{1,0:T(8,128)(2,1)S(1)}, bf16[256,1024]{1,0:T(8,128)(2,1)}, u32[]{:S(2)}, u32[]{:S(2)}) collective-permute-start(bf16[256,1024]{1,0:T(8,128)(2,1)S(1)} %collective-permute-done.11), channel_id=1, source_target_pairs={{8,12},{10,14},{9,13},{11,15},{24,28},{26,30},{25,29},{27,31}} | collective-permute-start | bytes 1572872 | tf_op jit(solution)/shard_map/ppermute | solution.py:618
  133.1 17.4 %collective-permute-start.22 = (bf16[256,1024]{1,0:T(8,128)(2,1)S(1)}, bf16[256,1024]{1,0:T(8,128)(2,1)}, u32[]{:S(2)}, u32[]{:S(2)}) collective-permute-start(bf16[256,1024]{1,0:T(8,128)(2,1)S(1)} %collective-permute-done.12), channel_id=1, source_target_pairs={{4,0},{6,2},{5,1},{7,3},{20,16},{22,18},{21,17},{23,19}} | collective-permute-start | bytes 1572872 | tf_op jit(solution)/shard_map/ppermute | solution.py:618
  135.4 29.4 %collective-permute-start.20 = (bf16[256,1024]{1,0:T(8,128)(2,1)S(1)}, bf16[256,1024]{1,0:T(8,128)(2,1)S(1)}, u32[]{:S(2)}, u32[]{:S(2)}) collective-permute-start(bf16[256,1024]{1,0:T(8,128)(2,1)S(1)} %broadcast_select_fusion.2.refs_10_.refs_8_.refs_4_), channel_id=1, source_target_pairs={{0,16},{16,0},{1,17},{17,1},{2,18},{18,2},{3,19},{19,3},{4,20},{20... | collective-permute-start | bytes 1572872 | tf_op jit(solution)/shard_map/ppermute | solution.py:608
  142.3 16.9 %collective-permute-start.15 = (bf16[256,1024]{1,0:T(8,128)(2,1)}, bf16[256,1024]{1,0:T(8,128)(2,1)S(1)}, u32[]{:S(2)}, u32[]{:S(2)}) collective-permute-start(bf16[256,1024]{1,0:T(8,128)(2,1)} %get-tuple-element.118.refs_0_), channel_id=1, source_target_pairs={{0,4},{2,6},{4,8},{6,10},{8,12},{10,14},{1,5},{3,7},{5,9},{7,11},{... | collective-permute-start | bytes 1572872 | tf_op jit(solution)/shard_map/ppermute | solution.py:618
  147.6 15.6 %collective-permute-start.16 = (bf16[256,1024]{1,0:T(8,128)(2,1)}, bf16[256,1024]{1,0:T(8,128)(2,1)S(1)}, u32[]{:S(2)}, u32[]{:S(2)}) collective-permute-start(bf16[256,1024]{1,0:T(8,128)(2,1)} %get-tuple-element.118.refs_0_), channel_id=1, source_target_pairs={{12,8},{14,10},{8,4},{10,6},{4,0},{6,2},{13,9},{15,11},{9,5},{11,7... | collective-permute-start | bytes 1572872 | tf_op jit(solution)/shard_map/ppermute | solution.py:618
  148.9 17.1 %collective-permute-start.19 = (bf16[256,1024]{1,0:T(8,128)(2,1)}, bf16[256,1024]{1,0:T(8,128)(2,1)}, u32[]{:S(2)}, u32[]{:S(2)}) collective-permute-start(bf16[256,1024]{1,0:T(8,128)(2,1)} %get-tuple-element.118.refs_0_), channel_id=1, source_target_pairs={{0,2},{2,0},{4,6},{6,4},{8,10},{10,8},{12,14},{14,12},{1,3},{3,1},... | collective-permute-start | bytes 1572872 | tf_op jit(solution)/shard_map/ppermute | solution.py:611
  151.6 16.0 %collective-permute-start.23 = (bf16[256,1024]{1,0:T(8,128)(2,1)S(1)}, bf16[256,1024]{1,0:T(8,128)(2,1)S(1)}, u32[]{:S(2)}, u32[]{:S(2)}) collective-permute-start(bf16[256,1024]{1,0:T(8,128)(2,1)S(1)} %broadcast_select_fusion.1.refs_12_.refs_10_.refs_6_), channel_id=1, source_target_pairs={{0,16},{16,0},{1,17},{17,1},{2,18},{18,2},{3,19},{19,3},{4,20},{20... | collective-permute-start | bytes 1572872 | tf_op jit(solution)/shard_map/ppermute | solution.py:608
  159.2 17.0 %copy-start.15 = (bf16[256,1024]{1,0:T(8,128)(2,1)}, bf16[256,1024]{1,0:T(8,128)(2,1)S(1)}, u32[]{:S(2)}) copy-start(bf16[256,1024]{1,0:T(8,128)(2,1)S(1)} %collective-permute-done.15) | copy-start | bytes 1572868
  159.2 17.0 %collective-permute-start.24 = (bf16[256,1024]{1,0:T(8,128)(2,1)S(1)}, bf16[256,1024]{1,0:T(8,128)(2,1)S(1)}, u32[]{:S(2)}, u32[]{:S(2)}) collective-permute-start(bf16[256,1024]{1,0:T(8,128)(2,1)S(1)} %broadcast_select_fusion.refs_14_.refs_12_.refs_8_), channel_id=1, source_target_pairs={{0,16},{16,0},{1,17},{17,1},{2,18},{18,2},{3,19},{19,3},{4,20},{20... | collective-permute-start | bytes 1572872 | tf_op jit(solution)/shard_map/ppermute | solution.py:608
  163.2 13.7 %collective-permute-start.17 = (bf16[256,1024]{1,0:T(8,128)(2,1)S(1)}, bf16[256,1024]{1,0:T(8,128)(2,1)S(1)}, u32[]{:S(2)}, u32[]{:S(2)}) collective-permute-start(bf16[256,1024]{1,0:T(8,128)(2,1)S(1)} %collective-permute-done.15), channel_id=1, source_target_pairs={{4,8},{6,10},{8,12},{10,14},{5,9},{7,11},{9,13},{11,15},{20,24},{2... | collective-permute-start | bytes 1572872 | tf_op jit(solution)/shard_map/ppermute | solution.py:618
  164.8 16.5 %collective-permute-start.18 = (bf16[256,1024]{1,0:T(8,128)(2,1)S(1)}, bf16[256,1024]{1,0:T(8,128)(2,1)S(1)}, u32[]{:S(2)}, u32[]{:S(2)}) collective-permute-start(bf16[256,1024]{1,0:T(8,128)(2,1)S(1)} %collective-permute-done.16), channel_id=1, source_target_pairs={{8,4},{10,6},{4,0},{6,2},{9,5},{11,7},{5,1},{7,3},{24,20},{26,22},... | collective-permute-start | bytes 1572872 | tf_op jit(solution)/shard_map/ppermute | solution.py:618
  166.1 16.0 %collective-permute-start.25 = (bf16[256,1024]{1,0:T(8,128)(2,1)}, bf16[256,1024]{1,0:T(8,128)(2,1)}, u32[]{:S(2)}, u32[]{:S(2)}) collective-permute-start(bf16[256,1024]{1,0:T(8,128)(2,1)} %broadcast_select_fusion.3.refs_2_), channel_id=1, source_target_pairs={{0,2},{2,0},{4,6},{6,4},{8,10},{10,8},{12,14},{14,12},{1,3},{3,1},... | collective-permute-start | bytes 1572872 | tf_op jit(solution)/shard_map/ppermute | solution.py:611
  182.0 5.5 %collective-permute-start.28 = (bf16[256,1024]{1,0:T(8,128)(2,1)}, bf16[256,1024]{1,0:T(8,128)(2,1)}, u32[]{:S(2)}, u32[]{:S(2)}) collective-permute-start(bf16[256,1024]{1,0:T(8,128)(2,1)} %collective-permute-done.19.refs_1_), channel_id=1, source_target_pairs={{0,1},{1,0},{2,3},{3,2},{4,5},{5,4},{6,7},{7,6},{8,9},{9,8},{10,11... | collective-permute-start | bytes 1572872 | tf_op jit(solution)/shard_map/ppermute | solution.py:725
  182.0 7.1 %collective-permute-start.29 = (bf16[256,1024]{1,0:T(8,128)(2,1)}, bf16[256,1024]{1,0:T(8,128)(2,1)}, u32[]{:S(2)}, u32[]{:S(2)}) collective-permute-start(bf16[256,1024]{1,0:T(8,128)(2,1)} %broadcast_select_fusion.3.refs_2_), channel_id=1, source_target_pairs={{0,1},{1,0},{2,3},{3,2},{4,5},{5,4},{6,7},{7,6},{8,9},{9,8},{10,11... | collective-permute-start | bytes 1572872 | tf_op jit(solution)/shard_map/ppermute | solution.py:725
  182.5 6.6 %collective-permute-start.30 = (bf16[256,1024]{1,0:T(8,128)(2,1)}, bf16[256,1024]{1,0:T(8,128)(2,1)}, u32[]{:S(2)}, u32[]{:S(2)}) collective-permute-start(bf16[256,1024]{1,0:T(8,128)(2,1)} %collective-permute-done.25.refs_3_), channel_id=1, source_target_pairs={{0,1},{1,0},{2,3},{3,2},{4,5},{5,4},{6,7},{7,6},{8,9},{9,8},{10,11... | collective-permute-start | bytes 1572872 | tf_op jit(solution)/shard_map/ppermute | solution.py:725
  182.5 18.8 %collective-permute-start.26 = (bf16[256,1024]{1,0:T(8,128)(2,1)}, bf16[256,1024]{1,0:T(8,128)(2,1)}, u32[]{:S(2)}, u32[]{:S(2)}) collective-permute-start(bf16[256,1024]{1,0:T(8,128)(2,1)} %copy-done.16), channel_id=1, source_target_pairs={{8,12},{10,14},{9,13},{11,15},{24,28},{26,30},{25,29},{27,31}} | collective-permute-start | bytes 1572872 | tf_op jit(solution)/shard_map/ppermute | solution.py:618
  184.0 17.4 %collective-permute-start.27 = (bf16[256,1024]{1,0:T(8,128)(2,1)}, bf16[256,1024]{1,0:T(8,128)(2,1)}, u32[]{:S(2)}, u32[]{:S(2)}) collective-permute-start(bf16[256,1024]{1,0:T(8,128)(2,1)} %copy-done.18), channel_id=1, source_target_pairs={{4,0},{6,2},{5,1},{7,3},{20,16},{22,18},{21,17},{23,19}} | collective-permute-start | bytes 1572872 | tf_op jit(solution)/shard_map/ppermute | solution.py:618
  187.5 14.7 %collective-permute-start.31 = (bf16[256,1024]{1,0:T(8,128)(2,1)}, bf16[256,1024]{1,0:T(8,128)(2,1)}, u32[]{:S(2)}, u32[]{:S(2)}) collective-permute-start(bf16[256,1024]{1,0:T(8,128)(2,1)} %fusion.1.refs_0_), channel_id=1, source_target_pairs={{0,2},{2,0},{4,6},{6,4},{8,10},{10,8},{12,14},{14,12},{1,3},{3,1},... | collective-permute-start | bytes 1572872 | tf_op jit(solution)/shard_map/ppermute | solution.py:611
  193.3 9.4 %copy-start.19 = (bf16[256,1024]{1,0:T(8,128)(2,1)S(1)}, bf16[256,1024]{1,0:T(8,128)(2,1)}, u32[]{:S(2)}) copy-start(bf16[256,1024]{1,0:T(8,128)(2,1)} %copy-done.18) | copy-start | bytes 1572868
  202.2 3.4 %collective-permute-start.33 = (bf16[256,1024]{1,0:T(8,128)(2,1)}, bf16[256,1024]{1,0:T(8,128)(2,1)S(1)}, u32[]{:S(2)}, u32[]{:S(2)}) collective-permute-start(bf16[256,1024]{1,0:T(8,128)(2,1)} %fusion.1.refs_0_), channel_id=1, source_target_pairs={{0,1},{1,0},{2,3},{3,2},{4,5},{5,4},{6,7},{7,6},{8,9},{9,8},{10,11... | collective-permute-start | bytes 1572872 | tf_op jit(solution)/shard_map/ppermute | solution.py:725
  202.2 3.4 %collective-permute-start.34 = (bf16[256,1024]{1,0:T(8,128)(2,1)}, bf16[256,1024]{1,0:T(8,128)(2,1)S(1)}, u32[]{:S(2)}, u32[]{:S(2)}) collective-permute-start(bf16[256,1024]{1,0:T(8,128)(2,1)} %collective-permute-done.31.refs_1_), channel_id=1, source_target_pairs={{0,1},{1,0},{2,3},{3,2},{4,5},{5,4},{6,7},{7,6},{8,9},{9,8},{10,11... | collective-permute-start | bytes 1572872 | tf_op jit(solution)/shard_map/ppermute | solution.py:725
  203.9 2.0 collective-permute-start.35
  204.0 16.5 %collective-permute-start.32 = (bf16[256,1024]{1,0:T(8,128)(2,1)S(1)}, bf16[256,1024]{1,0:T(8,128)(2,1)}, u32[]{:S(2)}, u32[]{:S(2)}) collective-permute-start(bf16[256,1024]{1,0:T(8,128)(2,1)S(1)} %select_select_fusion.1.refs_2_), channel_id=1, source_target_pairs={{0,2},{2,0},{4,6},{6,4},{8,10},{10,8},{12,14},{14,12},{1,3},{3,1},... | collective-permute-start | bytes 1572872 | tf_op jit(solution)/shard_map/ppermute | solution.py:611
  220.6 2.3 collective-permute-start.36
  232.6 14.2 %collective-permute-start.37 = (bf16[512,512]{1,0:T(8,128)(2,1)}, bf16[512,512]{1,0:T(8,128)(2,1)S(1)}, u32[]{:S(2)}, u32[]{:S(2)}) collective-permute-start(bf16[512,512]{1,0:T(8,128)(2,1)} %decode_rows.5), channel_id=1, source_target_pairs={{0,2},{2,0},{4,6},{6,4},{8,10},{10,8},{12,14},{14,12},{1,3},{3,1},... | collective-permute-start | bytes 1572872 | tf_op jit(solution)/shard_map/ppermute | solution.py:780
  (23 other events, 58.4 us)
